TPU v7x, 32 devices: a whole 2x2x4 slice. The times are simulated.
32 devices in a mesh: groups: 2 (over y), row: 16 (over z, x, core).
Axes of the slice: x: 2, y: 2, z: 4, core: 2. Of those that a mesh axis runs over, the one named last changes fastest.
Arguments:
- pair_rep: bfloat16 [96, 48, 128], P(('groups', 'row')), parts along dimension 0, may hold values from -6 to 6
- residue_valid: int32 [96], P('groups'), parts along dimension 0, may hold values from 0 to 1
- tri_norm_gain: float32 [128], replicated, may hold values from 0.5 to 1.5
- tri_norm_bias: float32 [128], replicated, may hold values from -3 to 3
- w_edges: bfloat16 [128, 512], replicated, may hold values from -0.5 to 0.5
- w_tri_gate: bfloat16 [128, 128], replicated, may hold values from -0.5 to 0.5
- out_norm_gain: float32 [128], replicated, may hold values from 0.5 to 1.5
- out_norm_bias: float32 [128], replicated, may hold values from -3 to 3
- w_tri_out: bfloat16 [128, 128], replicated, may hold values from -0.5 to 0.5
- att_norm_gain: float32 [128], replicated, may hold values from 0.5 to 1.5
- att_norm_bias: float32 [128], replicated, may hold values from -3 to 3
- w_query: bfloat16 [128, 128], replicated, may hold values from -2.4748737 to 2.4748737
- w_key: bfloat16 [128, 128], replicated, may hold values from -2.4748737 to 2.4748737
- w_value: bfloat16 [128, 128], replicated, may hold values from -0.5 to 0.5
- w_att_gate: bfloat16 [128, 128], replicated, may hold values from -0.5 to 0.5
- w_pair_bias: bfloat16 [128, 4], replicated, may hold values from -1.0546875 to 1.0546875
- w_att_out: bfloat16 [128, 128], replicated, may hold values from -0.5 to 0.5
Outputs:
- updated_pair: bfloat16 [96, 48, 128], P(('groups', 'row')), parts along dimension 0
There are 2 independent parts, one for each index of `groups`. A program takes and returns all parts, laid end to end along the dimension named above; an argument that names none is the same for every part. Nothing has to cross between parts.
All inputs are finite; a program needn't handle non-finite values.
Results may differ from a plain program's by a relative error of at most 0.0097.
Values may be sent and summed in bfloat16 or wider, within the bound.
No kernel may reach another device: no remote copies, remote signals or barrier semaphores. Data moves between devices by JAX's collectives and lax.ppermute only.
A program may use at most 64 MiB of HBM per device.

v0:
```python
import math

import jax
import jax.numpy as jnp
from jax import lax
from jax.sharding import PartitionSpec as P

HEADS = 4
HEAD_DIM = 32


def layer_norm(values, norm_gain, norm_bias, along_axis):
    centre = values - jnp.mean(values, axis=along_axis, keepdims=True)
    spread = jnp.mean(centre * centre, axis=along_axis, keepdims=True)
    return centre * lax.rsqrt(spread + 1e-05) * norm_gain + norm_bias


def attend(query_cols, key_cols, value_cols, whole_bias, key_mask):
    factor = 1.0 / math.sqrt(HEAD_DIM)
    scores = (
        jnp.einsum("kjhd,ijhd->jhki", key_cols, query_cols, preferred_element_type=jnp.float32)
        * factor
    )
    scores = scores + whole_bias.astype(jnp.float32)[None] + key_mask[None, None, :, None]
    scores = scores - jnp.max(scores, axis=2, keepdims=True)
    exponent = jnp.exp(scores)
    weights = (exponent / jnp.sum(exponent, axis=2, keepdims=True)).astype(jnp.bfloat16)
    return jnp.einsum("jhki,kjhd->ijhd", weights, value_cols, preferred_element_type=jnp.float32)


def per_device(
    pair_rep,
    residue_valid,
    tri_norm_gain,
    tri_norm_bias,
    w_edges,
    w_tri_gate,
    out_norm_gain,
    out_norm_bias,
    w_tri_out,
    att_norm_gain,
    att_norm_bias,
    w_query,
    w_key,
    w_value,
    w_att_gate,
    w_pair_bias,
    w_att_out,
):
    row_count = pair_rep.shape[0]
    res_count = pair_rep.shape[1]
    channels = pair_rep.shape[2]
    hidden_width = HEADS * HEAD_DIM
    row_start = lax.axis_index("row") * row_count
    valid_flags = residue_valid.astype(jnp.float32)
    own_valid = lax.dynamic_slice_in_dim(valid_flags, row_start, row_count)
    normed = layer_norm(pair_rep.astype(jnp.float32), tri_norm_gain, tri_norm_bias, 2).astype(
        jnp.bfloat16
    )
    projected = jnp.einsum("ikd,de->eik", normed, w_edges, preferred_element_type=jnp.float32)
    projected = projected.reshape(4, channels, row_count, res_count)
    pair_mask = (own_valid[:, None] * valid_flags[None, :])[None, :, :]
    left_edges = (jax.nn.sigmoid(projected[1]) * projected[0] * pair_mask).astype(jnp.bfloat16)
    right_edges = (jax.nn.sigmoid(projected[3]) * projected[2] * pair_mask).astype(jnp.bfloat16)
    left_cols, right_cols = (
        lax.all_to_all(left_edges, "row", split_axis=0, concat_axis=1, tiled=True),
        lax.all_to_all(right_edges, "row", split_axis=0, concat_axis=1, tiled=True),
    )
    block_product = jnp.einsum(
        "cik,cjk->cij", left_cols, right_cols, preferred_element_type=jnp.float32
    ).astype(jnp.bfloat16)
    triangle = lax.all_to_all(block_product, "row", split_axis=1, concat_axis=0, tiled=True)
    tri_normed = layer_norm(
        triangle.astype(jnp.float32), out_norm_gain[:, None, None], out_norm_bias[:, None, None], 0
    ).astype(jnp.bfloat16)
    tri_gate = jax.nn.sigmoid(
        jnp.einsum("ijc,ce->ije", normed, w_tri_gate, preferred_element_type=jnp.float32)
    )
    tri_update = jnp.einsum(
        "cij,ce->ije", tri_normed, w_tri_out, preferred_element_type=jnp.float32
    )
    after_tri = pair_rep.astype(jnp.float32) + tri_gate * tri_update
    att_in = layer_norm(after_tri, att_norm_gain, att_norm_bias, 2).astype(jnp.bfloat16)
    pair_bias = jnp.einsum(
        "kic,ch->hki", att_in, w_pair_bias, preferred_element_type=jnp.float32
    ).astype(jnp.bfloat16)
    whole_bias = lax.all_gather(pair_bias, "row", axis=1, tiled=True)
    key_mask = 1000000000.0 * (valid_flags - 1.0)
    columns = lax.all_to_all(att_in, "row", split_axis=1, concat_axis=0, tiled=True)
    all_weights = jnp.concatenate([w_query, w_key, w_value, w_att_gate], axis=1)
    joined = jnp.dot(columns.reshape(-1, channels), all_weights, preferred_element_type=jnp.float32)
    query_cols = (
        joined[:, :hidden_width].astype(jnp.bfloat16).reshape(res_count, row_count, HEADS, HEAD_DIM)
    )
    key_cols = (
        joined[:, hidden_width : 2 * hidden_width]
        .astype(jnp.bfloat16)
        .reshape(res_count, row_count, HEADS, HEAD_DIM)
    )
    value_cols = (
        joined[:, 2 * hidden_width : 3 * hidden_width]
        .astype(jnp.bfloat16)
        .reshape(res_count, row_count, HEADS, HEAD_DIM)
    )
    gate_cols = jax.nn.sigmoid(joined[:, 3 * hidden_width :]).reshape(
        res_count, row_count, hidden_width
    )
    attended = attend(query_cols, key_cols, value_cols, whole_bias, key_mask)
    gated = (attended.reshape(res_count, row_count, hidden_width) * gate_cols).astype(jnp.bfloat16)
    gated_rows = lax.all_to_all(gated, "row", split_axis=0, concat_axis=1, tiled=True)
    final = after_tri + jnp.einsum(
        "ije,ec->ijc", gated_rows, w_att_out, preferred_element_type=jnp.float32
    )
    return final.astype(jnp.bfloat16)


def solution(mesh):
    return jax.shard_map(
        per_device,
        mesh=mesh,
        in_specs=(
            P(("groups", "row"), None, None),
            P("groups"),
            P(),
            P(),
            P(),
            P(),
            P(),
            P(),
            P(),
            P(),
            P(),
            P(),
            P(),
            P(),
            P(),
            P(),
            P(),
        ),
        out_specs=P(("groups", "row"), None, None),
        check_vma=False,
    )
```

profile of v0, /device:TPU:0, one launch (start us, length us, event | category | flops | bytes accessed | tf_op | source)
XLA Modules:
  0.0 81.1 jit_solution(12793788514076153670)
XLA Ops:
  0.0 0.7 convert_element_type.66
  0.9 0.9 %convert_reduce_fusion = f32[3,48]{1,0:T(4,128)S(1)} fusion(bf16[3,48,128]{2,1,0:T(8,128)(2,1)} %param.17), kind=kLoop, calls=%fused_computation.40 | loop fusion | flops 36720 | bytes 37440 | tf_op jit(solution)/shard_map/reduce_sum | solution.py:13
  2.0 0.6 copy-done.8
  2.6 0.2 convolution_bitcast_fusion
  3.1 0.8 reshape.123
  3.8 7.4 %all-to-all-start = ((bf16[16,2,576]{2,1,0:T(2,128)(2,1)}), bf16[16,2,576]{2,1,0:T(2,128)(2,1)S(1)}, u32[]{:S(2)}, u32[]{:S(2)}) async-start(bf16[16,2,576]{2,1,0:T(2,128)(2,1)} %reshape.123), calls=%async_computation | async-start | bytes 81920 | tf_op jit(solution)/shard_map/all_to_all | solution.py:66
  11.3 0.8 reshape.121
  12.1 5.8 %all-to-all-done = bf16[16,2,576]{2,1,0:T(2,128)(2,1)S(1)} async-done(((bf16[16,2,576]{2,1,0:T(2,128)(2,1)}), bf16[16,2,576]{2,1,0:T(2,128)(2,1)S(1)}, u32[]{:S(2)}, u32[]{:S(2)}) %all-to-all-start) | async-done | bytes 36896 | tf_op jit(solution)/shard_map/all_to_all | solution.py:66
  17.9 3.5 %all-to-all-start.1 = ((bf16[16,2,576]{2,1,0:T(2,128)(2,1)}), bf16[16,2,576]{2,1,0:T(2,128)(2,1)S(1)}, u32[]{:S(2)}, u32[]{:S(2)}) async-start(bf16[16,2,576]{2,1,0:T(2,128)(2,1)} %reshape.121), calls=%async_computation.1 | async-start | bytes 81920 | tf_op jit(solution)/shard_map/all_to_all | solution.py:67
  21.4 0.2 fusion.8
  21.9 6.2 %all-to-all-done.1 = bf16[16,2,576]{2,1,0:T(2,128)(2,1)S(1)} async-done(((bf16[16,2,576]{2,1,0:T(2,128)(2,1)}), bf16[16,2,576]{2,1,0:T(2,128)(2,1)S(1)}, u32[]{:S(2)}, u32[]{:S(2)}) %all-to-all-start.1) | async-done | bytes 36896 | tf_op jit(solution)/shard_map/all_to_all | solution.py:67
  28.5 0.8 reshape.125
  29.3 3.6 %all-to-all-start.2 = ((bf16[16,2,576]{2,1,0:T(2,128)(2,1)}), bf16[16,2,576]{2,1,0:T(2,128)(2,1)S(1)}, u32[]{:S(2)}, u32[]{:S(2)}) async-start(bf16[16,2,576]{2,1,0:T(2,128)(2,1)} %reshape.125), calls=%async_computation.2 | async-start | bytes 81920 | tf_op jit(solution)/shard_map/all_to_all | solution.py:72
  32.9 6.6 %all-to-all-done.2 = bf16[16,2,576]{2,1,0:T(2,128)(2,1)S(1)} async-done(((bf16[16,2,576]{2,1,0:T(2,128)(2,1)}), bf16[16,2,576]{2,1,0:T(2,128)(2,1)S(1)}, u32[]{:S(2)}, u32[]{:S(2)}) %all-to-all-start.2) | async-done | bytes 36896 | tf_op jit(solution)/shard_map/all_to_all | solution.py:72
  39.9 0.7 copy-done.13
  40.5 0.4 fusion.64
  41.1 0.6 copy-done.10
  41.9 0.6 copy.74
  42.7 3.5 %all-to-all-start.3 = ((bf16[3,48,128]{2,0,1:T(4,128)(2,1)}), bf16[3,48,128]{2,0,1:T(4,128)(2,1)S(1)}, u32[]{:S(2)}, u32[]{:S(2)}) async-start(bf16[3,48,128]{2,0,1:T(4,128)(2,1)} %copy.74), calls=%async_computation.3 | async-start | bytes 98304 | tf_op jit(solution)/shard_map/all_to_all | solution.py:89
  46.2 21.8 %all_gather.3 = bf16[4,48,48]{2,0,1:T(4,128)(2,1)S(1)} all-gather(bf16[4,3,48]{2,0,1:T(4,128)(2,1)S(1)} %fusion.10), channel_id=1, replica_groups=mesh['groups'=2,'row'=16] {'row'}, dimensions={1}, use_global_device_ids=true | all-gather | bytes 19584 | tf_op jit(solution)/shard_map/all_gather | solution.py:87
  68.1 0.6 copy-done.4
  70.2 9.3 %all_to_all.78 = bf16[48,3,128]{2,1,0:T(4,128)(2,1)S(1)} all-to-all(bf16[48,3,128]{2,1,0:T(4,128)(2,1)S(1)} %multiply_convert_fusion), channel_id=1, replica_groups=mesh['groups'=2,'row'=16] {'row'}, dimensions={0} | all-to-all | bytes 73728 | tf_op jit(solution)/shard_map/all_to_all | solution.py:110
  79.6 0.7 copy-done.6
  80.3 0.8 fusion.9
  (74 shorter events, 3.6 us)
Async XLA Ops:
  0.0 1.9 %copy-start = (bf16[128,512]{1,0:T(8,128)(2,1)S(1)}, bf16[128,512]{1,0:T(8,128)(2,1)}, u32[]{:S(2)}) copy-start(bf16[128,512]{1,0:T(8,128)(2,1)} %param.21) | copy-start | bytes 393220
  0.0 1.7 %copy-start.1 = (bf16[3,48,128]{2,1,0:T(8,128)(2,1)S(1)}, bf16[3,48,128]{2,1,0:T(8,128)(2,1)}, u32[]{:S(2)}) copy-start(bf16[3,48,128]{2,1,0:T(8,128)(2,1)} %param.17) | copy-start | bytes 110596
  1.9 0.7 copy-start.8
  1.9 0.7 copy-start.9
  3.8 14.1 %all-to-all-start = ((bf16[16,2,576]{2,1,0:T(2,128)(2,1)}), bf16[16,2,576]{2,1,0:T(2,128)(2,1)S(1)}, u32[]{:S(2)}, u32[]{:S(2)}) async-start(bf16[16,2,576]{2,1,0:T(2,128)(2,1)} %reshape.123), calls=%async_computation | async-start | bytes 81920 | tf_op jit(solution)/shard_map/all_to_all | solution.py:66
  12.1 9.3 %copy-start.12 = (bf16[128,128]{1,0:T(8,128)(2,1)S(1)}, bf16[128,128]{1,0:T(8,128)(2,1)}, u32[]{:S(2)}) copy-start(bf16[128,128]{1,0:T(8,128)(2,1)} %param.22) | copy-start | bytes 98308
  17.9 10.2 %all-to-all-start.1 = ((bf16[16,2,576]{2,1,0:T(2,128)(2,1)}), bf16[16,2,576]{2,1,0:T(2,128)(2,1)S(1)}, u32[]{:S(2)}, u32[]{:S(2)}) async-start(bf16[16,2,576]{2,1,0:T(2,128)(2,1)} %reshape.121), calls=%async_computation.1 | async-start | bytes 81920 | tf_op jit(solution)/shard_map/all_to_all | solution.py:67
  29.3 3.6 %copy-start.14 = (s32[48]{0:T(128)S(1)}, s32[48]{0:T(128)}, u32[]{:S(2)}) copy-start(s32[48]{0:T(128)} %param.18) | copy-start | bytes 580
  29.3 10.3 %all-to-all-start.2 = ((bf16[16,2,576]{2,1,0:T(2,128)(2,1)}), bf16[16,2,576]{2,1,0:T(2,128)(2,1)S(1)}, u32[]{:S(2)}, u32[]{:S(2)}) async-start(bf16[16,2,576]{2,1,0:T(2,128)(2,1)} %reshape.125), calls=%async_computation.2 | async-start | bytes 81920 | tf_op jit(solution)/shard_map/all_to_all | solution.py:72
  39.7 0.8 copy-start.13
  39.8 0.7 copy-start.15
  39.8 0.7 copy-start.16
  41.1 0.7 copy-start.10
  41.1 0.7 copy-start.11
  41.9 0.7 copy-start.7
  42.7 25.3 %all-to-all-start.3 = ((bf16[3,48,128]{2,0,1:T(4,128)(2,1)}), bf16[3,48,128]{2,0,1:T(4,128)(2,1)S(1)}, u32[]{:S(2)}, u32[]{:S(2)}) async-start(bf16[3,48,128]{2,0,1:T(4,128)(2,1)} %copy.74), calls=%async_computation.3 | async-start | bytes 98304 | tf_op jit(solution)/shard_map/all_to_all | solution.py:89
  68.0 0.8 copy-start.4
  68.0 0.8 copy-start.5
  68.1 0.8 copy-start.2
  68.1 0.8 copy-start.3
  79.6 0.8 copy-start.6
where the time goes:
time: 81.8 us; the launch traced here: 81.1 us
  blocking collectives  31.1 us (38%)
  waiting for transfers between devices  18.6 us (23%)
  starting transfers between devices  18 us (22%)
  local copies, waits for them, and re-layouts  7.97 us (10%)
  matrix products  2.53 us (3%)
  other arithmetic  2.46 us (3%)
    all_gather x1, blocking collectives, per_device(): whole_bias = lax.all_gather(pair_bias, 'row', axis=1, tiled=True)  21.8 us
    all_to_all x1, blocking collectives, per_device(): lax.all_to_all(gated, 'row', split_axis=0, concat_axis=1, tiled=True)  9.34 us
    all_to_all x1, starting transfers between devices, per_device(): lax.all_to_all(left_edges, 'row', split_axis=0, concat_axis=1, tiled=True)  7.36 us
    all_to_all x1, waiting for transfers between devices, per_device(): lax.all_to_all(block_product, 'row', split_axis=1, concat_axis=0, tiled=T...  6.64 us
    unnamed x40, local copies, waits for them, and re-layouts  6.27 us
    all_to_all x1, waiting for transfers between devices, per_device(): lax.all_to_all(right_edges, 'row', split_axis=0, concat_axis=1, tiled=True)  6.18 us
    all_to_all x1, waiting for transfers between devices, per_device(): lax.all_to_all(left_edges, 'row', split_axis=0, concat_axis=1, tiled=True)  5.78 us
    all_to_all x1, starting transfers between devices, per_device(): lax.all_to_all(block_product, 'row', split_axis=1, concat_axis=0, tiled=T...  3.61 us
  transfers between devices with their start and end apart: 4, of which 3 were waited for; matrix products, arithmetic and copies ran while one was open for 2% of the time, Pallas kernels for 0%

commit v1 on v0

--- a/solution.py
+++ b/solution.py
@@ -1,8 +1,11 @@
+import functools
 import math
 
 import jax
 import jax.numpy as jnp
 from jax import lax
+from jax.experimental import pallas as pl
+from jax.experimental.pallas import tpu as pltpu
 from jax.sharding import PartitionSpec as P
 
 HEADS = 4
@@ -28,7 +31,7 @@
     return jnp.einsum("jhki,kjhd->ijhd", weights, value_cols, preferred_element_type=jnp.float32)
 
 
-def per_device(
+def split_over_devices(
     pair_rep,
     residue_valid,
     tri_norm_gain,
@@ -114,6 +117,197 @@
     return final.astype(jnp.bfloat16)
 
 
+def sigmoid(values):
+    return 0.5 * jnp.tanh(0.5 * values) + 0.5
+
+
+def dot(left, right):
+    return jnp.dot(left, right, preferred_element_type=jnp.float32)
+
+
+def whole_complex_kernel(
+    row_count,
+    pair_ref,
+    valid_scalars,
+    valid_ref,
+    tri_norm_gain,
+    tri_norm_bias,
+    w_edges,
+    w_tri_gate,
+    out_norm_gain,
+    out_norm_bias,
+    w_tri_out,
+    att_norm_gain,
+    att_norm_bias,
+    w_query,
+    w_key,
+    w_value,
+    w_att_gate,
+    w_pair_bias,
+    w_att_out,
+    out_ref,
+    normed_ref,
+    left_ref,
+    right_ref,
+    after_ref,
+    att_ref,
+    key_ref,
+    value_ref,
+    score_ref,
+    bias_ref,
+):
+    f32, bf16 = jnp.float32, jnp.bfloat16
+    res = pair_ref.shape[0]
+    channels = pair_ref.shape[2]
+    chunk = 4
+    height = chunk * res
+    own = lax.axis_index("row") * row_count
+
+    diagonal = lax.broadcasted_iota(jnp.int32, (res, res), 0) == lax.broadcasted_iota(
+        jnp.int32, (res, res), 1
+    )
+    spread_valid = jnp.where(diagonal, valid_ref[...].astype(f32), 0.0)
+    valid_column = jnp.broadcast_to(
+        jnp.sum(spread_valid, axis=1, keepdims=True), (res, channels)
+    )
+
+    def edges_of(step, carry):
+        first = step * chunk
+        start = pl.multiple_of(first * res, height)
+        pairs = pair_ref[pl.ds(first, chunk)].astype(f32).reshape(height, channels)
+        normed = layer_norm(pairs, tri_norm_gain[...], tri_norm_bias[...], 1).astype(bf16)
+        normed_ref[pl.ds(start, height), :] = normed
+        projected = dot(normed, w_edges[...])
+        pa, ga, pb, gb = (projected[:, e * channels : (e + 1) * channels] for e in range(4))
+        left = sigmoid(ga) * pa
+        right = sigmoid(gb) * pb
+        for r in range(chunk):
+            rows = slice(r * res, (r + 1) * res)
+            mask = valid_column * valid_scalars[first + r].astype(f32)
+            left_ref[pl.ds(start + r * res, res), :] = (left[rows] * mask).astype(bf16).astype(f32)
+            right_ref[pl.ds(first + r, res, stride=res), :] = (
+                (right[rows] * mask).astype(bf16).astype(f32)
+            )
+        return carry
+
+    lax.fori_loop(0, res // chunk, edges_of, 0)
+
+    key_value = jnp.concatenate([w_key[...], w_value[...]], axis=1)
+
+    def triangle_of(step, carry):
+        first = step * chunk
+        start = pl.multiple_of(first * res, height)
+        totals = [jnp.zeros((res, channels), f32) for _ in range(chunk)]
+        for k in range(res):
+            right = right_ref[pl.ds(k * res, res), :]
+            for r in range(chunk):
+                totals[r] = totals[r] + left_ref[pl.ds(start + r * res + k, 1), :] * right
+        triangle = jnp.concatenate(totals, axis=0).astype(bf16).astype(f32)
+        tri_normed = layer_norm(triangle, out_norm_gain[...], out_norm_bias[...], 1).astype(bf16)
+        gate = sigmoid(dot(normed_ref[pl.ds(start, height), :], w_tri_gate[...]))
+        pairs = pair_ref[pl.ds(first, chunk)].astype(f32).reshape(height, channels)
+        after_tri = pairs + gate * dot(tri_normed, w_tri_out[...])
+        after_ref[pl.ds(start, height), :] = after_tri
+        att_in = layer_norm(after_tri, att_norm_gain[...], att_norm_bias[...], 1).astype(bf16)
+        att_ref[pl.ds(start, height), :] = att_in.astype(f32)
+        joined = dot(att_in, key_value)
+        key_ref[pl.ds(start, height), :] = joined[:, :channels].astype(bf16).astype(f32)
+        value_ref[pl.ds(start, height), :] = joined[:, channels:].astype(bf16).astype(f32)
+        return carry
+
+    lax.fori_loop(0, res // chunk, triangle_of, 0)
+
+    factor = 1.0 / math.sqrt(HEAD_DIM)
+    head_of_row = lax.broadcasted_iota(jnp.int32, (2 * channels, channels), 0) % channels // HEAD_DIM
+    head_of_column = lax.broadcasted_iota(jnp.int32, (2 * channels, channels), 1) // HEAD_DIM
+    same_head = jnp.where(head_of_row == head_of_column, 1.0, 0.0).astype(bf16)
+    to_head = lax.broadcasted_iota(jnp.int32, (HEADS, channels), 0)
+    to_column = lax.broadcasted_iota(jnp.int32, (HEADS, channels), 1) // HEAD_DIM
+    repeat_head = jnp.where(to_head == to_column, 1.0, 0.0).astype(bf16)
+    wide_bias = dot(w_pair_bias[...], repeat_head).astype(bf16)
+
+    own_start = pl.multiple_of(own * res, res)
+    own_in = att_ref[pl.ds(own_start, row_count * res), :].astype(bf16)
+    query = dot(own_in, w_query[...]).astype(bf16).astype(f32)
+    att_gate = sigmoid(dot(own_in, w_att_gate[...]))
+    for r in range(row_count):
+        column = att_ref[pl.ds(own + r, res, stride=res), :].astype(bf16)
+        bias_ref[r * res : (r + 1) * res, :] = dot(column, wide_bias).astype(bf16).astype(f32)
+
+    def scores_of(step, maxima):
+        maxima = list(maxima)
+        for offset in range(chunk):
+            k = step * chunk + offset
+            key_mask = 1000000000.0 * (valid_scalars[k].astype(f32) - 1.0)
+            keys = key_ref[pl.ds(k * res, res), :]
+            for r in range(row_count):
+                product = query[r * res : (r + 1) * res] * keys
+                high = product.astype(bf16)
+                low = (product - high.astype(f32)).astype(bf16)
+                scores = dot(jnp.concatenate([high, low], axis=1), same_head) * factor
+                scores = scores + bias_ref[pl.ds(r * res + k, 1), :] + key_mask
+                score_ref[pl.ds((r * res + k) * res, res), :] = scores
+                maxima[r] = jnp.maximum(maxima[r], scores)
+        return tuple(maxima)
+
+    lowest = jnp.full((res, channels), -jnp.inf, f32)
+    maxima = lax.fori_loop(0, res // chunk, scores_of, (lowest,) * row_count)
+
+    zeros = jnp.zeros((res, channels), f32)
+    attended = []
+    for r in range(row_count):
+
+        def weigh(step, totals, r=r):
+            total, mixed = totals
+            for offset in range(chunk):
+                k = step * chunk + offset
+                weight = jnp.exp(score_ref[pl.ds((r * res + k) * res, res), :] - maxima[r])
+                total = total + weight
+                mixed = mixed + weight * value_ref[pl.ds(k * res, res), :]
+            return total, mixed
+
+        total, mixed = lax.fori_loop(0, res // chunk, weigh, (zeros, zeros))
+        attended.append(mixed / total)
+    gated = (jnp.concatenate(attended, axis=0) * att_gate).astype(bf16)
+    after_own = after_ref[pl.ds(own_start, row_count * res), :]
+    final = after_own + dot(gated, w_att_out[...])
+    out_ref[...] = final.astype(bf16).reshape(row_count, res, channels)
+
+
+def on_whole_complex(pair_rep, residue_valid, *parameters):
+    row_count, res, channels = pair_rep.shape
+    whole = lax.all_gather(pair_rep, "row", axis=0, tiled=True)
+    parameters = [p[None, :] if p.ndim == 1 else p for p in parameters]
+    in_vmem = pl.BlockSpec(memory_space=pltpu.VMEM)
+    in_smem = pl.BlockSpec(memory_space=pltpu.SMEM)
+    pairs = res * res
+    return pl.pallas_call(
+        functools.partial(whole_complex_kernel, row_count),
+        out_shape=jax.ShapeDtypeStruct((row_count, res, channels), jnp.bfloat16),
+        in_specs=[in_vmem, in_smem, in_vmem] + [in_vmem] * len(parameters),
+        out_specs=in_vmem,
+        scratch_shapes=[
+            pltpu.VMEM((pairs, channels), jnp.bfloat16),
+            pltpu.VMEM((pairs, channels), jnp.float32),
+            pltpu.VMEM((pairs, channels), jnp.float32),
+            pltpu.VMEM((pairs, channels), jnp.float32),
+            pltpu.VMEM((pairs, channels), jnp.float32),
+            pltpu.VMEM((pairs, channels), jnp.float32),
+            pltpu.VMEM((pairs, channels), jnp.float32),
+            pltpu.VMEM((row_count * pairs, channels), jnp.float32),
+            pltpu.VMEM((row_count * res, channels), jnp.float32),
+        ],
+        compiler_params=pltpu.CompilerParams(vmem_limit_bytes=40 * 1024 * 1024),
+    )(whole, residue_valid, residue_valid[None, :], *parameters)
+
+
+def per_device(pair_rep, residue_valid, *parameters):
+    row_count, res, channels = pair_rep.shape
+    if res % 16 == 0 and 40 * res * res * channels <= 32 * 1024 * 1024:
+        return on_whole_complex(pair_rep, residue_valid, *parameters)
+    return split_over_devices(pair_rep, residue_valid, *parameters)
+
+
 def solution(mesh):
     return jax.shard_map(
         per_device,

time: 81.8 us -> 47.7 us (0.58)
  Pallas kernels: 0 us -> 21.4 us
  waiting for transfers between devices: 18.6 us -> 0 us
  starting transfers between devices: 18 us -> 0 us
  local copies, waits for them, and re-layouts: 7.97 us -> 0.91 us
  blocking collectives: 31.1 us -> 25 us
  matrix products: 2.53 us -> 0 us
  other arithmetic: 2.46 us -> 0 us
    pallas_call x0 -> x1, Pallas kernels: none -> 21.4 us  [on_whole_complex(): pl.pallas_call(functools.partial(whole_complex_kernel, row_count), out_sh...]
    all_to_all x4 -> x0, waiting for transfers between devices: 18.6 us -> none  [the longest x1 6.64 us: per_device(): lax.all_to_all(block_product, 'row', split_axis=1, concat_axis=0, tiled=T...]
    all_to_all x4 -> x0, starting transfers between devices: 18 us -> none  [the longest x1 7.36 us: per_device(): lax.all_to_all(left_edges, 'row', split_axis=0, concat_axis=1, tiled=True)]
    all_to_all x1 -> x0, blocking collectives: 9.34 us -> none  [per_device(): lax.all_to_all(gated, 'row', split_axis=0, concat_axis=1, tiled=True)]
    unnamed x40 -> x33, local copies, waits for them, and re-layouts: 6.27 us -> 0.91 us
    all_gather x1, blocking collectives: 21.8 us -> 25 us  [on_whole_complex(): whole = lax.all_gather(pair_rep, 'row', axis=0, tiled=True)]
    dot_general x9 -> x0, matrix products: 2.53 us -> none  [the longest x1 0.78 us: per_device(): jnp.einsum('ije,ec->ijc', gated_rows, w_att_out, preferred_element_type=j...]
    reduce_sum x5 -> x0, other arithmetic: 1.28 us -> none  [the longest x2 0.9 us: layer_norm(): centre = values - jnp.mean(values, axis=along_axis, keepdims=True)]
  transfers between devices with their start and end apart: 4 -> 0, of which waited for: 3 -> 0; matrix products, arithmetic and copies ran while one was open for 2% -> 0% of each run, Pallas kernels for 0% -> 0%
where the time goes in v1:
time: 47.7 us; the launch traced here: 47.6 us
  blocking collectives  25 us (52%)
  Pallas kernels  21.4 us (45%)
  local copies, waits for them, and re-layouts  0.91 us (2%)
    all_gather x1, blocking collectives, on_whole_complex(): whole = lax.all_gather(pair_rep, 'row', axis=0, tiled=True)  25 us
    pallas_call x1, Pallas kernels, on_whole_complex(): pl.pallas_call(functools.partial(whole_complex_kernel, row_count), out_sh...  21.4 us

profile of v1, /device:TPU:0, one launch (start us, length us, event | category | flops | bytes accessed | tf_op | source)
XLA Modules:
  0.0 47.6 jit_solution(12396066175033137896)
XLA Ops:
  0.0 0.8 %copy.19.w_pair_bias = bf16[128,4]{1,0:T(8,128)(2,1)S(1)} copy(bf16[128,4]{0,1:T(4,128)(2,1)} %param.32) | data formatting | bytes 2048 | tf_op args[15]
  0.8 0.0 copy-done.15
  0.8 0.0 copy-start
  0.8 0.0 copy-start.1
  0.8 0.0 copy-start.2
  0.9 0.0 copy-start.3
  0.9 0.0 copy-start.4
  0.9 0.0 copy-start.5
  0.9 0.0 copy-start.6
  0.9 0.0 copy-start.7
  0.9 0.0 copy-start.8
  0.9 0.0 copy-start.9
  0.9 0.0 copy-start.10
  1.0 0.0 copy-start.11
  1.0 0.0 copy-start.12
  1.0 0.0 copy-start.13
  1.0 0.0 copy-start.14
  1.0 25.0 %all_gather.3.pair_ref = bf16[48,48,128]{2,1,0:T(8,128)(2,1)S(1)} all-gather(bf16[3,48,128]{2,1,0:T(8,128)(2,1)S(1)} %copy-done.15), channel_id=1, replica_groups=mesh['groups'=2,'row'=16] {'row'}, dimensions={0}, use_global_device_ids=true | all-gather | bytes 626688 | tf_op jit(solution)/shard_map/all_gather | solution.py:279
  26.0 0.0 copy-done
  26.0 0.0 copy-done.1
  26.0 0.0 copy-done.2
  26.0 0.0 copy-done.3
  26.0 0.0 copy-done.4
  26.1 21.4 %shard_map.163 = bf16[3,48,128]{2,1,0:T(8,128)(2,1)} custom-call(bf16[48,48,128]{2,1,0:T(8,128)(2,1)S(1)} %all_gather.3.pair_ref, s32[48]{0:T(128)S(1)} %copy-done.8, s32[1,48]{1,0:T(1,128)S(1)} %bitcast.7, f32[1,128]{1,0:T(1,128)S(1)} %bitcast.8, f32[1,128]{1,0:T(1,128)S(1)} %bitcast.9, bf16[128,512]{1,0:T(8,128)(2,1)S(1)} %copy-done, ...), custom_call_target="tpu_custom_call" | custom-call | tf_op jit(solution)/shard_map/pallas_call | solution.py:284
  (11 shorter events, 0.0 us)
Async XLA Ops:
  0.0 0.8 %copy-start.15 = (bf16[3,48,128]{2,1,0:T(8,128)(2,1)S(1)}, bf16[3,48,128]{2,1,0:T(8,128)(2,1)}, u32[]{:S(2)}) copy-start(bf16[3,48,128]{2,1,0:T(8,128)(2,1)} %param.17) | copy-start | bytes 110596
  0.8 25.2 %copy-start = (bf16[128,512]{1,0:T(8,128)(2,1)S(1)}, bf16[128,512]{1,0:T(8,128)(2,1)}, u32[]{:S(2)}) copy-start(bf16[128,512]{1,0:T(8,128)(2,1)} %w_edges.1) | copy-start | bytes 393220
  0.8 25.2 %copy-start.1 = (bf16[128,128]{1,0:T(8,128)(2,1)S(1)}, bf16[128,128]{1,0:T(8,128)(2,1)}, u32[]{:S(2)}) copy-start(bf16[128,128]{1,0:T(8,128)(2,1)} %w_tri_gate.1) | copy-start | bytes 98308
  0.8 25.1 %copy-start.2 = (bf16[128,128]{1,0:T(8,128)(2,1)S(1)}, bf16[128,128]{1,0:T(8,128)(2,1)}, u32[]{:S(2)}) copy-start(bf16[128,128]{1,0:T(8,128)(2,1)} %w_tri_out.1) | copy-start | bytes 98308
  0.9 25.1 %copy-start.3 = (bf16[128,128]{1,0:T(8,128)(2,1)S(1)}, bf16[128,128]{1,0:T(8,128)(2,1)}, u32[]{:S(2)}) copy-start(bf16[128,128]{1,0:T(8,128)(2,1)} %w_query.1) | copy-start | bytes 98308
  0.9 25.1 %copy-start.4 = (bf16[128,128]{1,0:T(8,128)(2,1)S(1)}, bf16[128,128]{1,0:T(8,128)(2,1)}, u32[]{:S(2)}) copy-start(bf16[128,128]{1,0:T(8,128)(2,1)} %w_key.1) | copy-start | bytes 98308
  0.9 25.1 %copy-start.5 = (bf16[128,128]{1,0:T(8,128)(2,1)S(1)}, bf16[128,128]{1,0:T(8,128)(2,1)}, u32[]{:S(2)}) copy-start(bf16[128,128]{1,0:T(8,128)(2,1)} %w_value.1) | copy-start | bytes 98308
  0.9 25.1 %copy-start.6 = (bf16[128,128]{1,0:T(8,128)(2,1)S(1)}, bf16[128,128]{1,0:T(8,128)(2,1)}, u32[]{:S(2)}) copy-start(bf16[128,128]{1,0:T(8,128)(2,1)} %w_att_gate.1) | copy-start | bytes 98308
  0.9 25.1 %copy-start.7 = (bf16[128,128]{1,0:T(8,128)(2,1)S(1)}, bf16[128,128]{1,0:T(8,128)(2,1)}, u32[]{:S(2)}) copy-start(bf16[128,128]{1,0:T(8,128)(2,1)} %w_att_out.1) | copy-start | bytes 98308
  0.9 25.1 %copy-start.8 = (s32[48]{0:T(128)S(1)}, s32[48]{0:T(128)}, u32[]{:S(2)}) copy-start(s32[48]{0:T(128)} %valid_scalars.1) | copy-start | bytes 580
  0.9 25.1 %copy-start.9 = (f32[128]{0:T(128)S(1)}, f32[128]{0:T(128)}, u32[]{:S(2)}) copy-start(f32[128]{0:T(128)} %param.19) | copy-start | bytes 1540
  0.9 25.1 %copy-start.10 = (f32[128]{0:T(128)S(1)}, f32[128]{0:T(128)}, u32[]{:S(2)}) copy-start(f32[128]{0:T(128)} %param.20) | copy-start | bytes 1540
  1.0 25.1 %copy-start.11 = (f32[128]{0:T(128)S(1)}, f32[128]{0:T(128)}, u32[]{:S(2)}) copy-start(f32[128]{0:T(128)} %param.23) | copy-start | bytes 1540
  1.0 25.1 %copy-start.12 = (f32[128]{0:T(128)S(1)}, f32[128]{0:T(128)}, u32[]{:S(2)}) copy-start(f32[128]{0:T(128)} %param.24) | copy-start | bytes 1540
  1.0 25.1 %copy-start.13 = (f32[128]{0:T(128)S(1)}, f32[128]{0:T(128)}, u32[]{:S(2)}) copy-start(f32[128]{0:T(128)} %param.26) | copy-start | bytes 1540
  1.0 25.1 %copy-start.14 = (f32[128]{0:T(128)S(1)}, f32[128]{0:T(128)}, u32[]{:S(2)}) copy-start(f32[128]{0:T(128)} %param.27) | copy-start | bytes 1540

commit v2 on v1

--- a/solution.py
+++ b/solution.py
@@ -125,9 +125,15 @@
     return jnp.dot(left, right, preferred_element_type=jnp.float32)
 
 
+def rounded(values):
+    return values.astype(jnp.bfloat16).astype(jnp.float32)
+
+
 def whole_complex_kernel(
     row_count,
-    pair_ref,
+    exchange_bits,
+    near_ref,
+    far_ref,
     valid_scalars,
     valid_ref,
     tri_norm_gain,
@@ -149,6 +155,8 @@
     normed_ref,
     left_ref,
     right_ref,
+    gate_ref,
+    triangle_ref,
     after_ref,
     att_ref,
     key_ref,
@@ -157,11 +165,10 @@
     bias_ref,
 ):
     f32, bf16 = jnp.float32, jnp.bfloat16
-    res = pair_ref.shape[0]
-    channels = pair_ref.shape[2]
-    chunk = 4
-    height = chunk * res
-    own = lax.axis_index("row") * row_count
+    res = near_ref.shape[1]
+    channels = near_ref.shape[2]
+    device = lax.axis_index("row")
+    own = device * row_count
 
     diagonal = lax.broadcasted_iota(jnp.int32, (res, res), 0) == lax.broadcasted_iota(
         jnp.int32, (res, res), 1
@@ -171,51 +178,93 @@
         jnp.sum(spread_valid, axis=1, keepdims=True), (res, channels)
     )
 
-    def edges_of(step, carry):
-        first = step * chunk
-        start = pl.multiple_of(first * res, height)
-        pairs = pair_ref[pl.ds(first, chunk)].astype(f32).reshape(height, channels)
-        normed = layer_norm(pairs, tri_norm_gain[...], tri_norm_bias[...], 1).astype(bf16)
-        normed_ref[pl.ds(start, height), :] = normed
-        projected = dot(normed, w_edges[...])
-        pa, ga, pb, gb = (projected[:, e * channels : (e + 1) * channels] for e in range(4))
-        left = sigmoid(ga) * pa
-        right = sigmoid(gb) * pb
-        for r in range(chunk):
-            rows = slice(r * res, (r + 1) * res)
-            mask = valid_column * valid_scalars[first + r].astype(f32)
-            left_ref[pl.ds(start + r * res, res), :] = (left[rows] * mask).astype(bf16).astype(f32)
-            right_ref[pl.ds(first + r, res, stride=res), :] = (
-                (right[rows] * mask).astype(bf16).astype(f32)
+    blocks = 2
+    block_height = row_count * res
+    height = blocks * block_height
+    edge_weights = jnp.concatenate([w_edges[...], w_tri_gate[...]], axis=1)
+
+    def first_row(position):
+        sender = device
+        for level, bit in enumerate(exchange_bits):
+            sender = jnp.bitwise_xor(sender, jnp.bitwise_and(position >> level, 1) * bit)
+        return sender * row_count
+
+    for part, pairs_ref in enumerate((near_ref, far_ref)):
+        steps = pairs_ref.shape[0] // (blocks * row_count)
+        position = part * steps * blocks
+
+        def norm_of(step, pairs_ref=pairs_ref, position=position):
+            pairs = pairs_ref[pl.ds(step * blocks * row_count, blocks * row_count)]
+            pairs = pairs.astype(f32).reshape(height, channels)
+            for b in range(blocks):
+                start = pl.multiple_of(first_row(position + step * blocks + b) * res, res)
+                after_ref[pl.ds(start, block_height), :] = pairs[
+                    b * block_height : (b + 1) * block_height
+                ]
+            return layer_norm(pairs, tri_norm_gain[...], tri_norm_bias[...], 1).astype(bf16)
+
+        def edges_of(step, carry, steps=steps, position=position, norm_of=norm_of):
+            normed = normed_ref[lax.rem(step, 2)]
+            later = norm_of(jnp.minimum(step + 1, steps - 1))
+            projected = dot(normed, edge_weights)
+            pa, ga, pb, gb, gt = (
+                projected[:, e * channels : (e + 1) * channels] for e in range(5)
             )
-        return carry
-
-    lax.fori_loop(0, res // chunk, edges_of, 0)
-
+            left = sigmoid(ga) * pa
+            right = sigmoid(gb) * pb
+            gate = sigmoid(gt)
+            for b in range(blocks):
+                first = first_row(position + step * blocks + b)
+                for r in range(row_count):
+                    i = first + r
+                    start = pl.multiple_of(i * res, res)
+                    rows = slice(b * block_height + r * res, b * block_height + (r + 1) * res)
+                    mask = valid_column * valid_scalars[i].astype(f32)
+                    left_ref[pl.ds(start, res), :] = rounded(left[rows] * mask)
+                    right_ref[pl.ds(i, res, stride=res), :] = rounded(right[rows] * mask)
+                    gate_ref[pl.ds(start, res), :] = gate[rows]
+            normed_ref[lax.rem(step + 1, 2)] = later
+            return carry
+
+        normed_ref[0] = norm_of(0)
+        lax.fori_loop(0, steps, edges_of, 0)
+
+    chunk = 6
+    while res % chunk:
+        chunk -= 1
+    tall = chunk * res
     key_value = jnp.concatenate([w_key[...], w_value[...]], axis=1)
 
-    def triangle_of(step, carry):
-        first = step * chunk
-        start = pl.multiple_of(first * res, height)
+    def triangle_of(step):
+        start = pl.multiple_of(step * tall, tall)
         totals = [jnp.zeros((res, channels), f32) for _ in range(chunk)]
         for k in range(res):
             right = right_ref[pl.ds(k * res, res), :]
             for r in range(chunk):
                 totals[r] = totals[r] + left_ref[pl.ds(start + r * res + k, 1), :] * right
-        triangle = jnp.concatenate(totals, axis=0).astype(bf16).astype(f32)
+        for r in range(chunk):
+            triangle_ref[lax.rem(step, 2), pl.ds(r * res, res), :] = rounded(totals[r])
+
+    def attention_inputs_of(step):
+        rows = pl.ds(pl.multiple_of(step * tall, tall), tall)
+        triangle = triangle_ref[lax.rem(step, 2)]
         tri_normed = layer_norm(triangle, out_norm_gain[...], out_norm_bias[...], 1).astype(bf16)
-        gate = sigmoid(dot(normed_ref[pl.ds(start, height), :], w_tri_gate[...]))
-        pairs = pair_ref[pl.ds(first, chunk)].astype(f32).reshape(height, channels)
-        after_tri = pairs + gate * dot(tri_normed, w_tri_out[...])
-        after_ref[pl.ds(start, height), :] = after_tri
+        after_tri = after_ref[rows, :] + gate_ref[rows, :] * dot(tri_normed, w_tri_out[...])
+        after_ref[rows, :] = after_tri
         att_in = layer_norm(after_tri, att_norm_gain[...], att_norm_bias[...], 1).astype(bf16)
-        att_ref[pl.ds(start, height), :] = att_in.astype(f32)
+        att_ref[rows, :] = att_in.astype(f32)
         joined = dot(att_in, key_value)
-        key_ref[pl.ds(start, height), :] = joined[:, :channels].astype(bf16).astype(f32)
-        value_ref[pl.ds(start, height), :] = joined[:, channels:].astype(bf16).astype(f32)
+        key_ref[rows, :] = rounded(joined[:, :channels])
+        value_ref[rows, :] = rounded(joined[:, channels:])
+
+    def both_of(step, carry):
+        attention_inputs_of(step - 1)
+        triangle_of(step)
         return carry
 
-    lax.fori_loop(0, res // chunk, triangle_of, 0)
+    triangle_of(0)
+    lax.fori_loop(1, res // chunk, both_of, 0)
+    attention_inputs_of(res // chunk - 1)
 
     factor = 1.0 / math.sqrt(HEAD_DIM)
     head_of_row = lax.broadcasted_iota(jnp.int32, (2 * channels, channels), 0) % channels // HEAD_DIM
@@ -227,17 +276,19 @@
     wide_bias = dot(w_pair_bias[...], repeat_head).astype(bf16)
 
     own_start = pl.multiple_of(own * res, res)
-    own_in = att_ref[pl.ds(own_start, row_count * res), :].astype(bf16)
-    query = dot(own_in, w_query[...]).astype(bf16).astype(f32)
+    own_in = att_ref[pl.ds(own_start, block_height), :].astype(bf16)
+    query = rounded(dot(own_in, w_query[...]))
     att_gate = sigmoid(dot(own_in, w_att_gate[...]))
     for r in range(row_count):
         column = att_ref[pl.ds(own + r, res, stride=res), :].astype(bf16)
-        bias_ref[r * res : (r + 1) * res, :] = dot(column, wide_bias).astype(bf16).astype(f32)
+        bias_ref[r * res : (r + 1) * res, :] = rounded(dot(column, wide_bias))
+
+    key_chunk = 8
 
     def scores_of(step, maxima):
         maxima = list(maxima)
-        for offset in range(chunk):
-            k = step * chunk + offset
+        for offset in range(key_chunk):
+            k = step * key_chunk + offset
             key_mask = 1000000000.0 * (valid_scalars[k].astype(f32) - 1.0)
             keys = key_ref[pl.ds(k * res, res), :]
             for r in range(row_count):
@@ -251,59 +302,72 @@
         return tuple(maxima)
 
     lowest = jnp.full((res, channels), -jnp.inf, f32)
-    maxima = lax.fori_loop(0, res // chunk, scores_of, (lowest,) * row_count)
+    maxima = lax.fori_loop(0, res // key_chunk, scores_of, (lowest,) * row_count)
 
     zeros = jnp.zeros((res, channels), f32)
+    weigh_chunk = 16
     attended = []
     for r in range(row_count):
 
         def weigh(step, totals, r=r):
             total, mixed = totals
-            for offset in range(chunk):
-                k = step * chunk + offset
+            for offset in range(weigh_chunk):
+                k = step * weigh_chunk + offset
                 weight = jnp.exp(score_ref[pl.ds((r * res + k) * res, res), :] - maxima[r])
                 total = total + weight
                 mixed = mixed + weight * value_ref[pl.ds(k * res, res), :]
             return total, mixed
 
-        total, mixed = lax.fori_loop(0, res // chunk, weigh, (zeros, zeros))
+        total, mixed = lax.fori_loop(0, res // weigh_chunk, weigh, (zeros, zeros))
         attended.append(mixed / total)
     gated = (jnp.concatenate(attended, axis=0) * att_gate).astype(bf16)
-    after_own = after_ref[pl.ds(own_start, row_count * res), :]
+    after_own = after_ref[pl.ds(own_start, block_height), :]
     final = after_own + dot(gated, w_att_out[...])
     out_ref[...] = final.astype(bf16).reshape(row_count, res, channels)
 
 
 def on_whole_complex(pair_rep, residue_valid, *parameters):
     row_count, res, channels = pair_rep.shape
-    whole = lax.all_gather(pair_rep, "row", axis=0, tiled=True)
+    devices = res // row_count
+    exchange_bits = []
+    while devices >> (len(exchange_bits) + 1):
+        exchange_bits.append(devices >> (len(exchange_bits) + 1))
+    near = pair_rep
+    for bit in exchange_bits:
+        far = lax.ppermute(near, "row", [(d, d ^ bit) for d in range(devices)])
+        if bit > 1:
+            near = jnp.concatenate([near, far], axis=0)
     parameters = [p[None, :] if p.ndim == 1 else p for p in parameters]
     in_vmem = pl.BlockSpec(memory_space=pltpu.VMEM)
     in_smem = pl.BlockSpec(memory_space=pltpu.SMEM)
     pairs = res * res
+    tall = pltpu.VMEM((pairs, channels), jnp.float32)
     return pl.pallas_call(
-        functools.partial(whole_complex_kernel, row_count),
+        functools.partial(whole_complex_kernel, row_count, tuple(exchange_bits)),
         out_shape=jax.ShapeDtypeStruct((row_count, res, channels), jnp.bfloat16),
-        in_specs=[in_vmem, in_smem, in_vmem] + [in_vmem] * len(parameters),
+        in_specs=[in_vmem, in_vmem, in_smem, in_vmem] + [in_vmem] * len(parameters),
         out_specs=in_vmem,
         scratch_shapes=[
-            pltpu.VMEM((pairs, channels), jnp.bfloat16),
-            pltpu.VMEM((pairs, channels), jnp.float32),
-            pltpu.VMEM((pairs, channels), jnp.float32),
-            pltpu.VMEM((pairs, channels), jnp.float32),
-            pltpu.VMEM((pairs, channels), jnp.float32),
-            pltpu.VMEM((pairs, channels), jnp.float32),
-            pltpu.VMEM((pairs, channels), jnp.float32),
+            pltpu.VMEM((2, 2 * row_count * res, channels), jnp.bfloat16),
+            tall,
+            tall,
+            tall,
+            pltpu.VMEM((2, 6 * res, channels), jnp.float32),
+            tall,
+            tall,
+            tall,
+            tall,
             pltpu.VMEM((row_count * pairs, channels), jnp.float32),
             pltpu.VMEM((row_count * res, channels), jnp.float32),
         ],
         compiler_params=pltpu.CompilerParams(vmem_limit_bytes=40 * 1024 * 1024),
-    )(whole, residue_valid, residue_valid[None, :], *parameters)
+    )(near, far, residue_valid, residue_valid[None, :], *parameters)
 
 
 def per_device(pair_rep, residue_valid, *parameters):
     row_count, res, channels = pair_rep.shape
-    if res % 16 == 0 and 40 * res * res * channels <= 32 * 1024 * 1024:
+    devices = res // row_count
+    if res % 48 == 0 and devices in (4, 8, 16) and 40 * res * res * channels <= 32 * 1024 * 1024:
         return on_whole_complex(pair_rep, residue_valid, *parameters)
     return split_over_devices(pair_rep, residue_valid, *parameters)
 

time: 47.7 us -> 35.6 us (0.75)
  blocking collectives: 25 us -> 0 us
  waiting for transfers between devices: 0 us -> 10.4 us
  starting transfers between devices: 0 us -> 7.26 us
  Pallas kernels: 21.4 us -> 16 us
  other arithmetic: 0 us -> 0.79 us
    all_gather x1 -> x0, blocking collectives: 25 us -> none  [on_whole_complex(): whole = lax.all_gather(pair_rep, 'row', axis=0, tiled=True)]
    ppermute x0 -> x4, waiting for transfers between devices: none -> 10.4 us  [on_whole_complex(): far = lax.ppermute(near, 'row', [(d, d ^ bit) for d in range(devices)])]
    ppermute x0 -> x4, starting transfers between devices: none -> 7.26 us  [on_whole_complex(): far = lax.ppermute(near, 'row', [(d, d ^ bit) for d in range(devices)])]
    pallas_call x1, Pallas kernels: 21.4 us -> 16 us  [on_whole_complex(): pl.pallas_call(functools.partial(whole_complex_kernel, row_count, tuple(e...]
    concatenate x0 -> x2, other arithmetic: none -> 0.79 us  [on_whole_complex(): near = jnp.concatenate([near, far], axis=0)]
  transfers between devices with their start and end apart: 0 -> 4, of which waited for: 0 -> 4; matrix products, arithmetic and copies ran while one was open for 0% -> 0% of each run, Pallas kernels for 0% -> 0%
where the time goes in v2:
time: 35.6 us; the launch traced here: 35.4 us
  Pallas kernels  16 us (45%)
  waiting for transfers between devices  10.4 us (29%)
  starting transfers between devices  7.26 us (20%)
  local copies, waits for them, and re-layouts  0.87 us (2%)
  other arithmetic  0.79 us (2%)
    pallas_call x1, Pallas kernels, on_whole_complex(): pl.pallas_call(functools.partial(whole_complex_kernel, row_count, tuple(e...  16 us
    ppermute x4, waiting for transfers between devices, on_whole_complex(): far = lax.ppermute(near, 'row', [(d, d ^ bit) for d in range(devices)])  10.4 us
    ppermute x4, starting transfers between devices, on_whole_complex(): far = lax.ppermute(near, 'row', [(d, d ^ bit) for d in range(devices)])  7.26 us
    unnamed x38, local copies, waits for them, and re-layouts  0.85 us
    concatenate x2, other arithmetic, on_whole_complex(): near = jnp.concatenate([near, far], axis=0)  0.79 us
  transfers between devices with their start and end apart: 4, of which 4 were waited for; matrix products, arithmetic and copies ran while one was open for 0% of the time, Pallas kernels for 0%

profile of v2, /device:TPU:0, one launch (start us, length us, event | category | flops | bytes accessed | tf_op | source)
XLA Modules:
  0.0 35.4 jit_solution(16034559487113265135)
XLA Ops:
  0.0 4.0 %collective-permute-start = (bf16[3,48,128]{2,1,0:T(8,128)(2,1)}, bf16[3,48,128]{2,1,0:T(8,128)(2,1)S(1)}, u32[]{:S(2)}, u32[]{:S(2)}) collective-permute-start(bf16[3,48,128]{2,1,0:T(8,128)(2,1)} %param.17), channel_id=1, source_target_pairs={{0,8},{1,9},{2,10},{3,11},{4,12},{5,13},{6,14},{7,15},{8,0},{9,1},... | collective-permute-start | bytes 110600 | tf_op jit(solution)/shard_map/ppermute | solution.py:337
  4.0 2.6 %collective-permute-done = bf16[3,48,128]{2,1,0:T(8,128)(2,1)S(1)} collective-permute-done((bf16[3,48,128]{2,1,0:T(8,128)(2,1)}, bf16[3,48,128]{2,1,0:T(8,128)(2,1)S(1)}, u32[]{:S(2)}, u32[]{:S(2)}) %collective-permute-start) | collective-permute-done | bytes 36896 | tf_op jit(solution)/shard_map/ppermute | solution.py:337
  6.7 0.8 %pad_maximum_fusion.1 = bf16[6,48,128]{2,1,0:T(8,128)(2,1)S(1)} fusion(bf16[3,48,128]{2,1,0:T(8,128)(2,1)S(1)} %collective-permute-done, bf16[3,48,128]{2,1,0:T(8,128)(2,1)} %param.17), kind=kLoop, calls=%fused_computation.1 | loop fusion | flops 36864 | bytes 147456 | tf_op jit(solution)/shard_map/concatenate | solution.py:339
  7.4 1.4 %collective-permute-start.1 = (bf16[6,48,128]{2,1,0:T(8,128)(2,1)S(1)}, bf16[6,48,128]{2,1,0:T(8,128)(2,1)S(1)}, u32[]{:S(2)}, u32[]{:S(2)}) collective-permute-start(bf16[6,48,128]{2,1,0:T(8,128)(2,1)S(1)} %pad_maximum_fusion.1), channel_id=1, source_target_pairs={{0,4},{1,5},{2,6},{3,7},{4,0},{5,1},{6,2},{7,3},{8,12},{9,13},{10,... | collective-permute-start | bytes 221192 | tf_op jit(solution)/shard_map/ppermute | solution.py:337
  8.9 2.9 %collective-permute-done.1 = bf16[6,48,128]{2,1,0:T(8,128)(2,1)S(1)} collective-permute-done((bf16[6,48,128]{2,1,0:T(8,128)(2,1)S(1)}, bf16[6,48,128]{2,1,0:T(8,128)(2,1)S(1)}, u32[]{:S(2)}, u32[]{:S(2)}) %collective-permute-start.1) | collective-permute-done | bytes 73760 | tf_op jit(solution)/shard_map/ppermute | solution.py:337
  11.8 1.7 %collective-permute-start.2 = (bf16[12,48,128]{2,1,0:T(8,128)(2,1)S(1)}, bf16[12,48,128]{2,1,0:T(8,128)(2,1)S(1)}, u32[]{:S(2)}, u32[]{:S(2)}) collective-permute-start(bf16[12,48,128]{2,1,0:T(8,128)(2,1)S(1)} %pad_maximum_fusion), channel_id=1, source_target_pairs={{0,2},{1,3},{2,0},{3,1},{4,6},{5,7},{6,4},{7,5},{8,10},{9,11},{10,... | collective-permute-start | bytes 442376 | tf_op jit(solution)/shard_map/ppermute | solution.py:337
  13.6 0.0 copy-start.16
  13.6 0.0 copy-start
  13.6 3.4 %collective-permute-done.2 = bf16[12,48,128]{2,1,0:T(8,128)(2,1)S(1)} collective-permute-done((bf16[12,48,128]{2,1,0:T(8,128)(2,1)S(1)}, bf16[12,48,128]{2,1,0:T(8,128)(2,1)S(1)}, u32[]{:S(2)}, u32[]{:S(2)}) %collective-permute-start.2) | collective-permute-done | bytes 147488 | tf_op jit(solution)/shard_map/ppermute | solution.py:337
  17.0 0.0 copy-start.6
  17.1 0.0 copy-start.1
  17.1 0.1 collective-permute-start.3
  17.2 0.1 copy.18.w_pair_bias
  17.3 1.4 %collective-permute-done.3.far_ref = bf16[24,48,128]{2,1,0:T(8,128)(2,1)S(1)} collective-permute-done((bf16[24,48,128]{2,1,0:T(8,128)(2,1)S(1)}, bf16[24,48,128]{2,1,0:T(8,128)(2,1)S(1)}, u32[]{:S(2)}, u32[]{:S(2)}) %collective-permute-start.3) | collective-permute-done | bytes 294944 | tf_op jit(solution)/shard_map/ppermute | solution.py:337
  18.7 0.0 copy-start.8
  18.8 0.0 copy-start.10
  18.9 0.5 %copy-done.11 = f32[128]{0:T(128)S(1)} copy-done((f32[128]{0:T(128)S(1)}, f32[128]{0:T(128)}, u32[]{:S(2)}) %copy-start.11) | copy-done | bytes 536
  19.4 0.0 copy-done.12
  19.4 0.0 copy-done.13
  19.4 0.0 copy-done.14
  19.4 0.0 copy-done.8
  19.4 0.0 copy-done.9
  19.5 0.0 copy-done.10
  19.5 16.0 %shard_map.163 = bf16[3,48,128]{2,1,0:T(8,128)(2,1)} custom-call(bf16[24,48,128]{2,1,0:T(8,128)(2,1)S(1)} %constant_dynamic-update-slice_fusion.near_ref, bf16[24,48,128]{2,1,0:T(8,128)(2,1)S(1)} %collective-permute-done.3.far_ref, s32[48]{0:T(128)S(1)} %copy-done.8, s32[1,48]{1,0:T(1,128)S(1)} %bitcast.7, f32[1,128]{1,0:T(1,128)S(1)} %bitcast.8, ...), custom_call_target="tpu_custom_call" | custom-call | tf_op jit(solution)/shard_map/pallas_call | solution.py:345
  (26 shorter events, 0.1 us)
Async XLA Ops:
  0.0 8.9 %copy-start.15 = (bf16[3,48,128]{2,1,0:T(8,128)(2,1)S(1)}, bf16[3,48,128]{2,1,0:T(8,128)(2,1)}, u32[]{:S(2)}) copy-start(bf16[3,48,128]{2,1,0:T(8,128)(2,1)} %param.17) | copy-start | bytes 110596
  0.0 6.6 %collective-permute-start = (bf16[3,48,128]{2,1,0:T(8,128)(2,1)}, bf16[3,48,128]{2,1,0:T(8,128)(2,1)S(1)}, u32[]{:S(2)}, u32[]{:S(2)}) collective-permute-start(bf16[3,48,128]{2,1,0:T(8,128)(2,1)} %param.17), channel_id=1, source_target_pairs={{0,8},{1,9},{2,10},{3,11},{4,12},{5,13},{6,14},{7,15},{8,0},{9,1},... | collective-permute-start | bytes 110600 | tf_op jit(solution)/shard_map/ppermute | solution.py:337
  7.4 4.4 %collective-permute-start.1 = (bf16[6,48,128]{2,1,0:T(8,128)(2,1)S(1)}, bf16[6,48,128]{2,1,0:T(8,128)(2,1)S(1)}, u32[]{:S(2)}, u32[]{:S(2)}) collective-permute-start(bf16[6,48,128]{2,1,0:T(8,128)(2,1)S(1)} %pad_maximum_fusion.1), channel_id=1, source_target_pairs={{0,4},{1,5},{2,6},{3,7},{4,0},{5,1},{6,2},{7,3},{8,12},{9,13},{10,... | collective-permute-start | bytes 221192 | tf_op jit(solution)/shard_map/ppermute | solution.py:337
  11.8 5.2 %collective-permute-start.2 = (bf16[12,48,128]{2,1,0:T(8,128)(2,1)S(1)}, bf16[12,48,128]{2,1,0:T(8,128)(2,1)S(1)}, u32[]{:S(2)}, u32[]{:S(2)}) collective-permute-start(bf16[12,48,128]{2,1,0:T(8,128)(2,1)S(1)} %pad_maximum_fusion), channel_id=1, source_target_pairs={{0,2},{1,3},{2,0},{3,1},{4,6},{5,7},{6,4},{7,5},{8,10},{9,11},{10,... | collective-permute-start | bytes 442376 | tf_op jit(solution)/shard_map/ppermute | solution.py:337
  13.5 5.2 %copy-start.7 = (bf16[128,128]{1,0:T(8,128)(2,1)S(1)}, bf16[128,128]{1,0:T(8,128)(2,1)}, u32[]{:S(2)}) copy-start(bf16[128,128]{1,0:T(8,128)(2,1)} %w_att_out.1) | copy-start | bytes 98308
  13.6 3.6 %copy-start.16 = (bf16[128,4]{0,1:T(4,128)(2,1)S(1)}, bf16[128,4]{0,1:T(4,128)(2,1)}, u32[]{:S(2)}) copy-start(bf16[128,4]{0,1:T(4,128)(2,1)} %param.32) | copy-start | bytes 3076
  13.6 5.2 %copy-start = (bf16[128,512]{1,0:T(8,128)(2,1)S(1)}, bf16[128,512]{1,0:T(8,128)(2,1)}, u32[]{:S(2)}) copy-start(bf16[128,512]{1,0:T(8,128)(2,1)} %w_edges.1) | copy-start | bytes 393220
  17.0 1.8 %copy-start.2 = (bf16[128,128]{1,0:T(8,128)(2,1)S(1)}, bf16[128,128]{1,0:T(8,128)(2,1)}, u32[]{:S(2)}) copy-start(bf16[128,128]{1,0:T(8,128)(2,1)} %w_tri_out.1) | copy-start | bytes 98308
  17.0 1.8 %copy-start.3 = (bf16[128,128]{1,0:T(8,128)(2,1)S(1)}, bf16[128,128]{1,0:T(8,128)(2,1)}, u32[]{:S(2)}) copy-start(bf16[128,128]{1,0:T(8,128)(2,1)} %w_query.1) | copy-start | bytes 98308
  17.0 1.8 %copy-start.4 = (bf16[128,128]{1,0:T(8,128)(2,1)S(1)}, bf16[128,128]{1,0:T(8,128)(2,1)}, u32[]{:S(2)}) copy-start(bf16[128,128]{1,0:T(8,128)(2,1)} %w_key.1) | copy-start | bytes 98308
  17.0 1.8 %copy-start.5 = (bf16[128,128]{1,0:T(8,128)(2,1)S(1)}, bf16[128,128]{1,0:T(8,128)(2,1)}, u32[]{:S(2)}) copy-start(bf16[128,128]{1,0:T(8,128)(2,1)} %w_value.1) | copy-start | bytes 98308
  17.0 1.8 %copy-start.6 = (bf16[128,128]{1,0:T(8,128)(2,1)S(1)}, bf16[128,128]{1,0:T(8,128)(2,1)}, u32[]{:S(2)}) copy-start(bf16[128,128]{1,0:T(8,128)(2,1)} %w_att_gate.1) | copy-start | bytes 98308
  17.1 1.8 %copy-start.1 = (bf16[128,128]{1,0:T(8,128)(2,1)S(1)}, bf16[128,128]{1,0:T(8,128)(2,1)}, u32[]{:S(2)}) copy-start(bf16[128,128]{1,0:T(8,128)(2,1)} %w_tri_gate.1) | copy-start | bytes 98308
  17.1 1.6 %collective-permute-start.3 = (bf16[24,48,128]{2,1,0:T(8,128)(2,1)S(1)}, bf16[24,48,128]{2,1,0:T(8,128)(2,1)S(1)}, u32[]{:S(2)}, u32[]{:S(2)}) collective-permute-start(bf16[24,48,128]{2,1,0:T(8,128)(2,1)S(1)} %constant_dynamic-update-slice_fusion.near_ref), channel_id=1, source_target_pairs={{0,1},{1,0},{2,3},{3,2},{4,5},{5,4},{6,7},{7,6},{8,9},{9,8},{10,11... | collective-permute-start | bytes 884744 | tf_op jit(solution)/shard_map/ppermute | solution.py:337
  18.7 0.7 %copy-start.11 = (f32[128]{0:T(128)S(1)}, f32[128]{0:T(128)}, u32[]{:S(2)}) copy-start(f32[128]{0:T(128)} %param.23) | copy-start | bytes 1540
  18.7 0.7 %copy-start.12 = (f32[128]{0:T(128)S(1)}, f32[128]{0:T(128)}, u32[]{:S(2)}) copy-start(f32[128]{0:T(128)} %param.24) | copy-start | bytes 1540
  18.7 0.7 %copy-start.13 = (f32[128]{0:T(128)S(1)}, f32[128]{0:T(128)}, u32[]{:S(2)}) copy-start(f32[128]{0:T(128)} %param.26) | copy-start | bytes 1540
  18.7 0.7 %copy-start.14 = (f32[128]{0:T(128)S(1)}, f32[128]{0:T(128)}, u32[]{:S(2)}) copy-start(f32[128]{0:T(128)} %param.27) | copy-start | bytes 1540
  18.7 0.7 %copy-start.8 = (s32[48]{0:T(128)S(1)}, s32[48]{0:T(128)}, u32[]{:S(2)}) copy-start(s32[48]{0:T(128)} %valid_scalars.1) | copy-start | bytes 580
  18.7 0.7 %copy-start.9 = (f32[128]{0:T(128)S(1)}, f32[128]{0:T(128)}, u32[]{:S(2)}) copy-start(f32[128]{0:T(128)} %param.19) | copy-start | bytes 1540
  18.8 0.7 %copy-start.10 = (f32[128]{0:T(128)S(1)}, f32[128]{0:T(128)}, u32[]{:S(2)}) copy-start(f32[128]{0:T(128)} %param.20) | copy-start | bytes 1540

commit v3 on v0

--- a/solution.py
+++ b/solution.py
@@ -1,8 +1,11 @@
+import functools
 import math
 
 import jax
 import jax.numpy as jnp
 from jax import lax
+from jax.experimental import pallas as pl
+from jax.experimental.pallas import tpu as pltpu
 from jax.sharding import PartitionSpec as P
 
 HEADS = 4
@@ -28,7 +31,7 @@
     return jnp.einsum("jhki,kjhd->ijhd", weights, value_cols, preferred_element_type=jnp.float32)
 
 
-def per_device(
+def split_over_devices(
     pair_rep,
     residue_valid,
     tri_norm_gain,
@@ -114,6 +117,321 @@
     return final.astype(jnp.bfloat16)
 
 
+def sigmoid(values):
+    return 0.5 * jnp.tanh(0.5 * values) + 0.5
+
+
+def dot(left, right):
+    return jnp.dot(left, right, preferred_element_type=jnp.float32)
+
+
+def rounded(values):
+    return values.astype(jnp.bfloat16).astype(jnp.float32)
+
+
+def head_repeat(rows, row_of_head):
+    head = lax.broadcasted_iota(jnp.int32, (rows, HEADS * HEAD_DIM), 0)
+    column = lax.broadcasted_iota(jnp.int32, (rows, HEADS * HEAD_DIM), 1)
+    return jnp.where(row_of_head(head) == column // HEAD_DIM, 1.0, 0.0).astype(jnp.bfloat16)
+
+
+def prepare_kernel(
+    pair_ref,
+    valid_ref,
+    tri_norm_gain,
+    tri_norm_bias,
+    w_edges,
+    w_tri_gate,
+    out_norm_gain,
+    out_norm_bias,
+    w_tri_out,
+    att_norm_gain,
+    att_norm_bias,
+    w_query,
+    w_key,
+    w_value,
+    w_att_gate,
+    w_pair_bias,
+    w_att_out,
+    own_ref,
+    valid_column_ref,
+    norms_ref,
+    edge_weights_ref,
+    square_weights_ref,
+):
+    res = pair_ref.shape[1]
+    channels = pair_ref.shape[2]
+    own_ref[...] = pair_ref[...]
+    diagonal = lax.broadcasted_iota(jnp.int32, (res, res), 0) == lax.broadcasted_iota(
+        jnp.int32, (res, res), 1
+    )
+    spread_valid = jnp.where(diagonal, valid_ref[...].astype(jnp.float32), 0.0)
+    valid_column_ref[...] = jnp.broadcast_to(
+        jnp.sum(spread_valid, axis=1, keepdims=True), (res, channels)
+    )
+    vectors = (
+        tri_norm_gain,
+        tri_norm_bias,
+        out_norm_gain,
+        out_norm_bias,
+        att_norm_gain,
+        att_norm_bias,
+    )
+    for row, vector in enumerate(vectors):
+        norms_ref[row : row + 1, :] = vector[...]
+    edge_weights_ref[:, : 4 * channels] = w_edges[...]
+    edge_weights_ref[:, 4 * channels :] = w_tri_gate[...]
+    wide_bias = dot(w_pair_bias[...], head_repeat(HEADS, lambda head: head))
+    squares = (w_tri_out, w_key, w_value, w_query, w_att_gate, w_att_out)
+    for column, square in enumerate(squares):
+        square_weights_ref[:, column * channels : (column + 1) * channels] = square[...]
+    square_weights_ref[:, len(squares) * channels :] = wide_bias.astype(jnp.bfloat16)
+
+
+def edges_kernel(
+    row_count,
+    senders,
+    valid_scalars,
+    pairs_ref,
+    valid_column,
+    norms,
+    edge_weights,
+    *refs,
+):
+    left_ref, right_ref, gate_ref, after_ref = refs[-4:]
+    f32, bf16 = jnp.float32, jnp.bfloat16
+    res = pairs_ref.shape[1]
+    channels = pairs_ref.shape[2]
+    device = lax.axis_index("row")
+    for block, bits in enumerate(senders):
+        first = jnp.bitwise_xor(device, bits) * row_count
+        pairs = pairs_ref[block * row_count : (block + 1) * row_count].astype(f32)
+        pairs = pairs.reshape(row_count * res, channels)
+        start = pl.multiple_of(first * res, res)
+        after_ref[pl.ds(start, row_count * res), :] = pairs
+        normed = layer_norm(pairs, norms[0:1, :], norms[1:2, :], 1).astype(bf16)
+        projected = dot(normed, edge_weights[...])
+        pa, ga, pb, gb, gt = (projected[:, e * channels : (e + 1) * channels] for e in range(5))
+        left = sigmoid(ga) * pa
+        right = sigmoid(gb) * pb
+        gate_ref[pl.ds(start, row_count * res), :] = sigmoid(gt)
+        for r in range(row_count):
+            i = first + r
+            rows = slice(r * res, (r + 1) * res)
+            mask = valid_column[...] * valid_scalars[i].astype(f32)
+            left_ref[pl.ds(pl.multiple_of(i * res, res), res), :] = rounded(left[rows] * mask)
+            right_ref[pl.ds(i, res, stride=res), :] = rounded(right[rows] * mask)
+
+
+def triangle_kernel(
+    res,
+    chunk,
+    norms,
+    square_weights,
+    left_ref,
+    right_ref,
+    gate_ref,
+    pairs_ref,
+    after_ref,
+    att_ref,
+    key_ref,
+    value_ref,
+    triangle_ref,
+):
+    f32, bf16 = jnp.float32, jnp.bfloat16
+    channels = left_ref.shape[1]
+    tall = chunk * res
+
+    def triangle_of(step):
+        start = pl.multiple_of(step * tall, tall)
+        totals = [jnp.zeros((res, channels), f32) for _ in range(chunk)]
+        for k in range(res):
+            right = right_ref[pl.ds(k * res, res), :]
+            for r in range(chunk):
+                totals[r] = totals[r] + left_ref[pl.ds(start + r * res + k, 1), :] * right
+        for r in range(chunk):
+            triangle_ref[lax.rem(step, 2), pl.ds(r * res, res), :] = rounded(totals[r])
+
+    def attention_inputs_of(step):
+        rows = pl.ds(pl.multiple_of(step * tall, tall), tall)
+        triangle = triangle_ref[lax.rem(step, 2)]
+        tri_normed = layer_norm(triangle, norms[2:3, :], norms[3:4, :], 1).astype(bf16)
+        update = dot(tri_normed, square_weights[:, :channels])
+        after_tri = pairs_ref[rows, :] + gate_ref[rows, :] * update
+        after_ref[rows, :] = after_tri
+        att_in = layer_norm(after_tri, norms[4:5, :], norms[5:6, :], 1).astype(bf16)
+        att_ref[rows, :] = att_in.astype(f32)
+        joined = dot(att_in, square_weights[:, channels : 3 * channels])
+        key_ref[rows, :] = rounded(joined[:, :channels])
+        value_ref[rows, :] = rounded(joined[:, channels:])
+
+    def both_of(step, carry):
+        attention_inputs_of(step - 1)
+        triangle_of(step)
+        return carry
+
+    triangle_of(0)
+    lax.fori_loop(1, res // chunk, both_of, 0)
+    attention_inputs_of(res // chunk - 1)
+
+
+def attention_kernel(
+    row_count,
+    res,
+    key_chunk,
+    weigh_chunk,
+    valid_scalars,
+    square_weights,
+    after_ref,
+    att_ref,
+    key_ref,
+    value_ref,
+    out_ref,
+    score_ref,
+    bias_ref,
+):
+    f32, bf16 = jnp.float32, jnp.bfloat16
+    channels = key_ref.shape[1]
+    own = lax.axis_index("row") * row_count
+    own_start = pl.multiple_of(own * res, res)
+    own_in = att_ref[pl.ds(own_start, row_count * res), :].astype(bf16)
+    joined = dot(own_in, square_weights[:, 3 * channels : 5 * channels])
+    query = rounded(joined[:, :channels])
+    att_gate = sigmoid(joined[:, channels:])
+    wide_bias = square_weights[:, 6 * channels :]
+    for r in range(row_count):
+        column = att_ref[pl.ds(own + r, res, stride=res), :].astype(bf16)
+        bias_ref[r * res : (r + 1) * res, :] = rounded(dot(column, wide_bias))
+
+    factor = 1.0 / math.sqrt(HEAD_DIM)
+    same_head = head_repeat(2 * channels, lambda row: row % channels // HEAD_DIM)
+
+    def scores_of(step, maxima):
+        maxima = list(maxima)
+        for offset in range(key_chunk):
+            k = step * key_chunk + offset
+            key_mask = 1000000000.0 * (valid_scalars[k].astype(f32) - 1.0)
+            keys = key_ref[pl.ds(k * res, res), :]
+            for r in range(row_count):
+                product = query[r * res : (r + 1) * res] * keys
+                high = product.astype(bf16)
+                low = (product - high.astype(f32)).astype(bf16)
+                scores = dot(jnp.concatenate([high, low], axis=1), same_head) * factor
+                scores = scores + bias_ref[pl.ds(r * res + k, 1), :] + key_mask
+                score_ref[pl.ds((r * res + k) * res, res), :] = scores
+                maxima[r] = jnp.maximum(maxima[r], scores)
+        return tuple(maxima)
+
+    lowest = jnp.full((res, channels), -jnp.inf, f32)
+    maxima = lax.fori_loop(0, res // key_chunk, scores_of, (lowest,) * row_count)
+
+    zeros = jnp.zeros((res, channels), f32)
+    attended = []
+    for r in range(row_count):
+
+        def weigh(step, totals, r=r):
+            total, mixed = totals
+            for offset in range(weigh_chunk):
+                k = step * weigh_chunk + offset
+                weight = jnp.exp(score_ref[pl.ds((r * res + k) * res, res), :] - maxima[r])
+                total = total + weight
+                mixed = mixed + weight * value_ref[pl.ds(k * res, res), :]
+            return total, mixed
+
+        total, mixed = lax.fori_loop(0, res // weigh_chunk, weigh, (zeros, zeros))
+        attended.append(mixed / total)
+    gated = (jnp.concatenate(attended, axis=0) * att_gate).astype(bf16)
+    after_own = after_ref[pl.ds(own_start, row_count * res), :]
+    final = after_own + dot(gated, square_weights[:, 5 * channels : 6 * channels])
+    out_ref[...] = final.astype(bf16).reshape(row_count, res, channels)
+
+
+def on_whole_complex(pair_rep, residue_valid, *parameters):
+    row_count, res, channels = pair_rep.shape
+    devices = res // row_count
+    f32, bf16 = jnp.float32, jnp.bfloat16
+    in_vmem = pl.BlockSpec(memory_space=pltpu.VMEM)
+    in_smem = pl.BlockSpec(memory_space=pltpu.SMEM)
+    compiler_params = pltpu.CompilerParams(vmem_limit_bytes=24 * 1024 * 1024)
+    tall = jax.ShapeDtypeStruct((res * res, channels), f32)
+
+    def exchange(values, bit):
+        return lax.ppermute(values, "row", [(d, d ^ bit) for d in range(devices)])
+
+    parameters = [p[None, :] if p.ndim == 1 else p for p in parameters]
+    own, valid_column, norms, edge_weights, square_weights = pl.pallas_call(
+        prepare_kernel,
+        out_shape=(
+            jax.ShapeDtypeStruct(pair_rep.shape, bf16),
+            jax.ShapeDtypeStruct((res, channels), f32),
+            jax.ShapeDtypeStruct((8, channels), f32),
+            jax.ShapeDtypeStruct((channels, 5 * channels), bf16),
+            jax.ShapeDtypeStruct((channels, 7 * channels), bf16),
+        ),
+        in_specs=[in_vmem] * (2 + len(parameters)),
+        out_specs=(in_vmem,) * 5,
+        compiler_params=compiler_params,
+    )(pair_rep, residue_valid[None, :], *parameters)
+
+    def edges_of(pairs, senders, edges):
+        return pl.pallas_call(
+            functools.partial(edges_kernel, row_count, senders),
+            out_shape=(tall,) * 4,
+            in_specs=[in_smem] + [in_vmem] * (4 + len(edges)),
+            out_specs=(in_vmem,) * 4,
+            input_output_aliases={5 + e: e for e in range(len(edges))},
+            compiler_params=compiler_params,
+            cost_estimate=pl.CostEstimate(
+                flops=10 * pairs.size * channels, bytes_accessed=6 * 1024 * 1024, transcendentals=0
+            ),
+        )(residue_valid, pairs, valid_column, norms, edge_weights, *edges)
+
+    senders = (0,)
+    quarter = pair_rep
+    bit = devices // 2
+    while bit > 2:
+        kept = own if bit == devices // 2 else quarter
+        quarter = jnp.concatenate([kept, exchange(quarter, bit)], axis=0)
+        senders = senders + tuple(s ^ bit for s in senders)
+        bit //= 2
+    beside = exchange(quarter, 2)
+    across = exchange(quarter, 1)
+    edges = edges_of(quarter, senders, ())
+    edges = edges_of(across, tuple(s ^ 1 for s in senders), edges)
+    corner = exchange(beside, 1)
+    edges = edges_of(beside, tuple(s ^ 2 for s in senders), edges)
+    edges = edges_of(corner, tuple(s ^ 3 for s in senders), edges)
+
+    chunk = 6
+    after_tri, att_in, keys, values = pl.pallas_call(
+        functools.partial(triangle_kernel, res, chunk),
+        out_shape=(tall,) * 4,
+        in_specs=[in_vmem] * 6,
+        out_specs=(in_vmem,) * 4,
+        scratch_shapes=[pltpu.VMEM((2, chunk * res, channels), f32)],
+        compiler_params=compiler_params,
+    )(norms, square_weights, *edges)
+    return pl.pallas_call(
+        functools.partial(attention_kernel, row_count, res, 8, 16),
+        out_shape=jax.ShapeDtypeStruct(pair_rep.shape, bf16),
+        in_specs=[in_smem] + [in_vmem] * 5,
+        out_specs=in_vmem,
+        scratch_shapes=[
+            pltpu.VMEM((row_count * res * res, channels), f32),
+            pltpu.VMEM((row_count * res, channels), f32),
+        ],
+        compiler_params=compiler_params,
+    )(residue_valid, square_weights, after_tri, att_in, keys, values)
+
+
+def per_device(pair_rep, residue_valid, *parameters):
+    row_count, res, channels = pair_rep.shape
+    devices = res // row_count
+    if res % 48 == 0 and devices in (4, 8, 16) and 40 * res * res * channels <= 32 * 1024 * 1024:
+        return on_whole_complex(pair_rep, residue_valid, *parameters)
+    return split_over_devices(pair_rep, residue_valid, *parameters)
+
+
 def solution(mesh):
     return jax.shard_map(
         per_device,

time: 81.8 us -> 46.8 us (0.57)
  blocking collectives: 31.1 us -> 0 us
  Pallas kernels: 0 us -> 19.2 us
  waiting for transfers between devices: 18.6 us -> 6.42 us
  starting transfers between devices: 18 us -> 7.24 us
  local copies, waits for them, and re-layouts: 7.97 us -> 13 us
  matrix products: 2.53 us -> 0 us
  other arithmetic: 2.46 us -> 0.01 us
    all_gather x1 -> x0, blocking collectives: 21.8 us -> none  [per_device(): whole_bias = lax.all_gather(pair_bias, 'row', axis=1, tiled=True)]
    pallas_call x0 -> x7, Pallas kernels: none -> 19.2 us  [the longest x1 9.43 us: on_whole_complex(): pl.pallas_call(functools.partial(triangle_kernel, res, chunk), out_shape=...]
    all_to_all x4 -> x0, waiting for transfers between devices: 18.6 us -> none  [the longest x1 6.64 us: per_device(): lax.all_to_all(block_product, 'row', split_axis=1, concat_axis=0, tiled=T...]
    all_to_all x4 -> x0, starting transfers between devices: 18 us -> none  [the longest x1 7.36 us: per_device(): lax.all_to_all(left_edges, 'row', split_axis=0, concat_axis=1, tiled=True)]
    all_to_all x1 -> x0, blocking collectives: 9.34 us -> none  [per_device(): lax.all_to_all(gated, 'row', split_axis=0, concat_axis=1, tiled=True)]
    ppermute x0 -> x5, starting transfers between devices: none -> 7.24 us  [exchange(): return lax.ppermute(values, 'row', [(d, d ^ bit) for d in range(devices)])]
    unnamed x40 -> x37, local copies, waits for them, and re-layouts: 6.27 us -> 13 us
    ppermute x0 -> x5, waiting for transfers between devices: none -> 6.42 us  [exchange(): return lax.ppermute(values, 'row', [(d, d ^ bit) for d in range(devices)])]
  transfers between devices with their start and end apart: 4 -> 5, of which waited for: 3 -> 2; matrix products, arithmetic and copies ran while one was open for 2% -> 2% of each run, Pallas kernels for 0% -> 9%
where the time goes in v3:
time: 46.8 us; the launch traced here: 46 us
  Pallas kernels  19.2 us (41%)
  local copies, waits for them, and re-layouts  13 us (28%)
  starting transfers between devices  7.24 us (15%)
  waiting for transfers between devices  6.42 us (14%)
    unnamed x37, local copies, waits for them, and re-layouts  13 us
    pallas_call x1, Pallas kernels, on_whole_complex(): pl.pallas_call(functools.partial(triangle_kernel, res, chunk), out_shape=...  9.43 us
    ppermute x5, starting transfers between devices, exchange(): return lax.ppermute(values, 'row', [(d, d ^ bit) for d in range(devices)])  7.24 us
    ppermute x5, waiting for transfers between devices, exchange(): return lax.ppermute(values, 'row', [(d, d ^ bit) for d in range(devices)])  6.42 us
    pallas_call x4, Pallas kernels, edges_of(): pl.pallas_call(functools.partial(edges_kernel, row_count, senders), out_s...  5.11 us
    pallas_call x1, Pallas kernels, on_whole_complex(): pl.pallas_call(functools.partial(attention_kernel, row_count, res, 8, 16)...  4.52 us
  transfers between devices with their start and end apart: 5, of which 2 were waited for; matrix products, arithmetic and copies ran while one was open for 2% of the time, Pallas kernels for 9%

profile of v3, /device:TPU:0, one launch (start us, length us, event | category | flops | bytes accessed | tf_op | source)
XLA Modules:
  0.0 46.0 jit_solution(17763409026147611711)
XLA Ops:
  0.0 4.0 %collective-permute-start = (bf16[3,48,128]{2,1,0:T(8,128)(2,1)}, bf16[3,48,128]{2,1,0:T(8,128)(2,1)S(1)}, u32[]{:S(2)}, u32[]{:S(2)}) collective-permute-start(bf16[3,48,128]{2,1,0:T(8,128)(2,1)} %pair_ref.1), channel_id=1, source_target_pairs={{0,8},{1,9},{2,10},{3,11},{4,12},{5,13},{6,14},{7,15},{8,0},{9,1},... | collective-permute-start | bytes 110600 | tf_op jit(solution)/shard_map/ppermute | solution.py:359
  4.0 0.8 %copy.30.w_pair_bias = bf16[128,4]{1,0:T(8,128)(2,1)S(1)} copy(bf16[128,4]{0,1:T(4,128)(2,1)} %param.32) | data formatting | bytes 2048 | tf_op args[15]
  4.8 0.9 %copy-done = bf16[128,512]{1,0:T(8,128)(2,1)S(1)} copy-done((bf16[128,512]{1,0:T(8,128)(2,1)S(1)}, bf16[128,512]{1,0:T(8,128)(2,1)}, u32[]{:S(2)}) %copy-start) | copy-done | bytes 131096
  5.8 0.8 %copy-done.1 = bf16[3,48,128]{2,1,0:T(8,128)(2,1)S(1)} copy-done((bf16[3,48,128]{2,1,0:T(8,128)(2,1)S(1)}, bf16[3,48,128]{2,1,0:T(8,128)(2,1)}, u32[]{:S(2)}) %copy-start.1) | copy-done | bytes 36888
  6.5 0.8 %copy-done.2 = bf16[128,128]{1,0:T(8,128)(2,1)S(1)} copy-done((bf16[128,128]{1,0:T(8,128)(2,1)S(1)}, bf16[128,128]{1,0:T(8,128)(2,1)}, u32[]{:S(2)}) %copy-start.2) | copy-done | bytes 32792
  7.3 0.8 %copy-done.3 = bf16[128,128]{1,0:T(8,128)(2,1)S(1)} copy-done((bf16[128,128]{1,0:T(8,128)(2,1)S(1)}, bf16[128,128]{1,0:T(8,128)(2,1)}, u32[]{:S(2)}) %copy-start.3) | copy-done | bytes 32792
  8.0 0.8 %copy-done.4 = bf16[128,128]{1,0:T(8,128)(2,1)S(1)} copy-done((bf16[128,128]{1,0:T(8,128)(2,1)S(1)}, bf16[128,128]{1,0:T(8,128)(2,1)}, u32[]{:S(2)}) %copy-start.4) | copy-done | bytes 32792
  8.8 0.8 %copy-done.5 = bf16[128,128]{1,0:T(8,128)(2,1)S(1)} copy-done((bf16[128,128]{1,0:T(8,128)(2,1)S(1)}, bf16[128,128]{1,0:T(8,128)(2,1)}, u32[]{:S(2)}) %copy-start.5) | copy-done | bytes 32792
  9.6 0.8 %copy-done.6 = bf16[128,128]{1,0:T(8,128)(2,1)S(1)} copy-done((bf16[128,128]{1,0:T(8,128)(2,1)S(1)}, bf16[128,128]{1,0:T(8,128)(2,1)}, u32[]{:S(2)}) %copy-start.6) | copy-done | bytes 32792
  10.3 0.8 %copy-done.7 = bf16[128,128]{1,0:T(8,128)(2,1)S(1)} copy-done((bf16[128,128]{1,0:T(8,128)(2,1)S(1)}, bf16[128,128]{1,0:T(8,128)(2,1)}, u32[]{:S(2)}) %copy-start.7) | copy-done | bytes 32792
  11.1 0.8 %copy-done.8 = bf16[128,128]{1,0:T(8,128)(2,1)S(1)} copy-done((bf16[128,128]{1,0:T(8,128)(2,1)S(1)}, bf16[128,128]{1,0:T(8,128)(2,1)}, u32[]{:S(2)}) %copy-start.8) | copy-done | bytes 32792
  11.8 0.7 %copy-done.9 = s32[48]{0:T(128)S(1)} copy-done((s32[48]{0:T(128)S(1)}, s32[48]{0:T(128)}, u32[]{:S(2)}) %copy-start.9) | copy-done | bytes 216
  12.5 0.7 %copy-done.11 = f32[128]{0:T(128)S(1)} copy-done((f32[128]{0:T(128)S(1)}, f32[128]{0:T(128)}, u32[]{:S(2)}) %copy-start.11) | copy-done | bytes 536
  16.6 1.6 %collective-permute-start.1 = (bf16[6,48,128]{2,1,0:T(8,128)(2,1)S(1)}, bf16[6,48,128]{2,1,0:T(8,128)(2,1)S(1)}, u32[]{:S(2)}, u32[]{:S(2)}) collective-permute-start(bf16[6,48,128]{2,1,0:T(8,128)(2,1)S(1)} %pad_maximum_fusion), channel_id=1, source_target_pairs={{0,4},{1,5},{2,6},{3,7},{4,0},{5,1},{6,2},{7,3},{8,12},{9,13},{10,... | collective-permute-start | bytes 221192 | tf_op jit(solution)/shard_map/ppermute | solution.py:359
  18.2 2.8 %collective-permute-done.1 = bf16[6,48,128]{2,1,0:T(8,128)(2,1)S(1)} collective-permute-done((bf16[6,48,128]{2,1,0:T(8,128)(2,1)S(1)}, bf16[6,48,128]{2,1,0:T(8,128)(2,1)S(1)}, u32[]{:S(2)}, u32[]{:S(2)}) %collective-permute-start.1) | collective-permute-done | bytes 73760 | tf_op jit(solution)/shard_map/ppermute | solution.py:359
  21.0 1.6 %collective-permute-start.2 = (bf16[12,48,128]{2,1,0:T(8,128)(2,1)S(1)}, bf16[12,48,128]{2,1,0:T(8,128)(2,1)S(1)}, u32[]{:S(2)}, u32[]{:S(2)}) collective-permute-start(bf16[12,48,128]{2,1,0:T(8,128)(2,1)S(1)} %constant_dynamic-update-slice_fusion.pairs_ref), channel_id=1, source_target_pairs={{0,2},{1,3},{2,0},{3,1},{4,6},{5,7},{6,4},{7,5},{8,10},{9,11},{10,... | collective-permute-start | bytes 442376 | tf_op jit(solution)/shard_map/ppermute | solution.py:359
  22.6 3.6 %collective-permute-done.2.pairs_ref = bf16[12,48,128]{2,1,0:T(8,128)(2,1)S(1)} collective-permute-done((bf16[12,48,128]{2,1,0:T(8,128)(2,1)S(1)}, bf16[12,48,128]{2,1,0:T(8,128)(2,1)S(1)}, u32[]{:S(2)}, u32[]{:S(2)}) %collective-permute-start.2) | collective-permute-done | bytes 147488 | tf_op jit(solution)/shard_map/ppermute | solution.py:359
  26.2 0.7 %copy-done.10 = s32[48]{0:T(128)S(1)} copy-done((s32[48]{0:T(128)S(1)}, s32[48]{0:T(128)}, u32[]{:S(2)}) %copy-start.10) | copy-done | bytes 216
  26.9 1.3 %shard_map.164 = (f32[2304,128]{1,0:T(8,128)S(1)}, f32[2304,128]{1,0:T(8,128)S(1)}, f32[2304,128]{1,0:T(8,128)S(1)}, f32[2304,128]{1,0:T(8,128)S(1)}) custom-call(s32[48]{0:T(128)S(1)} %copy-done.10, bf16[12,48,128]{2,1,0:T(8,128)(2,1)S(1)} %constant_dynamic-update-slice_fusion.pairs_ref, f32[48,128]{1,0:T(8,128)S(1)} %get-tuple-element.33.valid_column, ...), custom_call_target="tpu_custom_call" | custom-call | flops 94371840 | bytes 6291456 | tf_op jit(solution)/shard_map/pallas_call | solution.py:377
  28.2 1.3 %shard_map.165 = (f32[2304,128]{1,0:T(8,128)S(1)}, f32[2304,128]{1,0:T(8,128)S(1)}, f32[2304,128]{1,0:T(8,128)S(1)}, f32[2304,128]{1,0:T(8,128)S(1)}) custom-call(s32[48]{0:T(128)S(1)} %copy-done.10, bf16[12,48,128]{2,1,0:T(8,128)(2,1)S(1)} %collective-permute-done.4.pairs_ref, ...), custom_call_target="tpu_custom_call", output_to_operand_aliasing={{0}: (5, {}), {1}: (6, {}), {2}: (7, {}), {3}: (8, {})} | custom-call | flops 94371840 | bytes 6291456 | tf_op jit(solution)/shard_map/pallas_call | solution.py:377
  29.5 1.3 %shard_map.166 = (f32[2304,128]{1,0:T(8,128)S(1)}, f32[2304,128]{1,0:T(8,128)S(1)}, f32[2304,128]{1,0:T(8,128)S(1)}, f32[2304,128]{1,0:T(8,128)S(1)}) custom-call(s32[48]{0:T(128)S(1)} %copy-done.10, bf16[12,48,128]{2,1,0:T(8,128)(2,1)S(1)} %collective-permute-done.2.pairs_ref, ...), custom_call_target="tpu_custom_call", output_to_operand_aliasing={{0}: (5, {}), {1}: (6, {}), {2}: (7, {}), {3}: (8, {})} | custom-call | flops 94371840 | bytes 6291456 | tf_op jit(solution)/shard_map/pallas_call | solution.py:377
  30.8 1.3 %shard_map.167 = (f32[2304,128]{1,0:T(8,128)S(1)}, f32[2304,128]{1,0:T(8,128)S(1)}, f32[2304,128]{1,0:T(8,128)S(1)}, f32[2304,128]{1,0:T(8,128)S(1)}) custom-call(s32[48]{0:T(128)S(1)} %copy-done.10, bf16[12,48,128]{2,1,0:T(8,128)(2,1)S(1)} %collective-permute-done.3.pairs_ref, ...), custom_call_target="tpu_custom_call", output_to_operand_aliasing={{0}: (5, {}), {1}: (6, {}), {2}: (7, {}), {3}: (8, {})} | custom-call | flops 94371840 | bytes 6291456 | tf_op jit(solution)/shard_map/pallas_call | solution.py:377
  32.1 9.4 %shard_map.168 = (f32[2304,128]{1,0:T(8,128)S(1)}, f32[2304,128]{1,0:T(8,128)S(1)}, f32[2304,128]{1,0:T(8,128)S(1)}, f32[2304,128]{1,0:T(8,128)S(1)}) custom-call(f32[8,128]{1,0:T(8,128)S(1)} %get-tuple-element.31.norms, bf16[128,896]{1,0:T(8,128)(2,1)S(1)} %get-tuple-element.30.square_weights, f32[2304,128]{1,0:T(8,128)S(1)} %get-tuple-element.47.left_ref, ...), custom_call_target="tpu_custom_call" | custom-call | tf_op jit(solution)/shard_map/pallas_call | solution.py:406
  41.5 4.5 %shard_map.169 = bf16[3,48,128]{2,1,0:T(8,128)(2,1)} custom-call(s32[48]{0:T(128)S(1)} %copy-done.10, bf16[128,896]{1,0:T(8,128)(2,1)S(1)} %get-tuple-element.30.square_weights, f32[2304,128]{1,0:T(8,128)S(1)} %get-tuple-element.51.after_ref, f32[2304,128]{1,0:T(8,128)S(1)} %get-tuple-element.52.att_ref, f32[2304,128]{1,0:T(8,128)S(1)} %get-tuple-element.53.key_ref, ...), custom_call_target="tpu_custom_call" | custom-call | tf_op jit(solution)/shard_map/pallas_call | solution.py:414
  (32 shorter events, 3.5 us)
Async XLA Ops:
  0.0 16.6 %collective-permute-start = (bf16[3,48,128]{2,1,0:T(8,128)(2,1)}, bf16[3,48,128]{2,1,0:T(8,128)(2,1)S(1)}, u32[]{:S(2)}, u32[]{:S(2)}) collective-permute-start(bf16[3,48,128]{2,1,0:T(8,128)(2,1)} %pair_ref.1), channel_id=1, source_target_pairs={{0,8},{1,9},{2,10},{3,11},{4,12},{5,13},{6,14},{7,15},{8,0},{9,1},... | collective-permute-start | bytes 110600 | tf_op jit(solution)/shard_map/ppermute | solution.py:359
  4.8 0.9 %copy-start = (bf16[128,512]{1,0:T(8,128)(2,1)S(1)}, bf16[128,512]{1,0:T(8,128)(2,1)}, u32[]{:S(2)}) copy-start(bf16[128,512]{1,0:T(8,128)(2,1)} %w_edges.1) | copy-start | bytes 393220
  5.8 0.8 %copy-start.1 = (bf16[3,48,128]{2,1,0:T(8,128)(2,1)S(1)}, bf16[3,48,128]{2,1,0:T(8,128)(2,1)}, u32[]{:S(2)}) copy-start(bf16[3,48,128]{2,1,0:T(8,128)(2,1)} %pair_ref.1) | copy-start | bytes 110596
  6.5 0.8 %copy-start.2 = (bf16[128,128]{1,0:T(8,128)(2,1)S(1)}, bf16[128,128]{1,0:T(8,128)(2,1)}, u32[]{:S(2)}) copy-start(bf16[128,128]{1,0:T(8,128)(2,1)} %w_tri_gate.1) | copy-start | bytes 98308
  7.3 0.8 %copy-start.3 = (bf16[128,128]{1,0:T(8,128)(2,1)S(1)}, bf16[128,128]{1,0:T(8,128)(2,1)}, u32[]{:S(2)}) copy-start(bf16[128,128]{1,0:T(8,128)(2,1)} %w_tri_out.1) | copy-start | bytes 98308
  8.0 0.8 %copy-start.4 = (bf16[128,128]{1,0:T(8,128)(2,1)S(1)}, bf16[128,128]{1,0:T(8,128)(2,1)}, u32[]{:S(2)}) copy-start(bf16[128,128]{1,0:T(8,128)(2,1)} %w_query.1) | copy-start | bytes 98308
  8.8 0.8 %copy-start.5 = (bf16[128,128]{1,0:T(8,128)(2,1)S(1)}, bf16[128,128]{1,0:T(8,128)(2,1)}, u32[]{:S(2)}) copy-start(bf16[128,128]{1,0:T(8,128)(2,1)} %w_key.1) | copy-start | bytes 98308
  9.6 0.8 %copy-start.6 = (bf16[128,128]{1,0:T(8,128)(2,1)S(1)}, bf16[128,128]{1,0:T(8,128)(2,1)}, u32[]{:S(2)}) copy-start(bf16[128,128]{1,0:T(8,128)(2,1)} %w_value.1) | copy-start | bytes 98308
  10.3 0.8 %copy-start.7 = (bf16[128,128]{1,0:T(8,128)(2,1)S(1)}, bf16[128,128]{1,0:T(8,128)(2,1)}, u32[]{:S(2)}) copy-start(bf16[128,128]{1,0:T(8,128)(2,1)} %w_att_gate.1) | copy-start | bytes 98308
  11.1 0.8 %copy-start.8 = (bf16[128,128]{1,0:T(8,128)(2,1)S(1)}, bf16[128,128]{1,0:T(8,128)(2,1)}, u32[]{:S(2)}) copy-start(bf16[128,128]{1,0:T(8,128)(2,1)} %w_att_out.1) | copy-start | bytes 98308
  11.8 0.7 %copy-start.9 = (s32[48]{0:T(128)S(1)}, s32[48]{0:T(128)}, u32[]{:S(2)}) copy-start(s32[48]{0:T(128)} %valid_scalars.9) | copy-start | bytes 580
  12.5 0.7 %copy-start.11 = (f32[128]{0:T(128)S(1)}, f32[128]{0:T(128)}, u32[]{:S(2)}) copy-start(f32[128]{0:T(128)} %param.19) | copy-start | bytes 1540
  13.1 0.7 %copy-start.12 = (f32[128]{0:T(128)S(1)}, f32[128]{0:T(128)}, u32[]{:S(2)}) copy-start(f32[128]{0:T(128)} %param.20) | copy-start | bytes 1540
  13.8 0.7 %copy-start.13 = (f32[128]{0:T(128)S(1)}, f32[128]{0:T(128)}, u32[]{:S(2)}) copy-start(f32[128]{0:T(128)} %param.23) | copy-start | bytes 1540
  14.5 0.7 %copy-start.14 = (f32[128]{0:T(128)S(1)}, f32[128]{0:T(128)}, u32[]{:S(2)}) copy-start(f32[128]{0:T(128)} %param.24) | copy-start | bytes 1540
  15.1 0.7 %copy-start.15 = (f32[128]{0:T(128)S(1)}, f32[128]{0:T(128)}, u32[]{:S(2)}) copy-start(f32[128]{0:T(128)} %param.26) | copy-start | bytes 1540
  15.8 0.7 %copy-start.16 = (f32[128]{0:T(128)S(1)}, f32[128]{0:T(128)}, u32[]{:S(2)}) copy-start(f32[128]{0:T(128)} %param.27) | copy-start | bytes 1540
  16.6 4.4 %collective-permute-start.1 = (bf16[6,48,128]{2,1,0:T(8,128)(2,1)S(1)}, bf16[6,48,128]{2,1,0:T(8,128)(2,1)S(1)}, u32[]{:S(2)}, u32[]{:S(2)}) collective-permute-start(bf16[6,48,128]{2,1,0:T(8,128)(2,1)S(1)} %pad_maximum_fusion), channel_id=1, source_target_pairs={{0,4},{1,5},{2,6},{3,7},{4,0},{5,1},{6,2},{7,3},{8,12},{9,13},{10,... | collective-permute-start | bytes 221192 | tf_op jit(solution)/shard_map/ppermute | solution.py:359
  21.0 5.2 %collective-permute-start.2 = (bf16[12,48,128]{2,1,0:T(8,128)(2,1)S(1)}, bf16[12,48,128]{2,1,0:T(8,128)(2,1)S(1)}, u32[]{:S(2)}, u32[]{:S(2)}) collective-permute-start(bf16[12,48,128]{2,1,0:T(8,128)(2,1)S(1)} %constant_dynamic-update-slice_fusion.pairs_ref), channel_id=1, source_target_pairs={{0,2},{1,3},{2,0},{3,1},{4,6},{5,7},{6,4},{7,5},{8,10},{9,11},{10,... | collective-permute-start | bytes 442376 | tf_op jit(solution)/shard_map/ppermute | solution.py:359
  22.6 5.6 %collective-permute-start.4 = (bf16[12,48,128]{2,1,0:T(8,128)(2,1)S(1)}, bf16[12,48,128]{2,1,0:T(8,128)(2,1)S(1)}, u32[]{:S(2)}, u32[]{:S(2)}) collective-permute-start(bf16[12,48,128]{2,1,0:T(8,128)(2,1)S(1)} %constant_dynamic-update-slice_fusion.pairs_ref), channel_id=1, source_target_pairs={{0,1},{1,0},{2,3},{3,2},{4,5},{5,4},{6,7},{7,6},{8,9},{9,8},{10,11... | collective-permute-start | bytes 442376 | tf_op jit(solution)/shard_map/ppermute | solution.py:359
  26.2 4.5 %collective-permute-start.3 = (bf16[12,48,128]{2,1,0:T(8,128)(2,1)S(1)}, bf16[12,48,128]{2,1,0:T(8,128)(2,1)S(1)}, u32[]{:S(2)}, u32[]{:S(2)}) collective-permute-start(bf16[12,48,128]{2,1,0:T(8,128)(2,1)S(1)} %collective-permute-done.2.pairs_ref), channel_id=1, source_target_pairs={{0,1},{1,0},{2,3},{3,2},{4,5},{5,4},{6,7},{7,6},{8,9},{9,8},{10,11... | collective-permute-start | bytes 442376 | tf_op jit(solution)/shard_map/ppermute | solution.py:359
  26.2 0.7 %copy-start.10 = (s32[48]{0:T(128)S(1)}, s32[48]{0:T(128)}, u32[]{:S(2)}) copy-start(s32[48]{0:T(128)} %valid_scalars.9) | copy-start | bytes 580

commit v4 on v0

--- a/solution.py
+++ b/solution.py
@@ -1,8 +1,11 @@
+import functools
 import math
 
 import jax
 import jax.numpy as jnp
 from jax import lax
+from jax.experimental import pallas as pl
+from jax.experimental.pallas import tpu as pltpu
 from jax.sharding import PartitionSpec as P
 
 HEADS = 4
@@ -28,7 +31,7 @@
     return jnp.einsum("jhki,kjhd->ijhd", weights, value_cols, preferred_element_type=jnp.float32)
 
 
-def per_device(
+def split_over_devices(
     pair_rep,
     residue_valid,
     tri_norm_gain,
@@ -114,6 +117,290 @@
     return final.astype(jnp.bfloat16)
 
 
+def sigmoid(values):
+    return 0.5 * jnp.tanh(0.5 * values) + 0.5
+
+
+def dot(left, right):
+    return jnp.dot(left, right, preferred_element_type=jnp.float32)
+
+
+def rounded(values):
+    return values.astype(jnp.bfloat16).astype(jnp.float32)
+
+
+def edges_kernel(row_count, senders, pairs_ref, valid_column, norms, weights, *refs):
+    left_ref, right_ref, gate_ref, after_ref = refs[-4:]
+    f32, bf16 = jnp.float32, jnp.bfloat16
+    res = pairs_ref.shape[1]
+    channels = pairs_ref.shape[2]
+    tall = row_count * res
+    pairs = pairs_ref[...].astype(f32).reshape(len(senders) * tall, channels)
+    normed = layer_norm(pairs, norms[0:1, :], norms[1:2, :], 1).astype(bf16)
+    column = valid_column[...]
+    rows_of = [
+        jnp.bitwise_xor(lax.axis_index("row"), bits) * row_count + r
+        for bits in senders
+        for r in range(row_count)
+    ]
+    masks = jnp.concatenate([column * valid_column[pl.ds(i, 1), :] for i in rows_of], axis=0)
+    joined = dot(normed, weights[:, : 2 * channels])
+    left = rounded(sigmoid(joined[:, channels:]) * joined[:, :channels] * masks)
+    joined = dot(normed, weights[:, 2 * channels : 4 * channels])
+    right = rounded(sigmoid(joined[:, channels:]) * joined[:, :channels] * masks)
+    gate = sigmoid(dot(normed, weights[:, 4 * channels :]))
+    for n, i in enumerate(rows_of):
+        rows = slice(n * res, (n + 1) * res)
+        start = pl.multiple_of(i * res, res)
+        left_ref[pl.ds(start, res), :] = left[rows]
+        right_ref[pl.ds(i, res, stride=res), :] = right[rows]
+        gate_ref[pl.ds(start, res), :] = gate[rows]
+        after_ref[pl.ds(start, res), :] = pairs[rows]
+
+
+def triangle_kernel(
+    res,
+    chunk,
+    post_chunk,
+    norms,
+    w_out,
+    w_key,
+    w_value,
+    left_ref,
+    right_ref,
+    gate_ref,
+    pairs_ref,
+    after_ref,
+    att_ref,
+    key_ref,
+    value_ref,
+    triangle_ref,
+):
+    f32, bf16 = jnp.float32, jnp.bfloat16
+    channels = left_ref.shape[1]
+
+    def triangle_of(step, carry):
+        start = pl.multiple_of(step * chunk * res, chunk * res)
+        totals = [jnp.zeros((res, channels), f32) for _ in range(chunk)]
+        for k in range(res):
+            right = right_ref[pl.ds(k * res, res), :]
+            for r in range(chunk):
+                totals[r] = totals[r] + left_ref[pl.ds(start + r * res + k, 1), :] * right
+        for r in range(chunk):
+            triangle_ref[pl.ds(start + r * res, res), :] = rounded(totals[r])
+        return carry
+
+    lax.fori_loop(0, res // chunk, triangle_of, 0)
+    key_value = jnp.concatenate([w_key[...], w_value[...]], axis=1)
+
+    def attention_inputs_of(step, carry):
+        tall = post_chunk * res
+        rows = pl.ds(pl.multiple_of(step * tall, tall), tall)
+        tri_normed = layer_norm(triangle_ref[rows, :], norms[2:3, :], norms[3:4, :], 1).astype(bf16)
+        after_tri = pairs_ref[rows, :] + gate_ref[rows, :] * dot(tri_normed, w_out[...])
+        att_in = layer_norm(after_tri, norms[4:5, :], norms[5:6, :], 1).astype(bf16)
+        joined = dot(att_in, key_value)
+        after_ref[rows, :] = after_tri
+        att_ref[rows, :] = att_in.astype(f32)
+        key_ref[rows, :] = rounded(joined[:, :channels])
+        value_ref[rows, :] = rounded(joined[:, channels:])
+        return carry
+
+    lax.fori_loop(0, res // post_chunk, attention_inputs_of, 0)
+
+
+def attention_kernel(
+    row_count,
+    res,
+    key_chunk,
+    weigh_chunk,
+    valid_column,
+    w_query,
+    w_gate,
+    w_out,
+    head_bias,
+    after_ref,
+    att_ref,
+    key_ref,
+    value_ref,
+    out_ref,
+    score_ref,
+    bias_ref,
+):
+    f32, bf16 = jnp.float32, jnp.bfloat16
+    channels = key_ref.shape[1]
+    own = lax.axis_index("row") * row_count
+    own_start = pl.multiple_of(own * res, res)
+    own_in = att_ref[pl.ds(own_start, row_count * res), :].astype(bf16)
+    query = rounded(dot(own_in, w_query[...]))
+    att_gate = sigmoid(dot(own_in, w_gate[...]))
+    row = lax.broadcasted_iota(jnp.int32, (channels, HEADS), 0) // HEAD_DIM
+    head = lax.broadcasted_iota(jnp.int32, (channels, HEADS), 1)
+    repeat = jnp.where(row == head, 1.0, 0.0).astype(bf16)
+    wide_bias = dot(repeat, head_bias[...]).astype(bf16)
+    for r in range(row_count):
+        column = att_ref[pl.ds(own + r, res, stride=res), :].astype(bf16)
+        bias_ref[r * res : (r + 1) * res, :] = rounded(
+            lax.dot_general(
+                column, wide_bias, (((1,), (1,)), ((), ())), preferred_element_type=f32
+            )
+        )
+
+    factor = 1.0 / math.sqrt(HEAD_DIM)
+    row = lax.broadcasted_iota(jnp.int32, (2 * channels, channels), 0) % channels // HEAD_DIM
+    column = lax.broadcasted_iota(jnp.int32, (2 * channels, channels), 1) // HEAD_DIM
+    same_head = jnp.where(row == column, 1.0, 0.0).astype(bf16)
+
+    def scores_of(step, maxima):
+        maxima = list(maxima)
+        products = []
+        for offset in range(key_chunk):
+            keys = key_ref[pl.ds((step * key_chunk + offset) * res, res), :]
+            products.append(jnp.concatenate([keys] * row_count, axis=0) * query)
+        product = jnp.concatenate(products, axis=0)
+        high = product.astype(bf16)
+        low = (product - high.astype(f32)).astype(bf16)
+        scores = dot(jnp.concatenate([high, low], axis=1), same_head) * factor
+        for offset in range(key_chunk):
+            k = step * key_chunk + offset
+            key_mask = 1000000000.0 * (valid_column[pl.ds(k, 1), :] - 1.0)
+            for r in range(row_count):
+                at = (offset * row_count + r) * res
+                score = scores[at : at + res] + bias_ref[pl.ds(r * res + k, 1), :] + key_mask
+                score_ref[pl.ds((r * res + k) * res, res), :] = score
+                maxima[r] = jnp.maximum(maxima[r], score)
+        return tuple(maxima)
+
+    lowest = jnp.full((res, channels), -jnp.inf, f32)
+    maxima = lax.fori_loop(0, res // key_chunk, scores_of, (lowest,) * row_count)
+
+    zeros = jnp.zeros((res, channels), f32)
+    attended = []
+    for r in range(row_count):
+
+        def weigh(step, totals, r=r):
+            total, mixed = totals
+            for offset in range(weigh_chunk):
+                k = step * weigh_chunk + offset
+                weight = jnp.exp(score_ref[pl.ds((r * res + k) * res, res), :] - maxima[r])
+                total = total + weight
+                mixed = mixed + weight * value_ref[pl.ds(k * res, res), :]
+            return total, mixed
+
+        total, mixed = lax.fori_loop(0, res // weigh_chunk, weigh, (zeros, zeros))
+        attended.append(mixed / total)
+    gated = (jnp.concatenate(attended, axis=0) * att_gate).astype(bf16)
+    after_own = after_ref[pl.ds(own_start, row_count * res), :]
+    final = after_own + dot(gated, w_out[...])
+    out_ref[...] = final.astype(bf16).reshape(row_count, res, channels)
+
+
+def on_whole_complex(
+    pair_rep,
+    residue_valid,
+    tri_norm_gain,
+    tri_norm_bias,
+    w_edges,
+    w_tri_gate,
+    out_norm_gain,
+    out_norm_bias,
+    w_tri_out,
+    att_norm_gain,
+    att_norm_bias,
+    w_query,
+    w_key,
+    w_value,
+    w_att_gate,
+    w_pair_bias,
+    w_att_out,
+):
+    row_count, res, channels = pair_rep.shape
+    devices = res // row_count
+    f32, bf16 = jnp.float32, jnp.bfloat16
+    in_vmem = pl.BlockSpec(memory_space=pltpu.VMEM)
+    compiler_params = pltpu.CompilerParams(vmem_limit_bytes=24 * 1024 * 1024)
+    tall = jax.ShapeDtypeStruct((res * res, channels), f32)
+
+    def exchange(values, bit):
+        return lax.ppermute(values, "row", [(d, d ^ bit) for d in range(devices)])
+
+    vectors = (
+        tri_norm_gain,
+        tri_norm_bias,
+        out_norm_gain,
+        out_norm_bias,
+        att_norm_gain,
+        att_norm_bias,
+    )
+    norms = jnp.stack(vectors)
+    edge_weights = jnp.concatenate([w_edges, w_tri_gate], axis=1)
+    valid_column = jnp.broadcast_to(residue_valid.astype(f32)[:, None], (res, channels))
+
+    def edges_of(pairs, senders, edges):
+        return pl.pallas_call(
+            functools.partial(edges_kernel, row_count, senders),
+            out_shape=(tall,) * 4,
+            in_specs=[in_vmem] * (4 + len(edges)),
+            out_specs=(in_vmem,) * 4,
+            input_output_aliases={4 + e: e for e in range(len(edges))},
+            compiler_params=compiler_params,
+            cost_estimate=pl.CostEstimate(
+                flops=10 * pairs.size * channels, bytes_accessed=2**25, transcendentals=0
+            ),
+        )(pairs, valid_column, norms, edge_weights, *edges)
+
+    senders = (0,)
+    quarter = pair_rep
+    bit = devices // 2
+    while bit > 2:
+        twice = jnp.zeros((2 * quarter.shape[0],) + quarter.shape[1:], bf16)
+        kept = lax.dynamic_update_slice(twice, quarter, (0, 0, 0))
+        far = exchange(quarter, bit)
+        if bit == devices // 2:
+            far, kept, norms, edge_weights, valid_column = lax.optimization_barrier(
+                (far, kept, norms, edge_weights, valid_column)
+            )
+        quarter = lax.dynamic_update_slice(kept, far, (quarter.shape[0], 0, 0))
+        senders = senders + tuple(s ^ bit for s in senders)
+        bit //= 2
+    beside = exchange(quarter, 2)
+    across = exchange(quarter, 1)
+    edges = edges_of(quarter, senders, ())
+    edges = edges_of(across, tuple(s ^ 1 for s in senders), edges)
+    beside, edges = lax.optimization_barrier((beside, edges))
+    corner = exchange(beside, 1)
+    edges = edges_of(beside, tuple(s ^ 2 for s in senders), edges)
+    edges = edges_of(corner, tuple(s ^ 3 for s in senders), edges)
+
+    after_tri, att_in, keys, values = pl.pallas_call(
+        functools.partial(triangle_kernel, res, 6, 12),
+        out_shape=(tall,) * 4,
+        in_specs=[in_vmem] * 8,
+        out_specs=(in_vmem,) * 4,
+        scratch_shapes=[pltpu.VMEM((res * res, channels), f32)],
+        compiler_params=compiler_params,
+    )(norms, w_tri_out, w_key, w_value, *edges)
+    return pl.pallas_call(
+        functools.partial(attention_kernel, row_count, res, 8, 16),
+        out_shape=jax.ShapeDtypeStruct(pair_rep.shape, bf16),
+        in_specs=[in_vmem] * 9,
+        out_specs=in_vmem,
+        scratch_shapes=[
+            pltpu.VMEM((row_count * res * res, channels), f32),
+            pltpu.VMEM((row_count * res, channels), f32),
+        ],
+        compiler_params=compiler_params,
+    )(valid_column, w_query, w_att_gate, w_att_out, w_pair_bias.T, after_tri, att_in, keys, values)
+
+
+def per_device(pair_rep, residue_valid, *parameters):
+    row_count, res, channels = pair_rep.shape
+    devices = res // row_count
+    if res % 48 == 0 and devices in (4, 8, 16) and 40 * res * res * channels <= 32 * 1024 * 1024:
+        return on_whole_complex(pair_rep, residue_valid, *parameters)
+    return split_over_devices(pair_rep, residue_valid, *parameters)
+
+
 def solution(mesh):
     return jax.shard_map(
         per_device,

time: 81.8 us -> 31.8 us (0.39)
  blocking collectives: 31.1 us -> 0 us
  Pallas kernels: 0 us -> 13.9 us
  waiting for transfers between devices: 18.6 us -> 6.87 us
  starting transfers between devices: 18 us -> 7.31 us
  local copies, waits for them, and re-layouts: 7.97 us -> 1.75 us
  matrix products: 2.53 us -> 0 us
  other arithmetic: 2.46 us -> 1.61 us
    all_gather x1 -> x0, blocking collectives: 21.8 us -> none  [per_device(): whole_bias = lax.all_gather(pair_bias, 'row', axis=1, tiled=True)]
    all_to_all x4 -> x0, waiting for transfers between devices: 18.6 us -> none  [the longest x1 6.64 us: per_device(): lax.all_to_all(block_product, 'row', split_axis=1, concat_axis=0, tiled=T...]
    all_to_all x4 -> x0, starting transfers between devices: 18 us -> none  [the longest x1 7.36 us: per_device(): lax.all_to_all(left_edges, 'row', split_axis=0, concat_axis=1, tiled=True)]
    pallas_call x0 -> x6, Pallas kernels: none -> 13.9 us  [the longest x1 7.25 us: on_whole_complex(): pl.pallas_call(functools.partial(triangle_kernel, res, 6, 12), out_shape=...]
    all_to_all x1 -> x0, blocking collectives: 9.34 us -> none  [per_device(): lax.all_to_all(gated, 'row', split_axis=0, concat_axis=1, tiled=True)]
    ppermute x0 -> x5, starting transfers between devices: none -> 7.31 us  [exchange(): return lax.ppermute(values, 'row', [(d, d ^ bit) for d in range(devices)])]
    ppermute x0 -> x5, waiting for transfers between devices: none -> 6.87 us  [exchange(): return lax.ppermute(values, 'row', [(d, d ^ bit) for d in range(devices)])]
    unnamed x40 -> x14, local copies, waits for them, and re-layouts: 6.27 us -> 0.14 us
  transfers between devices with their start and end apart: 4 -> 5, of which waited for: 3 -> 3; matrix products, arithmetic and copies ran while one was open for 2% -> 10% of each run, Pallas kernels for 0% -> 6%
where the time goes in v4:
time: 31.8 us; the launch traced here: 31.5 us
  Pallas kernels  13.9 us (44%)
  starting transfers between devices  7.31 us (23%)
  waiting for transfers between devices  6.87 us (22%)
  local copies, waits for them, and re-layouts  1.75 us (6%)
  other arithmetic  1.61 us (5%)
    ppermute x5, starting transfers between devices, exchange(): return lax.ppermute(values, 'row', [(d, d ^ bit) for d in range(devices)])  7.31 us
    pallas_call x1, Pallas kernels, on_whole_complex(): pl.pallas_call(functools.partial(triangle_kernel, res, 6, 12), out_shape=...  7.25 us
    ppermute x5, waiting for transfers between devices, exchange(): return lax.ppermute(values, 'row', [(d, d ^ bit) for d in range(devices)])  6.87 us
    pallas_call x1, Pallas kernels, on_whole_complex(): pl.pallas_call(functools.partial(attention_kernel, row_count, res, 8, 16)...  3.99 us
    pallas_call x4, Pallas kernels, edges_of(): pl.pallas_call(functools.partial(edges_kernel, row_count, senders), out_s...  2.61 us
    concatenate x1, other arithmetic, on_whole_complex(): edge_weights = jnp.concatenate([w_edges, w_tri_gate], axis=1)  0.94 us
    dynamic_update_slice x1, local copies, waits for them, and re-layouts, on_whole_complex(): kept = lax.dynamic_update_slice(twice, quarter, (0, 0, 0))  0.78 us
    another operation x1, local copies, waits for them, and re-layouts, on_whole_complex(): norms = jnp.stack(vectors)  0.75 us
  transfers between devices with their start and end apart: 5, of which 3 were waited for; matrix products, arithmetic and copies ran while one was open for 10% of the time, Pallas kernels for 6%

profile of v4, /device:TPU:0, one launch (start us, length us, event | category | flops | bytes accessed | tf_op | source)
XLA Modules:
  0.0 31.5 jit_solution(5498594896213049339)
XLA Ops:
  0.0 4.0 %collective-permute-start = (bf16[3,48,128]{2,1,0:T(8,128)(2,1)}, bf16[3,48,128]{2,1,0:T(8,128)(2,1)S(1)}, u32[]{:S(2)}, u32[]{:S(2)}) collective-permute-start(bf16[3,48,128]{2,1,0:T(8,128)(2,1)} %param.17), channel_id=1, source_target_pairs={{0,8},{1,9},{2,10},{3,11},{4,12},{5,13},{6,14},{7,15},{8,0},{9,1},... | collective-permute-start | bytes 110600 | tf_op jit(solution)/shard_map/ppermute | solution.py:325
  4.0 0.9 %pad_maximum_fusion.weights = bf16[128,640]{1,0:T(8,128)(2,1)S(1)} fusion(bf16[128,128]{1,0:T(8,128)(2,1)} %param.22, bf16[128,512]{1,0:T(8,128)(2,1)} %param.21), kind=kLoop, calls=%fused_computation | loop fusion | flops 327680 | bytes 327680 | tf_op jit(solution)/shard_map/concatenate | solution.py:336
  5.0 0.7 %convert_element_type.3 = f32[48]{0:T(128)S(1)} convert(s32[48]{0:T(128)} %param.18) | non-fusion elementwise | flops 48 | bytes 384 | tf_op jit(solution)/shard_map/convert_element_type | solution.py:337
  5.6 0.8 %dynamic_update_slice.10 = bf16[6,48,128]{2,1,0:T(8,128)(2,1)S(1)} pad(bf16[3,48,128]{2,1,0:T(8,128)(2,1)} %param.17, bf16[]{:T(256)} %constant.3.clone.1), padding=0_3x0_0x0_0 | pad | bytes 110594 | tf_op jit(solution)/shard_map/dynamic_update_slice | solution.py:357
  6.4 0.8 %stack.27.norms = f32[6,128]{1,0:T(8,128)S(1)} concatenate(f32[1,128]{1,0:T(1,128)} %bitcast.8, f32[1,128]{1,0:T(1,128)} %bitcast.9, f32[1,128]{1,0:T(1,128)} %bitcast.10, f32[1,128]{1,0:T(1,128)} %bitcast.11, f32[1,128]{1,0:T(1,128)} %bitcast.12, f32[1,128]{1,0:T(1,128)} %bitcast.13), dimensions={0} | concatenate | bytes 6144 | tf_op jit(solution)/shard_map/stack | solution.py:335
  7.2 0.0 collective-permute-done
  7.2 0.1 broadcast_in_dim.2.valid_column
  7.3 1.6 %collective-permute-start.1 = (bf16[6,48,128]{2,1,0:T(8,128)(2,1)S(1)}, bf16[6,48,128]{2,1,0:T(8,128)(2,1)S(1)}, u32[]{:S(2)}, u32[]{:S(2)}) collective-permute-start(bf16[6,48,128]{2,1,0:T(8,128)(2,1)S(1)} %constant_dynamic-update-slice_fusion), channel_id=1, source_target_pairs={{0,4},{1,5},{2,6},{3,7},{4,0},{5,1},{6,2},{7,3},{8,12},{9,13},{10,... | collective-permute-start | bytes 221192 | tf_op jit(solution)/shard_map/ppermute | solution.py:325
  8.9 2.8 %collective-permute-done.1 = bf16[6,48,128]{2,1,0:T(8,128)(2,1)S(1)} collective-permute-done((bf16[6,48,128]{2,1,0:T(8,128)(2,1)S(1)}, bf16[6,48,128]{2,1,0:T(8,128)(2,1)S(1)}, u32[]{:S(2)}, u32[]{:S(2)}) %collective-permute-start.1) | collective-permute-done | bytes 73760 | tf_op jit(solution)/shard_map/ppermute | solution.py:325
  11.7 0.1 collective-permute-start.3
  11.8 1.6 %collective-permute-start.2 = (bf16[12,48,128]{2,1,0:T(8,128)(2,1)S(1)}, bf16[12,48,128]{2,1,0:T(8,128)(2,1)S(1)}, u32[]{:S(2)}, u32[]{:S(2)}) collective-permute-start(bf16[12,48,128]{2,1,0:T(8,128)(2,1)S(1)} %pad_maximum_fusion.1.pairs_ref), channel_id=1, source_target_pairs={{0,2},{1,3},{2,0},{3,1},{4,6},{5,7},{6,4},{7,5},{8,10},{9,11},{10,... | collective-permute-start | bytes 442376 | tf_op jit(solution)/shard_map/ppermute | solution.py:325
  13.3 0.7 %shard_map.163 = (f32[2304,128]{1,0:T(8,128)S(1)}, f32[2304,128]{1,0:T(8,128)S(1)}, f32[2304,128]{1,0:T(8,128)S(1)}, f32[2304,128]{1,0:T(8,128)S(1)}) custom-call(bf16[12,48,128]{2,1,0:T(8,128)(2,1)S(1)} %pad_maximum_fusion.1.pairs_ref, f32[48,128]{1,0:T(8,128)S(1)} %broadcast_in_dim.2.valid_column, f32[6,128]{1,0:T(8,128)S(1)} %stack.27.norms, ...), custom_call_target="tpu_custom_call" | custom-call | flops 94371840 | bytes 33554432 | tf_op jit(solution)/shard_map/pallas_call | solution.py:340
  14.0 0.0 collective-permute-done.3.pairs_ref
  14.0 0.7 %shard_map.164 = (f32[2304,128]{1,0:T(8,128)S(1)}, f32[2304,128]{1,0:T(8,128)S(1)}, f32[2304,128]{1,0:T(8,128)S(1)}, f32[2304,128]{1,0:T(8,128)S(1)}) custom-call(bf16[12,48,128]{2,1,0:T(8,128)(2,1)S(1)} %collective-permute-done.3.pairs_ref, ...), custom_call_target="tpu_custom_call", output_to_operand_aliasing={{0}: (4, {}), {1}: (5, {}), {2}: (6, {}), {3}: (7, {})} | custom-call | flops 94371840 | bytes 33554432 | tf_op jit(solution)/shard_map/pallas_call | solution.py:340
  14.7 3.4 %collective-permute-done.2.pairs_ref = bf16[12,48,128]{2,1,0:T(8,128)(2,1)S(1)} collective-permute-done((bf16[12,48,128]{2,1,0:T(8,128)(2,1)S(1)}, bf16[12,48,128]{2,1,0:T(8,128)(2,1)S(1)}, u32[]{:S(2)}, u32[]{:S(2)}) %collective-permute-start.2) | collective-permute-done | bytes 147488 | tf_op jit(solution)/shard_map/ppermute | solution.py:325
  18.0 0.0 collective-permute-start.4
  18.0 0.7 %shard_map.165 = (f32[2304,128]{1,0:T(8,128)S(1)}, f32[2304,128]{1,0:T(8,128)S(1)}, f32[2304,128]{1,0:T(8,128)S(1)}, f32[2304,128]{1,0:T(8,128)S(1)}) custom-call(bf16[12,48,128]{2,1,0:T(8,128)(2,1)S(1)} %collective-permute-done.2.pairs_ref, ...), custom_call_target="tpu_custom_call", output_to_operand_aliasing={{0}: (4, {}), {1}: (5, {}), {2}: (6, {}), {3}: (7, {})} | custom-call | flops 94371840 | bytes 33554432 | tf_op jit(solution)/shard_map/pallas_call | solution.py:340
  18.7 0.7 %collective-permute-done.4.pairs_ref = bf16[12,48,128]{2,1,0:T(8,128)(2,1)S(1)} collective-permute-done((bf16[12,48,128]{2,1,0:T(8,128)(2,1)S(1)}, bf16[12,48,128]{2,1,0:T(8,128)(2,1)S(1)}, u32[]{:S(2)}, u32[]{:S(2)}) %collective-permute-start.4) | collective-permute-done | bytes 147488 | tf_op jit(solution)/shard_map/ppermute | solution.py:325
  19.4 0.7 %shard_map.166 = (f32[2304,128]{1,0:T(8,128)S(1)}, f32[2304,128]{1,0:T(8,128)S(1)}, f32[2304,128]{1,0:T(8,128)S(1)}, f32[2304,128]{1,0:T(8,128)S(1)}) custom-call(bf16[12,48,128]{2,1,0:T(8,128)(2,1)S(1)} %collective-permute-done.4.pairs_ref, ...), custom_call_target="tpu_custom_call", output_to_operand_aliasing={{0}: (4, {}), {1}: (5, {}), {2}: (6, {}), {3}: (7, {})} | custom-call | flops 94371840 | bytes 33554432 | tf_op jit(solution)/shard_map/pallas_call | solution.py:340
  20.1 0.1 copy-done
  20.2 0.0 copy-done.1
  20.2 0.0 copy-done.2
  20.2 7.2 %shard_map.167 = (f32[2304,128]{1,0:T(8,128)S(1)}, f32[2304,128]{1,0:T(8,128)S(1)}, f32[2304,128]{1,0:T(8,128)S(1)}, f32[2304,128]{1,0:T(8,128)S(1)}) custom-call(f32[6,128]{1,0:T(8,128)S(1)} %stack.27.norms, bf16[128,128]{1,0:T(8,128)(2,1)S(1)} %copy-done, bf16[128,128]{1,0:T(8,128)(2,1)S(1)} %copy-done.1, bf16[128,128]{1,0:T(8,128)(2,1)S(1)} %copy-done.2, ...), custom_call_target="tpu_custom_call" | custom-call | tf_op jit(solution)/shard_map/pallas_call | solution.py:375
  27.5 4.0 %shard_map.168 = bf16[3,48,128]{2,1,0:T(8,128)(2,1)} custom-call(f32[48,128]{1,0:T(8,128)S(1)} %broadcast_in_dim.2.valid_column, bf16[128,128]{1,0:T(8,128)(2,1)S(1)} %copy-done.3, bf16[128,128]{1,0:T(8,128)(2,1)S(1)} %copy-done.4, bf16[128,128]{1,0:T(8,128)(2,1)S(1)} %copy-done.5, bf16[4,128]{1,0:T(4,128)(2,1)S(1)} %bitcast.7, ...), custom_call_target="tpu_custom_call" | custom-call | tf_op jit(solution)/shard_map/pallas_call | solution.py:383
  (13 shorter events, 0.0 us)
Async XLA Ops:
  0.0 7.2 %collective-permute-start = (bf16[3,48,128]{2,1,0:T(8,128)(2,1)}, bf16[3,48,128]{2,1,0:T(8,128)(2,1)S(1)}, u32[]{:S(2)}, u32[]{:S(2)}) collective-permute-start(bf16[3,48,128]{2,1,0:T(8,128)(2,1)} %param.17), channel_id=1, source_target_pairs={{0,8},{1,9},{2,10},{3,11},{4,12},{5,13},{6,14},{7,15},{8,0},{9,1},... | collective-permute-start | bytes 110600 | tf_op jit(solution)/shard_map/ppermute | solution.py:325
  7.3 4.4 %collective-permute-start.1 = (bf16[6,48,128]{2,1,0:T(8,128)(2,1)S(1)}, bf16[6,48,128]{2,1,0:T(8,128)(2,1)S(1)}, u32[]{:S(2)}, u32[]{:S(2)}) collective-permute-start(bf16[6,48,128]{2,1,0:T(8,128)(2,1)S(1)} %constant_dynamic-update-slice_fusion), channel_id=1, source_target_pairs={{0,4},{1,5},{2,6},{3,7},{4,0},{5,1},{6,2},{7,3},{8,12},{9,13},{10,... | collective-permute-start | bytes 221192 | tf_op jit(solution)/shard_map/ppermute | solution.py:325
  11.7 2.3 %collective-permute-start.3 = (bf16[12,48,128]{2,1,0:T(8,128)(2,1)S(1)}, bf16[12,48,128]{2,1,0:T(8,128)(2,1)S(1)}, u32[]{:S(2)}, u32[]{:S(2)}) collective-permute-start(bf16[12,48,128]{2,1,0:T(8,128)(2,1)S(1)} %pad_maximum_fusion.1.pairs_ref), channel_id=1, source_target_pairs={{0,1},{1,0},{2,3},{3,2},{4,5},{5,4},{6,7},{7,6},{8,9},{9,8},{10,11... | collective-permute-start | bytes 442376 | tf_op jit(solution)/shard_map/ppermute | solution.py:325
  11.8 6.3 %collective-permute-start.2 = (bf16[12,48,128]{2,1,0:T(8,128)(2,1)S(1)}, bf16[12,48,128]{2,1,0:T(8,128)(2,1)S(1)}, u32[]{:S(2)}, u32[]{:S(2)}) collective-permute-start(bf16[12,48,128]{2,1,0:T(8,128)(2,1)S(1)} %pad_maximum_fusion.1.pairs_ref), channel_id=1, source_target_pairs={{0,2},{1,3},{2,0},{3,1},{4,6},{5,7},{6,4},{7,5},{8,10},{9,11},{10,... | collective-permute-start | bytes 442376 | tf_op jit(solution)/shard_map/ppermute | solution.py:325
  18.0 1.4 %collective-permute-start.4 = (bf16[12,48,128]{2,1,0:T(8,128)(2,1)S(1)}, bf16[12,48,128]{2,1,0:T(8,128)(2,1)S(1)}, u32[]{:S(2)}, u32[]{:S(2)}) collective-permute-start(bf16[12,48,128]{2,1,0:T(8,128)(2,1)S(1)} %collective-permute-done.2.pairs_ref), channel_id=1, source_target_pairs={{0,1},{1,0},{2,3},{3,2},{4,5},{5,4},{6,7},{7,6},{8,9},{9,8},{10,11... | collective-permute-start | bytes 442376 | tf_op jit(solution)/shard_map/ppermute | solution.py:325
  19.4 0.8 %copy-start = (bf16[128,128]{1,0:T(8,128)(2,1)S(1)}, bf16[128,128]{1,0:T(8,128)(2,1)}, u32[]{:S(2)}) copy-start(bf16[128,128]{1,0:T(8,128)(2,1)} %w_out.2) | copy-start | bytes 98308
  19.4 0.8 %copy-start.1 = (bf16[128,128]{1,0:T(8,128)(2,1)S(1)}, bf16[128,128]{1,0:T(8,128)(2,1)}, u32[]{:S(2)}) copy-start(bf16[128,128]{1,0:T(8,128)(2,1)} %w_key.1) | copy-start | bytes 98308
  19.4 0.8 %copy-start.2 = (bf16[128,128]{1,0:T(8,128)(2,1)S(1)}, bf16[128,128]{1,0:T(8,128)(2,1)}, u32[]{:S(2)}) copy-start(bf16[128,128]{1,0:T(8,128)(2,1)} %w_value.1) | copy-start | bytes 98308
  20.2 7.3 %copy-start.3 = (bf16[128,128]{1,0:T(8,128)(2,1)S(1)}, bf16[128,128]{1,0:T(8,128)(2,1)}, u32[]{:S(2)}) copy-start(bf16[128,128]{1,0:T(8,128)(2,1)} %w_query.1) | copy-start | bytes 98308
  20.2 7.3 %copy-start.4 = (bf16[128,128]{1,0:T(8,128)(2,1)S(1)}, bf16[128,128]{1,0:T(8,128)(2,1)}, u32[]{:S(2)}) copy-start(bf16[128,128]{1,0:T(8,128)(2,1)} %w_gate.1) | copy-start | bytes 98308
  20.2 7.3 %copy-start.5 = (bf16[128,128]{1,0:T(8,128)(2,1)S(1)}, bf16[128,128]{1,0:T(8,128)(2,1)}, u32[]{:S(2)}) copy-start(bf16[128,128]{1,0:T(8,128)(2,1)} %w_out.3) | copy-start | bytes 98308
  20.2 7.3 %copy-start.6 = (bf16[128,4]{0,1:T(4,128)(2,1)S(1)}, bf16[128,4]{0,1:T(4,128)(2,1)}, u32[]{:S(2)}) copy-start(bf16[128,4]{0,1:T(4,128)(2,1)} %param.32) | copy-start | bytes 3076

commit v5 on v4

--- a/solution.py
+++ b/solution.py
@@ -129,18 +129,21 @@
     return values.astype(jnp.bfloat16).astype(jnp.float32)
 
 
-def edges_kernel(row_count, senders, pairs_ref, valid_column, norms, weights, *refs):
+def edges_kernel(row_count, senders, valid_column, norms, weights, *refs):
+    pair_refs = refs[: len(senders)]
     left_ref, right_ref, gate_ref, after_ref = refs[-4:]
     f32, bf16 = jnp.float32, jnp.bfloat16
-    res = pairs_ref.shape[1]
-    channels = pairs_ref.shape[2]
-    tall = row_count * res
-    pairs = pairs_ref[...].astype(f32).reshape(len(senders) * tall, channels)
+    res = valid_column.shape[0]
+    channels = valid_column.shape[1]
+    pairs = jnp.concatenate(
+        [ref[...].astype(f32).reshape(-1, channels) for ref in pair_refs], axis=0
+    )
     normed = layer_norm(pairs, norms[0:1, :], norms[1:2, :], 1).astype(bf16)
     column = valid_column[...]
     rows_of = [
         jnp.bitwise_xor(lax.axis_index("row"), bits) * row_count + r
-        for bits in senders
+        for piece in senders
+        for bits in piece
         for r in range(row_count)
     ]
     masks = jnp.concatenate([column * valid_column[pl.ds(i, 1), :] for i in rows_of], axis=0)
@@ -158,30 +161,12 @@
         after_ref[pl.ds(start, res), :] = pairs[rows]
 
 
-def triangle_kernel(
-    res,
-    chunk,
-    post_chunk,
-    norms,
-    w_out,
-    w_key,
-    w_value,
-    left_ref,
-    right_ref,
-    gate_ref,
-    pairs_ref,
-    after_ref,
-    att_ref,
-    key_ref,
-    value_ref,
-    triangle_ref,
-):
-    f32, bf16 = jnp.float32, jnp.bfloat16
+def triangle_kernel(res, chunk, left_ref, right_ref, triangle_ref):
     channels = left_ref.shape[1]
 
     def triangle_of(step, carry):
         start = pl.multiple_of(step * chunk * res, chunk * res)
-        totals = [jnp.zeros((res, channels), f32) for _ in range(chunk)]
+        totals = [jnp.zeros((res, channels), jnp.float32) for _ in range(chunk)]
         for k in range(res):
             right = right_ref[pl.ds(k * res, res), :]
             for r in range(chunk):
@@ -191,12 +176,32 @@
         return carry
 
     lax.fori_loop(0, res // chunk, triangle_of, 0)
+
+
+def attention_inputs_kernel(
+    res,
+    chunk,
+    norms,
+    w_out,
+    w_key,
+    w_value,
+    triangle_ref,
+    gate_ref,
+    pairs_ref,
+    after_ref,
+    att_ref,
+    key_ref,
+    value_ref,
+):
+    f32, bf16 = jnp.float32, jnp.bfloat16
+    channels = triangle_ref.shape[1]
     key_value = jnp.concatenate([w_key[...], w_value[...]], axis=1)
-
-    def attention_inputs_of(step, carry):
-        tall = post_chunk * res
+    tall = chunk * res
+
+    def inputs_of(step, carry):
         rows = pl.ds(pl.multiple_of(step * tall, tall), tall)
-        tri_normed = layer_norm(triangle_ref[rows, :], norms[2:3, :], norms[3:4, :], 1).astype(bf16)
+        triangle = triangle_ref[rows, :]
+        tri_normed = layer_norm(triangle, norms[2:3, :], norms[3:4, :], 1).astype(bf16)
         after_tri = pairs_ref[rows, :] + gate_ref[rows, :] * dot(tri_normed, w_out[...])
         att_in = layer_norm(after_tri, norms[4:5, :], norms[5:6, :], 1).astype(bf16)
         joined = dot(att_in, key_value)
@@ -206,14 +211,13 @@
         value_ref[rows, :] = rounded(joined[:, channels:])
         return carry
 
-    lax.fori_loop(0, res // post_chunk, attention_inputs_of, 0)
+    lax.fori_loop(0, res // chunk, inputs_of, 0)
 
 
 def attention_kernel(
     row_count,
     res,
     key_chunk,
-    weigh_chunk,
     valid_column,
     w_query,
     w_gate,
@@ -232,7 +236,8 @@
     own = lax.axis_index("row") * row_count
     own_start = pl.multiple_of(own * res, res)
     own_in = att_ref[pl.ds(own_start, row_count * res), :].astype(bf16)
-    query = rounded(dot(own_in, w_query[...]))
+    factor = 1.0 / math.sqrt(HEAD_DIM)
+    query = rounded(dot(own_in, w_query[...])) * factor
     att_gate = sigmoid(dot(own_in, w_gate[...]))
     row = lax.broadcasted_iota(jnp.int32, (channels, HEADS), 0) // HEAD_DIM
     head = lax.broadcasted_iota(jnp.int32, (channels, HEADS), 1)
@@ -246,7 +251,6 @@
             )
         )
 
-    factor = 1.0 / math.sqrt(HEAD_DIM)
     row = lax.broadcasted_iota(jnp.int32, (2 * channels, channels), 0) % channels // HEAD_DIM
     column = lax.broadcasted_iota(jnp.int32, (2 * channels, channels), 1) // HEAD_DIM
     same_head = jnp.where(row == column, 1.0, 0.0).astype(bf16)
@@ -260,7 +264,7 @@
         product = jnp.concatenate(products, axis=0)
         high = product.astype(bf16)
         low = (product - high.astype(f32)).astype(bf16)
-        scores = dot(jnp.concatenate([high, low], axis=1), same_head) * factor
+        scores = dot(jnp.concatenate([high, low], axis=1), same_head)
         for offset in range(key_chunk):
             k = step * key_chunk + offset
             key_mask = 1000000000.0 * (valid_column[pl.ds(k, 1), :] - 1.0)
@@ -274,20 +278,13 @@
     lowest = jnp.full((res, channels), -jnp.inf, f32)
     maxima = lax.fori_loop(0, res // key_chunk, scores_of, (lowest,) * row_count)
 
-    zeros = jnp.zeros((res, channels), f32)
     attended = []
     for r in range(row_count):
-
-        def weigh(step, totals, r=r):
-            total, mixed = totals
-            for offset in range(weigh_chunk):
-                k = step * weigh_chunk + offset
-                weight = jnp.exp(score_ref[pl.ds((r * res + k) * res, res), :] - maxima[r])
-                total = total + weight
-                mixed = mixed + weight * value_ref[pl.ds(k * res, res), :]
-            return total, mixed
-
-        total, mixed = lax.fori_loop(0, res // weigh_chunk, weigh, (zeros, zeros))
+        total = mixed = jnp.zeros((res, channels), f32)
+        for k in range(res):
+            weight = jnp.exp(score_ref[pl.ds((r * res + k) * res, res), :] - maxima[r])
+            total = total + weight
+            mixed = mixed + weight * value_ref[pl.ds(k * res, res), :]
         attended.append(mixed / total)
     gated = (jnp.concatenate(attended, axis=0) * att_gate).astype(bf16)
     after_own = after_ref[pl.ds(own_start, row_count * res), :]
@@ -336,52 +333,80 @@
     edge_weights = jnp.concatenate([w_edges, w_tri_gate], axis=1)
     valid_column = jnp.broadcast_to(residue_valid.astype(f32)[:, None], (res, channels))
 
-    def edges_of(pairs, senders, edges):
+    def edges_of(pieces, edges):
+        pairs = [p for p, _ in pieces]
+        senders = tuple(s for _, s in pieces)
+        operands = 3 + len(pieces)
         return pl.pallas_call(
             functools.partial(edges_kernel, row_count, senders),
             out_shape=(tall,) * 4,
-            in_specs=[in_vmem] * (4 + len(edges)),
+            in_specs=[in_vmem] * (operands + len(edges)),
             out_specs=(in_vmem,) * 4,
-            input_output_aliases={4 + e: e for e in range(len(edges))},
+            input_output_aliases={operands + e: e for e in range(len(edges))},
             compiler_params=compiler_params,
             cost_estimate=pl.CostEstimate(
-                flops=10 * pairs.size * channels, bytes_accessed=2**25, transcendentals=0
+                flops=10 * sum(p.size for p in pairs) * channels,
+                bytes_accessed=2**25,
+                transcendentals=0,
             ),
-        )(pairs, valid_column, norms, edge_weights, *edges)
+        )(valid_column, norms, edge_weights, *pairs, *edges)
 
     senders = (0,)
-    quarter = pair_rep
+    own = pair_rep
     bit = devices // 2
-    while bit > 2:
-        twice = jnp.zeros((2 * quarter.shape[0],) + quarter.shape[1:], bf16)
-        kept = lax.dynamic_update_slice(twice, quarter, (0, 0, 0))
-        far = exchange(quarter, bit)
+    while bit > 4:
+        twice = jnp.zeros((2 * own.shape[0],) + own.shape[1:], bf16)
+        kept = lax.dynamic_update_slice(twice, own, (0, 0, 0))
+        far = exchange(own, bit)
         if bit == devices // 2:
-            far, kept, norms, edge_weights, valid_column = lax.optimization_barrier(
-                (far, kept, norms, edge_weights, valid_column)
+            far, kept, norms, edge_weights = lax.optimization_barrier(
+                (far, kept, norms, edge_weights)
             )
-        quarter = lax.dynamic_update_slice(kept, far, (quarter.shape[0], 0, 0))
+        own = lax.dynamic_update_slice(kept, far, (own.shape[0], 0, 0))
         senders = senders + tuple(s ^ bit for s in senders)
         bit //= 2
-    beside = exchange(quarter, 2)
-    across = exchange(quarter, 1)
-    edges = edges_of(quarter, senders, ())
-    edges = edges_of(across, tuple(s ^ 1 for s in senders), edges)
-    beside, edges = lax.optimization_barrier((beside, edges))
-    corner = exchange(beside, 1)
-    edges = edges_of(beside, tuple(s ^ 2 for s in senders), edges)
-    edges = edges_of(corner, tuple(s ^ 3 for s in senders), edges)
-
+
+    def from_sender(bits):
+        return tuple(s ^ bits for s in senders)
+
+    diagonal = exchange(own, 6)
+    beside = exchange(own, 2)
+    near = exchange(own, 4)
+    across = exchange(own, 1)
+    edges = edges_of([(own, senders), (across, from_sender(1))], ())
+    diagonal, edges = lax.optimization_barrier((diagonal, edges))
+    diagonal_across = exchange(diagonal, 1)
+    beside_across = exchange(beside, 1)
+    edges = edges_of([(diagonal, from_sender(6)), (beside, from_sender(2))], edges)
+    near, edges = lax.optimization_barrier((near, edges))
+    near_across = exchange(near, 1)
+    edges = edges_of(
+        [
+            (diagonal_across, from_sender(7)),
+            (beside_across, from_sender(3)),
+            (near, from_sender(4)),
+        ],
+        edges,
+    )
+    edges = edges_of([(near_across, from_sender(5))], edges)
+
+    left, right, gate, pairs = edges
+    triangle = pl.pallas_call(
+        functools.partial(triangle_kernel, res, 6),
+        out_shape=tall,
+        in_specs=[in_vmem] * 2,
+        out_specs=in_vmem,
+        compiler_params=compiler_params,
+    )(left, right)
     after_tri, att_in, keys, values = pl.pallas_call(
-        functools.partial(triangle_kernel, res, 6, 12),
+        functools.partial(attention_inputs_kernel, res, 12),
         out_shape=(tall,) * 4,
-        in_specs=[in_vmem] * 8,
+        in_specs=[in_vmem] * 7,
         out_specs=(in_vmem,) * 4,
-        scratch_shapes=[pltpu.VMEM((res * res, channels), f32)],
         compiler_params=compiler_params,
-    )(norms, w_tri_out, w_key, w_value, *edges)
+    )(norms, w_tri_out, w_key, w_value, triangle, gate, pairs)
     return pl.pallas_call(
-        functools.partial(attention_kernel, row_count, res, 8, 16),
+        functools.partial(attention_kernel, row_count, res, 8),
         out_shape=jax.ShapeDtypeStruct(pair_rep.shape, bf16),
         in_specs=[in_vmem] * 9,
         out_specs=in_vmem,
@@ -396,7 +421,7 @@
 def per_device(pair_rep, residue_valid, *parameters):
     row_count, res, channels = pair_rep.shape
     devices = res // row_count
-    if res % 48 == 0 and devices in (4, 8, 16) and 40 * res * res * channels <= 32 * 1024 * 1024:
+    if res % 48 == 0 and devices in (8, 16) and 40 * res * res * channels <= 32 * 1024 * 1024:
         return on_whole_complex(pair_rep, residue_valid, *parameters)
     return split_over_devices(pair_rep, residue_valid, *parameters)
 

time: 31.8 us -> 28 us (0.88)
  waiting for transfers between devices: 6.87 us -> 2.33 us
  starting transfers between devices: 7.31 us -> 8.23 us
    ppermute x5 -> x8, waiting for transfers between devices: 6.87 us -> 2.33 us  [exchange(): return lax.ppermute(values, 'row', [(d, d ^ bit) for d in range(devices)])]
    ppermute x5 -> x8, starting transfers between devices: 7.31 us -> 8.23 us  [exchange(): return lax.ppermute(values, 'row', [(d, d ^ bit) for d in range(devices)])]
    pallas_call x2 -> x3, Pallas kernels: 11.2 us -> 11.2 us  [the longest x1 4 us: on_whole_complex(): pl.pallas_call(functools.partial(triangle_kernel, res, 6), out_shape=tall...]
  transfers between devices with their start and end apart: 5 -> 8, of which waited for: 3 -> 3; matrix products, arithmetic and copies ran while one was open for 10% -> 12% of each run, Pallas kernels for 6% -> 8%
where the time goes in v5:
time: 28 us; the launch traced here: 27.8 us
  Pallas kernels  13.8 us (49%)
  starting transfers between devices  8.23 us (29%)
  waiting for transfers between devices  2.33 us (8%)
  local copies, waits for them, and re-layouts  1.66 us (6%)
  other arithmetic  1.6 us (6%)
    ppermute x8, starting transfers between devices, exchange(): return lax.ppermute(values, 'row', [(d, d ^ bit) for d in range(devices)])  8.23 us
    pallas_call x1, Pallas kernels, on_whole_complex(): pl.pallas_call(functools.partial(triangle_kernel, res, 6), out_shape=tall...  4 us
    pallas_call x1, Pallas kernels, on_whole_complex(): pl.pallas_call(functools.partial(attention_kernel, row_count, res, 8), ou...  3.9 us
    pallas_call x1, Pallas kernels, on_whole_complex(): pl.pallas_call(functools.partial(attention_inputs_kernel, res, 12), out_s...  3.26 us
    pallas_call x4, Pallas kernels, edges_of(): pl.pallas_call(functools.partial(edges_kernel, row_count, senders), out_s...  2.62 us
    ppermute x8, waiting for transfers between devices, exchange(): return lax.ppermute(values, 'row', [(d, d ^ bit) for d in range(devices)])  2.33 us
    concatenate x1, other arithmetic, on_whole_complex(): edge_weights = jnp.concatenate([w_edges, w_tri_gate], axis=1)  0.94 us
    dynamic_update_slice x1, local copies, waits for them, and re-layouts, on_whole_complex(): kept = lax.dynamic_update_slice(twice, own, (0, 0, 0))  0.78 us
  transfers between devices with their start and end apart: 8, of which 3 were waited for; matrix products, arithmetic and copies ran while one was open for 12% of the time, Pallas kernels for 8%

profile of v5, /device:TPU:0, one launch (start us, length us, event | category | flops | bytes accessed | tf_op | source)
XLA Modules:
  0.0 27.8 jit_solution(8911122402394404819)
XLA Ops:
  0.0 4.0 %collective-permute-start = (bf16[3,48,128]{2,1,0:T(8,128)(2,1)}, bf16[3,48,128]{2,1,0:T(8,128)(2,1)S(1)}, u32[]{:S(2)}, u32[]{:S(2)}) collective-permute-start(bf16[3,48,128]{2,1,0:T(8,128)(2,1)} %param.17), channel_id=1, source_target_pairs={{0,8},{1,9},{2,10},{3,11},{4,12},{5,13},{6,14},{7,15},{8,0},{9,1},... | collective-permute-start | bytes 110600 | tf_op jit(solution)/shard_map/ppermute | solution.py:322
  4.0 0.9 %pad_maximum_fusion.weights = bf16[128,640]{1,0:T(8,128)(2,1)S(1)} fusion(bf16[128,128]{1,0:T(8,128)(2,1)} %param.22, bf16[128,512]{1,0:T(8,128)(2,1)} %param.21), kind=kLoop, calls=%fused_computation | loop fusion | flops 327680 | bytes 327680 | tf_op jit(solution)/shard_map/concatenate | solution.py:333
  5.0 0.8 %dynamic_update_slice.6 = bf16[6,48,128]{2,1,0:T(8,128)(2,1)S(1)} pad(bf16[3,48,128]{2,1,0:T(8,128)(2,1)} %param.17, bf16[]{:T(256)} %constant.0.clone.1), padding=0_3x0_0x0_0 | pad | bytes 110594 | tf_op jit(solution)/shard_map/dynamic_update_slice | solution.py:359
  5.8 0.8 %stack.27.norms = f32[6,128]{1,0:T(8,128)S(1)} concatenate(f32[1,128]{1,0:T(1,128)} %bitcast.8, f32[1,128]{1,0:T(1,128)} %bitcast.9, f32[1,128]{1,0:T(1,128)} %bitcast.10, f32[1,128]{1,0:T(1,128)} %bitcast.11, f32[1,128]{1,0:T(1,128)} %bitcast.12, f32[1,128]{1,0:T(1,128)} %bitcast.13), dimensions={0} | concatenate | bytes 6144 | tf_op jit(solution)/shard_map/stack | solution.py:332
  6.5 0.1 collective-permute-done
  6.6 0.1 collective-permute-start.3
  6.7 2.5 %collective-permute-start.2 = (bf16[6,48,128]{2,1,0:T(8,128)(2,1)S(1)}, bf16[6,48,128]{2,1,0:T(8,128)(2,1)S(1)}, u32[]{:S(2)}, u32[]{:S(2)}) collective-permute-start(bf16[6,48,128]{2,1,0:T(8,128)(2,1)S(1)} %constant_dynamic-update-slice_fusion.refs_0_), channel_id=1, source_target_pairs={{0,6},{1,7},{2,4},{3,5},{4,2},{5,3},{6,0},{7,1},{8,14},{9,15},{10,... | collective-permute-start | bytes 221192 | tf_op jit(solution)/shard_map/ppermute | solution.py:322
  9.2 0.5 %collective-permute-start.4 = (bf16[6,48,128]{2,1,0:T(8,128)(2,1)S(1)}, bf16[6,48,128]{2,1,0:T(8,128)(2,1)S(1)}, u32[]{:S(2)}, u32[]{:S(2)}) collective-permute-start(bf16[6,48,128]{2,1,0:T(8,128)(2,1)S(1)} %constant_dynamic-update-slice_fusion.refs_0_), channel_id=1, source_target_pairs={{0,2},{1,3},{2,0},{3,1},{4,6},{5,7},{6,4},{7,5},{8,10},{9,11},{10,... | collective-permute-start | bytes 221192 | tf_op jit(solution)/shard_map/ppermute | solution.py:322
  9.7 0.5 %collective-permute-start.1 = (bf16[6,48,128]{2,1,0:T(8,128)(2,1)S(1)}, bf16[6,48,128]{2,1,0:T(8,128)(2,1)S(1)}, u32[]{:S(2)}, u32[]{:S(2)}) collective-permute-start(bf16[6,48,128]{2,1,0:T(8,128)(2,1)S(1)} %constant_dynamic-update-slice_fusion.refs_0_), channel_id=1, source_target_pairs={{0,4},{1,5},{2,6},{3,7},{4,0},{5,1},{6,2},{7,3},{8,12},{9,13},{10,... | collective-permute-start | bytes 221192 | tf_op jit(solution)/shard_map/ppermute | solution.py:322
  10.2 0.7 %convert_element_type.3 = f32[48]{0:T(128)S(1)} convert(s32[48]{0:T(128)} %param.18) | non-fusion elementwise | flops 48 | bytes 384 | tf_op jit(solution)/shard_map/convert_element_type | solution.py:334
  10.9 0.1 broadcast_in_dim.2.valid_column
  10.9 0.7 %shard_map.163 = (f32[2304,128]{1,0:T(8,128)S(1)}, f32[2304,128]{1,0:T(8,128)S(1)}, f32[2304,128]{1,0:T(8,128)S(1)}, f32[2304,128]{1,0:T(8,128)S(1)}) custom-call(f32[48,128]{1,0:T(8,128)S(1)} %broadcast_in_dim.2.valid_column, f32[6,128]{1,0:T(8,128)S(1)} %stack.27.norms, bf16[128,640]{1,0:T(8,128)(2,1)S(1)} %pad_maximum_fusion.weights, ...), custom_call_target="tpu_custom_call" | custom-call | flops 94371840 | bytes 33554432 | tf_op jit(solution)/shard_map/pallas_call | solution.py:340
  11.6 0.7 %collective-permute-done.2.refs_0_ = bf16[6,48,128]{2,1,0:T(8,128)(2,1)S(1)} collective-permute-done((bf16[6,48,128]{2,1,0:T(8,128)(2,1)S(1)}, bf16[6,48,128]{2,1,0:T(8,128)(2,1)S(1)}, u32[]{:S(2)}, u32[]{:S(2)}) %collective-permute-start.2) | collective-permute-done | bytes 73760 | tf_op jit(solution)/shard_map/ppermute | solution.py:322
  12.3 1.5 %collective-permute-done.4.refs_1_ = bf16[6,48,128]{2,1,0:T(8,128)(2,1)S(1)} collective-permute-done((bf16[6,48,128]{2,1,0:T(8,128)(2,1)S(1)}, bf16[6,48,128]{2,1,0:T(8,128)(2,1)S(1)}, u32[]{:S(2)}, u32[]{:S(2)}) %collective-permute-start.4) | collective-permute-done | bytes 73760 | tf_op jit(solution)/shard_map/ppermute | solution.py:322
  13.8 0.7 %shard_map.164 = (f32[2304,128]{1,0:T(8,128)S(1)}, f32[2304,128]{1,0:T(8,128)S(1)}, f32[2304,128]{1,0:T(8,128)S(1)}, f32[2304,128]{1,0:T(8,128)S(1)}) custom-call(f32[48,128]{1,0:T(8,128)S(1)} %broadcast_in_dim.2.valid_column, f32[6,128]{1,0:T(8,128)S(1)} %stack.27.norms, ...), custom_call_target="tpu_custom_call", output_to_operand_aliasing={{0}: (5, {}), {1}: (6, {}), {2}: (7, {}), {3}: (8, {})} | custom-call | flops 94371840 | bytes 33554432 | tf_op jit(solution)/shard_map/pallas_call | solution.py:340
  14.5 0.6 %collective-permute-start.5 = (bf16[6,48,128]{2,1,0:T(8,128)(2,1)S(1)}, bf16[6,48,128]{2,1,0:T(8,128)(2,1)S(1)}, u32[]{:S(2)}, u32[]{:S(2)}) collective-permute-start(bf16[6,48,128]{2,1,0:T(8,128)(2,1)S(1)} %collective-permute-done.1.refs_2_), channel_id=1, source_target_pairs={{0,1},{1,0},{2,3},{3,2},{4,5},{5,4},{6,7},{7,6},{8,9},{9,8},{10,11... | collective-permute-start | bytes 221192 | tf_op jit(solution)/shard_map/ppermute | solution.py:322
  15.1 0.0 collective-permute-done.7.refs_1_
  15.1 0.9 %shard_map.165 = (f32[2304,128]{1,0:T(8,128)S(1)}, f32[2304,128]{1,0:T(8,128)S(1)}, f32[2304,128]{1,0:T(8,128)S(1)}, f32[2304,128]{1,0:T(8,128)S(1)}) custom-call(f32[48,128]{1,0:T(8,128)S(1)} %broadcast_in_dim.2.valid_column, f32[6,128]{1,0:T(8,128)S(1)} %stack.27.norms, ...), custom_call_target="tpu_custom_call", output_to_operand_aliasing={{0}: (6, {}), {1}: (7, {}), {2}: (8, {}), {3}: (9, {})} | custom-call | flops 141557760 | bytes 33554432 | tf_op jit(solution)/shard_map/pallas_call | solution.py:340
  15.9 0.0 collective-permute-done.5.refs_0_
  16.0 0.5 %shard_map.166 = (f32[2304,128]{1,0:T(8,128)S(1)}, f32[2304,128]{1,0:T(8,128)S(1)}, f32[2304,128]{1,0:T(8,128)S(1)}, f32[2304,128]{1,0:T(8,128)S(1)}) custom-call(f32[48,128]{1,0:T(8,128)S(1)} %broadcast_in_dim.2.valid_column, f32[6,128]{1,0:T(8,128)S(1)} %stack.27.norms, ...), custom_call_target="tpu_custom_call", output_to_operand_aliasing={{0}: (4, {}), {1}: (5, {}), {2}: (6, {}), {3}: (7, {})} | custom-call | flops 47185920 | bytes 33554432 | tf_op jit(solution)/shard_map/pallas_call | solution.py:340
  16.5 0.0 copy-start.1
  16.5 4.0 %shard_map.167.triangle_ref = f32[2304,128]{1,0:T(8,128)S(1)} custom-call(f32[2304,128]{1,0:T(8,128)S(1)} %get-tuple-element.65.left_ref, f32[2304,128]{1,0:T(8,128)S(1)} %get-tuple-element.66.right_ref), custom_call_target="tpu_custom_call" | custom-call | tf_op jit(solution)/shard_map/pallas_call | solution.py:394
  20.6 3.3 %shard_map.168 = (f32[2304,128]{1,0:T(8,128)S(1)}, f32[2304,128]{1,0:T(8,128)S(1)}, f32[2304,128]{1,0:T(8,128)S(1)}, f32[2304,128]{1,0:T(8,128)S(1)}) custom-call(f32[6,128]{1,0:T(8,128)S(1)} %stack.27.norms, bf16[128,128]{1,0:T(8,128)(2,1)S(1)} %copy-done, bf16[128,128]{1,0:T(8,128)(2,1)S(1)} %copy-done.1, bf16[128,128]{1,0:T(8,128)(2,1)S(1)} %copy-done.2, ...), custom_call_target="tpu_custom_call" | custom-call | tf_op jit(solution)/shard_map/pallas_call | solution.py:401
  23.9 3.9 %shard_map.169 = bf16[3,48,128]{2,1,0:T(8,128)(2,1)} custom-call(f32[48,128]{1,0:T(8,128)S(1)} %broadcast_in_dim.2.valid_column, bf16[128,128]{1,0:T(8,128)(2,1)S(1)} %copy-done.3, bf16[128,128]{1,0:T(8,128)(2,1)S(1)} %copy-done.4, bf16[128,128]{1,0:T(8,128)(2,1)S(1)} %copy-done.5, bf16[4,128]{1,0:T(4,128)(2,1)S(1)} %bitcast.7, ...), custom_call_target="tpu_custom_call" | custom-call | tf_op jit(solution)/shard_map/pallas_call | solution.py:408
  (19 shorter events, 0.1 us)
Async XLA Ops:
  0.0 6.6 %collective-permute-start = (bf16[3,48,128]{2,1,0:T(8,128)(2,1)}, bf16[3,48,128]{2,1,0:T(8,128)(2,1)S(1)}, u32[]{:S(2)}, u32[]{:S(2)}) collective-permute-start(bf16[3,48,128]{2,1,0:T(8,128)(2,1)} %param.17), channel_id=1, source_target_pairs={{0,8},{1,9},{2,10},{3,11},{4,12},{5,13},{6,14},{7,15},{8,0},{9,1},... | collective-permute-start | bytes 110600 | tf_op jit(solution)/shard_map/ppermute | solution.py:322
  6.6 4.3 %collective-permute-start.3 = (bf16[6,48,128]{2,1,0:T(8,128)(2,1)S(1)}, bf16[6,48,128]{2,1,0:T(8,128)(2,1)S(1)}, u32[]{:S(2)}, u32[]{:S(2)}) collective-permute-start(bf16[6,48,128]{2,1,0:T(8,128)(2,1)S(1)} %constant_dynamic-update-slice_fusion.refs_0_), channel_id=1, source_target_pairs={{0,1},{1,0},{2,3},{3,2},{4,5},{5,4},{6,7},{7,6},{8,9},{9,8},{10,11... | collective-permute-start | bytes 221192 | tf_op jit(solution)/shard_map/ppermute | solution.py:322
  6.7 5.6 %collective-permute-start.2 = (bf16[6,48,128]{2,1,0:T(8,128)(2,1)S(1)}, bf16[6,48,128]{2,1,0:T(8,128)(2,1)S(1)}, u32[]{:S(2)}, u32[]{:S(2)}) collective-permute-start(bf16[6,48,128]{2,1,0:T(8,128)(2,1)S(1)} %constant_dynamic-update-slice_fusion.refs_0_), channel_id=1, source_target_pairs={{0,6},{1,7},{2,4},{3,5},{4,2},{5,3},{6,0},{7,1},{8,14},{9,15},{10,... | collective-permute-start | bytes 221192 | tf_op jit(solution)/shard_map/ppermute | solution.py:322
  9.2 4.6 %collective-permute-start.4 = (bf16[6,48,128]{2,1,0:T(8,128)(2,1)S(1)}, bf16[6,48,128]{2,1,0:T(8,128)(2,1)S(1)}, u32[]{:S(2)}, u32[]{:S(2)}) collective-permute-start(bf16[6,48,128]{2,1,0:T(8,128)(2,1)S(1)} %constant_dynamic-update-slice_fusion.refs_0_), channel_id=1, source_target_pairs={{0,2},{1,3},{2,0},{3,1},{4,6},{5,7},{6,4},{7,5},{8,10},{9,11},{10,... | collective-permute-start | bytes 221192 | tf_op jit(solution)/shard_map/ppermute | solution.py:322
  9.7 4.8 %collective-permute-start.1 = (bf16[6,48,128]{2,1,0:T(8,128)(2,1)S(1)}, bf16[6,48,128]{2,1,0:T(8,128)(2,1)S(1)}, u32[]{:S(2)}, u32[]{:S(2)}) collective-permute-start(bf16[6,48,128]{2,1,0:T(8,128)(2,1)S(1)} %constant_dynamic-update-slice_fusion.refs_0_), channel_id=1, source_target_pairs={{0,4},{1,5},{2,6},{3,7},{4,0},{5,1},{6,2},{7,3},{8,12},{9,13},{10,... | collective-permute-start | bytes 221192 | tf_op jit(solution)/shard_map/ppermute | solution.py:322
  12.3 2.8 %collective-permute-start.6 = (bf16[6,48,128]{2,1,0:T(8,128)(2,1)S(1)}, bf16[6,48,128]{2,1,0:T(8,128)(2,1)S(1)}, u32[]{:S(2)}, u32[]{:S(2)}) collective-permute-start(bf16[6,48,128]{2,1,0:T(8,128)(2,1)S(1)} %collective-permute-done.2.refs_0_), channel_id=1, source_target_pairs={{0,1},{1,0},{2,3},{3,2},{4,5},{5,4},{6,7},{7,6},{8,9},{9,8},{10,11... | collective-permute-start | bytes 221192 | tf_op jit(solution)/shard_map/ppermute | solution.py:322
  13.8 1.3 %collective-permute-start.7 = (bf16[6,48,128]{2,1,0:T(8,128)(2,1)S(1)}, bf16[6,48,128]{2,1,0:T(8,128)(2,1)S(1)}, u32[]{:S(2)}, u32[]{:S(2)}) collective-permute-start(bf16[6,48,128]{2,1,0:T(8,128)(2,1)S(1)} %collective-permute-done.4.refs_1_), channel_id=1, source_target_pairs={{0,1},{1,0},{2,3},{3,2},{4,5},{5,4},{6,7},{7,6},{8,9},{9,8},{10,11... | collective-permute-start | bytes 221192 | tf_op jit(solution)/shard_map/ppermute | solution.py:322
  14.5 1.5 %collective-permute-start.5 = (bf16[6,48,128]{2,1,0:T(8,128)(2,1)S(1)}, bf16[6,48,128]{2,1,0:T(8,128)(2,1)S(1)}, u32[]{:S(2)}, u32[]{:S(2)}) collective-permute-start(bf16[6,48,128]{2,1,0:T(8,128)(2,1)S(1)} %collective-permute-done.1.refs_2_), channel_id=1, source_target_pairs={{0,1},{1,0},{2,3},{3,2},{4,5},{5,4},{6,7},{7,6},{8,9},{9,8},{10,11... | collective-permute-start | bytes 221192 | tf_op jit(solution)/shard_map/ppermute | solution.py:322
  16.5 4.0 %copy-start = (bf16[128,128]{1,0:T(8,128)(2,1)S(1)}, bf16[128,128]{1,0:T(8,128)(2,1)}, u32[]{:S(2)}) copy-start(bf16[128,128]{1,0:T(8,128)(2,1)} %w_out.2) | copy-start | bytes 98308
  16.5 4.0 %copy-start.1 = (bf16[128,128]{1,0:T(8,128)(2,1)S(1)}, bf16[128,128]{1,0:T(8,128)(2,1)}, u32[]{:S(2)}) copy-start(bf16[128,128]{1,0:T(8,128)(2,1)} %w_key.1) | copy-start | bytes 98308
  16.5 4.0 %copy-start.2 = (bf16[128,128]{1,0:T(8,128)(2,1)S(1)}, bf16[128,128]{1,0:T(8,128)(2,1)}, u32[]{:S(2)}) copy-start(bf16[128,128]{1,0:T(8,128)(2,1)} %w_value.1) | copy-start | bytes 98308
  20.5 3.3 %copy-start.3 = (bf16[128,128]{1,0:T(8,128)(2,1)S(1)}, bf16[128,128]{1,0:T(8,128)(2,1)}, u32[]{:S(2)}) copy-start(bf16[128,128]{1,0:T(8,128)(2,1)} %w_query.1) | copy-start | bytes 98308
  20.5 3.3 %copy-start.4 = (bf16[128,128]{1,0:T(8,128)(2,1)S(1)}, bf16[128,128]{1,0:T(8,128)(2,1)}, u32[]{:S(2)}) copy-start(bf16[128,128]{1,0:T(8,128)(2,1)} %w_gate.1) | copy-start | bytes 98308
  20.5 3.3 %copy-start.5 = (bf16[128,128]{1,0:T(8,128)(2,1)S(1)}, bf16[128,128]{1,0:T(8,128)(2,1)}, u32[]{:S(2)}) copy-start(bf16[128,128]{1,0:T(8,128)(2,1)} %w_out.3) | copy-start | bytes 98308
  20.6 3.3 %copy-start.6 = (bf16[128,4]{0,1:T(4,128)(2,1)S(1)}, bf16[128,4]{0,1:T(4,128)(2,1)}, u32[]{:S(2)}) copy-start(bf16[128,4]{0,1:T(4,128)(2,1)} %param.32) | copy-start | bytes 3076

commit v6 on v0

--- a/solution.py
+++ b/solution.py
@@ -1,8 +1,11 @@
+import functools
 import math
 
 import jax
 import jax.numpy as jnp
 from jax import lax
+from jax.experimental import pallas as pl
+from jax.experimental.pallas import tpu as pltpu
 from jax.sharding import PartitionSpec as P
 
 HEADS = 4
@@ -28,7 +31,7 @@
     return jnp.einsum("jhki,kjhd->ijhd", weights, value_cols, preferred_element_type=jnp.float32)
 
 
-def per_device(
+def split_over_devices(
     pair_rep,
     residue_valid,
     tri_norm_gain,
@@ -114,6 +117,496 @@
     return final.astype(jnp.bfloat16)
 
 
+def sigmoid(values):
+    return 0.5 * jnp.tanh(0.5 * values) + 0.5
+
+
+def dot(left, right):
+    return jnp.dot(left, right, preferred_element_type=jnp.float32)
+
+
+def rounded(values):
+    return values.astype(jnp.bfloat16).astype(jnp.float32)
+
+
+def chip_and_core():
+    device = lax.axis_index("row")
+    return lax.shift_right_logical(device, 1), jnp.bitwise_and(device, 1)
+
+
+def rows_of_blocks(row_count, blocks):
+    chip, _ = chip_and_core()
+    return [(jnp.bitwise_xor(chip, bits), r) for bits in blocks for r in range(row_count)]
+
+
+def edges_kernel(row_count, chips, pieces, valid_column, norms, weights, *refs):
+    pair_refs = refs[: len(pieces)]
+    left_ref, right_ref, gate_ref, pairs_ref, send_ref = refs[-5:]
+    f32, bf16 = jnp.float32, jnp.bfloat16
+    res, channels = valid_column.shape
+    _, core = chip_and_core()
+    pairs = jnp.concatenate(
+        [ref[...].astype(f32).reshape(-1, channels) for ref in pair_refs], axis=0
+    )
+    normed = layer_norm(pairs, norms[0:1, :], norms[1:2, :], 1).astype(bf16)
+    column = valid_column[...]
+    rows_of = rows_of_blocks(row_count, [bits for piece in pieces for bits in piece])
+    masks = jnp.concatenate(
+        [
+            column * valid_column[pl.ds((2 * chip + core) * row_count + r, 1), :]
+            for chip, r in rows_of
+        ],
+        axis=0,
+    )
+    joined = dot(normed, weights[:, : 2 * channels])
+    left = rounded(sigmoid(joined[:, channels:]) * joined[:, :channels] * masks)
+    joined = dot(normed, weights[:, 2 * channels : 4 * channels])
+    right = (sigmoid(joined[:, channels:]) * joined[:, :channels] * masks).astype(bf16)
+    gate = sigmoid(dot(normed, weights[:, 4 * channels :]))
+    for n, (chip, r) in enumerate(rows_of):
+        rows = slice(n * res, (n + 1) * res)
+        start = pl.multiple_of((chip * row_count + r) * res, res)
+        send_ref[n] = right[rows]
+        left_ref[pl.ds(start, res), :] = left[rows]
+        place_right(right_ref, row_count, chips, chip, r, right[rows])
+        gate_ref[pl.ds(start, res), :] = gate[rows]
+        pairs_ref[pl.ds(start, res), :] = pairs[rows]
+
+
+def place_right(right_ref, row_count, chips, chip, r, edges):
+    right_ref[pl.ds(r * chips + chip, edges.shape[0], stride=row_count * chips), :] = edges.astype(
+        jnp.float32
+    )
+
+
+def triangle_rows(row_count, chips, left_ref, right_ref, triangle_ref, first, count, core):
+    channels = left_ref.shape[1]
+    columns = row_count * chips
+    res = 2 * columns
+    start = pl.multiple_of(first * res, res)
+    totals = [jnp.zeros((columns, channels), jnp.float32) for _ in range(count)]
+    for k in range(res):
+        right = right_ref[pl.ds(k * columns, columns), :]
+        for n in range(count):
+            totals[n] = totals[n] + left_ref[pl.ds(start + n * res + k, 1), :] * right
+    for n in range(count):
+        for r in range(row_count):
+            triangle_ref[
+                pl.ds(start + n * res + core * row_count + r, chips, stride=2 * row_count), :
+            ] = rounded(totals[n][r * chips : (r + 1) * chips])
+
+
+def near_triangle_kernel(row_count, chips, chunk, pieces, left_ref, right_ref, *refs):
+    received, (triangle_ref, across_ref) = refs[:-2], refs[-2:]
+    _, core = chip_and_core()
+
+    def some_rows(step, carry):
+        first = step * chunk
+        triangle_rows(
+            row_count, chips, left_ref, right_ref, triangle_ref, first, chunk, core
+        )
+        return carry
+
+    for ref, blocks in zip(received, pieces):
+        for n, (chip, r) in enumerate(rows_of_blocks(row_count, blocks)):
+            place_right(across_ref, row_count, chips, chip, r, ref[n])
+    lax.fori_loop(0, row_count * chips // chunk, some_rows, 0)
+
+
+def attention_inputs_kernel(
+    row_count, chips, chunk, part, pieces, norms, w_out, left_ref, gate_ref, pairs_ref, *refs
+):
+    f32, bf16 = jnp.float32, jnp.bfloat16
+    received = refs[: len(pieces)]
+    triangle_ref, across_ref, after_ref, att_ref = refs[-4:]
+    _, core = chip_and_core()
+    half = row_count * chips
+    tall = (half // 2) * 2 * half
+    for ref, blocks in zip(received, pieces):
+        for n, (chip, r) in enumerate(rows_of_blocks(row_count, blocks)):
+            place_right(across_ref, row_count, chips, chip, r, ref[n])
+
+    def some_rows(step, carry):
+        first = part * (half // 2) + step * chunk
+        triangle_rows(
+            row_count, chips, left_ref, across_ref, triangle_ref, first, chunk, 1 - core
+        )
+        return carry
+
+    lax.fori_loop(0, half // 2 // chunk, some_rows, 0)
+    rows = slice(part * tall, (part + 1) * tall)
+    tri_normed = layer_norm(triangle_ref[rows, :], norms[2:3, :], norms[3:4, :], 1).astype(bf16)
+    after_tri = pairs_ref[rows, :] + gate_ref[rows, :] * dot(tri_normed, w_out[...])
+    att_in = layer_norm(after_tri, norms[4:5, :], norms[5:6, :], 1).astype(bf16)
+    after_ref[...] = after_tri
+    att_ref[...] = att_in
+
+
+def column_bias(att_ref, row_count, keys, res, head_bias):
+    bf16, channels = jnp.bfloat16, att_ref.shape[1]
+    row = lax.broadcasted_iota(jnp.int32, (channels, HEADS), 0) // HEAD_DIM
+    head = lax.broadcasted_iota(jnp.int32, (channels, HEADS), 1)
+    repeat = jnp.where(row == head, 1.0, 0.0).astype(bf16)
+    wide_bias = dot(repeat, head_bias[...]).astype(bf16)
+    own = lax.axis_index("row") * row_count
+    for r in range(row_count):
+        column = att_ref[pl.ds(own + r, keys, stride=res), :].astype(bf16)
+        yield rounded(
+            lax.dot_general(
+                column, wide_bias, (((1,), (1,)), ((), ())), preferred_element_type=jnp.float32
+            )
+        )
+
+
+def scores_of_keys(row_count, chips, query, key_ref, bias_ref, valid_column, first, at, core, res):
+    bf16, f32, channels = jnp.bfloat16, jnp.float32, key_ref.shape[1]
+    count = row_count * chips // 2
+    row = lax.broadcasted_iota(jnp.int32, (2 * channels, channels), 0) % channels // HEAD_DIM
+    column = lax.broadcasted_iota(jnp.int32, (2 * channels, channels), 1) // HEAD_DIM
+    same_head = jnp.where(row == column, 1.0, 0.0).astype(bf16)
+    products = []
+    for n in range(count):
+        keys = key_ref[pl.ds(pl.multiple_of((at + n) * res, res), res), :]
+        products.append(jnp.concatenate([keys] * row_count, axis=0) * query)
+    product = jnp.concatenate(products, axis=0)
+    high = product.astype(bf16)
+    low = (product - high.astype(f32)).astype(bf16)
+    scores = dot(jnp.concatenate([high, low], axis=1), same_head)
+    for n in range(count):
+        k = (2 * (first + n // row_count) + core) * row_count + n % row_count
+        key_mask = 1000000000.0 * (valid_column[pl.ds(k, 1), :] - 1.0)
+        for r in range(row_count):
+            score = scores[(n * row_count + r) * res : (n * row_count + r + 1) * res]
+            yield r, n, score + bias_ref[r, pl.ds(at + n, 1), :] + key_mask
+
+
+def most_scores_kernel(
+    row_count,
+    chips,
+    valid_column,
+    w_query,
+    w_gate,
+    w_key,
+    w_value,
+    head_bias,
+    own_att_a,
+    own_att_b,
+    far_att_a,
+    own_after_a,
+    own_after_b,
+    score_ref,
+    maxima_ref,
+    value_ref,
+    query_ref,
+    gate_ref,
+    after_ref,
+    att_ref,
+    key_ref,
+    bias_ref,
+):
+    f32, bf16 = jnp.float32, jnp.bfloat16
+    chip, core = chip_and_core()
+    half = row_count * chips
+    res = 2 * half
+    channels = att_ref.shape[1]
+    tall = half // 2 * res
+    att = [ref[...] for ref in (own_att_a, own_att_b, far_att_a)]
+    key_value = jnp.concatenate([w_key[...], w_value[...]], axis=1)
+    for n, values in enumerate(att):
+        att_ref[n * tall : (n + 1) * tall, :] = values.astype(f32)
+        joined = dot(values, key_value)
+        key_ref[n * tall : (n + 1) * tall, :] = rounded(joined[:, :channels])
+        value_ref[n * tall : (n + 1) * tall, :] = rounded(joined[:, channels:])
+    own = row_count * res
+    own_in = att_ref[pl.ds(pl.multiple_of(chip * own, own), own), :].astype(bf16)
+    query = rounded(dot(own_in, w_query[...])) * (1.0 / math.sqrt(HEAD_DIM))
+    query_ref[...] = query
+    gate_ref[...] = sigmoid(dot(own_in, w_gate[...]))
+    chip_a = pl.multiple_of(jnp.minimum(chip, chips // 2 - 1) * own, own)
+    chip_b = pl.multiple_of(jnp.maximum(chip - chips // 2, 0) * own, own)
+    after_ref[...] = jnp.where(
+        chip < chips // 2, own_after_a[pl.ds(chip_a, own), :], own_after_b[pl.ds(chip_b, own), :]
+    )
+    keys = 3 * half // 2
+    for r, bias in enumerate(column_bias(att_ref, row_count, keys, res, head_bias)):
+        bias_ref[r, :keys, :] = bias
+
+    def scores_of(step, maxima):
+        maxima = list(maxima)
+        at = step * (half // 2)
+        first = lax.rem(step, 2) * (chips // 2)
+        sender = jnp.where(step < 2, core, 1 - core)
+        for r, n, score in scores_of_keys(
+            row_count, chips, query, key_ref, bias_ref, valid_column, first, at, sender, res
+        ):
+            start = pl.multiple_of((r * keys + at + n) * res, res)
+            score_ref[pl.ds(start, res), :] = score
+            maxima[r] = jnp.maximum(maxima[r], score)
+        return tuple(maxima)
+
+    lowest = jnp.full((res, channels), -jnp.inf, f32)
+    maxima = lax.fori_loop(0, 3, scores_of, (lowest,) * row_count)
+    for r in range(row_count):
+        maxima_ref[r] = maxima[r]
+
+
+def attention_kernel(
+    row_count,
+    chips,
+    valid_column,
+    w_key,
+    w_value,
+    w_out,
+    head_bias,
+    far_att_b,
+    score_ref,
+    maxima_ref,
+    value_ref,
+    query_ref,
+    gate_ref,
+    after_ref,
+    out_ref,
+    att_ref,
+    key_ref,
+    bias_ref,
+):
+    f32, bf16 = jnp.float32, jnp.bfloat16
+    _, core = chip_and_core()
+    half = row_count * chips
+    res = 2 * half
+    channels = att_ref.shape[1]
+    key_value = jnp.concatenate([w_key[...], w_value[...]], axis=1)
+    far_att = far_att_b[...]
+    att_ref[...] = far_att.astype(f32)
+    joined = dot(far_att, key_value)
+    key_ref[...] = rounded(joined[:, :channels])
+    last_values = rounded(joined[:, channels:])
+    for r, bias in enumerate(column_bias(att_ref, row_count, half // 2, res, head_bias)):
+        bias_ref[r, : half // 2, :] = bias
+    maxima = [maxima_ref[r] for r in range(row_count)]
+    last_scores = [[] for _ in range(row_count)]
+    for r, _, score in scores_of_keys(
+        row_count,
+        chips,
+        query_ref[...],
+        key_ref,
+        bias_ref,
+        valid_column,
+        chips // 2,
+        0,
+        1 - core,
+        res,
+    ):
+        last_scores[r].append(score)
+        maxima[r] = jnp.maximum(maxima[r], score)
+    keys = 3 * half // 2
+    attended = []
+    for r in range(row_count):
+        total = mixed = jnp.zeros((res, channels), f32)
+        for n in range(half // 2):
+            weight = jnp.exp(last_scores[r][n] - maxima[r])
+            total = total + weight
+            mixed = mixed + weight * last_values[n * res : (n + 1) * res]
+        for n in range(keys):
+            weight = jnp.exp(score_ref[(r * keys + n) * res : (r * keys + n + 1) * res] - maxima[r])
+            total = total + weight
+            mixed = mixed + weight * value_ref[n * res : (n + 1) * res]
+        attended.append(mixed / total)
+    gated = (jnp.concatenate(attended, axis=0) * gate_ref[...]).astype(bf16)
+    final = after_ref[...] + dot(gated, w_out[...])
+    out_ref[...] = final.astype(bf16).reshape(row_count, res, channels)
+
+
+def on_whole_complex(
+    pair_rep,
+    residue_valid,
+    tri_norm_gain,
+    tri_norm_bias,
+    w_edges,
+    w_tri_gate,
+    out_norm_gain,
+    out_norm_bias,
+    w_tri_out,
+    att_norm_gain,
+    att_norm_bias,
+    w_query,
+    w_key,
+    w_value,
+    w_att_gate,
+    w_pair_bias,
+    w_att_out,
+):
+    row_count, res, channels = pair_rep.shape
+    devices = res // row_count
+    chips = devices // 2
+    half = res // 2
+    f32, bf16 = jnp.float32, jnp.bfloat16
+    in_vmem = pl.BlockSpec(memory_space=pltpu.VMEM)
+
+    def shaped(dtype, *shape):
+        return jax.ShapeDtypeStruct(shape, dtype)
+
+    def call(kernel, outs, operands, aliases=None, scratch=(), cost=2**25):
+        return pl.pallas_call(
+            kernel,
+            out_shape=outs,
+            in_specs=[in_vmem] * len(operands),
+            out_specs=jax.tree.map(lambda _: in_vmem, outs),
+            input_output_aliases=aliases or {},
+            scratch_shapes=list(scratch),
+            compiler_params=pltpu.CompilerParams(vmem_limit_bytes=24 * 1024 * 1024),
+            cost_estimate=pl.CostEstimate(flops=2**20, bytes_accessed=cost, transcendentals=0),
+        )(*operands)
+
+    def exchange(values, bit):
+        return lax.ppermute(values, "row", [(d, d ^ bit) for d in range(devices)])
+
+    vectors = (
+        tri_norm_gain,
+        tri_norm_bias,
+        out_norm_gain,
+        out_norm_bias,
+        att_norm_gain,
+        att_norm_bias,
+    )
+    norms = jnp.stack(vectors)
+    edge_weights = jnp.concatenate([w_edges, w_tri_gate], axis=1)
+    valid_column = jnp.broadcast_to(residue_valid.astype(f32)[:, None], (res, channels))
+
+    kept = lax.dynamic_update_slice(
+        jnp.zeros((2 * row_count, res, channels), bf16), pair_rep, (0, 0, 0)
+    )
+    far = exchange(pair_rep, devices // 2)
+    far, kept, norms, edge_weights, valid_column = lax.optimization_barrier(
+        (far, kept, norms, edge_weights, valid_column)
+    )
+    own = lax.dynamic_update_slice(kept, far, (row_count, 0, 0))
+    own_blocks = (0, chips // 2)
+
+    def blocks_from(bits):
+        return tuple(s ^ bits for s in own_blocks)
+
+    edge_shapes = (shaped(f32, half * res, channels),) * 4
+
+    def edges_of(pieces, edges):
+        pairs = tuple(p for p, _ in pieces)
+        blocks = tuple(b for _, b in pieces)
+        sent = shaped(bf16, sum(p.shape[0] for p in pairs), res, channels)
+        operands = (valid_column, norms, edge_weights) + pairs + edges
+        first = len(operands) - len(edges)
+        *edges, right = call(
+            functools.partial(edges_kernel, row_count, chips, blocks),
+            edge_shapes + (sent,),
+            operands,
+            {first + e: e for e in range(len(edges))},
+        )
+        return tuple(edges), (right, sum(blocks, ()))
+
+    diagonal = exchange(own, 6)
+    beside = exchange(own, 2)
+    near = exchange(own, 4)
+    edges, own_right = edges_of([(own, own_blocks)], ())
+    diagonal, edges = lax.optimization_barrier((diagonal, edges))
+    edges, side_right = edges_of(
+        [(diagonal, blocks_from(3)), (beside, blocks_from(1))], edges
+    )
+    near, edges = lax.optimization_barrier((near, edges))
+    edges, near_right = edges_of([(near, blocks_from(2))], edges)
+    received = [(exchange(right, 1), b) for right, b in (own_right, side_right, near_right)]
+
+    left, right, gate, pairs = edges
+    tall = edge_shapes[0]
+    triangle, across = call(
+        functools.partial(
+            near_triangle_kernel, row_count, chips, half // 2, [b for _, b in received[:2]]
+        ),
+        (tall, tall),
+        (left, right) + tuple(r for r, _ in received[:2]),
+    )
+    part = half // 2 * res
+    piece = (shaped(f32, part, channels), shaped(bf16, part, channels))
+
+    def inputs_of(n, fresh, triangle, across):
+        operands = (norms, w_tri_out, left, gate, pairs)
+        operands += tuple(r for r, _ in fresh) + (triangle, across)
+        return call(
+            functools.partial(
+                attention_inputs_kernel, row_count, chips, half // 2, n, [b for _, b in fresh]
+            ),
+            (tall, tall) + piece,
+            operands,
+            {len(operands) - 2: 0, len(operands) - 1: 1},
+        )
+
+    triangle, across, after_a, att_a = inputs_of(0, received[2:], triangle, across)
+    far_att_a = exchange(att_a, 1)
+    triangle, across, after_b, att_b = inputs_of(1, [], triangle, across)
+    far_att_b = exchange(att_b, 1)
+
+    keys = 3 * half // 2
+    own_shape = shaped(f32, row_count * res, channels)
+    scores, maxima, values, query, att_gate, after_own = call(
+        functools.partial(most_scores_kernel, row_count, chips),
+        (
+            shaped(f32, row_count * keys * res, channels),
+            shaped(f32, row_count, res, channels),
+            shaped(f32, keys * res, channels),
+            own_shape,
+            own_shape,
+            own_shape,
+        ),
+        (
+            valid_column,
+            w_query,
+            w_att_gate,
+            w_key,
+            w_value,
+            w_pair_bias.T,
+            att_a,
+            att_b,
+            far_att_a,
+            after_a,
+            after_b,
+        ),
+        scratch=(
+            pltpu.VMEM((keys * res, channels), f32),
+            pltpu.VMEM((keys * res, channels), f32),
+            pltpu.VMEM((row_count, 40, channels), f32),
+        ),
+    )
+    return call(
+        functools.partial(attention_kernel, row_count, chips),
+        shaped(bf16, *pair_rep.shape),
+        (
+            valid_column,
+            w_key,
+            w_value,
+            w_att_out,
+            w_pair_bias.T,
+            far_att_b,
+            scores,
+            maxima,
+            values,
+            query,
+            att_gate,
+            after_own,
+        ),
+        scratch=(
+            pltpu.VMEM((part, channels), f32),
+            pltpu.VMEM((part, channels), f32),
+            pltpu.VMEM((row_count, 16, channels), f32),
+        ),
+    )
+
+
+def per_device(pair_rep, residue_valid, *parameters):
+    row_count, res, channels = pair_rep.shape
+    devices = res // row_count
+    if res % 48 == 0 and devices == 16 and 40 * res * res * channels <= 32 * 1024 * 1024:
+        return on_whole_complex(pair_rep, residue_valid, *parameters)
+    return split_over_devices(pair_rep, residue_valid, *parameters)
+
+
 def solution(mesh):
     return jax.shard_map(
         per_device,

time: 81.8 us -> 25.2 us (0.31)
  blocking collectives: 31.1 us -> 0 us
  waiting for transfers between devices: 18.6 us -> 3.31 us
  Pallas kernels: 0 us -> 9.28 us
  starting transfers between devices: 18 us -> 8.94 us
  local copies, waits for them, and re-layouts: 7.97 us -> 1.65 us
  matrix products: 2.53 us -> 0 us
  other arithmetic: 2.46 us -> 1.6 us
    all_gather x1 -> x0, blocking collectives: 21.8 us -> none  [per_device(): whole_bias = lax.all_gather(pair_bias, 'row', axis=1, tiled=True)]
    all_to_all x4 -> x0, waiting for transfers between devices: 18.6 us -> none  [the longest x1 6.64 us: per_device(): lax.all_to_all(block_product, 'row', split_axis=1, concat_axis=0, tiled=T...]
    all_to_all x4 -> x0, starting transfers between devices: 18 us -> none  [the longest x1 7.36 us: per_device(): lax.all_to_all(left_edges, 'row', split_axis=0, concat_axis=1, tiled=True)]
    all_to_all x1 -> x0, blocking collectives: 9.34 us -> none  [per_device(): lax.all_to_all(gated, 'row', split_axis=0, concat_axis=1, tiled=True)]
    pallas_call x0 -> x8, Pallas kernels: none -> 9.28 us  [call(): pl.pallas_call(kernel, out_shape=outs, in_specs=[in_vmem] * len(operands)...]
    ppermute x0 -> x9, starting transfers between devices: none -> 8.94 us  [exchange(): return lax.ppermute(values, 'row', [(d, d ^ bit) for d in range(devices)])]
    unnamed x40 -> x14, local copies, waits for them, and re-layouts: 6.27 us -> 0.04 us
    ppermute x0 -> x9, waiting for transfers between devices: none -> 3.31 us  [exchange(): return lax.ppermute(values, 'row', [(d, d ^ bit) for d in range(devices)])]
  transfers between devices with their start and end apart: 4 -> 9, of which waited for: 3 -> 3; matrix products, arithmetic and copies ran while one was open for 2% -> 13% of each run, Pallas kernels for 0% -> 24%
where the time goes in v6:
time: 25.2 us; the launch traced here: 25 us
  Pallas kernels  9.28 us (37%)
  starting transfers between devices  8.94 us (35%)
  waiting for transfers between devices  3.31 us (13%)
  local copies, waits for them, and re-layouts  1.65 us (7%)
  other arithmetic  1.6 us (6%)
    pallas_call x8, Pallas kernels, call(): pl.pallas_call(kernel, out_shape=outs, in_specs=[in_vmem] * len(operands)...  9.28 us
    ppermute x9, starting transfers between devices, exchange(): return lax.ppermute(values, 'row', [(d, d ^ bit) for d in range(devices)])  8.94 us
    ppermute x9, waiting for transfers between devices, exchange(): return lax.ppermute(values, 'row', [(d, d ^ bit) for d in range(devices)])  3.31 us
    concatenate x1, other arithmetic, on_whole_complex(): edge_weights = jnp.concatenate([w_edges, w_tri_gate], axis=1)  0.94 us
    dynamic_update_slice x1, local copies, waits for them, and re-layouts, on_whole_complex(): lax.dynamic_update_slice(jnp.zeros((2 * row_count, res, channels), bf16),...  0.78 us
    another operation x1, local copies, waits for them, and re-layouts, on_whole_complex(): norms = jnp.stack(vectors)  0.75 us
    convert_element_type x1, other arithmetic, on_whole_complex(): residue_valid.astype(f32)[:, None]  0.66 us
  transfers between devices with their start and end apart: 9, of which 3 were waited for; matrix products, arithmetic and copies ran while one was open for 13% of the time, Pallas kernels for 24%

profile of v6, /device:TPU:0, one launch (start us, length us, event | category | flops | bytes accessed | tf_op | source)
XLA Modules:
  0.0 25.0 jit_solution(12184775674357083938)
XLA Ops:
  0.0 4.0 %collective-permute-start = (bf16[3,48,128]{2,1,0:T(8,128)(2,1)}, bf16[3,48,128]{2,1,0:T(8,128)(2,1)S(1)}, u32[]{:S(2)}, u32[]{:S(2)}) collective-permute-start(bf16[3,48,128]{2,1,0:T(8,128)(2,1)} %param.17), channel_id=1, source_target_pairs={{0,8},{1,9},{2,10},{3,11},{4,12},{5,13},{6,14},{7,15},{8,0},{9,1},... | collective-permute-start | bytes 110600 | tf_op jit(solution)/shard_map/ppermute | solution.py:462
  4.0 0.9 %pad_maximum_fusion.weights = bf16[128,640]{1,0:T(8,128)(2,1)S(1)} fusion(bf16[128,128]{1,0:T(8,128)(2,1)} %param.22, bf16[128,512]{1,0:T(8,128)(2,1)} %param.21), kind=kLoop, calls=%fused_computation | loop fusion | flops 327680 | bytes 327680 | tf_op jit(solution)/shard_map/concatenate | solution.py:473
  5.0 0.7 %convert_element_type.3 = f32[48]{0:T(128)S(1)} convert(s32[48]{0:T(128)} %param.18) | non-fusion elementwise | flops 48 | bytes 384 | tf_op jit(solution)/shard_map/convert_element_type | solution.py:474
  5.6 0.8 %dynamic_update_slice.6 = bf16[6,48,128]{2,1,0:T(8,128)(2,1)S(1)} pad(bf16[3,48,128]{2,1,0:T(8,128)(2,1)} %param.17, bf16[]{:T(256)} %constant.0.clone.1), padding=0_3x0_0x0_0 | pad | bytes 110594 | tf_op jit(solution)/shard_map/dynamic_update_slice | solution.py:476
  6.4 0.8 %stack.27.norms = f32[6,128]{1,0:T(8,128)S(1)} concatenate(f32[1,128]{1,0:T(1,128)} %bitcast.9, f32[1,128]{1,0:T(1,128)} %bitcast.10, f32[1,128]{1,0:T(1,128)} %bitcast.11, f32[1,128]{1,0:T(1,128)} %bitcast.12, f32[1,128]{1,0:T(1,128)} %bitcast.13, f32[1,128]{1,0:T(1,128)} %bitcast.14), dimensions={0} | concatenate | bytes 6144 | tf_op jit(solution)/shard_map/stack | solution.py:472
  7.3 2.6 %collective-permute-start.2 = (bf16[6,48,128]{2,1,0:T(8,128)(2,1)S(1)}, bf16[6,48,128]{2,1,0:T(8,128)(2,1)S(1)}, u32[]{:S(2)}, u32[]{:S(2)}) collective-permute-start(bf16[6,48,128]{2,1,0:T(8,128)(2,1)S(1)} %constant_dynamic-update-slice_fusion.refs_0_), channel_id=1, source_target_pairs={{0,6},{1,7},{2,4},{3,5},{4,2},{5,3},{6,0},{7,1},{8,14},{9,15},{10,... | collective-permute-start | bytes 221192 | tf_op jit(solution)/shard_map/ppermute | solution.py:462
  9.8 0.5 %collective-permute-start.3 = (bf16[6,48,128]{2,1,0:T(8,128)(2,1)S(1)}, bf16[6,48,128]{2,1,0:T(8,128)(2,1)S(1)}, u32[]{:S(2)}, u32[]{:S(2)}) collective-permute-start(bf16[6,48,128]{2,1,0:T(8,128)(2,1)S(1)} %constant_dynamic-update-slice_fusion.refs_0_), channel_id=1, source_target_pairs={{0,2},{1,3},{2,0},{3,1},{4,6},{5,7},{6,4},{7,5},{8,10},{9,11},{10,... | collective-permute-start | bytes 221192 | tf_op jit(solution)/shard_map/ppermute | solution.py:462
  10.4 0.4 %collective-permute-start.1 = (bf16[6,48,128]{2,1,0:T(8,128)(2,1)S(1)}, bf16[6,48,128]{2,1,0:T(8,128)(2,1)S(1)}, u32[]{:S(2)}, u32[]{:S(2)}) collective-permute-start(bf16[6,48,128]{2,1,0:T(8,128)(2,1)S(1)} %constant_dynamic-update-slice_fusion.refs_0_), channel_id=1, source_target_pairs={{0,4},{1,5},{2,6},{3,7},{4,0},{5,1},{6,2},{7,3},{8,12},{9,13},{10,... | collective-permute-start | bytes 221192 | tf_op jit(solution)/shard_map/ppermute | solution.py:462
  10.8 0.4 %shard_map.163 = (f32[1152,128]{1,0:T(8,128)S(1)}, f32[1152,128]{1,0:T(8,128)S(1)}, f32[1152,128]{1,0:T(8,128)S(1)}, f32[1152,128]{1,0:T(8,128)S(1)}, bf16[6,48,128]{2,1,0:T(8,128)(2,1)S(1)}) custom-call(f32[48,128]{1,0:T(8,128)S(1)} %broadcast_in_dim.2.valid_column, f32[6,128]{1,0:T(8,128)S(1)} %stack.27.norms, ...), custom_call_target="tpu_custom_call" | custom-call | flops 1048576 | bytes 33554432 | tf_op jit(solution)/shard_map/pallas_call | solution.py:450
  11.3 1.4 %collective-permute-done.2.refs_0_ = bf16[6,48,128]{2,1,0:T(8,128)(2,1)S(1)} collective-permute-done((bf16[6,48,128]{2,1,0:T(8,128)(2,1)S(1)}, bf16[6,48,128]{2,1,0:T(8,128)(2,1)S(1)}, u32[]{:S(2)}, u32[]{:S(2)}) %collective-permute-start.2) | collective-permute-done | bytes 73760 | tf_op jit(solution)/shard_map/ppermute | solution.py:462
  12.7 1.5 %collective-permute-done.3.refs_1_ = bf16[6,48,128]{2,1,0:T(8,128)(2,1)S(1)} collective-permute-done((bf16[6,48,128]{2,1,0:T(8,128)(2,1)S(1)}, bf16[6,48,128]{2,1,0:T(8,128)(2,1)S(1)}, u32[]{:S(2)}, u32[]{:S(2)}) %collective-permute-start.3) | collective-permute-done | bytes 73760 | tf_op jit(solution)/shard_map/ppermute | solution.py:462
  14.2 0.6 %shard_map.164 = (f32[1152,128]{1,0:T(8,128)S(1)}, f32[1152,128]{1,0:T(8,128)S(1)}, f32[1152,128]{1,0:T(8,128)S(1)}, f32[1152,128]{1,0:T(8,128)S(1)}, bf16[12,48,128]{2,1,0:T(8,128)(2,1)S(1)}) custom-call(f32[48,128]{1,0:T(8,128)S(1)} %broadcast_in_dim.2.valid_column, ...), custom_call_target="tpu_custom_call", output_to_operand_aliasing={{0}: (5, {}), {1}: (6, {}), {2}: (7, {}), {3}: (8, {})} | custom-call | flops 1048576 | bytes 33554432 | tf_op jit(solution)/shard_map/pallas_call | solution.py:450
  14.8 0.1 collective-permute-start.6
  14.9 0.5 %collective-permute-start.5 = (bf16[6,48,128]{2,1,0:T(8,128)(2,1)S(1)}, bf16[6,48,128]{2,1,0:T(8,128)(2,1)S(1)}, u32[]{:S(2)}, u32[]{:S(2)}) collective-permute-start(bf16[6,48,128]{2,1,0:T(8,128)(2,1)S(1)} %get-tuple-element.77), channel_id=1, source_target_pairs={{0,1},{1,0},{2,3},{3,2},{4,5},{5,4},{6,7},{7,6},{8,9},{9,8},{10,11... | collective-permute-start | bytes 221192 | tf_op jit(solution)/shard_map/ppermute | solution.py:462
  15.4 0.4 %shard_map.165 = (f32[1152,128]{1,0:T(8,128)S(1)}, f32[1152,128]{1,0:T(8,128)S(1)}, f32[1152,128]{1,0:T(8,128)S(1)}, f32[1152,128]{1,0:T(8,128)S(1)}, bf16[6,48,128]{2,1,0:T(8,128)(2,1)S(1)}) custom-call(f32[48,128]{1,0:T(8,128)S(1)} %broadcast_in_dim.2.valid_column, ...), custom_call_target="tpu_custom_call", output_to_operand_aliasing={{0}: (4, {}), {1}: (5, {}), {2}: (6, {}), {3}: (7, {})} | custom-call | flops 1048576 | bytes 33554432 | tf_op jit(solution)/shard_map/pallas_call | solution.py:450
  15.9 0.1 collective-permute-start.4
  16.0 0.4 %collective-permute-done.5.refs_0_ = bf16[6,48,128]{2,1,0:T(8,128)(2,1)S(1)} collective-permute-done((bf16[6,48,128]{2,1,0:T(8,128)(2,1)S(1)}, bf16[6,48,128]{2,1,0:T(8,128)(2,1)S(1)}, u32[]{:S(2)}, u32[]{:S(2)}) %collective-permute-start.5) | collective-permute-done | bytes 73760 | tf_op jit(solution)/shard_map/ppermute | solution.py:462
  16.4 1.4 %shard_map.166 = (f32[1152,128]{1,0:T(8,128)S(1)}, f32[1152,128]{1,0:T(8,128)S(1)}) custom-call(f32[1152,128]{1,0:T(8,128)S(1)} %get-tuple-element.72.left_ref, f32[1152,128]{1,0:T(8,128)S(1)} %get-tuple-element.76.right_ref, bf16[6,48,128]{2,1,0:T(8,128)(2,1)S(1)} %collective-permute-done.5.refs_0_, bf16[12,48,128]{2,1,0:T(8,128)(2,1)S(1)} %collective-permute-done.6.refs_1_), custom_call_target="tpu_custom_call" | custom-call | flops 1048576 | bytes 33554432 | tf_op jit(solution)/shard_map/pallas_call | solution.py:450
  17.9 1.2 %shard_map.167 = (f32[1152,128]{1,0:T(8,128)S(1)}, f32[1152,128]{1,0:T(8,128)S(1)}, f32[576,128]{1,0:T(8,128)S(1)}, bf16[576,128]{1,0:T(8,128)(2,1)S(1)}) custom-call(f32[6,128]{1,0:T(8,128)S(1)} %stack.27.norms, bf16[128,128]{1,0:T(8,128)(2,1)S(1)} %copy-done, ...), custom_call_target="tpu_custom_call", output_to_operand_aliasing={{0}: (6, {}), {1}: (7, {})} | custom-call | flops 1048576 | bytes 33554432 | tf_op jit(solution)/shard_map/pallas_call | solution.py:450
  19.1 0.4 %collective-permute-start.8 = (bf16[576,128]{1,0:T(8,128)(2,1)S(1)}, bf16[576,128]{1,0:T(8,128)(2,1)S(1)}, u32[]{:S(2)}, u32[]{:S(2)}) collective-permute-start(bf16[576,128]{1,0:T(8,128)(2,1)S(1)} %get-tuple-element.84.own_att_a), channel_id=1, source_target_pairs={{0,1},{1,0},{2,3},{3,2},{4,5},{5,4},{6,7},{7,6},{8,9},{9,8},{10,11... | collective-permute-start | bytes 442376 | tf_op jit(solution)/shard_map/ppermute | solution.py:462
  19.5 1.1 %shard_map.168 = (f32[1152,128]{1,0:T(8,128)S(1)}, f32[1152,128]{1,0:T(8,128)S(1)}, f32[576,128]{1,0:T(8,128)S(1)}, bf16[576,128]{1,0:T(8,128)(2,1)S(1)}) custom-call(f32[6,128]{1,0:T(8,128)S(1)} %stack.27.norms, bf16[128,128]{1,0:T(8,128)(2,1)S(1)} %copy-done, ...), custom_call_target="tpu_custom_call", output_to_operand_aliasing={{0}: (5, {}), {1}: (6, {})} | custom-call | flops 1048576 | bytes 33554432 | tf_op jit(solution)/shard_map/pallas_call | solution.py:450
  20.6 0.3 %collective-permute-start.7 = (bf16[576,128]{1,0:T(8,128)(2,1)S(1)}, bf16[576,128]{1,0:T(8,128)(2,1)S(1)}, u32[]{:S(2)}, u32[]{:S(2)}) collective-permute-start(bf16[576,128]{1,0:T(8,128)(2,1)S(1)} %get-tuple-element.83.own_att_b), channel_id=1, source_target_pairs={{0,1},{1,0},{2,3},{3,2},{4,5},{5,4},{6,7},{7,6},{8,9},{9,8},{10,11... | collective-permute-start | bytes 442376 | tf_op jit(solution)/shard_map/ppermute | solution.py:462
  20.9 1.9 %shard_map.169 = (f32[5184,128]{1,0:T(8,128)S(1)}, f32[3,48,128]{2,1,0:T(8,128)S(1)}, f32[1728,128]{1,0:T(8,128)S(1)}, f32[144,128]{1,0:T(8,128)S(1)}, f32[144,128]{1,0:T(8,128)S(1)}, /*index=5*/f32[144,128]{1,0:T(8,128)S(1)}) custom-call(f32[48,128]{1,0:T(8,128)S(1)} %broadcast_in_dim.2.valid_column, bf16[128,128]{1,0:T(8,128)(2,1)S(1)} %copy-done.4, ...), custom_call_target="tpu_custom_call" | custom-call | flops 1048576 | bytes 33554432 | tf_op jit(solution)/shard_map/pallas_call | solution.py:450
  22.8 2.2 %shard_map.170 = bf16[3,48,128]{2,1,0:T(8,128)(2,1)} custom-call(f32[48,128]{1,0:T(8,128)S(1)} %broadcast_in_dim.2.valid_column, bf16[128,128]{1,0:T(8,128)(2,1)S(1)} %copy-done.1, bf16[128,128]{1,0:T(8,128)(2,1)S(1)} %copy-done.2, bf16[128,128]{1,0:T(8,128)(2,1)S(1)} %copy-done.3, bf16[4,128]{1,0:T(4,128)(2,1)S(1)} %bitcast.8, ...), custom_call_target="tpu_custom_call" | custom-call | flops 1048576 | bytes 33554432 | tf_op jit(solution)/shard_map/pallas_call | solution.py:450
  (22 shorter events, 0.1 us)
Async XLA Ops:
  0.0 7.2 %collective-permute-start = (bf16[3,48,128]{2,1,0:T(8,128)(2,1)}, bf16[3,48,128]{2,1,0:T(8,128)(2,1)S(1)}, u32[]{:S(2)}, u32[]{:S(2)}) collective-permute-start(bf16[3,48,128]{2,1,0:T(8,128)(2,1)} %param.17), channel_id=1, source_target_pairs={{0,8},{1,9},{2,10},{3,11},{4,12},{5,13},{6,14},{7,15},{8,0},{9,1},... | collective-permute-start | bytes 110600 | tf_op jit(solution)/shard_map/ppermute | solution.py:462
  7.3 5.4 %collective-permute-start.2 = (bf16[6,48,128]{2,1,0:T(8,128)(2,1)S(1)}, bf16[6,48,128]{2,1,0:T(8,128)(2,1)S(1)}, u32[]{:S(2)}, u32[]{:S(2)}) collective-permute-start(bf16[6,48,128]{2,1,0:T(8,128)(2,1)S(1)} %constant_dynamic-update-slice_fusion.refs_0_), channel_id=1, source_target_pairs={{0,6},{1,7},{2,4},{3,5},{4,2},{5,3},{6,0},{7,1},{8,14},{9,15},{10,... | collective-permute-start | bytes 221192 | tf_op jit(solution)/shard_map/ppermute | solution.py:462
  9.8 4.4 %collective-permute-start.3 = (bf16[6,48,128]{2,1,0:T(8,128)(2,1)S(1)}, bf16[6,48,128]{2,1,0:T(8,128)(2,1)S(1)}, u32[]{:S(2)}, u32[]{:S(2)}) collective-permute-start(bf16[6,48,128]{2,1,0:T(8,128)(2,1)S(1)} %constant_dynamic-update-slice_fusion.refs_0_), channel_id=1, source_target_pairs={{0,2},{1,3},{2,0},{3,1},{4,6},{5,7},{6,4},{7,5},{8,10},{9,11},{10,... | collective-permute-start | bytes 221192 | tf_op jit(solution)/shard_map/ppermute | solution.py:462
  10.4 5.1 %collective-permute-start.1 = (bf16[6,48,128]{2,1,0:T(8,128)(2,1)S(1)}, bf16[6,48,128]{2,1,0:T(8,128)(2,1)S(1)}, u32[]{:S(2)}, u32[]{:S(2)}) collective-permute-start(bf16[6,48,128]{2,1,0:T(8,128)(2,1)S(1)} %constant_dynamic-update-slice_fusion.refs_0_), channel_id=1, source_target_pairs={{0,4},{1,5},{2,6},{3,7},{4,0},{5,1},{6,2},{7,3},{8,12},{9,13},{10,... | collective-permute-start | bytes 221192 | tf_op jit(solution)/shard_map/ppermute | solution.py:462
  14.8 3.0 %copy-start = (bf16[128,128]{1,0:T(8,128)(2,1)S(1)}, bf16[128,128]{1,0:T(8,128)(2,1)}, u32[]{:S(2)}) copy-start(bf16[128,128]{1,0:T(8,128)(2,1)} %w_out.4) | copy-start | bytes 98308
  14.8 1.5 %collective-permute-start.6 = (bf16[12,48,128]{2,1,0:T(8,128)(2,1)S(1)}, bf16[12,48,128]{2,1,0:T(8,128)(2,1)S(1)}, u32[]{:S(2)}, u32[]{:S(2)}) collective-permute-start(bf16[12,48,128]{2,1,0:T(8,128)(2,1)S(1)} %get-tuple-element.78), channel_id=1, source_target_pairs={{0,1},{1,0},{2,3},{3,2},{4,5},{5,4},{6,7},{7,6},{8,9},{9,8},{10,11... | collective-permute-start | bytes 442376 | tf_op jit(solution)/shard_map/ppermute | solution.py:462
  14.9 1.5 %collective-permute-start.5 = (bf16[6,48,128]{2,1,0:T(8,128)(2,1)S(1)}, bf16[6,48,128]{2,1,0:T(8,128)(2,1)S(1)}, u32[]{:S(2)}, u32[]{:S(2)}) collective-permute-start(bf16[6,48,128]{2,1,0:T(8,128)(2,1)S(1)} %get-tuple-element.77), channel_id=1, source_target_pairs={{0,1},{1,0},{2,3},{3,2},{4,5},{5,4},{6,7},{7,6},{8,9},{9,8},{10,11... | collective-permute-start | bytes 221192 | tf_op jit(solution)/shard_map/ppermute | solution.py:462
  15.9 2.0 %collective-permute-start.4 = (bf16[6,48,128]{2,1,0:T(8,128)(2,1)S(1)}, bf16[6,48,128]{2,1,0:T(8,128)(2,1)S(1)}, u32[]{:S(2)}, u32[]{:S(2)}) collective-permute-start(bf16[6,48,128]{2,1,0:T(8,128)(2,1)S(1)} %get-tuple-element.75), channel_id=1, source_target_pairs={{0,1},{1,0},{2,3},{3,2},{4,5},{5,4},{6,7},{7,6},{8,9},{9,8},{10,11... | collective-permute-start | bytes 221192 | tf_op jit(solution)/shard_map/ppermute | solution.py:462
  17.8 3.0 %copy-start.1 = (bf16[128,128]{1,0:T(8,128)(2,1)S(1)}, bf16[128,128]{1,0:T(8,128)(2,1)}, u32[]{:S(2)}) copy-start(bf16[128,128]{1,0:T(8,128)(2,1)} %w_key.3) | copy-start | bytes 98308
  17.9 3.0 %copy-start.2 = (bf16[128,128]{1,0:T(8,128)(2,1)S(1)}, bf16[128,128]{1,0:T(8,128)(2,1)}, u32[]{:S(2)}) copy-start(bf16[128,128]{1,0:T(8,128)(2,1)} %w_value.3) | copy-start | bytes 98308
  17.9 3.0 %copy-start.4 = (bf16[128,128]{1,0:T(8,128)(2,1)S(1)}, bf16[128,128]{1,0:T(8,128)(2,1)}, u32[]{:S(2)}) copy-start(bf16[128,128]{1,0:T(8,128)(2,1)} %w_query.1) | copy-start | bytes 98308
  17.9 3.0 %copy-start.5 = (bf16[128,128]{1,0:T(8,128)(2,1)S(1)}, bf16[128,128]{1,0:T(8,128)(2,1)}, u32[]{:S(2)}) copy-start(bf16[128,128]{1,0:T(8,128)(2,1)} %w_gate.1) | copy-start | bytes 98308
  17.9 3.0 %copy-start.6 = (bf16[128,4]{0,1:T(4,128)(2,1)S(1)}, bf16[128,4]{0,1:T(4,128)(2,1)}, u32[]{:S(2)}) copy-start(bf16[128,4]{0,1:T(4,128)(2,1)} %param.32) | copy-start | bytes 3076
  19.1 3.7 %copy-start.3 = (bf16[128,128]{1,0:T(8,128)(2,1)S(1)}, bf16[128,128]{1,0:T(8,128)(2,1)}, u32[]{:S(2)}) copy-start(bf16[128,128]{1,0:T(8,128)(2,1)} %w_out.5) | copy-start | bytes 98308
  19.1 1.8 %collective-permute-start.8 = (bf16[576,128]{1,0:T(8,128)(2,1)S(1)}, bf16[576,128]{1,0:T(8,128)(2,1)S(1)}, u32[]{:S(2)}, u32[]{:S(2)}) collective-permute-start(bf16[576,128]{1,0:T(8,128)(2,1)S(1)} %get-tuple-element.84.own_att_a), channel_id=1, source_target_pairs={{0,1},{1,0},{2,3},{3,2},{4,5},{5,4},{6,7},{7,6},{8,9},{9,8},{10,11... | collective-permute-start | bytes 442376 | tf_op jit(solution)/shard_map/ppermute | solution.py:462
  20.6 2.2 %collective-permute-start.7 = (bf16[576,128]{1,0:T(8,128)(2,1)S(1)}, bf16[576,128]{1,0:T(8,128)(2,1)S(1)}, u32[]{:S(2)}, u32[]{:S(2)}) collective-permute-start(bf16[576,128]{1,0:T(8,128)(2,1)S(1)} %get-tuple-element.83.own_att_b), channel_id=1, source_target_pairs={{0,1},{1,0},{2,3},{3,2},{4,5},{5,4},{6,7},{7,6},{8,9},{9,8},{10,11... | collective-permute-start | bytes 442376 | tf_op jit(solution)/shard_map/ppermute | solution.py:462

commit v7 on v6

--- a/solution.py
+++ b/solution.py
@@ -139,7 +139,7 @@
     return [(jnp.bitwise_xor(chip, bits), r) for bits in blocks for r in range(row_count)]
 
 
-def edges_kernel(row_count, chips, pieces, valid_column, norms, weights, *refs):
+def edges_kernel(row_count, chips, pieces, send_row, valid_column, norms, weights, *refs):
     pair_refs = refs[: len(pieces)]
     left_ref, right_ref, gate_ref, pairs_ref, send_ref = refs[-5:]
     f32, bf16 = jnp.float32, jnp.bfloat16
@@ -166,17 +166,22 @@
     for n, (chip, r) in enumerate(rows_of):
         rows = slice(n * res, (n + 1) * res)
         start = pl.multiple_of((chip * row_count + r) * res, res)
-        send_ref[n] = right[rows]
+        send_ref[send_row + n] = right[rows]
         left_ref[pl.ds(start, res), :] = left[rows]
-        place_right(right_ref, row_count, chips, chip, r, right[rows])
+        place_right(right_ref, chips, chip, r, right[rows])
         gate_ref[pl.ds(start, res), :] = gate[rows]
         pairs_ref[pl.ds(start, res), :] = pairs[rows]
 
 
-def place_right(right_ref, row_count, chips, chip, r, edges):
-    right_ref[pl.ds(r * chips + chip, edges.shape[0], stride=row_count * chips), :] = edges.astype(
-        jnp.float32
-    )
+def right_strides(res):
+    return 3 * res + 1, 3
+
+
+def place_right(right_ref, chips, chip, r, edges):
+    res = edges.shape[0]
+    column_stride, key_stride = right_strides(res)
+    start = (r * chips + chip) * column_stride
+    right_ref[pl.ds(start, res, stride=key_stride), :] = edges.astype(jnp.float32)
 
 
 def triangle_rows(row_count, chips, left_ref, right_ref, triangle_ref, first, count, core):
@@ -184,9 +189,10 @@
     columns = row_count * chips
     res = 2 * columns
     start = pl.multiple_of(first * res, res)
+    column_stride, key_stride = right_strides(res)
     totals = [jnp.zeros((columns, channels), jnp.float32) for _ in range(count)]
     for k in range(res):
-        right = right_ref[pl.ds(k * columns, columns), :]
+        right = right_ref[pl.ds(k * key_stride, columns, stride=column_stride), :]
         for n in range(count):
             totals[n] = totals[n] + left_ref[pl.ds(start + n * res + k, 1), :] * right
     for n in range(count):
@@ -209,7 +215,7 @@
 
     for ref, blocks in zip(received, pieces):
         for n, (chip, r) in enumerate(rows_of_blocks(row_count, blocks)):
-            place_right(across_ref, row_count, chips, chip, r, ref[n])
+            place_right(across_ref, chips, chip, r, ref[n])
     lax.fori_loop(0, row_count * chips // chunk, some_rows, 0)
 
 
@@ -224,7 +230,7 @@
     tall = (half // 2) * 2 * half
     for ref, blocks in zip(received, pieces):
         for n, (chip, r) in enumerate(rows_of_blocks(row_count, blocks)):
-            place_right(across_ref, row_count, chips, chip, r, ref[n])
+            place_right(across_ref, chips, chip, r, ref[n])
 
     def some_rows(step, carry):
         first = part * (half // 2) + step * chunk
@@ -258,29 +264,63 @@
         )
 
 
-def scores_of_keys(row_count, chips, query, key_ref, bias_ref, valid_column, first, at, core, res):
+def partial_attention(
+    row_count, chips, query, key_ref, value_ref, bias_ref, valid_column, score_ref, halves
+):
     bf16, f32, channels = jnp.bfloat16, jnp.float32, key_ref.shape[1]
+    res = 2 * row_count * chips
     count = row_count * chips // 2
-    row = lax.broadcasted_iota(jnp.int32, (2 * channels, channels), 0) % channels // HEAD_DIM
-    column = lax.broadcasted_iota(jnp.int32, (2 * channels, channels), 1) // HEAD_DIM
+    row = lax.broadcasted_iota(jnp.int32, (2 * channels, 2 * channels), 0) // HEAD_DIM
+    column = lax.broadcasted_iota(jnp.int32, (2 * channels, 2 * channels), 1) // HEAD_DIM
     same_head = jnp.where(row == column, 1.0, 0.0).astype(bf16)
-    products = []
-    for n in range(count):
-        keys = key_ref[pl.ds(pl.multiple_of((at + n) * res, res), res), :]
-        products.append(jnp.concatenate([keys] * row_count, axis=0) * query)
-    product = jnp.concatenate(products, axis=0)
-    high = product.astype(bf16)
-    low = (product - high.astype(f32)).astype(bf16)
-    scores = dot(jnp.concatenate([high, low], axis=1), same_head)
-    for n in range(count):
-        k = (2 * (first + n // row_count) + core) * row_count + n % row_count
-        key_mask = 1000000000.0 * (valid_column[pl.ds(k, 1), :] - 1.0)
-        for r in range(row_count):
-            score = scores[(n * row_count + r) * res : (n * row_count + r + 1) * res]
-            yield r, n, score + bias_ref[r, pl.ds(at + n, 1), :] + key_mask
-
-
-def most_scores_kernel(
+    maxima = [jnp.full((res, channels), -jnp.inf, f32) for _ in range(row_count)]
+    for part, (core, first) in enumerate(halves):
+        products = []
+        for n in range(part * count, (part + 1) * count, 2):
+            pair = [
+                jnp.concatenate([key_ref[m * res : (m + 1) * res, :]] * row_count, axis=0) * query
+                for m in (n, n + 1)
+            ]
+            products.append(jnp.concatenate([p.astype(bf16) for p in pair], axis=1))
+        scores = dot(jnp.concatenate(products, axis=0), same_head)
+        for n in range(count):
+            k = (2 * (first + n // row_count) + core) * row_count + n % row_count
+            key_mask = 1000000000.0 * (valid_column[pl.ds(k, 1), :] - 1.0)
+            at = part * count + n
+            lanes = slice(n % 2 * channels, (n % 2 + 1) * channels)
+            for r in range(row_count):
+                start = (n // 2 * row_count + r) * res
+                score = scores[start : start + res, lanes] + bias_ref[r, at : at + 1, :] + key_mask
+                place = (r * len(halves) * count + at) * res
+                score_ref[place : place + res, :] = score
+                maxima[r] = jnp.maximum(maxima[r], score)
+    totals, mixed = [], []
+    for r in range(row_count):
+        total = mix = jnp.zeros((res, channels), f32)
+        for n in range(len(halves) * count):
+            start = (r * len(halves) * count + n) * res
+            weight = jnp.exp(score_ref[start : start + res, :] - maxima[r])
+            total = total + weight
+            mix = mix + weight * value_ref[n * res : (n + 1) * res, :]
+        totals.append(total)
+        mixed.append(mix)
+    return maxima, totals, mixed
+
+
+def keys_and_values(att, w_key, w_value, att_ref, key_ref, value_ref):
+    channels = att_ref.shape[1]
+    key_value = jnp.concatenate([w_key[...], w_value[...]], axis=1)
+    start = 0
+    for values in att:
+        rows = slice(start, start + values.shape[0])
+        att_ref[rows, :] = values.astype(jnp.float32)
+        joined = dot(values, key_value)
+        key_ref[rows, :] = rounded(joined[:, :channels])
+        value_ref[rows, :] = rounded(joined[:, channels:])
+        start = rows.stop
+
+
+def most_attention_kernel(
     row_count,
     chips,
     valid_column,
@@ -294,29 +334,21 @@
     far_att_a,
     own_after_a,
     own_after_b,
-    score_ref,
-    maxima_ref,
-    value_ref,
+    sums_ref,
     query_ref,
     gate_ref,
     after_ref,
     att_ref,
     key_ref,
+    value_ref,
     bias_ref,
+    score_ref,
 ):
-    f32, bf16 = jnp.float32, jnp.bfloat16
+    bf16 = jnp.bfloat16
     chip, core = chip_and_core()
-    half = row_count * chips
-    res = 2 * half
-    channels = att_ref.shape[1]
-    tall = half // 2 * res
+    res = 2 * row_count * chips
     att = [ref[...] for ref in (own_att_a, own_att_b, far_att_a)]
-    key_value = jnp.concatenate([w_key[...], w_value[...]], axis=1)
-    for n, values in enumerate(att):
-        att_ref[n * tall : (n + 1) * tall, :] = values.astype(f32)
-        joined = dot(values, key_value)
-        key_ref[n * tall : (n + 1) * tall, :] = rounded(joined[:, :channels])
-        value_ref[n * tall : (n + 1) * tall, :] = rounded(joined[:, channels:])
+    keys_and_values(att, w_key, w_value, att_ref, key_ref, value_ref)
     own = row_count * res
     own_in = att_ref[pl.ds(pl.multiple_of(chip * own, own), own), :].astype(bf16)
     query = rounded(dot(own_in, w_query[...])) * (1.0 / math.sqrt(HEAD_DIM))
@@ -327,27 +359,17 @@
     after_ref[...] = jnp.where(
         chip < chips // 2, own_after_a[pl.ds(chip_a, own), :], own_after_b[pl.ds(chip_b, own), :]
     )
-    keys = 3 * half // 2
+    keys = 3 * row_count * chips // 2
     for r, bias in enumerate(column_bias(att_ref, row_count, keys, res, head_bias)):
         bias_ref[r, :keys, :] = bias
-
-    def scores_of(step, maxima):
-        maxima = list(maxima)
-        at = step * (half // 2)
-        first = lax.rem(step, 2) * (chips // 2)
-        sender = jnp.where(step < 2, core, 1 - core)
-        for r, n, score in scores_of_keys(
-            row_count, chips, query, key_ref, bias_ref, valid_column, first, at, sender, res
-        ):
-            start = pl.multiple_of((r * keys + at + n) * res, res)
-            score_ref[pl.ds(start, res), :] = score
-            maxima[r] = jnp.maximum(maxima[r], score)
-        return tuple(maxima)
-
-    lowest = jnp.full((res, channels), -jnp.inf, f32)
-    maxima = lax.fori_loop(0, 3, scores_of, (lowest,) * row_count)
+    halves = ((core, 0), (core, chips // 2), (1 - core, 0))
+    maxima, totals, mixed = partial_attention(
+        row_count, chips, query, key_ref, value_ref, bias_ref, valid_column, score_ref, halves
+    )
     for r in range(row_count):
-        maxima_ref[r] = maxima[r]
+        sums_ref[r, 0] = maxima[r]
+        sums_ref[r, 1] = totals[r]
+        sums_ref[r, 2] = mixed[r]
 
 
 def attention_kernel(
@@ -359,59 +381,43 @@
     w_out,
     head_bias,
     far_att_b,
-    score_ref,
-    maxima_ref,
-    value_ref,
+    sums_ref,
     query_ref,
     gate_ref,
     after_ref,
     out_ref,
     att_ref,
     key_ref,
+    value_ref,
     bias_ref,
+    score_ref,
 ):
-    f32, bf16 = jnp.float32, jnp.bfloat16
+    bf16 = jnp.bfloat16
     _, core = chip_and_core()
-    half = row_count * chips
-    res = 2 * half
+    res = 2 * row_count * chips
     channels = att_ref.shape[1]
-    key_value = jnp.concatenate([w_key[...], w_value[...]], axis=1)
-    far_att = far_att_b[...]
-    att_ref[...] = far_att.astype(f32)
-    joined = dot(far_att, key_value)
-    key_ref[...] = rounded(joined[:, :channels])
-    last_values = rounded(joined[:, channels:])
-    for r, bias in enumerate(column_bias(att_ref, row_count, half // 2, res, head_bias)):
-        bias_ref[r, : half // 2, :] = bias
-    maxima = [maxima_ref[r] for r in range(row_count)]
-    last_scores = [[] for _ in range(row_count)]
-    for r, _, score in scores_of_keys(
+    keys_and_values([far_att_b[...]], w_key, w_value, att_ref, key_ref, value_ref)
+    keys = row_count * chips // 2
+    for r, bias in enumerate(column_bias(att_ref, row_count, keys, res, head_bias)):
+        bias_ref[r, :keys, :] = bias
+    last = partial_attention(
         row_count,
         chips,
         query_ref[...],
         key_ref,
+        value_ref,
         bias_ref,
         valid_column,
-        chips // 2,
-        0,
-        1 - core,
-        res,
-    ):
-        last_scores[r].append(score)
-        maxima[r] = jnp.maximum(maxima[r], score)
-    keys = 3 * half // 2
+        score_ref,
+        ((1 - core, chips // 2),),
+    )
     attended = []
-    for r in range(row_count):
-        total = mixed = jnp.zeros((res, channels), f32)
-        for n in range(half // 2):
-            weight = jnp.exp(last_scores[r][n] - maxima[r])
-            total = total + weight
-            mixed = mixed + weight * last_values[n * res : (n + 1) * res]
-        for n in range(keys):
-            weight = jnp.exp(score_ref[(r * keys + n) * res : (r * keys + n + 1) * res] - maxima[r])
-            total = total + weight
-            mixed = mixed + weight * value_ref[n * res : (n + 1) * res]
-        attended.append(mixed / total)
+    for r, (last_maximum, last_total, last_mixed) in enumerate(zip(*last)):
+        maximum = jnp.maximum(sums_ref[r, 0], last_maximum)
+        most_scale = jnp.exp(sums_ref[r, 0] - maximum)
+        last_scale = jnp.exp(last_maximum - maximum)
+        total = sums_ref[r, 1] * most_scale + last_total * last_scale
+        attended.append((sums_ref[r, 2] * most_scale + last_mixed * last_scale) / total)
     gated = (jnp.concatenate(attended, axis=0) * gate_ref[...]).astype(bf16)
     final = after_ref[...] + dot(gated, w_out[...])
     out_ref[...] = final.astype(bf16).reshape(row_count, res, channels)
@@ -477,51 +483,48 @@
         jnp.zeros((2 * row_count, res, channels), bf16), pair_rep, (0, 0, 0)
     )
     far = exchange(pair_rep, devices // 2)
-    far, kept, norms, edge_weights, valid_column = lax.optimization_barrier(
-        (far, kept, norms, edge_weights, valid_column)
-    )
+    far, kept, norms, edge_weights = lax.optimization_barrier((far, kept, norms, edge_weights))
     own = lax.dynamic_update_slice(kept, far, (row_count, 0, 0))
     own_blocks = (0, chips // 2)
 
     def blocks_from(bits):
         return tuple(s ^ bits for s in own_blocks)
 
-    edge_shapes = (shaped(f32, half * res, channels),) * 4
-
-    def edges_of(pieces, edges):
+    tall = shaped(f32, half * res, channels)
+    spread = shaped(f32, half * right_strides(res)[0], channels)
+
+    def edges_of(pieces, send_row, *held):
         pairs = tuple(p for p, _ in pieces)
         blocks = tuple(b for _, b in pieces)
-        sent = shaped(bf16, sum(p.shape[0] for p in pairs), res, channels)
-        operands = (valid_column, norms, edge_weights) + pairs + edges
-        first = len(operands) - len(edges)
-        *edges, right = call(
-            functools.partial(edges_kernel, row_count, chips, blocks),
-            edge_shapes + (sent,),
+        operands = (valid_column, norms, edge_weights) + pairs + held
+        first = len(operands) - len(held)
+        return call(
+            functools.partial(edges_kernel, row_count, chips, blocks, send_row),
+            (tall, spread, tall, tall, shaped(bf16, 4 * row_count, res, channels)),
             operands,
-            {first + e: e for e in range(len(edges))},
+            {first + e: e for e in range(len(held))},
         )
-        return tuple(edges), (right, sum(blocks, ()))
 
     diagonal = exchange(own, 6)
     beside = exchange(own, 2)
     near = exchange(own, 4)
-    edges, own_right = edges_of([(own, own_blocks)], ())
+    *edges, early_right = edges_of([(own, own_blocks)], 0)
     diagonal, edges = lax.optimization_barrier((diagonal, edges))
-    edges, side_right = edges_of(
-        [(diagonal, blocks_from(3)), (beside, blocks_from(1))], edges
-    )
-    near, edges = lax.optimization_barrier((near, edges))
-    edges, near_right = edges_of([(near, blocks_from(2))], edges)
-    received = [(exchange(right, 1), b) for right, b in (own_right, side_right, near_right)]
+    *edges, early_right = edges_of(
+        [(diagonal, blocks_from(3))], 2 * row_count, *edges, early_right
+    )
+    beside, edges, early_right = lax.optimization_barrier((beside, edges, early_right))
+    early = (exchange(early_right, 1), own_blocks + blocks_from(3))
+    *edges, late_right = edges_of(
+        [(beside, blocks_from(1)), (near, blocks_from(2))], 0, *edges
+    )
+    late = (exchange(late_right, 1), blocks_from(1) + blocks_from(2))
 
     left, right, gate, pairs = edges
-    tall = edge_shapes[0]
     triangle, across = call(
-        functools.partial(
-            near_triangle_kernel, row_count, chips, half // 2, [b for _, b in received[:2]]
-        ),
-        (tall, tall),
-        (left, right) + tuple(r for r, _ in received[:2]),
+        functools.partial(near_triangle_kernel, row_count, chips, half // 2, [early[1]]),
+        (tall, spread),
+        (left, right, early[0]),
     )
     part = half // 2 * res
     piece = (shaped(f32, part, channels), shaped(bf16, part, channels))
@@ -533,28 +536,30 @@
             functools.partial(
                 attention_inputs_kernel, row_count, chips, half // 2, n, [b for _, b in fresh]
             ),
-            (tall, tall) + piece,
+            (tall, spread) + piece,
             operands,
             {len(operands) - 2: 0, len(operands) - 1: 1},
         )
 
-    triangle, across, after_a, att_a = inputs_of(0, received[2:], triangle, across)
+    triangle, across, after_a, att_a = inputs_of(0, [late], triangle, across)
     far_att_a = exchange(att_a, 1)
     triangle, across, after_b, att_b = inputs_of(1, [], triangle, across)
     far_att_b = exchange(att_b, 1)
 
-    keys = 3 * half // 2
     own_shape = shaped(f32, row_count * res, channels)
-    scores, maxima, values, query, att_gate, after_own = call(
-        functools.partial(most_scores_kernel, row_count, chips),
-        (
-            shaped(f32, row_count * keys * res, channels),
-            shaped(f32, row_count, res, channels),
-            shaped(f32, keys * res, channels),
-            own_shape,
-            own_shape,
-            own_shape,
-        ),
+
+    def attention_scratch(keys):
+        return (
+            pltpu.VMEM((keys * res, channels), f32),
+            pltpu.VMEM((keys * res, channels), f32),
+            pltpu.VMEM((keys * res, channels), f32),
+            pltpu.VMEM((row_count, 40, channels), f32),
+            pltpu.VMEM((row_count * keys * res, channels), f32),
+        )
+
+    sums, query, att_gate, after_own = call(
+        functools.partial(most_attention_kernel, row_count, chips),
+        (shaped(f32, row_count, 3, res, channels), own_shape, own_shape, own_shape),
         (
             valid_column,
             w_query,
@@ -568,11 +573,7 @@
             after_a,
             after_b,
         ),
-        scratch=(
-            pltpu.VMEM((keys * res, channels), f32),
-            pltpu.VMEM((keys * res, channels), f32),
-            pltpu.VMEM((row_count, 40, channels), f32),
-        ),
+        scratch=attention_scratch(3 * half // 2),
     )
     return call(
         functools.partial(attention_kernel, row_count, chips),
@@ -584,18 +585,12 @@
             w_att_out,
             w_pair_bias.T,
             far_att_b,
-            scores,
-            maxima,
-            values,
+            sums,
             query,
             att_gate,
             after_own,
         ),
-        scratch=(
-            pltpu.VMEM((part, channels), f32),
-            pltpu.VMEM((part, channels), f32),
-            pltpu.VMEM((row_count, 16, channels), f32),
-        ),
+        scratch=attention_scratch(half // 2),
     )
 
 

time: 25.2 us -> 22.6 us (0.90)
  Pallas kernels: 9.28 us -> 8.27 us
  waiting for transfers between devices: 3.31 us -> 2.41 us
  starting transfers between devices: 8.94 us -> 8.3 us
    pallas_call x8, Pallas kernels: 9.28 us -> 8.27 us  [call(): pl.pallas_call(kernel, out_shape=outs, in_specs=[in_vmem] * len(operands)...]
    ppermute x9 -> x8, waiting for transfers between devices: 3.31 us -> 2.41 us  [exchange(): return lax.ppermute(values, 'row', [(d, d ^ bit) for d in range(devices)])]
    ppermute x9 -> x8, starting transfers between devices: 8.94 us -> 8.3 us  [exchange(): return lax.ppermute(values, 'row', [(d, d ^ bit) for d in range(devices)])]
  transfers between devices with their start and end apart: 9 -> 8, of which waited for: 3 -> 5; matrix products, arithmetic and copies ran while one was open for 13% -> 14% of each run, Pallas kernels for 24% -> 25%
where the time goes in v7:
time: 22.6 us; the launch traced here: 22.4 us
  starting transfers between devices  8.3 us (37%)
  Pallas kernels  8.27 us (37%)
  waiting for transfers between devices  2.41 us (11%)
  local copies, waits for them, and re-layouts  1.65 us (7%)
  other arithmetic  1.6 us (7%)
    ppermute x8, starting transfers between devices, exchange(): return lax.ppermute(values, 'row', [(d, d ^ bit) for d in range(devices)])  8.3 us
    pallas_call x8, Pallas kernels, call(): pl.pallas_call(kernel, out_shape=outs, in_specs=[in_vmem] * len(operands)...  8.27 us
    ppermute x8, waiting for transfers between devices, exchange(): return lax.ppermute(values, 'row', [(d, d ^ bit) for d in range(devices)])  2.41 us
    concatenate x1, other arithmetic, on_whole_complex(): edge_weights = jnp.concatenate([w_edges, w_tri_gate], axis=1)  0.94 us
    dynamic_update_slice x1, local copies, waits for them, and re-layouts, on_whole_complex(): lax.dynamic_update_slice(jnp.zeros((2 * row_count, res, channels), bf16),...  0.78 us
    another operation x1, local copies, waits for them, and re-layouts, on_whole_complex(): norms = jnp.stack(vectors)  0.75 us
    convert_element_type x1, other arithmetic, on_whole_complex(): residue_valid.astype(f32)[:, None]  0.66 us
  transfers between devices with their start and end apart: 8, of which 5 were waited for; matrix products, arithmetic and copies ran while one was open for 14% of the time, Pallas kernels for 25%

profile of v7, /device:TPU:0, one launch (start us, length us, event | category | flops | bytes accessed | tf_op | source)
XLA Modules:
  0.0 22.4 jit_solution(12661655824608933715)
XLA Ops:
  0.0 4.0 %collective-permute-start = (bf16[3,48,128]{2,1,0:T(8,128)(2,1)}, bf16[3,48,128]{2,1,0:T(8,128)(2,1)S(1)}, u32[]{:S(2)}, u32[]{:S(2)}) collective-permute-start(bf16[3,48,128]{2,1,0:T(8,128)(2,1)} %param.17), channel_id=1, source_target_pairs={{0,8},{1,9},{2,10},{3,11},{4,12},{5,13},{6,14},{7,15},{8,0},{9,1},... | collective-permute-start | bytes 110600 | tf_op jit(solution)/shard_map/ppermute | solution.py:468
  4.0 0.9 %pad_maximum_fusion.weights = bf16[128,640]{1,0:T(8,128)(2,1)S(1)} fusion(bf16[128,128]{1,0:T(8,128)(2,1)} %param.22, bf16[128,512]{1,0:T(8,128)(2,1)} %param.21), kind=kLoop, calls=%fused_computation | loop fusion | flops 327680 | bytes 327680 | tf_op jit(solution)/shard_map/concatenate | solution.py:479
  5.0 0.8 %dynamic_update_slice.6 = bf16[6,48,128]{2,1,0:T(8,128)(2,1)S(1)} pad(bf16[3,48,128]{2,1,0:T(8,128)(2,1)} %param.17, bf16[]{:T(256)} %constant.0.clone.1), padding=0_3x0_0x0_0 | pad | bytes 110594 | tf_op jit(solution)/shard_map/dynamic_update_slice | solution.py:482
  5.8 0.8 %stack.27.norms = f32[6,128]{1,0:T(8,128)S(1)} concatenate(f32[1,128]{1,0:T(1,128)} %bitcast.9, f32[1,128]{1,0:T(1,128)} %bitcast.10, f32[1,128]{1,0:T(1,128)} %bitcast.11, f32[1,128]{1,0:T(1,128)} %bitcast.12, f32[1,128]{1,0:T(1,128)} %bitcast.13, f32[1,128]{1,0:T(1,128)} %bitcast.14), dimensions={0} | concatenate | bytes 6144 | tf_op jit(solution)/shard_map/stack | solution.py:478
  6.6 2.5 %collective-permute-start.2 = (bf16[6,48,128]{2,1,0:T(8,128)(2,1)S(1)}, bf16[6,48,128]{2,1,0:T(8,128)(2,1)S(1)}, u32[]{:S(2)}, u32[]{:S(2)}) collective-permute-start(bf16[6,48,128]{2,1,0:T(8,128)(2,1)S(1)} %constant_dynamic-update-slice_fusion.refs_0_), channel_id=1, source_target_pairs={{0,6},{1,7},{2,4},{3,5},{4,2},{5,3},{6,0},{7,1},{8,14},{9,15},{10,... | collective-permute-start | bytes 221192 | tf_op jit(solution)/shard_map/ppermute | solution.py:468
  9.1 0.5 %collective-permute-start.1 = (bf16[6,48,128]{2,1,0:T(8,128)(2,1)S(1)}, bf16[6,48,128]{2,1,0:T(8,128)(2,1)S(1)}, u32[]{:S(2)}, u32[]{:S(2)}) collective-permute-start(bf16[6,48,128]{2,1,0:T(8,128)(2,1)S(1)} %constant_dynamic-update-slice_fusion.refs_0_), channel_id=1, source_target_pairs={{0,2},{1,3},{2,0},{3,1},{4,6},{5,7},{6,4},{7,5},{8,10},{9,11},{10,... | collective-permute-start | bytes 221192 | tf_op jit(solution)/shard_map/ppermute | solution.py:468
  9.6 0.5 %collective-permute-start.3 = (bf16[6,48,128]{2,1,0:T(8,128)(2,1)S(1)}, bf16[6,48,128]{2,1,0:T(8,128)(2,1)S(1)}, u32[]{:S(2)}, u32[]{:S(2)}) collective-permute-start(bf16[6,48,128]{2,1,0:T(8,128)(2,1)S(1)} %constant_dynamic-update-slice_fusion.refs_0_), channel_id=1, source_target_pairs={{0,4},{1,5},{2,6},{3,7},{4,0},{5,1},{6,2},{7,3},{8,12},{9,13},{10,... | collective-permute-start | bytes 221192 | tf_op jit(solution)/shard_map/ppermute | solution.py:468
  10.1 0.7 %convert_element_type.3 = f32[48]{0:T(128)S(1)} convert(s32[48]{0:T(128)} %param.18) | non-fusion elementwise | flops 48 | bytes 384 | tf_op jit(solution)/shard_map/convert_element_type | solution.py:480
  10.8 0.1 broadcast_in_dim.2.valid_column
  10.9 0.4 %shard_map.163 = (f32[1152,128]{1,0:T(8,128)S(1)}, f32[3480,128]{1,0:T(8,128)S(1)}, f32[1152,128]{1,0:T(8,128)S(1)}, f32[1152,128]{1,0:T(8,128)S(1)}, bf16[12,48,128]{2,1,0:T(8,128)(2,1)S(1)}) custom-call(f32[48,128]{1,0:T(8,128)S(1)} %broadcast_in_dim.2.valid_column, f32[6,128]{1,0:T(8,128)S(1)} %stack.27.norms, ...), custom_call_target="tpu_custom_call" | custom-call | flops 1048576 | bytes 33554432 | tf_op jit(solution)/shard_map/pallas_call | solution.py:456
  11.3 0.7 %collective-permute-done.2.refs_0_ = bf16[6,48,128]{2,1,0:T(8,128)(2,1)S(1)} collective-permute-done((bf16[6,48,128]{2,1,0:T(8,128)(2,1)S(1)}, bf16[6,48,128]{2,1,0:T(8,128)(2,1)S(1)}, u32[]{:S(2)}, u32[]{:S(2)}) %collective-permute-start.2) | collective-permute-done | bytes 73760 | tf_op jit(solution)/shard_map/ppermute | solution.py:468
  12.0 0.4 %shard_map.164 = (f32[1152,128]{1,0:T(8,128)S(1)}, f32[3480,128]{1,0:T(8,128)S(1)}, f32[1152,128]{1,0:T(8,128)S(1)}, f32[1152,128]{1,0:T(8,128)S(1)}, bf16[12,48,128]{2,1,0:T(8,128)(2,1)S(1)}) custom-call(f32[48,128]{1,0:T(8,128)S(1)} %broadcast_in_dim.2.valid_column, ...), custom_call_target="tpu_custom_call", output_to_operand_aliasing={{0}: (4, {}), {1}: (5, {}), {2}: (6, {}), {3}: (7, {}), {4}... | custom-call | flops 1048576 | bytes 33554432 | tf_op jit(solution)/shard_map/pallas_call | solution.py:456
  12.4 1.0 %collective-permute-done.1.refs_0_ = bf16[6,48,128]{2,1,0:T(8,128)(2,1)S(1)} collective-permute-done((bf16[6,48,128]{2,1,0:T(8,128)(2,1)S(1)}, bf16[6,48,128]{2,1,0:T(8,128)(2,1)S(1)}, u32[]{:S(2)}, u32[]{:S(2)}) %collective-permute-start.1) | collective-permute-done | bytes 73760 | tf_op jit(solution)/shard_map/ppermute | solution.py:468
  13.5 0.5 %collective-permute-done.3.refs_1_ = bf16[6,48,128]{2,1,0:T(8,128)(2,1)S(1)} collective-permute-done((bf16[6,48,128]{2,1,0:T(8,128)(2,1)S(1)}, bf16[6,48,128]{2,1,0:T(8,128)(2,1)S(1)}, u32[]{:S(2)}, u32[]{:S(2)}) %collective-permute-start.3) | collective-permute-done | bytes 73760 | tf_op jit(solution)/shard_map/ppermute | solution.py:468
  14.0 0.6 %shard_map.165 = (f32[1152,128]{1,0:T(8,128)S(1)}, f32[3480,128]{1,0:T(8,128)S(1)}, f32[1152,128]{1,0:T(8,128)S(1)}, f32[1152,128]{1,0:T(8,128)S(1)}, bf16[12,48,128]{2,1,0:T(8,128)(2,1)S(1)}) custom-call(f32[48,128]{1,0:T(8,128)S(1)} %broadcast_in_dim.2.valid_column, ...), custom_call_target="tpu_custom_call", output_to_operand_aliasing={{0}: (5, {}), {1}: (6, {}), {2}: (7, {}), {3}: (8, {})} | custom-call | flops 1048576 | bytes 33554432 | tf_op jit(solution)/shard_map/pallas_call | solution.py:456
  14.6 0.1 collective-permute-start.4
  14.7 0.1 collective-permute-done.5.refs_0_
  14.8 1.4 %shard_map.166 = (f32[1152,128]{1,0:T(8,128)S(1)}, f32[3480,128]{1,0:T(8,128)S(1)}) custom-call(f32[1152,128]{1,0:T(8,128)S(1)} %get-tuple-element.71.left_ref, f32[3480,128]{1,0:T(8,128)S(1)} %get-tuple-element.75.right_ref, bf16[12,48,128]{2,1,0:T(8,128)(2,1)S(1)} %collective-permute-done.5.refs_0_), custom_call_target="tpu_custom_call" | custom-call | flops 1048576 | bytes 33554432 | tf_op jit(solution)/shard_map/pallas_call | solution.py:456
  16.3 1.1 %shard_map.167 = (f32[1152,128]{1,0:T(8,128)S(1)}, f32[3480,128]{1,0:T(8,128)S(1)}, f32[576,128]{1,0:T(8,128)S(1)}, bf16[576,128]{1,0:T(8,128)(2,1)S(1)}) custom-call(f32[6,128]{1,0:T(8,128)S(1)} %stack.27.norms, bf16[128,128]{1,0:T(8,128)(2,1)S(1)} %copy-done, ...), custom_call_target="tpu_custom_call", output_to_operand_aliasing={{0}: (6, {}), {1}: (7, {})} | custom-call | flops 1048576 | bytes 33554432 | tf_op jit(solution)/shard_map/pallas_call | solution.py:456
  17.4 0.5 %collective-permute-start.7 = (bf16[576,128]{1,0:T(8,128)(2,1)S(1)}, bf16[576,128]{1,0:T(8,128)(2,1)S(1)}, u32[]{:S(2)}, u32[]{:S(2)}) collective-permute-start(bf16[576,128]{1,0:T(8,128)(2,1)S(1)} %get-tuple-element.82.own_att_a), channel_id=1, source_target_pairs={{0,1},{1,0},{2,3},{3,2},{4,5},{5,4},{6,7},{7,6},{8,9},{9,8},{10,11... | collective-permute-start | bytes 442376 | tf_op jit(solution)/shard_map/ppermute | solution.py:468
  17.9 1.1 %shard_map.168 = (f32[1152,128]{1,0:T(8,128)S(1)}, f32[3480,128]{1,0:T(8,128)S(1)}, f32[576,128]{1,0:T(8,128)S(1)}, bf16[576,128]{1,0:T(8,128)(2,1)S(1)}) custom-call(f32[6,128]{1,0:T(8,128)S(1)} %stack.27.norms, bf16[128,128]{1,0:T(8,128)(2,1)S(1)} %copy-done, ...), custom_call_target="tpu_custom_call", output_to_operand_aliasing={{0}: (5, {}), {1}: (6, {})} | custom-call | flops 1048576 | bytes 33554432 | tf_op jit(solution)/shard_map/pallas_call | solution.py:456
  19.0 0.2 collective-permute-start.6
  19.2 1.6 %shard_map.169 = (f32[3,3,48,128]{3,2,1,0:T(8,128)S(1)}, f32[144,128]{1,0:T(8,128)S(1)}, f32[144,128]{1,0:T(8,128)S(1)}, f32[144,128]{1,0:T(8,128)S(1)}) custom-call(f32[48,128]{1,0:T(8,128)S(1)} %broadcast_in_dim.2.valid_column, bf16[128,128]{1,0:T(8,128)(2,1)S(1)} %copy-done.3, bf16[128,128]{1,0:T(8,128)(2,1)S(1)} %copy-done.4, ...), custom_call_target="tpu_custom_call" | custom-call | flops 1048576 | bytes 33554432 | tf_op jit(solution)/shard_map/pallas_call | solution.py:456
  20.9 1.5 %shard_map.170 = bf16[3,48,128]{2,1,0:T(8,128)(2,1)} custom-call(f32[48,128]{1,0:T(8,128)S(1)} %broadcast_in_dim.2.valid_column, bf16[128,128]{1,0:T(8,128)(2,1)S(1)} %copy-done.1, bf16[128,128]{1,0:T(8,128)(2,1)S(1)} %copy-done.2, bf16[128,128]{1,0:T(8,128)(2,1)S(1)} %copy-done.5, bf16[4,128]{1,0:T(4,128)(2,1)S(1)} %bitcast.8, ...), custom_call_target="tpu_custom_call" | custom-call | flops 1048576 | bytes 33554432 | tf_op jit(solution)/shard_map/pallas_call | solution.py:456
  (20 shorter events, 0.1 us)
Async XLA Ops:
  0.0 6.6 %collective-permute-start = (bf16[3,48,128]{2,1,0:T(8,128)(2,1)}, bf16[3,48,128]{2,1,0:T(8,128)(2,1)S(1)}, u32[]{:S(2)}, u32[]{:S(2)}) collective-permute-start(bf16[3,48,128]{2,1,0:T(8,128)(2,1)} %param.17), channel_id=1, source_target_pairs={{0,8},{1,9},{2,10},{3,11},{4,12},{5,13},{6,14},{7,15},{8,0},{9,1},... | collective-permute-start | bytes 110600 | tf_op jit(solution)/shard_map/ppermute | solution.py:468
  6.6 5.4 %collective-permute-start.2 = (bf16[6,48,128]{2,1,0:T(8,128)(2,1)S(1)}, bf16[6,48,128]{2,1,0:T(8,128)(2,1)S(1)}, u32[]{:S(2)}, u32[]{:S(2)}) collective-permute-start(bf16[6,48,128]{2,1,0:T(8,128)(2,1)S(1)} %constant_dynamic-update-slice_fusion.refs_0_), channel_id=1, source_target_pairs={{0,6},{1,7},{2,4},{3,5},{4,2},{5,3},{6,0},{7,1},{8,14},{9,15},{10,... | collective-permute-start | bytes 221192 | tf_op jit(solution)/shard_map/ppermute | solution.py:468
  9.1 4.4 %collective-permute-start.1 = (bf16[6,48,128]{2,1,0:T(8,128)(2,1)S(1)}, bf16[6,48,128]{2,1,0:T(8,128)(2,1)S(1)}, u32[]{:S(2)}, u32[]{:S(2)}) collective-permute-start(bf16[6,48,128]{2,1,0:T(8,128)(2,1)S(1)} %constant_dynamic-update-slice_fusion.refs_0_), channel_id=1, source_target_pairs={{0,2},{1,3},{2,0},{3,1},{4,6},{5,7},{6,4},{7,5},{8,10},{9,11},{10,... | collective-permute-start | bytes 221192 | tf_op jit(solution)/shard_map/ppermute | solution.py:468
  9.6 4.4 %collective-permute-start.3 = (bf16[6,48,128]{2,1,0:T(8,128)(2,1)S(1)}, bf16[6,48,128]{2,1,0:T(8,128)(2,1)S(1)}, u32[]{:S(2)}, u32[]{:S(2)}) collective-permute-start(bf16[6,48,128]{2,1,0:T(8,128)(2,1)S(1)} %constant_dynamic-update-slice_fusion.refs_0_), channel_id=1, source_target_pairs={{0,4},{1,5},{2,6},{3,7},{4,0},{5,1},{6,2},{7,3},{8,12},{9,13},{10,... | collective-permute-start | bytes 221192 | tf_op jit(solution)/shard_map/ppermute | solution.py:468
  13.5 1.4 %collective-permute-start.5 = (bf16[12,48,128]{2,1,0:T(8,128)(2,1)S(1)}, bf16[12,48,128]{2,1,0:T(8,128)(2,1)S(1)}, u32[]{:S(2)}, u32[]{:S(2)}) collective-permute-start(bf16[12,48,128]{2,1,0:T(8,128)(2,1)S(1)} %get-tuple-element.76), channel_id=1, source_target_pairs={{0,1},{1,0},{2,3},{3,2},{4,5},{5,4},{6,7},{7,6},{8,9},{9,8},{10,11... | collective-permute-start | bytes 442376 | tf_op jit(solution)/shard_map/ppermute | solution.py:468
  14.6 1.6 %copy-start = (bf16[128,128]{1,0:T(8,128)(2,1)S(1)}, bf16[128,128]{1,0:T(8,128)(2,1)}, u32[]{:S(2)}) copy-start(bf16[128,128]{1,0:T(8,128)(2,1)} %w_out.4) | copy-start | bytes 98308
  14.6 1.6 %collective-permute-start.4 = (bf16[12,48,128]{2,1,0:T(8,128)(2,1)S(1)}, bf16[12,48,128]{2,1,0:T(8,128)(2,1)S(1)}, u32[]{:S(2)}, u32[]{:S(2)}) collective-permute-start(bf16[12,48,128]{2,1,0:T(8,128)(2,1)S(1)} %get-tuple-element.74), channel_id=1, source_target_pairs={{0,1},{1,0},{2,3},{3,2},{4,5},{5,4},{6,7},{7,6},{8,9},{9,8},{10,11... | collective-permute-start | bytes 442376 | tf_op jit(solution)/shard_map/ppermute | solution.py:468
  17.4 1.8 %collective-permute-start.7 = (bf16[576,128]{1,0:T(8,128)(2,1)S(1)}, bf16[576,128]{1,0:T(8,128)(2,1)S(1)}, u32[]{:S(2)}, u32[]{:S(2)}) collective-permute-start(bf16[576,128]{1,0:T(8,128)(2,1)S(1)} %get-tuple-element.82.own_att_a), channel_id=1, source_target_pairs={{0,1},{1,0},{2,3},{3,2},{4,5},{5,4},{6,7},{7,6},{8,9},{9,8},{10,11... | collective-permute-start | bytes 442376 | tf_op jit(solution)/shard_map/ppermute | solution.py:468
  17.9 1.3 %copy-start.1 = (bf16[128,128]{1,0:T(8,128)(2,1)S(1)}, bf16[128,128]{1,0:T(8,128)(2,1)}, u32[]{:S(2)}) copy-start(bf16[128,128]{1,0:T(8,128)(2,1)} %w_key.3) | copy-start | bytes 98308
  17.9 1.3 %copy-start.2 = (bf16[128,128]{1,0:T(8,128)(2,1)S(1)}, bf16[128,128]{1,0:T(8,128)(2,1)}, u32[]{:S(2)}) copy-start(bf16[128,128]{1,0:T(8,128)(2,1)} %w_value.3) | copy-start | bytes 98308
  17.9 1.3 %copy-start.3 = (bf16[128,128]{1,0:T(8,128)(2,1)S(1)}, bf16[128,128]{1,0:T(8,128)(2,1)}, u32[]{:S(2)}) copy-start(bf16[128,128]{1,0:T(8,128)(2,1)} %w_query.1) | copy-start | bytes 98308
  17.9 1.3 %copy-start.4 = (bf16[128,128]{1,0:T(8,128)(2,1)S(1)}, bf16[128,128]{1,0:T(8,128)(2,1)}, u32[]{:S(2)}) copy-start(bf16[128,128]{1,0:T(8,128)(2,1)} %w_gate.1) | copy-start | bytes 98308
  17.9 1.3 %copy-start.6 = (bf16[128,4]{0,1:T(4,128)(2,1)S(1)}, bf16[128,4]{0,1:T(4,128)(2,1)}, u32[]{:S(2)}) copy-start(bf16[128,4]{0,1:T(4,128)(2,1)} %param.32) | copy-start | bytes 3076
  17.9 3.0 %copy-start.5 = (bf16[128,128]{1,0:T(8,128)(2,1)S(1)}, bf16[128,128]{1,0:T(8,128)(2,1)}, u32[]{:S(2)}) copy-start(bf16[128,128]{1,0:T(8,128)(2,1)} %w_out.5) | copy-start | bytes 98308
  19.0 1.9 %collective-permute-start.6 = (bf16[576,128]{1,0:T(8,128)(2,1)S(1)}, bf16[576,128]{1,0:T(8,128)(2,1)S(1)}, u32[]{:S(2)}, u32[]{:S(2)}) collective-permute-start(bf16[576,128]{1,0:T(8,128)(2,1)S(1)} %get-tuple-element.81.own_att_b), channel_id=1, source_target_pairs={{0,1},{1,0},{2,3},{3,2},{4,5},{5,4},{6,7},{7,6},{8,9},{9,8},{10,11... | collective-permute-start | bytes 442376 | tf_op jit(solution)/shard_map/ppermute | solution.py:468

commit v8 on v7

--- a/solution.py
+++ b/solution.py
@@ -141,7 +141,14 @@
 
 def edges_kernel(row_count, chips, pieces, send_row, valid_column, norms, weights, *refs):
     pair_refs = refs[: len(pieces)]
-    left_ref, right_ref, gate_ref, pairs_ref, send_ref = refs[-5:]
+    if send_row or len(pieces) > 1:
+        left_ref, right_ref, gate_ref, pairs_ref, send_ref = refs[-5:]
+    else:
+        left_ref, right_ref, gate_ref, pairs_ref, send_ref, same_head_ref = refs[-6:]
+        wide = same_head_ref.shape
+        row = lax.broadcasted_iota(jnp.int32, wide, 0) // HEAD_DIM
+        column = lax.broadcasted_iota(jnp.int32, wide, 1) // HEAD_DIM
+        same_head_ref[...] = jnp.where(row == column, 1.0, 0.0).astype(jnp.bfloat16)
     f32, bf16 = jnp.float32, jnp.bfloat16
     res, channels = valid_column.shape
     _, core = chip_and_core()
@@ -173,33 +180,41 @@
         pairs_ref[pl.ds(start, res), :] = pairs[rows]
 
 
-def right_strides(res):
-    return 3 * res + 1, 3
-
-
 def place_right(right_ref, chips, chip, r, edges):
     res = edges.shape[0]
-    column_stride, key_stride = right_strides(res)
-    start = (r * chips + chip) * column_stride
-    right_ref[pl.ds(start, res, stride=key_stride), :] = edges.astype(jnp.float32)
+    start = pl.multiple_of((r * chips + chip) * res, res)
+    right_ref[pl.ds(start, res), :] = edges.astype(jnp.float32)
+
+
+def sum_sublanes(parts):
+    row = lax.broadcasted_iota(jnp.int32, parts[0].shape, 0)
+    for shift in (1, 2, 4):
+        high = jnp.bitwise_and(row, shift) > 0
+        parts = [
+            jnp.where(high, odd, even) + pltpu.roll(jnp.where(high, even, odd), shift, 0)
+            for even, odd in zip(parts[0::2], parts[1::2])
+        ]
+    return parts[0]
 
 
 def triangle_rows(row_count, chips, left_ref, right_ref, triangle_ref, first, count, core):
-    channels = left_ref.shape[1]
-    columns = row_count * chips
-    res = 2 * columns
+    res = 2 * row_count * chips
     start = pl.multiple_of(first * res, res)
-    column_stride, key_stride = right_strides(res)
-    totals = [jnp.zeros((columns, channels), jnp.float32) for _ in range(count)]
-    for k in range(res):
-        right = right_ref[pl.ds(k * key_stride, columns, stride=column_stride), :]
+    lefts = [left_ref[pl.ds(start + n * res, res), :] for n in range(count)]
+    for r in range(row_count):
+        parts = [[] for _ in range(count)]
+        for chip in range(chips):
+            at = (r * chips + chip) * res
+            right = right_ref[at : at + res, :]
+            for n in range(count):
+                product = lefts[n] * right
+                parts[n].append(
+                    sum(product[k : k + 8] for k in range(8, res, 8)) + product[:8]
+                )
         for n in range(count):
-            totals[n] = totals[n] + left_ref[pl.ds(start + n * res + k, 1), :] * right
-    for n in range(count):
-        for r in range(row_count):
             triangle_ref[
                 pl.ds(start + n * res + core * row_count + r, chips, stride=2 * row_count), :
-            ] = rounded(totals[n][r * chips : (r + 1) * chips])
+            ] = rounded(sum_sublanes(parts[n]))
 
 
 def near_triangle_kernel(row_count, chips, chunk, pieces, left_ref, right_ref, *refs):
@@ -219,28 +234,30 @@
     lax.fori_loop(0, row_count * chips // chunk, some_rows, 0)
 
 
-def attention_inputs_kernel(
-    row_count, chips, chunk, part, pieces, norms, w_out, left_ref, gate_ref, pairs_ref, *refs
+def attention_inputs(
+    row_count, chips, chunk, first, norms, w_out, left_ref, gate_ref, pairs_ref, refs
 ):
     f32, bf16 = jnp.float32, jnp.bfloat16
-    received = refs[: len(pieces)]
-    triangle_ref, across_ref, after_ref, att_ref = refs[-4:]
+    triangle_ref, across_ref, after_ref, att_ref = refs
     _, core = chip_and_core()
     half = row_count * chips
     tall = (half // 2) * 2 * half
-    for ref, blocks in zip(received, pieces):
-        for n, (chip, r) in enumerate(rows_of_blocks(row_count, blocks)):
-            place_right(across_ref, chips, chip, r, ref[n])
 
     def some_rows(step, carry):
-        first = part * (half // 2) + step * chunk
         triangle_rows(
-            row_count, chips, left_ref, across_ref, triangle_ref, first, chunk, 1 - core
+            row_count,
+            chips,
+            left_ref,
+            across_ref,
+            triangle_ref,
+            first + step * chunk,
+            chunk,
+            1 - core,
         )
         return carry
 
     lax.fori_loop(0, half // 2 // chunk, some_rows, 0)
-    rows = slice(part * tall, (part + 1) * tall)
+    rows = pl.ds(pl.multiple_of(first * 2 * half, tall), tall)
     tri_normed = layer_norm(triangle_ref[rows, :], norms[2:3, :], norms[3:4, :], 1).astype(bf16)
     after_tri = pairs_ref[rows, :] + gate_ref[rows, :] * dot(tri_normed, w_out[...])
     att_in = layer_norm(after_tri, norms[4:5, :], norms[5:6, :], 1).astype(bf16)
@@ -248,41 +265,100 @@
     att_ref[...] = att_in
 
 
-def column_bias(att_ref, row_count, keys, res, head_bias):
-    bf16, channels = jnp.bfloat16, att_ref.shape[1]
-    row = lax.broadcasted_iota(jnp.int32, (channels, HEADS), 0) // HEAD_DIM
-    head = lax.broadcasted_iota(jnp.int32, (channels, HEADS), 1)
-    repeat = jnp.where(row == head, 1.0, 0.0).astype(bf16)
-    wide_bias = dot(repeat, head_bias[...]).astype(bf16)
+def first_chip(chips, part):
+    chip, _ = chip_and_core()
+    return jnp.bitwise_xor(jnp.bitwise_and(chip, chips // 2), part * (chips // 2))
+
+
+def own_inputs_kernel(
+    row_count, chips, chunk, blocks, norms, w_out, left_ref, gate_ref, pairs_ref, received, *refs
+):
+    for n, (chip, r) in enumerate(rows_of_blocks(row_count, blocks)):
+        place_right(refs[-3], chips, chip, r, received[n])
+    first = first_chip(chips, 0) * row_count
+    attention_inputs(
+        row_count, chips, chunk, first, norms, w_out, left_ref, gate_ref, pairs_ref, refs[-4:]
+    )
+
+
+def other_inputs_kernel(
+    row_count,
+    chips,
+    chunk,
+    norms,
+    w_out,
+    left_ref,
+    gate_ref,
+    pairs_ref,
+    w_query,
+    w_gate,
+    w_key,
+    w_value,
+    own_att,
+    own_after,
+    held_triangle,
+    across_ref,
+    triangle_ref,
+    after_ref,
+    att_ref,
+    query_ref,
+    att_gate_ref,
+    own_after_ref,
+    key_ref,
+    value_ref,
+):
+    keys_and_values([own_att[...]], w_key, w_value, key_ref, value_ref)
+    chip, _ = chip_and_core()
+    own = row_count * 2 * row_count * chips
+    rows = pl.ds(pl.multiple_of(jnp.bitwise_and(chip, chips // 2 - 1) * own, own), own)
+    own_in = own_att[rows, :]
+    query_ref[...] = rounded(dot(own_in, w_query[...])) * (1.0 / math.sqrt(HEAD_DIM))
+    att_gate_ref[...] = sigmoid(dot(own_in, w_gate[...]))
+    own_after_ref[...] = own_after[rows, :]
+    first = first_chip(chips, 1) * row_count
+    refs = (triangle_ref, across_ref, after_ref, att_ref)
+    attention_inputs(
+        row_count, chips, chunk, first, norms, w_out, left_ref, gate_ref, pairs_ref, refs
+    )
+
+
+def keys_and_values(att, w_key, w_value, key_ref, value_ref):
+    channels = key_ref.shape[1]
+    key_value = jnp.concatenate([w_key[...], w_value[...]], axis=1)
+    start = 0
+    for values in att:
+        rows = slice(start, start + values.shape[0])
+        joined = dot(values, key_value)
+        key_ref[rows, :] = rounded(joined[:, :channels])
+        value_ref[rows, :] = rounded(joined[:, channels:])
+        start = rows.stop
+
+
+def column_bias(row_count, res, att, wide_bias, att_ref, bias_ref):
+    start = 0
+    for values in att:
+        att_ref[start : start + values.shape[0], :] = values.astype(jnp.float32)
+        start += values.shape[0]
+    keys = start // res
     own = lax.axis_index("row") * row_count
     for r in range(row_count):
-        column = att_ref[pl.ds(own + r, keys, stride=res), :].astype(bf16)
-        yield rounded(
-            lax.dot_general(
-                column, wide_bias, (((1,), (1,)), ((), ())), preferred_element_type=jnp.float32
-            )
-        )
-
-
-def partial_attention(
-    row_count, chips, query, key_ref, value_ref, bias_ref, valid_column, score_ref, halves
-):
-    bf16, f32, channels = jnp.bfloat16, jnp.float32, key_ref.shape[1]
+        column = att_ref[pl.ds(own + r, keys, stride=res), :].astype(jnp.bfloat16)
+        bias_ref[r, :keys, :] = rounded(dot(column, wide_bias[...]))
+
+
+def partial_attention(row_count, chips, query, parts, bias_ref, same_head, valid_column, score_ref):
+    bf16, f32 = jnp.bfloat16, jnp.float32
     res = 2 * row_count * chips
+    channels = valid_column.shape[1]
     count = row_count * chips // 2
-    row = lax.broadcasted_iota(jnp.int32, (2 * channels, 2 * channels), 0) // HEAD_DIM
-    column = lax.broadcasted_iota(jnp.int32, (2 * channels, 2 * channels), 1) // HEAD_DIM
-    same_head = jnp.where(row == column, 1.0, 0.0).astype(bf16)
+    keys = len(parts) * count
     maxima = [jnp.full((res, channels), -jnp.inf, f32) for _ in range(row_count)]
-    for part, (core, first) in enumerate(halves):
+    for part, (core, first, key_of, _) in enumerate(parts):
         products = []
-        for n in range(part * count, (part + 1) * count, 2):
-            pair = [
-                jnp.concatenate([key_ref[m * res : (m + 1) * res, :]] * row_count, axis=0) * query
-                for m in (n, n + 1)
-            ]
+        for n in range(0, count, 2):
+            pair = [jnp.concatenate([key_of(m)] * row_count, axis=0) * query for m in (n, n + 1)]
             products.append(jnp.concatenate([p.astype(bf16) for p in pair], axis=1))
-        scores = dot(jnp.concatenate(products, axis=0), same_head)
+        scores = dot(jnp.concatenate(products, axis=0), same_head[...])
         for n in range(count):
             k = (2 * (first + n // row_count) + core) * row_count + n % row_count
             key_mask = 1000000000.0 * (valid_column[pl.ds(k, 1), :] - 1.0)
@@ -291,100 +367,81 @@
             for r in range(row_count):
                 start = (n // 2 * row_count + r) * res
                 score = scores[start : start + res, lanes] + bias_ref[r, at : at + 1, :] + key_mask
-                place = (r * len(halves) * count + at) * res
-                score_ref[place : place + res, :] = score
+                score_ref[(r * keys + at) * res : (r * keys + at + 1) * res, :] = score
                 maxima[r] = jnp.maximum(maxima[r], score)
     totals, mixed = [], []
     for r in range(row_count):
         total = mix = jnp.zeros((res, channels), f32)
-        for n in range(len(halves) * count):
-            start = (r * len(halves) * count + n) * res
-            weight = jnp.exp(score_ref[start : start + res, :] - maxima[r])
-            total = total + weight
-            mix = mix + weight * value_ref[n * res : (n + 1) * res, :]
+        for part, (_, _, _, value_of) in enumerate(parts):
+            for n in range(count):
+                start = (r * keys + part * count + n) * res
+                weight = jnp.exp(score_ref[start : start + res, :] - maxima[r])
+                total = total + weight
+                mix = mix + weight * value_of(n)
         totals.append(total)
         mixed.append(mix)
     return maxima, totals, mixed
-
-
-def keys_and_values(att, w_key, w_value, att_ref, key_ref, value_ref):
-    channels = att_ref.shape[1]
-    key_value = jnp.concatenate([w_key[...], w_value[...]], axis=1)
-    start = 0
-    for values in att:
-        rows = slice(start, start + values.shape[0])
-        att_ref[rows, :] = values.astype(jnp.float32)
-        joined = dot(values, key_value)
-        key_ref[rows, :] = rounded(joined[:, :channels])
-        value_ref[rows, :] = rounded(joined[:, channels:])
-        start = rows.stop
 
 
 def most_attention_kernel(
     row_count,
     chips,
     valid_column,
-    w_query,
-    w_gate,
+    same_head,
     w_key,
     w_value,
-    head_bias,
+    wide_bias,
     own_att_a,
     own_att_b,
     far_att_a,
-    own_after_a,
-    own_after_b,
+    query_ref,
+    own_key_a,
+    own_value_a,
     sums_ref,
-    query_ref,
-    gate_ref,
-    after_ref,
     att_ref,
     key_ref,
     value_ref,
     bias_ref,
     score_ref,
 ):
-    bf16 = jnp.bfloat16
-    chip, core = chip_and_core()
-    res = 2 * row_count * chips
+    _, core = chip_and_core()
+    res, channels = valid_column.shape
+    keys_and_values([own_att_b[...], far_att_a[...]], w_key, w_value, key_ref, value_ref)
     att = [ref[...] for ref in (own_att_a, own_att_b, far_att_a)]
-    keys_and_values(att, w_key, w_value, att_ref, key_ref, value_ref)
-    own = row_count * res
-    own_in = att_ref[pl.ds(pl.multiple_of(chip * own, own), own), :].astype(bf16)
-    query = rounded(dot(own_in, w_query[...])) * (1.0 / math.sqrt(HEAD_DIM))
-    query_ref[...] = query
-    gate_ref[...] = sigmoid(dot(own_in, w_gate[...]))
-    chip_a = pl.multiple_of(jnp.minimum(chip, chips // 2 - 1) * own, own)
-    chip_b = pl.multiple_of(jnp.maximum(chip - chips // 2, 0) * own, own)
-    after_ref[...] = jnp.where(
-        chip < chips // 2, own_after_a[pl.ds(chip_a, own), :], own_after_b[pl.ds(chip_b, own), :]
-    )
-    keys = 3 * row_count * chips // 2
-    for r, bias in enumerate(column_bias(att_ref, row_count, keys, res, head_bias)):
-        bias_ref[r, :keys, :] = bias
-    halves = ((core, 0), (core, chips // 2), (1 - core, 0))
-    maxima, totals, mixed = partial_attention(
-        row_count, chips, query, key_ref, value_ref, bias_ref, valid_column, score_ref, halves
-    )
-    for r in range(row_count):
-        sums_ref[r, 0] = maxima[r]
-        sums_ref[r, 1] = totals[r]
-        sums_ref[r, 2] = mixed[r]
+    column_bias(row_count, res, att, wide_bias, att_ref, bias_ref)
+    count = row_count * chips // 2
+
+    def rows_of(ref, first):
+        return lambda n: ref[(first + n) * res : (first + n + 1) * res, :]
+
+    a, b = first_chip(chips, 0), first_chip(chips, 1)
+    parts = (
+        (core, a, rows_of(own_key_a, 0), rows_of(own_value_a, 0)),
+        (core, b, rows_of(key_ref, 0), rows_of(value_ref, 0)),
+        (1 - core, a, rows_of(key_ref, count), rows_of(value_ref, count)),
+    )
+    sums = partial_attention(
+        row_count, chips, query_ref[...], parts, bias_ref, same_head, valid_column, score_ref
+    )
+    for n, each in enumerate(sums):
+        for r in range(row_count):
+            sums_ref[r, n] = each[r]
 
 
 def attention_kernel(
     row_count,
     chips,
     valid_column,
+    same_head,
     w_key,
     w_value,
     w_out,
-    head_bias,
+    wide_bias,
     far_att_b,
-    sums_ref,
     query_ref,
     gate_ref,
     after_ref,
+    sums_ref,
     out_ref,
     att_ref,
     key_ref,
@@ -392,24 +449,18 @@
     bias_ref,
     score_ref,
 ):
-    bf16 = jnp.bfloat16
     _, core = chip_and_core()
-    res = 2 * row_count * chips
-    channels = att_ref.shape[1]
-    keys_and_values([far_att_b[...]], w_key, w_value, att_ref, key_ref, value_ref)
-    keys = row_count * chips // 2
-    for r, bias in enumerate(column_bias(att_ref, row_count, keys, res, head_bias)):
-        bias_ref[r, :keys, :] = bias
+    res, channels = valid_column.shape
+    far_att = far_att_b[...]
+    keys_and_values([far_att], w_key, w_value, key_ref, value_ref)
+    column_bias(row_count, res, [far_att], wide_bias, att_ref, bias_ref)
+
+    def rows_of(ref):
+        return lambda n: ref[n * res : (n + 1) * res, :]
+
+    parts = ((1 - core, first_chip(chips, 1), rows_of(key_ref), rows_of(value_ref)),)
     last = partial_attention(
-        row_count,
-        chips,
-        query_ref[...],
-        key_ref,
-        value_ref,
-        bias_ref,
-        valid_column,
-        score_ref,
-        ((1 - core, chips // 2),),
+        row_count, chips, query_ref[...], parts, bias_ref, same_head, valid_column, score_ref
     )
     attended = []
     for r, (last_maximum, last_total, last_mixed) in enumerate(zip(*last)):
@@ -418,9 +469,9 @@
         last_scale = jnp.exp(last_maximum - maximum)
         total = sums_ref[r, 1] * most_scale + last_total * last_scale
         attended.append((sums_ref[r, 2] * most_scale + last_mixed * last_scale) / total)
-    gated = (jnp.concatenate(attended, axis=0) * gate_ref[...]).astype(bf16)
+    gated = (jnp.concatenate(attended, axis=0) * gate_ref[...]).astype(jnp.bfloat16)
     final = after_ref[...] + dot(gated, w_out[...])
-    out_ref[...] = final.astype(bf16).reshape(row_count, res, channels)
+    out_ref[...] = final.astype(jnp.bfloat16).reshape(row_count, res, channels)
 
 
 def on_whole_complex(
@@ -479,6 +530,11 @@
     edge_weights = jnp.concatenate([w_edges, w_tri_gate], axis=1)
     valid_column = jnp.broadcast_to(residue_valid.astype(f32)[:, None], (res, channels))
 
+    head = lax.broadcasted_iota(jnp.int32, (HEADS, channels), 0)
+    head_of_channel = lax.broadcasted_iota(jnp.int32, (HEADS, channels), 1) // HEAD_DIM
+    repeat = jnp.where(head == head_of_channel, 1.0, 0.0).astype(bf16)
+    wide_bias = dot(w_pair_bias, repeat).astype(bf16)
+
     kept = lax.dynamic_update_slice(
         jnp.zeros((2 * row_count, res, channels), bf16), pair_rep, (0, 0, 0)
     )
@@ -491,7 +547,6 @@
         return tuple(s ^ bits for s in own_blocks)
 
     tall = shaped(f32, half * res, channels)
-    spread = shaped(f32, half * right_strides(res)[0], channels)
 
     def edges_of(pieces, send_row, *held):
         pairs = tuple(p for p, _ in pieces)
@@ -500,7 +555,8 @@
         first = len(operands) - len(held)
         return call(
             functools.partial(edges_kernel, row_count, chips, blocks, send_row),
-            (tall, spread, tall, tall, shaped(bf16, 4 * row_count, res, channels)),
+            (tall, tall, tall, tall, shaped(bf16, 4 * row_count, res, channels))
+            + (() if held else (shaped(bf16, 2 * channels, 2 * channels),)),
             operands,
             {first + e: e for e in range(len(held))},
         )
@@ -508,12 +564,14 @@
     diagonal = exchange(own, 6)
     beside = exchange(own, 2)
     near = exchange(own, 4)
-    *edges, early_right = edges_of([(own, own_blocks)], 0)
+    *edges, early_right, same_head = edges_of([(own, own_blocks)], 0)
     diagonal, edges = lax.optimization_barrier((diagonal, edges))
     *edges, early_right = edges_of(
         [(diagonal, blocks_from(3))], 2 * row_count, *edges, early_right
     )
-    beside, edges, early_right = lax.optimization_barrier((beside, edges, early_right))
+    beside, edges, early_right, wide_bias = lax.optimization_barrier(
+        (beside, edges, early_right, wide_bias)
+    )
     early = (exchange(early_right, 1), own_blocks + blocks_from(3))
     *edges, late_right = edges_of(
         [(beside, blocks_from(1)), (near, blocks_from(2))], 0, *edges
@@ -522,75 +580,51 @@
 
     left, right, gate, pairs = edges
     triangle, across = call(
-        functools.partial(near_triangle_kernel, row_count, chips, half // 2, [early[1]]),
-        (tall, spread),
+        functools.partial(near_triangle_kernel, row_count, chips, 4, [early[1]]),
+        (tall, tall),
         (left, right, early[0]),
     )
     part = half // 2 * res
-    piece = (shaped(f32, part, channels), shaped(bf16, part, channels))
-
-    def inputs_of(n, fresh, triangle, across):
-        operands = (norms, w_tri_out, left, gate, pairs)
-        operands += tuple(r for r, _ in fresh) + (triangle, across)
-        return call(
-            functools.partial(
-                attention_inputs_kernel, row_count, chips, half // 2, n, [b for _, b in fresh]
-            ),
-            (tall, spread) + piece,
-            operands,
-            {len(operands) - 2: 0, len(operands) - 1: 1},
-        )
-
-    triangle, across, after_a, att_a = inputs_of(0, [late], triangle, across)
+    in_part, own_shape = shaped(f32, part, channels), shaped(f32, row_count * res, channels)
+    att_part = shaped(bf16, part, channels)
+    shared = (norms, w_tri_out, left, gate, pairs)
+    triangle, across, after_a, att_a = call(
+        functools.partial(own_inputs_kernel, row_count, chips, 4, late[1]),
+        (tall, tall, in_part, att_part),
+        shared + (late[0], triangle, across),
+        {6: 0, 7: 1},
+    )
     far_att_a = exchange(att_a, 1)
-    triangle, across, after_b, att_b = inputs_of(1, [], triangle, across)
+    _, _, att_b, query, att_gate, after_own, keys_a, values_a = call(
+        functools.partial(other_inputs_kernel, row_count, chips, 4),
+        (tall, in_part, att_part, own_shape, own_shape, own_shape, in_part, in_part),
+        shared + (w_query, w_att_gate, w_key, w_value, att_a, after_a, triangle, across),
+        {11: 0},
+    )
     far_att_b = exchange(att_b, 1)
 
-    own_shape = shaped(f32, row_count * res, channels)
-
-    def attention_scratch(keys):
+    def attention_scratch(keys, projected):
         return (
             pltpu.VMEM((keys * res, channels), f32),
-            pltpu.VMEM((keys * res, channels), f32),
-            pltpu.VMEM((keys * res, channels), f32),
+            pltpu.VMEM((projected * res, channels), f32),
+            pltpu.VMEM((projected * res, channels), f32),
             pltpu.VMEM((row_count, 40, channels), f32),
             pltpu.VMEM((row_count * keys * res, channels), f32),
         )
 
-    sums, query, att_gate, after_own = call(
+    sums = call(
         functools.partial(most_attention_kernel, row_count, chips),
-        (shaped(f32, row_count, 3, res, channels), own_shape, own_shape, own_shape),
-        (
-            valid_column,
-            w_query,
-            w_att_gate,
-            w_key,
-            w_value,
-            w_pair_bias.T,
-            att_a,
-            att_b,
-            far_att_a,
-            after_a,
-            after_b,
-        ),
-        scratch=attention_scratch(3 * half // 2),
+        shaped(f32, row_count, 3, res, channels),
+        (valid_column, same_head, w_key, w_value, wide_bias, att_a, att_b, far_att_a)
+        + (query, keys_a, values_a),
+        scratch=attention_scratch(3 * half // 2, half),
     )
     return call(
         functools.partial(attention_kernel, row_count, chips),
         shaped(bf16, *pair_rep.shape),
-        (
-            valid_column,
-            w_key,
-            w_value,
-            w_att_out,
-            w_pair_bias.T,
-            far_att_b,
-            sums,
-            query,
-            att_gate,
-            after_own,
-        ),
-        scratch=attention_scratch(half // 2),
+        (valid_column, same_head, w_key, w_value, w_att_out, wide_bias, far_att_b)
+        + (query, att_gate, after_own, sums),
+        scratch=attention_scratch(half // 2, half // 2),
     )
 
 

time: 22.6 us -> 23 us (1.018)
  waiting for transfers between devices: 2.41 us -> 3.12 us
  other arithmetic: 1.6 us -> 0.96 us
  Pallas kernels: 8.27 us -> 8.8 us
  local copies, waits for them, and re-layouts: 1.65 us -> 1.29 us
    unnamed x14 -> x30, local copies, waits for them, and re-layouts: 0.03 us -> 1.17 us
    dynamic_update_slice x1, local copies, waits for them, and re-layouts: 0.78 us -> 0.01 us  [on_whole_complex(): lax.dynamic_update_slice(jnp.zeros((2 * row_count, res, channels), bf16),...]
    another operation x1, local copies, waits for them, and re-layouts: 0.75 us -> 0.02 us  [on_whole_complex(): norms = jnp.stack(vectors)]
    ppermute x8, waiting for transfers between devices: 2.41 us -> 3.12 us  [exchange(): return lax.ppermute(values, 'row', [(d, d ^ bit) for d in range(devices)])]
    convert_element_type x1, other arithmetic: 0.66 us -> 0.01 us  [on_whole_complex(): residue_valid.astype(f32)[:, None]]
    pallas_call x8, Pallas kernels: 8.27 us -> 8.8 us  [call(): pl.pallas_call(kernel, out_shape=outs, in_specs=[in_vmem] * len(operands)...]
  transfers between devices with their start and end apart: 8 -> 8, of which waited for: 5 -> 5; matrix products, arithmetic and copies ran while one was open for 14% -> 6% of each run, Pallas kernels for 25% -> 27%
where the time goes in v8:
time: 23 us; the launch traced here: 22.8 us
  Pallas kernels  8.8 us (38%)
  starting transfers between devices  8.23 us (36%)
  waiting for transfers between devices  3.12 us (14%)
  local copies, waits for them, and re-layouts  1.29 us (6%)
  other arithmetic  0.96 us (4%)
    pallas_call x8, Pallas kernels, call(): pl.pallas_call(kernel, out_shape=outs, in_specs=[in_vmem] * len(operands)...  8.8 us
    ppermute x8, starting transfers between devices, exchange(): return lax.ppermute(values, 'row', [(d, d ^ bit) for d in range(devices)])  8.23 us
    ppermute x8, waiting for transfers between devices, exchange(): return lax.ppermute(values, 'row', [(d, d ^ bit) for d in range(devices)])  3.12 us
    unnamed x30, local copies, waits for them, and re-layouts  1.17 us
    concatenate x1, other arithmetic, on_whole_complex(): edge_weights = jnp.concatenate([w_edges, w_tri_gate], axis=1)  0.95 us
  transfers between devices with their start and end apart: 8, of which 5 were waited for; matrix products, arithmetic and copies ran while one was open for 6% of the time, Pallas kernels for 27%

profile of v8, /device:TPU:0, one launch (start us, length us, event | category | flops | bytes accessed | tf_op | source)
XLA Modules:
  0.0 22.8 jit_solution(11386779911982512559)
XLA Ops:
  0.0 4.0 %collective-permute-start = (bf16[3,48,128]{2,1,0:T(8,128)(2,1)}, bf16[3,48,128]{2,1,0:T(8,128)(2,1)S(1)}, u32[]{:S(2)}, u32[]{:S(2)}) collective-permute-start(bf16[3,48,128]{2,1,0:T(8,128)(2,1)} %param.17), channel_id=1, source_target_pairs={{0,8},{1,9},{2,10},{3,11},{4,12},{5,13},{6,14},{7,15},{8,0},{9,1},... | collective-permute-start | bytes 110600 | tf_op jit(solution)/shard_map/ppermute | solution.py:519
  4.0 0.9 %pad_maximum_fusion.weights = bf16[128,640]{1,0:T(8,128)(2,1)S(1)} fusion(bf16[128,128]{1,0:T(8,128)(2,1)} %param.22, bf16[128,512]{1,0:T(8,128)(2,1)} %param.21), kind=kLoop, calls=%fused_computation.2 | loop fusion | flops 327680 | bytes 327680 | tf_op jit(solution)/shard_map/concatenate | solution.py:530
  5.1 0.6 %copy-done.11 = f32[128]{0:T(128)S(1)} copy-done((f32[128]{0:T(128)S(1)}, f32[128]{0:T(128)}, u32[]{:S(2)}) %copy-start.11) | copy-done | bytes 536
  5.8 0.8 %collective-permute-done = bf16[3,48,128]{2,1,0:T(8,128)(2,1)S(1)} collective-permute-done((bf16[3,48,128]{2,1,0:T(8,128)(2,1)}, bf16[3,48,128]{2,1,0:T(8,128)(2,1)S(1)}, u32[]{:S(2)}, u32[]{:S(2)}) %collective-permute-start) | collective-permute-done | bytes 36896 | tf_op jit(solution)/shard_map/ppermute | solution.py:519
  6.6 2.5 %collective-permute-start.2 = (bf16[6,48,128]{2,1,0:T(8,128)(2,1)S(1)}, bf16[6,48,128]{2,1,0:T(8,128)(2,1)S(1)}, u32[]{:S(2)}, u32[]{:S(2)}) collective-permute-start(bf16[6,48,128]{2,1,0:T(8,128)(2,1)S(1)} %constant_dynamic-update-slice_fusion.refs_0_), channel_id=1, source_target_pairs={{0,6},{1,7},{2,4},{3,5},{4,2},{5,3},{6,0},{7,1},{8,14},{9,15},{10,... | collective-permute-start | bytes 221192 | tf_op jit(solution)/shard_map/ppermute | solution.py:519
  9.1 0.5 %collective-permute-start.1 = (bf16[6,48,128]{2,1,0:T(8,128)(2,1)S(1)}, bf16[6,48,128]{2,1,0:T(8,128)(2,1)S(1)}, u32[]{:S(2)}, u32[]{:S(2)}) collective-permute-start(bf16[6,48,128]{2,1,0:T(8,128)(2,1)S(1)} %constant_dynamic-update-slice_fusion.refs_0_), channel_id=1, source_target_pairs={{0,2},{1,3},{2,0},{3,1},{4,6},{5,7},{6,4},{7,5},{8,10},{9,11},{10,... | collective-permute-start | bytes 221192 | tf_op jit(solution)/shard_map/ppermute | solution.py:519
  9.6 0.5 %collective-permute-start.3 = (bf16[6,48,128]{2,1,0:T(8,128)(2,1)S(1)}, bf16[6,48,128]{2,1,0:T(8,128)(2,1)S(1)}, u32[]{:S(2)}, u32[]{:S(2)}) collective-permute-start(bf16[6,48,128]{2,1,0:T(8,128)(2,1)S(1)} %constant_dynamic-update-slice_fusion.refs_0_), channel_id=1, source_target_pairs={{0,4},{1,5},{2,6},{3,7},{4,0},{5,1},{6,2},{7,3},{8,12},{9,13},{10,... | collective-permute-start | bytes 221192 | tf_op jit(solution)/shard_map/ppermute | solution.py:519
  10.1 0.2 fusion.wide_bias
  10.4 0.4 %copy-done.14 = s32[48]{0:T(128)S(1)} copy-done((s32[48]{0:T(128)S(1)}, s32[48]{0:T(128)}, u32[]{:S(2)}) %copy-start.14) | copy-done | bytes 216
  10.8 0.1 broadcast_in_dim.15.valid_column
  10.9 0.4 %shard_map.163 = (f32[1152,128]{1,0:T(8,128)S(1)}, f32[1152,128]{1,0:T(8,128)S(1)}, f32[1152,128]{1,0:T(8,128)S(1)}, f32[1152,128]{1,0:T(8,128)S(1)}, bf16[12,48...) custom-call(f32[48,128]{1,0:T(8,128)S(1)} %broadcast_in_dim.15.valid_column, f32[6,128]{1,0:T(8,128)S(1)} %stack.27.norms, ...), custom_call_target="tpu_custom_call" | custom-call | flops 1048576 | bytes 33554432 | tf_op jit(solution)/shard_map/pallas_call | solution.py:507
  11.3 1.0 %collective-permute-done.2.refs_0_ = bf16[6,48,128]{2,1,0:T(8,128)(2,1)S(1)} collective-permute-done((bf16[6,48,128]{2,1,0:T(8,128)(2,1)S(1)}, bf16[6,48,128]{2,1,0:T(8,128)(2,1)S(1)}, u32[]{:S(2)}, u32[]{:S(2)}) %collective-permute-start.2) | collective-permute-done | bytes 73760 | tf_op jit(solution)/shard_map/ppermute | solution.py:519
  12.4 0.4 %shard_map.164 = (f32[1152,128]{1,0:T(8,128)S(1)}, f32[1152,128]{1,0:T(8,128)S(1)}, f32[1152,128]{1,0:T(8,128)S(1)}, f32[1152,128]{1,0:T(8,128)S(1)}, bf16[12,48,128]{2,1,0:T(8,128)(2,1)S(1)}) custom-call(f32[48,128]{1,0:T(8,128)S(1)} %broadcast_in_dim.15.valid_column, ...), custom_call_target="tpu_custom_call", output_to_operand_aliasing={{0}: (4, {}), {1}: (5, {}), {2}: (6, {}), {3}: (7, {}), {4}... | custom-call | flops 1048576 | bytes 33554432 | tf_op jit(solution)/shard_map/pallas_call | solution.py:507
  12.8 0.6 %collective-permute-done.1.refs_0_ = bf16[6,48,128]{2,1,0:T(8,128)(2,1)S(1)} collective-permute-done((bf16[6,48,128]{2,1,0:T(8,128)(2,1)S(1)}, bf16[6,48,128]{2,1,0:T(8,128)(2,1)S(1)}, u32[]{:S(2)}, u32[]{:S(2)}) %collective-permute-start.1) | collective-permute-done | bytes 73760 | tf_op jit(solution)/shard_map/ppermute | solution.py:519
  13.4 0.5 %collective-permute-done.3.refs_1_ = bf16[6,48,128]{2,1,0:T(8,128)(2,1)S(1)} collective-permute-done((bf16[6,48,128]{2,1,0:T(8,128)(2,1)S(1)}, bf16[6,48,128]{2,1,0:T(8,128)(2,1)S(1)}, u32[]{:S(2)}, u32[]{:S(2)}) %collective-permute-start.3) | collective-permute-done | bytes 73760 | tf_op jit(solution)/shard_map/ppermute | solution.py:519
  14.0 0.6 %shard_map.165 = (f32[1152,128]{1,0:T(8,128)S(1)}, f32[1152,128]{1,0:T(8,128)S(1)}, f32[1152,128]{1,0:T(8,128)S(1)}, f32[1152,128]{1,0:T(8,128)S(1)}, bf16[12,48,128]{2,1,0:T(8,128)(2,1)S(1)}) custom-call(f32[48,128]{1,0:T(8,128)S(1)} %broadcast_in_dim.15.valid_column, ...), custom_call_target="tpu_custom_call", output_to_operand_aliasing={{0}: (5, {}), {1}: (6, {}), {2}: (7, {}), {3}: (8, {})} | custom-call | flops 1048576 | bytes 33554432 | tf_op jit(solution)/shard_map/pallas_call | solution.py:507
  14.7 0.1 collective-permute-done.5.refs_0_
  14.8 1.3 %shard_map.166 = (f32[1152,128]{1,0:T(8,128)S(1)}, f32[1152,128]{1,0:T(8,128)S(1)}) custom-call(f32[1152,128]{1,0:T(8,128)S(1)} %get-tuple-element.75.left_ref, f32[1152,128]{1,0:T(8,128)S(1)} %get-tuple-element.79.right_ref, bf16[12,48,128]{2,1,0:T(8,128)(2,1)S(1)} %collective-permute-done.5.refs_0_), custom_call_target="tpu_custom_call" | custom-call | flops 1048576 | bytes 33554432 | tf_op jit(solution)/shard_map/pallas_call | solution.py:507
  16.2 1.2 %shard_map.167 = (f32[1152,128]{1,0:T(8,128)S(1)}, f32[1152,128]{1,0:T(8,128)S(1)}, f32[576,128]{1,0:T(8,128)S(1)}, bf16[576,128]{1,0:T(8,128)(2,1)S(1)}) custom-call(f32[6,128]{1,0:T(8,128)S(1)} %stack.27.norms, bf16[128,128]{1,0:T(8,128)(2,1)S(1)} %copy-done.3, ...), custom_call_target="tpu_custom_call", output_to_operand_aliasing={{0}: (6, {}), {1}: (7, {})} | custom-call | flops 1048576 | bytes 33554432 | tf_op jit(solution)/shard_map/pallas_call | solution.py:507
  17.3 0.4 %collective-permute-start.7 = (bf16[576,128]{1,0:T(8,128)(2,1)S(1)}, bf16[576,128]{1,0:T(8,128)(2,1)S(1)}, u32[]{:S(2)}, u32[]{:S(2)}) collective-permute-start(bf16[576,128]{1,0:T(8,128)(2,1)S(1)} %get-tuple-element.83.own_att.own_att_a), channel_id=1, source_target_pairs={{0,1},{1,0},{2,3},{3,2},{4,5},{5,4},{6,7},{7,6},{8,9},{9,8},{10,11... | collective-permute-start | bytes 442376 | tf_op jit(solution)/shard_map/ppermute | solution.py:519
  17.8 2.1 %shard_map.168 = (f32[1152,128]{1,0:T(8,128)S(1)}, f32[576,128]{1,0:T(8,128)}, bf16[576,128]{1,0:T(8,128)(2,1)S(1)}, f32[144,128]{1,0:T(8,128)S(1)}, f32[144,128...) custom-call(f32[6,128]{1,0:T(8,128)S(1)} %stack.27.norms, ...), custom_call_target="tpu_custom_call", output_to_operand_aliasing={{0}: (11, {})} | custom-call | flops 1048576 | bytes 33554432 | tf_op jit(solution)/shard_map/pallas_call | solution.py:507
  19.9 0.1 collective-permute-start.6
  20.0 1.4 %shard_map.169.sums_ref = f32[3,3,48,128]{3,2,1,0:T(8,128)S(1)} custom-call(f32[48,128]{1,0:T(8,128)S(1)} %broadcast_in_dim.15.valid_column, bf16[256,256]{1,0:T(8,128)(2,1)S(1)} %get-tuple-element.53.same_head, bf16[128,128]{1,0:T(8,128)(2,1)S(1)} %copy-done.1, bf16[128,128]{1,0:T(8,128)(2,1)S(1)} %copy-done.2, bf16[128,128]{1,0:T(8,128)(2,1)S(1)} %fusion.wide_bias, ...), custom_call_target="tpu_custom_call" | custom-call | flops 1048576 | bytes 33554432 | tf_op jit(solution)/shard_map/pallas_call | solution.py:507
  21.4 1.4 %shard_map.170 = bf16[3,48,128]{2,1,0:T(8,128)(2,1)} custom-call(f32[48,128]{1,0:T(8,128)S(1)} %broadcast_in_dim.15.valid_column, bf16[256,256]{1,0:T(8,128)(2,1)S(1)} %get-tuple-element.53.same_head, bf16[128,128]{1,0:T(8,128)(2,1)S(1)} %copy-done.1, bf16[128,128]{1,0:T(8,128)(2,1)S(1)} %copy-done.2, bf16[128,128]{1,0:T(8,128)(2,1)S(1)} %copy-done.6, ...), custom_call_target="tpu_custom_call" | custom-call | flops 1048576 | bytes 33554432 | tf_op jit(solution)/shard_map/pallas_call | solution.py:507
  (39 shorter events, 0.3 us)
Async XLA Ops:
  0.0 10.1 %copy-start = (bf16[128,4]{0,1:T(4,128)(2,1)S(1)}, bf16[128,4]{0,1:T(4,128)(2,1)}, u32[]{:S(2)}) copy-start(bf16[128,4]{0,1:T(4,128)(2,1)} %param.32) | copy-start | bytes 3076
  0.0 6.6 %collective-permute-start = (bf16[3,48,128]{2,1,0:T(8,128)(2,1)}, bf16[3,48,128]{2,1,0:T(8,128)(2,1)S(1)}, u32[]{:S(2)}, u32[]{:S(2)}) collective-permute-start(bf16[3,48,128]{2,1,0:T(8,128)(2,1)} %param.17), channel_id=1, source_target_pairs={{0,8},{1,9},{2,10},{3,11},{4,12},{5,13},{6,14},{7,15},{8,0},{9,1},... | collective-permute-start | bytes 110600 | tf_op jit(solution)/shard_map/ppermute | solution.py:519
  4.0 1.0 %copy-start.7 = (bf16[3,48,128]{2,1,0:T(8,128)(2,1)S(1)}, bf16[3,48,128]{2,1,0:T(8,128)(2,1)}, u32[]{:S(2)}) copy-start(bf16[3,48,128]{2,1,0:T(8,128)(2,1)} %param.17) | copy-start | bytes 110596
  5.0 0.7 %copy-start.11 = (f32[128]{0:T(128)S(1)}, f32[128]{0:T(128)}, u32[]{:S(2)}) copy-start(f32[128]{0:T(128)} %param.24) | copy-start | bytes 1540
  5.0 0.7 %copy-start.12 = (f32[128]{0:T(128)S(1)}, f32[128]{0:T(128)}, u32[]{:S(2)}) copy-start(f32[128]{0:T(128)} %param.26) | copy-start | bytes 1540
  5.1 0.7 %copy-start.13 = (f32[128]{0:T(128)S(1)}, f32[128]{0:T(128)}, u32[]{:S(2)}) copy-start(f32[128]{0:T(128)} %param.27) | copy-start | bytes 1540
  5.1 0.7 %copy-start.8 = (f32[128]{0:T(128)S(1)}, f32[128]{0:T(128)}, u32[]{:S(2)}) copy-start(f32[128]{0:T(128)} %param.19) | copy-start | bytes 1540
  5.1 0.7 %copy-start.9 = (f32[128]{0:T(128)S(1)}, f32[128]{0:T(128)}, u32[]{:S(2)}) copy-start(f32[128]{0:T(128)} %param.20) | copy-start | bytes 1540
  5.1 0.7 %copy-start.10 = (f32[128]{0:T(128)S(1)}, f32[128]{0:T(128)}, u32[]{:S(2)}) copy-start(f32[128]{0:T(128)} %param.23) | copy-start | bytes 1540
  6.6 5.8 %collective-permute-start.2 = (bf16[6,48,128]{2,1,0:T(8,128)(2,1)S(1)}, bf16[6,48,128]{2,1,0:T(8,128)(2,1)S(1)}, u32[]{:S(2)}, u32[]{:S(2)}) collective-permute-start(bf16[6,48,128]{2,1,0:T(8,128)(2,1)S(1)} %constant_dynamic-update-slice_fusion.refs_0_), channel_id=1, source_target_pairs={{0,6},{1,7},{2,4},{3,5},{4,2},{5,3},{6,0},{7,1},{8,14},{9,15},{10,... | collective-permute-start | bytes 221192 | tf_op jit(solution)/shard_map/ppermute | solution.py:519
  9.1 4.4 %collective-permute-start.1 = (bf16[6,48,128]{2,1,0:T(8,128)(2,1)S(1)}, bf16[6,48,128]{2,1,0:T(8,128)(2,1)S(1)}, u32[]{:S(2)}, u32[]{:S(2)}) collective-permute-start(bf16[6,48,128]{2,1,0:T(8,128)(2,1)S(1)} %constant_dynamic-update-slice_fusion.refs_0_), channel_id=1, source_target_pairs={{0,2},{1,3},{2,0},{3,1},{4,6},{5,7},{6,4},{7,5},{8,10},{9,11},{10,... | collective-permute-start | bytes 221192 | tf_op jit(solution)/shard_map/ppermute | solution.py:519
  9.6 4.4 %collective-permute-start.3 = (bf16[6,48,128]{2,1,0:T(8,128)(2,1)S(1)}, bf16[6,48,128]{2,1,0:T(8,128)(2,1)S(1)}, u32[]{:S(2)}, u32[]{:S(2)}) collective-permute-start(bf16[6,48,128]{2,1,0:T(8,128)(2,1)S(1)} %constant_dynamic-update-slice_fusion.refs_0_), channel_id=1, source_target_pairs={{0,4},{1,5},{2,6},{3,7},{4,0},{5,1},{6,2},{7,3},{8,12},{9,13},{10,... | collective-permute-start | bytes 221192 | tf_op jit(solution)/shard_map/ppermute | solution.py:519
  10.1 0.7 %copy-start.14 = (s32[48]{0:T(128)S(1)}, s32[48]{0:T(128)}, u32[]{:S(2)}) copy-start(s32[48]{0:T(128)} %param.18) | copy-start | bytes 580
  13.4 1.4 %collective-permute-start.5 = (bf16[12,48,128]{2,1,0:T(8,128)(2,1)S(1)}, bf16[12,48,128]{2,1,0:T(8,128)(2,1)S(1)}, u32[]{:S(2)}, u32[]{:S(2)}) collective-permute-start(bf16[12,48,128]{2,1,0:T(8,128)(2,1)S(1)} %get-tuple-element.80), channel_id=1, source_target_pairs={{0,1},{1,0},{2,3},{3,2},{4,5},{5,4},{6,7},{7,6},{8,9},{9,8},{10,11... | collective-permute-start | bytes 442376 | tf_op jit(solution)/shard_map/ppermute | solution.py:519
  14.6 1.5 %collective-permute-start.4 = (bf16[12,48,128]{2,1,0:T(8,128)(2,1)S(1)}, bf16[12,48,128]{2,1,0:T(8,128)(2,1)S(1)}, u32[]{:S(2)}, u32[]{:S(2)}) collective-permute-start(bf16[12,48,128]{2,1,0:T(8,128)(2,1)S(1)} %get-tuple-element.78), channel_id=1, source_target_pairs={{0,1},{1,0},{2,3},{3,2},{4,5},{5,4},{6,7},{7,6},{8,9},{9,8},{10,11... | collective-permute-start | bytes 442376 | tf_op jit(solution)/shard_map/ppermute | solution.py:519
  14.8 1.3 %copy-start.3 = (bf16[128,128]{1,0:T(8,128)(2,1)S(1)}, bf16[128,128]{1,0:T(8,128)(2,1)}, u32[]{:S(2)}) copy-start(bf16[128,128]{1,0:T(8,128)(2,1)} %w_out.4) | copy-start | bytes 98308
  16.1 1.7 %copy-start.1 = (bf16[128,128]{1,0:T(8,128)(2,1)S(1)}, bf16[128,128]{1,0:T(8,128)(2,1)}, u32[]{:S(2)}) copy-start(bf16[128,128]{1,0:T(8,128)(2,1)} %w_key.5) | copy-start | bytes 98308
  16.1 1.7 %copy-start.2 = (bf16[128,128]{1,0:T(8,128)(2,1)S(1)}, bf16[128,128]{1,0:T(8,128)(2,1)}, u32[]{:S(2)}) copy-start(bf16[128,128]{1,0:T(8,128)(2,1)} %w_value.5) | copy-start | bytes 98308
  16.1 1.7 %copy-start.4 = (bf16[128,128]{1,0:T(8,128)(2,1)S(1)}, bf16[128,128]{1,0:T(8,128)(2,1)}, u32[]{:S(2)}) copy-start(bf16[128,128]{1,0:T(8,128)(2,1)} %w_query.1) | copy-start | bytes 98308
  16.1 1.7 %copy-start.5 = (bf16[128,128]{1,0:T(8,128)(2,1)S(1)}, bf16[128,128]{1,0:T(8,128)(2,1)}, u32[]{:S(2)}) copy-start(bf16[128,128]{1,0:T(8,128)(2,1)} %w_gate.1) | copy-start | bytes 98308
  17.3 2.7 %collective-permute-start.7 = (bf16[576,128]{1,0:T(8,128)(2,1)S(1)}, bf16[576,128]{1,0:T(8,128)(2,1)S(1)}, u32[]{:S(2)}, u32[]{:S(2)}) collective-permute-start(bf16[576,128]{1,0:T(8,128)(2,1)S(1)} %get-tuple-element.83.own_att.own_att_a), channel_id=1, source_target_pairs={{0,1},{1,0},{2,3},{3,2},{4,5},{5,4},{6,7},{7,6},{8,9},{9,8},{10,11... | collective-permute-start | bytes 442376 | tf_op jit(solution)/shard_map/ppermute | solution.py:519
  19.9 1.5 %collective-permute-start.6 = (bf16[576,128]{1,0:T(8,128)(2,1)S(1)}, bf16[576,128]{1,0:T(8,128)(2,1)S(1)}, u32[]{:S(2)}, u32[]{:S(2)}) collective-permute-start(bf16[576,128]{1,0:T(8,128)(2,1)S(1)} %get-tuple-element.87.own_att_b), channel_id=1, source_target_pairs={{0,1},{1,0},{2,3},{3,2},{4,5},{5,4},{6,7},{7,6},{8,9},{9,8},{10,11... | collective-permute-start | bytes 442376 | tf_op jit(solution)/shard_map/ppermute | solution.py:519
  20.0 1.4 %copy-start.6 = (bf16[128,128]{1,0:T(8,128)(2,1)S(1)}, bf16[128,128]{1,0:T(8,128)(2,1)}, u32[]{:S(2)}) copy-start(bf16[128,128]{1,0:T(8,128)(2,1)} %w_out.5) | copy-start | bytes 98308

commit v9 on v8

--- a/solution.py
+++ b/solution.py
@@ -139,11 +139,12 @@
     return [(jnp.bitwise_xor(chip, bits), r) for bits in blocks for r in range(row_count)]
 
 
-def edges_kernel(row_count, chips, pieces, send_row, valid_column, norms, weights, *refs):
+def edges_kernel(
+    row_count, chips, pieces, send_row, makes_heads, valid_column, norms, weights, *refs
+):
     pair_refs = refs[: len(pieces)]
-    if send_row or len(pieces) > 1:
-        left_ref, right_ref, gate_ref, pairs_ref, send_ref = refs[-5:]
-    else:
+    left_ref, right_ref, gate_ref, pairs_ref, send_ref = refs[-5:]
+    if makes_heads:
         left_ref, right_ref, gate_ref, pairs_ref, send_ref, same_head_ref = refs[-6:]
         wide = same_head_ref.shape
         row = lax.broadcasted_iota(jnp.int32, wide, 0) // HEAD_DIM
@@ -200,21 +201,24 @@
 def triangle_rows(row_count, chips, left_ref, right_ref, triangle_ref, first, count, core):
     res = 2 * row_count * chips
     start = pl.multiple_of(first * res, res)
-    lefts = [left_ref[pl.ds(start + n * res, res), :] for n in range(count)]
-    for r in range(row_count):
-        parts = [[] for _ in range(count)]
-        for chip in range(chips):
-            at = (r * chips + chip) * res
-            right = right_ref[at : at + res, :]
-            for n in range(count):
-                product = lefts[n] * right
-                parts[n].append(
-                    sum(product[k : k + 8] for k in range(8, res, 8)) + product[:8]
+    block = 4
+    for n in range(0, count, block):
+        lefts = [left_ref[pl.ds(start + m * res, res), :] for m in range(n, n + block)]
+        for r in range(row_count):
+            parts = [[] for _ in range(block)]
+            for chip in range(chips):
+                at = (r * chips + chip) * res
+                right = right_ref[at : at + res, :]
+                for m in range(block):
+                    product = lefts[m] * right
+                    parts[m].append(
+                        sum(product[k : k + 8] for k in range(8, res, 8)) + product[:8]
+                    )
+            for m in range(block):
+                place = start + (n + m) * res + core * row_count + r
+                triangle_ref[pl.ds(place, chips, stride=2 * row_count), :] = rounded(
+                    sum_sublanes(parts[m])
                 )
-        for n in range(count):
-            triangle_ref[
-                pl.ds(start + n * res + core * row_count + r, chips, stride=2 * row_count), :
-            ] = rounded(sum_sublanes(parts[n]))
 
 
 def near_triangle_kernel(row_count, chips, chunk, pieces, left_ref, right_ref, *refs):
@@ -235,7 +239,7 @@
 
 
 def attention_inputs(
-    row_count, chips, chunk, first, norms, w_out, left_ref, gate_ref, pairs_ref, refs
+    row_count, chips, first, norms, w_out, left_ref, gate_ref, pairs_ref, refs
 ):
     f32, bf16 = jnp.float32, jnp.bfloat16
     triangle_ref, across_ref, after_ref, att_ref = refs
@@ -243,20 +247,9 @@
     half = row_count * chips
     tall = (half // 2) * 2 * half
 
-    def some_rows(step, carry):
-        triangle_rows(
-            row_count,
-            chips,
-            left_ref,
-            across_ref,
-            triangle_ref,
-            first + step * chunk,
-            chunk,
-            1 - core,
-        )
-        return carry
-
-    lax.fori_loop(0, half // 2 // chunk, some_rows, 0)
+    triangle_rows(
+        row_count, chips, left_ref, across_ref, triangle_ref, first, half // 2, 1 - core
+    )
     rows = pl.ds(pl.multiple_of(first * 2 * half, tall), tall)
     tri_normed = layer_norm(triangle_ref[rows, :], norms[2:3, :], norms[3:4, :], 1).astype(bf16)
     after_tri = pairs_ref[rows, :] + gate_ref[rows, :] * dot(tri_normed, w_out[...])
@@ -271,54 +264,34 @@
 
 
 def own_inputs_kernel(
-    row_count, chips, chunk, blocks, norms, w_out, left_ref, gate_ref, pairs_ref, received, *refs
+    row_count, chips, blocks, norms, w_out, left_ref, gate_ref, pairs_ref, received, *refs
 ):
     for n, (chip, r) in enumerate(rows_of_blocks(row_count, blocks)):
         place_right(refs[-3], chips, chip, r, received[n])
     first = first_chip(chips, 0) * row_count
     attention_inputs(
-        row_count, chips, chunk, first, norms, w_out, left_ref, gate_ref, pairs_ref, refs[-4:]
+        row_count, chips, first, norms, w_out, left_ref, gate_ref, pairs_ref, refs[-4:]
     )
 
 
 def other_inputs_kernel(
     row_count,
     chips,
-    chunk,
     norms,
     w_out,
     left_ref,
     gate_ref,
     pairs_ref,
-    w_query,
-    w_gate,
-    w_key,
-    w_value,
-    own_att,
-    own_after,
     held_triangle,
     across_ref,
     triangle_ref,
     after_ref,
     att_ref,
-    query_ref,
-    att_gate_ref,
-    own_after_ref,
-    key_ref,
-    value_ref,
-):
-    keys_and_values([own_att[...]], w_key, w_value, key_ref, value_ref)
-    chip, _ = chip_and_core()
-    own = row_count * 2 * row_count * chips
-    rows = pl.ds(pl.multiple_of(jnp.bitwise_and(chip, chips // 2 - 1) * own, own), own)
-    own_in = own_att[rows, :]
-    query_ref[...] = rounded(dot(own_in, w_query[...])) * (1.0 / math.sqrt(HEAD_DIM))
-    att_gate_ref[...] = sigmoid(dot(own_in, w_gate[...]))
-    own_after_ref[...] = own_after[rows, :]
+):
     first = first_chip(chips, 1) * row_count
     refs = (triangle_ref, across_ref, after_ref, att_ref)
     attention_inputs(
-        row_count, chips, chunk, first, norms, w_out, left_ref, gate_ref, pairs_ref, refs
+        row_count, chips, first, norms, w_out, left_ref, gate_ref, pairs_ref, refs
     )
 
 
@@ -388,26 +361,33 @@
     chips,
     valid_column,
     same_head,
+    w_query,
+    w_gate,
     w_key,
     w_value,
     wide_bias,
     own_att_a,
     own_att_b,
     far_att_a,
+    own_after,
+    sums_ref,
     query_ref,
-    own_key_a,
-    own_value_a,
-    sums_ref,
+    gate_ref,
+    after_ref,
     att_ref,
     key_ref,
     value_ref,
     bias_ref,
     score_ref,
 ):
-    _, core = chip_and_core()
+    chip, core = chip_and_core()
     res, channels = valid_column.shape
-    keys_and_values([own_att_b[...], far_att_a[...]], w_key, w_value, key_ref, value_ref)
+    own = row_count * res
+    rows = pl.ds(pl.multiple_of(jnp.bitwise_and(chip, chips // 2 - 1) * own, own), own)
+    own_in = own_att_a[rows, :]
+    query = rounded(dot(own_in, w_query[...])) * (1.0 / math.sqrt(HEAD_DIM))
     att = [ref[...] for ref in (own_att_a, own_att_b, far_att_a)]
+    keys_and_values(att, w_key, w_value, key_ref, value_ref)
     column_bias(row_count, res, att, wide_bias, att_ref, bias_ref)
     count = row_count * chips // 2
 
@@ -415,17 +395,19 @@
         return lambda n: ref[(first + n) * res : (first + n + 1) * res, :]
 
     a, b = first_chip(chips, 0), first_chip(chips, 1)
-    parts = (
-        (core, a, rows_of(own_key_a, 0), rows_of(own_value_a, 0)),
-        (core, b, rows_of(key_ref, 0), rows_of(value_ref, 0)),
-        (1 - core, a, rows_of(key_ref, count), rows_of(value_ref, count)),
-    )
+    parts = [
+        (sender, first, rows_of(key_ref, n * count), rows_of(value_ref, n * count))
+        for n, (sender, first) in enumerate(((core, a), (core, b), (1 - core, a)))
+    ]
     sums = partial_attention(
-        row_count, chips, query_ref[...], parts, bias_ref, same_head, valid_column, score_ref
+        row_count, chips, query, parts, bias_ref, same_head, valid_column, score_ref
     )
     for n, each in enumerate(sums):
         for r in range(row_count):
             sums_ref[r, n] = each[r]
+    query_ref[...] = query
+    gate_ref[...] = sigmoid(dot(own_in, w_gate[...]))
+    after_ref[...] = own_after[rows, :]
 
 
 def attention_kernel(
@@ -535,52 +517,51 @@
     repeat = jnp.where(head == head_of_channel, 1.0, 0.0).astype(bf16)
     wide_bias = dot(w_pair_bias, repeat).astype(bf16)
 
-    kept = lax.dynamic_update_slice(
-        jnp.zeros((2 * row_count, res, channels), bf16), pair_rep, (0, 0, 0)
-    )
-    far = exchange(pair_rep, devices // 2)
-    far, kept, norms, edge_weights = lax.optimization_barrier((far, kept, norms, edge_weights))
-    own = lax.dynamic_update_slice(kept, far, (row_count, 0, 0))
-    own_blocks = (0, chips // 2)
-
-    def blocks_from(bits):
-        return tuple(s ^ bits for s in own_blocks)
+    far = exchange(pair_rep, 8)
+    near = exchange(pair_rep, 4)
+    beside = exchange(pair_rep, 2)
+    far, near, beside, norms, edge_weights = lax.optimization_barrier(
+        (far, near, beside, norms, edge_weights)
+    )
 
     tall = shaped(f32, half * res, channels)
 
     def edges_of(pieces, send_row, *held):
+        to_send = (2 if send_row == 0 and held else 6) * row_count
         pairs = tuple(p for p, _ in pieces)
         blocks = tuple(b for _, b in pieces)
         operands = (valid_column, norms, edge_weights) + pairs + held
         first = len(operands) - len(held)
         return call(
-            functools.partial(edges_kernel, row_count, chips, blocks, send_row),
-            (tall, tall, tall, tall, shaped(bf16, 4 * row_count, res, channels))
+            functools.partial(edges_kernel, row_count, chips, blocks, send_row, not held),
+            (tall, tall, tall, tall, shaped(bf16, to_send, res, channels))
             + (() if held else (shaped(bf16, 2 * channels, 2 * channels),)),
             operands,
             {first + e: e for e in range(len(held))},
         )
 
-    diagonal = exchange(own, 6)
-    beside = exchange(own, 2)
-    near = exchange(own, 4)
-    *edges, early_right, same_head = edges_of([(own, own_blocks)], 0)
-    diagonal, edges = lax.optimization_barrier((diagonal, edges))
+    diagonal_far = exchange(far, 6)
+    beside_more = exchange(jnp.concatenate([far, near], axis=0), 2)
+    near_far = exchange(far, 4)
+    *edges, early_right, same_head = edges_of(
+        [(pair_rep, (0,)), (far, (4,)), (near, (2,)), (beside, (1,))], 0
+    )
+    diagonal_far, near_far, edges, early_right = lax.optimization_barrier(
+        (diagonal_far, near_far, edges, early_right)
+    )
     *edges, early_right = edges_of(
-        [(diagonal, blocks_from(3))], 2 * row_count, *edges, early_right
-    )
-    beside, edges, early_right, wide_bias = lax.optimization_barrier(
-        (beside, edges, early_right, wide_bias)
-    )
-    early = (exchange(early_right, 1), own_blocks + blocks_from(3))
-    *edges, late_right = edges_of(
-        [(beside, blocks_from(1)), (near, blocks_from(2))], 0, *edges
-    )
-    late = (exchange(late_right, 1), blocks_from(1) + blocks_from(2))
+        [(diagonal_far, (7,)), (near_far, (6,))], 4 * row_count, *edges, early_right
+    )
+    beside_more, edges, early_right, wide_bias = lax.optimization_barrier(
+        (beside_more, edges, early_right, wide_bias)
+    )
+    early = (exchange(early_right, 1), (0, 4, 2, 1, 7, 6))
+    *edges, late_right = edges_of([(beside_more, (5, 3))], 0, *edges)
+    late = (exchange(late_right, 1), (5, 3))
 
     left, right, gate, pairs = edges
     triangle, across = call(
-        functools.partial(near_triangle_kernel, row_count, chips, 4, [early[1]]),
+        functools.partial(near_triangle_kernel, row_count, chips, half // 2, [early[1]]),
         (tall, tall),
         (left, right, early[0]),
     )
@@ -589,17 +570,17 @@
     att_part = shaped(bf16, part, channels)
     shared = (norms, w_tri_out, left, gate, pairs)
     triangle, across, after_a, att_a = call(
-        functools.partial(own_inputs_kernel, row_count, chips, 4, late[1]),
+        functools.partial(own_inputs_kernel, row_count, chips, late[1]),
         (tall, tall, in_part, att_part),
         shared + (late[0], triangle, across),
         {6: 0, 7: 1},
     )
     far_att_a = exchange(att_a, 1)
-    _, _, att_b, query, att_gate, after_own, keys_a, values_a = call(
-        functools.partial(other_inputs_kernel, row_count, chips, 4),
-        (tall, in_part, att_part, own_shape, own_shape, own_shape, in_part, in_part),
-        shared + (w_query, w_att_gate, w_key, w_value, att_a, after_a, triangle, across),
-        {11: 0},
+    _, _, att_b = call(
+        functools.partial(other_inputs_kernel, row_count, chips),
+        (tall, in_part, att_part),
+        shared + (triangle, across),
+        {5: 0},
     )
     far_att_b = exchange(att_b, 1)
 
@@ -612,12 +593,12 @@
             pltpu.VMEM((row_count * keys * res, channels), f32),
         )
 
-    sums = call(
+    sums, query, att_gate, after_own = call(
         functools.partial(most_attention_kernel, row_count, chips),
-        shaped(f32, row_count, 3, res, channels),
-        (valid_column, same_head, w_key, w_value, wide_bias, att_a, att_b, far_att_a)
-        + (query, keys_a, values_a),
-        scratch=attention_scratch(3 * half // 2, half),
+        (shaped(f32, row_count, 3, res, channels), own_shape, own_shape, own_shape),
+        (valid_column, same_head, w_query, w_att_gate, w_key, w_value, wide_bias)
+        + (att_a, att_b, far_att_a, after_a),
+        scratch=attention_scratch(3 * half // 2, 3 * half // 2),
     )
     return call(
         functools.partial(attention_kernel, row_count, chips),

time: 23 us -> 26.4 us (1.15)
  starting transfers between devices: 8.23 us -> 11.8 us
  Pallas kernels: 8.8 us -> 8.39 us
    ppermute x8 -> x10, starting transfers between devices: 8.23 us -> 11.8 us  [exchange(): return lax.ppermute(values, 'row', [(d, d ^ bit) for d in range(devices)])]
    pallas_call x8, Pallas kernels: 8.8 us -> 8.39 us  [call(): pl.pallas_call(kernel, out_shape=outs, in_specs=[in_vmem] * len(operands)...]
    ppermute x8 -> x10, waiting for transfers between devices: 3.12 us -> 3.34 us  [exchange(): return lax.ppermute(values, 'row', [(d, d ^ bit) for d in range(devices)])]
  transfers between devices with their start and end apart: 8 -> 10, of which waited for: 5 -> 4; matrix products, arithmetic and copies ran while one was open for 6% -> 5% of each run, Pallas kernels for 27% -> 22%
where the time goes in v9:
time: 26.4 us; the launch traced here: 26.2 us
  starting transfers between devices  11.8 us (45%)
  Pallas kernels  8.39 us (32%)
  waiting for transfers between devices  3.34 us (13%)
  local copies, waits for them, and re-layouts  1.31 us (5%)
  other arithmetic  0.96 us (4%)
    ppermute x10, starting transfers between devices, exchange(): return lax.ppermute(values, 'row', [(d, d ^ bit) for d in range(devices)])  11.8 us
    pallas_call x8, Pallas kernels, call(): pl.pallas_call(kernel, out_shape=outs, in_specs=[in_vmem] * len(operands)...  8.39 us
    ppermute x10, waiting for transfers between devices, exchange(): return lax.ppermute(values, 'row', [(d, d ^ bit) for d in range(devices)])  3.34 us
    unnamed x30, local copies, waits for them, and re-layouts  1.21 us
    concatenate x1, other arithmetic, on_whole_complex(): edge_weights = jnp.concatenate([w_edges, w_tri_gate], axis=1)  0.94 us
  transfers between devices with their start and end apart: 10, of which 4 were waited for; matrix products, arithmetic and copies ran while one was open for 5% of the time, Pallas kernels for 22%

profile of v9, /device:TPU:0, one launch (start us, length us, event | category | flops | bytes accessed | tf_op | source)
XLA Modules:
  0.0 26.2 jit_solution(9404426051247702594)
XLA Ops:
  0.0 4.0 %collective-permute-start = (bf16[3,48,128]{2,1,0:T(8,128)(2,1)}, bf16[3,48,128]{2,1,0:T(8,128)(2,1)S(1)}, u32[]{:S(2)}, u32[]{:S(2)}) collective-permute-start(bf16[3,48,128]{2,1,0:T(8,128)(2,1)} %refs_0_.1), channel_id=1, source_target_pairs={{0,8},{1,9},{2,10},{3,11},{4,12},{5,13},{6,14},{7,15},{8,0},{9,1},... | collective-permute-start | bytes 110600 | tf_op jit(solution)/shard_map/ppermute | solution.py:501
  4.0 1.6 %collective-permute-start.1 = (bf16[3,48,128]{2,1,0:T(8,128)(2,1)}, bf16[3,48,128]{2,1,0:T(8,128)(2,1)S(1)}, u32[]{:S(2)}, u32[]{:S(2)}) collective-permute-start(bf16[3,48,128]{2,1,0:T(8,128)(2,1)} %refs_0_.1), channel_id=1, source_target_pairs={{0,4},{1,5},{2,6},{3,7},{4,0},{5,1},{6,2},{7,3},{8,12},{9,13},{10,... | collective-permute-start | bytes 110600 | tf_op jit(solution)/shard_map/ppermute | solution.py:501
  5.6 1.5 %collective-permute-start.2 = (bf16[3,48,128]{2,1,0:T(8,128)(2,1)}, bf16[3,48,128]{2,1,0:T(8,128)(2,1)S(1)}, u32[]{:S(2)}, u32[]{:S(2)}) collective-permute-start(bf16[3,48,128]{2,1,0:T(8,128)(2,1)} %refs_0_.1), channel_id=1, source_target_pairs={{0,2},{1,3},{2,0},{3,1},{4,6},{5,7},{6,4},{7,5},{8,10},{9,11},{10,... | collective-permute-start | bytes 110600 | tf_op jit(solution)/shard_map/ppermute | solution.py:501
  7.1 0.9 %pad_maximum_fusion.weights = bf16[128,640]{1,0:T(8,128)(2,1)S(1)} fusion(bf16[128,128]{1,0:T(8,128)(2,1)} %param.22, bf16[128,512]{1,0:T(8,128)(2,1)} %param.21), kind=kLoop, calls=%fused_computation.2 | loop fusion | flops 327680 | bytes 327680 | tf_op jit(solution)/shard_map/concatenate | solution.py:512
  8.1 0.6 %copy-done.11 = f32[128]{0:T(128)S(1)} copy-done((f32[128]{0:T(128)S(1)}, f32[128]{0:T(128)}, u32[]{:S(2)}) %copy-start.11) | copy-done | bytes 536
  8.8 0.9 %collective-permute-done.2.refs_3_ = bf16[3,48,128]{2,1,0:T(8,128)(2,1)S(1)} collective-permute-done((bf16[3,48,128]{2,1,0:T(8,128)(2,1)}, bf16[3,48,128]{2,1,0:T(8,128)(2,1)S(1)}, u32[]{:S(2)}, u32[]{:S(2)}) %collective-permute-start.2) | collective-permute-done | bytes 36896 | tf_op jit(solution)/shard_map/ppermute | solution.py:501
  9.8 1.4 %collective-permute-start.4 = (bf16[3,48,128]{2,1,0:T(8,128)(2,1)S(1)}, bf16[3,48,128]{2,1,0:T(8,128)(2,1)S(1)}, u32[]{:S(2)}, u32[]{:S(2)}) collective-permute-start(bf16[3,48,128]{2,1,0:T(8,128)(2,1)S(1)} %collective-permute-done.refs_1_), channel_id=1, source_target_pairs={{0,6},{1,7},{2,4},{3,5},{4,2},{5,3},{6,0},{7,1},{8,14},{9,15},{10,... | collective-permute-start | bytes 110600 | tf_op jit(solution)/shard_map/ppermute | solution.py:501
  11.2 1.6 %collective-permute-start.5 = (bf16[3,48,128]{2,1,0:T(8,128)(2,1)S(1)}, bf16[3,48,128]{2,1,0:T(8,128)(2,1)S(1)}, u32[]{:S(2)}, u32[]{:S(2)}) collective-permute-start(bf16[3,48,128]{2,1,0:T(8,128)(2,1)S(1)} %collective-permute-done.refs_1_), channel_id=1, source_target_pairs={{0,4},{1,5},{2,6},{3,7},{4,0},{5,1},{6,2},{7,3},{8,12},{9,13},{10,... | collective-permute-start | bytes 110600 | tf_op jit(solution)/shard_map/ppermute | solution.py:501
  12.8 0.6 %collective-permute-start.3 = (bf16[6,48,128]{2,1,0:T(8,128)(2,1)S(1)}, bf16[6,48,128]{2,1,0:T(8,128)(2,1)S(1)}, u32[]{:S(2)}, u32[]{:S(2)}) collective-permute-start(bf16[6,48,128]{2,1,0:T(8,128)(2,1)S(1)} %pad_maximum_fusion.1), channel_id=1, source_target_pairs={{0,2},{1,3},{2,0},{3,1},{4,6},{5,7},{6,4},{7,5},{8,10},{9,11},{10,... | collective-permute-start | bytes 221192 | tf_op jit(solution)/shard_map/ppermute | solution.py:501
  13.4 0.2 fusion.wide_bias
  13.6 0.4 %copy-done.14 = s32[48]{0:T(128)S(1)} copy-done((s32[48]{0:T(128)S(1)}, s32[48]{0:T(128)}, u32[]{:S(2)}) %copy-start.14) | copy-done | bytes 216
  14.1 0.6 %shard_map.163 = (f32[1152,128]{1,0:T(8,128)S(1)}, f32[1152,128]{1,0:T(8,128)S(1)}, f32[1152,128]{1,0:T(8,128)S(1)}, f32[1152,128]{1,0:T(8,128)S(1)}, bf16[18,48...) custom-call(f32[48,128]{1,0:T(8,128)S(1)} %broadcast_in_dim.14.valid_column, f32[6,128]{1,0:T(8,128)S(1)} %stack.27.norms, ...), custom_call_target="tpu_custom_call" | custom-call | flops 1048576 | bytes 33554432 | tf_op jit(solution)/shard_map/pallas_call | solution.py:489
  14.8 0.3 %collective-permute-done.5.refs_1_ = bf16[3,48,128]{2,1,0:T(8,128)(2,1)S(1)} collective-permute-done((bf16[3,48,128]{2,1,0:T(8,128)(2,1)S(1)}, bf16[3,48,128]{2,1,0:T(8,128)(2,1)S(1)}, u32[]{:S(2)}, u32[]{:S(2)}) %collective-permute-start.5) | collective-permute-done | bytes 36896 | tf_op jit(solution)/shard_map/ppermute | solution.py:501
  15.1 0.4 %shard_map.164 = (f32[1152,128]{1,0:T(8,128)S(1)}, f32[1152,128]{1,0:T(8,128)S(1)}, f32[1152,128]{1,0:T(8,128)S(1)}, f32[1152,128]{1,0:T(8,128)S(1)}, bf16[18,48,128]{2,1,0:T(8,128)(2,1)S(1)}) custom-call(f32[48,128]{1,0:T(8,128)S(1)} %broadcast_in_dim.14.valid_column, ...), custom_call_target="tpu_custom_call", output_to_operand_aliasing={{0}: (5, {}), {1}: (6, {}), {2}: (7, {}), {3}: (8, {}), {4}... | custom-call | flops 1048576 | bytes 33554432 | tf_op jit(solution)/shard_map/pallas_call | solution.py:489
  15.6 1.6 %collective-permute-done.3.refs_0_ = bf16[6,48,128]{2,1,0:T(8,128)(2,1)S(1)} collective-permute-done((bf16[6,48,128]{2,1,0:T(8,128)(2,1)S(1)}, bf16[6,48,128]{2,1,0:T(8,128)(2,1)S(1)}, u32[]{:S(2)}, u32[]{:S(2)}) %collective-permute-start.3) | collective-permute-done | bytes 73760 | tf_op jit(solution)/shard_map/ppermute | solution.py:501
  17.2 0.4 %shard_map.165 = (f32[1152,128]{1,0:T(8,128)S(1)}, f32[1152,128]{1,0:T(8,128)S(1)}, f32[1152,128]{1,0:T(8,128)S(1)}, f32[1152,128]{1,0:T(8,128)S(1)}, bf16[6,48,128]{2,1,0:T(8,128)(2,1)S(1)}) custom-call(f32[48,128]{1,0:T(8,128)S(1)} %broadcast_in_dim.14.valid_column, ...), custom_call_target="tpu_custom_call", output_to_operand_aliasing={{0}: (4, {}), {1}: (5, {}), {2}: (6, {}), {3}: (7, {})} | custom-call | flops 1048576 | bytes 33554432 | tf_op jit(solution)/shard_map/pallas_call | solution.py:489
  17.6 0.6 %collective-permute-start.6 = (bf16[6,48,128]{2,1,0:T(8,128)(2,1)S(1)}, bf16[6,48,128]{2,1,0:T(8,128)(2,1)S(1)}, u32[]{:S(2)}, u32[]{:S(2)}) collective-permute-start(bf16[6,48,128]{2,1,0:T(8,128)(2,1)S(1)} %get-tuple-element.83), channel_id=1, source_target_pairs={{0,1},{1,0},{2,3},{3,2},{4,5},{5,4},{6,7},{7,6},{8,9},{9,8},{10,11... | collective-permute-start | bytes 221192 | tf_op jit(solution)/shard_map/ppermute | solution.py:501
  18.2 0.5 %collective-permute-done.7.refs_0_ = bf16[18,48,128]{2,1,0:T(8,128)(2,1)S(1)} collective-permute-done((bf16[18,48,128]{2,1,0:T(8,128)(2,1)S(1)}, bf16[18,48,128]{2,1,0:T(8,128)(2,1)S(1)}, u32[]{:S(2)}, u32[]{:S(2)}) %collective-permute-start.7) | collective-permute-done | bytes 221216 | tf_op jit(solution)/shard_map/ppermute | solution.py:501
  18.7 1.2 %shard_map.166 = (f32[1152,128]{1,0:T(8,128)S(1)}, f32[1152,128]{1,0:T(8,128)S(1)}) custom-call(f32[1152,128]{1,0:T(8,128)S(1)} %get-tuple-element.80.left_ref, f32[1152,128]{1,0:T(8,128)S(1)} %get-tuple-element.84.right_ref, bf16[18,48,128]{2,1,0:T(8,128)(2,1)S(1)} %collective-permute-done.7.refs_0_), custom_call_target="tpu_custom_call" | custom-call | flops 1048576 | bytes 33554432 | tf_op jit(solution)/shard_map/pallas_call | solution.py:489
  19.9 1.1 %shard_map.167 = (f32[1152,128]{1,0:T(8,128)S(1)}, f32[1152,128]{1,0:T(8,128)S(1)}, f32[576,128]{1,0:T(8,128)S(1)}, bf16[576,128]{1,0:T(8,128)(2,1)S(1)}) custom-call(f32[6,128]{1,0:T(8,128)S(1)} %stack.27.norms, bf16[128,128]{1,0:T(8,128)(2,1)S(1)} %copy-done.1, ...), custom_call_target="tpu_custom_call", output_to_operand_aliasing={{0}: (6, {}), {1}: (7, {})} | custom-call | flops 1048576 | bytes 33554432 | tf_op jit(solution)/shard_map/pallas_call | solution.py:489
  21.2 1.7 %shard_map.168 = (f32[1152,128]{1,0:T(8,128)S(1)}, f32[576,128]{1,0:T(8,128)}, bf16[576,128]{1,0:T(8,128)(2,1)S(1)}) custom-call(f32[6,128]{1,0:T(8,128)S(1)} %stack.27.norms, bf16[128,128]{1,0:T(8,128)(2,1)S(1)} %copy-done.1, f32[1152,128]{1,0:T(8,128)S(1)} %get-tuple-element.80.left_ref, ...), custom_call_target="tpu_custom_call", output_to_operand_aliasing={{0}: (5, {})} | custom-call | flops 1048576 | bytes 33554432 | tf_op jit(solution)/shard_map/pallas_call | solution.py:489
  22.9 0.4 %collective-permute-start.8 = (bf16[576,128]{1,0:T(8,128)(2,1)S(1)}, bf16[576,128]{1,0:T(8,128)(2,1)S(1)}, u32[]{:S(2)}, u32[]{:S(2)}) collective-permute-start(bf16[576,128]{1,0:T(8,128)(2,1)S(1)} %get-tuple-element.90.own_att_b), channel_id=1, source_target_pairs={{0,1},{1,0},{2,3},{3,2},{4,5},{5,4},{6,7},{7,6},{8,9},{9,8},{10,11... | collective-permute-start | bytes 442376 | tf_op jit(solution)/shard_map/ppermute | solution.py:501
  23.3 1.4 %shard_map.169 = (f32[3,3,48,128]{3,2,1,0:T(8,128)S(1)}, f32[144,128]{1,0:T(8,128)S(1)}, f32[144,128]{1,0:T(8,128)S(1)}, f32[144,128]{1,0:T(8,128)S(1)}) custom-call(f32[48,128]{1,0:T(8,128)S(1)} %broadcast_in_dim.14.valid_column, bf16[256,256]{1,0:T(8,128)(2,1)S(1)} %get-tuple-element.56.same_head, bf16[128,128]{1,0:T(8,128)(2,1)S(1)} %copy-done.5, ...), custom_call_target="tpu_custom_call" | custom-call | flops 1048576 | bytes 33554432 | tf_op jit(solution)/shard_map/pallas_call | solution.py:489
  24.8 1.4 %shard_map.170 = bf16[3,48,128]{2,1,0:T(8,128)(2,1)} custom-call(f32[48,128]{1,0:T(8,128)S(1)} %broadcast_in_dim.14.valid_column, bf16[256,256]{1,0:T(8,128)(2,1)S(1)} %get-tuple-element.56.same_head, bf16[128,128]{1,0:T(8,128)(2,1)S(1)} %copy-done.2, bf16[128,128]{1,0:T(8,128)(2,1)S(1)} %copy-done.3, bf16[128,128]{1,0:T(8,128)(2,1)S(1)} %copy-done.7, ...), custom_call_target="tpu_custom_call" | custom-call | flops 1048576 | bytes 33554432 | tf_op jit(solution)/shard_map/pallas_call | solution.py:489
  (42 shorter events, 0.5 us)
Async XLA Ops:
  0.0 13.4 %copy-start = (bf16[128,4]{0,1:T(4,128)(2,1)S(1)}, bf16[128,4]{0,1:T(4,128)(2,1)}, u32[]{:S(2)}) copy-start(bf16[128,4]{0,1:T(4,128)(2,1)} %param.32) | copy-start | bytes 3076
  0.0 8.8 %collective-permute-start = (bf16[3,48,128]{2,1,0:T(8,128)(2,1)}, bf16[3,48,128]{2,1,0:T(8,128)(2,1)S(1)}, u32[]{:S(2)}, u32[]{:S(2)}) collective-permute-start(bf16[3,48,128]{2,1,0:T(8,128)(2,1)} %refs_0_.1), channel_id=1, source_target_pairs={{0,8},{1,9},{2,10},{3,11},{4,12},{5,13},{6,14},{7,15},{8,0},{9,1},... | collective-permute-start | bytes 110600 | tf_op jit(solution)/shard_map/ppermute | solution.py:501
  4.0 4.8 %collective-permute-start.1 = (bf16[3,48,128]{2,1,0:T(8,128)(2,1)}, bf16[3,48,128]{2,1,0:T(8,128)(2,1)S(1)}, u32[]{:S(2)}, u32[]{:S(2)}) collective-permute-start(bf16[3,48,128]{2,1,0:T(8,128)(2,1)} %refs_0_.1), channel_id=1, source_target_pairs={{0,4},{1,5},{2,6},{3,7},{4,0},{5,1},{6,2},{7,3},{8,12},{9,13},{10,... | collective-permute-start | bytes 110600 | tf_op jit(solution)/shard_map/ppermute | solution.py:501
  5.6 4.2 %collective-permute-start.2 = (bf16[3,48,128]{2,1,0:T(8,128)(2,1)}, bf16[3,48,128]{2,1,0:T(8,128)(2,1)S(1)}, u32[]{:S(2)}, u32[]{:S(2)}) collective-permute-start(bf16[3,48,128]{2,1,0:T(8,128)(2,1)} %refs_0_.1), channel_id=1, source_target_pairs={{0,2},{1,3},{2,0},{3,1},{4,6},{5,7},{6,4},{7,5},{8,10},{9,11},{10,... | collective-permute-start | bytes 110600 | tf_op jit(solution)/shard_map/ppermute | solution.py:501
  8.1 0.7 %copy-start.11 = (f32[128]{0:T(128)S(1)}, f32[128]{0:T(128)}, u32[]{:S(2)}) copy-start(f32[128]{0:T(128)} %param.24) | copy-start | bytes 1540
  8.1 0.7 %copy-start.12 = (f32[128]{0:T(128)S(1)}, f32[128]{0:T(128)}, u32[]{:S(2)}) copy-start(f32[128]{0:T(128)} %param.26) | copy-start | bytes 1540
  8.1 0.7 %copy-start.13 = (f32[128]{0:T(128)S(1)}, f32[128]{0:T(128)}, u32[]{:S(2)}) copy-start(f32[128]{0:T(128)} %param.27) | copy-start | bytes 1540
  8.1 0.7 %copy-start.8 = (f32[128]{0:T(128)S(1)}, f32[128]{0:T(128)}, u32[]{:S(2)}) copy-start(f32[128]{0:T(128)} %param.19) | copy-start | bytes 1540
  8.1 0.7 %copy-start.9 = (f32[128]{0:T(128)S(1)}, f32[128]{0:T(128)}, u32[]{:S(2)}) copy-start(f32[128]{0:T(128)} %param.20) | copy-start | bytes 1540
  8.1 0.7 %copy-start.10 = (f32[128]{0:T(128)S(1)}, f32[128]{0:T(128)}, u32[]{:S(2)}) copy-start(f32[128]{0:T(128)} %param.23) | copy-start | bytes 1540
  9.8 5.0 %collective-permute-start.4 = (bf16[3,48,128]{2,1,0:T(8,128)(2,1)S(1)}, bf16[3,48,128]{2,1,0:T(8,128)(2,1)S(1)}, u32[]{:S(2)}, u32[]{:S(2)}) collective-permute-start(bf16[3,48,128]{2,1,0:T(8,128)(2,1)S(1)} %collective-permute-done.refs_1_), channel_id=1, source_target_pairs={{0,6},{1,7},{2,4},{3,5},{4,2},{5,3},{6,0},{7,1},{8,14},{9,15},{10,... | collective-permute-start | bytes 110600 | tf_op jit(solution)/shard_map/ppermute | solution.py:501
  11.2 4.0 %collective-permute-start.5 = (bf16[3,48,128]{2,1,0:T(8,128)(2,1)S(1)}, bf16[3,48,128]{2,1,0:T(8,128)(2,1)S(1)}, u32[]{:S(2)}, u32[]{:S(2)}) collective-permute-start(bf16[3,48,128]{2,1,0:T(8,128)(2,1)S(1)} %collective-permute-done.refs_1_), channel_id=1, source_target_pairs={{0,4},{1,5},{2,6},{3,7},{4,0},{5,1},{6,2},{7,3},{8,12},{9,13},{10,... | collective-permute-start | bytes 110600 | tf_op jit(solution)/shard_map/ppermute | solution.py:501
  12.8 4.4 %collective-permute-start.3 = (bf16[6,48,128]{2,1,0:T(8,128)(2,1)S(1)}, bf16[6,48,128]{2,1,0:T(8,128)(2,1)S(1)}, u32[]{:S(2)}, u32[]{:S(2)}) collective-permute-start(bf16[6,48,128]{2,1,0:T(8,128)(2,1)S(1)} %pad_maximum_fusion.1), channel_id=1, source_target_pairs={{0,2},{1,3},{2,0},{3,1},{4,6},{5,7},{6,4},{7,5},{8,10},{9,11},{10,... | collective-permute-start | bytes 221192 | tf_op jit(solution)/shard_map/ppermute | solution.py:501
  13.4 0.8 %copy-start.4 = (bf16[3,48,128]{2,1,0:T(8,128)(2,1)S(1)}, bf16[3,48,128]{2,1,0:T(8,128)(2,1)}, u32[]{:S(2)}) copy-start(bf16[3,48,128]{2,1,0:T(8,128)(2,1)} %refs_0_.1) | copy-start | bytes 110596
  17.2 1.5 %collective-permute-start.7 = (bf16[18,48,128]{2,1,0:T(8,128)(2,1)S(1)}, bf16[18,48,128]{2,1,0:T(8,128)(2,1)S(1)}, u32[]{:S(2)}, u32[]{:S(2)}) collective-permute-start(bf16[18,48,128]{2,1,0:T(8,128)(2,1)S(1)} %get-tuple-element.85), channel_id=1, source_target_pairs={{0,1},{1,0},{2,3},{3,2},{4,5},{5,4},{6,7},{7,6},{8,9},{9,8},{10,11... | collective-permute-start | bytes 663560 | tf_op jit(solution)/shard_map/ppermute | solution.py:501
  17.6 2.2 %collective-permute-start.6 = (bf16[6,48,128]{2,1,0:T(8,128)(2,1)S(1)}, bf16[6,48,128]{2,1,0:T(8,128)(2,1)S(1)}, u32[]{:S(2)}, u32[]{:S(2)}) collective-permute-start(bf16[6,48,128]{2,1,0:T(8,128)(2,1)S(1)} %get-tuple-element.83), channel_id=1, source_target_pairs={{0,1},{1,0},{2,3},{3,2},{4,5},{5,4},{6,7},{7,6},{8,9},{9,8},{10,11... | collective-permute-start | bytes 221192 | tf_op jit(solution)/shard_map/ppermute | solution.py:501
  18.6 1.2 %copy-start.1 = (bf16[128,128]{1,0:T(8,128)(2,1)S(1)}, bf16[128,128]{1,0:T(8,128)(2,1)}, u32[]{:S(2)}) copy-start(bf16[128,128]{1,0:T(8,128)(2,1)} %w_out.4) | copy-start | bytes 98308
  21.0 2.3 %collective-permute-start.9 = (bf16[576,128]{1,0:T(8,128)(2,1)S(1)}, bf16[576,128]{1,0:T(8,128)(2,1)S(1)}, u32[]{:S(2)}, u32[]{:S(2)}) collective-permute-start(bf16[576,128]{1,0:T(8,128)(2,1)S(1)} %get-tuple-element.91.own_att_a), channel_id=1, source_target_pairs={{0,1},{1,0},{2,3},{3,2},{4,5},{5,4},{6,7},{7,6},{8,9},{9,8},{10,11... | collective-permute-start | bytes 442376 | tf_op jit(solution)/shard_map/ppermute | solution.py:501
  21.2 2.1 %copy-start.2 = (bf16[128,128]{1,0:T(8,128)(2,1)S(1)}, bf16[128,128]{1,0:T(8,128)(2,1)}, u32[]{:S(2)}) copy-start(bf16[128,128]{1,0:T(8,128)(2,1)} %w_key.3) | copy-start | bytes 98308
  21.2 2.1 %copy-start.3 = (bf16[128,128]{1,0:T(8,128)(2,1)S(1)}, bf16[128,128]{1,0:T(8,128)(2,1)}, u32[]{:S(2)}) copy-start(bf16[128,128]{1,0:T(8,128)(2,1)} %w_value.3) | copy-start | bytes 98308
  21.2 2.1 %copy-start.5 = (bf16[128,128]{1,0:T(8,128)(2,1)S(1)}, bf16[128,128]{1,0:T(8,128)(2,1)}, u32[]{:S(2)}) copy-start(bf16[128,128]{1,0:T(8,128)(2,1)} %w_query.1) | copy-start | bytes 98308
  21.2 2.1 %copy-start.6 = (bf16[128,128]{1,0:T(8,128)(2,1)S(1)}, bf16[128,128]{1,0:T(8,128)(2,1)}, u32[]{:S(2)}) copy-start(bf16[128,128]{1,0:T(8,128)(2,1)} %w_gate.1) | copy-start | bytes 98308
  22.9 1.9 %collective-permute-start.8 = (bf16[576,128]{1,0:T(8,128)(2,1)S(1)}, bf16[576,128]{1,0:T(8,128)(2,1)S(1)}, u32[]{:S(2)}, u32[]{:S(2)}) collective-permute-start(bf16[576,128]{1,0:T(8,128)(2,1)S(1)} %get-tuple-element.90.own_att_b), channel_id=1, source_target_pairs={{0,1},{1,0},{2,3},{3,2},{4,5},{5,4},{6,7},{7,6},{8,9},{9,8},{10,11... | collective-permute-start | bytes 442376 | tf_op jit(solution)/shard_map/ppermute | solution.py:501
  23.3 1.5 %copy-start.7 = (bf16[128,128]{1,0:T(8,128)(2,1)S(1)}, bf16[128,128]{1,0:T(8,128)(2,1)}, u32[]{:S(2)}) copy-start(bf16[128,128]{1,0:T(8,128)(2,1)} %w_out.5) | copy-start | bytes 98308
  (1 other events, 0.7 us)

commit v10 on v9

--- a/solution.py
+++ b/solution.py
@@ -198,7 +198,9 @@
     return parts[0]
 
 
-def triangle_rows(row_count, chips, left_ref, right_ref, triangle_ref, first, count, core):
+def triangle_rows(
+    row_count, chips, left_ref, right_ref, triangle_ref, first, count, core, triangle_first
+):
     res = 2 * row_count * chips
     start = pl.multiple_of(first * res, res)
     block = 4
@@ -215,7 +217,7 @@
                         sum(product[k : k + 8] for k in range(8, res, 8)) + product[:8]
                     )
             for m in range(block):
-                place = start + (n + m) * res + core * row_count + r
+                place = (triangle_first + n + m) * res + core * row_count + r
                 triangle_ref[pl.ds(place, chips, stride=2 * row_count), :] = rounded(
                     sum_sublanes(parts[m])
                 )
@@ -228,7 +230,7 @@
     def some_rows(step, carry):
         first = step * chunk
         triangle_rows(
-            row_count, chips, left_ref, right_ref, triangle_ref, first, chunk, core
+            row_count, chips, left_ref, right_ref, triangle_ref, first, chunk, core, first
         )
         return carry
 
@@ -239,23 +241,22 @@
 
 
 def attention_inputs(
-    row_count, chips, first, norms, w_out, left_ref, gate_ref, pairs_ref, refs
-):
-    f32, bf16 = jnp.float32, jnp.bfloat16
-    triangle_ref, across_ref, after_ref, att_ref = refs
+    row_count, chips, first, norms, w_out, left_ref, gate_ref, pairs_ref, held_triangle, across_ref,
+    triangle_ref,
+):
+    bf16 = jnp.bfloat16
     _, core = chip_and_core()
     half = row_count * chips
     tall = (half // 2) * 2 * half
-
+    rows = pl.ds(pl.multiple_of(first * 2 * half, tall), tall)
+    triangle_ref[...] = held_triangle[rows, :]
     triangle_rows(
-        row_count, chips, left_ref, across_ref, triangle_ref, first, half // 2, 1 - core
-    )
-    rows = pl.ds(pl.multiple_of(first * 2 * half, tall), tall)
-    tri_normed = layer_norm(triangle_ref[rows, :], norms[2:3, :], norms[3:4, :], 1).astype(bf16)
+        row_count, chips, left_ref, across_ref, triangle_ref, first, half // 2, 1 - core, 0
+    )
+    tri_normed = layer_norm(triangle_ref[...], norms[2:3, :], norms[3:4, :], 1).astype(bf16)
     after_tri = pairs_ref[rows, :] + gate_ref[rows, :] * dot(tri_normed, w_out[...])
     att_in = layer_norm(after_tri, norms[4:5, :], norms[5:6, :], 1).astype(bf16)
-    after_ref[...] = after_tri
-    att_ref[...] = att_in
+    return after_tri, att_in
 
 
 def first_chip(chips, part):
@@ -264,35 +265,35 @@
 
 
 def own_inputs_kernel(
-    row_count, chips, blocks, norms, w_out, left_ref, gate_ref, pairs_ref, received, *refs
-):
-    for n, (chip, r) in enumerate(rows_of_blocks(row_count, blocks)):
-        place_right(refs[-3], chips, chip, r, received[n])
-    first = first_chip(chips, 0) * row_count
-    attention_inputs(
-        row_count, chips, first, norms, w_out, left_ref, gate_ref, pairs_ref, refs[-4:]
-    )
-
-
-def other_inputs_kernel(
     row_count,
     chips,
+    blocks,
     norms,
     w_out,
     left_ref,
     gate_ref,
     pairs_ref,
-    held_triangle,
+    received,
+    triangle_ref,
+    held_across,
     across_ref,
-    triangle_ref,
     after_ref,
     att_ref,
-):
+    scratch_ref,
+):
+    for n, (chip, r) in enumerate(rows_of_blocks(row_count, blocks)):
+        place_right(across_ref, chips, chip, r, received[n])
+    first = first_chip(chips, 0) * row_count
+    refs = (left_ref, gate_ref, pairs_ref, triangle_ref, across_ref, scratch_ref)
+    after_ref[...], att_ref[...] = attention_inputs(
+        row_count, chips, first, norms, w_out, *refs
+    )
+
+
+def other_inputs_kernel(row_count, chips, norms, w_out, *refs):
+    *refs, att_ref, scratch_ref = refs
     first = first_chip(chips, 1) * row_count
-    refs = (triangle_ref, across_ref, after_ref, att_ref)
-    attention_inputs(
-        row_count, chips, first, norms, w_out, left_ref, gate_ref, pairs_ref, refs
-    )
+    _, att_ref[...] = attention_inputs(row_count, chips, first, norms, w_out, *refs, scratch_ref)
 
 
 def keys_and_values(att, w_key, w_value, key_ref, value_ref):
@@ -336,10 +337,14 @@
             k = (2 * (first + n // row_count) + core) * row_count + n % row_count
             key_mask = 1000000000.0 * (valid_column[pl.ds(k, 1), :] - 1.0)
             at = part * count + n
+            shifts = [
+                (bias_ref[r, at : at + 1, :] + key_mask) * math.log2(math.e)
+                for r in range(row_count)
+            ]
             lanes = slice(n % 2 * channels, (n % 2 + 1) * channels)
             for r in range(row_count):
                 start = (n // 2 * row_count + r) * res
-                score = scores[start : start + res, lanes] + bias_ref[r, at : at + 1, :] + key_mask
+                score = scores[start : start + res, lanes] + shifts[r]
                 score_ref[(r * keys + at) * res : (r * keys + at + 1) * res, :] = score
                 maxima[r] = jnp.maximum(maxima[r], score)
     totals, mixed = [], []
@@ -348,7 +353,7 @@
         for part, (_, _, _, value_of) in enumerate(parts):
             for n in range(count):
                 start = (r * keys + part * count + n) * res
-                weight = jnp.exp(score_ref[start : start + res, :] - maxima[r])
+                weight = jnp.exp2(score_ref[start : start + res, :] - maxima[r])
                 total = total + weight
                 mix = mix + weight * value_of(n)
         totals.append(total)
@@ -385,7 +390,7 @@
     own = row_count * res
     rows = pl.ds(pl.multiple_of(jnp.bitwise_and(chip, chips // 2 - 1) * own, own), own)
     own_in = own_att_a[rows, :]
-    query = rounded(dot(own_in, w_query[...])) * (1.0 / math.sqrt(HEAD_DIM))
+    query = rounded(dot(own_in, w_query[...])) * (math.log2(math.e) / math.sqrt(HEAD_DIM))
     att = [ref[...] for ref in (own_att_a, own_att_b, far_att_a)]
     keys_and_values(att, w_key, w_value, key_ref, value_ref)
     column_bias(row_count, res, att, wide_bias, att_ref, bias_ref)
@@ -447,8 +452,8 @@
     attended = []
     for r, (last_maximum, last_total, last_mixed) in enumerate(zip(*last)):
         maximum = jnp.maximum(sums_ref[r, 0], last_maximum)
-        most_scale = jnp.exp(sums_ref[r, 0] - maximum)
-        last_scale = jnp.exp(last_maximum - maximum)
+        most_scale = jnp.exp2(sums_ref[r, 0] - maximum)
+        last_scale = jnp.exp2(last_maximum - maximum)
         total = sums_ref[r, 1] * most_scale + last_total * last_scale
         attended.append((sums_ref[r, 2] * most_scale + last_mixed * last_scale) / total)
     gated = (jnp.concatenate(attended, axis=0) * gate_ref[...]).astype(jnp.bfloat16)
@@ -517,47 +522,48 @@
     repeat = jnp.where(head == head_of_channel, 1.0, 0.0).astype(bf16)
     wide_bias = dot(w_pair_bias, repeat).astype(bf16)
 
-    far = exchange(pair_rep, 8)
-    near = exchange(pair_rep, 4)
-    beside = exchange(pair_rep, 2)
-    far, near, beside, norms, edge_weights = lax.optimization_barrier(
-        (far, near, beside, norms, edge_weights)
-    )
+    kept = lax.dynamic_update_slice(
+        jnp.zeros((2 * row_count, res, channels), bf16), pair_rep, (0, 0, 0)
+    )
+    far = exchange(pair_rep, devices // 2)
+    far, kept, norms, edge_weights = lax.optimization_barrier((far, kept, norms, edge_weights))
+    own = lax.dynamic_update_slice(kept, far, (row_count, 0, 0))
+    own_blocks = (0, chips // 2)
+
+    def blocks_from(bits):
+        return tuple(s ^ bits for s in own_blocks)
 
     tall = shaped(f32, half * res, channels)
 
     def edges_of(pieces, send_row, *held):
-        to_send = (2 if send_row == 0 and held else 6) * row_count
         pairs = tuple(p for p, _ in pieces)
         blocks = tuple(b for _, b in pieces)
         operands = (valid_column, norms, edge_weights) + pairs + held
         first = len(operands) - len(held)
         return call(
             functools.partial(edges_kernel, row_count, chips, blocks, send_row, not held),
-            (tall, tall, tall, tall, shaped(bf16, to_send, res, channels))
+            (tall, tall, tall, tall, shaped(bf16, 4 * row_count, res, channels))
             + (() if held else (shaped(bf16, 2 * channels, 2 * channels),)),
             operands,
             {first + e: e for e in range(len(held))},
         )
 
-    diagonal_far = exchange(far, 6)
-    beside_more = exchange(jnp.concatenate([far, near], axis=0), 2)
-    near_far = exchange(far, 4)
-    *edges, early_right, same_head = edges_of(
-        [(pair_rep, (0,)), (far, (4,)), (near, (2,)), (beside, (1,))], 0
-    )
-    diagonal_far, near_far, edges, early_right = lax.optimization_barrier(
-        (diagonal_far, near_far, edges, early_right)
-    )
+    diagonal = exchange(own, 6)
+    beside = exchange(own, 2)
+    near = exchange(own, 4)
+    *edges, early_right, same_head = edges_of([(own, own_blocks)], 0)
+    diagonal, edges = lax.optimization_barrier((diagonal, edges))
     *edges, early_right = edges_of(
-        [(diagonal_far, (7,)), (near_far, (6,))], 4 * row_count, *edges, early_right
-    )
-    beside_more, edges, early_right, wide_bias = lax.optimization_barrier(
-        (beside_more, edges, early_right, wide_bias)
-    )
-    early = (exchange(early_right, 1), (0, 4, 2, 1, 7, 6))
-    *edges, late_right = edges_of([(beside_more, (5, 3))], 0, *edges)
-    late = (exchange(late_right, 1), (5, 3))
+        [(diagonal, blocks_from(3))], 2 * row_count, *edges, early_right
+    )
+    beside, edges, early_right, wide_bias = lax.optimization_barrier(
+        (beside, edges, early_right, wide_bias)
+    )
+    early = (exchange(early_right, 1), own_blocks + blocks_from(3))
+    *edges, late_right = edges_of(
+        [(beside, blocks_from(1)), (near, blocks_from(2))], 0, *edges
+    )
+    late = (exchange(late_right, 1), blocks_from(1) + blocks_from(2))
 
     left, right, gate, pairs = edges
     triangle, across = call(
@@ -569,18 +575,20 @@
     in_part, own_shape = shaped(f32, part, channels), shaped(f32, row_count * res, channels)
     att_part = shaped(bf16, part, channels)
     shared = (norms, w_tri_out, left, gate, pairs)
-    triangle, across, after_a, att_a = call(
+    scratch = (pltpu.VMEM((part, channels), f32),)
+    across, after_a, att_a = call(
         functools.partial(own_inputs_kernel, row_count, chips, late[1]),
-        (tall, tall, in_part, att_part),
+        (tall, in_part, att_part),
         shared + (late[0], triangle, across),
-        {6: 0, 7: 1},
+        {7: 0},
+        scratch=scratch,
     )
     far_att_a = exchange(att_a, 1)
-    _, _, att_b = call(
+    att_b = call(
         functools.partial(other_inputs_kernel, row_count, chips),
-        (tall, in_part, att_part),
+        att_part,
         shared + (triangle, across),
-        {5: 0},
+        scratch=scratch,
     )
     far_att_b = exchange(att_b, 1)
 

time: 26.4 us -> 21.9 us (0.83)
  starting transfers between devices: 11.8 us -> 8.3 us
  Pallas kernels: 8.39 us -> 7.61 us
    ppermute x10 -> x8, starting transfers between devices: 11.8 us -> 8.3 us  [exchange(): return lax.ppermute(values, 'row', [(d, d ^ bit) for d in range(devices)])]
    pallas_call x8, Pallas kernels: 8.39 us -> 7.61 us  [call(): pl.pallas_call(kernel, out_shape=outs, in_specs=[in_vmem] * len(operands)...]
    ppermute x10 -> x8, waiting for transfers between devices: 3.34 us -> 3.15 us  [exchange(): return lax.ppermute(values, 'row', [(d, d ^ bit) for d in range(devices)])]
  transfers between devices with their start and end apart: 10 -> 8, of which waited for: 4 -> 5; matrix products, arithmetic and copies ran while one was open for 5% -> 6% of each run, Pallas kernels for 22% -> 23%
where the time goes in v10:
time: 21.9 us; the launch traced here: 21.7 us
  starting transfers between devices  8.3 us (38%)
  Pallas kernels  7.61 us (35%)
  waiting for transfers between devices  3.15 us (14%)
  local copies, waits for them, and re-layouts  1.28 us (6%)
  other arithmetic  0.96 us (4%)
    ppermute x8, starting transfers between devices, exchange(): return lax.ppermute(values, 'row', [(d, d ^ bit) for d in range(devices)])  8.3 us
    pallas_call x8, Pallas kernels, call(): pl.pallas_call(kernel, out_shape=outs, in_specs=[in_vmem] * len(operands)...  7.61 us
    ppermute x8, waiting for transfers between devices, exchange(): return lax.ppermute(values, 'row', [(d, d ^ bit) for d in range(devices)])  3.15 us
    unnamed x30, local copies, waits for them, and re-layouts  1.16 us
    concatenate x1, other arithmetic, on_whole_complex(): edge_weights = jnp.concatenate([w_edges, w_tri_gate], axis=1)  0.95 us
  transfers between devices with their start and end apart: 8, of which 5 were waited for; matrix products, arithmetic and copies ran while one was open for 6% of the time, Pallas kernels for 23%

profile of v10, /device:TPU:0, one launch (start us, length us, event | category | flops | bytes accessed | tf_op | source)
XLA Modules:
  0.0 21.7 jit_solution(8321147612569950624)
XLA Ops:
  0.0 4.0 %collective-permute-start = (bf16[3,48,128]{2,1,0:T(8,128)(2,1)}, bf16[3,48,128]{2,1,0:T(8,128)(2,1)S(1)}, u32[]{:S(2)}, u32[]{:S(2)}) collective-permute-start(bf16[3,48,128]{2,1,0:T(8,128)(2,1)} %param.17), channel_id=1, source_target_pairs={{0,8},{1,9},{2,10},{3,11},{4,12},{5,13},{6,14},{7,15},{8,0},{9,1},... | collective-permute-start | bytes 110600 | tf_op jit(solution)/shard_map/ppermute | solution.py:506
  4.0 0.9 %pad_maximum_fusion.weights = bf16[128,640]{1,0:T(8,128)(2,1)S(1)} fusion(bf16[128,128]{1,0:T(8,128)(2,1)} %param.22, bf16[128,512]{1,0:T(8,128)(2,1)} %param.21), kind=kLoop, calls=%fused_computation.2 | loop fusion | flops 327680 | bytes 327680 | tf_op jit(solution)/shard_map/concatenate | solution.py:517
  5.1 0.6 %copy-done.11 = f32[128]{0:T(128)S(1)} copy-done((f32[128]{0:T(128)S(1)}, f32[128]{0:T(128)}, u32[]{:S(2)}) %copy-start.11) | copy-done | bytes 536
  5.8 0.8 %collective-permute-done = bf16[3,48,128]{2,1,0:T(8,128)(2,1)S(1)} collective-permute-done((bf16[3,48,128]{2,1,0:T(8,128)(2,1)}, bf16[3,48,128]{2,1,0:T(8,128)(2,1)S(1)}, u32[]{:S(2)}, u32[]{:S(2)}) %collective-permute-start) | collective-permute-done | bytes 36896 | tf_op jit(solution)/shard_map/ppermute | solution.py:506
  6.6 2.5 %collective-permute-start.2 = (bf16[6,48,128]{2,1,0:T(8,128)(2,1)S(1)}, bf16[6,48,128]{2,1,0:T(8,128)(2,1)S(1)}, u32[]{:S(2)}, u32[]{:S(2)}) collective-permute-start(bf16[6,48,128]{2,1,0:T(8,128)(2,1)S(1)} %constant_dynamic-update-slice_fusion.refs_0_), channel_id=1, source_target_pairs={{0,6},{1,7},{2,4},{3,5},{4,2},{5,3},{6,0},{7,1},{8,14},{9,15},{10,... | collective-permute-start | bytes 221192 | tf_op jit(solution)/shard_map/ppermute | solution.py:506
  9.1 0.5 %collective-permute-start.1 = (bf16[6,48,128]{2,1,0:T(8,128)(2,1)S(1)}, bf16[6,48,128]{2,1,0:T(8,128)(2,1)S(1)}, u32[]{:S(2)}, u32[]{:S(2)}) collective-permute-start(bf16[6,48,128]{2,1,0:T(8,128)(2,1)S(1)} %constant_dynamic-update-slice_fusion.refs_0_), channel_id=1, source_target_pairs={{0,2},{1,3},{2,0},{3,1},{4,6},{5,7},{6,4},{7,5},{8,10},{9,11},{10,... | collective-permute-start | bytes 221192 | tf_op jit(solution)/shard_map/ppermute | solution.py:506
  9.6 0.5 %collective-permute-start.3 = (bf16[6,48,128]{2,1,0:T(8,128)(2,1)S(1)}, bf16[6,48,128]{2,1,0:T(8,128)(2,1)S(1)}, u32[]{:S(2)}, u32[]{:S(2)}) collective-permute-start(bf16[6,48,128]{2,1,0:T(8,128)(2,1)S(1)} %constant_dynamic-update-slice_fusion.refs_0_), channel_id=1, source_target_pairs={{0,4},{1,5},{2,6},{3,7},{4,0},{5,1},{6,2},{7,3},{8,12},{9,13},{10,... | collective-permute-start | bytes 221192 | tf_op jit(solution)/shard_map/ppermute | solution.py:506
  10.1 0.2 fusion.wide_bias
  10.4 0.4 %copy-done.14 = s32[48]{0:T(128)S(1)} copy-done((s32[48]{0:T(128)S(1)}, s32[48]{0:T(128)}, u32[]{:S(2)}) %copy-start.14) | copy-done | bytes 216
  10.8 0.1 broadcast_in_dim.15.valid_column
  10.9 0.4 %shard_map.163 = (f32[1152,128]{1,0:T(8,128)S(1)}, f32[1152,128]{1,0:T(8,128)S(1)}, f32[1152,128]{1,0:T(8,128)S(1)}, f32[1152,128]{1,0:T(8,128)S(1)}, bf16[12,48...) custom-call(f32[48,128]{1,0:T(8,128)S(1)} %broadcast_in_dim.15.valid_column, f32[6,128]{1,0:T(8,128)S(1)} %stack.27.norms, ...), custom_call_target="tpu_custom_call" | custom-call | flops 1048576 | bytes 33554432 | tf_op jit(solution)/shard_map/pallas_call | solution.py:494
  11.3 1.0 %collective-permute-done.2.refs_0_ = bf16[6,48,128]{2,1,0:T(8,128)(2,1)S(1)} collective-permute-done((bf16[6,48,128]{2,1,0:T(8,128)(2,1)S(1)}, bf16[6,48,128]{2,1,0:T(8,128)(2,1)S(1)}, u32[]{:S(2)}, u32[]{:S(2)}) %collective-permute-start.2) | collective-permute-done | bytes 73760 | tf_op jit(solution)/shard_map/ppermute | solution.py:506
  12.4 0.4 %shard_map.164 = (f32[1152,128]{1,0:T(8,128)S(1)}, f32[1152,128]{1,0:T(8,128)S(1)}, f32[1152,128]{1,0:T(8,128)S(1)}, f32[1152,128]{1,0:T(8,128)S(1)}, bf16[12,48,128]{2,1,0:T(8,128)(2,1)S(1)}) custom-call(f32[48,128]{1,0:T(8,128)S(1)} %broadcast_in_dim.15.valid_column, ...), custom_call_target="tpu_custom_call", output_to_operand_aliasing={{0}: (4, {}), {1}: (5, {}), {2}: (6, {}), {3}: (7, {}), {4}... | custom-call | flops 1048576 | bytes 33554432 | tf_op jit(solution)/shard_map/pallas_call | solution.py:494
  12.8 0.6 %collective-permute-done.1.refs_0_ = bf16[6,48,128]{2,1,0:T(8,128)(2,1)S(1)} collective-permute-done((bf16[6,48,128]{2,1,0:T(8,128)(2,1)S(1)}, bf16[6,48,128]{2,1,0:T(8,128)(2,1)S(1)}, u32[]{:S(2)}, u32[]{:S(2)}) %collective-permute-start.1) | collective-permute-done | bytes 73760 | tf_op jit(solution)/shard_map/ppermute | solution.py:506
  13.4 0.5 %collective-permute-done.3.refs_1_ = bf16[6,48,128]{2,1,0:T(8,128)(2,1)S(1)} collective-permute-done((bf16[6,48,128]{2,1,0:T(8,128)(2,1)S(1)}, bf16[6,48,128]{2,1,0:T(8,128)(2,1)S(1)}, u32[]{:S(2)}, u32[]{:S(2)}) %collective-permute-start.3) | collective-permute-done | bytes 73760 | tf_op jit(solution)/shard_map/ppermute | solution.py:506
  14.0 0.6 %shard_map.165 = (f32[1152,128]{1,0:T(8,128)S(1)}, f32[1152,128]{1,0:T(8,128)S(1)}, f32[1152,128]{1,0:T(8,128)S(1)}, f32[1152,128]{1,0:T(8,128)S(1)}, bf16[12,48,128]{2,1,0:T(8,128)(2,1)S(1)}) custom-call(f32[48,128]{1,0:T(8,128)S(1)} %broadcast_in_dim.15.valid_column, ...), custom_call_target="tpu_custom_call", output_to_operand_aliasing={{0}: (5, {}), {1}: (6, {}), {2}: (7, {}), {3}: (8, {})} | custom-call | flops 1048576 | bytes 33554432 | tf_op jit(solution)/shard_map/pallas_call | solution.py:494
  14.7 0.1 collective-permute-done.4.refs_0_
  14.8 1.2 %shard_map.166 = (f32[1152,128]{1,0:T(8,128)S(1)}, f32[1152,128]{1,0:T(8,128)S(1)}) custom-call(f32[1152,128]{1,0:T(8,128)S(1)} %get-tuple-element.72.left_ref.refs_0_, f32[1152,128]{1,0:T(8,128)S(1)} %get-tuple-element.75.right_ref, bf16[12,48,128]{2,1,0:T(8,128)(2,1)S(1)} %collective-permute-done.4.refs_0_), custom_call_target="tpu_custom_call" | custom-call | flops 1048576 | bytes 33554432 | tf_op jit(solution)/shard_map/pallas_call | solution.py:494
  16.1 1.1 %shard_map.167 = (f32[1152,128]{1,0:T(8,128)S(1)}, f32[576,128]{1,0:T(8,128)S(1)}, bf16[576,128]{1,0:T(8,128)(2,1)S(1)}) custom-call(f32[6,128]{1,0:T(8,128)S(1)} %stack.27.norms, bf16[128,128]{1,0:T(8,128)(2,1)S(1)} %copy-done.1, f32[1152,128]{1,0:T(8,128)S(1)} %get-tuple-element.72.left_ref.refs_0_, ...), custom_call_target="tpu_custom_call", output_to_operand_aliasing={{0}: (7, {})} | custom-call | flops 1048576 | bytes 33554432 | tf_op jit(solution)/shard_map/pallas_call | solution.py:494
  17.2 0.4 %collective-permute-start.7 = (bf16[576,128]{1,0:T(8,128)(2,1)S(1)}, bf16[576,128]{1,0:T(8,128)(2,1)S(1)}, u32[]{:S(2)}, u32[]{:S(2)}) collective-permute-start(bf16[576,128]{1,0:T(8,128)(2,1)S(1)} %get-tuple-element.81.own_att_a), channel_id=1, source_target_pairs={{0,1},{1,0},{2,3},{3,2},{4,5},{5,4},{6,7},{7,6},{8,9},{9,8},{10,11... | collective-permute-start | bytes 442376 | tf_op jit(solution)/shard_map/ppermute | solution.py:506
  17.6 1.1 %shard_map.168.own_att_b = bf16[576,128]{1,0:T(8,128)(2,1)S(1)} custom-call(f32[6,128]{1,0:T(8,128)S(1)} %stack.27.norms, bf16[128,128]{1,0:T(8,128)(2,1)S(1)} %copy-done.1, f32[1152,128]{1,0:T(8,128)S(1)} %get-tuple-element.72.left_ref.refs_0_, f32[1152,128]{1,0:T(8,128)S(1)} %get-tuple-element.73.gate_ref.refs_1_, ...), custom_call_target="tpu_custom_call" | custom-call | flops 1048576 | bytes 33554432 | tf_op jit(solution)/shard_map/pallas_call | solution.py:494
  18.7 0.2 collective-permute-start.6
  19.0 1.3 %shard_map.169 = (f32[3,3,48,128]{3,2,1,0:T(8,128)S(1)}, f32[144,128]{1,0:T(8,128)S(1)}, f32[144,128]{1,0:T(8,128)S(1)}, f32[144,128]{1,0:T(8,128)S(1)}) custom-call(f32[48,128]{1,0:T(8,128)S(1)} %broadcast_in_dim.15.valid_column, bf16[256,256]{1,0:T(8,128)(2,1)S(1)} %get-tuple-element.50.same_head, bf16[128,128]{1,0:T(8,128)(2,1)S(1)} %copy-done.4, ...), custom_call_target="tpu_custom_call" | custom-call | flops 1048576 | bytes 33554432 | tf_op jit(solution)/shard_map/pallas_call | solution.py:494
  20.3 1.4 %shard_map.170 = bf16[3,48,128]{2,1,0:T(8,128)(2,1)} custom-call(f32[48,128]{1,0:T(8,128)S(1)} %broadcast_in_dim.15.valid_column, bf16[256,256]{1,0:T(8,128)(2,1)S(1)} %get-tuple-element.50.same_head, bf16[128,128]{1,0:T(8,128)(2,1)S(1)} %copy-done.2, bf16[128,128]{1,0:T(8,128)(2,1)S(1)} %copy-done.3, bf16[128,128]{1,0:T(8,128)(2,1)S(1)} %copy-done.6, ...), custom_call_target="tpu_custom_call" | custom-call | flops 1048576 | bytes 33554432 | tf_op jit(solution)/shard_map/pallas_call | solution.py:494
  (39 shorter events, 0.3 us)
Async XLA Ops:
  0.0 10.1 %copy-start = (bf16[128,4]{0,1:T(4,128)(2,1)S(1)}, bf16[128,4]{0,1:T(4,128)(2,1)}, u32[]{:S(2)}) copy-start(bf16[128,4]{0,1:T(4,128)(2,1)} %param.32) | copy-start | bytes 3076
  0.0 6.6 %collective-permute-start = (bf16[3,48,128]{2,1,0:T(8,128)(2,1)}, bf16[3,48,128]{2,1,0:T(8,128)(2,1)S(1)}, u32[]{:S(2)}, u32[]{:S(2)}) collective-permute-start(bf16[3,48,128]{2,1,0:T(8,128)(2,1)} %param.17), channel_id=1, source_target_pairs={{0,8},{1,9},{2,10},{3,11},{4,12},{5,13},{6,14},{7,15},{8,0},{9,1},... | collective-permute-start | bytes 110600 | tf_op jit(solution)/shard_map/ppermute | solution.py:506
  4.0 1.0 %copy-start.7 = (bf16[3,48,128]{2,1,0:T(8,128)(2,1)S(1)}, bf16[3,48,128]{2,1,0:T(8,128)(2,1)}, u32[]{:S(2)}) copy-start(bf16[3,48,128]{2,1,0:T(8,128)(2,1)} %param.17) | copy-start | bytes 110596
  5.0 0.7 %copy-start.11 = (f32[128]{0:T(128)S(1)}, f32[128]{0:T(128)}, u32[]{:S(2)}) copy-start(f32[128]{0:T(128)} %param.24) | copy-start | bytes 1540
  5.0 0.7 %copy-start.12 = (f32[128]{0:T(128)S(1)}, f32[128]{0:T(128)}, u32[]{:S(2)}) copy-start(f32[128]{0:T(128)} %param.26) | copy-start | bytes 1540
  5.1 0.7 %copy-start.13 = (f32[128]{0:T(128)S(1)}, f32[128]{0:T(128)}, u32[]{:S(2)}) copy-start(f32[128]{0:T(128)} %param.27) | copy-start | bytes 1540
  5.1 0.7 %copy-start.8 = (f32[128]{0:T(128)S(1)}, f32[128]{0:T(128)}, u32[]{:S(2)}) copy-start(f32[128]{0:T(128)} %param.19) | copy-start | bytes 1540
  5.1 0.7 %copy-start.9 = (f32[128]{0:T(128)S(1)}, f32[128]{0:T(128)}, u32[]{:S(2)}) copy-start(f32[128]{0:T(128)} %param.20) | copy-start | bytes 1540
  5.1 0.7 %copy-start.10 = (f32[128]{0:T(128)S(1)}, f32[128]{0:T(128)}, u32[]{:S(2)}) copy-start(f32[128]{0:T(128)} %param.23) | copy-start | bytes 1540
  6.6 5.8 %collective-permute-start.2 = (bf16[6,48,128]{2,1,0:T(8,128)(2,1)S(1)}, bf16[6,48,128]{2,1,0:T(8,128)(2,1)S(1)}, u32[]{:S(2)}, u32[]{:S(2)}) collective-permute-start(bf16[6,48,128]{2,1,0:T(8,128)(2,1)S(1)} %constant_dynamic-update-slice_fusion.refs_0_), channel_id=1, source_target_pairs={{0,6},{1,7},{2,4},{3,5},{4,2},{5,3},{6,0},{7,1},{8,14},{9,15},{10,... | collective-permute-start | bytes 221192 | tf_op jit(solution)/shard_map/ppermute | solution.py:506
  9.1 4.4 %collective-permute-start.1 = (bf16[6,48,128]{2,1,0:T(8,128)(2,1)S(1)}, bf16[6,48,128]{2,1,0:T(8,128)(2,1)S(1)}, u32[]{:S(2)}, u32[]{:S(2)}) collective-permute-start(bf16[6,48,128]{2,1,0:T(8,128)(2,1)S(1)} %constant_dynamic-update-slice_fusion.refs_0_), channel_id=1, source_target_pairs={{0,2},{1,3},{2,0},{3,1},{4,6},{5,7},{6,4},{7,5},{8,10},{9,11},{10,... | collective-permute-start | bytes 221192 | tf_op jit(solution)/shard_map/ppermute | solution.py:506
  9.6 4.4 %collective-permute-start.3 = (bf16[6,48,128]{2,1,0:T(8,128)(2,1)S(1)}, bf16[6,48,128]{2,1,0:T(8,128)(2,1)S(1)}, u32[]{:S(2)}, u32[]{:S(2)}) collective-permute-start(bf16[6,48,128]{2,1,0:T(8,128)(2,1)S(1)} %constant_dynamic-update-slice_fusion.refs_0_), channel_id=1, source_target_pairs={{0,4},{1,5},{2,6},{3,7},{4,0},{5,1},{6,2},{7,3},{8,12},{9,13},{10,... | collective-permute-start | bytes 221192 | tf_op jit(solution)/shard_map/ppermute | solution.py:506
  10.1 0.7 %copy-start.14 = (s32[48]{0:T(128)S(1)}, s32[48]{0:T(128)}, u32[]{:S(2)}) copy-start(s32[48]{0:T(128)} %param.18) | copy-start | bytes 580
  13.4 1.4 %collective-permute-start.4 = (bf16[12,48,128]{2,1,0:T(8,128)(2,1)S(1)}, bf16[12,48,128]{2,1,0:T(8,128)(2,1)S(1)}, u32[]{:S(2)}, u32[]{:S(2)}) collective-permute-start(bf16[12,48,128]{2,1,0:T(8,128)(2,1)S(1)} %get-tuple-element.76), channel_id=1, source_target_pairs={{0,1},{1,0},{2,3},{3,2},{4,5},{5,4},{6,7},{7,6},{8,9},{9,8},{10,11... | collective-permute-start | bytes 442376 | tf_op jit(solution)/shard_map/ppermute | solution.py:506
  14.6 1.4 %collective-permute-start.5 = (bf16[12,48,128]{2,1,0:T(8,128)(2,1)S(1)}, bf16[12,48,128]{2,1,0:T(8,128)(2,1)S(1)}, u32[]{:S(2)}, u32[]{:S(2)}) collective-permute-start(bf16[12,48,128]{2,1,0:T(8,128)(2,1)S(1)} %get-tuple-element.78), channel_id=1, source_target_pairs={{0,1},{1,0},{2,3},{3,2},{4,5},{5,4},{6,7},{7,6},{8,9},{9,8},{10,11... | collective-permute-start | bytes 442376 | tf_op jit(solution)/shard_map/ppermute | solution.py:506
  14.8 1.2 %copy-start.1 = (bf16[128,128]{1,0:T(8,128)(2,1)S(1)}, bf16[128,128]{1,0:T(8,128)(2,1)}, u32[]{:S(2)}) copy-start(bf16[128,128]{1,0:T(8,128)(2,1)} %w_out.4) | copy-start | bytes 98308
  17.2 1.8 %collective-permute-start.7 = (bf16[576,128]{1,0:T(8,128)(2,1)S(1)}, bf16[576,128]{1,0:T(8,128)(2,1)S(1)}, u32[]{:S(2)}, u32[]{:S(2)}) collective-permute-start(bf16[576,128]{1,0:T(8,128)(2,1)S(1)} %get-tuple-element.81.own_att_a), channel_id=1, source_target_pairs={{0,1},{1,0},{2,3},{3,2},{4,5},{5,4},{6,7},{7,6},{8,9},{9,8},{10,11... | collective-permute-start | bytes 442376 | tf_op jit(solution)/shard_map/ppermute | solution.py:506
  17.6 1.3 %copy-start.2 = (bf16[128,128]{1,0:T(8,128)(2,1)S(1)}, bf16[128,128]{1,0:T(8,128)(2,1)}, u32[]{:S(2)}) copy-start(bf16[128,128]{1,0:T(8,128)(2,1)} %w_key.3) | copy-start | bytes 98308
  17.6 1.3 %copy-start.3 = (bf16[128,128]{1,0:T(8,128)(2,1)S(1)}, bf16[128,128]{1,0:T(8,128)(2,1)}, u32[]{:S(2)}) copy-start(bf16[128,128]{1,0:T(8,128)(2,1)} %w_value.3) | copy-start | bytes 98308
  17.6 1.3 %copy-start.4 = (bf16[128,128]{1,0:T(8,128)(2,1)S(1)}, bf16[128,128]{1,0:T(8,128)(2,1)}, u32[]{:S(2)}) copy-start(bf16[128,128]{1,0:T(8,128)(2,1)} %w_query.1) | copy-start | bytes 98308
  17.6 1.3 %copy-start.5 = (bf16[128,128]{1,0:T(8,128)(2,1)S(1)}, bf16[128,128]{1,0:T(8,128)(2,1)}, u32[]{:S(2)}) copy-start(bf16[128,128]{1,0:T(8,128)(2,1)} %w_gate.1) | copy-start | bytes 98308
  18.7 1.6 %collective-permute-start.6 = (bf16[576,128]{1,0:T(8,128)(2,1)S(1)}, bf16[576,128]{1,0:T(8,128)(2,1)S(1)}, u32[]{:S(2)}, u32[]{:S(2)}) collective-permute-start(bf16[576,128]{1,0:T(8,128)(2,1)S(1)} %shard_map.168.own_att_b), channel_id=1, source_target_pairs={{0,1},{1,0},{2,3},{3,2},{4,5},{5,4},{6,7},{7,6},{8,9},{9,8},{10,11... | collective-permute-start | bytes 442376 | tf_op jit(solution)/shard_map/ppermute | solution.py:506
  18.9 1.3 %copy-start.6 = (bf16[128,128]{1,0:T(8,128)(2,1)S(1)}, bf16[128,128]{1,0:T(8,128)(2,1)}, u32[]{:S(2)}) copy-start(bf16[128,128]{1,0:T(8,128)(2,1)} %w_out.5) | copy-start | bytes 98308

commit v11 on v10

--- a/solution.py
+++ b/solution.py
@@ -142,7 +142,7 @@
 def edges_kernel(
     row_count, chips, pieces, send_row, makes_heads, valid_column, norms, weights, *refs
 ):
-    pair_refs = refs[: len(pieces)]
+    pairs_ref_in = refs[0]
     left_ref, right_ref, gate_ref, pairs_ref, send_ref = refs[-5:]
     if makes_heads:
         left_ref, right_ref, gate_ref, pairs_ref, send_ref, same_head_ref = refs[-6:]
@@ -153,9 +153,13 @@
     f32, bf16 = jnp.float32, jnp.bfloat16
     res, channels = valid_column.shape
     _, core = chip_and_core()
-    pairs = jnp.concatenate(
-        [ref[...].astype(f32).reshape(-1, channels) for ref in pair_refs], axis=0
-    )
+    own_place = jnp.bitwise_and(lax.shift_right_logical(lax.axis_index("row"), 1), 3)
+    pairs = []
+    for piece in pieces:
+        rows = len(piece) * row_count
+        place = 0 if makes_heads else jnp.bitwise_xor(own_place, piece[0])
+        pairs.append(pairs_ref_in[pl.ds(place * rows, rows)].astype(f32).reshape(-1, channels))
+    pairs = jnp.concatenate(pairs, axis=0)
     normed = layer_norm(pairs, norms[0:1, :], norms[1:2, :], 1).astype(bf16)
     column = valid_column[...]
     rows_of = rows_of_blocks(row_count, [bits for piece in pieces for bits in piece])
@@ -535,35 +539,37 @@
 
     tall = shaped(f32, half * res, channels)
 
-    def edges_of(pieces, send_row, *held):
-        pairs = tuple(p for p, _ in pieces)
-        blocks = tuple(b for _, b in pieces)
-        operands = (valid_column, norms, edge_weights) + pairs + held
+    def edges_of(pairs, blocks, send_row, *held):
+        operands = (valid_column, norms, edge_weights, pairs) + held
         first = len(operands) - len(held)
+        sent = sum(len(b) for b in blocks) * row_count
         return call(
             functools.partial(edges_kernel, row_count, chips, blocks, send_row, not held),
-            (tall, tall, tall, tall, shaped(bf16, 4 * row_count, res, channels))
+            (tall, tall, tall, tall, shaped(bf16, sent, res, channels))
             + (() if held else (shaped(bf16, 2 * channels, 2 * channels),)),
             operands,
             {first + e: e for e in range(len(held))},
         )
 
-    diagonal = exchange(own, 6)
-    beside = exchange(own, 2)
-    near = exchange(own, 4)
-    *edges, early_right, same_head = edges_of([(own, own_blocks)], 0)
-    diagonal, edges = lax.optimization_barrier((diagonal, edges))
-    *edges, early_right = edges_of(
-        [(diagonal, blocks_from(3))], 2 * row_count, *edges, early_right
-    )
-    beside, edges, early_right, wide_bias = lax.optimization_barrier(
-        (beside, edges, early_right, wide_bias)
-    )
-    early = (exchange(early_right, 1), own_blocks + blocks_from(3))
-    *edges, late_right = edges_of(
-        [(beside, blocks_from(1)), (near, blocks_from(2))], 0, *edges
-    )
-    late = (exchange(late_right, 1), blocks_from(1) + blocks_from(2))
+    groups = [
+        [far_bit + 2 * place + core for place in range(4)]
+        for far_bit in range(0, devices, 8)
+        for core in range(2)
+    ]
+    gathered = lax.all_to_all(
+        jnp.concatenate([own] * 4, axis=0),
+        "row",
+        split_axis=0,
+        concat_axis=0,
+        axis_index_groups=groups,
+        tiled=True,
+    )
+    *edges, early_right, same_head = edges_of(own, (own_blocks,), 0)
+    edges, wide_bias = lax.optimization_barrier((edges, wide_bias))
+    early = (exchange(early_right, 1), own_blocks)
+    new_blocks = tuple(blocks_from(bits) for bits in (1, 2, 3))
+    *edges, late_right = edges_of(gathered, new_blocks, 0, *edges)
+    late = (exchange(late_right, 1), sum(new_blocks, ()))
 
     left, right, gate, pairs = edges
     triangle, across = call(

time: 21.9 us -> 26.1 us (1.19)
  waiting for transfers between devices: 3.15 us -> 6.56 us
  other arithmetic: 0.96 us -> 1.69 us
  starting transfers between devices: 8.3 us -> 9.02 us
  local copies, waits for them, and re-layouts: 1.28 us -> 0.84 us
    all_to_all x0 -> x1, waiting for transfers between devices: none -> 4.69 us  [on_whole_complex(): lax.all_to_all(jnp.concatenate([own] * 4, axis=0), 'row', split_axis=0, c...]
    all_to_all x0 -> x1, starting transfers between devices: none -> 3.71 us  [on_whole_complex(): lax.all_to_all(jnp.concatenate([own] * 4, axis=0), 'row', split_axis=0, c...]
    ppermute x8 -> x5, starting transfers between devices: 8.3 us -> 5.31 us  [exchange(): return lax.ppermute(values, 'row', [(d, d ^ bit) for d in range(devices)])]
    ppermute x8 -> x5, waiting for transfers between devices: 3.15 us -> 1.87 us  [exchange(): return lax.ppermute(values, 'row', [(d, d ^ bit) for d in range(devices)])]
    concatenate x0 -> x1, other arithmetic: none -> 0.74 us  [on_whole_complex(): jnp.concatenate([own] * 4, axis=0)]
    unnamed x30, local copies, waits for them, and re-layouts: 1.16 us -> 0.72 us
    pallas_call x8 -> x7, Pallas kernels: 7.61 us -> 7.37 us  [call(): pl.pallas_call(kernel, out_shape=outs, in_specs=[in_vmem] * len(operands)...]
  transfers between devices with their start and end apart: 8 -> 6, of which waited for: 5 -> 3; matrix products, arithmetic and copies ran while one was open for 6% -> 5% of each run, Pallas kernels for 23% -> 16%
where the time goes in v11:
time: 26.1 us; the launch traced here: 25.9 us
  starting transfers between devices  9.02 us (35%)
  Pallas kernels  7.37 us (28%)
  waiting for transfers between devices  6.56 us (25%)
  other arithmetic  1.69 us (6%)
  local copies, waits for them, and re-layouts  0.84 us (3%)
    pallas_call x7, Pallas kernels, call(): pl.pallas_call(kernel, out_shape=outs, in_specs=[in_vmem] * len(operands)...  7.37 us
    ppermute x5, starting transfers between devices, exchange(): return lax.ppermute(values, 'row', [(d, d ^ bit) for d in range(devices)])  5.31 us
    all_to_all x1, waiting for transfers between devices, on_whole_complex(): lax.all_to_all(jnp.concatenate([own] * 4, axis=0), 'row', split_axis=0, c...  4.69 us
    all_to_all x1, starting transfers between devices, on_whole_complex(): lax.all_to_all(jnp.concatenate([own] * 4, axis=0), 'row', split_axis=0, c...  3.71 us
    ppermute x5, waiting for transfers between devices, exchange(): return lax.ppermute(values, 'row', [(d, d ^ bit) for d in range(devices)])  1.87 us
    concatenate x1, other arithmetic, on_whole_complex(): edge_weights = jnp.concatenate([w_edges, w_tri_gate], axis=1)  0.94 us
    concatenate x1, other arithmetic, on_whole_complex(): jnp.concatenate([own] * 4, axis=0)  0.74 us
    unnamed x30, local copies, waits for them, and re-layouts  0.72 us
  transfers between devices with their start and end apart: 6, of which 3 were waited for; matrix products, arithmetic and copies ran while one was open for 5% of the time, Pallas kernels for 16%

profile of v11, /device:TPU:0, one launch (start us, length us, event | category | flops | bytes accessed | tf_op | source)
XLA Modules:
  0.0 25.9 jit_solution(13451183276927394012)
XLA Ops:
  0.0 4.1 %collective-permute-start = (bf16[3,48,128]{2,1,0:T(8,128)(2,1)}, bf16[3,48,128]{2,1,0:T(8,128)(2,1)S(1)}, u32[]{:S(2)}, u32[]{:S(2)}) collective-permute-start(bf16[3,48,128]{2,1,0:T(8,128)(2,1)} %param.17), channel_id=1, source_target_pairs={{0,8},{1,9},{2,10},{3,11},{4,12},{5,13},{6,14},{7,15},{8,0},{9,1},... | collective-permute-start | bytes 110600 | tf_op jit(solution)/shard_map/ppermute | solution.py:510
  4.1 0.9 %pad_maximum_fusion.1.weights = bf16[128,640]{1,0:T(8,128)(2,1)S(1)} fusion(bf16[128,128]{1,0:T(8,128)(2,1)} %param.22, bf16[128,512]{1,0:T(8,128)(2,1)} %param.21), kind=kLoop, calls=%fused_computation.3 | loop fusion | flops 327680 | bytes 327680 | tf_op jit(solution)/shard_map/concatenate | solution.py:521
  5.2 0.6 %copy-done.11 = f32[128]{0:T(128)S(1)} copy-done((f32[128]{0:T(128)S(1)}, f32[128]{0:T(128)}, u32[]{:S(2)}) %copy-start.11) | copy-done | bytes 536
  5.8 0.0 copy-done.12
  5.8 0.0 copy-done.13
  5.8 0.0 copy-done.8
  5.9 0.8 %collective-permute-done = bf16[3,48,128]{2,1,0:T(8,128)(2,1)S(1)} collective-permute-done((bf16[3,48,128]{2,1,0:T(8,128)(2,1)}, bf16[3,48,128]{2,1,0:T(8,128)(2,1)S(1)}, u32[]{:S(2)}, u32[]{:S(2)}) %collective-permute-start) | collective-permute-done | bytes 36896 | tf_op jit(solution)/shard_map/ppermute | solution.py:510
  6.7 0.7 %pad_maximum_fusion = bf16[24,48,128]{2,1,0:T(8,128)(2,1)} fusion(bf16[6,48,128]{2,1,0:T(8,128)(2,1)S(1)} %constant_dynamic-update-slice_fusion.refs_0_), kind=kLoop, calls=%fused_computation.2 | loop fusion | flops 442368 | bytes 368640 | tf_op jit(solution)/shard_map/concatenate | solution.py:560
  7.4 3.7 %all-to-all-start = ((bf16[24,48,128]{2,1,0:T(8,128)(2,1)}), bf16[24,48,128]{2,1,0:T(8,128)(2,1)S(1)}, u32[]{:S(2)}, u32[]{:S(2)}) async-start(bf16[24,48,128]{2,1,0:T(8,128)(2,1)} %pad_maximum_fusion), calls=%async_computation | async-start | bytes 589824 | tf_op jit(solution)/shard_map/all_to_all | solution.py:559
  11.1 0.2 fusion.wide_bias
  11.4 0.1 broadcast_in_dim.15.valid_column
  11.4 0.5 %shard_map.163 = (f32[1152,128]{1,0:T(8,128)S(1)}, f32[1152,128]{1,0:T(8,128)S(1)}, f32[1152,128]{1,0:T(8,128)S(1)}, f32[1152,128]{1,0:T(8,128)S(1)}, bf16[6,48,...) custom-call(f32[48,128]{1,0:T(8,128)S(1)} %broadcast_in_dim.15.valid_column, f32[6,128]{1,0:T(8,128)S(1)} %stack.27.norms, ...), custom_call_target="tpu_custom_call" | custom-call | flops 1048576 | bytes 33554432 | tf_op jit(solution)/shard_map/pallas_call | solution.py:498
  11.9 4.7 %all-to-all-done.refs_0_ = bf16[24,48,128]{2,1,0:T(8,128)(2,1)S(1)} async-done(((bf16[24,48,128]{2,1,0:T(8,128)(2,1)}), bf16[24,48,128]{2,1,0:T(8,128)(2,1)S(1)}, u32[]{:S(2)}, u32[]{:S(2)}) %all-to-all-start) | async-done | bytes 294944 | tf_op jit(solution)/shard_map/all_to_all | solution.py:559
  16.6 0.8 %shard_map.164 = (f32[1152,128]{1,0:T(8,128)S(1)}, f32[1152,128]{1,0:T(8,128)S(1)}, f32[1152,128]{1,0:T(8,128)S(1)}, f32[1152,128]{1,0:T(8,128)S(1)}, bf16[18,48,128]{2,1,0:T(8,128)(2,1)S(1)}) custom-call(f32[48,128]{1,0:T(8,128)S(1)} %broadcast_in_dim.15.valid_column, ...), custom_call_target="tpu_custom_call", output_to_operand_aliasing={{0}: (4, {}), {1}: (5, {}), {2}: (6, {}), {3}: (7, {})} | custom-call | flops 1048576 | bytes 33554432 | tf_op jit(solution)/shard_map/pallas_call | solution.py:498
  17.4 0.1 collective-permute-start.2
  17.5 0.5 %collective-permute-start.1 = (bf16[6,48,128]{2,1,0:T(8,128)(2,1)S(1)}, bf16[6,48,128]{2,1,0:T(8,128)(2,1)S(1)}, u32[]{:S(2)}, u32[]{:S(2)}) collective-permute-start(bf16[6,48,128]{2,1,0:T(8,128)(2,1)S(1)} %get-tuple-element.52), channel_id=1, source_target_pairs={{0,1},{1,0},{2,3},{3,2},{4,5},{5,4},{6,7},{7,6},{8,9},{9,8},{10,11... | collective-permute-start | bytes 221192 | tf_op jit(solution)/shard_map/ppermute | solution.py:510
  18.0 1.1 %collective-permute-done.1.refs_0_ = bf16[6,48,128]{2,1,0:T(8,128)(2,1)S(1)} collective-permute-done((bf16[6,48,128]{2,1,0:T(8,128)(2,1)S(1)}, bf16[6,48,128]{2,1,0:T(8,128)(2,1)S(1)}, u32[]{:S(2)}, u32[]{:S(2)}) %collective-permute-start.1) | collective-permute-done | bytes 73760 | tf_op jit(solution)/shard_map/ppermute | solution.py:510
  19.0 1.2 %shard_map.165 = (f32[1152,128]{1,0:T(8,128)S(1)}, f32[1152,128]{1,0:T(8,128)S(1)}) custom-call(f32[1152,128]{1,0:T(8,128)S(1)} %get-tuple-element.48.left_ref.refs_0_, f32[1152,128]{1,0:T(8,128)S(1)} %get-tuple-element.51.right_ref, bf16[6,48,128]{2,1,0:T(8,128)(2,1)S(1)} %collective-permute-done.1.refs_0_), custom_call_target="tpu_custom_call" | custom-call | flops 1048576 | bytes 33554432 | tf_op jit(solution)/shard_map/pallas_call | solution.py:498
  20.2 1.1 %shard_map.166 = (f32[1152,128]{1,0:T(8,128)S(1)}, f32[576,128]{1,0:T(8,128)S(1)}, bf16[576,128]{1,0:T(8,128)(2,1)S(1)}) custom-call(f32[6,128]{1,0:T(8,128)S(1)} %stack.27.norms, bf16[128,128]{1,0:T(8,128)(2,1)S(1)} %copy-done.1, f32[1152,128]{1,0:T(8,128)S(1)} %get-tuple-element.48.left_ref.refs_0_, ...), custom_call_target="tpu_custom_call", output_to_operand_aliasing={{0}: (7, {})} | custom-call | flops 1048576 | bytes 33554432 | tf_op jit(solution)/shard_map/pallas_call | solution.py:498
  21.4 0.3 %collective-permute-start.4 = (bf16[576,128]{1,0:T(8,128)(2,1)S(1)}, bf16[576,128]{1,0:T(8,128)(2,1)S(1)}, u32[]{:S(2)}, u32[]{:S(2)}) collective-permute-start(bf16[576,128]{1,0:T(8,128)(2,1)S(1)} %get-tuple-element.57.own_att_a), channel_id=1, source_target_pairs={{0,1},{1,0},{2,3},{3,2},{4,5},{5,4},{6,7},{7,6},{8,9},{9,8},{10,11... | collective-permute-start | bytes 442376 | tf_op jit(solution)/shard_map/ppermute | solution.py:510
  21.6 1.1 %shard_map.167.own_att_b = bf16[576,128]{1,0:T(8,128)(2,1)S(1)} custom-call(f32[6,128]{1,0:T(8,128)S(1)} %stack.27.norms, bf16[128,128]{1,0:T(8,128)(2,1)S(1)} %copy-done.1, f32[1152,128]{1,0:T(8,128)S(1)} %get-tuple-element.48.left_ref.refs_0_, f32[1152,128]{1,0:T(8,128)S(1)} %get-tuple-element.49.gate_ref.refs_1_, ...), custom_call_target="tpu_custom_call" | custom-call | flops 1048576 | bytes 33554432 | tf_op jit(solution)/shard_map/pallas_call | solution.py:498
  22.8 0.4 %collective-permute-start.3 = (bf16[576,128]{1,0:T(8,128)(2,1)S(1)}, bf16[576,128]{1,0:T(8,128)(2,1)S(1)}, u32[]{:S(2)}, u32[]{:S(2)}) collective-permute-start(bf16[576,128]{1,0:T(8,128)(2,1)S(1)} %shard_map.167.own_att_b), channel_id=1, source_target_pairs={{0,1},{1,0},{2,3},{3,2},{4,5},{5,4},{6,7},{7,6},{8,9},{9,8},{10,11... | collective-permute-start | bytes 442376 | tf_op jit(solution)/shard_map/ppermute | solution.py:510
  23.2 1.3 %shard_map.168 = (f32[3,3,48,128]{3,2,1,0:T(8,128)S(1)}, f32[144,128]{1,0:T(8,128)S(1)}, f32[144,128]{1,0:T(8,128)S(1)}, f32[144,128]{1,0:T(8,128)S(1)}) custom-call(f32[48,128]{1,0:T(8,128)S(1)} %broadcast_in_dim.15.valid_column, bf16[256,256]{1,0:T(8,128)(2,1)S(1)} %get-tuple-element.38.same_head, bf16[128,128]{1,0:T(8,128)(2,1)S(1)} %copy-done.4, ...), custom_call_target="tpu_custom_call" | custom-call | flops 1048576 | bytes 33554432 | tf_op jit(solution)/shard_map/pallas_call | solution.py:498
  24.5 1.4 %shard_map.169 = bf16[3,48,128]{2,1,0:T(8,128)(2,1)} custom-call(f32[48,128]{1,0:T(8,128)S(1)} %broadcast_in_dim.15.valid_column, bf16[256,256]{1,0:T(8,128)(2,1)S(1)} %get-tuple-element.38.same_head, bf16[128,128]{1,0:T(8,128)(2,1)S(1)} %copy-done.2, bf16[128,128]{1,0:T(8,128)(2,1)S(1)} %copy-done.3, bf16[128,128]{1,0:T(8,128)(2,1)S(1)} %copy-done.6, ...), custom_call_target="tpu_custom_call" | custom-call | flops 1048576 | bytes 33554432 | tf_op jit(solution)/shard_map/pallas_call | solution.py:498
  (35 shorter events, 0.2 us)
Async XLA Ops:
  0.0 11.1 %copy-start = (bf16[128,4]{0,1:T(4,128)(2,1)S(1)}, bf16[128,4]{0,1:T(4,128)(2,1)}, u32[]{:S(2)}) copy-start(bf16[128,4]{0,1:T(4,128)(2,1)} %param.32) | copy-start | bytes 3076
  0.0 5.1 %copy-start.7 = (bf16[3,48,128]{2,1,0:T(8,128)(2,1)S(1)}, bf16[3,48,128]{2,1,0:T(8,128)(2,1)}, u32[]{:S(2)}) copy-start(bf16[3,48,128]{2,1,0:T(8,128)(2,1)} %param.17) | copy-start | bytes 110596
  0.0 5.1 %copy-start.14 = (s32[48]{0:T(128)S(1)}, s32[48]{0:T(128)}, u32[]{:S(2)}) copy-start(s32[48]{0:T(128)} %param.18) | copy-start | bytes 580
  0.0 6.6 %collective-permute-start = (bf16[3,48,128]{2,1,0:T(8,128)(2,1)}, bf16[3,48,128]{2,1,0:T(8,128)(2,1)S(1)}, u32[]{:S(2)}, u32[]{:S(2)}) collective-permute-start(bf16[3,48,128]{2,1,0:T(8,128)(2,1)} %param.17), channel_id=1, source_target_pairs={{0,8},{1,9},{2,10},{3,11},{4,12},{5,13},{6,14},{7,15},{8,0},{9,1},... | collective-permute-start | bytes 110600 | tf_op jit(solution)/shard_map/ppermute | solution.py:510
  5.1 0.7 %copy-start.11 = (f32[128]{0:T(128)S(1)}, f32[128]{0:T(128)}, u32[]{:S(2)}) copy-start(f32[128]{0:T(128)} %param.24) | copy-start | bytes 1540
  5.1 0.7 %copy-start.12 = (f32[128]{0:T(128)S(1)}, f32[128]{0:T(128)}, u32[]{:S(2)}) copy-start(f32[128]{0:T(128)} %param.26) | copy-start | bytes 1540
  5.1 0.7 %copy-start.13 = (f32[128]{0:T(128)S(1)}, f32[128]{0:T(128)}, u32[]{:S(2)}) copy-start(f32[128]{0:T(128)} %param.27) | copy-start | bytes 1540
  5.1 0.7 %copy-start.8 = (f32[128]{0:T(128)S(1)}, f32[128]{0:T(128)}, u32[]{:S(2)}) copy-start(f32[128]{0:T(128)} %param.19) | copy-start | bytes 1540
  5.2 0.7 %copy-start.9 = (f32[128]{0:T(128)S(1)}, f32[128]{0:T(128)}, u32[]{:S(2)}) copy-start(f32[128]{0:T(128)} %param.20) | copy-start | bytes 1540
  5.2 0.7 %copy-start.10 = (f32[128]{0:T(128)S(1)}, f32[128]{0:T(128)}, u32[]{:S(2)}) copy-start(f32[128]{0:T(128)} %param.23) | copy-start | bytes 1540
  7.4 9.2 %all-to-all-start = ((bf16[24,48,128]{2,1,0:T(8,128)(2,1)}), bf16[24,48,128]{2,1,0:T(8,128)(2,1)S(1)}, u32[]{:S(2)}, u32[]{:S(2)}) async-start(bf16[24,48,128]{2,1,0:T(8,128)(2,1)} %pad_maximum_fusion), calls=%async_computation | async-start | bytes 589824 | tf_op jit(solution)/shard_map/all_to_all | solution.py:559
  17.4 2.8 %collective-permute-start.2 = (bf16[18,48,128]{2,1,0:T(8,128)(2,1)S(1)}, bf16[18,48,128]{2,1,0:T(8,128)(2,1)S(1)}, u32[]{:S(2)}, u32[]{:S(2)}) collective-permute-start(bf16[18,48,128]{2,1,0:T(8,128)(2,1)S(1)} %get-tuple-element.54), channel_id=1, source_target_pairs={{0,1},{1,0},{2,3},{3,2},{4,5},{5,4},{6,7},{7,6},{8,9},{9,8},{10,11... | collective-permute-start | bytes 663560 | tf_op jit(solution)/shard_map/ppermute | solution.py:510
  17.5 1.6 %collective-permute-start.1 = (bf16[6,48,128]{2,1,0:T(8,128)(2,1)S(1)}, bf16[6,48,128]{2,1,0:T(8,128)(2,1)S(1)}, u32[]{:S(2)}, u32[]{:S(2)}) collective-permute-start(bf16[6,48,128]{2,1,0:T(8,128)(2,1)S(1)} %get-tuple-element.52), channel_id=1, source_target_pairs={{0,1},{1,0},{2,3},{3,2},{4,5},{5,4},{6,7},{7,6},{8,9},{9,8},{10,11... | collective-permute-start | bytes 221192 | tf_op jit(solution)/shard_map/ppermute | solution.py:510
  19.0 1.2 %copy-start.1 = (bf16[128,128]{1,0:T(8,128)(2,1)S(1)}, bf16[128,128]{1,0:T(8,128)(2,1)}, u32[]{:S(2)}) copy-start(bf16[128,128]{1,0:T(8,128)(2,1)} %w_out.4) | copy-start | bytes 98308
  21.4 1.8 %collective-permute-start.4 = (bf16[576,128]{1,0:T(8,128)(2,1)S(1)}, bf16[576,128]{1,0:T(8,128)(2,1)S(1)}, u32[]{:S(2)}, u32[]{:S(2)}) collective-permute-start(bf16[576,128]{1,0:T(8,128)(2,1)S(1)} %get-tuple-element.57.own_att_a), channel_id=1, source_target_pairs={{0,1},{1,0},{2,3},{3,2},{4,5},{5,4},{6,7},{7,6},{8,9},{9,8},{10,11... | collective-permute-start | bytes 442376 | tf_op jit(solution)/shard_map/ppermute | solution.py:510
  21.6 1.5 %copy-start.2 = (bf16[128,128]{1,0:T(8,128)(2,1)S(1)}, bf16[128,128]{1,0:T(8,128)(2,1)}, u32[]{:S(2)}) copy-start(bf16[128,128]{1,0:T(8,128)(2,1)} %w_key.3) | copy-start | bytes 98308
  21.6 1.5 %copy-start.3 = (bf16[128,128]{1,0:T(8,128)(2,1)S(1)}, bf16[128,128]{1,0:T(8,128)(2,1)}, u32[]{:S(2)}) copy-start(bf16[128,128]{1,0:T(8,128)(2,1)} %w_value.3) | copy-start | bytes 98308
  21.6 1.5 %copy-start.4 = (bf16[128,128]{1,0:T(8,128)(2,1)S(1)}, bf16[128,128]{1,0:T(8,128)(2,1)}, u32[]{:S(2)}) copy-start(bf16[128,128]{1,0:T(8,128)(2,1)} %w_query.1) | copy-start | bytes 98308
  21.6 1.5 %copy-start.5 = (bf16[128,128]{1,0:T(8,128)(2,1)S(1)}, bf16[128,128]{1,0:T(8,128)(2,1)}, u32[]{:S(2)}) copy-start(bf16[128,128]{1,0:T(8,128)(2,1)} %w_gate.1) | copy-start | bytes 98308
  22.8 1.7 %collective-permute-start.3 = (bf16[576,128]{1,0:T(8,128)(2,1)S(1)}, bf16[576,128]{1,0:T(8,128)(2,1)S(1)}, u32[]{:S(2)}, u32[]{:S(2)}) collective-permute-start(bf16[576,128]{1,0:T(8,128)(2,1)S(1)} %shard_map.167.own_att_b), channel_id=1, source_target_pairs={{0,1},{1,0},{2,3},{3,2},{4,5},{5,4},{6,7},{7,6},{8,9},{9,8},{10,11... | collective-permute-start | bytes 442376 | tf_op jit(solution)/shard_map/ppermute | solution.py:510
  23.2 1.3 %copy-start.6 = (bf16[128,128]{1,0:T(8,128)(2,1)S(1)}, bf16[128,128]{1,0:T(8,128)(2,1)}, u32[]{:S(2)}) copy-start(bf16[128,128]{1,0:T(8,128)(2,1)} %w_out.5) | copy-start | bytes 98308

commit v12 on v10

--- a/solution.py
+++ b/solution.py
@@ -121,6 +121,13 @@
     return 0.5 * jnp.tanh(0.5 * values) + 0.5
 
 
+def row_norm(values, norm_gain, norm_bias):
+    count = values.shape[1]
+    centre = values - jnp.sum(values, axis=1, keepdims=True) * (1.0 / count)
+    squares = jnp.sum(centre * centre, axis=1, keepdims=True)
+    return centre * lax.rsqrt(squares + 1e-05 * count) * (norm_gain * count**0.5) + norm_bias
+
+
 def dot(left, right):
     return jnp.dot(left, right, preferred_element_type=jnp.float32)
 
@@ -156,8 +163,8 @@
     pairs = jnp.concatenate(
         [ref[...].astype(f32).reshape(-1, channels) for ref in pair_refs], axis=0
     )
-    normed = layer_norm(pairs, norms[0:1, :], norms[1:2, :], 1).astype(bf16)
-    column = valid_column[...]
+    normed = row_norm(pairs, norms[0:1, :], norms[1:2, :]).astype(bf16)
+    column = 0.5 * valid_column[...]
     rows_of = rows_of_blocks(row_count, [bits for piece in pieces for bits in piece])
     masks = jnp.concatenate(
         [
@@ -167,10 +174,10 @@
         axis=0,
     )
     joined = dot(normed, weights[:, : 2 * channels])
-    left = rounded(sigmoid(joined[:, channels:]) * joined[:, :channels] * masks)
+    left = rounded((jnp.tanh(joined[:, channels:]) + 1.0) * joined[:, :channels] * masks)
     joined = dot(normed, weights[:, 2 * channels : 4 * channels])
-    right = (sigmoid(joined[:, channels:]) * joined[:, :channels] * masks).astype(bf16)
-    gate = sigmoid(dot(normed, weights[:, 4 * channels :]))
+    right = ((jnp.tanh(joined[:, channels:]) + 1.0) * joined[:, :channels] * masks).astype(bf16)
+    gate = 0.5 * jnp.tanh(dot(normed, weights[:, 4 * channels :])) + 0.5
     for n, (chip, r) in enumerate(rows_of):
         rows = slice(n * res, (n + 1) * res)
         start = pl.multiple_of((chip * row_count + r) * res, res)
@@ -253,9 +260,9 @@
     triangle_rows(
         row_count, chips, left_ref, across_ref, triangle_ref, first, half // 2, 1 - core, 0
     )
-    tri_normed = layer_norm(triangle_ref[...], norms[2:3, :], norms[3:4, :], 1).astype(bf16)
+    tri_normed = row_norm(triangle_ref[...], norms[2:3, :], norms[3:4, :]).astype(bf16)
     after_tri = pairs_ref[rows, :] + gate_ref[rows, :] * dot(tri_normed, w_out[...])
-    att_in = layer_norm(after_tri, norms[4:5, :], norms[5:6, :], 1).astype(bf16)
+    att_in = row_norm(after_tri, norms[4:5, :], norms[5:6, :]).astype(bf16)
     return after_tri, att_in
 
 
@@ -303,8 +310,8 @@
     for values in att:
         rows = slice(start, start + values.shape[0])
         joined = dot(values, key_value)
-        key_ref[rows, :] = rounded(joined[:, :channels])
-        value_ref[rows, :] = rounded(joined[:, channels:])
+        key_ref[rows, :] = joined[:, :channels]
+        value_ref[rows, :] = joined[:, channels:]
         start = rows.stop
 
 
@@ -315,9 +322,15 @@
         start += values.shape[0]
     keys = start // res
     own = lax.axis_index("row") * row_count
+    height = -(-keys // 8) * 8
+    columns = []
     for r in range(row_count):
-        column = att_ref[pl.ds(own + r, keys, stride=res), :].astype(jnp.bfloat16)
-        bias_ref[r, :keys, :] = rounded(dot(column, wide_bias[...]))
+        column = att_ref[pl.ds(own + r, keys, stride=res), :]
+        columns.append(jnp.concatenate([column, jnp.zeros((height - keys, column.shape[1]), jnp.float32)]))
+    columns = jnp.concatenate(columns, axis=0).astype(jnp.bfloat16)
+    bias = rounded(dot(columns, wide_bias[...]))
+    for r in range(row_count):
+        bias_ref[r, :height, :] = bias[r * height : (r + 1) * height]
 
 
 def partial_attention(row_count, chips, query, parts, bias_ref, same_head, valid_column, score_ref):
@@ -514,7 +527,9 @@
         att_norm_bias,
     )
     norms = jnp.stack(vectors)
-    edge_weights = jnp.concatenate([w_edges, w_tri_gate], axis=1)
+    is_gate = lax.broadcasted_iota(jnp.int32, (1, 5 * channels), 1) // channels
+    halves = jnp.where((is_gate == 0) | (is_gate == 2), 1.0, 0.5).astype(bf16)
+    edge_weights = jnp.concatenate([w_edges, w_tri_gate], axis=1) * halves
     valid_column = jnp.broadcast_to(residue_valid.astype(f32)[:, None], (res, channels))
 
     head = lax.broadcasted_iota(jnp.int32, (HEADS, channels), 0)

time: 21.9 us -> 21.8 us (level)
    mul x0 -> x1, other arithmetic: none -> 0.97 us  [on_whole_complex(): edge_weights = jnp.concatenate([w_edges, w_tri_gate], axis=1) * halves]
    concatenate x1 -> x0, other arithmetic: 0.95 us -> none  [on_whole_complex(): edge_weights = jnp.concatenate([w_edges, w_tri_gate], axis=1)]
where the time goes in v12:
time: 21.8 us; the launch traced here: 21.7 us
  starting transfers between devices  8.3 us (38%)
  Pallas kernels  7.53 us (35%)
  waiting for transfers between devices  3.18 us (15%)
  local copies, waits for them, and re-layouts  1.28 us (6%)
  other arithmetic  0.99 us (5%)
    ppermute x8, starting transfers between devices, exchange(): return lax.ppermute(values, 'row', [(d, d ^ bit) for d in range(devices)])  8.3 us
    pallas_call x8, Pallas kernels, call(): pl.pallas_call(kernel, out_shape=outs, in_specs=[in_vmem] * len(operands)...  7.53 us
    ppermute x8, waiting for transfers between devices, exchange(): return lax.ppermute(values, 'row', [(d, d ^ bit) for d in range(devices)])  3.18 us
    unnamed x30, local copies, waits for them, and re-layouts  1.16 us
    mul x1, other arithmetic, on_whole_complex(): edge_weights = jnp.concatenate([w_edges, w_tri_gate], axis=1) * halves  0.97 us
  transfers between devices with their start and end apart: 8, of which 5 were waited for; matrix products, arithmetic and copies ran while one was open for 6% of the time, Pallas kernels for 23%

profile of v12, /device:TPU:0, one launch (start us, length us, event | category | flops | bytes accessed | tf_op | source)
XLA Modules:
  0.0 21.7 jit_solution(15708136850875935325)
XLA Ops:
  0.0 4.0 %collective-permute-start = (bf16[3,48,128]{2,1,0:T(8,128)(2,1)}, bf16[3,48,128]{2,1,0:T(8,128)(2,1)S(1)}, u32[]{:S(2)}, u32[]{:S(2)}) collective-permute-start(bf16[3,48,128]{2,1,0:T(8,128)(2,1)} %param.17), channel_id=1, source_target_pairs={{0,8},{1,9},{2,10},{3,11},{4,12},{5,13},{6,14},{7,15},{8,0},{9,1},... | collective-permute-start | bytes 110600 | tf_op jit(solution)/shard_map/ppermute | solution.py:519
  4.1 1.0 %maximum_multiply_fusion.weights = bf16[128,640]{1,0:T(8,128)(2,1)S(1)} fusion(bf16[128,128]{1,0:T(8,128)(2,1)} %param.22, bf16[128,512]{1,0:T(8,128)(2,1)} %param.21, bf16[640]{0:T(1024)(128)(2,1)S(1)} %select_convert_fusion), kind=kLoop, calls=%fused_computation.2 | loop fusion | flops 491520 | bytes 328960 | tf_op jit(solution)/shard_map/mul | solution.py:532
  5.1 0.6 %copy-done.11 = f32[128]{0:T(128)S(1)} copy-done((f32[128]{0:T(128)S(1)}, f32[128]{0:T(128)}, u32[]{:S(2)}) %copy-start.11) | copy-done | bytes 536
  5.8 0.8 %collective-permute-done = bf16[3,48,128]{2,1,0:T(8,128)(2,1)S(1)} collective-permute-done((bf16[3,48,128]{2,1,0:T(8,128)(2,1)}, bf16[3,48,128]{2,1,0:T(8,128)(2,1)S(1)}, u32[]{:S(2)}, u32[]{:S(2)}) %collective-permute-start) | collective-permute-done | bytes 36896 | tf_op jit(solution)/shard_map/ppermute | solution.py:519
  6.6 2.5 %collective-permute-start.2 = (bf16[6,48,128]{2,1,0:T(8,128)(2,1)S(1)}, bf16[6,48,128]{2,1,0:T(8,128)(2,1)S(1)}, u32[]{:S(2)}, u32[]{:S(2)}) collective-permute-start(bf16[6,48,128]{2,1,0:T(8,128)(2,1)S(1)} %constant_dynamic-update-slice_fusion.refs_0_), channel_id=1, source_target_pairs={{0,6},{1,7},{2,4},{3,5},{4,2},{5,3},{6,0},{7,1},{8,14},{9,15},{10,... | collective-permute-start | bytes 221192 | tf_op jit(solution)/shard_map/ppermute | solution.py:519
  9.1 0.5 %collective-permute-start.1 = (bf16[6,48,128]{2,1,0:T(8,128)(2,1)S(1)}, bf16[6,48,128]{2,1,0:T(8,128)(2,1)S(1)}, u32[]{:S(2)}, u32[]{:S(2)}) collective-permute-start(bf16[6,48,128]{2,1,0:T(8,128)(2,1)S(1)} %constant_dynamic-update-slice_fusion.refs_0_), channel_id=1, source_target_pairs={{0,2},{1,3},{2,0},{3,1},{4,6},{5,7},{6,4},{7,5},{8,10},{9,11},{10,... | collective-permute-start | bytes 221192 | tf_op jit(solution)/shard_map/ppermute | solution.py:519
  9.6 0.5 %collective-permute-start.3 = (bf16[6,48,128]{2,1,0:T(8,128)(2,1)S(1)}, bf16[6,48,128]{2,1,0:T(8,128)(2,1)S(1)}, u32[]{:S(2)}, u32[]{:S(2)}) collective-permute-start(bf16[6,48,128]{2,1,0:T(8,128)(2,1)S(1)} %constant_dynamic-update-slice_fusion.refs_0_), channel_id=1, source_target_pairs={{0,4},{1,5},{2,6},{3,7},{4,0},{5,1},{6,2},{7,3},{8,12},{9,13},{10,... | collective-permute-start | bytes 221192 | tf_op jit(solution)/shard_map/ppermute | solution.py:519
  10.1 0.2 fusion.wide_bias
  10.4 0.4 %copy-done.14 = s32[48]{0:T(128)S(1)} copy-done((s32[48]{0:T(128)S(1)}, s32[48]{0:T(128)}, u32[]{:S(2)}) %copy-start.14) | copy-done | bytes 216
  10.8 0.1 broadcast_in_dim.23.valid_column
  10.9 0.4 %shard_map.163 = (f32[1152,128]{1,0:T(8,128)S(1)}, f32[1152,128]{1,0:T(8,128)S(1)}, f32[1152,128]{1,0:T(8,128)S(1)}, f32[1152,128]{1,0:T(8,128)S(1)}, bf16[12,48...) custom-call(f32[48,128]{1,0:T(8,128)S(1)} %broadcast_in_dim.23.valid_column, f32[6,128]{1,0:T(8,128)S(1)} %stack.27.norms, ...), custom_call_target="tpu_custom_call" | custom-call | flops 1048576 | bytes 33554432 | tf_op jit(solution)/shard_map/pallas_call | solution.py:507
  11.3 1.1 %collective-permute-done.2.refs_0_ = bf16[6,48,128]{2,1,0:T(8,128)(2,1)S(1)} collective-permute-done((bf16[6,48,128]{2,1,0:T(8,128)(2,1)S(1)}, bf16[6,48,128]{2,1,0:T(8,128)(2,1)S(1)}, u32[]{:S(2)}, u32[]{:S(2)}) %collective-permute-start.2) | collective-permute-done | bytes 73760 | tf_op jit(solution)/shard_map/ppermute | solution.py:519
  12.4 0.4 %shard_map.164 = (f32[1152,128]{1,0:T(8,128)S(1)}, f32[1152,128]{1,0:T(8,128)S(1)}, f32[1152,128]{1,0:T(8,128)S(1)}, f32[1152,128]{1,0:T(8,128)S(1)}, bf16[12,48,128]{2,1,0:T(8,128)(2,1)S(1)}) custom-call(f32[48,128]{1,0:T(8,128)S(1)} %broadcast_in_dim.23.valid_column, ...), custom_call_target="tpu_custom_call", output_to_operand_aliasing={{0}: (4, {}), {1}: (5, {}), {2}: (6, {}), {3}: (7, {}), {4}... | custom-call | flops 1048576 | bytes 33554432 | tf_op jit(solution)/shard_map/pallas_call | solution.py:507
  12.8 0.6 %collective-permute-done.1.refs_0_ = bf16[6,48,128]{2,1,0:T(8,128)(2,1)S(1)} collective-permute-done((bf16[6,48,128]{2,1,0:T(8,128)(2,1)S(1)}, bf16[6,48,128]{2,1,0:T(8,128)(2,1)S(1)}, u32[]{:S(2)}, u32[]{:S(2)}) %collective-permute-start.1) | collective-permute-done | bytes 73760 | tf_op jit(solution)/shard_map/ppermute | solution.py:519
  13.4 0.5 %collective-permute-done.3.refs_1_ = bf16[6,48,128]{2,1,0:T(8,128)(2,1)S(1)} collective-permute-done((bf16[6,48,128]{2,1,0:T(8,128)(2,1)S(1)}, bf16[6,48,128]{2,1,0:T(8,128)(2,1)S(1)}, u32[]{:S(2)}, u32[]{:S(2)}) %collective-permute-start.3) | collective-permute-done | bytes 73760 | tf_op jit(solution)/shard_map/ppermute | solution.py:519
  14.0 0.6 %shard_map.165 = (f32[1152,128]{1,0:T(8,128)S(1)}, f32[1152,128]{1,0:T(8,128)S(1)}, f32[1152,128]{1,0:T(8,128)S(1)}, f32[1152,128]{1,0:T(8,128)S(1)}, bf16[12,48,128]{2,1,0:T(8,128)(2,1)S(1)}) custom-call(f32[48,128]{1,0:T(8,128)S(1)} %broadcast_in_dim.23.valid_column, ...), custom_call_target="tpu_custom_call", output_to_operand_aliasing={{0}: (5, {}), {1}: (6, {}), {2}: (7, {}), {3}: (8, {})} | custom-call | flops 1048576 | bytes 33554432 | tf_op jit(solution)/shard_map/pallas_call | solution.py:507
  14.7 0.1 collective-permute-done.4.refs_0_
  14.8 1.2 %shard_map.166 = (f32[1152,128]{1,0:T(8,128)S(1)}, f32[1152,128]{1,0:T(8,128)S(1)}) custom-call(f32[1152,128]{1,0:T(8,128)S(1)} %get-tuple-element.72.left_ref.refs_0_, f32[1152,128]{1,0:T(8,128)S(1)} %get-tuple-element.75.right_ref, bf16[12,48,128]{2,1,0:T(8,128)(2,1)S(1)} %collective-permute-done.4.refs_0_), custom_call_target="tpu_custom_call" | custom-call | flops 1048576 | bytes 33554432 | tf_op jit(solution)/shard_map/pallas_call | solution.py:507
  16.0 1.1 %shard_map.167 = (f32[1152,128]{1,0:T(8,128)S(1)}, f32[576,128]{1,0:T(8,128)S(1)}, bf16[576,128]{1,0:T(8,128)(2,1)S(1)}) custom-call(f32[6,128]{1,0:T(8,128)S(1)} %stack.27.norms, bf16[128,128]{1,0:T(8,128)(2,1)S(1)} %copy-done.1, f32[1152,128]{1,0:T(8,128)S(1)} %get-tuple-element.72.left_ref.refs_0_, ...), custom_call_target="tpu_custom_call", output_to_operand_aliasing={{0}: (7, {})} | custom-call | flops 1048576 | bytes 33554432 | tf_op jit(solution)/shard_map/pallas_call | solution.py:507
  17.2 0.4 %collective-permute-start.7 = (bf16[576,128]{1,0:T(8,128)(2,1)S(1)}, bf16[576,128]{1,0:T(8,128)(2,1)S(1)}, u32[]{:S(2)}, u32[]{:S(2)}) collective-permute-start(bf16[576,128]{1,0:T(8,128)(2,1)S(1)} %get-tuple-element.81.own_att_a), channel_id=1, source_target_pairs={{0,1},{1,0},{2,3},{3,2},{4,5},{5,4},{6,7},{7,6},{8,9},{9,8},{10,11... | collective-permute-start | bytes 442376 | tf_op jit(solution)/shard_map/ppermute | solution.py:519
  17.6 1.1 %shard_map.168.own_att_b = bf16[576,128]{1,0:T(8,128)(2,1)S(1)} custom-call(f32[6,128]{1,0:T(8,128)S(1)} %stack.27.norms, bf16[128,128]{1,0:T(8,128)(2,1)S(1)} %copy-done.1, f32[1152,128]{1,0:T(8,128)S(1)} %get-tuple-element.72.left_ref.refs_0_, f32[1152,128]{1,0:T(8,128)S(1)} %get-tuple-element.73.gate_ref.refs_1_, ...), custom_call_target="tpu_custom_call" | custom-call | flops 1048576 | bytes 33554432 | tf_op jit(solution)/shard_map/pallas_call | solution.py:507
  18.7 0.2 %collective-permute-start.6 = (bf16[576,128]{1,0:T(8,128)(2,1)S(1)}, bf16[576,128]{1,0:T(8,128)(2,1)S(1)}, u32[]{:S(2)}, u32[]{:S(2)}) collective-permute-start(bf16[576,128]{1,0:T(8,128)(2,1)S(1)} %shard_map.168.own_att_b), channel_id=1, source_target_pairs={{0,1},{1,0},{2,3},{3,2},{4,5},{5,4},{6,7},{7,6},{8,9},{9,8},{10,11... | collective-permute-start | bytes 442376 | tf_op jit(solution)/shard_map/ppermute | solution.py:519
  18.9 1.3 %shard_map.169 = (f32[3,3,48,128]{3,2,1,0:T(8,128)S(1)}, f32[144,128]{1,0:T(8,128)S(1)}, f32[144,128]{1,0:T(8,128)S(1)}, f32[144,128]{1,0:T(8,128)S(1)}) custom-call(f32[48,128]{1,0:T(8,128)S(1)} %broadcast_in_dim.23.valid_column, bf16[256,256]{1,0:T(8,128)(2,1)S(1)} %get-tuple-element.50.same_head, bf16[128,128]{1,0:T(8,128)(2,1)S(1)} %copy-done.4, ...), custom_call_target="tpu_custom_call" | custom-call | flops 1048576 | bytes 33554432 | tf_op jit(solution)/shard_map/pallas_call | solution.py:507
  20.3 1.4 %shard_map.170 = bf16[3,48,128]{2,1,0:T(8,128)(2,1)} custom-call(f32[48,128]{1,0:T(8,128)S(1)} %broadcast_in_dim.23.valid_column, bf16[256,256]{1,0:T(8,128)(2,1)S(1)} %get-tuple-element.50.same_head, bf16[128,128]{1,0:T(8,128)(2,1)S(1)} %copy-done.2, bf16[128,128]{1,0:T(8,128)(2,1)S(1)} %copy-done.3, bf16[128,128]{1,0:T(8,128)(2,1)S(1)} %copy-done.6, ...), custom_call_target="tpu_custom_call" | custom-call | flops 1048576 | bytes 33554432 | tf_op jit(solution)/shard_map/pallas_call | solution.py:507
  (40 shorter events, 0.3 us)
Async XLA Ops:
  0.0 10.1 %copy-start = (bf16[128,4]{0,1:T(4,128)(2,1)S(1)}, bf16[128,4]{0,1:T(4,128)(2,1)}, u32[]{:S(2)}) copy-start(bf16[128,4]{0,1:T(4,128)(2,1)} %param.32) | copy-start | bytes 3076
  0.0 6.6 %collective-permute-start = (bf16[3,48,128]{2,1,0:T(8,128)(2,1)}, bf16[3,48,128]{2,1,0:T(8,128)(2,1)S(1)}, u32[]{:S(2)}, u32[]{:S(2)}) collective-permute-start(bf16[3,48,128]{2,1,0:T(8,128)(2,1)} %param.17), channel_id=1, source_target_pairs={{0,8},{1,9},{2,10},{3,11},{4,12},{5,13},{6,14},{7,15},{8,0},{9,1},... | collective-permute-start | bytes 110600 | tf_op jit(solution)/shard_map/ppermute | solution.py:519
  4.1 1.0 %copy-start.7 = (bf16[3,48,128]{2,1,0:T(8,128)(2,1)S(1)}, bf16[3,48,128]{2,1,0:T(8,128)(2,1)}, u32[]{:S(2)}) copy-start(bf16[3,48,128]{2,1,0:T(8,128)(2,1)} %param.17) | copy-start | bytes 110596
  5.1 0.7 %copy-start.11 = (f32[128]{0:T(128)S(1)}, f32[128]{0:T(128)}, u32[]{:S(2)}) copy-start(f32[128]{0:T(128)} %param.24) | copy-start | bytes 1540
  5.1 0.7 %copy-start.12 = (f32[128]{0:T(128)S(1)}, f32[128]{0:T(128)}, u32[]{:S(2)}) copy-start(f32[128]{0:T(128)} %param.26) | copy-start | bytes 1540
  5.1 0.7 %copy-start.13 = (f32[128]{0:T(128)S(1)}, f32[128]{0:T(128)}, u32[]{:S(2)}) copy-start(f32[128]{0:T(128)} %param.27) | copy-start | bytes 1540
  5.1 0.7 %copy-start.8 = (f32[128]{0:T(128)S(1)}, f32[128]{0:T(128)}, u32[]{:S(2)}) copy-start(f32[128]{0:T(128)} %param.19) | copy-start | bytes 1540
  5.1 0.7 %copy-start.9 = (f32[128]{0:T(128)S(1)}, f32[128]{0:T(128)}, u32[]{:S(2)}) copy-start(f32[128]{0:T(128)} %param.20) | copy-start | bytes 1540
  5.1 0.7 %copy-start.10 = (f32[128]{0:T(128)S(1)}, f32[128]{0:T(128)}, u32[]{:S(2)}) copy-start(f32[128]{0:T(128)} %param.23) | copy-start | bytes 1540
  6.6 5.8 %collective-permute-start.2 = (bf16[6,48,128]{2,1,0:T(8,128)(2,1)S(1)}, bf16[6,48,128]{2,1,0:T(8,128)(2,1)S(1)}, u32[]{:S(2)}, u32[]{:S(2)}) collective-permute-start(bf16[6,48,128]{2,1,0:T(8,128)(2,1)S(1)} %constant_dynamic-update-slice_fusion.refs_0_), channel_id=1, source_target_pairs={{0,6},{1,7},{2,4},{3,5},{4,2},{5,3},{6,0},{7,1},{8,14},{9,15},{10,... | collective-permute-start | bytes 221192 | tf_op jit(solution)/shard_map/ppermute | solution.py:519
  9.1 4.4 %collective-permute-start.1 = (bf16[6,48,128]{2,1,0:T(8,128)(2,1)S(1)}, bf16[6,48,128]{2,1,0:T(8,128)(2,1)S(1)}, u32[]{:S(2)}, u32[]{:S(2)}) collective-permute-start(bf16[6,48,128]{2,1,0:T(8,128)(2,1)S(1)} %constant_dynamic-update-slice_fusion.refs_0_), channel_id=1, source_target_pairs={{0,2},{1,3},{2,0},{3,1},{4,6},{5,7},{6,4},{7,5},{8,10},{9,11},{10,... | collective-permute-start | bytes 221192 | tf_op jit(solution)/shard_map/ppermute | solution.py:519
  9.6 4.4 %collective-permute-start.3 = (bf16[6,48,128]{2,1,0:T(8,128)(2,1)S(1)}, bf16[6,48,128]{2,1,0:T(8,128)(2,1)S(1)}, u32[]{:S(2)}, u32[]{:S(2)}) collective-permute-start(bf16[6,48,128]{2,1,0:T(8,128)(2,1)S(1)} %constant_dynamic-update-slice_fusion.refs_0_), channel_id=1, source_target_pairs={{0,4},{1,5},{2,6},{3,7},{4,0},{5,1},{6,2},{7,3},{8,12},{9,13},{10,... | collective-permute-start | bytes 221192 | tf_op jit(solution)/shard_map/ppermute | solution.py:519
  10.1 0.7 %copy-start.14 = (s32[48]{0:T(128)S(1)}, s32[48]{0:T(128)}, u32[]{:S(2)}) copy-start(s32[48]{0:T(128)} %param.18) | copy-start | bytes 580
  13.4 1.4 %collective-permute-start.4 = (bf16[12,48,128]{2,1,0:T(8,128)(2,1)S(1)}, bf16[12,48,128]{2,1,0:T(8,128)(2,1)S(1)}, u32[]{:S(2)}, u32[]{:S(2)}) collective-permute-start(bf16[12,48,128]{2,1,0:T(8,128)(2,1)S(1)} %get-tuple-element.76), channel_id=1, source_target_pairs={{0,1},{1,0},{2,3},{3,2},{4,5},{5,4},{6,7},{7,6},{8,9},{9,8},{10,11... | collective-permute-start | bytes 442376 | tf_op jit(solution)/shard_map/ppermute | solution.py:519
  14.6 1.4 %collective-permute-start.5 = (bf16[12,48,128]{2,1,0:T(8,128)(2,1)S(1)}, bf16[12,48,128]{2,1,0:T(8,128)(2,1)S(1)}, u32[]{:S(2)}, u32[]{:S(2)}) collective-permute-start(bf16[12,48,128]{2,1,0:T(8,128)(2,1)S(1)} %get-tuple-element.78), channel_id=1, source_target_pairs={{0,1},{1,0},{2,3},{3,2},{4,5},{5,4},{6,7},{7,6},{8,9},{9,8},{10,11... | collective-permute-start | bytes 442376 | tf_op jit(solution)/shard_map/ppermute | solution.py:519
  14.8 1.2 %copy-start.1 = (bf16[128,128]{1,0:T(8,128)(2,1)S(1)}, bf16[128,128]{1,0:T(8,128)(2,1)}, u32[]{:S(2)}) copy-start(bf16[128,128]{1,0:T(8,128)(2,1)} %w_out.4) | copy-start | bytes 98308
  17.2 1.8 %collective-permute-start.7 = (bf16[576,128]{1,0:T(8,128)(2,1)S(1)}, bf16[576,128]{1,0:T(8,128)(2,1)S(1)}, u32[]{:S(2)}, u32[]{:S(2)}) collective-permute-start(bf16[576,128]{1,0:T(8,128)(2,1)S(1)} %get-tuple-element.81.own_att_a), channel_id=1, source_target_pairs={{0,1},{1,0},{2,3},{3,2},{4,5},{5,4},{6,7},{7,6},{8,9},{9,8},{10,11... | collective-permute-start | bytes 442376 | tf_op jit(solution)/shard_map/ppermute | solution.py:519
  17.6 1.3 %copy-start.2 = (bf16[128,128]{1,0:T(8,128)(2,1)S(1)}, bf16[128,128]{1,0:T(8,128)(2,1)}, u32[]{:S(2)}) copy-start(bf16[128,128]{1,0:T(8,128)(2,1)} %w_key.3) | copy-start | bytes 98308
  17.6 1.3 %copy-start.3 = (bf16[128,128]{1,0:T(8,128)(2,1)S(1)}, bf16[128,128]{1,0:T(8,128)(2,1)}, u32[]{:S(2)}) copy-start(bf16[128,128]{1,0:T(8,128)(2,1)} %w_value.3) | copy-start | bytes 98308
  17.6 1.3 %copy-start.4 = (bf16[128,128]{1,0:T(8,128)(2,1)S(1)}, bf16[128,128]{1,0:T(8,128)(2,1)}, u32[]{:S(2)}) copy-start(bf16[128,128]{1,0:T(8,128)(2,1)} %w_query.1) | copy-start | bytes 98308
  17.6 1.3 %copy-start.5 = (bf16[128,128]{1,0:T(8,128)(2,1)S(1)}, bf16[128,128]{1,0:T(8,128)(2,1)}, u32[]{:S(2)}) copy-start(bf16[128,128]{1,0:T(8,128)(2,1)} %w_gate.1) | copy-start | bytes 98308
  18.7 1.6 %collective-permute-start.6 = (bf16[576,128]{1,0:T(8,128)(2,1)S(1)}, bf16[576,128]{1,0:T(8,128)(2,1)S(1)}, u32[]{:S(2)}, u32[]{:S(2)}) collective-permute-start(bf16[576,128]{1,0:T(8,128)(2,1)S(1)} %shard_map.168.own_att_b), channel_id=1, source_target_pairs={{0,1},{1,0},{2,3},{3,2},{4,5},{5,4},{6,7},{7,6},{8,9},{9,8},{10,11... | collective-permute-start | bytes 442376 | tf_op jit(solution)/shard_map/ppermute | solution.py:519
  18.9 1.3 %copy-start.6 = (bf16[128,128]{1,0:T(8,128)(2,1)S(1)}, bf16[128,128]{1,0:T(8,128)(2,1)}, u32[]{:S(2)}) copy-start(bf16[128,128]{1,0:T(8,128)(2,1)} %w_out.5) | copy-start | bytes 98308

commit v13 on v12

--- a/solution.py
+++ b/solution.py
@@ -230,8 +230,7 @@
                 )
 
 
-def near_triangle_kernel(row_count, chips, chunk, pieces, left_ref, right_ref, *refs):
-    received, (triangle_ref, across_ref) = refs[:-2], refs[-2:]
+def near_triangle_kernel(row_count, chips, chunk, left_ref, right_ref, triangle_ref):
     _, core = chip_and_core()
 
     def some_rows(step, carry):
@@ -241,9 +240,6 @@
         )
         return carry
 
-    for ref, blocks in zip(received, pieces):
-        for n, (chip, r) in enumerate(rows_of_blocks(row_count, blocks)):
-            place_right(across_ref, chips, chip, r, ref[n])
     lax.fori_loop(0, row_count * chips // chunk, some_rows, 0)
 
 
@@ -280,16 +276,17 @@
     left_ref,
     gate_ref,
     pairs_ref,
-    received,
+    early,
+    late,
     triangle_ref,
-    held_across,
     across_ref,
     after_ref,
     att_ref,
     scratch_ref,
 ):
-    for n, (chip, r) in enumerate(rows_of_blocks(row_count, blocks)):
-        place_right(across_ref, chips, chip, r, received[n])
+    for received, senders in zip((early, late), blocks):
+        for n, (chip, r) in enumerate(rows_of_blocks(row_count, senders)):
+            place_right(across_ref, chips, chip, r, received[n])
     first = first_chip(chips, 0) * row_count
     refs = (left_ref, gate_ref, pairs_ref, triangle_ref, across_ref, scratch_ref)
     after_ref[...], att_ref[...] = attention_inputs(
@@ -310,8 +307,8 @@
     for values in att:
         rows = slice(start, start + values.shape[0])
         joined = dot(values, key_value)
-        key_ref[rows, :] = joined[:, :channels]
-        value_ref[rows, :] = joined[:, channels:]
+        key_ref[rows, :] = rounded(joined[:, :channels])
+        value_ref[rows, :] = rounded(joined[:, channels:])
         start = rows.stop
 
 
@@ -333,45 +330,47 @@
         bias_ref[r, :height, :] = bias[r * height : (r + 1) * height]
 
 
-def partial_attention(row_count, chips, query, parts, bias_ref, same_head, valid_column, score_ref):
-    bf16, f32 = jnp.bfloat16, jnp.float32
+def partial_attention(
+    row_count, chips, query, parts, bias_ref, same_head, valid_column, sums
+):
+    bf16 = jnp.bfloat16
     res = 2 * row_count * chips
     channels = valid_column.shape[1]
     count = row_count * chips // 2
-    keys = len(parts) * count
-    maxima = [jnp.full((res, channels), -jnp.inf, f32) for _ in range(row_count)]
-    for part, (core, first, key_of, _) in enumerate(parts):
+    for part, (core, first, key_of, value_of) in enumerate(parts):
         products = []
         for n in range(0, count, 2):
             pair = [jnp.concatenate([key_of(m)] * row_count, axis=0) * query for m in (n, n + 1)]
             products.append(jnp.concatenate([p.astype(bf16) for p in pair], axis=1))
         scores = dot(jnp.concatenate(products, axis=0), same_head[...])
-        for n in range(count):
+
+        def score_of(n, r):
+            start = (n // 2 * row_count + r) * res
+            lanes = slice(n % 2 * channels, (n % 2 + 1) * channels)
             k = (2 * (first + n // row_count) + core) * row_count + n % row_count
             key_mask = 1000000000.0 * (valid_column[pl.ds(k, 1), :] - 1.0)
             at = part * count + n
-            shifts = [
-                (bias_ref[r, at : at + 1, :] + key_mask) * math.log2(math.e)
-                for r in range(row_count)
-            ]
-            lanes = slice(n % 2 * channels, (n % 2 + 1) * channels)
-            for r in range(row_count):
-                start = (n // 2 * row_count + r) * res
-                score = scores[start : start + res, lanes] + shifts[r]
-                score_ref[(r * keys + at) * res : (r * keys + at + 1) * res, :] = score
-                maxima[r] = jnp.maximum(maxima[r], score)
-    totals, mixed = [], []
-    for r in range(row_count):
-        total = mix = jnp.zeros((res, channels), f32)
-        for part, (_, _, _, value_of) in enumerate(parts):
+            shift = (bias_ref[r, at : at + 1, :] + key_mask) * math.log2(math.e)
+            return scores[start : start + res, lanes] + shift
+
+        later = []
+        for r, (maximum, total, mixed) in enumerate(sums):
+            highest = score_of(0, r)
+            for n in range(1, count):
+                highest = jnp.maximum(highest, score_of(n, r))
+            if maximum is None:
+                maximum, total, mixed = highest, 0.0, 0.0
+            else:
+                highest = jnp.maximum(highest, maximum)
+                scale = jnp.exp2(maximum - highest)
+                maximum, total, mixed = highest, total * scale, mixed * scale
             for n in range(count):
-                start = (r * keys + part * count + n) * res
-                weight = jnp.exp2(score_ref[start : start + res, :] - maxima[r])
+                weight = jnp.exp2(score_of(n, r) - maximum)
                 total = total + weight
-                mix = mix + weight * value_of(n)
-        totals.append(total)
-        mixed.append(mix)
-    return maxima, totals, mixed
+                mixed = mixed + weight * value_of(n)
+            later.append((maximum, total, mixed))
+        sums = later
+    return sums
 
 
 def most_attention_kernel(
@@ -396,7 +395,6 @@
     key_ref,
     value_ref,
     bias_ref,
-    score_ref,
 ):
     chip, core = chip_and_core()
     res, channels = valid_column.shape
@@ -417,12 +415,13 @@
         (sender, first, rows_of(key_ref, n * count), rows_of(value_ref, n * count))
         for n, (sender, first) in enumerate(((core, a), (core, b), (1 - core, a)))
     ]
+    none = [(None, None, None)] * row_count
     sums = partial_attention(
-        row_count, chips, query, parts, bias_ref, same_head, valid_column, score_ref
-    )
-    for n, each in enumerate(sums):
-        for r in range(row_count):
-            sums_ref[r, n] = each[r]
+        row_count, chips, query, parts, bias_ref, same_head, valid_column, none
+    )
+    for r in range(row_count):
+        for n, each in enumerate(sums[r]):
+            sums_ref[r, n] = each
     query_ref[...] = query
     gate_ref[...] = sigmoid(dot(own_in, w_gate[...]))
     after_ref[...] = own_after[rows, :]
@@ -447,7 +446,6 @@
     key_ref,
     value_ref,
     bias_ref,
-    score_ref,
 ):
     _, core = chip_and_core()
     res, channels = valid_column.shape
@@ -459,16 +457,11 @@
         return lambda n: ref[n * res : (n + 1) * res, :]
 
     parts = ((1 - core, first_chip(chips, 1), rows_of(key_ref), rows_of(value_ref)),)
-    last = partial_attention(
-        row_count, chips, query_ref[...], parts, bias_ref, same_head, valid_column, score_ref
-    )
-    attended = []
-    for r, (last_maximum, last_total, last_mixed) in enumerate(zip(*last)):
-        maximum = jnp.maximum(sums_ref[r, 0], last_maximum)
-        most_scale = jnp.exp2(sums_ref[r, 0] - maximum)
-        last_scale = jnp.exp2(last_maximum - maximum)
-        total = sums_ref[r, 1] * most_scale + last_total * last_scale
-        attended.append((sums_ref[r, 2] * most_scale + last_mixed * last_scale) / total)
+    sums = [tuple(sums_ref[r, n] for n in range(3)) for r in range(row_count)]
+    sums = partial_attention(
+        row_count, chips, query_ref[...], parts, bias_ref, same_head, valid_column, sums
+    )
+    attended = [mixed / total for _, total, mixed in sums]
     gated = (jnp.concatenate(attended, axis=0) * gate_ref[...]).astype(jnp.bfloat16)
     final = after_ref[...] + dot(gated, w_out[...])
     out_ref[...] = final.astype(jnp.bfloat16).reshape(row_count, res, channels)
@@ -553,11 +546,12 @@
     def edges_of(pieces, send_row, *held):
         pairs = tuple(p for p, _ in pieces)
         blocks = tuple(b for _, b in pieces)
+        sent = (2 if held and send_row == 0 else 6) * row_count
         operands = (valid_column, norms, edge_weights) + pairs + held
         first = len(operands) - len(held)
         return call(
             functools.partial(edges_kernel, row_count, chips, blocks, send_row, not held),
-            (tall, tall, tall, tall, shaped(bf16, 4 * row_count, res, channels))
+            (tall, tall, tall, tall, shaped(bf16, sent, res, channels))
             + (() if held else (shaped(bf16, 2 * channels, 2 * channels),)),
             operands,
             {first + e: e for e in range(len(held))},
@@ -571,20 +565,16 @@
     *edges, early_right = edges_of(
         [(diagonal, blocks_from(3))], 2 * row_count, *edges, early_right
     )
-    beside, edges, early_right, wide_bias = lax.optimization_barrier(
-        (beside, edges, early_right, wide_bias)
-    )
-    early = (exchange(early_right, 1), own_blocks + blocks_from(3))
-    *edges, late_right = edges_of(
-        [(beside, blocks_from(1)), (near, blocks_from(2))], 0, *edges
-    )
-    late = (exchange(late_right, 1), blocks_from(1) + blocks_from(2))
+    beside, edges, wide_bias = lax.optimization_barrier((beside, edges, wide_bias))
+    *edges, early_right = edges_of([(beside, blocks_from(1))], 4 * row_count, *edges, early_right)
+    near, edges, early_right = lax.optimization_barrier((near, edges, early_right))
+    early = (exchange(early_right, 1), own_blocks + blocks_from(3) + blocks_from(1))
+    *edges, late_right = edges_of([(near, blocks_from(2))], 0, *edges)
+    late = (exchange(late_right, 1), blocks_from(2))
 
     left, right, gate, pairs = edges
-    triangle, across = call(
-        functools.partial(near_triangle_kernel, row_count, chips, half // 2, [early[1]]),
-        (tall, tall),
-        (left, right, early[0]),
+    triangle = call(
+        functools.partial(near_triangle_kernel, row_count, chips, half // 2), tall, (left, right)
     )
     part = half // 2 * res
     in_part, own_shape = shaped(f32, part, channels), shaped(f32, row_count * res, channels)
@@ -592,10 +582,9 @@
     shared = (norms, w_tri_out, left, gate, pairs)
     scratch = (pltpu.VMEM((part, channels), f32),)
     across, after_a, att_a = call(
-        functools.partial(own_inputs_kernel, row_count, chips, late[1]),
+        functools.partial(own_inputs_kernel, row_count, chips, (early[1], late[1])),
         (tall, in_part, att_part),
-        shared + (late[0], triangle, across),
-        {7: 0},
+        shared + (early[0], late[0], triangle),
         scratch=scratch,
     )
     far_att_a = exchange(att_a, 1)
@@ -613,7 +602,6 @@
             pltpu.VMEM((projected * res, channels), f32),
             pltpu.VMEM((projected * res, channels), f32),
             pltpu.VMEM((row_count, 40, channels), f32),
-            pltpu.VMEM((row_count * keys * res, channels), f32),
         )
 
     sums, query, att_gate, after_own = call(

time: 21.8 us -> 22 us (level)
  waiting for transfers between devices: 3.18 us -> 2.61 us
  starting transfers between devices: 8.3 us -> 8.8 us
    ppermute x8, waiting for transfers between devices: 3.18 us -> 2.61 us  [exchange(): return lax.ppermute(values, 'row', [(d, d ^ bit) for d in range(devices)])]
    ppermute x8, starting transfers between devices: 8.3 us -> 8.8 us  [exchange(): return lax.ppermute(values, 'row', [(d, d ^ bit) for d in range(devices)])]
    pallas_call x8 -> x9, Pallas kernels: 7.53 us -> 7.73 us  [call(): pl.pallas_call(kernel, out_shape=outs, in_specs=[in_vmem] * len(operands)...]
  transfers between devices with their start and end apart: 8 -> 8, of which waited for: 5 -> 4; matrix products, arithmetic and copies ran while one was open for 6% -> 6% of each run, Pallas kernels for 23% -> 24%
where the time goes in v13:
time: 22 us; the launch traced here: 21.8 us
  starting transfers between devices  8.8 us (40%)
  Pallas kernels  7.73 us (35%)
  waiting for transfers between devices  2.61 us (12%)
  local copies, waits for them, and re-layouts  1.28 us (6%)
  other arithmetic  0.99 us (4%)
  between operations  0.22 us (1%)
    ppermute x8, starting transfers between devices, exchange(): return lax.ppermute(values, 'row', [(d, d ^ bit) for d in range(devices)])  8.8 us
    pallas_call x9, Pallas kernels, call(): pl.pallas_call(kernel, out_shape=outs, in_specs=[in_vmem] * len(operands)...  7.73 us
    ppermute x8, waiting for transfers between devices, exchange(): return lax.ppermute(values, 'row', [(d, d ^ bit) for d in range(devices)])  2.61 us
    unnamed x30, local copies, waits for them, and re-layouts  1.17 us
    mul x1, other arithmetic, on_whole_complex(): edge_weights = jnp.concatenate([w_edges, w_tri_gate], axis=1) * halves  0.97 us
  transfers between devices with their start and end apart: 8, of which 4 were waited for; matrix products, arithmetic and copies ran while one was open for 6% of the time, Pallas kernels for 24%

profile of v13, /device:TPU:0, one launch (start us, length us, event | category | flops | bytes accessed | tf_op | source)
XLA Modules:
  0.0 21.8 jit_solution(1460666082702090198)
XLA Ops:
  0.0 4.0 %collective-permute-start = (bf16[3,48,128]{2,1,0:T(8,128)(2,1)}, bf16[3,48,128]{2,1,0:T(8,128)(2,1)S(1)}, u32[]{:S(2)}, u32[]{:S(2)}) collective-permute-start(bf16[3,48,128]{2,1,0:T(8,128)(2,1)} %param.17), channel_id=1, source_target_pairs={{0,8},{1,9},{2,10},{3,11},{4,12},{5,13},{6,14},{7,15},{8,0},{9,1},... | collective-permute-start | bytes 110600 | tf_op jit(solution)/shard_map/ppermute | solution.py:512
  4.1 1.0 %maximum_multiply_fusion.weights = bf16[128,640]{1,0:T(8,128)(2,1)S(1)} fusion(bf16[128,128]{1,0:T(8,128)(2,1)} %param.22, bf16[128,512]{1,0:T(8,128)(2,1)} %param.21, bf16[640]{0:T(1024)(128)(2,1)S(1)} %select_convert_fusion), kind=kLoop, calls=%fused_computation.2 | loop fusion | flops 491520 | bytes 328960 | tf_op jit(solution)/shard_map/mul | solution.py:525
  5.1 0.6 %copy-done.11 = f32[128]{0:T(128)S(1)} copy-done((f32[128]{0:T(128)S(1)}, f32[128]{0:T(128)}, u32[]{:S(2)}) %copy-start.11) | copy-done | bytes 536
  5.8 0.8 %collective-permute-done = bf16[3,48,128]{2,1,0:T(8,128)(2,1)S(1)} collective-permute-done((bf16[3,48,128]{2,1,0:T(8,128)(2,1)}, bf16[3,48,128]{2,1,0:T(8,128)(2,1)S(1)}, u32[]{:S(2)}, u32[]{:S(2)}) %collective-permute-start) | collective-permute-done | bytes 36896 | tf_op jit(solution)/shard_map/ppermute | solution.py:512
  6.6 2.5 %collective-permute-start.2 = (bf16[6,48,128]{2,1,0:T(8,128)(2,1)S(1)}, bf16[6,48,128]{2,1,0:T(8,128)(2,1)S(1)}, u32[]{:S(2)}, u32[]{:S(2)}) collective-permute-start(bf16[6,48,128]{2,1,0:T(8,128)(2,1)S(1)} %constant_dynamic-update-slice_fusion.refs_0_), channel_id=1, source_target_pairs={{0,6},{1,7},{2,4},{3,5},{4,2},{5,3},{6,0},{7,1},{8,14},{9,15},{10,... | collective-permute-start | bytes 221192 | tf_op jit(solution)/shard_map/ppermute | solution.py:512
  9.1 0.5 %collective-permute-start.1 = (bf16[6,48,128]{2,1,0:T(8,128)(2,1)S(1)}, bf16[6,48,128]{2,1,0:T(8,128)(2,1)S(1)}, u32[]{:S(2)}, u32[]{:S(2)}) collective-permute-start(bf16[6,48,128]{2,1,0:T(8,128)(2,1)S(1)} %constant_dynamic-update-slice_fusion.refs_0_), channel_id=1, source_target_pairs={{0,2},{1,3},{2,0},{3,1},{4,6},{5,7},{6,4},{7,5},{8,10},{9,11},{10,... | collective-permute-start | bytes 221192 | tf_op jit(solution)/shard_map/ppermute | solution.py:512
  9.6 0.5 %collective-permute-start.3 = (bf16[6,48,128]{2,1,0:T(8,128)(2,1)S(1)}, bf16[6,48,128]{2,1,0:T(8,128)(2,1)S(1)}, u32[]{:S(2)}, u32[]{:S(2)}) collective-permute-start(bf16[6,48,128]{2,1,0:T(8,128)(2,1)S(1)} %constant_dynamic-update-slice_fusion.refs_0_), channel_id=1, source_target_pairs={{0,4},{1,5},{2,6},{3,7},{4,0},{5,1},{6,2},{7,3},{8,12},{9,13},{10,... | collective-permute-start | bytes 221192 | tf_op jit(solution)/shard_map/ppermute | solution.py:512
  10.1 0.2 fusion.wide_bias
  10.4 0.4 %copy-done.14 = s32[48]{0:T(128)S(1)} copy-done((s32[48]{0:T(128)S(1)}, s32[48]{0:T(128)}, u32[]{:S(2)}) %copy-start.14) | copy-done | bytes 216
  10.9 0.4 %shard_map.163 = (f32[1152,128]{1,0:T(8,128)S(1)}, f32[1152,128]{1,0:T(8,128)S(1)}, f32[1152,128]{1,0:T(8,128)S(1)}, f32[1152,128]{1,0:T(8,128)S(1)}, bf16[18,48...) custom-call(f32[48,128]{1,0:T(8,128)S(1)} %broadcast_in_dim.23.valid_column, f32[6,128]{1,0:T(8,128)S(1)} %stack.27.norms, ...), custom_call_target="tpu_custom_call" | custom-call | flops 1048576 | bytes 33554432 | tf_op jit(solution)/shard_map/pallas_call | solution.py:500
  11.3 1.1 %collective-permute-done.2.refs_0_ = bf16[6,48,128]{2,1,0:T(8,128)(2,1)S(1)} collective-permute-done((bf16[6,48,128]{2,1,0:T(8,128)(2,1)S(1)}, bf16[6,48,128]{2,1,0:T(8,128)(2,1)S(1)}, u32[]{:S(2)}, u32[]{:S(2)}) %collective-permute-start.2) | collective-permute-done | bytes 73760 | tf_op jit(solution)/shard_map/ppermute | solution.py:512
  12.4 0.4 %shard_map.164 = (f32[1152,128]{1,0:T(8,128)S(1)}, f32[1152,128]{1,0:T(8,128)S(1)}, f32[1152,128]{1,0:T(8,128)S(1)}, f32[1152,128]{1,0:T(8,128)S(1)}, bf16[18,48,128]{2,1,0:T(8,128)(2,1)S(1)}) custom-call(f32[48,128]{1,0:T(8,128)S(1)} %broadcast_in_dim.23.valid_column, ...), custom_call_target="tpu_custom_call", output_to_operand_aliasing={{0}: (4, {}), {1}: (5, {}), {2}: (6, {}), {3}: (7, {}), {4}... | custom-call | flops 1048576 | bytes 33554432 | tf_op jit(solution)/shard_map/pallas_call | solution.py:500
  12.8 0.6 %collective-permute-done.1.refs_0_ = bf16[6,48,128]{2,1,0:T(8,128)(2,1)S(1)} collective-permute-done((bf16[6,48,128]{2,1,0:T(8,128)(2,1)S(1)}, bf16[6,48,128]{2,1,0:T(8,128)(2,1)S(1)}, u32[]{:S(2)}, u32[]{:S(2)}) %collective-permute-start.1) | collective-permute-done | bytes 73760 | tf_op jit(solution)/shard_map/ppermute | solution.py:512
  13.4 0.4 %shard_map.165 = (f32[1152,128]{1,0:T(8,128)S(1)}, f32[1152,128]{1,0:T(8,128)S(1)}, f32[1152,128]{1,0:T(8,128)S(1)}, f32[1152,128]{1,0:T(8,128)S(1)}, bf16[18,48,128]{2,1,0:T(8,128)(2,1)S(1)}) custom-call(f32[48,128]{1,0:T(8,128)S(1)} %broadcast_in_dim.23.valid_column, ...), custom_call_target="tpu_custom_call", output_to_operand_aliasing={{0}: (4, {}), {1}: (5, {}), {2}: (6, {}), {3}: (7, {}), {4}... | custom-call | flops 1048576 | bytes 33554432 | tf_op jit(solution)/shard_map/pallas_call | solution.py:500
  13.9 0.1 collective-permute-done.3.refs_0_
  14.0 0.4 %shard_map.166 = (f32[1152,128]{1,0:T(8,128)S(1)}, f32[1152,128]{1,0:T(8,128)S(1)}, f32[1152,128]{1,0:T(8,128)S(1)}, f32[1152,128]{1,0:T(8,128)S(1)}, bf16[6,48,128]{2,1,0:T(8,128)(2,1)S(1)}) custom-call(f32[48,128]{1,0:T(8,128)S(1)} %broadcast_in_dim.23.valid_column, ...), custom_call_target="tpu_custom_call", output_to_operand_aliasing={{0}: (4, {}), {1}: (5, {}), {2}: (6, {}), {3}: (7, {})} | custom-call | flops 1048576 | bytes 33554432 | tf_op jit(solution)/shard_map/pallas_call | solution.py:500
  14.4 0.6 %collective-permute-start.5 = (bf16[6,48,128]{2,1,0:T(8,128)(2,1)S(1)}, bf16[6,48,128]{2,1,0:T(8,128)(2,1)S(1)}, u32[]{:S(2)}, u32[]{:S(2)}) collective-permute-start(bf16[6,48,128]{2,1,0:T(8,128)(2,1)S(1)} %get-tuple-element.95), channel_id=1, source_target_pairs={{0,1},{1,0},{2,3},{3,2},{4,5},{5,4},{6,7},{7,6},{8,9},{9,8},{10,11... | collective-permute-start | bytes 221192 | tf_op jit(solution)/shard_map/ppermute | solution.py:512
  15.0 1.2 %shard_map.167.triangle_ref.refs_3_ = f32[1152,128]{1,0:T(8,128)S(1)} custom-call(f32[1152,128]{1,0:T(8,128)S(1)} %get-tuple-element.90.left_ref.refs_0_, f32[1152,128]{1,0:T(8,128)S(1)} %get-tuple-element.93.right_ref), custom_call_target="tpu_custom_call" | custom-call | flops 1048576 | bytes 33554432 | tf_op jit(solution)/shard_map/pallas_call | solution.py:500
  16.2 1.1 %shard_map.168 = (f32[1152,128]{1,0:T(8,128)S(1)}, f32[576,128]{1,0:T(8,128)S(1)}, bf16[576,128]{1,0:T(8,128)(2,1)S(1)}) custom-call(f32[6,128]{1,0:T(8,128)S(1)} %stack.27.norms, bf16[128,128]{1,0:T(8,128)(2,1)S(1)} %copy-done.1, f32[1152,128]{1,0:T(8,128)S(1)} %get-tuple-element.90.left_ref.refs_0_, f32[1152,128]{1,0:T(8,128)S(1)} %get-tuple-element.91.gate_ref.refs_1_, ...), custom_call_target="tpu_custom_call" | custom-call | flops 1048576 | bytes 33554432 | tf_op jit(solution)/shard_map/pallas_call | solution.py:500
  17.3 0.1 collective-permute-start.7
  17.5 1.1 %shard_map.169.own_att_b = bf16[576,128]{1,0:T(8,128)(2,1)S(1)} custom-call(f32[6,128]{1,0:T(8,128)S(1)} %stack.27.norms, bf16[128,128]{1,0:T(8,128)(2,1)S(1)} %copy-done.1, f32[1152,128]{1,0:T(8,128)S(1)} %get-tuple-element.90.left_ref.refs_0_, f32[1152,128]{1,0:T(8,128)S(1)} %get-tuple-element.91.gate_ref.refs_1_, ...), custom_call_target="tpu_custom_call" | custom-call | flops 1048576 | bytes 33554432 | tf_op jit(solution)/shard_map/pallas_call | solution.py:500
  18.6 0.5 %collective-permute-start.6 = (bf16[576,128]{1,0:T(8,128)(2,1)S(1)}, bf16[576,128]{1,0:T(8,128)(2,1)S(1)}, u32[]{:S(2)}, u32[]{:S(2)}) collective-permute-start(bf16[576,128]{1,0:T(8,128)(2,1)S(1)} %shard_map.169.own_att_b), channel_id=1, source_target_pairs={{0,1},{1,0},{2,3},{3,2},{4,5},{5,4},{6,7},{7,6},{8,9},{9,8},{10,11... | collective-permute-start | bytes 442376 | tf_op jit(solution)/shard_map/ppermute | solution.py:512
  19.1 1.3 %shard_map.170 = (f32[3,3,48,128]{3,2,1,0:T(8,128)S(1)}, f32[144,128]{1,0:T(8,128)S(1)}, f32[144,128]{1,0:T(8,128)S(1)}, f32[144,128]{1,0:T(8,128)S(1)}) custom-call(f32[48,128]{1,0:T(8,128)S(1)} %broadcast_in_dim.23.valid_column, bf16[256,256]{1,0:T(8,128)(2,1)S(1)} %get-tuple-element.58.same_head, bf16[128,128]{1,0:T(8,128)(2,1)S(1)} %copy-done.4, ...), custom_call_target="tpu_custom_call" | custom-call | flops 1048576 | bytes 33554432 | tf_op jit(solution)/shard_map/pallas_call | solution.py:500
  20.4 1.4 %shard_map.171 = bf16[3,48,128]{2,1,0:T(8,128)(2,1)} custom-call(f32[48,128]{1,0:T(8,128)S(1)} %broadcast_in_dim.23.valid_column, bf16[256,256]{1,0:T(8,128)(2,1)S(1)} %get-tuple-element.58.same_head, bf16[128,128]{1,0:T(8,128)(2,1)S(1)} %copy-done.2, bf16[128,128]{1,0:T(8,128)(2,1)S(1)} %copy-done.3, bf16[128,128]{1,0:T(8,128)(2,1)S(1)} %copy-done.6, ...), custom_call_target="tpu_custom_call" | custom-call | flops 1048576 | bytes 33554432 | tf_op jit(solution)/shard_map/pallas_call | solution.py:500
  (41 shorter events, 0.3 us)
Async XLA Ops:
  0.0 10.1 %copy-start = (bf16[128,4]{0,1:T(4,128)(2,1)S(1)}, bf16[128,4]{0,1:T(4,128)(2,1)}, u32[]{:S(2)}) copy-start(bf16[128,4]{0,1:T(4,128)(2,1)} %param.32) | copy-start | bytes 3076
  0.0 6.6 %collective-permute-start = (bf16[3,48,128]{2,1,0:T(8,128)(2,1)}, bf16[3,48,128]{2,1,0:T(8,128)(2,1)S(1)}, u32[]{:S(2)}, u32[]{:S(2)}) collective-permute-start(bf16[3,48,128]{2,1,0:T(8,128)(2,1)} %param.17), channel_id=1, source_target_pairs={{0,8},{1,9},{2,10},{3,11},{4,12},{5,13},{6,14},{7,15},{8,0},{9,1},... | collective-permute-start | bytes 110600 | tf_op jit(solution)/shard_map/ppermute | solution.py:512
  4.1 1.0 %copy-start.7 = (bf16[3,48,128]{2,1,0:T(8,128)(2,1)S(1)}, bf16[3,48,128]{2,1,0:T(8,128)(2,1)}, u32[]{:S(2)}) copy-start(bf16[3,48,128]{2,1,0:T(8,128)(2,1)} %param.17) | copy-start | bytes 110596
  5.1 0.7 %copy-start.11 = (f32[128]{0:T(128)S(1)}, f32[128]{0:T(128)}, u32[]{:S(2)}) copy-start(f32[128]{0:T(128)} %param.24) | copy-start | bytes 1540
  5.1 0.7 %copy-start.12 = (f32[128]{0:T(128)S(1)}, f32[128]{0:T(128)}, u32[]{:S(2)}) copy-start(f32[128]{0:T(128)} %param.26) | copy-start | bytes 1540
  5.1 0.7 %copy-start.13 = (f32[128]{0:T(128)S(1)}, f32[128]{0:T(128)}, u32[]{:S(2)}) copy-start(f32[128]{0:T(128)} %param.27) | copy-start | bytes 1540
  5.1 0.7 %copy-start.8 = (f32[128]{0:T(128)S(1)}, f32[128]{0:T(128)}, u32[]{:S(2)}) copy-start(f32[128]{0:T(128)} %param.19) | copy-start | bytes 1540
  5.1 0.7 %copy-start.9 = (f32[128]{0:T(128)S(1)}, f32[128]{0:T(128)}, u32[]{:S(2)}) copy-start(f32[128]{0:T(128)} %param.20) | copy-start | bytes 1540
  5.1 0.7 %copy-start.10 = (f32[128]{0:T(128)S(1)}, f32[128]{0:T(128)}, u32[]{:S(2)}) copy-start(f32[128]{0:T(128)} %param.23) | copy-start | bytes 1540
  6.6 5.8 %collective-permute-start.2 = (bf16[6,48,128]{2,1,0:T(8,128)(2,1)S(1)}, bf16[6,48,128]{2,1,0:T(8,128)(2,1)S(1)}, u32[]{:S(2)}, u32[]{:S(2)}) collective-permute-start(bf16[6,48,128]{2,1,0:T(8,128)(2,1)S(1)} %constant_dynamic-update-slice_fusion.refs_0_), channel_id=1, source_target_pairs={{0,6},{1,7},{2,4},{3,5},{4,2},{5,3},{6,0},{7,1},{8,14},{9,15},{10,... | collective-permute-start | bytes 221192 | tf_op jit(solution)/shard_map/ppermute | solution.py:512
  9.1 4.4 %collective-permute-start.1 = (bf16[6,48,128]{2,1,0:T(8,128)(2,1)S(1)}, bf16[6,48,128]{2,1,0:T(8,128)(2,1)S(1)}, u32[]{:S(2)}, u32[]{:S(2)}) collective-permute-start(bf16[6,48,128]{2,1,0:T(8,128)(2,1)S(1)} %constant_dynamic-update-slice_fusion.refs_0_), channel_id=1, source_target_pairs={{0,2},{1,3},{2,0},{3,1},{4,6},{5,7},{6,4},{7,5},{8,10},{9,11},{10,... | collective-permute-start | bytes 221192 | tf_op jit(solution)/shard_map/ppermute | solution.py:512
  9.6 4.4 %collective-permute-start.3 = (bf16[6,48,128]{2,1,0:T(8,128)(2,1)S(1)}, bf16[6,48,128]{2,1,0:T(8,128)(2,1)S(1)}, u32[]{:S(2)}, u32[]{:S(2)}) collective-permute-start(bf16[6,48,128]{2,1,0:T(8,128)(2,1)S(1)} %constant_dynamic-update-slice_fusion.refs_0_), channel_id=1, source_target_pairs={{0,4},{1,5},{2,6},{3,7},{4,0},{5,1},{6,2},{7,3},{8,12},{9,13},{10,... | collective-permute-start | bytes 221192 | tf_op jit(solution)/shard_map/ppermute | solution.py:512
  10.1 0.7 %copy-start.14 = (s32[48]{0:T(128)S(1)}, s32[48]{0:T(128)}, u32[]{:S(2)}) copy-start(s32[48]{0:T(128)} %param.18) | copy-start | bytes 580
  14.0 2.2 %collective-permute-start.4 = (bf16[18,48,128]{2,1,0:T(8,128)(2,1)S(1)}, bf16[18,48,128]{2,1,0:T(8,128)(2,1)S(1)}, u32[]{:S(2)}, u32[]{:S(2)}) collective-permute-start(bf16[18,48,128]{2,1,0:T(8,128)(2,1)S(1)} %get-tuple-element.94), channel_id=1, source_target_pairs={{0,1},{1,0},{2,3},{3,2},{4,5},{5,4},{6,7},{7,6},{8,9},{9,8},{10,11... | collective-permute-start | bytes 663560 | tf_op jit(solution)/shard_map/ppermute | solution.py:512
  14.4 1.8 %collective-permute-start.5 = (bf16[6,48,128]{2,1,0:T(8,128)(2,1)S(1)}, bf16[6,48,128]{2,1,0:T(8,128)(2,1)S(1)}, u32[]{:S(2)}, u32[]{:S(2)}) collective-permute-start(bf16[6,48,128]{2,1,0:T(8,128)(2,1)S(1)} %get-tuple-element.95), channel_id=1, source_target_pairs={{0,1},{1,0},{2,3},{3,2},{4,5},{5,4},{6,7},{7,6},{8,9},{9,8},{10,11... | collective-permute-start | bytes 221192 | tf_op jit(solution)/shard_map/ppermute | solution.py:512
  15.0 1.2 %copy-start.1 = (bf16[128,128]{1,0:T(8,128)(2,1)S(1)}, bf16[128,128]{1,0:T(8,128)(2,1)}, u32[]{:S(2)}) copy-start(bf16[128,128]{1,0:T(8,128)(2,1)} %w_out.4) | copy-start | bytes 98308
  17.3 1.8 %collective-permute-start.7 = (bf16[576,128]{1,0:T(8,128)(2,1)S(1)}, bf16[576,128]{1,0:T(8,128)(2,1)S(1)}, u32[]{:S(2)}, u32[]{:S(2)}) collective-permute-start(bf16[576,128]{1,0:T(8,128)(2,1)S(1)} %get-tuple-element.97.own_att_a), channel_id=1, source_target_pairs={{0,1},{1,0},{2,3},{3,2},{4,5},{5,4},{6,7},{7,6},{8,9},{9,8},{10,11... | collective-permute-start | bytes 442376 | tf_op jit(solution)/shard_map/ppermute | solution.py:512
  17.4 1.6 %copy-start.2 = (bf16[128,128]{1,0:T(8,128)(2,1)S(1)}, bf16[128,128]{1,0:T(8,128)(2,1)}, u32[]{:S(2)}) copy-start(bf16[128,128]{1,0:T(8,128)(2,1)} %w_key.3) | copy-start | bytes 98308
  17.4 1.6 %copy-start.3 = (bf16[128,128]{1,0:T(8,128)(2,1)S(1)}, bf16[128,128]{1,0:T(8,128)(2,1)}, u32[]{:S(2)}) copy-start(bf16[128,128]{1,0:T(8,128)(2,1)} %w_value.3) | copy-start | bytes 98308
  17.5 1.6 %copy-start.4 = (bf16[128,128]{1,0:T(8,128)(2,1)S(1)}, bf16[128,128]{1,0:T(8,128)(2,1)}, u32[]{:S(2)}) copy-start(bf16[128,128]{1,0:T(8,128)(2,1)} %w_query.1) | copy-start | bytes 98308
  17.5 1.7 %copy-start.5 = (bf16[128,128]{1,0:T(8,128)(2,1)S(1)}, bf16[128,128]{1,0:T(8,128)(2,1)}, u32[]{:S(2)}) copy-start(bf16[128,128]{1,0:T(8,128)(2,1)} %w_gate.1) | copy-start | bytes 98308
  18.6 1.9 %collective-permute-start.6 = (bf16[576,128]{1,0:T(8,128)(2,1)S(1)}, bf16[576,128]{1,0:T(8,128)(2,1)S(1)}, u32[]{:S(2)}, u32[]{:S(2)}) collective-permute-start(bf16[576,128]{1,0:T(8,128)(2,1)S(1)} %shard_map.169.own_att_b), channel_id=1, source_target_pairs={{0,1},{1,0},{2,3},{3,2},{4,5},{5,4},{6,7},{7,6},{8,9},{9,8},{10,11... | collective-permute-start | bytes 442376 | tf_op jit(solution)/shard_map/ppermute | solution.py:512
  19.1 1.3 %copy-start.6 = (bf16[128,128]{1,0:T(8,128)(2,1)S(1)}, bf16[128,128]{1,0:T(8,128)(2,1)}, u32[]{:S(2)}) copy-start(bf16[128,128]{1,0:T(8,128)(2,1)} %w_out.5) | copy-start | bytes 98308

commit v14 on v13

--- a/solution.py
+++ b/solution.py
@@ -174,7 +174,7 @@
         axis=0,
     )
     joined = dot(normed, weights[:, : 2 * channels])
-    left = rounded((jnp.tanh(joined[:, channels:]) + 1.0) * joined[:, :channels] * masks)
+    left = ((jnp.tanh(joined[:, channels:]) + 1.0) * joined[:, :channels] * masks).astype(bf16)
     joined = dot(normed, weights[:, 2 * channels : 4 * channels])
     right = ((jnp.tanh(joined[:, channels:]) + 1.0) * joined[:, :channels] * masks).astype(bf16)
     gate = 0.5 * jnp.tanh(dot(normed, weights[:, 4 * channels :])) + 0.5
@@ -191,7 +191,7 @@
 def place_right(right_ref, chips, chip, r, edges):
     res = edges.shape[0]
     start = pl.multiple_of((r * chips + chip) * res, res)
-    right_ref[pl.ds(start, res), :] = edges.astype(jnp.float32)
+    right_ref[pl.ds(start, res), :] = edges
 
 
 def sum_sublanes(parts):
@@ -220,14 +220,13 @@
                 right = right_ref[at : at + res, :]
                 for m in range(block):
                     product = lefts[m] * right
-                    parts[m].append(
-                        sum(product[k : k + 8] for k in range(8, res, 8)) + product[:8]
-                    )
+                    third = res // 3
+                    some = product[:third] + product[third : 2 * third] + product[2 * third :]
+                    some = some.astype(jnp.float32)
+                    parts[m].append(sum((some[k : k + 8] for k in range(8, third, 8)), some[:8]))
             for m in range(block):
                 place = (triangle_first + n + m) * res + core * row_count + r
-                triangle_ref[pl.ds(place, chips, stride=2 * row_count), :] = rounded(
-                    sum_sublanes(parts[m])
-                )
+                triangle_ref[pl.ds(place, chips, stride=2 * row_count), :] = sum_sublanes(parts[m])
 
 
 def near_triangle_kernel(row_count, chips, chunk, left_ref, right_ref, triangle_ref):
@@ -338,20 +337,20 @@
     channels = valid_column.shape[1]
     count = row_count * chips // 2
     for part, (core, first, key_of, value_of) in enumerate(parts):
-        products = []
-        for n in range(0, count, 2):
-            pair = [jnp.concatenate([key_of(m)] * row_count, axis=0) * query for m in (n, n + 1)]
-            products.append(jnp.concatenate([p.astype(bf16) for p in pair], axis=1))
-        scores = dot(jnp.concatenate(products, axis=0), same_head[...])
+        scores = []
+        for r in range(row_count):
+            own_query = query[r * res : (r + 1) * res]
+            products = [(key_of(n) * own_query).astype(bf16) for n in range(count)]
+            pairs = [jnp.concatenate(products[n : n + 2], axis=1) for n in range(0, count, 2)]
+            scores.append(dot(jnp.concatenate(pairs, axis=0), same_head[...]))
 
         def score_of(n, r):
-            start = (n // 2 * row_count + r) * res
             lanes = slice(n % 2 * channels, (n % 2 + 1) * channels)
             k = (2 * (first + n // row_count) + core) * row_count + n % row_count
             key_mask = 1000000000.0 * (valid_column[pl.ds(k, 1), :] - 1.0)
             at = part * count + n
             shift = (bias_ref[r, at : at + 1, :] + key_mask) * math.log2(math.e)
-            return scores[start : start + res, lanes] + shift
+            return scores[r][n // 2 * res : (n // 2 + 1) * res, lanes] + shift
 
         later = []
         for r, (maximum, total, mixed) in enumerate(sums):
@@ -542,6 +541,7 @@
         return tuple(s ^ bits for s in own_blocks)
 
     tall = shaped(f32, half * res, channels)
+    edge = shaped(bf16, half * res, channels)
 
     def edges_of(pieces, send_row, *held):
         pairs = tuple(p for p, _ in pieces)
@@ -551,7 +551,7 @@
         first = len(operands) - len(held)
         return call(
             functools.partial(edges_kernel, row_count, chips, blocks, send_row, not held),
-            (tall, tall, tall, tall, shaped(bf16, sent, res, channels))
+            (edge, edge, tall, tall, shaped(bf16, sent, res, channels))
             + (() if held else (shaped(bf16, 2 * channels, 2 * channels),)),
             operands,
             {first + e: e for e in range(len(held))},
@@ -583,7 +583,7 @@
     scratch = (pltpu.VMEM((part, channels), f32),)
     across, after_a, att_a = call(
         functools.partial(own_inputs_kernel, row_count, chips, (early[1], late[1])),
-        (tall, in_part, att_part),
+        (edge, in_part, att_part),
         shared + (early[0], late[0], triangle),
         scratch=scratch,
     )

time: 22 us -> 22.3 us (1.014)
  Pallas kernels: 7.73 us -> 7.99 us
    pallas_call x9, Pallas kernels: 7.73 us -> 7.99 us  [call(): pl.pallas_call(kernel, out_shape=outs, in_specs=[in_vmem] * len(operands)...]
  transfers between devices with their start and end apart: 8 -> 8, of which waited for: 4 -> 4; matrix products, arithmetic and copies ran while one was open for 6% -> 6% of each run, Pallas kernels for 24% -> 25%
where the time goes in v14:
time: 22.3 us; the launch traced here: 22.1 us
  starting transfers between devices  8.78 us (39%)
  Pallas kernels  7.99 us (36%)
  waiting for transfers between devices  2.62 us (12%)
  local copies, waits for them, and re-layouts  1.28 us (6%)
  other arithmetic  0.99 us (4%)
  between operations  0.23 us (1%)
    ppermute x8, starting transfers between devices, exchange(): return lax.ppermute(values, 'row', [(d, d ^ bit) for d in range(devices)])  8.78 us
    pallas_call x9, Pallas kernels, call(): pl.pallas_call(kernel, out_shape=outs, in_specs=[in_vmem] * len(operands)...  7.99 us
    ppermute x8, waiting for transfers between devices, exchange(): return lax.ppermute(values, 'row', [(d, d ^ bit) for d in range(devices)])  2.62 us
    unnamed x30, local copies, waits for them, and re-layouts  1.17 us
    mul x1, other arithmetic, on_whole_complex(): edge_weights = jnp.concatenate([w_edges, w_tri_gate], axis=1) * halves  0.97 us
  transfers between devices with their start and end apart: 8, of which 4 were waited for; matrix products, arithmetic and copies ran while one was open for 6% of the time, Pallas kernels for 25%

profile of v14, /device:TPU:0, one launch (start us, length us, event | category | flops | bytes accessed | tf_op | source)
XLA Modules:
  0.0 22.1 jit_solution(6094313307490677208)
XLA Ops:
  0.0 4.0 %collective-permute-start = (bf16[3,48,128]{2,1,0:T(8,128)(2,1)}, bf16[3,48,128]{2,1,0:T(8,128)(2,1)S(1)}, u32[]{:S(2)}, u32[]{:S(2)}) collective-permute-start(bf16[3,48,128]{2,1,0:T(8,128)(2,1)} %param.17), channel_id=1, source_target_pairs={{0,8},{1,9},{2,10},{3,11},{4,12},{5,13},{6,14},{7,15},{8,0},{9,1},... | collective-permute-start | bytes 110600 | tf_op jit(solution)/shard_map/ppermute | solution.py:511
  4.1 1.0 %maximum_multiply_fusion.weights = bf16[128,640]{1,0:T(8,128)(2,1)S(1)} fusion(bf16[128,128]{1,0:T(8,128)(2,1)} %param.22, bf16[128,512]{1,0:T(8,128)(2,1)} %param.21, bf16[640]{0:T(1024)(128)(2,1)S(1)} %select_convert_fusion), kind=kLoop, calls=%fused_computation.2 | loop fusion | flops 491520 | bytes 328960 | tf_op jit(solution)/shard_map/mul | solution.py:524
  5.1 0.6 %copy-done.11 = f32[128]{0:T(128)S(1)} copy-done((f32[128]{0:T(128)S(1)}, f32[128]{0:T(128)}, u32[]{:S(2)}) %copy-start.11) | copy-done | bytes 536
  5.8 0.8 %collective-permute-done = bf16[3,48,128]{2,1,0:T(8,128)(2,1)S(1)} collective-permute-done((bf16[3,48,128]{2,1,0:T(8,128)(2,1)}, bf16[3,48,128]{2,1,0:T(8,128)(2,1)S(1)}, u32[]{:S(2)}, u32[]{:S(2)}) %collective-permute-start) | collective-permute-done | bytes 36896 | tf_op jit(solution)/shard_map/ppermute | solution.py:511
  6.6 2.5 %collective-permute-start.2 = (bf16[6,48,128]{2,1,0:T(8,128)(2,1)S(1)}, bf16[6,48,128]{2,1,0:T(8,128)(2,1)S(1)}, u32[]{:S(2)}, u32[]{:S(2)}) collective-permute-start(bf16[6,48,128]{2,1,0:T(8,128)(2,1)S(1)} %constant_dynamic-update-slice_fusion.refs_0_), channel_id=1, source_target_pairs={{0,6},{1,7},{2,4},{3,5},{4,2},{5,3},{6,0},{7,1},{8,14},{9,15},{10,... | collective-permute-start | bytes 221192 | tf_op jit(solution)/shard_map/ppermute | solution.py:511
  9.1 0.5 %collective-permute-start.1 = (bf16[6,48,128]{2,1,0:T(8,128)(2,1)S(1)}, bf16[6,48,128]{2,1,0:T(8,128)(2,1)S(1)}, u32[]{:S(2)}, u32[]{:S(2)}) collective-permute-start(bf16[6,48,128]{2,1,0:T(8,128)(2,1)S(1)} %constant_dynamic-update-slice_fusion.refs_0_), channel_id=1, source_target_pairs={{0,2},{1,3},{2,0},{3,1},{4,6},{5,7},{6,4},{7,5},{8,10},{9,11},{10,... | collective-permute-start | bytes 221192 | tf_op jit(solution)/shard_map/ppermute | solution.py:511
  9.6 0.5 %collective-permute-start.3 = (bf16[6,48,128]{2,1,0:T(8,128)(2,1)S(1)}, bf16[6,48,128]{2,1,0:T(8,128)(2,1)S(1)}, u32[]{:S(2)}, u32[]{:S(2)}) collective-permute-start(bf16[6,48,128]{2,1,0:T(8,128)(2,1)S(1)} %constant_dynamic-update-slice_fusion.refs_0_), channel_id=1, source_target_pairs={{0,4},{1,5},{2,6},{3,7},{4,0},{5,1},{6,2},{7,3},{8,12},{9,13},{10,... | collective-permute-start | bytes 221192 | tf_op jit(solution)/shard_map/ppermute | solution.py:511
  10.1 0.2 fusion.wide_bias
  10.4 0.4 %copy-done.14 = s32[48]{0:T(128)S(1)} copy-done((s32[48]{0:T(128)S(1)}, s32[48]{0:T(128)}, u32[]{:S(2)}) %copy-start.14) | copy-done | bytes 216
  10.9 0.4 %shard_map.163 = (bf16[1152,128]{1,0:T(8,128)(2,1)S(1)}, bf16[1152,128]{1,0:T(8,128)(2,1)S(1)}, f32[1152,128]{1,0:T(8,128)S(1)}, f32[1152,128]{1,0:T(8,128)S(1)}...) custom-call(f32[48,128]{1,0:T(8,128)S(1)} %broadcast_in_dim.23.valid_column, f32[6,128]{1,0:T(8,128)S(1)} %stack.27.norms, ...), custom_call_target="tpu_custom_call" | custom-call | flops 1048576 | bytes 33554432 | tf_op jit(solution)/shard_map/pallas_call | solution.py:499
  11.3 1.1 %collective-permute-done.2.refs_0_ = bf16[6,48,128]{2,1,0:T(8,128)(2,1)S(1)} collective-permute-done((bf16[6,48,128]{2,1,0:T(8,128)(2,1)S(1)}, bf16[6,48,128]{2,1,0:T(8,128)(2,1)S(1)}, u32[]{:S(2)}, u32[]{:S(2)}) %collective-permute-start.2) | collective-permute-done | bytes 73760 | tf_op jit(solution)/shard_map/ppermute | solution.py:511
  12.4 0.4 %shard_map.164 = (bf16[1152,128]{1,0:T(8,128)(2,1)S(1)}, bf16[1152,128]{1,0:T(8,128)(2,1)S(1)}, f32[1152,128]{1,0:T(8,128)S(1)}, f32[1152,128]{1,0:T(8,128)S(1)}, bf16[18,48,128]{2,1,0:T(8,128)(2,1)S(1)}) custom-call(f32[48,128]{1,0:T(8,128)S(1)} %broadcast_in_dim.23.valid_column, ...), custom_call_target="tpu_custom_call", output_to_operand_aliasing={{0}: (4, {}), {1}: (5, {}), {2}: (6, {}), {3}: (7, {}), {4}... | custom-call | flops 1048576 | bytes 33554432 | tf_op jit(solution)/shard_map/pallas_call | solution.py:499
  12.8 0.6 %collective-permute-done.1.refs_0_ = bf16[6,48,128]{2,1,0:T(8,128)(2,1)S(1)} collective-permute-done((bf16[6,48,128]{2,1,0:T(8,128)(2,1)S(1)}, bf16[6,48,128]{2,1,0:T(8,128)(2,1)S(1)}, u32[]{:S(2)}, u32[]{:S(2)}) %collective-permute-start.1) | collective-permute-done | bytes 73760 | tf_op jit(solution)/shard_map/ppermute | solution.py:511
  13.4 0.4 %shard_map.165 = (bf16[1152,128]{1,0:T(8,128)(2,1)S(1)}, bf16[1152,128]{1,0:T(8,128)(2,1)S(1)}, f32[1152,128]{1,0:T(8,128)S(1)}, f32[1152,128]{1,0:T(8,128)S(1)}, bf16[18,48,128]{2,1,0:T(8,128)(2,1)S(1)}) custom-call(f32[48,128]{1,0:T(8,128)S(1)} %broadcast_in_dim.23.valid_column, ...), custom_call_target="tpu_custom_call", output_to_operand_aliasing={{0}: (4, {}), {1}: (5, {}), {2}: (6, {}), {3}: (7, {}), {4}... | custom-call | flops 1048576 | bytes 33554432 | tf_op jit(solution)/shard_map/pallas_call | solution.py:499
  13.9 0.1 collective-permute-done.3.refs_0_
  14.0 0.4 %shard_map.166 = (bf16[1152,128]{1,0:T(8,128)(2,1)S(1)}, bf16[1152,128]{1,0:T(8,128)(2,1)S(1)}, f32[1152,128]{1,0:T(8,128)S(1)}, f32[1152,128]{1,0:T(8,128)S(1)}, bf16[6,48,128]{2,1,0:T(8,128)(2,1)S(1)}) custom-call(f32[48,128]{1,0:T(8,128)S(1)} %broadcast_in_dim.23.valid_column, ...), custom_call_target="tpu_custom_call", output_to_operand_aliasing={{0}: (4, {}), {1}: (5, {}), {2}: (6, {}), {3}: (7, {})} | custom-call | flops 1048576 | bytes 33554432 | tf_op jit(solution)/shard_map/pallas_call | solution.py:499
  14.4 0.6 %collective-permute-start.5 = (bf16[6,48,128]{2,1,0:T(8,128)(2,1)S(1)}, bf16[6,48,128]{2,1,0:T(8,128)(2,1)S(1)}, u32[]{:S(2)}, u32[]{:S(2)}) collective-permute-start(bf16[6,48,128]{2,1,0:T(8,128)(2,1)S(1)} %get-tuple-element.95), channel_id=1, source_target_pairs={{0,1},{1,0},{2,3},{3,2},{4,5},{5,4},{6,7},{7,6},{8,9},{9,8},{10,11... | collective-permute-start | bytes 221192 | tf_op jit(solution)/shard_map/ppermute | solution.py:511
  15.0 1.3 %shard_map.167.triangle_ref.refs_3_ = f32[1152,128]{1,0:T(8,128)S(1)} custom-call(bf16[1152,128]{1,0:T(8,128)(2,1)S(1)} %get-tuple-element.90.left_ref.refs_0_, bf16[1152,128]{1,0:T(8,128)(2,1)S(1)} %get-tuple-element.93.right_ref), custom_call_target="tpu_custom_call" | custom-call | flops 1048576 | bytes 33554432 | tf_op jit(solution)/shard_map/pallas_call | solution.py:499
  16.3 1.2 %shard_map.168 = (bf16[1152,128]{1,0:T(8,128)(2,1)S(1)}, f32[576,128]{1,0:T(8,128)S(1)}, bf16[576,128]{1,0:T(8,128)(2,1)S(1)}) custom-call(f32[6,128]{1,0:T(8,128)S(1)} %stack.27.norms, bf16[128,128]{1,0:T(8,128)(2,1)S(1)} %copy-done.1, bf16[1152,128]{1,0:T(8,128)(2,1)S(1)} %get-tuple-element.90.left_ref.refs_0_, ...), custom_call_target="tpu_custom_call" | custom-call | flops 1048576 | bytes 33554432 | tf_op jit(solution)/shard_map/pallas_call | solution.py:499
  17.5 0.1 collective-permute-start.7
  17.6 1.1 %shard_map.169.own_att_b = bf16[576,128]{1,0:T(8,128)(2,1)S(1)} custom-call(f32[6,128]{1,0:T(8,128)S(1)} %stack.27.norms, bf16[128,128]{1,0:T(8,128)(2,1)S(1)} %copy-done.1, bf16[1152,128]{1,0:T(8,128)(2,1)S(1)} %get-tuple-element.90.left_ref.refs_0_, f32[1152,128]{1,0:T(8,128)S(1)} %get-tuple-element.91.gate_ref.refs_1_, ...), custom_call_target="tpu_custom_call" | custom-call | flops 1048576 | bytes 33554432 | tf_op jit(solution)/shard_map/pallas_call | solution.py:499
  18.8 0.5 %collective-permute-start.6 = (bf16[576,128]{1,0:T(8,128)(2,1)S(1)}, bf16[576,128]{1,0:T(8,128)(2,1)S(1)}, u32[]{:S(2)}, u32[]{:S(2)}) collective-permute-start(bf16[576,128]{1,0:T(8,128)(2,1)S(1)} %shard_map.169.own_att_b), channel_id=1, source_target_pairs={{0,1},{1,0},{2,3},{3,2},{4,5},{5,4},{6,7},{7,6},{8,9},{9,8},{10,11... | collective-permute-start | bytes 442376 | tf_op jit(solution)/shard_map/ppermute | solution.py:511
  19.3 1.4 %shard_map.170 = (f32[3,3,48,128]{3,2,1,0:T(8,128)S(1)}, f32[144,128]{1,0:T(8,128)S(1)}, f32[144,128]{1,0:T(8,128)S(1)}, f32[144,128]{1,0:T(8,128)S(1)}) custom-call(f32[48,128]{1,0:T(8,128)S(1)} %broadcast_in_dim.23.valid_column, bf16[256,256]{1,0:T(8,128)(2,1)S(1)} %get-tuple-element.58.same_head, bf16[128,128]{1,0:T(8,128)(2,1)S(1)} %copy-done.4, ...), custom_call_target="tpu_custom_call" | custom-call | flops 1048576 | bytes 33554432 | tf_op jit(solution)/shard_map/pallas_call | solution.py:499
  20.7 1.4 %shard_map.171 = bf16[3,48,128]{2,1,0:T(8,128)(2,1)} custom-call(f32[48,128]{1,0:T(8,128)S(1)} %broadcast_in_dim.23.valid_column, bf16[256,256]{1,0:T(8,128)(2,1)S(1)} %get-tuple-element.58.same_head, bf16[128,128]{1,0:T(8,128)(2,1)S(1)} %copy-done.2, bf16[128,128]{1,0:T(8,128)(2,1)S(1)} %copy-done.3, bf16[128,128]{1,0:T(8,128)(2,1)S(1)} %copy-done.6, ...), custom_call_target="tpu_custom_call" | custom-call | flops 1048576 | bytes 33554432 | tf_op jit(solution)/shard_map/pallas_call | solution.py:499
  (41 shorter events, 0.3 us)
Async XLA Ops:
  0.0 10.1 %copy-start = (bf16[128,4]{0,1:T(4,128)(2,1)S(1)}, bf16[128,4]{0,1:T(4,128)(2,1)}, u32[]{:S(2)}) copy-start(bf16[128,4]{0,1:T(4,128)(2,1)} %param.32) | copy-start | bytes 3076
  0.0 6.6 %collective-permute-start = (bf16[3,48,128]{2,1,0:T(8,128)(2,1)}, bf16[3,48,128]{2,1,0:T(8,128)(2,1)S(1)}, u32[]{:S(2)}, u32[]{:S(2)}) collective-permute-start(bf16[3,48,128]{2,1,0:T(8,128)(2,1)} %param.17), channel_id=1, source_target_pairs={{0,8},{1,9},{2,10},{3,11},{4,12},{5,13},{6,14},{7,15},{8,0},{9,1},... | collective-permute-start | bytes 110600 | tf_op jit(solution)/shard_map/ppermute | solution.py:511
  4.1 1.0 %copy-start.7 = (bf16[3,48,128]{2,1,0:T(8,128)(2,1)S(1)}, bf16[3,48,128]{2,1,0:T(8,128)(2,1)}, u32[]{:S(2)}) copy-start(bf16[3,48,128]{2,1,0:T(8,128)(2,1)} %param.17) | copy-start | bytes 110596
  5.1 0.7 %copy-start.11 = (f32[128]{0:T(128)S(1)}, f32[128]{0:T(128)}, u32[]{:S(2)}) copy-start(f32[128]{0:T(128)} %param.24) | copy-start | bytes 1540
  5.1 0.7 %copy-start.12 = (f32[128]{0:T(128)S(1)}, f32[128]{0:T(128)}, u32[]{:S(2)}) copy-start(f32[128]{0:T(128)} %param.26) | copy-start | bytes 1540
  5.1 0.7 %copy-start.13 = (f32[128]{0:T(128)S(1)}, f32[128]{0:T(128)}, u32[]{:S(2)}) copy-start(f32[128]{0:T(128)} %param.27) | copy-start | bytes 1540
  5.1 0.7 %copy-start.8 = (f32[128]{0:T(128)S(1)}, f32[128]{0:T(128)}, u32[]{:S(2)}) copy-start(f32[128]{0:T(128)} %param.19) | copy-start | bytes 1540
  5.1 0.7 %copy-start.9 = (f32[128]{0:T(128)S(1)}, f32[128]{0:T(128)}, u32[]{:S(2)}) copy-start(f32[128]{0:T(128)} %param.20) | copy-start | bytes 1540
  5.1 0.7 %copy-start.10 = (f32[128]{0:T(128)S(1)}, f32[128]{0:T(128)}, u32[]{:S(2)}) copy-start(f32[128]{0:T(128)} %param.23) | copy-start | bytes 1540
  6.6 5.8 %collective-permute-start.2 = (bf16[6,48,128]{2,1,0:T(8,128)(2,1)S(1)}, bf16[6,48,128]{2,1,0:T(8,128)(2,1)S(1)}, u32[]{:S(2)}, u32[]{:S(2)}) collective-permute-start(bf16[6,48,128]{2,1,0:T(8,128)(2,1)S(1)} %constant_dynamic-update-slice_fusion.refs_0_), channel_id=1, source_target_pairs={{0,6},{1,7},{2,4},{3,5},{4,2},{5,3},{6,0},{7,1},{8,14},{9,15},{10,... | collective-permute-start | bytes 221192 | tf_op jit(solution)/shard_map/ppermute | solution.py:511
  9.1 4.4 %collective-permute-start.1 = (bf16[6,48,128]{2,1,0:T(8,128)(2,1)S(1)}, bf16[6,48,128]{2,1,0:T(8,128)(2,1)S(1)}, u32[]{:S(2)}, u32[]{:S(2)}) collective-permute-start(bf16[6,48,128]{2,1,0:T(8,128)(2,1)S(1)} %constant_dynamic-update-slice_fusion.refs_0_), channel_id=1, source_target_pairs={{0,2},{1,3},{2,0},{3,1},{4,6},{5,7},{6,4},{7,5},{8,10},{9,11},{10,... | collective-permute-start | bytes 221192 | tf_op jit(solution)/shard_map/ppermute | solution.py:511
  9.6 4.4 %collective-permute-start.3 = (bf16[6,48,128]{2,1,0:T(8,128)(2,1)S(1)}, bf16[6,48,128]{2,1,0:T(8,128)(2,1)S(1)}, u32[]{:S(2)}, u32[]{:S(2)}) collective-permute-start(bf16[6,48,128]{2,1,0:T(8,128)(2,1)S(1)} %constant_dynamic-update-slice_fusion.refs_0_), channel_id=1, source_target_pairs={{0,4},{1,5},{2,6},{3,7},{4,0},{5,1},{6,2},{7,3},{8,12},{9,13},{10,... | collective-permute-start | bytes 221192 | tf_op jit(solution)/shard_map/ppermute | solution.py:511
  10.1 0.7 %copy-start.14 = (s32[48]{0:T(128)S(1)}, s32[48]{0:T(128)}, u32[]{:S(2)}) copy-start(s32[48]{0:T(128)} %param.18) | copy-start | bytes 580
  14.0 2.3 %collective-permute-start.4 = (bf16[18,48,128]{2,1,0:T(8,128)(2,1)S(1)}, bf16[18,48,128]{2,1,0:T(8,128)(2,1)S(1)}, u32[]{:S(2)}, u32[]{:S(2)}) collective-permute-start(bf16[18,48,128]{2,1,0:T(8,128)(2,1)S(1)} %get-tuple-element.94), channel_id=1, source_target_pairs={{0,1},{1,0},{2,3},{3,2},{4,5},{5,4},{6,7},{7,6},{8,9},{9,8},{10,11... | collective-permute-start | bytes 663560 | tf_op jit(solution)/shard_map/ppermute | solution.py:511
  14.4 1.9 %collective-permute-start.5 = (bf16[6,48,128]{2,1,0:T(8,128)(2,1)S(1)}, bf16[6,48,128]{2,1,0:T(8,128)(2,1)S(1)}, u32[]{:S(2)}, u32[]{:S(2)}) collective-permute-start(bf16[6,48,128]{2,1,0:T(8,128)(2,1)S(1)} %get-tuple-element.95), channel_id=1, source_target_pairs={{0,1},{1,0},{2,3},{3,2},{4,5},{5,4},{6,7},{7,6},{8,9},{9,8},{10,11... | collective-permute-start | bytes 221192 | tf_op jit(solution)/shard_map/ppermute | solution.py:511
  15.0 1.3 %copy-start.1 = (bf16[128,128]{1,0:T(8,128)(2,1)S(1)}, bf16[128,128]{1,0:T(8,128)(2,1)}, u32[]{:S(2)}) copy-start(bf16[128,128]{1,0:T(8,128)(2,1)} %w_out.4) | copy-start | bytes 98308
  17.5 1.8 %collective-permute-start.7 = (bf16[576,128]{1,0:T(8,128)(2,1)S(1)}, bf16[576,128]{1,0:T(8,128)(2,1)S(1)}, u32[]{:S(2)}, u32[]{:S(2)}) collective-permute-start(bf16[576,128]{1,0:T(8,128)(2,1)S(1)} %get-tuple-element.97.own_att_a), channel_id=1, source_target_pairs={{0,1},{1,0},{2,3},{3,2},{4,5},{5,4},{6,7},{7,6},{8,9},{9,8},{10,11... | collective-permute-start | bytes 442376 | tf_op jit(solution)/shard_map/ppermute | solution.py:511
  17.6 1.7 %copy-start.2 = (bf16[128,128]{1,0:T(8,128)(2,1)S(1)}, bf16[128,128]{1,0:T(8,128)(2,1)}, u32[]{:S(2)}) copy-start(bf16[128,128]{1,0:T(8,128)(2,1)} %w_key.3) | copy-start | bytes 98308
  17.6 1.7 %copy-start.3 = (bf16[128,128]{1,0:T(8,128)(2,1)S(1)}, bf16[128,128]{1,0:T(8,128)(2,1)}, u32[]{:S(2)}) copy-start(bf16[128,128]{1,0:T(8,128)(2,1)} %w_value.3) | copy-start | bytes 98308
  17.6 1.7 %copy-start.4 = (bf16[128,128]{1,0:T(8,128)(2,1)S(1)}, bf16[128,128]{1,0:T(8,128)(2,1)}, u32[]{:S(2)}) copy-start(bf16[128,128]{1,0:T(8,128)(2,1)} %w_query.1) | copy-start | bytes 98308
  17.6 1.7 %copy-start.5 = (bf16[128,128]{1,0:T(8,128)(2,1)S(1)}, bf16[128,128]{1,0:T(8,128)(2,1)}, u32[]{:S(2)}) copy-start(bf16[128,128]{1,0:T(8,128)(2,1)} %w_gate.1) | copy-start | bytes 98308
  18.8 1.9 %collective-permute-start.6 = (bf16[576,128]{1,0:T(8,128)(2,1)S(1)}, bf16[576,128]{1,0:T(8,128)(2,1)S(1)}, u32[]{:S(2)}, u32[]{:S(2)}) collective-permute-start(bf16[576,128]{1,0:T(8,128)(2,1)S(1)} %shard_map.169.own_att_b), channel_id=1, source_target_pairs={{0,1},{1,0},{2,3},{3,2},{4,5},{5,4},{6,7},{7,6},{8,9},{9,8},{10,11... | collective-permute-start | bytes 442376 | tf_op jit(solution)/shard_map/ppermute | solution.py:511
  19.3 1.4 %copy-start.6 = (bf16[128,128]{1,0:T(8,128)(2,1)S(1)}, bf16[128,128]{1,0:T(8,128)(2,1)}, u32[]{:S(2)}) copy-start(bf16[128,128]{1,0:T(8,128)(2,1)} %w_out.5) | copy-start | bytes 98308

commit v15 on v14

--- a/solution.py
+++ b/solution.py
@@ -174,7 +174,7 @@
         axis=0,
     )
     joined = dot(normed, weights[:, : 2 * channels])
-    left = ((jnp.tanh(joined[:, channels:]) + 1.0) * joined[:, :channels] * masks).astype(bf16)
+    left = rounded((jnp.tanh(joined[:, channels:]) + 1.0) * joined[:, :channels] * masks)
     joined = dot(normed, weights[:, 2 * channels : 4 * channels])
     right = ((jnp.tanh(joined[:, channels:]) + 1.0) * joined[:, :channels] * masks).astype(bf16)
     gate = 0.5 * jnp.tanh(dot(normed, weights[:, 4 * channels :])) + 0.5
@@ -191,18 +191,12 @@
 def place_right(right_ref, chips, chip, r, edges):
     res = edges.shape[0]
     start = pl.multiple_of((r * chips + chip) * res, res)
-    right_ref[pl.ds(start, res), :] = edges
-
-
-def sum_sublanes(parts):
-    row = lax.broadcasted_iota(jnp.int32, parts[0].shape, 0)
-    for shift in (1, 2, 4):
-        high = jnp.bitwise_and(row, shift) > 0
-        parts = [
-            jnp.where(high, odd, even) + pltpu.roll(jnp.where(high, even, odd), shift, 0)
-            for even, odd in zip(parts[0::2], parts[1::2])
-        ]
-    return parts[0]
+    right_ref[pl.ds(start, res), :] = edges.astype(jnp.float32)
+
+
+def join(even, odd, shift):
+    high = jnp.bitwise_and(lax.broadcasted_iota(jnp.int32, even.shape, 0), shift) > 0
+    return jnp.where(high, odd, even) + pltpu.roll(jnp.where(high, even, odd), shift, 0)
 
 
 def triangle_rows(
@@ -214,19 +208,21 @@
     for n in range(0, count, block):
         lefts = [left_ref[pl.ds(start + m * res, res), :] for m in range(n, n + block)]
         for r in range(row_count):
-            parts = [[] for _ in range(block)]
+            sums = [[] for _ in range(block)]
             for chip in range(chips):
                 at = (r * chips + chip) * res
                 right = right_ref[at : at + res, :]
                 for m in range(block):
                     product = lefts[m] * right
-                    third = res // 3
-                    some = product[:third] + product[third : 2 * third] + product[2 * third :]
-                    some = some.astype(jnp.float32)
-                    parts[m].append(sum((some[k : k + 8] for k in range(8, third, 8)), some[:8]))
+                    part = sum((product[k : k + 8] for k in range(8, res, 8)), product[:8])
+                    shift = 1
+                    while chip & shift:
+                        part = join(sums[m].pop(), part, shift)
+                        shift *= 2
+                    sums[m].append(part)
             for m in range(block):
                 place = (triangle_first + n + m) * res + core * row_count + r
-                triangle_ref[pl.ds(place, chips, stride=2 * row_count), :] = sum_sublanes(parts[m])
+                triangle_ref[pl.ds(place, chips, stride=2 * row_count), :] = rounded(sums[m][0])
 
 
 def near_triangle_kernel(row_count, chips, chunk, left_ref, right_ref, triangle_ref):
@@ -541,7 +537,6 @@
         return tuple(s ^ bits for s in own_blocks)
 
     tall = shaped(f32, half * res, channels)
-    edge = shaped(bf16, half * res, channels)
 
     def edges_of(pieces, send_row, *held):
         pairs = tuple(p for p, _ in pieces)
@@ -551,7 +546,7 @@
         first = len(operands) - len(held)
         return call(
             functools.partial(edges_kernel, row_count, chips, blocks, send_row, not held),
-            (edge, edge, tall, tall, shaped(bf16, sent, res, channels))
+            (tall, tall, tall, tall, shaped(bf16, sent, res, channels))
             + (() if held else (shaped(bf16, 2 * channels, 2 * channels),)),
             operands,
             {first + e: e for e in range(len(held))},
@@ -583,7 +578,7 @@
     scratch = (pltpu.VMEM((part, channels), f32),)
     across, after_a, att_a = call(
         functools.partial(own_inputs_kernel, row_count, chips, (early[1], late[1])),
-        (edge, in_part, att_part),
+        (tall, in_part, att_part),
         shared + (early[0], late[0], triangle),
         scratch=scratch,
     )

time: 22.3 us -> 22 us (0.987)
  Pallas kernels: 7.99 us -> 7.76 us
    pallas_call x9, Pallas kernels: 7.99 us -> 7.76 us  [call(): pl.pallas_call(kernel, out_shape=outs, in_specs=[in_vmem] * len(operands)...]
  transfers between devices with their start and end apart: 8 -> 8, of which waited for: 4 -> 4; matrix products, arithmetic and copies ran while one was open for 6% -> 6% of each run, Pallas kernels for 25% -> 24%
where the time goes in v15:
time: 22 us; the launch traced here: 21.9 us
  starting transfers between devices  8.8 us (40%)
  Pallas kernels  7.76 us (35%)
  waiting for transfers between devices  2.61 us (12%)
  local copies, waits for them, and re-layouts  1.28 us (6%)
  other arithmetic  0.99 us (4%)
  between operations  0.22 us (1%)
    ppermute x8, starting transfers between devices, exchange(): return lax.ppermute(values, 'row', [(d, d ^ bit) for d in range(devices)])  8.8 us
    pallas_call x9, Pallas kernels, call(): pl.pallas_call(kernel, out_shape=outs, in_specs=[in_vmem] * len(operands)...  7.76 us
    ppermute x8, waiting for transfers between devices, exchange(): return lax.ppermute(values, 'row', [(d, d ^ bit) for d in range(devices)])  2.61 us
    unnamed x30, local copies, waits for them, and re-layouts  1.16 us
    mul x1, other arithmetic, on_whole_complex(): edge_weights = jnp.concatenate([w_edges, w_tri_gate], axis=1) * halves  0.97 us
  transfers between devices with their start and end apart: 8, of which 4 were waited for; matrix products, arithmetic and copies ran while one was open for 6% of the time, Pallas kernels for 24%

profile of v15, /device:TPU:0, one launch (start us, length us, event | category | flops | bytes accessed | tf_op | source)
XLA Modules:
  0.0 21.9 jit_solution(480712574163726572)
XLA Ops:
  0.0 4.0 %collective-permute-start = (bf16[3,48,128]{2,1,0:T(8,128)(2,1)}, bf16[3,48,128]{2,1,0:T(8,128)(2,1)S(1)}, u32[]{:S(2)}, u32[]{:S(2)}) collective-permute-start(bf16[3,48,128]{2,1,0:T(8,128)(2,1)} %param.17), channel_id=1, source_target_pairs={{0,8},{1,9},{2,10},{3,11},{4,12},{5,13},{6,14},{7,15},{8,0},{9,1},... | collective-permute-start | bytes 110600 | tf_op jit(solution)/shard_map/ppermute | solution.py:507
  4.1 1.0 %maximum_multiply_fusion.weights = bf16[128,640]{1,0:T(8,128)(2,1)S(1)} fusion(bf16[128,128]{1,0:T(8,128)(2,1)} %param.22, bf16[128,512]{1,0:T(8,128)(2,1)} %param.21, bf16[640]{0:T(1024)(128)(2,1)S(1)} %select_convert_fusion), kind=kLoop, calls=%fused_computation.2 | loop fusion | flops 491520 | bytes 328960 | tf_op jit(solution)/shard_map/mul | solution.py:520
  5.1 0.6 %copy-done.11 = f32[128]{0:T(128)S(1)} copy-done((f32[128]{0:T(128)S(1)}, f32[128]{0:T(128)}, u32[]{:S(2)}) %copy-start.11) | copy-done | bytes 536
  5.8 0.8 %collective-permute-done = bf16[3,48,128]{2,1,0:T(8,128)(2,1)S(1)} collective-permute-done((bf16[3,48,128]{2,1,0:T(8,128)(2,1)}, bf16[3,48,128]{2,1,0:T(8,128)(2,1)S(1)}, u32[]{:S(2)}, u32[]{:S(2)}) %collective-permute-start) | collective-permute-done | bytes 36896 | tf_op jit(solution)/shard_map/ppermute | solution.py:507
  6.6 2.5 %collective-permute-start.2 = (bf16[6,48,128]{2,1,0:T(8,128)(2,1)S(1)}, bf16[6,48,128]{2,1,0:T(8,128)(2,1)S(1)}, u32[]{:S(2)}, u32[]{:S(2)}) collective-permute-start(bf16[6,48,128]{2,1,0:T(8,128)(2,1)S(1)} %constant_dynamic-update-slice_fusion.refs_0_), channel_id=1, source_target_pairs={{0,6},{1,7},{2,4},{3,5},{4,2},{5,3},{6,0},{7,1},{8,14},{9,15},{10,... | collective-permute-start | bytes 221192 | tf_op jit(solution)/shard_map/ppermute | solution.py:507
  9.1 0.5 %collective-permute-start.1 = (bf16[6,48,128]{2,1,0:T(8,128)(2,1)S(1)}, bf16[6,48,128]{2,1,0:T(8,128)(2,1)S(1)}, u32[]{:S(2)}, u32[]{:S(2)}) collective-permute-start(bf16[6,48,128]{2,1,0:T(8,128)(2,1)S(1)} %constant_dynamic-update-slice_fusion.refs_0_), channel_id=1, source_target_pairs={{0,2},{1,3},{2,0},{3,1},{4,6},{5,7},{6,4},{7,5},{8,10},{9,11},{10,... | collective-permute-start | bytes 221192 | tf_op jit(solution)/shard_map/ppermute | solution.py:507
  9.6 0.5 %collective-permute-start.3 = (bf16[6,48,128]{2,1,0:T(8,128)(2,1)S(1)}, bf16[6,48,128]{2,1,0:T(8,128)(2,1)S(1)}, u32[]{:S(2)}, u32[]{:S(2)}) collective-permute-start(bf16[6,48,128]{2,1,0:T(8,128)(2,1)S(1)} %constant_dynamic-update-slice_fusion.refs_0_), channel_id=1, source_target_pairs={{0,4},{1,5},{2,6},{3,7},{4,0},{5,1},{6,2},{7,3},{8,12},{9,13},{10,... | collective-permute-start | bytes 221192 | tf_op jit(solution)/shard_map/ppermute | solution.py:507
  10.1 0.2 fusion.wide_bias
  10.4 0.4 %copy-done.14 = s32[48]{0:T(128)S(1)} copy-done((s32[48]{0:T(128)S(1)}, s32[48]{0:T(128)}, u32[]{:S(2)}) %copy-start.14) | copy-done | bytes 216
  10.9 0.4 %shard_map.163 = (f32[1152,128]{1,0:T(8,128)S(1)}, f32[1152,128]{1,0:T(8,128)S(1)}, f32[1152,128]{1,0:T(8,128)S(1)}, f32[1152,128]{1,0:T(8,128)S(1)}, bf16[18,48...) custom-call(f32[48,128]{1,0:T(8,128)S(1)} %broadcast_in_dim.23.valid_column, f32[6,128]{1,0:T(8,128)S(1)} %stack.27.norms, ...), custom_call_target="tpu_custom_call" | custom-call | flops 1048576 | bytes 33554432 | tf_op jit(solution)/shard_map/pallas_call | solution.py:495
  11.3 1.1 %collective-permute-done.2.refs_0_ = bf16[6,48,128]{2,1,0:T(8,128)(2,1)S(1)} collective-permute-done((bf16[6,48,128]{2,1,0:T(8,128)(2,1)S(1)}, bf16[6,48,128]{2,1,0:T(8,128)(2,1)S(1)}, u32[]{:S(2)}, u32[]{:S(2)}) %collective-permute-start.2) | collective-permute-done | bytes 73760 | tf_op jit(solution)/shard_map/ppermute | solution.py:507
  12.4 0.4 %shard_map.164 = (f32[1152,128]{1,0:T(8,128)S(1)}, f32[1152,128]{1,0:T(8,128)S(1)}, f32[1152,128]{1,0:T(8,128)S(1)}, f32[1152,128]{1,0:T(8,128)S(1)}, bf16[18,48,128]{2,1,0:T(8,128)(2,1)S(1)}) custom-call(f32[48,128]{1,0:T(8,128)S(1)} %broadcast_in_dim.23.valid_column, ...), custom_call_target="tpu_custom_call", output_to_operand_aliasing={{0}: (4, {}), {1}: (5, {}), {2}: (6, {}), {3}: (7, {}), {4}... | custom-call | flops 1048576 | bytes 33554432 | tf_op jit(solution)/shard_map/pallas_call | solution.py:495
  12.8 0.6 %collective-permute-done.1.refs_0_ = bf16[6,48,128]{2,1,0:T(8,128)(2,1)S(1)} collective-permute-done((bf16[6,48,128]{2,1,0:T(8,128)(2,1)S(1)}, bf16[6,48,128]{2,1,0:T(8,128)(2,1)S(1)}, u32[]{:S(2)}, u32[]{:S(2)}) %collective-permute-start.1) | collective-permute-done | bytes 73760 | tf_op jit(solution)/shard_map/ppermute | solution.py:507
  13.4 0.4 %shard_map.165 = (f32[1152,128]{1,0:T(8,128)S(1)}, f32[1152,128]{1,0:T(8,128)S(1)}, f32[1152,128]{1,0:T(8,128)S(1)}, f32[1152,128]{1,0:T(8,128)S(1)}, bf16[18,48,128]{2,1,0:T(8,128)(2,1)S(1)}) custom-call(f32[48,128]{1,0:T(8,128)S(1)} %broadcast_in_dim.23.valid_column, ...), custom_call_target="tpu_custom_call", output_to_operand_aliasing={{0}: (4, {}), {1}: (5, {}), {2}: (6, {}), {3}: (7, {}), {4}... | custom-call | flops 1048576 | bytes 33554432 | tf_op jit(solution)/shard_map/pallas_call | solution.py:495
  13.9 0.1 collective-permute-done.3.refs_0_
  14.0 0.4 %shard_map.166 = (f32[1152,128]{1,0:T(8,128)S(1)}, f32[1152,128]{1,0:T(8,128)S(1)}, f32[1152,128]{1,0:T(8,128)S(1)}, f32[1152,128]{1,0:T(8,128)S(1)}, bf16[6,48,128]{2,1,0:T(8,128)(2,1)S(1)}) custom-call(f32[48,128]{1,0:T(8,128)S(1)} %broadcast_in_dim.23.valid_column, ...), custom_call_target="tpu_custom_call", output_to_operand_aliasing={{0}: (4, {}), {1}: (5, {}), {2}: (6, {}), {3}: (7, {})} | custom-call | flops 1048576 | bytes 33554432 | tf_op jit(solution)/shard_map/pallas_call | solution.py:495
  14.4 0.6 %collective-permute-start.5 = (bf16[6,48,128]{2,1,0:T(8,128)(2,1)S(1)}, bf16[6,48,128]{2,1,0:T(8,128)(2,1)S(1)}, u32[]{:S(2)}, u32[]{:S(2)}) collective-permute-start(bf16[6,48,128]{2,1,0:T(8,128)(2,1)S(1)} %get-tuple-element.95), channel_id=1, source_target_pairs={{0,1},{1,0},{2,3},{3,2},{4,5},{5,4},{6,7},{7,6},{8,9},{9,8},{10,11... | collective-permute-start | bytes 221192 | tf_op jit(solution)/shard_map/ppermute | solution.py:507
  15.0 1.2 %shard_map.167.triangle_ref.refs_3_ = f32[1152,128]{1,0:T(8,128)S(1)} custom-call(f32[1152,128]{1,0:T(8,128)S(1)} %get-tuple-element.90.left_ref.refs_0_, f32[1152,128]{1,0:T(8,128)S(1)} %get-tuple-element.93.right_ref), custom_call_target="tpu_custom_call" | custom-call | flops 1048576 | bytes 33554432 | tf_op jit(solution)/shard_map/pallas_call | solution.py:495
  16.2 1.1 %shard_map.168 = (f32[1152,128]{1,0:T(8,128)S(1)}, f32[576,128]{1,0:T(8,128)S(1)}, bf16[576,128]{1,0:T(8,128)(2,1)S(1)}) custom-call(f32[6,128]{1,0:T(8,128)S(1)} %stack.27.norms, bf16[128,128]{1,0:T(8,128)(2,1)S(1)} %copy-done.1, f32[1152,128]{1,0:T(8,128)S(1)} %get-tuple-element.90.left_ref.refs_0_, f32[1152,128]{1,0:T(8,128)S(1)} %get-tuple-element.91.gate_ref.refs_1_, ...), custom_call_target="tpu_custom_call" | custom-call | flops 1048576 | bytes 33554432 | tf_op jit(solution)/shard_map/pallas_call | solution.py:495
  17.3 0.1 collective-permute-start.7
  17.5 1.1 %shard_map.169.own_att_b = bf16[576,128]{1,0:T(8,128)(2,1)S(1)} custom-call(f32[6,128]{1,0:T(8,128)S(1)} %stack.27.norms, bf16[128,128]{1,0:T(8,128)(2,1)S(1)} %copy-done.1, f32[1152,128]{1,0:T(8,128)S(1)} %get-tuple-element.90.left_ref.refs_0_, f32[1152,128]{1,0:T(8,128)S(1)} %get-tuple-element.91.gate_ref.refs_1_, ...), custom_call_target="tpu_custom_call" | custom-call | flops 1048576 | bytes 33554432 | tf_op jit(solution)/shard_map/pallas_call | solution.py:495
  18.6 0.5 %collective-permute-start.6 = (bf16[576,128]{1,0:T(8,128)(2,1)S(1)}, bf16[576,128]{1,0:T(8,128)(2,1)S(1)}, u32[]{:S(2)}, u32[]{:S(2)}) collective-permute-start(bf16[576,128]{1,0:T(8,128)(2,1)S(1)} %shard_map.169.own_att_b), channel_id=1, source_target_pairs={{0,1},{1,0},{2,3},{3,2},{4,5},{5,4},{6,7},{7,6},{8,9},{9,8},{10,11... | collective-permute-start | bytes 442376 | tf_op jit(solution)/shard_map/ppermute | solution.py:507
  19.1 1.3 %shard_map.170 = (f32[3,3,48,128]{3,2,1,0:T(8,128)S(1)}, f32[144,128]{1,0:T(8,128)S(1)}, f32[144,128]{1,0:T(8,128)S(1)}, f32[144,128]{1,0:T(8,128)S(1)}) custom-call(f32[48,128]{1,0:T(8,128)S(1)} %broadcast_in_dim.23.valid_column, bf16[256,256]{1,0:T(8,128)(2,1)S(1)} %get-tuple-element.58.same_head, bf16[128,128]{1,0:T(8,128)(2,1)S(1)} %copy-done.4, ...), custom_call_target="tpu_custom_call" | custom-call | flops 1048576 | bytes 33554432 | tf_op jit(solution)/shard_map/pallas_call | solution.py:495
  20.5 1.4 %shard_map.171 = bf16[3,48,128]{2,1,0:T(8,128)(2,1)} custom-call(f32[48,128]{1,0:T(8,128)S(1)} %broadcast_in_dim.23.valid_column, bf16[256,256]{1,0:T(8,128)(2,1)S(1)} %get-tuple-element.58.same_head, bf16[128,128]{1,0:T(8,128)(2,1)S(1)} %copy-done.2, bf16[128,128]{1,0:T(8,128)(2,1)S(1)} %copy-done.3, bf16[128,128]{1,0:T(8,128)(2,1)S(1)} %copy-done.6, ...), custom_call_target="tpu_custom_call" | custom-call | flops 1048576 | bytes 33554432 | tf_op jit(solution)/shard_map/pallas_call | solution.py:495
  (41 shorter events, 0.3 us)
Async XLA Ops:
  0.0 10.1 %copy-start = (bf16[128,4]{0,1:T(4,128)(2,1)S(1)}, bf16[128,4]{0,1:T(4,128)(2,1)}, u32[]{:S(2)}) copy-start(bf16[128,4]{0,1:T(4,128)(2,1)} %param.32) | copy-start | bytes 3076
  0.0 6.6 %collective-permute-start = (bf16[3,48,128]{2,1,0:T(8,128)(2,1)}, bf16[3,48,128]{2,1,0:T(8,128)(2,1)S(1)}, u32[]{:S(2)}, u32[]{:S(2)}) collective-permute-start(bf16[3,48,128]{2,1,0:T(8,128)(2,1)} %param.17), channel_id=1, source_target_pairs={{0,8},{1,9},{2,10},{3,11},{4,12},{5,13},{6,14},{7,15},{8,0},{9,1},... | collective-permute-start | bytes 110600 | tf_op jit(solution)/shard_map/ppermute | solution.py:507
  4.1 1.0 %copy-start.7 = (bf16[3,48,128]{2,1,0:T(8,128)(2,1)S(1)}, bf16[3,48,128]{2,1,0:T(8,128)(2,1)}, u32[]{:S(2)}) copy-start(bf16[3,48,128]{2,1,0:T(8,128)(2,1)} %param.17) | copy-start | bytes 110596
  5.1 0.7 %copy-start.11 = (f32[128]{0:T(128)S(1)}, f32[128]{0:T(128)}, u32[]{:S(2)}) copy-start(f32[128]{0:T(128)} %param.24) | copy-start | bytes 1540
  5.1 0.7 %copy-start.12 = (f32[128]{0:T(128)S(1)}, f32[128]{0:T(128)}, u32[]{:S(2)}) copy-start(f32[128]{0:T(128)} %param.26) | copy-start | bytes 1540
  5.1 0.7 %copy-start.13 = (f32[128]{0:T(128)S(1)}, f32[128]{0:T(128)}, u32[]{:S(2)}) copy-start(f32[128]{0:T(128)} %param.27) | copy-start | bytes 1540
  5.1 0.7 %copy-start.8 = (f32[128]{0:T(128)S(1)}, f32[128]{0:T(128)}, u32[]{:S(2)}) copy-start(f32[128]{0:T(128)} %param.19) | copy-start | bytes 1540
  5.1 0.7 %copy-start.9 = (f32[128]{0:T(128)S(1)}, f32[128]{0:T(128)}, u32[]{:S(2)}) copy-start(f32[128]{0:T(128)} %param.20) | copy-start | bytes 1540
  5.1 0.7 %copy-start.10 = (f32[128]{0:T(128)S(1)}, f32[128]{0:T(128)}, u32[]{:S(2)}) copy-start(f32[128]{0:T(128)} %param.23) | copy-start | bytes 1540
  6.6 5.8 %collective-permute-start.2 = (bf16[6,48,128]{2,1,0:T(8,128)(2,1)S(1)}, bf16[6,48,128]{2,1,0:T(8,128)(2,1)S(1)}, u32[]{:S(2)}, u32[]{:S(2)}) collective-permute-start(bf16[6,48,128]{2,1,0:T(8,128)(2,1)S(1)} %constant_dynamic-update-slice_fusion.refs_0_), channel_id=1, source_target_pairs={{0,6},{1,7},{2,4},{3,5},{4,2},{5,3},{6,0},{7,1},{8,14},{9,15},{10,... | collective-permute-start | bytes 221192 | tf_op jit(solution)/shard_map/ppermute | solution.py:507
  9.1 4.4 %collective-permute-start.1 = (bf16[6,48,128]{2,1,0:T(8,128)(2,1)S(1)}, bf16[6,48,128]{2,1,0:T(8,128)(2,1)S(1)}, u32[]{:S(2)}, u32[]{:S(2)}) collective-permute-start(bf16[6,48,128]{2,1,0:T(8,128)(2,1)S(1)} %constant_dynamic-update-slice_fusion.refs_0_), channel_id=1, source_target_pairs={{0,2},{1,3},{2,0},{3,1},{4,6},{5,7},{6,4},{7,5},{8,10},{9,11},{10,... | collective-permute-start | bytes 221192 | tf_op jit(solution)/shard_map/ppermute | solution.py:507
  9.6 4.4 %collective-permute-start.3 = (bf16[6,48,128]{2,1,0:T(8,128)(2,1)S(1)}, bf16[6,48,128]{2,1,0:T(8,128)(2,1)S(1)}, u32[]{:S(2)}, u32[]{:S(2)}) collective-permute-start(bf16[6,48,128]{2,1,0:T(8,128)(2,1)S(1)} %constant_dynamic-update-slice_fusion.refs_0_), channel_id=1, source_target_pairs={{0,4},{1,5},{2,6},{3,7},{4,0},{5,1},{6,2},{7,3},{8,12},{9,13},{10,... | collective-permute-start | bytes 221192 | tf_op jit(solution)/shard_map/ppermute | solution.py:507
  10.1 0.7 %copy-start.14 = (s32[48]{0:T(128)S(1)}, s32[48]{0:T(128)}, u32[]{:S(2)}) copy-start(s32[48]{0:T(128)} %param.18) | copy-start | bytes 580
  14.0 2.2 %collective-permute-start.4 = (bf16[18,48,128]{2,1,0:T(8,128)(2,1)S(1)}, bf16[18,48,128]{2,1,0:T(8,128)(2,1)S(1)}, u32[]{:S(2)}, u32[]{:S(2)}) collective-permute-start(bf16[18,48,128]{2,1,0:T(8,128)(2,1)S(1)} %get-tuple-element.94), channel_id=1, source_target_pairs={{0,1},{1,0},{2,3},{3,2},{4,5},{5,4},{6,7},{7,6},{8,9},{9,8},{10,11... | collective-permute-start | bytes 663560 | tf_op jit(solution)/shard_map/ppermute | solution.py:507
  14.4 1.8 %collective-permute-start.5 = (bf16[6,48,128]{2,1,0:T(8,128)(2,1)S(1)}, bf16[6,48,128]{2,1,0:T(8,128)(2,1)S(1)}, u32[]{:S(2)}, u32[]{:S(2)}) collective-permute-start(bf16[6,48,128]{2,1,0:T(8,128)(2,1)S(1)} %get-tuple-element.95), channel_id=1, source_target_pairs={{0,1},{1,0},{2,3},{3,2},{4,5},{5,4},{6,7},{7,6},{8,9},{9,8},{10,11... | collective-permute-start | bytes 221192 | tf_op jit(solution)/shard_map/ppermute | solution.py:507
  15.0 1.2 %copy-start.1 = (bf16[128,128]{1,0:T(8,128)(2,1)S(1)}, bf16[128,128]{1,0:T(8,128)(2,1)}, u32[]{:S(2)}) copy-start(bf16[128,128]{1,0:T(8,128)(2,1)} %w_out.4) | copy-start | bytes 98308
  17.3 1.8 %collective-permute-start.7 = (bf16[576,128]{1,0:T(8,128)(2,1)S(1)}, bf16[576,128]{1,0:T(8,128)(2,1)S(1)}, u32[]{:S(2)}, u32[]{:S(2)}) collective-permute-start(bf16[576,128]{1,0:T(8,128)(2,1)S(1)} %get-tuple-element.97.own_att_a), channel_id=1, source_target_pairs={{0,1},{1,0},{2,3},{3,2},{4,5},{5,4},{6,7},{7,6},{8,9},{9,8},{10,11... | collective-permute-start | bytes 442376 | tf_op jit(solution)/shard_map/ppermute | solution.py:507
  17.4 1.6 %copy-start.2 = (bf16[128,128]{1,0:T(8,128)(2,1)S(1)}, bf16[128,128]{1,0:T(8,128)(2,1)}, u32[]{:S(2)}) copy-start(bf16[128,128]{1,0:T(8,128)(2,1)} %w_key.3) | copy-start | bytes 98308
  17.4 1.6 %copy-start.3 = (bf16[128,128]{1,0:T(8,128)(2,1)S(1)}, bf16[128,128]{1,0:T(8,128)(2,1)}, u32[]{:S(2)}) copy-start(bf16[128,128]{1,0:T(8,128)(2,1)} %w_value.3) | copy-start | bytes 98308
  17.5 1.6 %copy-start.4 = (bf16[128,128]{1,0:T(8,128)(2,1)S(1)}, bf16[128,128]{1,0:T(8,128)(2,1)}, u32[]{:S(2)}) copy-start(bf16[128,128]{1,0:T(8,128)(2,1)} %w_query.1) | copy-start | bytes 98308
  17.5 1.6 %copy-start.5 = (bf16[128,128]{1,0:T(8,128)(2,1)S(1)}, bf16[128,128]{1,0:T(8,128)(2,1)}, u32[]{:S(2)}) copy-start(bf16[128,128]{1,0:T(8,128)(2,1)} %w_gate.1) | copy-start | bytes 98308
  18.6 1.9 %collective-permute-start.6 = (bf16[576,128]{1,0:T(8,128)(2,1)S(1)}, bf16[576,128]{1,0:T(8,128)(2,1)S(1)}, u32[]{:S(2)}, u32[]{:S(2)}) collective-permute-start(bf16[576,128]{1,0:T(8,128)(2,1)S(1)} %shard_map.169.own_att_b), channel_id=1, source_target_pairs={{0,1},{1,0},{2,3},{3,2},{4,5},{5,4},{6,7},{7,6},{8,9},{9,8},{10,11... | collective-permute-start | bytes 442376 | tf_op jit(solution)/shard_map/ppermute | solution.py:507
  19.1 1.4 %copy-start.6 = (bf16[128,128]{1,0:T(8,128)(2,1)S(1)}, bf16[128,128]{1,0:T(8,128)(2,1)}, u32[]{:S(2)}) copy-start(bf16[128,128]{1,0:T(8,128)(2,1)} %w_out.5) | copy-start | bytes 98308

commit v16 on v15

--- a/solution.py
+++ b/solution.py
@@ -225,7 +225,8 @@
                 triangle_ref[pl.ds(place, chips, stride=2 * row_count), :] = rounded(sums[m][0])
 
 
-def near_triangle_kernel(row_count, chips, chunk, left_ref, right_ref, triangle_ref):
+def near_triangle_kernel(row_count, chips, chunk, pieces, left_ref, right_ref, *refs):
+    received, (triangle_ref, across_ref) = refs[:-2], refs[-2:]
     _, core = chip_and_core()
 
     def some_rows(step, carry):
@@ -235,6 +236,9 @@
         )
         return carry
 
+    for ref, blocks in zip(received, pieces):
+        for n, (chip, r) in enumerate(rows_of_blocks(row_count, blocks)):
+            place_right(across_ref, chips, chip, r, ref[n])
     lax.fori_loop(0, row_count * chips // chunk, some_rows, 0)
 
 
@@ -271,17 +275,16 @@
     left_ref,
     gate_ref,
     pairs_ref,
-    early,
-    late,
+    received,
     triangle_ref,
+    held_across,
     across_ref,
     after_ref,
     att_ref,
     scratch_ref,
 ):
-    for received, senders in zip((early, late), blocks):
-        for n, (chip, r) in enumerate(rows_of_blocks(row_count, senders)):
-            place_right(across_ref, chips, chip, r, received[n])
+    for n, (chip, r) in enumerate(rows_of_blocks(row_count, blocks)):
+        place_right(across_ref, chips, chip, r, received[n])
     first = first_chip(chips, 0) * row_count
     refs = (left_ref, gate_ref, pairs_ref, triangle_ref, across_ref, scratch_ref)
     after_ref[...], att_ref[...] = attention_inputs(
@@ -315,10 +318,7 @@
     keys = start // res
     own = lax.axis_index("row") * row_count
     height = -(-keys // 8) * 8
-    columns = []
-    for r in range(row_count):
-        column = att_ref[pl.ds(own + r, keys, stride=res), :]
-        columns.append(jnp.concatenate([column, jnp.zeros((height - keys, column.shape[1]), jnp.float32)]))
+    columns = [att_ref[pl.ds(own + r, height, stride=res), :] for r in range(row_count)]
     columns = jnp.concatenate(columns, axis=0).astype(jnp.bfloat16)
     bias = rounded(dot(columns, wide_bias[...]))
     for r in range(row_count):
@@ -326,19 +326,25 @@
 
 
 def partial_attention(
-    row_count, chips, query, parts, bias_ref, same_head, valid_column, sums
+    row_count, chips, query, parts, bias_ref, same_head, valid_column, sums, together
 ):
     bf16 = jnp.bfloat16
     res = 2 * row_count * chips
     channels = valid_column.shape[1]
     count = row_count * chips // 2
     for part, (core, first, key_of, value_of) in enumerate(parts):
-        scores = []
+        products = []
         for r in range(row_count):
             own_query = query[r * res : (r + 1) * res]
-            products = [(key_of(n) * own_query).astype(bf16) for n in range(count)]
-            pairs = [jnp.concatenate(products[n : n + 2], axis=1) for n in range(0, count, 2)]
-            scores.append(dot(jnp.concatenate(pairs, axis=0), same_head[...]))
+            row = [(key_of(n) * own_query).astype(bf16) for n in range(count)]
+            pairs = [jnp.concatenate(row[n : n + 2], axis=1) for n in range(0, count, 2)]
+            products.append(jnp.concatenate(pairs, axis=0))
+        if together:
+            scores = dot(jnp.concatenate(products, axis=0), same_head[...])
+            tall = count // 2 * res
+            scores = [scores[r * tall : (r + 1) * tall] for r in range(row_count)]
+        else:
+            scores = [dot(product, same_head[...]) for product in products]
 
         def score_of(n, r):
             lanes = slice(n % 2 * channels, (n % 2 + 1) * channels)
@@ -412,7 +418,7 @@
     ]
     none = [(None, None, None)] * row_count
     sums = partial_attention(
-        row_count, chips, query, parts, bias_ref, same_head, valid_column, none
+        row_count, chips, query, parts, bias_ref, same_head, valid_column, none, True
     )
     for r in range(row_count):
         for n, each in enumerate(sums[r]):
@@ -454,7 +460,7 @@
     parts = ((1 - core, first_chip(chips, 1), rows_of(key_ref), rows_of(value_ref)),)
     sums = [tuple(sums_ref[r, n] for n in range(3)) for r in range(row_count)]
     sums = partial_attention(
-        row_count, chips, query_ref[...], parts, bias_ref, same_head, valid_column, sums
+        row_count, chips, query_ref[...], parts, bias_ref, same_head, valid_column, sums, False
     )
     attended = [mixed / total for _, total, mixed in sums]
     gated = (jnp.concatenate(attended, axis=0) * gate_ref[...]).astype(jnp.bfloat16)
@@ -541,12 +547,11 @@
     def edges_of(pieces, send_row, *held):
         pairs = tuple(p for p, _ in pieces)
         blocks = tuple(b for _, b in pieces)
-        sent = (2 if held and send_row == 0 else 6) * row_count
         operands = (valid_column, norms, edge_weights) + pairs + held
         first = len(operands) - len(held)
         return call(
             functools.partial(edges_kernel, row_count, chips, blocks, send_row, not held),
-            (tall, tall, tall, tall, shaped(bf16, sent, res, channels))
+            (tall, tall, tall, tall, shaped(bf16, 4 * row_count, res, channels))
             + (() if held else (shaped(bf16, 2 * channels, 2 * channels),)),
             operands,
             {first + e: e for e in range(len(held))},
@@ -560,16 +565,20 @@
     *edges, early_right = edges_of(
         [(diagonal, blocks_from(3))], 2 * row_count, *edges, early_right
     )
-    beside, edges, wide_bias = lax.optimization_barrier((beside, edges, wide_bias))
-    *edges, early_right = edges_of([(beside, blocks_from(1))], 4 * row_count, *edges, early_right)
-    near, edges, early_right = lax.optimization_barrier((near, edges, early_right))
-    early = (exchange(early_right, 1), own_blocks + blocks_from(3) + blocks_from(1))
-    *edges, late_right = edges_of([(near, blocks_from(2))], 0, *edges)
-    late = (exchange(late_right, 1), blocks_from(2))
+    beside, edges, early_right, wide_bias = lax.optimization_barrier(
+        (beside, edges, early_right, wide_bias)
+    )
+    early = (exchange(early_right, 1), own_blocks + blocks_from(3))
+    *edges, late_right = edges_of(
+        [(beside, blocks_from(1)), (near, blocks_from(2))], 0, *edges
+    )
+    late = (exchange(late_right, 1), blocks_from(1) + blocks_from(2))
 
     left, right, gate, pairs = edges
-    triangle = call(
-        functools.partial(near_triangle_kernel, row_count, chips, half // 2), tall, (left, right)
+    triangle, across = call(
+        functools.partial(near_triangle_kernel, row_count, chips, half // 2, [early[1]]),
+        (tall, tall),
+        (left, right, early[0]),
     )
     part = half // 2 * res
     in_part, own_shape = shaped(f32, part, channels), shaped(f32, row_count * res, channels)
@@ -577,9 +586,10 @@
     shared = (norms, w_tri_out, left, gate, pairs)
     scratch = (pltpu.VMEM((part, channels), f32),)
     across, after_a, att_a = call(
-        functools.partial(own_inputs_kernel, row_count, chips, (early[1], late[1])),
+        functools.partial(own_inputs_kernel, row_count, chips, late[1]),
         (tall, in_part, att_part),
-        shared + (early[0], late[0], triangle),
+        shared + (late[0], triangle, across),
+        {7: 0},
         scratch=scratch,
     )
     far_att_a = exchange(att_a, 1)
@@ -593,7 +603,7 @@
 
     def attention_scratch(keys, projected):
         return (
-            pltpu.VMEM((keys * res, channels), f32),
+            pltpu.VMEM((-(-keys // 8) * 8 * res, channels), f32),
             pltpu.VMEM((projected * res, channels), f32),
             pltpu.VMEM((projected * res, channels), f32),
             pltpu.VMEM((row_count, 40, channels), f32),

time: 22 us -> 21.8 us (level)
  waiting for transfers between devices: 2.61 us -> 3.19 us
  starting transfers between devices: 8.8 us -> 8.3 us
  Pallas kernels: 7.76 us -> 7.5 us
    ppermute x8, waiting for transfers between devices: 2.61 us -> 3.19 us  [exchange(): return lax.ppermute(values, 'row', [(d, d ^ bit) for d in range(devices)])]
    ppermute x8, starting transfers between devices: 8.8 us -> 8.3 us  [exchange(): return lax.ppermute(values, 'row', [(d, d ^ bit) for d in range(devices)])]
    pallas_call x9 -> x8, Pallas kernels: 7.76 us -> 7.5 us  [call(): pl.pallas_call(kernel, out_shape=outs, in_specs=[in_vmem] * len(operands)...]
  transfers between devices with their start and end apart: 8 -> 8, of which waited for: 4 -> 5; matrix products, arithmetic and copies ran while one was open for 6% -> 6% of each run, Pallas kernels for 24% -> 23%
where the time goes in v16:
time: 21.8 us; the launch traced here: 21.7 us
  starting transfers between devices  8.3 us (38%)
  Pallas kernels  7.5 us (34%)
  waiting for transfers between devices  3.19 us (15%)
  local copies, waits for them, and re-layouts  1.28 us (6%)
  other arithmetic  0.99 us (5%)
    ppermute x8, starting transfers between devices, exchange(): return lax.ppermute(values, 'row', [(d, d ^ bit) for d in range(devices)])  8.3 us
    pallas_call x8, Pallas kernels, call(): pl.pallas_call(kernel, out_shape=outs, in_specs=[in_vmem] * len(operands)...  7.5 us
    ppermute x8, waiting for transfers between devices, exchange(): return lax.ppermute(values, 'row', [(d, d ^ bit) for d in range(devices)])  3.19 us
    unnamed x30, local copies, waits for them, and re-layouts  1.16 us
    mul x1, other arithmetic, on_whole_complex(): edge_weights = jnp.concatenate([w_edges, w_tri_gate], axis=1) * halves  0.97 us
  transfers between devices with their start and end apart: 8, of which 5 were waited for; matrix products, arithmetic and copies ran while one was open for 6% of the time, Pallas kernels for 23%

profile of v16, /device:TPU:0, one launch (start us, length us, event | category | flops | bytes accessed | tf_op | source)
XLA Modules:
  0.0 21.7 jit_solution(5485699425831165873)
XLA Ops:
  0.0 4.0 %collective-permute-start = (bf16[3,48,128]{2,1,0:T(8,128)(2,1)}, bf16[3,48,128]{2,1,0:T(8,128)(2,1)S(1)}, u32[]{:S(2)}, u32[]{:S(2)}) collective-permute-start(bf16[3,48,128]{2,1,0:T(8,128)(2,1)} %param.17), channel_id=1, source_target_pairs={{0,8},{1,9},{2,10},{3,11},{4,12},{5,13},{6,14},{7,15},{8,0},{9,1},... | collective-permute-start | bytes 110600 | tf_op jit(solution)/shard_map/ppermute | solution.py:513
  4.1 1.0 %maximum_multiply_fusion.weights = bf16[128,640]{1,0:T(8,128)(2,1)S(1)} fusion(bf16[128,128]{1,0:T(8,128)(2,1)} %param.22, bf16[128,512]{1,0:T(8,128)(2,1)} %param.21, bf16[640]{0:T(1024)(128)(2,1)S(1)} %select_convert_fusion), kind=kLoop, calls=%fused_computation.2 | loop fusion | flops 491520 | bytes 328960 | tf_op jit(solution)/shard_map/mul | solution.py:526
  5.1 0.6 %copy-done.11 = f32[128]{0:T(128)S(1)} copy-done((f32[128]{0:T(128)S(1)}, f32[128]{0:T(128)}, u32[]{:S(2)}) %copy-start.11) | copy-done | bytes 536
  5.8 0.8 %collective-permute-done = bf16[3,48,128]{2,1,0:T(8,128)(2,1)S(1)} collective-permute-done((bf16[3,48,128]{2,1,0:T(8,128)(2,1)}, bf16[3,48,128]{2,1,0:T(8,128)(2,1)S(1)}, u32[]{:S(2)}, u32[]{:S(2)}) %collective-permute-start) | collective-permute-done | bytes 36896 | tf_op jit(solution)/shard_map/ppermute | solution.py:513
  6.6 2.5 %collective-permute-start.2 = (bf16[6,48,128]{2,1,0:T(8,128)(2,1)S(1)}, bf16[6,48,128]{2,1,0:T(8,128)(2,1)S(1)}, u32[]{:S(2)}, u32[]{:S(2)}) collective-permute-start(bf16[6,48,128]{2,1,0:T(8,128)(2,1)S(1)} %constant_dynamic-update-slice_fusion.refs_0_), channel_id=1, source_target_pairs={{0,6},{1,7},{2,4},{3,5},{4,2},{5,3},{6,0},{7,1},{8,14},{9,15},{10,... | collective-permute-start | bytes 221192 | tf_op jit(solution)/shard_map/ppermute | solution.py:513
  9.1 0.5 %collective-permute-start.1 = (bf16[6,48,128]{2,1,0:T(8,128)(2,1)S(1)}, bf16[6,48,128]{2,1,0:T(8,128)(2,1)S(1)}, u32[]{:S(2)}, u32[]{:S(2)}) collective-permute-start(bf16[6,48,128]{2,1,0:T(8,128)(2,1)S(1)} %constant_dynamic-update-slice_fusion.refs_0_), channel_id=1, source_target_pairs={{0,2},{1,3},{2,0},{3,1},{4,6},{5,7},{6,4},{7,5},{8,10},{9,11},{10,... | collective-permute-start | bytes 221192 | tf_op jit(solution)/shard_map/ppermute | solution.py:513
  9.6 0.5 %collective-permute-start.3 = (bf16[6,48,128]{2,1,0:T(8,128)(2,1)S(1)}, bf16[6,48,128]{2,1,0:T(8,128)(2,1)S(1)}, u32[]{:S(2)}, u32[]{:S(2)}) collective-permute-start(bf16[6,48,128]{2,1,0:T(8,128)(2,1)S(1)} %constant_dynamic-update-slice_fusion.refs_0_), channel_id=1, source_target_pairs={{0,4},{1,5},{2,6},{3,7},{4,0},{5,1},{6,2},{7,3},{8,12},{9,13},{10,... | collective-permute-start | bytes 221192 | tf_op jit(solution)/shard_map/ppermute | solution.py:513
  10.1 0.2 fusion.wide_bias
  10.4 0.4 %copy-done.14 = s32[48]{0:T(128)S(1)} copy-done((s32[48]{0:T(128)S(1)}, s32[48]{0:T(128)}, u32[]{:S(2)}) %copy-start.14) | copy-done | bytes 216
  10.8 0.1 broadcast_in_dim.23.valid_column
  10.9 0.4 %shard_map.163 = (f32[1152,128]{1,0:T(8,128)S(1)}, f32[1152,128]{1,0:T(8,128)S(1)}, f32[1152,128]{1,0:T(8,128)S(1)}, f32[1152,128]{1,0:T(8,128)S(1)}, bf16[12,48...) custom-call(f32[48,128]{1,0:T(8,128)S(1)} %broadcast_in_dim.23.valid_column, f32[6,128]{1,0:T(8,128)S(1)} %stack.27.norms, ...), custom_call_target="tpu_custom_call" | custom-call | flops 1048576 | bytes 33554432 | tf_op jit(solution)/shard_map/pallas_call | solution.py:501
  11.3 1.1 %collective-permute-done.2.refs_0_ = bf16[6,48,128]{2,1,0:T(8,128)(2,1)S(1)} collective-permute-done((bf16[6,48,128]{2,1,0:T(8,128)(2,1)S(1)}, bf16[6,48,128]{2,1,0:T(8,128)(2,1)S(1)}, u32[]{:S(2)}, u32[]{:S(2)}) %collective-permute-start.2) | collective-permute-done | bytes 73760 | tf_op jit(solution)/shard_map/ppermute | solution.py:513
  12.4 0.4 %shard_map.164 = (f32[1152,128]{1,0:T(8,128)S(1)}, f32[1152,128]{1,0:T(8,128)S(1)}, f32[1152,128]{1,0:T(8,128)S(1)}, f32[1152,128]{1,0:T(8,128)S(1)}, bf16[12,48,128]{2,1,0:T(8,128)(2,1)S(1)}) custom-call(f32[48,128]{1,0:T(8,128)S(1)} %broadcast_in_dim.23.valid_column, ...), custom_call_target="tpu_custom_call", output_to_operand_aliasing={{0}: (4, {}), {1}: (5, {}), {2}: (6, {}), {3}: (7, {}), {4}... | custom-call | flops 1048576 | bytes 33554432 | tf_op jit(solution)/shard_map/pallas_call | solution.py:501
  12.8 0.6 %collective-permute-done.1.refs_0_ = bf16[6,48,128]{2,1,0:T(8,128)(2,1)S(1)} collective-permute-done((bf16[6,48,128]{2,1,0:T(8,128)(2,1)S(1)}, bf16[6,48,128]{2,1,0:T(8,128)(2,1)S(1)}, u32[]{:S(2)}, u32[]{:S(2)}) %collective-permute-start.1) | collective-permute-done | bytes 73760 | tf_op jit(solution)/shard_map/ppermute | solution.py:513
  13.4 0.5 %collective-permute-done.3.refs_1_ = bf16[6,48,128]{2,1,0:T(8,128)(2,1)S(1)} collective-permute-done((bf16[6,48,128]{2,1,0:T(8,128)(2,1)S(1)}, bf16[6,48,128]{2,1,0:T(8,128)(2,1)S(1)}, u32[]{:S(2)}, u32[]{:S(2)}) %collective-permute-start.3) | collective-permute-done | bytes 73760 | tf_op jit(solution)/shard_map/ppermute | solution.py:513
  14.0 0.6 %shard_map.165 = (f32[1152,128]{1,0:T(8,128)S(1)}, f32[1152,128]{1,0:T(8,128)S(1)}, f32[1152,128]{1,0:T(8,128)S(1)}, f32[1152,128]{1,0:T(8,128)S(1)}, bf16[12,48,128]{2,1,0:T(8,128)(2,1)S(1)}) custom-call(f32[48,128]{1,0:T(8,128)S(1)} %broadcast_in_dim.23.valid_column, ...), custom_call_target="tpu_custom_call", output_to_operand_aliasing={{0}: (5, {}), {1}: (6, {}), {2}: (7, {}), {3}: (8, {})} | custom-call | flops 1048576 | bytes 33554432 | tf_op jit(solution)/shard_map/pallas_call | solution.py:501
  14.7 0.1 collective-permute-done.4.refs_0_
  14.8 1.2 %shard_map.166 = (f32[1152,128]{1,0:T(8,128)S(1)}, f32[1152,128]{1,0:T(8,128)S(1)}) custom-call(f32[1152,128]{1,0:T(8,128)S(1)} %get-tuple-element.72.left_ref.refs_0_, f32[1152,128]{1,0:T(8,128)S(1)} %get-tuple-element.75.right_ref, bf16[12,48,128]{2,1,0:T(8,128)(2,1)S(1)} %collective-permute-done.4.refs_0_), custom_call_target="tpu_custom_call" | custom-call | flops 1048576 | bytes 33554432 | tf_op jit(solution)/shard_map/pallas_call | solution.py:501
  16.0 1.1 %shard_map.167 = (f32[1152,128]{1,0:T(8,128)S(1)}, f32[576,128]{1,0:T(8,128)S(1)}, bf16[576,128]{1,0:T(8,128)(2,1)S(1)}) custom-call(f32[6,128]{1,0:T(8,128)S(1)} %stack.27.norms, bf16[128,128]{1,0:T(8,128)(2,1)S(1)} %copy-done.1, f32[1152,128]{1,0:T(8,128)S(1)} %get-tuple-element.72.left_ref.refs_0_, ...), custom_call_target="tpu_custom_call", output_to_operand_aliasing={{0}: (7, {})} | custom-call | flops 1048576 | bytes 33554432 | tf_op jit(solution)/shard_map/pallas_call | solution.py:501
  17.1 0.4 %collective-permute-start.7 = (bf16[576,128]{1,0:T(8,128)(2,1)S(1)}, bf16[576,128]{1,0:T(8,128)(2,1)S(1)}, u32[]{:S(2)}, u32[]{:S(2)}) collective-permute-start(bf16[576,128]{1,0:T(8,128)(2,1)S(1)} %get-tuple-element.81.own_att_a), channel_id=1, source_target_pairs={{0,1},{1,0},{2,3},{3,2},{4,5},{5,4},{6,7},{7,6},{8,9},{9,8},{10,11... | collective-permute-start | bytes 442376 | tf_op jit(solution)/shard_map/ppermute | solution.py:513
  17.6 1.1 %shard_map.168.own_att_b = bf16[576,128]{1,0:T(8,128)(2,1)S(1)} custom-call(f32[6,128]{1,0:T(8,128)S(1)} %stack.27.norms, bf16[128,128]{1,0:T(8,128)(2,1)S(1)} %copy-done.1, f32[1152,128]{1,0:T(8,128)S(1)} %get-tuple-element.72.left_ref.refs_0_, f32[1152,128]{1,0:T(8,128)S(1)} %get-tuple-element.73.gate_ref.refs_1_, ...), custom_call_target="tpu_custom_call" | custom-call | flops 1048576 | bytes 33554432 | tf_op jit(solution)/shard_map/pallas_call | solution.py:501
  18.7 0.2 %collective-permute-start.6 = (bf16[576,128]{1,0:T(8,128)(2,1)S(1)}, bf16[576,128]{1,0:T(8,128)(2,1)S(1)}, u32[]{:S(2)}, u32[]{:S(2)}) collective-permute-start(bf16[576,128]{1,0:T(8,128)(2,1)S(1)} %shard_map.168.own_att_b), channel_id=1, source_target_pairs={{0,1},{1,0},{2,3},{3,2},{4,5},{5,4},{6,7},{7,6},{8,9},{9,8},{10,11... | collective-permute-start | bytes 442376 | tf_op jit(solution)/shard_map/ppermute | solution.py:513
  18.9 1.3 %shard_map.169 = (f32[3,3,48,128]{3,2,1,0:T(8,128)S(1)}, f32[144,128]{1,0:T(8,128)S(1)}, f32[144,128]{1,0:T(8,128)S(1)}, f32[144,128]{1,0:T(8,128)S(1)}) custom-call(f32[48,128]{1,0:T(8,128)S(1)} %broadcast_in_dim.23.valid_column, bf16[256,256]{1,0:T(8,128)(2,1)S(1)} %get-tuple-element.50.same_head, bf16[128,128]{1,0:T(8,128)(2,1)S(1)} %copy-done.4, ...), custom_call_target="tpu_custom_call" | custom-call | flops 1048576 | bytes 33554432 | tf_op jit(solution)/shard_map/pallas_call | solution.py:501
  20.3 1.4 %shard_map.170 = bf16[3,48,128]{2,1,0:T(8,128)(2,1)} custom-call(f32[48,128]{1,0:T(8,128)S(1)} %broadcast_in_dim.23.valid_column, bf16[256,256]{1,0:T(8,128)(2,1)S(1)} %get-tuple-element.50.same_head, bf16[128,128]{1,0:T(8,128)(2,1)S(1)} %copy-done.2, bf16[128,128]{1,0:T(8,128)(2,1)S(1)} %copy-done.3, bf16[128,128]{1,0:T(8,128)(2,1)S(1)} %copy-done.6, ...), custom_call_target="tpu_custom_call" | custom-call | flops 1048576 | bytes 33554432 | tf_op jit(solution)/shard_map/pallas_call | solution.py:501
  (40 shorter events, 0.3 us)
Async XLA Ops:
  0.0 10.1 %copy-start = (bf16[128,4]{0,1:T(4,128)(2,1)S(1)}, bf16[128,4]{0,1:T(4,128)(2,1)}, u32[]{:S(2)}) copy-start(bf16[128,4]{0,1:T(4,128)(2,1)} %param.32) | copy-start | bytes 3076
  0.0 6.6 %collective-permute-start = (bf16[3,48,128]{2,1,0:T(8,128)(2,1)}, bf16[3,48,128]{2,1,0:T(8,128)(2,1)S(1)}, u32[]{:S(2)}, u32[]{:S(2)}) collective-permute-start(bf16[3,48,128]{2,1,0:T(8,128)(2,1)} %param.17), channel_id=1, source_target_pairs={{0,8},{1,9},{2,10},{3,11},{4,12},{5,13},{6,14},{7,15},{8,0},{9,1},... | collective-permute-start | bytes 110600 | tf_op jit(solution)/shard_map/ppermute | solution.py:513
  4.1 1.0 %copy-start.7 = (bf16[3,48,128]{2,1,0:T(8,128)(2,1)S(1)}, bf16[3,48,128]{2,1,0:T(8,128)(2,1)}, u32[]{:S(2)}) copy-start(bf16[3,48,128]{2,1,0:T(8,128)(2,1)} %param.17) | copy-start | bytes 110596
  5.1 0.7 %copy-start.11 = (f32[128]{0:T(128)S(1)}, f32[128]{0:T(128)}, u32[]{:S(2)}) copy-start(f32[128]{0:T(128)} %param.24) | copy-start | bytes 1540
  5.1 0.7 %copy-start.12 = (f32[128]{0:T(128)S(1)}, f32[128]{0:T(128)}, u32[]{:S(2)}) copy-start(f32[128]{0:T(128)} %param.26) | copy-start | bytes 1540
  5.1 0.7 %copy-start.13 = (f32[128]{0:T(128)S(1)}, f32[128]{0:T(128)}, u32[]{:S(2)}) copy-start(f32[128]{0:T(128)} %param.27) | copy-start | bytes 1540
  5.1 0.7 %copy-start.8 = (f32[128]{0:T(128)S(1)}, f32[128]{0:T(128)}, u32[]{:S(2)}) copy-start(f32[128]{0:T(128)} %param.19) | copy-start | bytes 1540
  5.1 0.7 %copy-start.9 = (f32[128]{0:T(128)S(1)}, f32[128]{0:T(128)}, u32[]{:S(2)}) copy-start(f32[128]{0:T(128)} %param.20) | copy-start | bytes 1540
  5.1 0.7 %copy-start.10 = (f32[128]{0:T(128)S(1)}, f32[128]{0:T(128)}, u32[]{:S(2)}) copy-start(f32[128]{0:T(128)} %param.23) | copy-start | bytes 1540
  6.6 5.8 %collective-permute-start.2 = (bf16[6,48,128]{2,1,0:T(8,128)(2,1)S(1)}, bf16[6,48,128]{2,1,0:T(8,128)(2,1)S(1)}, u32[]{:S(2)}, u32[]{:S(2)}) collective-permute-start(bf16[6,48,128]{2,1,0:T(8,128)(2,1)S(1)} %constant_dynamic-update-slice_fusion.refs_0_), channel_id=1, source_target_pairs={{0,6},{1,7},{2,4},{3,5},{4,2},{5,3},{6,0},{7,1},{8,14},{9,15},{10,... | collective-permute-start | bytes 221192 | tf_op jit(solution)/shard_map/ppermute | solution.py:513
  9.1 4.4 %collective-permute-start.1 = (bf16[6,48,128]{2,1,0:T(8,128)(2,1)S(1)}, bf16[6,48,128]{2,1,0:T(8,128)(2,1)S(1)}, u32[]{:S(2)}, u32[]{:S(2)}) collective-permute-start(bf16[6,48,128]{2,1,0:T(8,128)(2,1)S(1)} %constant_dynamic-update-slice_fusion.refs_0_), channel_id=1, source_target_pairs={{0,2},{1,3},{2,0},{3,1},{4,6},{5,7},{6,4},{7,5},{8,10},{9,11},{10,... | collective-permute-start | bytes 221192 | tf_op jit(solution)/shard_map/ppermute | solution.py:513
  9.6 4.4 %collective-permute-start.3 = (bf16[6,48,128]{2,1,0:T(8,128)(2,1)S(1)}, bf16[6,48,128]{2,1,0:T(8,128)(2,1)S(1)}, u32[]{:S(2)}, u32[]{:S(2)}) collective-permute-start(bf16[6,48,128]{2,1,0:T(8,128)(2,1)S(1)} %constant_dynamic-update-slice_fusion.refs_0_), channel_id=1, source_target_pairs={{0,4},{1,5},{2,6},{3,7},{4,0},{5,1},{6,2},{7,3},{8,12},{9,13},{10,... | collective-permute-start | bytes 221192 | tf_op jit(solution)/shard_map/ppermute | solution.py:513
  10.1 0.7 %copy-start.14 = (s32[48]{0:T(128)S(1)}, s32[48]{0:T(128)}, u32[]{:S(2)}) copy-start(s32[48]{0:T(128)} %param.18) | copy-start | bytes 580
  13.4 1.4 %collective-permute-start.4 = (bf16[12,48,128]{2,1,0:T(8,128)(2,1)S(1)}, bf16[12,48,128]{2,1,0:T(8,128)(2,1)S(1)}, u32[]{:S(2)}, u32[]{:S(2)}) collective-permute-start(bf16[12,48,128]{2,1,0:T(8,128)(2,1)S(1)} %get-tuple-element.76), channel_id=1, source_target_pairs={{0,1},{1,0},{2,3},{3,2},{4,5},{5,4},{6,7},{7,6},{8,9},{9,8},{10,11... | collective-permute-start | bytes 442376 | tf_op jit(solution)/shard_map/ppermute | solution.py:513
  14.6 1.4 %collective-permute-start.5 = (bf16[12,48,128]{2,1,0:T(8,128)(2,1)S(1)}, bf16[12,48,128]{2,1,0:T(8,128)(2,1)S(1)}, u32[]{:S(2)}, u32[]{:S(2)}) collective-permute-start(bf16[12,48,128]{2,1,0:T(8,128)(2,1)S(1)} %get-tuple-element.78), channel_id=1, source_target_pairs={{0,1},{1,0},{2,3},{3,2},{4,5},{5,4},{6,7},{7,6},{8,9},{9,8},{10,11... | collective-permute-start | bytes 442376 | tf_op jit(solution)/shard_map/ppermute | solution.py:513
  14.8 1.2 %copy-start.1 = (bf16[128,128]{1,0:T(8,128)(2,1)S(1)}, bf16[128,128]{1,0:T(8,128)(2,1)}, u32[]{:S(2)}) copy-start(bf16[128,128]{1,0:T(8,128)(2,1)} %w_out.4) | copy-start | bytes 98308
  17.1 1.8 %collective-permute-start.7 = (bf16[576,128]{1,0:T(8,128)(2,1)S(1)}, bf16[576,128]{1,0:T(8,128)(2,1)S(1)}, u32[]{:S(2)}, u32[]{:S(2)}) collective-permute-start(bf16[576,128]{1,0:T(8,128)(2,1)S(1)} %get-tuple-element.81.own_att_a), channel_id=1, source_target_pairs={{0,1},{1,0},{2,3},{3,2},{4,5},{5,4},{6,7},{7,6},{8,9},{9,8},{10,11... | collective-permute-start | bytes 442376 | tf_op jit(solution)/shard_map/ppermute | solution.py:513
  17.6 1.3 %copy-start.2 = (bf16[128,128]{1,0:T(8,128)(2,1)S(1)}, bf16[128,128]{1,0:T(8,128)(2,1)}, u32[]{:S(2)}) copy-start(bf16[128,128]{1,0:T(8,128)(2,1)} %w_key.3) | copy-start | bytes 98308
  17.6 1.3 %copy-start.3 = (bf16[128,128]{1,0:T(8,128)(2,1)S(1)}, bf16[128,128]{1,0:T(8,128)(2,1)}, u32[]{:S(2)}) copy-start(bf16[128,128]{1,0:T(8,128)(2,1)} %w_value.3) | copy-start | bytes 98308
  17.6 1.3 %copy-start.4 = (bf16[128,128]{1,0:T(8,128)(2,1)S(1)}, bf16[128,128]{1,0:T(8,128)(2,1)}, u32[]{:S(2)}) copy-start(bf16[128,128]{1,0:T(8,128)(2,1)} %w_query.1) | copy-start | bytes 98308
  17.6 1.4 %copy-start.5 = (bf16[128,128]{1,0:T(8,128)(2,1)S(1)}, bf16[128,128]{1,0:T(8,128)(2,1)}, u32[]{:S(2)}) copy-start(bf16[128,128]{1,0:T(8,128)(2,1)} %w_gate.1) | copy-start | bytes 98308
  18.7 1.6 %collective-permute-start.6 = (bf16[576,128]{1,0:T(8,128)(2,1)S(1)}, bf16[576,128]{1,0:T(8,128)(2,1)S(1)}, u32[]{:S(2)}, u32[]{:S(2)}) collective-permute-start(bf16[576,128]{1,0:T(8,128)(2,1)S(1)} %shard_map.168.own_att_b), channel_id=1, source_target_pairs={{0,1},{1,0},{2,3},{3,2},{4,5},{5,4},{6,7},{7,6},{8,9},{9,8},{10,11... | collective-permute-start | bytes 442376 | tf_op jit(solution)/shard_map/ppermute | solution.py:513
  18.9 1.3 %copy-start.6 = (bf16[128,128]{1,0:T(8,128)(2,1)S(1)}, bf16[128,128]{1,0:T(8,128)(2,1)}, u32[]{:S(2)}) copy-start(bf16[128,128]{1,0:T(8,128)(2,1)} %w_out.5) | copy-start | bytes 98308

commit v17 on v16

--- a/solution.py
+++ b/solution.py
@@ -243,22 +243,49 @@
 
 
 def attention_inputs(
-    row_count, chips, first, norms, w_out, left_ref, gate_ref, pairs_ref, held_triangle, across_ref,
-    triangle_ref,
+    row_count,
+    chips,
+    first,
+    norms,
+    w_out,
+    left_ref,
+    gate_ref,
+    pairs_ref,
+    held_triangle,
+    across_ref,
+    after_ref,
+    att_ref,
+    scratch_refs,
 ):
     bf16 = jnp.bfloat16
     _, core = chip_and_core()
     half = row_count * chips
-    tall = (half // 2) * 2 * half
-    rows = pl.ds(pl.multiple_of(first * 2 * half, tall), tall)
-    triangle_ref[...] = held_triangle[rows, :]
-    triangle_rows(
-        row_count, chips, left_ref, across_ref, triangle_ref, first, half // 2, 1 - core, 0
-    )
-    tri_normed = row_norm(triangle_ref[...], norms[2:3, :], norms[3:4, :]).astype(bf16)
-    after_tri = pairs_ref[rows, :] + gate_ref[rows, :] * dot(tri_normed, w_out[...])
-    att_in = row_norm(after_tri, norms[4:5, :], norms[5:6, :]).astype(bf16)
-    return after_tri, att_in
+    res = 2 * half
+    count = half // 2 // len(scratch_refs)
+    tall = count * res
+
+    def rest_of_triangle(n):
+        start = first + n * count
+        rows = pl.ds(pl.multiple_of(start * res, tall), tall)
+        scratch_refs[n][...] = held_triangle[rows, :]
+        triangle_rows(
+            row_count, chips, left_ref, across_ref, scratch_refs[n], start, count, 1 - core, 0
+        )
+
+    def inputs_of(n):
+        rows = pl.ds(pl.multiple_of((first + n * count) * res, tall), tall)
+        tri_normed = row_norm(scratch_refs[n][...], norms[2:3, :], norms[3:4, :]).astype(bf16)
+        after_tri = pairs_ref[rows, :] + gate_ref[rows, :] * dot(tri_normed, w_out[...])
+        att_in = row_norm(after_tri, norms[4:5, :], norms[5:6, :]).astype(bf16)
+        if after_ref is not None:
+            after_ref[n * tall : (n + 1) * tall, :] = after_tri
+        att_ref[n * tall : (n + 1) * tall, :] = att_in
+
+    rest_of_triangle(0)
+    for n in range(1, len(scratch_refs)):
+        rest_of_triangle(n)
+        inputs_of(n - 1)
+    inputs_of(len(scratch_refs) - 1)
 
 
 def first_chip(chips, part):
@@ -281,21 +308,19 @@
     across_ref,
     after_ref,
     att_ref,
-    scratch_ref,
+    *scratch_refs,
 ):
     for n, (chip, r) in enumerate(rows_of_blocks(row_count, blocks)):
         place_right(across_ref, chips, chip, r, received[n])
     first = first_chip(chips, 0) * row_count
-    refs = (left_ref, gate_ref, pairs_ref, triangle_ref, across_ref, scratch_ref)
-    after_ref[...], att_ref[...] = attention_inputs(
-        row_count, chips, first, norms, w_out, *refs
-    )
+    refs = (left_ref, gate_ref, pairs_ref, triangle_ref, across_ref, after_ref, att_ref)
+    attention_inputs(row_count, chips, first, norms, w_out, *refs, scratch_refs)
 
 
 def other_inputs_kernel(row_count, chips, norms, w_out, *refs):
-    *refs, att_ref, scratch_ref = refs
+    refs, att_ref, scratch_refs = refs[:5], refs[5], refs[6:]
     first = first_chip(chips, 1) * row_count
-    _, att_ref[...] = attention_inputs(row_count, chips, first, norms, w_out, *refs, scratch_ref)
+    attention_inputs(row_count, chips, first, norms, w_out, *refs, None, att_ref, scratch_refs)
 
 
 def keys_and_values(att, w_key, w_value, key_ref, value_ref):
@@ -584,7 +609,7 @@
     in_part, own_shape = shaped(f32, part, channels), shaped(f32, row_count * res, channels)
     att_part = shaped(bf16, part, channels)
     shared = (norms, w_tri_out, left, gate, pairs)
-    scratch = (pltpu.VMEM((part, channels), f32),)
+    scratch = (pltpu.VMEM((part // 3, channels), f32),) * 3
     across, after_a, att_a = call(
         functools.partial(own_inputs_kernel, row_count, chips, late[1]),
         (tall, in_part, att_part),

time: 21.8 us -> 21.8 us (level)
  no operation moved by 1% of the time
where the time goes in v17:
time: 21.8 us; the launch traced here: 21.7 us
  starting transfers between devices  8.3 us (38%)
  Pallas kernels  7.51 us (34%)
  waiting for transfers between devices  3.19 us (15%)
  local copies, waits for them, and re-layouts  1.28 us (6%)
  other arithmetic  0.99 us (5%)
    ppermute x8, starting transfers between devices, exchange(): return lax.ppermute(values, 'row', [(d, d ^ bit) for d in range(devices)])  8.3 us
    pallas_call x8, Pallas kernels, call(): pl.pallas_call(kernel, out_shape=outs, in_specs=[in_vmem] * len(operands)...  7.51 us
    ppermute x8, waiting for transfers between devices, exchange(): return lax.ppermute(values, 'row', [(d, d ^ bit) for d in range(devices)])  3.19 us
    unnamed x30, local copies, waits for them, and re-layouts  1.16 us
    mul x1, other arithmetic, on_whole_complex(): edge_weights = jnp.concatenate([w_edges, w_tri_gate], axis=1) * halves  0.97 us
  transfers between devices with their start and end apart: 8, of which 5 were waited for; matrix products, arithmetic and copies ran while one was open for 6% of the time, Pallas kernels for 23%

profile of v17, /device:TPU:0, one launch (start us, length us, event | category | flops | bytes accessed | tf_op | source)
XLA Modules:
  0.0 21.7 jit_solution(13006503148929989130)
XLA Ops:
  0.0 4.0 %collective-permute-start = (bf16[3,48,128]{2,1,0:T(8,128)(2,1)}, bf16[3,48,128]{2,1,0:T(8,128)(2,1)S(1)}, u32[]{:S(2)}, u32[]{:S(2)}) collective-permute-start(bf16[3,48,128]{2,1,0:T(8,128)(2,1)} %param.17), channel_id=1, source_target_pairs={{0,8},{1,9},{2,10},{3,11},{4,12},{5,13},{6,14},{7,15},{8,0},{9,1},... | collective-permute-start | bytes 110600 | tf_op jit(solution)/shard_map/ppermute | solution.py:538
  4.1 1.0 %maximum_multiply_fusion.weights = bf16[128,640]{1,0:T(8,128)(2,1)S(1)} fusion(bf16[128,128]{1,0:T(8,128)(2,1)} %param.22, bf16[128,512]{1,0:T(8,128)(2,1)} %param.21, bf16[640]{0:T(1024)(128)(2,1)S(1)} %select_convert_fusion), kind=kLoop, calls=%fused_computation.2 | loop fusion | flops 491520 | bytes 328960 | tf_op jit(solution)/shard_map/mul | solution.py:551
  5.1 0.6 %copy-done.11 = f32[128]{0:T(128)S(1)} copy-done((f32[128]{0:T(128)S(1)}, f32[128]{0:T(128)}, u32[]{:S(2)}) %copy-start.11) | copy-done | bytes 536
  5.8 0.8 %collective-permute-done = bf16[3,48,128]{2,1,0:T(8,128)(2,1)S(1)} collective-permute-done((bf16[3,48,128]{2,1,0:T(8,128)(2,1)}, bf16[3,48,128]{2,1,0:T(8,128)(2,1)S(1)}, u32[]{:S(2)}, u32[]{:S(2)}) %collective-permute-start) | collective-permute-done | bytes 36896 | tf_op jit(solution)/shard_map/ppermute | solution.py:538
  6.6 2.5 %collective-permute-start.2 = (bf16[6,48,128]{2,1,0:T(8,128)(2,1)S(1)}, bf16[6,48,128]{2,1,0:T(8,128)(2,1)S(1)}, u32[]{:S(2)}, u32[]{:S(2)}) collective-permute-start(bf16[6,48,128]{2,1,0:T(8,128)(2,1)S(1)} %constant_dynamic-update-slice_fusion.refs_0_), channel_id=1, source_target_pairs={{0,6},{1,7},{2,4},{3,5},{4,2},{5,3},{6,0},{7,1},{8,14},{9,15},{10,... | collective-permute-start | bytes 221192 | tf_op jit(solution)/shard_map/ppermute | solution.py:538
  9.1 0.5 %collective-permute-start.1 = (bf16[6,48,128]{2,1,0:T(8,128)(2,1)S(1)}, bf16[6,48,128]{2,1,0:T(8,128)(2,1)S(1)}, u32[]{:S(2)}, u32[]{:S(2)}) collective-permute-start(bf16[6,48,128]{2,1,0:T(8,128)(2,1)S(1)} %constant_dynamic-update-slice_fusion.refs_0_), channel_id=1, source_target_pairs={{0,2},{1,3},{2,0},{3,1},{4,6},{5,7},{6,4},{7,5},{8,10},{9,11},{10,... | collective-permute-start | bytes 221192 | tf_op jit(solution)/shard_map/ppermute | solution.py:538
  9.6 0.5 %collective-permute-start.3 = (bf16[6,48,128]{2,1,0:T(8,128)(2,1)S(1)}, bf16[6,48,128]{2,1,0:T(8,128)(2,1)S(1)}, u32[]{:S(2)}, u32[]{:S(2)}) collective-permute-start(bf16[6,48,128]{2,1,0:T(8,128)(2,1)S(1)} %constant_dynamic-update-slice_fusion.refs_0_), channel_id=1, source_target_pairs={{0,4},{1,5},{2,6},{3,7},{4,0},{5,1},{6,2},{7,3},{8,12},{9,13},{10,... | collective-permute-start | bytes 221192 | tf_op jit(solution)/shard_map/ppermute | solution.py:538
  10.1 0.2 fusion.wide_bias
  10.4 0.4 %copy-done.14 = s32[48]{0:T(128)S(1)} copy-done((s32[48]{0:T(128)S(1)}, s32[48]{0:T(128)}, u32[]{:S(2)}) %copy-start.14) | copy-done | bytes 216
  10.8 0.1 broadcast_in_dim.23.valid_column
  10.9 0.4 %shard_map.163 = (f32[1152,128]{1,0:T(8,128)S(1)}, f32[1152,128]{1,0:T(8,128)S(1)}, f32[1152,128]{1,0:T(8,128)S(1)}, f32[1152,128]{1,0:T(8,128)S(1)}, bf16[12,48...) custom-call(f32[48,128]{1,0:T(8,128)S(1)} %broadcast_in_dim.23.valid_column, f32[6,128]{1,0:T(8,128)S(1)} %stack.27.norms, ...), custom_call_target="tpu_custom_call" | custom-call | flops 1048576 | bytes 33554432 | tf_op jit(solution)/shard_map/pallas_call | solution.py:526
  11.3 1.1 %collective-permute-done.2.refs_0_ = bf16[6,48,128]{2,1,0:T(8,128)(2,1)S(1)} collective-permute-done((bf16[6,48,128]{2,1,0:T(8,128)(2,1)S(1)}, bf16[6,48,128]{2,1,0:T(8,128)(2,1)S(1)}, u32[]{:S(2)}, u32[]{:S(2)}) %collective-permute-start.2) | collective-permute-done | bytes 73760 | tf_op jit(solution)/shard_map/ppermute | solution.py:538
  12.4 0.4 %shard_map.164 = (f32[1152,128]{1,0:T(8,128)S(1)}, f32[1152,128]{1,0:T(8,128)S(1)}, f32[1152,128]{1,0:T(8,128)S(1)}, f32[1152,128]{1,0:T(8,128)S(1)}, bf16[12,48,128]{2,1,0:T(8,128)(2,1)S(1)}) custom-call(f32[48,128]{1,0:T(8,128)S(1)} %broadcast_in_dim.23.valid_column, ...), custom_call_target="tpu_custom_call", output_to_operand_aliasing={{0}: (4, {}), {1}: (5, {}), {2}: (6, {}), {3}: (7, {}), {4}... | custom-call | flops 1048576 | bytes 33554432 | tf_op jit(solution)/shard_map/pallas_call | solution.py:526
  12.8 0.6 %collective-permute-done.1.refs_0_ = bf16[6,48,128]{2,1,0:T(8,128)(2,1)S(1)} collective-permute-done((bf16[6,48,128]{2,1,0:T(8,128)(2,1)S(1)}, bf16[6,48,128]{2,1,0:T(8,128)(2,1)S(1)}, u32[]{:S(2)}, u32[]{:S(2)}) %collective-permute-start.1) | collective-permute-done | bytes 73760 | tf_op jit(solution)/shard_map/ppermute | solution.py:538
  13.4 0.5 %collective-permute-done.3.refs_1_ = bf16[6,48,128]{2,1,0:T(8,128)(2,1)S(1)} collective-permute-done((bf16[6,48,128]{2,1,0:T(8,128)(2,1)S(1)}, bf16[6,48,128]{2,1,0:T(8,128)(2,1)S(1)}, u32[]{:S(2)}, u32[]{:S(2)}) %collective-permute-start.3) | collective-permute-done | bytes 73760 | tf_op jit(solution)/shard_map/ppermute | solution.py:538
  14.0 0.6 %shard_map.165 = (f32[1152,128]{1,0:T(8,128)S(1)}, f32[1152,128]{1,0:T(8,128)S(1)}, f32[1152,128]{1,0:T(8,128)S(1)}, f32[1152,128]{1,0:T(8,128)S(1)}, bf16[12,48,128]{2,1,0:T(8,128)(2,1)S(1)}) custom-call(f32[48,128]{1,0:T(8,128)S(1)} %broadcast_in_dim.23.valid_column, ...), custom_call_target="tpu_custom_call", output_to_operand_aliasing={{0}: (5, {}), {1}: (6, {}), {2}: (7, {}), {3}: (8, {})} | custom-call | flops 1048576 | bytes 33554432 | tf_op jit(solution)/shard_map/pallas_call | solution.py:526
  14.7 0.1 collective-permute-done.4.refs_0_
  14.8 1.2 %shard_map.166 = (f32[1152,128]{1,0:T(8,128)S(1)}, f32[1152,128]{1,0:T(8,128)S(1)}) custom-call(f32[1152,128]{1,0:T(8,128)S(1)} %get-tuple-element.72.left_ref.refs_0_, f32[1152,128]{1,0:T(8,128)S(1)} %get-tuple-element.75.right_ref, bf16[12,48,128]{2,1,0:T(8,128)(2,1)S(1)} %collective-permute-done.4.refs_0_), custom_call_target="tpu_custom_call" | custom-call | flops 1048576 | bytes 33554432 | tf_op jit(solution)/shard_map/pallas_call | solution.py:526
  16.0 1.1 %shard_map.167 = (f32[1152,128]{1,0:T(8,128)S(1)}, f32[576,128]{1,0:T(8,128)S(1)}, bf16[576,128]{1,0:T(8,128)(2,1)S(1)}) custom-call(f32[6,128]{1,0:T(8,128)S(1)} %stack.27.norms, bf16[128,128]{1,0:T(8,128)(2,1)S(1)} %copy-done.1, f32[1152,128]{1,0:T(8,128)S(1)} %get-tuple-element.72.left_ref.refs_0_, ...), custom_call_target="tpu_custom_call", output_to_operand_aliasing={{0}: (7, {})} | custom-call | flops 1048576 | bytes 33554432 | tf_op jit(solution)/shard_map/pallas_call | solution.py:526
  17.2 0.4 %collective-permute-start.7 = (bf16[576,128]{1,0:T(8,128)(2,1)S(1)}, bf16[576,128]{1,0:T(8,128)(2,1)S(1)}, u32[]{:S(2)}, u32[]{:S(2)}) collective-permute-start(bf16[576,128]{1,0:T(8,128)(2,1)S(1)} %get-tuple-element.81.own_att_a), channel_id=1, source_target_pairs={{0,1},{1,0},{2,3},{3,2},{4,5},{5,4},{6,7},{7,6},{8,9},{9,8},{10,11... | collective-permute-start | bytes 442376 | tf_op jit(solution)/shard_map/ppermute | solution.py:538
  17.6 1.1 %shard_map.168.own_att_b = bf16[576,128]{1,0:T(8,128)(2,1)S(1)} custom-call(f32[6,128]{1,0:T(8,128)S(1)} %stack.27.norms, bf16[128,128]{1,0:T(8,128)(2,1)S(1)} %copy-done.1, f32[1152,128]{1,0:T(8,128)S(1)} %get-tuple-element.72.left_ref.refs_0_, f32[1152,128]{1,0:T(8,128)S(1)} %get-tuple-element.73.gate_ref.refs_1_, ...), custom_call_target="tpu_custom_call" | custom-call | flops 1048576 | bytes 33554432 | tf_op jit(solution)/shard_map/pallas_call | solution.py:526
  18.7 0.2 %collective-permute-start.6 = (bf16[576,128]{1,0:T(8,128)(2,1)S(1)}, bf16[576,128]{1,0:T(8,128)(2,1)S(1)}, u32[]{:S(2)}, u32[]{:S(2)}) collective-permute-start(bf16[576,128]{1,0:T(8,128)(2,1)S(1)} %shard_map.168.own_att_b), channel_id=1, source_target_pairs={{0,1},{1,0},{2,3},{3,2},{4,5},{5,4},{6,7},{7,6},{8,9},{9,8},{10,11... | collective-permute-start | bytes 442376 | tf_op jit(solution)/shard_map/ppermute | solution.py:538
  19.0 1.3 %shard_map.169 = (f32[3,3,48,128]{3,2,1,0:T(8,128)S(1)}, f32[144,128]{1,0:T(8,128)S(1)}, f32[144,128]{1,0:T(8,128)S(1)}, f32[144,128]{1,0:T(8,128)S(1)}) custom-call(f32[48,128]{1,0:T(8,128)S(1)} %broadcast_in_dim.23.valid_column, bf16[256,256]{1,0:T(8,128)(2,1)S(1)} %get-tuple-element.50.same_head, bf16[128,128]{1,0:T(8,128)(2,1)S(1)} %copy-done.4, ...), custom_call_target="tpu_custom_call" | custom-call | flops 1048576 | bytes 33554432 | tf_op jit(solution)/shard_map/pallas_call | solution.py:526
  20.3 1.4 %shard_map.170 = bf16[3,48,128]{2,1,0:T(8,128)(2,1)} custom-call(f32[48,128]{1,0:T(8,128)S(1)} %broadcast_in_dim.23.valid_column, bf16[256,256]{1,0:T(8,128)(2,1)S(1)} %get-tuple-element.50.same_head, bf16[128,128]{1,0:T(8,128)(2,1)S(1)} %copy-done.2, bf16[128,128]{1,0:T(8,128)(2,1)S(1)} %copy-done.3, bf16[128,128]{1,0:T(8,128)(2,1)S(1)} %copy-done.6, ...), custom_call_target="tpu_custom_call" | custom-call | flops 1048576 | bytes 33554432 | tf_op jit(solution)/shard_map/pallas_call | solution.py:526
  (40 shorter events, 0.3 us)
Async XLA Ops:
  0.0 10.1 %copy-start = (bf16[128,4]{0,1:T(4,128)(2,1)S(1)}, bf16[128,4]{0,1:T(4,128)(2,1)}, u32[]{:S(2)}) copy-start(bf16[128,4]{0,1:T(4,128)(2,1)} %param.32) | copy-start | bytes 3076
  0.0 6.6 %collective-permute-start = (bf16[3,48,128]{2,1,0:T(8,128)(2,1)}, bf16[3,48,128]{2,1,0:T(8,128)(2,1)S(1)}, u32[]{:S(2)}, u32[]{:S(2)}) collective-permute-start(bf16[3,48,128]{2,1,0:T(8,128)(2,1)} %param.17), channel_id=1, source_target_pairs={{0,8},{1,9},{2,10},{3,11},{4,12},{5,13},{6,14},{7,15},{8,0},{9,1},... | collective-permute-start | bytes 110600 | tf_op jit(solution)/shard_map/ppermute | solution.py:538
  4.1 1.0 %copy-start.7 = (bf16[3,48,128]{2,1,0:T(8,128)(2,1)S(1)}, bf16[3,48,128]{2,1,0:T(8,128)(2,1)}, u32[]{:S(2)}) copy-start(bf16[3,48,128]{2,1,0:T(8,128)(2,1)} %param.17) | copy-start | bytes 110596
  5.1 0.7 %copy-start.11 = (f32[128]{0:T(128)S(1)}, f32[128]{0:T(128)}, u32[]{:S(2)}) copy-start(f32[128]{0:T(128)} %param.24) | copy-start | bytes 1540
  5.1 0.7 %copy-start.12 = (f32[128]{0:T(128)S(1)}, f32[128]{0:T(128)}, u32[]{:S(2)}) copy-start(f32[128]{0:T(128)} %param.26) | copy-start | bytes 1540
  5.1 0.7 %copy-start.13 = (f32[128]{0:T(128)S(1)}, f32[128]{0:T(128)}, u32[]{:S(2)}) copy-start(f32[128]{0:T(128)} %param.27) | copy-start | bytes 1540
  5.1 0.7 %copy-start.8 = (f32[128]{0:T(128)S(1)}, f32[128]{0:T(128)}, u32[]{:S(2)}) copy-start(f32[128]{0:T(128)} %param.19) | copy-start | bytes 1540
  5.1 0.7 %copy-start.9 = (f32[128]{0:T(128)S(1)}, f32[128]{0:T(128)}, u32[]{:S(2)}) copy-start(f32[128]{0:T(128)} %param.20) | copy-start | bytes 1540
  5.1 0.7 %copy-start.10 = (f32[128]{0:T(128)S(1)}, f32[128]{0:T(128)}, u32[]{:S(2)}) copy-start(f32[128]{0:T(128)} %param.23) | copy-start | bytes 1540
  6.6 5.8 %collective-permute-start.2 = (bf16[6,48,128]{2,1,0:T(8,128)(2,1)S(1)}, bf16[6,48,128]{2,1,0:T(8,128)(2,1)S(1)}, u32[]{:S(2)}, u32[]{:S(2)}) collective-permute-start(bf16[6,48,128]{2,1,0:T(8,128)(2,1)S(1)} %constant_dynamic-update-slice_fusion.refs_0_), channel_id=1, source_target_pairs={{0,6},{1,7},{2,4},{3,5},{4,2},{5,3},{6,0},{7,1},{8,14},{9,15},{10,... | collective-permute-start | bytes 221192 | tf_op jit(solution)/shard_map/ppermute | solution.py:538
  9.1 4.4 %collective-permute-start.1 = (bf16[6,48,128]{2,1,0:T(8,128)(2,1)S(1)}, bf16[6,48,128]{2,1,0:T(8,128)(2,1)S(1)}, u32[]{:S(2)}, u32[]{:S(2)}) collective-permute-start(bf16[6,48,128]{2,1,0:T(8,128)(2,1)S(1)} %constant_dynamic-update-slice_fusion.refs_0_), channel_id=1, source_target_pairs={{0,2},{1,3},{2,0},{3,1},{4,6},{5,7},{6,4},{7,5},{8,10},{9,11},{10,... | collective-permute-start | bytes 221192 | tf_op jit(solution)/shard_map/ppermute | solution.py:538
  9.6 4.4 %collective-permute-start.3 = (bf16[6,48,128]{2,1,0:T(8,128)(2,1)S(1)}, bf16[6,48,128]{2,1,0:T(8,128)(2,1)S(1)}, u32[]{:S(2)}, u32[]{:S(2)}) collective-permute-start(bf16[6,48,128]{2,1,0:T(8,128)(2,1)S(1)} %constant_dynamic-update-slice_fusion.refs_0_), channel_id=1, source_target_pairs={{0,4},{1,5},{2,6},{3,7},{4,0},{5,1},{6,2},{7,3},{8,12},{9,13},{10,... | collective-permute-start | bytes 221192 | tf_op jit(solution)/shard_map/ppermute | solution.py:538
  10.1 0.7 %copy-start.14 = (s32[48]{0:T(128)S(1)}, s32[48]{0:T(128)}, u32[]{:S(2)}) copy-start(s32[48]{0:T(128)} %param.18) | copy-start | bytes 580
  13.4 1.4 %collective-permute-start.4 = (bf16[12,48,128]{2,1,0:T(8,128)(2,1)S(1)}, bf16[12,48,128]{2,1,0:T(8,128)(2,1)S(1)}, u32[]{:S(2)}, u32[]{:S(2)}) collective-permute-start(bf16[12,48,128]{2,1,0:T(8,128)(2,1)S(1)} %get-tuple-element.76), channel_id=1, source_target_pairs={{0,1},{1,0},{2,3},{3,2},{4,5},{5,4},{6,7},{7,6},{8,9},{9,8},{10,11... | collective-permute-start | bytes 442376 | tf_op jit(solution)/shard_map/ppermute | solution.py:538
  14.6 1.4 %collective-permute-start.5 = (bf16[12,48,128]{2,1,0:T(8,128)(2,1)S(1)}, bf16[12,48,128]{2,1,0:T(8,128)(2,1)S(1)}, u32[]{:S(2)}, u32[]{:S(2)}) collective-permute-start(bf16[12,48,128]{2,1,0:T(8,128)(2,1)S(1)} %get-tuple-element.78), channel_id=1, source_target_pairs={{0,1},{1,0},{2,3},{3,2},{4,5},{5,4},{6,7},{7,6},{8,9},{9,8},{10,11... | collective-permute-start | bytes 442376 | tf_op jit(solution)/shard_map/ppermute | solution.py:538
  14.8 1.2 %copy-start.1 = (bf16[128,128]{1,0:T(8,128)(2,1)S(1)}, bf16[128,128]{1,0:T(8,128)(2,1)}, u32[]{:S(2)}) copy-start(bf16[128,128]{1,0:T(8,128)(2,1)} %w_out.4) | copy-start | bytes 98308
  17.2 1.8 %collective-permute-start.7 = (bf16[576,128]{1,0:T(8,128)(2,1)S(1)}, bf16[576,128]{1,0:T(8,128)(2,1)S(1)}, u32[]{:S(2)}, u32[]{:S(2)}) collective-permute-start(bf16[576,128]{1,0:T(8,128)(2,1)S(1)} %get-tuple-element.81.own_att_a), channel_id=1, source_target_pairs={{0,1},{1,0},{2,3},{3,2},{4,5},{5,4},{6,7},{7,6},{8,9},{9,8},{10,11... | collective-permute-start | bytes 442376 | tf_op jit(solution)/shard_map/ppermute | solution.py:538
  17.6 1.3 %copy-start.2 = (bf16[128,128]{1,0:T(8,128)(2,1)S(1)}, bf16[128,128]{1,0:T(8,128)(2,1)}, u32[]{:S(2)}) copy-start(bf16[128,128]{1,0:T(8,128)(2,1)} %w_key.3) | copy-start | bytes 98308
  17.6 1.3 %copy-start.3 = (bf16[128,128]{1,0:T(8,128)(2,1)S(1)}, bf16[128,128]{1,0:T(8,128)(2,1)}, u32[]{:S(2)}) copy-start(bf16[128,128]{1,0:T(8,128)(2,1)} %w_value.3) | copy-start | bytes 98308
  17.6 1.3 %copy-start.4 = (bf16[128,128]{1,0:T(8,128)(2,1)S(1)}, bf16[128,128]{1,0:T(8,128)(2,1)}, u32[]{:S(2)}) copy-start(bf16[128,128]{1,0:T(8,128)(2,1)} %w_query.1) | copy-start | bytes 98308
  17.6 1.4 %copy-start.5 = (bf16[128,128]{1,0:T(8,128)(2,1)S(1)}, bf16[128,128]{1,0:T(8,128)(2,1)}, u32[]{:S(2)}) copy-start(bf16[128,128]{1,0:T(8,128)(2,1)} %w_gate.1) | copy-start | bytes 98308
  18.7 1.6 %collective-permute-start.6 = (bf16[576,128]{1,0:T(8,128)(2,1)S(1)}, bf16[576,128]{1,0:T(8,128)(2,1)S(1)}, u32[]{:S(2)}, u32[]{:S(2)}) collective-permute-start(bf16[576,128]{1,0:T(8,128)(2,1)S(1)} %shard_map.168.own_att_b), channel_id=1, source_target_pairs={{0,1},{1,0},{2,3},{3,2},{4,5},{5,4},{6,7},{7,6},{8,9},{9,8},{10,11... | collective-permute-start | bytes 442376 | tf_op jit(solution)/shard_map/ppermute | solution.py:538
  18.9 1.3 %copy-start.6 = (bf16[128,128]{1,0:T(8,128)(2,1)S(1)}, bf16[128,128]{1,0:T(8,128)(2,1)}, u32[]{:S(2)}) copy-start(bf16[128,128]{1,0:T(8,128)(2,1)} %w_out.5) | copy-start | bytes 98308

commit v18 on v16

--- a/solution.py
+++ b/solution.py
@@ -535,7 +535,10 @@
         jnp.zeros((2 * row_count, res, channels), bf16), pair_rep, (0, 0, 0)
     )
     far = exchange(pair_rep, devices // 2)
-    far, kept, norms, edge_weights = lax.optimization_barrier((far, kept, norms, edge_weights))
+    near_own = exchange(pair_rep, 4)
+    far, near_own, kept, norms, edge_weights = lax.optimization_barrier(
+        (far, near_own, kept, norms, edge_weights)
+    )
     own = lax.dynamic_update_slice(kept, far, (row_count, 0, 0))
     own_blocks = (0, chips // 2)
 
@@ -547,11 +550,12 @@
     def edges_of(pieces, send_row, *held):
         pairs = tuple(p for p, _ in pieces)
         blocks = tuple(b for _, b in pieces)
+        sent = (3 if held and send_row == 0 else 5) * row_count
         operands = (valid_column, norms, edge_weights) + pairs + held
         first = len(operands) - len(held)
         return call(
             functools.partial(edges_kernel, row_count, chips, blocks, send_row, not held),
-            (tall, tall, tall, tall, shaped(bf16, 4 * row_count, res, channels))
+            (tall, tall, tall, tall, shaped(bf16, sent, res, channels))
             + (() if held else (shaped(bf16, 2 * channels, 2 * channels),)),
             operands,
             {first + e: e for e in range(len(held))},
@@ -559,20 +563,18 @@
 
     diagonal = exchange(own, 6)
     beside = exchange(own, 2)
-    near = exchange(own, 4)
-    *edges, early_right, same_head = edges_of([(own, own_blocks)], 0)
-    diagonal, edges = lax.optimization_barrier((diagonal, edges))
+    near_far = exchange(far, 4)
+    *edges, early_right, same_head = edges_of([(own, own_blocks), (near_own, (2,))], 0)
+    diagonal, edges, early_right = lax.optimization_barrier((diagonal, edges, early_right))
     *edges, early_right = edges_of(
-        [(diagonal, blocks_from(3))], 2 * row_count, *edges, early_right
+        [(diagonal, blocks_from(3))], 3 * row_count, *edges, early_right
     )
     beside, edges, early_right, wide_bias = lax.optimization_barrier(
         (beside, edges, early_right, wide_bias)
     )
-    early = (exchange(early_right, 1), own_blocks + blocks_from(3))
-    *edges, late_right = edges_of(
-        [(beside, blocks_from(1)), (near, blocks_from(2))], 0, *edges
-    )
-    late = (exchange(late_right, 1), blocks_from(1) + blocks_from(2))
+    early = (exchange(early_right, 1), own_blocks + (2,) + blocks_from(3))
+    *edges, late_right = edges_of([(beside, blocks_from(1)), (near_far, (6,))], 0, *edges)
+    late = (exchange(late_right, 1), blocks_from(1) + (6,))
 
     left, right, gate, pairs = edges
     triangle, across = call(

time: 21.8 us -> 27.2 us (1.25)
  starting transfers between devices: 8.3 us -> 11.1 us
  waiting for transfers between devices: 3.19 us -> 5.76 us
    ppermute x8 -> x9, starting transfers between devices: 8.3 us -> 11.1 us  [exchange(): return lax.ppermute(values, 'row', [(d, d ^ bit) for d in range(devices)])]
    ppermute x8 -> x9, waiting for transfers between devices: 3.19 us -> 5.76 us  [exchange(): return lax.ppermute(values, 'row', [(d, d ^ bit) for d in range(devices)])]
  transfers between devices with their start and end apart: 8 -> 9, of which waited for: 5 -> 4; matrix products, arithmetic and copies ran while one was open for 6% -> 5% of each run, Pallas kernels for 23% -> 18%
where the time goes in v18:
time: 27.2 us; the launch traced here: 27 us
  starting transfers between devices  11.1 us (41%)
  Pallas kernels  7.44 us (27%)
  waiting for transfers between devices  5.76 us (21%)
  local copies, waits for them, and re-layouts  1.28 us (5%)
  other arithmetic  0.99 us (4%)
    ppermute x9, starting transfers between devices, exchange(): return lax.ppermute(values, 'row', [(d, d ^ bit) for d in range(devices)])  11.1 us
    pallas_call x8, Pallas kernels, call(): pl.pallas_call(kernel, out_shape=outs, in_specs=[in_vmem] * len(operands)...  7.44 us
    ppermute x9, waiting for transfers between devices, exchange(): return lax.ppermute(values, 'row', [(d, d ^ bit) for d in range(devices)])  5.76 us
    unnamed x30, local copies, waits for them, and re-layouts  1.17 us
    mul x1, other arithmetic, on_whole_complex(): edge_weights = jnp.concatenate([w_edges, w_tri_gate], axis=1) * halves  0.97 us
  transfers between devices with their start and end apart: 9, of which 4 were waited for; matrix products, arithmetic and copies ran while one was open for 5% of the time, Pallas kernels for 18%

profile of v18, /device:TPU:0, one launch (start us, length us, event | category | flops | bytes accessed | tf_op | source)
XLA Modules:
  0.0 27.0 jit_solution(8705916853103413176)
XLA Ops:
  0.0 4.0 %collective-permute-start = (bf16[3,48,128]{2,1,0:T(8,128)(2,1)}, bf16[3,48,128]{2,1,0:T(8,128)(2,1)S(1)}, u32[]{:S(2)}, u32[]{:S(2)}) collective-permute-start(bf16[3,48,128]{2,1,0:T(8,128)(2,1)} %param.17), channel_id=1, source_target_pairs={{0,8},{1,9},{2,10},{3,11},{4,12},{5,13},{6,14},{7,15},{8,0},{9,1},... | collective-permute-start | bytes 110600 | tf_op jit(solution)/shard_map/ppermute | solution.py:513
  4.0 1.6 %collective-permute-start.1 = (bf16[3,48,128]{2,1,0:T(8,128)(2,1)}, bf16[3,48,128]{2,1,0:T(8,128)(2,1)S(1)}, u32[]{:S(2)}, u32[]{:S(2)}) collective-permute-start(bf16[3,48,128]{2,1,0:T(8,128)(2,1)} %param.17), channel_id=1, source_target_pairs={{0,4},{1,5},{2,6},{3,7},{4,0},{5,1},{6,2},{7,3},{8,12},{9,13},{10,... | collective-permute-start | bytes 110600 | tf_op jit(solution)/shard_map/ppermute | solution.py:513
  5.6 1.0 %maximum_multiply_fusion.weights = bf16[128,640]{1,0:T(8,128)(2,1)S(1)} fusion(bf16[128,128]{1,0:T(8,128)(2,1)} %param.22, bf16[128,512]{1,0:T(8,128)(2,1)} %param.21, bf16[640]{0:T(1024)(128)(2,1)S(1)} %select_convert_fusion), kind=kLoop, calls=%fused_computation.2 | loop fusion | flops 491520 | bytes 328960 | tf_op jit(solution)/shard_map/mul | solution.py:526
  6.7 0.6 %copy-done.11 = f32[128]{0:T(128)S(1)} copy-done((f32[128]{0:T(128)S(1)}, f32[128]{0:T(128)}, u32[]{:S(2)}) %copy-start.11) | copy-done | bytes 536
  7.4 0.8 %collective-permute-done.1.refs_1_ = bf16[3,48,128]{2,1,0:T(8,128)(2,1)S(1)} collective-permute-done((bf16[3,48,128]{2,1,0:T(8,128)(2,1)}, bf16[3,48,128]{2,1,0:T(8,128)(2,1)S(1)}, u32[]{:S(2)}, u32[]{:S(2)}) %collective-permute-start.1) | collective-permute-done | bytes 36896 | tf_op jit(solution)/shard_map/ppermute | solution.py:513
  8.2 1.5 %collective-permute-start.2 = (bf16[6,48,128]{2,1,0:T(8,128)(2,1)S(1)}, bf16[6,48,128]{2,1,0:T(8,128)(2,1)S(1)}, u32[]{:S(2)}, u32[]{:S(2)}) collective-permute-start(bf16[6,48,128]{2,1,0:T(8,128)(2,1)S(1)} %constant_dynamic-update-slice_fusion.refs_0_), channel_id=1, source_target_pairs={{0,2},{1,3},{2,0},{3,1},{4,6},{5,7},{6,4},{7,5},{8,10},{9,11},{10,... | collective-permute-start | bytes 221192 | tf_op jit(solution)/shard_map/ppermute | solution.py:513
  9.8 1.5 %collective-permute-start.3 = (bf16[6,48,128]{2,1,0:T(8,128)(2,1)S(1)}, bf16[6,48,128]{2,1,0:T(8,128)(2,1)S(1)}, u32[]{:S(2)}, u32[]{:S(2)}) collective-permute-start(bf16[6,48,128]{2,1,0:T(8,128)(2,1)S(1)} %constant_dynamic-update-slice_fusion.refs_0_), channel_id=1, source_target_pairs={{0,6},{1,7},{2,4},{3,5},{4,2},{5,3},{6,0},{7,1},{8,14},{9,15},{10,... | collective-permute-start | bytes 221192 | tf_op jit(solution)/shard_map/ppermute | solution.py:513
  11.3 0.2 fusion.wide_bias
  11.5 0.4 %copy-done.14 = s32[48]{0:T(128)S(1)} copy-done((s32[48]{0:T(128)S(1)}, s32[48]{0:T(128)}, u32[]{:S(2)}) %copy-start.14) | copy-done | bytes 216
  12.0 0.1 broadcast_in_dim.23.valid_column
  12.1 0.5 %shard_map.163 = (f32[1152,128]{1,0:T(8,128)S(1)}, f32[1152,128]{1,0:T(8,128)S(1)}, f32[1152,128]{1,0:T(8,128)S(1)}, f32[1152,128]{1,0:T(8,128)S(1)}, bf16[15,48...) custom-call(f32[48,128]{1,0:T(8,128)S(1)} %broadcast_in_dim.23.valid_column, f32[6,128]{1,0:T(8,128)S(1)} %stack.27.norms, ...), custom_call_target="tpu_custom_call" | custom-call | flops 1048576 | bytes 33554432 | tf_op jit(solution)/shard_map/pallas_call | solution.py:501
  12.5 2.5 %collective-permute-done.3.refs_0_ = bf16[6,48,128]{2,1,0:T(8,128)(2,1)S(1)} collective-permute-done((bf16[6,48,128]{2,1,0:T(8,128)(2,1)S(1)}, bf16[6,48,128]{2,1,0:T(8,128)(2,1)S(1)}, u32[]{:S(2)}, u32[]{:S(2)}) %collective-permute-start.3) | collective-permute-done | bytes 73760 | tf_op jit(solution)/shard_map/ppermute | solution.py:513
  15.0 0.4 %shard_map.164 = (f32[1152,128]{1,0:T(8,128)S(1)}, f32[1152,128]{1,0:T(8,128)S(1)}, f32[1152,128]{1,0:T(8,128)S(1)}, f32[1152,128]{1,0:T(8,128)S(1)}, bf16[15,48,128]{2,1,0:T(8,128)(2,1)S(1)}) custom-call(f32[48,128]{1,0:T(8,128)S(1)} %broadcast_in_dim.23.valid_column, ...), custom_call_target="tpu_custom_call", output_to_operand_aliasing={{0}: (4, {}), {1}: (5, {}), {2}: (6, {}), {3}: (7, {}), {4}... | custom-call | flops 1048576 | bytes 33554432 | tf_op jit(solution)/shard_map/pallas_call | solution.py:501
  15.5 1.6 %collective-permute-start.4 = (bf16[3,48,128]{2,1,0:T(8,128)(2,1)S(1)}, bf16[3,48,128]{2,1,0:T(8,128)(2,1)S(1)}, u32[]{:S(2)}, u32[]{:S(2)}) collective-permute-start(bf16[3,48,128]{2,1,0:T(8,128)(2,1)S(1)} %collective-permute-done), channel_id=1, source_target_pairs={{0,4},{1,5},{2,6},{3,7},{4,0},{5,1},{6,2},{7,3},{8,12},{9,13},{10,... | collective-permute-start | bytes 110600 | tf_op jit(solution)/shard_map/ppermute | solution.py:513
  17.2 2.4 %collective-permute-done.4.refs_1_ = bf16[3,48,128]{2,1,0:T(8,128)(2,1)S(1)} collective-permute-done((bf16[3,48,128]{2,1,0:T(8,128)(2,1)S(1)}, bf16[3,48,128]{2,1,0:T(8,128)(2,1)S(1)}, u32[]{:S(2)}, u32[]{:S(2)}) %collective-permute-start.4) | collective-permute-done | bytes 36896 | tf_op jit(solution)/shard_map/ppermute | solution.py:513
  19.6 0.5 %shard_map.165 = (f32[1152,128]{1,0:T(8,128)S(1)}, f32[1152,128]{1,0:T(8,128)S(1)}, f32[1152,128]{1,0:T(8,128)S(1)}, f32[1152,128]{1,0:T(8,128)S(1)}, bf16[9,48,128]{2,1,0:T(8,128)(2,1)S(1)}) custom-call(f32[48,128]{1,0:T(8,128)S(1)} %broadcast_in_dim.23.valid_column, ...), custom_call_target="tpu_custom_call", output_to_operand_aliasing={{0}: (5, {}), {1}: (6, {}), {2}: (7, {}), {3}: (8, {})} | custom-call | flops 1048576 | bytes 33554432 | tf_op jit(solution)/shard_map/pallas_call | solution.py:501
  20.1 1.2 %shard_map.166 = (f32[1152,128]{1,0:T(8,128)S(1)}, f32[1152,128]{1,0:T(8,128)S(1)}) custom-call(f32[1152,128]{1,0:T(8,128)S(1)} %get-tuple-element.76.left_ref.refs_0_, f32[1152,128]{1,0:T(8,128)S(1)} %get-tuple-element.79.right_ref, bf16[15,48,128]{2,1,0:T(8,128)(2,1)S(1)} %collective-permute-done.5.refs_0_), custom_call_target="tpu_custom_call" | custom-call | flops 1048576 | bytes 33554432 | tf_op jit(solution)/shard_map/pallas_call | solution.py:501
  21.3 0.1 collective-permute-done.6.received
  21.4 1.1 %shard_map.167 = (f32[1152,128]{1,0:T(8,128)S(1)}, f32[576,128]{1,0:T(8,128)S(1)}, bf16[576,128]{1,0:T(8,128)(2,1)S(1)}) custom-call(f32[6,128]{1,0:T(8,128)S(1)} %stack.27.norms, bf16[128,128]{1,0:T(8,128)(2,1)S(1)} %copy-done.1, f32[1152,128]{1,0:T(8,128)S(1)} %get-tuple-element.76.left_ref.refs_0_, ...), custom_call_target="tpu_custom_call", output_to_operand_aliasing={{0}: (7, {})} | custom-call | flops 1048576 | bytes 33554432 | tf_op jit(solution)/shard_map/pallas_call | solution.py:501
  22.5 0.5 %collective-permute-start.8 = (bf16[576,128]{1,0:T(8,128)(2,1)S(1)}, bf16[576,128]{1,0:T(8,128)(2,1)S(1)}, u32[]{:S(2)}, u32[]{:S(2)}) collective-permute-start(bf16[576,128]{1,0:T(8,128)(2,1)S(1)} %get-tuple-element.85.own_att_a), channel_id=1, source_target_pairs={{0,1},{1,0},{2,3},{3,2},{4,5},{5,4},{6,7},{7,6},{8,9},{9,8},{10,11... | collective-permute-start | bytes 442376 | tf_op jit(solution)/shard_map/ppermute | solution.py:513
  23.0 1.1 %shard_map.168.own_att_b = bf16[576,128]{1,0:T(8,128)(2,1)S(1)} custom-call(f32[6,128]{1,0:T(8,128)S(1)} %stack.27.norms, bf16[128,128]{1,0:T(8,128)(2,1)S(1)} %copy-done.1, f32[1152,128]{1,0:T(8,128)S(1)} %get-tuple-element.76.left_ref.refs_0_, f32[1152,128]{1,0:T(8,128)S(1)} %get-tuple-element.77.gate_ref.refs_1_, ...), custom_call_target="tpu_custom_call" | custom-call | flops 1048576 | bytes 33554432 | tf_op jit(solution)/shard_map/pallas_call | solution.py:501
  24.1 0.2 collective-permute-start.7
  24.3 1.3 %shard_map.169 = (f32[3,3,48,128]{3,2,1,0:T(8,128)S(1)}, f32[144,128]{1,0:T(8,128)S(1)}, f32[144,128]{1,0:T(8,128)S(1)}, f32[144,128]{1,0:T(8,128)S(1)}) custom-call(f32[48,128]{1,0:T(8,128)S(1)} %broadcast_in_dim.23.valid_column, bf16[256,256]{1,0:T(8,128)(2,1)S(1)} %get-tuple-element.53.same_head, bf16[128,128]{1,0:T(8,128)(2,1)S(1)} %copy-done.4, ...), custom_call_target="tpu_custom_call" | custom-call | flops 1048576 | bytes 33554432 | tf_op jit(solution)/shard_map/pallas_call | solution.py:501
  25.7 1.4 %shard_map.170 = bf16[3,48,128]{2,1,0:T(8,128)(2,1)} custom-call(f32[48,128]{1,0:T(8,128)S(1)} %broadcast_in_dim.23.valid_column, bf16[256,256]{1,0:T(8,128)(2,1)S(1)} %get-tuple-element.53.same_head, bf16[128,128]{1,0:T(8,128)(2,1)S(1)} %copy-done.2, bf16[128,128]{1,0:T(8,128)(2,1)S(1)} %copy-done.3, bf16[128,128]{1,0:T(8,128)(2,1)S(1)} %copy-done.6, ...), custom_call_target="tpu_custom_call" | custom-call | flops 1048576 | bytes 33554432 | tf_op jit(solution)/shard_map/pallas_call | solution.py:501
  (42 shorter events, 0.4 us)
Async XLA Ops:
  0.0 11.3 %copy-start = (bf16[128,4]{0,1:T(4,128)(2,1)S(1)}, bf16[128,4]{0,1:T(4,128)(2,1)}, u32[]{:S(2)}) copy-start(bf16[128,4]{0,1:T(4,128)(2,1)} %param.32) | copy-start | bytes 3076
  0.0 7.4 %collective-permute-start = (bf16[3,48,128]{2,1,0:T(8,128)(2,1)}, bf16[3,48,128]{2,1,0:T(8,128)(2,1)S(1)}, u32[]{:S(2)}, u32[]{:S(2)}) collective-permute-start(bf16[3,48,128]{2,1,0:T(8,128)(2,1)} %param.17), channel_id=1, source_target_pairs={{0,8},{1,9},{2,10},{3,11},{4,12},{5,13},{6,14},{7,15},{8,0},{9,1},... | collective-permute-start | bytes 110600 | tf_op jit(solution)/shard_map/ppermute | solution.py:513
  4.0 4.2 %collective-permute-start.1 = (bf16[3,48,128]{2,1,0:T(8,128)(2,1)}, bf16[3,48,128]{2,1,0:T(8,128)(2,1)S(1)}, u32[]{:S(2)}, u32[]{:S(2)}) collective-permute-start(bf16[3,48,128]{2,1,0:T(8,128)(2,1)} %param.17), channel_id=1, source_target_pairs={{0,4},{1,5},{2,6},{3,7},{4,0},{5,1},{6,2},{7,3},{8,12},{9,13},{10,... | collective-permute-start | bytes 110600 | tf_op jit(solution)/shard_map/ppermute | solution.py:513
  5.6 1.0 %copy-start.7 = (bf16[3,48,128]{2,1,0:T(8,128)(2,1)S(1)}, bf16[3,48,128]{2,1,0:T(8,128)(2,1)}, u32[]{:S(2)}) copy-start(bf16[3,48,128]{2,1,0:T(8,128)(2,1)} %param.17) | copy-start | bytes 110596
  6.6 0.7 %copy-start.11 = (f32[128]{0:T(128)S(1)}, f32[128]{0:T(128)}, u32[]{:S(2)}) copy-start(f32[128]{0:T(128)} %param.24) | copy-start | bytes 1540
  6.7 0.7 %copy-start.12 = (f32[128]{0:T(128)S(1)}, f32[128]{0:T(128)}, u32[]{:S(2)}) copy-start(f32[128]{0:T(128)} %param.26) | copy-start | bytes 1540
  6.7 0.7 %copy-start.13 = (f32[128]{0:T(128)S(1)}, f32[128]{0:T(128)}, u32[]{:S(2)}) copy-start(f32[128]{0:T(128)} %param.27) | copy-start | bytes 1540
  6.7 0.7 %copy-start.8 = (f32[128]{0:T(128)S(1)}, f32[128]{0:T(128)}, u32[]{:S(2)}) copy-start(f32[128]{0:T(128)} %param.19) | copy-start | bytes 1540
  6.7 0.7 %copy-start.9 = (f32[128]{0:T(128)S(1)}, f32[128]{0:T(128)}, u32[]{:S(2)}) copy-start(f32[128]{0:T(128)} %param.20) | copy-start | bytes 1540
  6.7 0.7 %copy-start.10 = (f32[128]{0:T(128)S(1)}, f32[128]{0:T(128)}, u32[]{:S(2)}) copy-start(f32[128]{0:T(128)} %param.23) | copy-start | bytes 1540
  8.2 7.2 %collective-permute-start.2 = (bf16[6,48,128]{2,1,0:T(8,128)(2,1)S(1)}, bf16[6,48,128]{2,1,0:T(8,128)(2,1)S(1)}, u32[]{:S(2)}, u32[]{:S(2)}) collective-permute-start(bf16[6,48,128]{2,1,0:T(8,128)(2,1)S(1)} %constant_dynamic-update-slice_fusion.refs_0_), channel_id=1, source_target_pairs={{0,2},{1,3},{2,0},{3,1},{4,6},{5,7},{6,4},{7,5},{8,10},{9,11},{10,... | collective-permute-start | bytes 221192 | tf_op jit(solution)/shard_map/ppermute | solution.py:513
  9.8 5.3 %collective-permute-start.3 = (bf16[6,48,128]{2,1,0:T(8,128)(2,1)S(1)}, bf16[6,48,128]{2,1,0:T(8,128)(2,1)S(1)}, u32[]{:S(2)}, u32[]{:S(2)}) collective-permute-start(bf16[6,48,128]{2,1,0:T(8,128)(2,1)S(1)} %constant_dynamic-update-slice_fusion.refs_0_), channel_id=1, source_target_pairs={{0,6},{1,7},{2,4},{3,5},{4,2},{5,3},{6,0},{7,1},{8,14},{9,15},{10,... | collective-permute-start | bytes 221192 | tf_op jit(solution)/shard_map/ppermute | solution.py:513
  11.3 0.7 %copy-start.14 = (s32[48]{0:T(128)S(1)}, s32[48]{0:T(128)}, u32[]{:S(2)}) copy-start(s32[48]{0:T(128)} %param.18) | copy-start | bytes 580
  15.4 4.7 %collective-permute-start.5 = (bf16[15,48,128]{2,1,0:T(8,128)(2,1)S(1)}, bf16[15,48,128]{2,1,0:T(8,128)(2,1)S(1)}, u32[]{:S(2)}, u32[]{:S(2)}) collective-permute-start(bf16[15,48,128]{2,1,0:T(8,128)(2,1)S(1)} %get-tuple-element.80), channel_id=1, source_target_pairs={{0,1},{1,0},{2,3},{3,2},{4,5},{5,4},{6,7},{7,6},{8,9},{9,8},{10,11... | collective-permute-start | bytes 552968 | tf_op jit(solution)/shard_map/ppermute | solution.py:513
  15.5 4.0 %collective-permute-start.4 = (bf16[3,48,128]{2,1,0:T(8,128)(2,1)S(1)}, bf16[3,48,128]{2,1,0:T(8,128)(2,1)S(1)}, u32[]{:S(2)}, u32[]{:S(2)}) collective-permute-start(bf16[3,48,128]{2,1,0:T(8,128)(2,1)S(1)} %collective-permute-done), channel_id=1, source_target_pairs={{0,4},{1,5},{2,6},{3,7},{4,0},{5,1},{6,2},{7,3},{8,12},{9,13},{10,... | collective-permute-start | bytes 110600 | tf_op jit(solution)/shard_map/ppermute | solution.py:513
  20.0 1.4 %collective-permute-start.6 = (bf16[9,48,128]{2,1,0:T(8,128)(2,1)S(1)}, bf16[9,48,128]{2,1,0:T(8,128)(2,1)S(1)}, u32[]{:S(2)}, u32[]{:S(2)}) collective-permute-start(bf16[9,48,128]{2,1,0:T(8,128)(2,1)S(1)} %get-tuple-element.82), channel_id=1, source_target_pairs={{0,1},{1,0},{2,3},{3,2},{4,5},{5,4},{6,7},{7,6},{8,9},{9,8},{10,11... | collective-permute-start | bytes 331784 | tf_op jit(solution)/shard_map/ppermute | solution.py:513
  20.1 1.3 %copy-start.1 = (bf16[128,128]{1,0:T(8,128)(2,1)S(1)}, bf16[128,128]{1,0:T(8,128)(2,1)}, u32[]{:S(2)}) copy-start(bf16[128,128]{1,0:T(8,128)(2,1)} %w_out.4) | copy-start | bytes 98308
  22.5 1.8 %collective-permute-start.8 = (bf16[576,128]{1,0:T(8,128)(2,1)S(1)}, bf16[576,128]{1,0:T(8,128)(2,1)S(1)}, u32[]{:S(2)}, u32[]{:S(2)}) collective-permute-start(bf16[576,128]{1,0:T(8,128)(2,1)S(1)} %get-tuple-element.85.own_att_a), channel_id=1, source_target_pairs={{0,1},{1,0},{2,3},{3,2},{4,5},{5,4},{6,7},{7,6},{8,9},{9,8},{10,11... | collective-permute-start | bytes 442376 | tf_op jit(solution)/shard_map/ppermute | solution.py:513
  23.0 1.3 %copy-start.2 = (bf16[128,128]{1,0:T(8,128)(2,1)S(1)}, bf16[128,128]{1,0:T(8,128)(2,1)}, u32[]{:S(2)}) copy-start(bf16[128,128]{1,0:T(8,128)(2,1)} %w_key.3) | copy-start | bytes 98308
  23.0 1.3 %copy-start.3 = (bf16[128,128]{1,0:T(8,128)(2,1)S(1)}, bf16[128,128]{1,0:T(8,128)(2,1)}, u32[]{:S(2)}) copy-start(bf16[128,128]{1,0:T(8,128)(2,1)} %w_value.3) | copy-start | bytes 98308
  23.0 1.3 %copy-start.4 = (bf16[128,128]{1,0:T(8,128)(2,1)S(1)}, bf16[128,128]{1,0:T(8,128)(2,1)}, u32[]{:S(2)}) copy-start(bf16[128,128]{1,0:T(8,128)(2,1)} %w_query.1) | copy-start | bytes 98308
  23.0 1.3 %copy-start.5 = (bf16[128,128]{1,0:T(8,128)(2,1)S(1)}, bf16[128,128]{1,0:T(8,128)(2,1)}, u32[]{:S(2)}) copy-start(bf16[128,128]{1,0:T(8,128)(2,1)} %w_gate.1) | copy-start | bytes 98308
  24.1 1.5 %collective-permute-start.7 = (bf16[576,128]{1,0:T(8,128)(2,1)S(1)}, bf16[576,128]{1,0:T(8,128)(2,1)S(1)}, u32[]{:S(2)}, u32[]{:S(2)}) collective-permute-start(bf16[576,128]{1,0:T(8,128)(2,1)S(1)} %shard_map.168.own_att_b), channel_id=1, source_target_pairs={{0,1},{1,0},{2,3},{3,2},{4,5},{5,4},{6,7},{7,6},{8,9},{9,8},{10,11... | collective-permute-start | bytes 442376 | tf_op jit(solution)/shard_map/ppermute | solution.py:513
  24.3 1.3 %copy-start.6 = (bf16[128,128]{1,0:T(8,128)(2,1)S(1)}, bf16[128,128]{1,0:T(8,128)(2,1)}, u32[]{:S(2)}) copy-start(bf16[128,128]{1,0:T(8,128)(2,1)} %w_out.5) | copy-start | bytes 98308

commit v19 on v16

--- a/solution.py
+++ b/solution.py
@@ -558,21 +558,21 @@
         )
 
     diagonal = exchange(own, 6)
+    near = exchange(own, 4)
     beside = exchange(own, 2)
-    near = exchange(own, 4)
     *edges, early_right, same_head = edges_of([(own, own_blocks)], 0)
     diagonal, edges = lax.optimization_barrier((diagonal, edges))
     *edges, early_right = edges_of(
         [(diagonal, blocks_from(3))], 2 * row_count, *edges, early_right
     )
-    beside, edges, early_right, wide_bias = lax.optimization_barrier(
-        (beside, edges, early_right, wide_bias)
+    near, edges, early_right, wide_bias = lax.optimization_barrier(
+        (near, edges, early_right, wide_bias)
     )
     early = (exchange(early_right, 1), own_blocks + blocks_from(3))
     *edges, late_right = edges_of(
-        [(beside, blocks_from(1)), (near, blocks_from(2))], 0, *edges
-    )
-    late = (exchange(late_right, 1), blocks_from(1) + blocks_from(2))
+        [(near, blocks_from(2)), (beside, blocks_from(1))], 0, *edges
+    )
+    late = (exchange(late_right, 1), blocks_from(2) + blocks_from(1))
 
     left, right, gate, pairs = edges
     triangle, across = call(

time: 21.8 us -> 22 us (level)
  no operation moved by 1% of the time
where the time goes in v19:
time: 22 us; the launch traced here: 21.8 us
  starting transfers between devices  8.3 us (38%)
  Pallas kernels  7.5 us (34%)
  waiting for transfers between devices  3.36 us (15%)
  local copies, waits for them, and re-layouts  1.28 us (6%)
  other arithmetic  0.99 us (4%)
    ppermute x8, starting transfers between devices, exchange(): return lax.ppermute(values, 'row', [(d, d ^ bit) for d in range(devices)])  8.3 us
    pallas_call x8, Pallas kernels, call(): pl.pallas_call(kernel, out_shape=outs, in_specs=[in_vmem] * len(operands)...  7.5 us
    ppermute x8, waiting for transfers between devices, exchange(): return lax.ppermute(values, 'row', [(d, d ^ bit) for d in range(devices)])  3.36 us
    unnamed x30, local copies, waits for them, and re-layouts  1.17 us
    mul x1, other arithmetic, on_whole_complex(): edge_weights = jnp.concatenate([w_edges, w_tri_gate], axis=1) * halves  0.97 us
  transfers between devices with their start and end apart: 8, of which 5 were waited for; matrix products, arithmetic and copies ran while one was open for 6% of the time, Pallas kernels for 23%

profile of v19, /device:TPU:0, one launch (start us, length us, event | category | flops | bytes accessed | tf_op | source)
XLA Modules:
  0.0 21.8 jit_solution(13824615558496592719)
XLA Ops:
  0.0 4.0 %collective-permute-start = (bf16[3,48,128]{2,1,0:T(8,128)(2,1)}, bf16[3,48,128]{2,1,0:T(8,128)(2,1)S(1)}, u32[]{:S(2)}, u32[]{:S(2)}) collective-permute-start(bf16[3,48,128]{2,1,0:T(8,128)(2,1)} %param.17), channel_id=1, source_target_pairs={{0,8},{1,9},{2,10},{3,11},{4,12},{5,13},{6,14},{7,15},{8,0},{9,1},... | collective-permute-start | bytes 110600 | tf_op jit(solution)/shard_map/ppermute | solution.py:513
  4.1 1.0 %maximum_multiply_fusion.weights = bf16[128,640]{1,0:T(8,128)(2,1)S(1)} fusion(bf16[128,128]{1,0:T(8,128)(2,1)} %param.22, bf16[128,512]{1,0:T(8,128)(2,1)} %param.21, bf16[640]{0:T(1024)(128)(2,1)S(1)} %select_convert_fusion), kind=kLoop, calls=%fused_computation.2 | loop fusion | flops 491520 | bytes 328960 | tf_op jit(solution)/shard_map/mul | solution.py:526
  5.1 0.6 %copy-done.11 = f32[128]{0:T(128)S(1)} copy-done((f32[128]{0:T(128)S(1)}, f32[128]{0:T(128)}, u32[]{:S(2)}) %copy-start.11) | copy-done | bytes 536
  5.8 0.8 %collective-permute-done = bf16[3,48,128]{2,1,0:T(8,128)(2,1)S(1)} collective-permute-done((bf16[3,48,128]{2,1,0:T(8,128)(2,1)}, bf16[3,48,128]{2,1,0:T(8,128)(2,1)S(1)}, u32[]{:S(2)}, u32[]{:S(2)}) %collective-permute-start) | collective-permute-done | bytes 36896 | tf_op jit(solution)/shard_map/ppermute | solution.py:513
  6.6 2.5 %collective-permute-start.2 = (bf16[6,48,128]{2,1,0:T(8,128)(2,1)S(1)}, bf16[6,48,128]{2,1,0:T(8,128)(2,1)S(1)}, u32[]{:S(2)}, u32[]{:S(2)}) collective-permute-start(bf16[6,48,128]{2,1,0:T(8,128)(2,1)S(1)} %constant_dynamic-update-slice_fusion.refs_0_), channel_id=1, source_target_pairs={{0,6},{1,7},{2,4},{3,5},{4,2},{5,3},{6,0},{7,1},{8,14},{9,15},{10,... | collective-permute-start | bytes 221192 | tf_op jit(solution)/shard_map/ppermute | solution.py:513
  9.1 0.7 %collective-permute-start.1 = (bf16[6,48,128]{2,1,0:T(8,128)(2,1)S(1)}, bf16[6,48,128]{2,1,0:T(8,128)(2,1)S(1)}, u32[]{:S(2)}, u32[]{:S(2)}) collective-permute-start(bf16[6,48,128]{2,1,0:T(8,128)(2,1)S(1)} %constant_dynamic-update-slice_fusion.refs_0_), channel_id=1, source_target_pairs={{0,4},{1,5},{2,6},{3,7},{4,0},{5,1},{6,2},{7,3},{8,12},{9,13},{10,... | collective-permute-start | bytes 221192 | tf_op jit(solution)/shard_map/ppermute | solution.py:513
  9.8 0.3 %collective-permute-start.3 = (bf16[6,48,128]{2,1,0:T(8,128)(2,1)S(1)}, bf16[6,48,128]{2,1,0:T(8,128)(2,1)S(1)}, u32[]{:S(2)}, u32[]{:S(2)}) collective-permute-start(bf16[6,48,128]{2,1,0:T(8,128)(2,1)S(1)} %constant_dynamic-update-slice_fusion.refs_0_), channel_id=1, source_target_pairs={{0,2},{1,3},{2,0},{3,1},{4,6},{5,7},{6,4},{7,5},{8,10},{9,11},{10,... | collective-permute-start | bytes 221192 | tf_op jit(solution)/shard_map/ppermute | solution.py:513
  10.1 0.2 fusion.wide_bias
  10.4 0.4 %copy-done.14 = s32[48]{0:T(128)S(1)} copy-done((s32[48]{0:T(128)S(1)}, s32[48]{0:T(128)}, u32[]{:S(2)}) %copy-start.14) | copy-done | bytes 216
  10.8 0.1 broadcast_in_dim.23.valid_column
  10.9 0.4 %shard_map.163 = (f32[1152,128]{1,0:T(8,128)S(1)}, f32[1152,128]{1,0:T(8,128)S(1)}, f32[1152,128]{1,0:T(8,128)S(1)}, f32[1152,128]{1,0:T(8,128)S(1)}, bf16[12,48...) custom-call(f32[48,128]{1,0:T(8,128)S(1)} %broadcast_in_dim.23.valid_column, f32[6,128]{1,0:T(8,128)S(1)} %stack.27.norms, ...), custom_call_target="tpu_custom_call" | custom-call | flops 1048576 | bytes 33554432 | tf_op jit(solution)/shard_map/pallas_call | solution.py:501
  11.3 0.7 %collective-permute-done.2.refs_0_ = bf16[6,48,128]{2,1,0:T(8,128)(2,1)S(1)} collective-permute-done((bf16[6,48,128]{2,1,0:T(8,128)(2,1)S(1)}, bf16[6,48,128]{2,1,0:T(8,128)(2,1)S(1)}, u32[]{:S(2)}, u32[]{:S(2)}) %collective-permute-start.2) | collective-permute-done | bytes 73760 | tf_op jit(solution)/shard_map/ppermute | solution.py:513
  12.0 0.4 %shard_map.164 = (f32[1152,128]{1,0:T(8,128)S(1)}, f32[1152,128]{1,0:T(8,128)S(1)}, f32[1152,128]{1,0:T(8,128)S(1)}, f32[1152,128]{1,0:T(8,128)S(1)}, bf16[12,48,128]{2,1,0:T(8,128)(2,1)S(1)}) custom-call(f32[48,128]{1,0:T(8,128)S(1)} %broadcast_in_dim.23.valid_column, ...), custom_call_target="tpu_custom_call", output_to_operand_aliasing={{0}: (4, {}), {1}: (5, {}), {2}: (6, {}), {3}: (7, {}), {4}... | custom-call | flops 1048576 | bytes 33554432 | tf_op jit(solution)/shard_map/pallas_call | solution.py:501
  12.4 1.0 %collective-permute-done.1.refs_0_ = bf16[6,48,128]{2,1,0:T(8,128)(2,1)S(1)} collective-permute-done((bf16[6,48,128]{2,1,0:T(8,128)(2,1)S(1)}, bf16[6,48,128]{2,1,0:T(8,128)(2,1)S(1)}, u32[]{:S(2)}, u32[]{:S(2)}) %collective-permute-start.1) | collective-permute-done | bytes 73760 | tf_op jit(solution)/shard_map/ppermute | solution.py:513
  13.4 0.7 %collective-permute-done.3.refs_1_ = bf16[6,48,128]{2,1,0:T(8,128)(2,1)S(1)} collective-permute-done((bf16[6,48,128]{2,1,0:T(8,128)(2,1)S(1)}, bf16[6,48,128]{2,1,0:T(8,128)(2,1)S(1)}, u32[]{:S(2)}, u32[]{:S(2)}) %collective-permute-start.3) | collective-permute-done | bytes 73760 | tf_op jit(solution)/shard_map/ppermute | solution.py:513
  14.2 0.6 %shard_map.165 = (f32[1152,128]{1,0:T(8,128)S(1)}, f32[1152,128]{1,0:T(8,128)S(1)}, f32[1152,128]{1,0:T(8,128)S(1)}, f32[1152,128]{1,0:T(8,128)S(1)}, bf16[12,48,128]{2,1,0:T(8,128)(2,1)S(1)}) custom-call(f32[48,128]{1,0:T(8,128)S(1)} %broadcast_in_dim.23.valid_column, ...), custom_call_target="tpu_custom_call", output_to_operand_aliasing={{0}: (5, {}), {1}: (6, {}), {2}: (7, {}), {3}: (8, {})} | custom-call | flops 1048576 | bytes 33554432 | tf_op jit(solution)/shard_map/pallas_call | solution.py:501
  14.9 1.2 %shard_map.166 = (f32[1152,128]{1,0:T(8,128)S(1)}, f32[1152,128]{1,0:T(8,128)S(1)}) custom-call(f32[1152,128]{1,0:T(8,128)S(1)} %get-tuple-element.72.left_ref.refs_0_, f32[1152,128]{1,0:T(8,128)S(1)} %get-tuple-element.75.right_ref, bf16[12,48,128]{2,1,0:T(8,128)(2,1)S(1)} %collective-permute-done.4.refs_0_), custom_call_target="tpu_custom_call" | custom-call | flops 1048576 | bytes 33554432 | tf_op jit(solution)/shard_map/pallas_call | solution.py:501
  16.1 0.1 collective-permute-done.5.received
  16.2 1.1 %shard_map.167 = (f32[1152,128]{1,0:T(8,128)S(1)}, f32[576,128]{1,0:T(8,128)S(1)}, bf16[576,128]{1,0:T(8,128)(2,1)S(1)}) custom-call(f32[6,128]{1,0:T(8,128)S(1)} %stack.27.norms, bf16[128,128]{1,0:T(8,128)(2,1)S(1)} %copy-done.1, f32[1152,128]{1,0:T(8,128)S(1)} %get-tuple-element.72.left_ref.refs_0_, ...), custom_call_target="tpu_custom_call", output_to_operand_aliasing={{0}: (7, {})} | custom-call | flops 1048576 | bytes 33554432 | tf_op jit(solution)/shard_map/pallas_call | solution.py:501
  17.3 0.4 %collective-permute-start.7 = (bf16[576,128]{1,0:T(8,128)(2,1)S(1)}, bf16[576,128]{1,0:T(8,128)(2,1)S(1)}, u32[]{:S(2)}, u32[]{:S(2)}) collective-permute-start(bf16[576,128]{1,0:T(8,128)(2,1)S(1)} %get-tuple-element.81.own_att_a), channel_id=1, source_target_pairs={{0,1},{1,0},{2,3},{3,2},{4,5},{5,4},{6,7},{7,6},{8,9},{9,8},{10,11... | collective-permute-start | bytes 442376 | tf_op jit(solution)/shard_map/ppermute | solution.py:513
  17.8 1.1 %shard_map.168.own_att_b = bf16[576,128]{1,0:T(8,128)(2,1)S(1)} custom-call(f32[6,128]{1,0:T(8,128)S(1)} %stack.27.norms, bf16[128,128]{1,0:T(8,128)(2,1)S(1)} %copy-done.1, f32[1152,128]{1,0:T(8,128)S(1)} %get-tuple-element.72.left_ref.refs_0_, f32[1152,128]{1,0:T(8,128)S(1)} %get-tuple-element.73.gate_ref.refs_1_, ...), custom_call_target="tpu_custom_call" | custom-call | flops 1048576 | bytes 33554432 | tf_op jit(solution)/shard_map/pallas_call | solution.py:501
  18.9 0.2 %collective-permute-start.6 = (bf16[576,128]{1,0:T(8,128)(2,1)S(1)}, bf16[576,128]{1,0:T(8,128)(2,1)S(1)}, u32[]{:S(2)}, u32[]{:S(2)}) collective-permute-start(bf16[576,128]{1,0:T(8,128)(2,1)S(1)} %shard_map.168.own_att_b), channel_id=1, source_target_pairs={{0,1},{1,0},{2,3},{3,2},{4,5},{5,4},{6,7},{7,6},{8,9},{9,8},{10,11... | collective-permute-start | bytes 442376 | tf_op jit(solution)/shard_map/ppermute | solution.py:513
  19.1 1.3 %shard_map.169 = (f32[3,3,48,128]{3,2,1,0:T(8,128)S(1)}, f32[144,128]{1,0:T(8,128)S(1)}, f32[144,128]{1,0:T(8,128)S(1)}, f32[144,128]{1,0:T(8,128)S(1)}) custom-call(f32[48,128]{1,0:T(8,128)S(1)} %broadcast_in_dim.23.valid_column, bf16[256,256]{1,0:T(8,128)(2,1)S(1)} %get-tuple-element.50.same_head, bf16[128,128]{1,0:T(8,128)(2,1)S(1)} %copy-done.4, ...), custom_call_target="tpu_custom_call" | custom-call | flops 1048576 | bytes 33554432 | tf_op jit(solution)/shard_map/pallas_call | solution.py:501
  20.5 1.4 %shard_map.170 = bf16[3,48,128]{2,1,0:T(8,128)(2,1)} custom-call(f32[48,128]{1,0:T(8,128)S(1)} %broadcast_in_dim.23.valid_column, bf16[256,256]{1,0:T(8,128)(2,1)S(1)} %get-tuple-element.50.same_head, bf16[128,128]{1,0:T(8,128)(2,1)S(1)} %copy-done.2, bf16[128,128]{1,0:T(8,128)(2,1)S(1)} %copy-done.3, bf16[128,128]{1,0:T(8,128)(2,1)S(1)} %copy-done.6, ...), custom_call_target="tpu_custom_call" | custom-call | flops 1048576 | bytes 33554432 | tf_op jit(solution)/shard_map/pallas_call | solution.py:501
  (40 shorter events, 0.3 us)
Async XLA Ops:
  0.0 10.1 %copy-start = (bf16[128,4]{0,1:T(4,128)(2,1)S(1)}, bf16[128,4]{0,1:T(4,128)(2,1)}, u32[]{:S(2)}) copy-start(bf16[128,4]{0,1:T(4,128)(2,1)} %param.32) | copy-start | bytes 3076
  0.0 6.6 %collective-permute-start = (bf16[3,48,128]{2,1,0:T(8,128)(2,1)}, bf16[3,48,128]{2,1,0:T(8,128)(2,1)S(1)}, u32[]{:S(2)}, u32[]{:S(2)}) collective-permute-start(bf16[3,48,128]{2,1,0:T(8,128)(2,1)} %param.17), channel_id=1, source_target_pairs={{0,8},{1,9},{2,10},{3,11},{4,12},{5,13},{6,14},{7,15},{8,0},{9,1},... | collective-permute-start | bytes 110600 | tf_op jit(solution)/shard_map/ppermute | solution.py:513
  4.1 1.0 %copy-start.7 = (bf16[3,48,128]{2,1,0:T(8,128)(2,1)S(1)}, bf16[3,48,128]{2,1,0:T(8,128)(2,1)}, u32[]{:S(2)}) copy-start(bf16[3,48,128]{2,1,0:T(8,128)(2,1)} %param.17) | copy-start | bytes 110596
  5.1 0.7 %copy-start.11 = (f32[128]{0:T(128)S(1)}, f32[128]{0:T(128)}, u32[]{:S(2)}) copy-start(f32[128]{0:T(128)} %param.24) | copy-start | bytes 1540
  5.1 0.7 %copy-start.12 = (f32[128]{0:T(128)S(1)}, f32[128]{0:T(128)}, u32[]{:S(2)}) copy-start(f32[128]{0:T(128)} %param.26) | copy-start | bytes 1540
  5.1 0.7 %copy-start.13 = (f32[128]{0:T(128)S(1)}, f32[128]{0:T(128)}, u32[]{:S(2)}) copy-start(f32[128]{0:T(128)} %param.27) | copy-start | bytes 1540
  5.1 0.7 %copy-start.8 = (f32[128]{0:T(128)S(1)}, f32[128]{0:T(128)}, u32[]{:S(2)}) copy-start(f32[128]{0:T(128)} %param.19) | copy-start | bytes 1540
  5.1 0.7 %copy-start.9 = (f32[128]{0:T(128)S(1)}, f32[128]{0:T(128)}, u32[]{:S(2)}) copy-start(f32[128]{0:T(128)} %param.20) | copy-start | bytes 1540
  5.1 0.7 %copy-start.10 = (f32[128]{0:T(128)S(1)}, f32[128]{0:T(128)}, u32[]{:S(2)}) copy-start(f32[128]{0:T(128)} %param.23) | copy-start | bytes 1540
  6.6 5.4 %collective-permute-start.2 = (bf16[6,48,128]{2,1,0:T(8,128)(2,1)S(1)}, bf16[6,48,128]{2,1,0:T(8,128)(2,1)S(1)}, u32[]{:S(2)}, u32[]{:S(2)}) collective-permute-start(bf16[6,48,128]{2,1,0:T(8,128)(2,1)S(1)} %constant_dynamic-update-slice_fusion.refs_0_), channel_id=1, source_target_pairs={{0,6},{1,7},{2,4},{3,5},{4,2},{5,3},{6,0},{7,1},{8,14},{9,15},{10,... | collective-permute-start | bytes 221192 | tf_op jit(solution)/shard_map/ppermute | solution.py:513
  9.1 4.4 %collective-permute-start.1 = (bf16[6,48,128]{2,1,0:T(8,128)(2,1)S(1)}, bf16[6,48,128]{2,1,0:T(8,128)(2,1)S(1)}, u32[]{:S(2)}, u32[]{:S(2)}) collective-permute-start(bf16[6,48,128]{2,1,0:T(8,128)(2,1)S(1)} %constant_dynamic-update-slice_fusion.refs_0_), channel_id=1, source_target_pairs={{0,4},{1,5},{2,6},{3,7},{4,0},{5,1},{6,2},{7,3},{8,12},{9,13},{10,... | collective-permute-start | bytes 221192 | tf_op jit(solution)/shard_map/ppermute | solution.py:513
  9.8 4.4 %collective-permute-start.3 = (bf16[6,48,128]{2,1,0:T(8,128)(2,1)S(1)}, bf16[6,48,128]{2,1,0:T(8,128)(2,1)S(1)}, u32[]{:S(2)}, u32[]{:S(2)}) collective-permute-start(bf16[6,48,128]{2,1,0:T(8,128)(2,1)S(1)} %constant_dynamic-update-slice_fusion.refs_0_), channel_id=1, source_target_pairs={{0,2},{1,3},{2,0},{3,1},{4,6},{5,7},{6,4},{7,5},{8,10},{9,11},{10,... | collective-permute-start | bytes 221192 | tf_op jit(solution)/shard_map/ppermute | solution.py:513
  10.1 0.7 %copy-start.14 = (s32[48]{0:T(128)S(1)}, s32[48]{0:T(128)}, u32[]{:S(2)}) copy-start(s32[48]{0:T(128)} %param.18) | copy-start | bytes 580
  13.4 1.4 %collective-permute-start.4 = (bf16[12,48,128]{2,1,0:T(8,128)(2,1)S(1)}, bf16[12,48,128]{2,1,0:T(8,128)(2,1)S(1)}, u32[]{:S(2)}, u32[]{:S(2)}) collective-permute-start(bf16[12,48,128]{2,1,0:T(8,128)(2,1)S(1)} %get-tuple-element.76), channel_id=1, source_target_pairs={{0,1},{1,0},{2,3},{3,2},{4,5},{5,4},{6,7},{7,6},{8,9},{9,8},{10,11... | collective-permute-start | bytes 442376 | tf_op jit(solution)/shard_map/ppermute | solution.py:513
  14.8 1.4 %collective-permute-start.5 = (bf16[12,48,128]{2,1,0:T(8,128)(2,1)S(1)}, bf16[12,48,128]{2,1,0:T(8,128)(2,1)S(1)}, u32[]{:S(2)}, u32[]{:S(2)}) collective-permute-start(bf16[12,48,128]{2,1,0:T(8,128)(2,1)S(1)} %get-tuple-element.78), channel_id=1, source_target_pairs={{0,1},{1,0},{2,3},{3,2},{4,5},{5,4},{6,7},{7,6},{8,9},{9,8},{10,11... | collective-permute-start | bytes 442376 | tf_op jit(solution)/shard_map/ppermute | solution.py:513
  14.9 1.4 %copy-start.1 = (bf16[128,128]{1,0:T(8,128)(2,1)S(1)}, bf16[128,128]{1,0:T(8,128)(2,1)}, u32[]{:S(2)}) copy-start(bf16[128,128]{1,0:T(8,128)(2,1)} %w_out.4) | copy-start | bytes 98308
  17.3 1.8 %collective-permute-start.7 = (bf16[576,128]{1,0:T(8,128)(2,1)S(1)}, bf16[576,128]{1,0:T(8,128)(2,1)S(1)}, u32[]{:S(2)}, u32[]{:S(2)}) collective-permute-start(bf16[576,128]{1,0:T(8,128)(2,1)S(1)} %get-tuple-element.81.own_att_a), channel_id=1, source_target_pairs={{0,1},{1,0},{2,3},{3,2},{4,5},{5,4},{6,7},{7,6},{8,9},{9,8},{10,11... | collective-permute-start | bytes 442376 | tf_op jit(solution)/shard_map/ppermute | solution.py:513
  17.8 1.3 %copy-start.2 = (bf16[128,128]{1,0:T(8,128)(2,1)S(1)}, bf16[128,128]{1,0:T(8,128)(2,1)}, u32[]{:S(2)}) copy-start(bf16[128,128]{1,0:T(8,128)(2,1)} %w_key.3) | copy-start | bytes 98308
  17.8 1.3 %copy-start.3 = (bf16[128,128]{1,0:T(8,128)(2,1)S(1)}, bf16[128,128]{1,0:T(8,128)(2,1)}, u32[]{:S(2)}) copy-start(bf16[128,128]{1,0:T(8,128)(2,1)} %w_value.3) | copy-start | bytes 98308
  17.8 1.3 %copy-start.4 = (bf16[128,128]{1,0:T(8,128)(2,1)S(1)}, bf16[128,128]{1,0:T(8,128)(2,1)}, u32[]{:S(2)}) copy-start(bf16[128,128]{1,0:T(8,128)(2,1)} %w_query.1) | copy-start | bytes 98308
  17.8 1.4 %copy-start.5 = (bf16[128,128]{1,0:T(8,128)(2,1)S(1)}, bf16[128,128]{1,0:T(8,128)(2,1)}, u32[]{:S(2)}) copy-start(bf16[128,128]{1,0:T(8,128)(2,1)} %w_gate.1) | copy-start | bytes 98308
  18.9 1.6 %collective-permute-start.6 = (bf16[576,128]{1,0:T(8,128)(2,1)S(1)}, bf16[576,128]{1,0:T(8,128)(2,1)S(1)}, u32[]{:S(2)}, u32[]{:S(2)}) collective-permute-start(bf16[576,128]{1,0:T(8,128)(2,1)S(1)} %shard_map.168.own_att_b), channel_id=1, source_target_pairs={{0,1},{1,0},{2,3},{3,2},{4,5},{5,4},{6,7},{7,6},{8,9},{9,8},{10,11... | collective-permute-start | bytes 442376 | tf_op jit(solution)/shard_map/ppermute | solution.py:513
  19.1 1.3 %copy-start.6 = (bf16[128,128]{1,0:T(8,128)(2,1)S(1)}, bf16[128,128]{1,0:T(8,128)(2,1)}, u32[]{:S(2)}) copy-start(bf16[128,128]{1,0:T(8,128)(2,1)} %w_out.5) | copy-start | bytes 98308

commit v20 on v19

--- a/solution.py
+++ b/solution.py
@@ -557,22 +557,22 @@
             {first + e: e for e in range(len(held))},
         )
 
+    beside = exchange(own, 2)
     diagonal = exchange(own, 6)
     near = exchange(own, 4)
-    beside = exchange(own, 2)
     *edges, early_right, same_head = edges_of([(own, own_blocks)], 0)
-    diagonal, edges = lax.optimization_barrier((diagonal, edges))
+    beside, edges = lax.optimization_barrier((beside, edges))
     *edges, early_right = edges_of(
-        [(diagonal, blocks_from(3))], 2 * row_count, *edges, early_right
-    )
-    near, edges, early_right, wide_bias = lax.optimization_barrier(
-        (near, edges, early_right, wide_bias)
-    )
-    early = (exchange(early_right, 1), own_blocks + blocks_from(3))
+        [(beside, blocks_from(1))], 2 * row_count, *edges, early_right
+    )
+    diagonal, edges, early_right, wide_bias = lax.optimization_barrier(
+        (diagonal, edges, early_right, wide_bias)
+    )
+    early = (exchange(early_right, 1), own_blocks + blocks_from(1))
     *edges, late_right = edges_of(
-        [(near, blocks_from(2)), (beside, blocks_from(1))], 0, *edges
-    )
-    late = (exchange(late_right, 1), blocks_from(2) + blocks_from(1))
+        [(diagonal, blocks_from(3)), (near, blocks_from(2))], 0, *edges
+    )
+    late = (exchange(late_right, 1), blocks_from(3) + blocks_from(2))
 
     left, right, gate, pairs = edges
     triangle, across = call(

time: 22 us -> 22 us (level)
  no operation moved by 1% of the time
where the time goes in v20:
time: 22 us; the launch traced here: 21.8 us
  starting transfers between devices  8.43 us (38%)
  Pallas kernels  7.5 us (34%)
  waiting for transfers between devices  3.2 us (15%)
  local copies, waits for them, and re-layouts  1.28 us (6%)
  other arithmetic  0.99 us (4%)
    ppermute x8, starting transfers between devices, exchange(): return lax.ppermute(values, 'row', [(d, d ^ bit) for d in range(devices)])  8.43 us
    pallas_call x8, Pallas kernels, call(): pl.pallas_call(kernel, out_shape=outs, in_specs=[in_vmem] * len(operands)...  7.5 us
    ppermute x8, waiting for transfers between devices, exchange(): return lax.ppermute(values, 'row', [(d, d ^ bit) for d in range(devices)])  3.2 us
    unnamed x30, local copies, waits for them, and re-layouts  1.16 us
    mul x1, other arithmetic, on_whole_complex(): edge_weights = jnp.concatenate([w_edges, w_tri_gate], axis=1) * halves  0.97 us
  transfers between devices with their start and end apart: 8, of which 5 were waited for; matrix products, arithmetic and copies ran while one was open for 6% of the time, Pallas kernels for 23%

profile of v20, /device:TPU:0, one launch (start us, length us, event | category | flops | bytes accessed | tf_op | source)
XLA Modules:
  0.0 21.8 jit_solution(3599089781908773730)
XLA Ops:
  0.0 4.0 %collective-permute-start = (bf16[3,48,128]{2,1,0:T(8,128)(2,1)}, bf16[3,48,128]{2,1,0:T(8,128)(2,1)S(1)}, u32[]{:S(2)}, u32[]{:S(2)}) collective-permute-start(bf16[3,48,128]{2,1,0:T(8,128)(2,1)} %param.17), channel_id=1, source_target_pairs={{0,8},{1,9},{2,10},{3,11},{4,12},{5,13},{6,14},{7,15},{8,0},{9,1},... | collective-permute-start | bytes 110600 | tf_op jit(solution)/shard_map/ppermute | solution.py:513
  4.1 1.0 %maximum_multiply_fusion.weights = bf16[128,640]{1,0:T(8,128)(2,1)S(1)} fusion(bf16[128,128]{1,0:T(8,128)(2,1)} %param.22, bf16[128,512]{1,0:T(8,128)(2,1)} %param.21, bf16[640]{0:T(1024)(128)(2,1)S(1)} %select_convert_fusion), kind=kLoop, calls=%fused_computation.2 | loop fusion | flops 491520 | bytes 328960 | tf_op jit(solution)/shard_map/mul | solution.py:526
  5.1 0.6 %copy-done.11 = f32[128]{0:T(128)S(1)} copy-done((f32[128]{0:T(128)S(1)}, f32[128]{0:T(128)}, u32[]{:S(2)}) %copy-start.11) | copy-done | bytes 536
  5.8 0.8 %collective-permute-done = bf16[3,48,128]{2,1,0:T(8,128)(2,1)S(1)} collective-permute-done((bf16[3,48,128]{2,1,0:T(8,128)(2,1)}, bf16[3,48,128]{2,1,0:T(8,128)(2,1)S(1)}, u32[]{:S(2)}, u32[]{:S(2)}) %collective-permute-start) | collective-permute-done | bytes 36896 | tf_op jit(solution)/shard_map/ppermute | solution.py:513
  6.6 1.8 %collective-permute-start.2 = (bf16[6,48,128]{2,1,0:T(8,128)(2,1)S(1)}, bf16[6,48,128]{2,1,0:T(8,128)(2,1)S(1)}, u32[]{:S(2)}, u32[]{:S(2)}) collective-permute-start(bf16[6,48,128]{2,1,0:T(8,128)(2,1)S(1)} %constant_dynamic-update-slice_fusion.refs_0_), channel_id=1, source_target_pairs={{0,2},{1,3},{2,0},{3,1},{4,6},{5,7},{6,4},{7,5},{8,10},{9,11},{10,... | collective-permute-start | bytes 221192 | tf_op jit(solution)/shard_map/ppermute | solution.py:513
  8.4 1.3 %collective-permute-start.1 = (bf16[6,48,128]{2,1,0:T(8,128)(2,1)S(1)}, bf16[6,48,128]{2,1,0:T(8,128)(2,1)S(1)}, u32[]{:S(2)}, u32[]{:S(2)}) collective-permute-start(bf16[6,48,128]{2,1,0:T(8,128)(2,1)S(1)} %constant_dynamic-update-slice_fusion.refs_0_), channel_id=1, source_target_pairs={{0,6},{1,7},{2,4},{3,5},{4,2},{5,3},{6,0},{7,1},{8,14},{9,15},{10,... | collective-permute-start | bytes 221192 | tf_op jit(solution)/shard_map/ppermute | solution.py:513
  9.6 0.5 %collective-permute-start.3 = (bf16[6,48,128]{2,1,0:T(8,128)(2,1)S(1)}, bf16[6,48,128]{2,1,0:T(8,128)(2,1)S(1)}, u32[]{:S(2)}, u32[]{:S(2)}) collective-permute-start(bf16[6,48,128]{2,1,0:T(8,128)(2,1)S(1)} %constant_dynamic-update-slice_fusion.refs_0_), channel_id=1, source_target_pairs={{0,4},{1,5},{2,6},{3,7},{4,0},{5,1},{6,2},{7,3},{8,12},{9,13},{10,... | collective-permute-start | bytes 221192 | tf_op jit(solution)/shard_map/ppermute | solution.py:513
  10.1 0.2 fusion.wide_bias
  10.4 0.4 %copy-done.14 = s32[48]{0:T(128)S(1)} copy-done((s32[48]{0:T(128)S(1)}, s32[48]{0:T(128)}, u32[]{:S(2)}) %copy-start.14) | copy-done | bytes 216
  10.9 0.4 %shard_map.163 = (f32[1152,128]{1,0:T(8,128)S(1)}, f32[1152,128]{1,0:T(8,128)S(1)}, f32[1152,128]{1,0:T(8,128)S(1)}, f32[1152,128]{1,0:T(8,128)S(1)}, bf16[12,48...) custom-call(f32[48,128]{1,0:T(8,128)S(1)} %broadcast_in_dim.23.valid_column, f32[6,128]{1,0:T(8,128)S(1)} %stack.27.norms, ...), custom_call_target="tpu_custom_call" | custom-call | flops 1048576 | bytes 33554432 | tf_op jit(solution)/shard_map/pallas_call | solution.py:501
  11.3 0.5 %collective-permute-done.2.refs_0_ = bf16[6,48,128]{2,1,0:T(8,128)(2,1)S(1)} collective-permute-done((bf16[6,48,128]{2,1,0:T(8,128)(2,1)S(1)}, bf16[6,48,128]{2,1,0:T(8,128)(2,1)S(1)}, u32[]{:S(2)}, u32[]{:S(2)}) %collective-permute-start.2) | collective-permute-done | bytes 73760 | tf_op jit(solution)/shard_map/ppermute | solution.py:513
  11.8 0.4 %shard_map.164 = (f32[1152,128]{1,0:T(8,128)S(1)}, f32[1152,128]{1,0:T(8,128)S(1)}, f32[1152,128]{1,0:T(8,128)S(1)}, f32[1152,128]{1,0:T(8,128)S(1)}, bf16[12,48,128]{2,1,0:T(8,128)(2,1)S(1)}) custom-call(f32[48,128]{1,0:T(8,128)S(1)} %broadcast_in_dim.23.valid_column, ...), custom_call_target="tpu_custom_call", output_to_operand_aliasing={{0}: (4, {}), {1}: (5, {}), {2}: (6, {}), {3}: (7, {}), {4}... | custom-call | flops 1048576 | bytes 33554432 | tf_op jit(solution)/shard_map/pallas_call | solution.py:501
  12.2 1.4 %collective-permute-done.1.refs_0_ = bf16[6,48,128]{2,1,0:T(8,128)(2,1)S(1)} collective-permute-done((bf16[6,48,128]{2,1,0:T(8,128)(2,1)S(1)}, bf16[6,48,128]{2,1,0:T(8,128)(2,1)S(1)}, u32[]{:S(2)}, u32[]{:S(2)}) %collective-permute-start.1) | collective-permute-done | bytes 73760 | tf_op jit(solution)/shard_map/ppermute | solution.py:513
  13.6 0.4 %collective-permute-done.3.refs_1_ = bf16[6,48,128]{2,1,0:T(8,128)(2,1)S(1)} collective-permute-done((bf16[6,48,128]{2,1,0:T(8,128)(2,1)S(1)}, bf16[6,48,128]{2,1,0:T(8,128)(2,1)S(1)}, u32[]{:S(2)}, u32[]{:S(2)}) %collective-permute-start.3) | collective-permute-done | bytes 73760 | tf_op jit(solution)/shard_map/ppermute | solution.py:513
  14.0 0.6 %shard_map.165 = (f32[1152,128]{1,0:T(8,128)S(1)}, f32[1152,128]{1,0:T(8,128)S(1)}, f32[1152,128]{1,0:T(8,128)S(1)}, f32[1152,128]{1,0:T(8,128)S(1)}, bf16[12,48,128]{2,1,0:T(8,128)(2,1)S(1)}) custom-call(f32[48,128]{1,0:T(8,128)S(1)} %broadcast_in_dim.23.valid_column, ...), custom_call_target="tpu_custom_call", output_to_operand_aliasing={{0}: (5, {}), {1}: (6, {}), {2}: (7, {}), {3}: (8, {})} | custom-call | flops 1048576 | bytes 33554432 | tf_op jit(solution)/shard_map/pallas_call | solution.py:501
  14.6 0.2 collective-permute-start.5
  14.8 0.2 collective-permute-done.4.refs_0_
  15.0 1.2 %shard_map.166 = (f32[1152,128]{1,0:T(8,128)S(1)}, f32[1152,128]{1,0:T(8,128)S(1)}) custom-call(f32[1152,128]{1,0:T(8,128)S(1)} %get-tuple-element.72.left_ref.refs_0_, f32[1152,128]{1,0:T(8,128)S(1)} %get-tuple-element.75.right_ref, bf16[12,48,128]{2,1,0:T(8,128)(2,1)S(1)} %collective-permute-done.4.refs_0_), custom_call_target="tpu_custom_call" | custom-call | flops 1048576 | bytes 33554432 | tf_op jit(solution)/shard_map/pallas_call | solution.py:501
  16.2 1.1 %shard_map.167 = (f32[1152,128]{1,0:T(8,128)S(1)}, f32[576,128]{1,0:T(8,128)S(1)}, bf16[576,128]{1,0:T(8,128)(2,1)S(1)}) custom-call(f32[6,128]{1,0:T(8,128)S(1)} %stack.27.norms, bf16[128,128]{1,0:T(8,128)(2,1)S(1)} %copy-done.1, f32[1152,128]{1,0:T(8,128)S(1)} %get-tuple-element.72.left_ref.refs_0_, ...), custom_call_target="tpu_custom_call", output_to_operand_aliasing={{0}: (7, {})} | custom-call | flops 1048576 | bytes 33554432 | tf_op jit(solution)/shard_map/pallas_call | solution.py:501
  17.3 0.3 %collective-permute-start.7 = (bf16[576,128]{1,0:T(8,128)(2,1)S(1)}, bf16[576,128]{1,0:T(8,128)(2,1)S(1)}, u32[]{:S(2)}, u32[]{:S(2)}) collective-permute-start(bf16[576,128]{1,0:T(8,128)(2,1)S(1)} %get-tuple-element.81.own_att_a), channel_id=1, source_target_pairs={{0,1},{1,0},{2,3},{3,2},{4,5},{5,4},{6,7},{7,6},{8,9},{9,8},{10,11... | collective-permute-start | bytes 442376 | tf_op jit(solution)/shard_map/ppermute | solution.py:513
  17.6 1.1 %shard_map.168.own_att_b = bf16[576,128]{1,0:T(8,128)(2,1)S(1)} custom-call(f32[6,128]{1,0:T(8,128)S(1)} %stack.27.norms, bf16[128,128]{1,0:T(8,128)(2,1)S(1)} %copy-done.1, f32[1152,128]{1,0:T(8,128)S(1)} %get-tuple-element.72.left_ref.refs_0_, f32[1152,128]{1,0:T(8,128)S(1)} %get-tuple-element.73.gate_ref.refs_1_, ...), custom_call_target="tpu_custom_call" | custom-call | flops 1048576 | bytes 33554432 | tf_op jit(solution)/shard_map/pallas_call | solution.py:501
  18.7 0.4 %collective-permute-start.6 = (bf16[576,128]{1,0:T(8,128)(2,1)S(1)}, bf16[576,128]{1,0:T(8,128)(2,1)S(1)}, u32[]{:S(2)}, u32[]{:S(2)}) collective-permute-start(bf16[576,128]{1,0:T(8,128)(2,1)S(1)} %shard_map.168.own_att_b), channel_id=1, source_target_pairs={{0,1},{1,0},{2,3},{3,2},{4,5},{5,4},{6,7},{7,6},{8,9},{9,8},{10,11... | collective-permute-start | bytes 442376 | tf_op jit(solution)/shard_map/ppermute | solution.py:513
  19.1 1.3 %shard_map.169 = (f32[3,3,48,128]{3,2,1,0:T(8,128)S(1)}, f32[144,128]{1,0:T(8,128)S(1)}, f32[144,128]{1,0:T(8,128)S(1)}, f32[144,128]{1,0:T(8,128)S(1)}) custom-call(f32[48,128]{1,0:T(8,128)S(1)} %broadcast_in_dim.23.valid_column, bf16[256,256]{1,0:T(8,128)(2,1)S(1)} %get-tuple-element.50.same_head, bf16[128,128]{1,0:T(8,128)(2,1)S(1)} %copy-done.4, ...), custom_call_target="tpu_custom_call" | custom-call | flops 1048576 | bytes 33554432 | tf_op jit(solution)/shard_map/pallas_call | solution.py:501
  20.4 1.4 %shard_map.170 = bf16[3,48,128]{2,1,0:T(8,128)(2,1)} custom-call(f32[48,128]{1,0:T(8,128)S(1)} %broadcast_in_dim.23.valid_column, bf16[256,256]{1,0:T(8,128)(2,1)S(1)} %get-tuple-element.50.same_head, bf16[128,128]{1,0:T(8,128)(2,1)S(1)} %copy-done.2, bf16[128,128]{1,0:T(8,128)(2,1)S(1)} %copy-done.3, bf16[128,128]{1,0:T(8,128)(2,1)S(1)} %copy-done.6, ...), custom_call_target="tpu_custom_call" | custom-call | flops 1048576 | bytes 33554432 | tf_op jit(solution)/shard_map/pallas_call | solution.py:501
  (40 shorter events, 0.3 us)
Async XLA Ops:
  0.0 10.1 %copy-start = (bf16[128,4]{0,1:T(4,128)(2,1)S(1)}, bf16[128,4]{0,1:T(4,128)(2,1)}, u32[]{:S(2)}) copy-start(bf16[128,4]{0,1:T(4,128)(2,1)} %param.32) | copy-start | bytes 3076
  0.0 6.6 %collective-permute-start = (bf16[3,48,128]{2,1,0:T(8,128)(2,1)}, bf16[3,48,128]{2,1,0:T(8,128)(2,1)S(1)}, u32[]{:S(2)}, u32[]{:S(2)}) collective-permute-start(bf16[3,48,128]{2,1,0:T(8,128)(2,1)} %param.17), channel_id=1, source_target_pairs={{0,8},{1,9},{2,10},{3,11},{4,12},{5,13},{6,14},{7,15},{8,0},{9,1},... | collective-permute-start | bytes 110600 | tf_op jit(solution)/shard_map/ppermute | solution.py:513
  4.1 1.0 %copy-start.7 = (bf16[3,48,128]{2,1,0:T(8,128)(2,1)S(1)}, bf16[3,48,128]{2,1,0:T(8,128)(2,1)}, u32[]{:S(2)}) copy-start(bf16[3,48,128]{2,1,0:T(8,128)(2,1)} %param.17) | copy-start | bytes 110596
  5.1 0.7 %copy-start.11 = (f32[128]{0:T(128)S(1)}, f32[128]{0:T(128)}, u32[]{:S(2)}) copy-start(f32[128]{0:T(128)} %param.24) | copy-start | bytes 1540
  5.1 0.7 %copy-start.12 = (f32[128]{0:T(128)S(1)}, f32[128]{0:T(128)}, u32[]{:S(2)}) copy-start(f32[128]{0:T(128)} %param.26) | copy-start | bytes 1540
  5.1 0.7 %copy-start.13 = (f32[128]{0:T(128)S(1)}, f32[128]{0:T(128)}, u32[]{:S(2)}) copy-start(f32[128]{0:T(128)} %param.27) | copy-start | bytes 1540
  5.1 0.7 %copy-start.8 = (f32[128]{0:T(128)S(1)}, f32[128]{0:T(128)}, u32[]{:S(2)}) copy-start(f32[128]{0:T(128)} %param.19) | copy-start | bytes 1540
  5.1 0.7 %copy-start.9 = (f32[128]{0:T(128)S(1)}, f32[128]{0:T(128)}, u32[]{:S(2)}) copy-start(f32[128]{0:T(128)} %param.20) | copy-start | bytes 1540
  5.1 0.7 %copy-start.10 = (f32[128]{0:T(128)S(1)}, f32[128]{0:T(128)}, u32[]{:S(2)}) copy-start(f32[128]{0:T(128)} %param.23) | copy-start | bytes 1540
  6.6 5.2 %collective-permute-start.2 = (bf16[6,48,128]{2,1,0:T(8,128)(2,1)S(1)}, bf16[6,48,128]{2,1,0:T(8,128)(2,1)S(1)}, u32[]{:S(2)}, u32[]{:S(2)}) collective-permute-start(bf16[6,48,128]{2,1,0:T(8,128)(2,1)S(1)} %constant_dynamic-update-slice_fusion.refs_0_), channel_id=1, source_target_pairs={{0,2},{1,3},{2,0},{3,1},{4,6},{5,7},{6,4},{7,5},{8,10},{9,11},{10,... | collective-permute-start | bytes 221192 | tf_op jit(solution)/shard_map/ppermute | solution.py:513
  8.4 5.3 %collective-permute-start.1 = (bf16[6,48,128]{2,1,0:T(8,128)(2,1)S(1)}, bf16[6,48,128]{2,1,0:T(8,128)(2,1)S(1)}, u32[]{:S(2)}, u32[]{:S(2)}) collective-permute-start(bf16[6,48,128]{2,1,0:T(8,128)(2,1)S(1)} %constant_dynamic-update-slice_fusion.refs_0_), channel_id=1, source_target_pairs={{0,6},{1,7},{2,4},{3,5},{4,2},{5,3},{6,0},{7,1},{8,14},{9,15},{10,... | collective-permute-start | bytes 221192 | tf_op jit(solution)/shard_map/ppermute | solution.py:513
  9.6 4.4 %collective-permute-start.3 = (bf16[6,48,128]{2,1,0:T(8,128)(2,1)S(1)}, bf16[6,48,128]{2,1,0:T(8,128)(2,1)S(1)}, u32[]{:S(2)}, u32[]{:S(2)}) collective-permute-start(bf16[6,48,128]{2,1,0:T(8,128)(2,1)S(1)} %constant_dynamic-update-slice_fusion.refs_0_), channel_id=1, source_target_pairs={{0,4},{1,5},{2,6},{3,7},{4,0},{5,1},{6,2},{7,3},{8,12},{9,13},{10,... | collective-permute-start | bytes 221192 | tf_op jit(solution)/shard_map/ppermute | solution.py:513
  10.1 0.7 %copy-start.14 = (s32[48]{0:T(128)S(1)}, s32[48]{0:T(128)}, u32[]{:S(2)}) copy-start(s32[48]{0:T(128)} %param.18) | copy-start | bytes 580
  13.6 1.4 %collective-permute-start.4 = (bf16[12,48,128]{2,1,0:T(8,128)(2,1)S(1)}, bf16[12,48,128]{2,1,0:T(8,128)(2,1)S(1)}, u32[]{:S(2)}, u32[]{:S(2)}) collective-permute-start(bf16[12,48,128]{2,1,0:T(8,128)(2,1)S(1)} %get-tuple-element.76), channel_id=1, source_target_pairs={{0,1},{1,0},{2,3},{3,2},{4,5},{5,4},{6,7},{7,6},{8,9},{9,8},{10,11... | collective-permute-start | bytes 442376 | tf_op jit(solution)/shard_map/ppermute | solution.py:513
  14.6 1.6 %collective-permute-start.5 = (bf16[12,48,128]{2,1,0:T(8,128)(2,1)S(1)}, bf16[12,48,128]{2,1,0:T(8,128)(2,1)S(1)}, u32[]{:S(2)}, u32[]{:S(2)}) collective-permute-start(bf16[12,48,128]{2,1,0:T(8,128)(2,1)S(1)} %get-tuple-element.78), channel_id=1, source_target_pairs={{0,1},{1,0},{2,3},{3,2},{4,5},{5,4},{6,7},{7,6},{8,9},{9,8},{10,11... | collective-permute-start | bytes 442376 | tf_op jit(solution)/shard_map/ppermute | solution.py:513
  15.0 1.2 %copy-start.1 = (bf16[128,128]{1,0:T(8,128)(2,1)S(1)}, bf16[128,128]{1,0:T(8,128)(2,1)}, u32[]{:S(2)}) copy-start(bf16[128,128]{1,0:T(8,128)(2,1)} %w_out.4) | copy-start | bytes 98308
  17.3 1.8 %collective-permute-start.7 = (bf16[576,128]{1,0:T(8,128)(2,1)S(1)}, bf16[576,128]{1,0:T(8,128)(2,1)S(1)}, u32[]{:S(2)}, u32[]{:S(2)}) collective-permute-start(bf16[576,128]{1,0:T(8,128)(2,1)S(1)} %get-tuple-element.81.own_att_a), channel_id=1, source_target_pairs={{0,1},{1,0},{2,3},{3,2},{4,5},{5,4},{6,7},{7,6},{8,9},{9,8},{10,11... | collective-permute-start | bytes 442376 | tf_op jit(solution)/shard_map/ppermute | solution.py:513
  17.6 1.5 %copy-start.2 = (bf16[128,128]{1,0:T(8,128)(2,1)S(1)}, bf16[128,128]{1,0:T(8,128)(2,1)}, u32[]{:S(2)}) copy-start(bf16[128,128]{1,0:T(8,128)(2,1)} %w_key.3) | copy-start | bytes 98308
  17.6 1.5 %copy-start.3 = (bf16[128,128]{1,0:T(8,128)(2,1)S(1)}, bf16[128,128]{1,0:T(8,128)(2,1)}, u32[]{:S(2)}) copy-start(bf16[128,128]{1,0:T(8,128)(2,1)} %w_value.3) | copy-start | bytes 98308
  17.6 1.5 %copy-start.4 = (bf16[128,128]{1,0:T(8,128)(2,1)S(1)}, bf16[128,128]{1,0:T(8,128)(2,1)}, u32[]{:S(2)}) copy-start(bf16[128,128]{1,0:T(8,128)(2,1)} %w_query.1) | copy-start | bytes 98308
  17.6 1.5 %copy-start.5 = (bf16[128,128]{1,0:T(8,128)(2,1)S(1)}, bf16[128,128]{1,0:T(8,128)(2,1)}, u32[]{:S(2)}) copy-start(bf16[128,128]{1,0:T(8,128)(2,1)} %w_gate.1) | copy-start | bytes 98308
  18.7 1.7 %collective-permute-start.6 = (bf16[576,128]{1,0:T(8,128)(2,1)S(1)}, bf16[576,128]{1,0:T(8,128)(2,1)S(1)}, u32[]{:S(2)}, u32[]{:S(2)}) collective-permute-start(bf16[576,128]{1,0:T(8,128)(2,1)S(1)} %shard_map.168.own_att_b), channel_id=1, source_target_pairs={{0,1},{1,0},{2,3},{3,2},{4,5},{5,4},{6,7},{7,6},{8,9},{9,8},{10,11... | collective-permute-start | bytes 442376 | tf_op jit(solution)/shard_map/ppermute | solution.py:513
  19.1 1.3 %copy-start.6 = (bf16[128,128]{1,0:T(8,128)(2,1)S(1)}, bf16[128,128]{1,0:T(8,128)(2,1)}, u32[]{:S(2)}) copy-start(bf16[128,128]{1,0:T(8,128)(2,1)} %w_out.5) | copy-start | bytes 98308

commit v21 on v16

--- a/solution.py
+++ b/solution.py
@@ -225,8 +225,7 @@
                 triangle_ref[pl.ds(place, chips, stride=2 * row_count), :] = rounded(sums[m][0])
 
 
-def near_triangle_kernel(row_count, chips, chunk, pieces, left_ref, right_ref, *refs):
-    received, (triangle_ref, across_ref) = refs[:-2], refs[-2:]
+def near_triangle_kernel(row_count, chips, chunk, left_ref, right_ref, triangle_ref):
     _, core = chip_and_core()
 
     def some_rows(step, carry):
@@ -236,9 +235,6 @@
         )
         return carry
 
-    for ref, blocks in zip(received, pieces):
-        for n, (chip, r) in enumerate(rows_of_blocks(row_count, blocks)):
-            place_right(across_ref, chips, chip, r, ref[n])
     lax.fori_loop(0, row_count * chips // chunk, some_rows, 0)
 
 
@@ -275,16 +271,17 @@
     left_ref,
     gate_ref,
     pairs_ref,
-    received,
+    early,
+    late,
     triangle_ref,
-    held_across,
     across_ref,
     after_ref,
     att_ref,
     scratch_ref,
 ):
-    for n, (chip, r) in enumerate(rows_of_blocks(row_count, blocks)):
-        place_right(across_ref, chips, chip, r, received[n])
+    for received, senders in zip((early, late), blocks):
+        for n, (chip, r) in enumerate(rows_of_blocks(row_count, senders)):
+            place_right(across_ref, chips, chip, r, received[n])
     first = first_chip(chips, 0) * row_count
     refs = (left_ref, gate_ref, pairs_ref, triangle_ref, across_ref, scratch_ref)
     after_ref[...], att_ref[...] = attention_inputs(
@@ -565,20 +562,16 @@
     *edges, early_right = edges_of(
         [(diagonal, blocks_from(3))], 2 * row_count, *edges, early_right
     )
-    beside, edges, early_right, wide_bias = lax.optimization_barrier(
-        (beside, edges, early_right, wide_bias)
-    )
     early = (exchange(early_right, 1), own_blocks + blocks_from(3))
-    *edges, late_right = edges_of(
-        [(beside, blocks_from(1)), (near, blocks_from(2))], 0, *edges
-    )
+    beside, edges, wide_bias = lax.optimization_barrier((beside, edges, wide_bias))
+    *edges, late_right = edges_of([(beside, blocks_from(1))], 0, *edges)
+    near, edges, late_right = lax.optimization_barrier((near, edges, late_right))
+    *edges, late_right = edges_of([(near, blocks_from(2))], 2 * row_count, *edges, late_right)
     late = (exchange(late_right, 1), blocks_from(1) + blocks_from(2))
 
     left, right, gate, pairs = edges
-    triangle, across = call(
-        functools.partial(near_triangle_kernel, row_count, chips, half // 2, [early[1]]),
-        (tall, tall),
-        (left, right, early[0]),
+    triangle = call(
+        functools.partial(near_triangle_kernel, row_count, chips, half // 2), tall, (left, right)
     )
     part = half // 2 * res
     in_part, own_shape = shaped(f32, part, channels), shaped(f32, row_count * res, channels)
@@ -586,10 +579,9 @@
     shared = (norms, w_tri_out, left, gate, pairs)
     scratch = (pltpu.VMEM((part, channels), f32),)
     across, after_a, att_a = call(
-        functools.partial(own_inputs_kernel, row_count, chips, late[1]),
+        functools.partial(own_inputs_kernel, row_count, chips, (early[1], late[1])),
         (tall, in_part, att_part),
-        shared + (late[0], triangle, across),
-        {7: 0},
+        shared + (early[0], late[0], triangle),
         scratch=scratch,
     )
     far_att_a = exchange(att_a, 1)

time: 21.8 us -> 22.6 us (1.037)
  starting transfers between devices: 8.3 us -> 8.79 us
  Pallas kernels: 7.5 us -> 7.73 us
    ppermute x8, starting transfers between devices: 8.3 us -> 8.79 us  [exchange(): return lax.ppermute(values, 'row', [(d, d ^ bit) for d in range(devices)])]
    pallas_call x8 -> x9, Pallas kernels: 7.5 us -> 7.73 us  [call(): pl.pallas_call(kernel, out_shape=outs, in_specs=[in_vmem] * len(operands)...]
  transfers between devices with their start and end apart: 8 -> 8, of which waited for: 5 -> 3; matrix products, arithmetic and copies ran while one was open for 6% -> 6% of each run, Pallas kernels for 23% -> 21%
where the time goes in v21:
time: 22.6 us; the launch traced here: 22.5 us
  starting transfers between devices  8.79 us (39%)
  Pallas kernels  7.73 us (34%)
  waiting for transfers between devices  3.26 us (14%)
  local copies, waits for them, and re-layouts  1.28 us (6%)
  other arithmetic  0.99 us (4%)
  between operations  0.23 us (1%)
    ppermute x8, starting transfers between devices, exchange(): return lax.ppermute(values, 'row', [(d, d ^ bit) for d in range(devices)])  8.79 us
    pallas_call x9, Pallas kernels, call(): pl.pallas_call(kernel, out_shape=outs, in_specs=[in_vmem] * len(operands)...  7.73 us
    ppermute x8, waiting for transfers between devices, exchange(): return lax.ppermute(values, 'row', [(d, d ^ bit) for d in range(devices)])  3.26 us
    unnamed x30, local copies, waits for them, and re-layouts  1.16 us
    mul x1, other arithmetic, on_whole_complex(): edge_weights = jnp.concatenate([w_edges, w_tri_gate], axis=1) * halves  0.97 us
  transfers between devices with their start and end apart: 8, of which 3 were waited for; matrix products, arithmetic and copies ran while one was open for 6% of the time, Pallas kernels for 21%

profile of v21, /device:TPU:0, one launch (start us, length us, event | category | flops | bytes accessed | tf_op | source)
XLA Modules:
  0.0 22.5 jit_solution(121282561499615933)
XLA Ops:
  0.0 4.0 %collective-permute-start = (bf16[3,48,128]{2,1,0:T(8,128)(2,1)}, bf16[3,48,128]{2,1,0:T(8,128)(2,1)S(1)}, u32[]{:S(2)}, u32[]{:S(2)}) collective-permute-start(bf16[3,48,128]{2,1,0:T(8,128)(2,1)} %param.17), channel_id=1, source_target_pairs={{0,8},{1,9},{2,10},{3,11},{4,12},{5,13},{6,14},{7,15},{8,0},{9,1},... | collective-permute-start | bytes 110600 | tf_op jit(solution)/shard_map/ppermute | solution.py:510
  4.1 1.0 %maximum_multiply_fusion.weights = bf16[128,640]{1,0:T(8,128)(2,1)S(1)} fusion(bf16[128,128]{1,0:T(8,128)(2,1)} %param.22, bf16[128,512]{1,0:T(8,128)(2,1)} %param.21, bf16[640]{0:T(1024)(128)(2,1)S(1)} %select_convert_fusion), kind=kLoop, calls=%fused_computation.2 | loop fusion | flops 491520 | bytes 328960 | tf_op jit(solution)/shard_map/mul | solution.py:523
  5.1 0.6 %copy-done.11 = f32[128]{0:T(128)S(1)} copy-done((f32[128]{0:T(128)S(1)}, f32[128]{0:T(128)}, u32[]{:S(2)}) %copy-start.11) | copy-done | bytes 536
  5.8 0.8 %collective-permute-done = bf16[3,48,128]{2,1,0:T(8,128)(2,1)S(1)} collective-permute-done((bf16[3,48,128]{2,1,0:T(8,128)(2,1)}, bf16[3,48,128]{2,1,0:T(8,128)(2,1)S(1)}, u32[]{:S(2)}, u32[]{:S(2)}) %collective-permute-start) | collective-permute-done | bytes 36896 | tf_op jit(solution)/shard_map/ppermute | solution.py:510
  6.6 1.6 %collective-permute-start.3 = (bf16[6,48,128]{2,1,0:T(8,128)(2,1)S(1)}, bf16[6,48,128]{2,1,0:T(8,128)(2,1)S(1)}, u32[]{:S(2)}, u32[]{:S(2)}) collective-permute-start(bf16[6,48,128]{2,1,0:T(8,128)(2,1)S(1)} %constant_dynamic-update-slice_fusion.refs_0_), channel_id=1, source_target_pairs={{0,4},{1,5},{2,6},{3,7},{4,0},{5,1},{6,2},{7,3},{8,12},{9,13},{10,... | collective-permute-start | bytes 221192 | tf_op jit(solution)/shard_map/ppermute | solution.py:510
  8.2 1.6 %collective-permute-start.2 = (bf16[6,48,128]{2,1,0:T(8,128)(2,1)S(1)}, bf16[6,48,128]{2,1,0:T(8,128)(2,1)S(1)}, u32[]{:S(2)}, u32[]{:S(2)}) collective-permute-start(bf16[6,48,128]{2,1,0:T(8,128)(2,1)S(1)} %constant_dynamic-update-slice_fusion.refs_0_), channel_id=1, source_target_pairs={{0,6},{1,7},{2,4},{3,5},{4,2},{5,3},{6,0},{7,1},{8,14},{9,15},{10,... | collective-permute-start | bytes 221192 | tf_op jit(solution)/shard_map/ppermute | solution.py:510
  9.8 0.3 %collective-permute-start.1 = (bf16[6,48,128]{2,1,0:T(8,128)(2,1)S(1)}, bf16[6,48,128]{2,1,0:T(8,128)(2,1)S(1)}, u32[]{:S(2)}, u32[]{:S(2)}) collective-permute-start(bf16[6,48,128]{2,1,0:T(8,128)(2,1)S(1)} %constant_dynamic-update-slice_fusion.refs_0_), channel_id=1, source_target_pairs={{0,2},{1,3},{2,0},{3,1},{4,6},{5,7},{6,4},{7,5},{8,10},{9,11},{10,... | collective-permute-start | bytes 221192 | tf_op jit(solution)/shard_map/ppermute | solution.py:510
  10.1 0.2 fusion.wide_bias
  10.4 0.4 %copy-done.14 = s32[48]{0:T(128)S(1)} copy-done((s32[48]{0:T(128)S(1)}, s32[48]{0:T(128)}, u32[]{:S(2)}) %copy-start.14) | copy-done | bytes 216
  10.8 0.1 broadcast_in_dim.23.valid_column
  10.9 0.4 %shard_map.163 = (f32[1152,128]{1,0:T(8,128)S(1)}, f32[1152,128]{1,0:T(8,128)S(1)}, f32[1152,128]{1,0:T(8,128)S(1)}, f32[1152,128]{1,0:T(8,128)S(1)}, bf16[12,48...) custom-call(f32[48,128]{1,0:T(8,128)S(1)} %broadcast_in_dim.23.valid_column, f32[6,128]{1,0:T(8,128)S(1)} %stack.27.norms, ...), custom_call_target="tpu_custom_call" | custom-call | flops 1048576 | bytes 33554432 | tf_op jit(solution)/shard_map/pallas_call | solution.py:498
  11.3 2.1 %collective-permute-done.2.refs_0_ = bf16[6,48,128]{2,1,0:T(8,128)(2,1)S(1)} collective-permute-done((bf16[6,48,128]{2,1,0:T(8,128)(2,1)S(1)}, bf16[6,48,128]{2,1,0:T(8,128)(2,1)S(1)}, u32[]{:S(2)}, u32[]{:S(2)}) %collective-permute-start.2) | collective-permute-done | bytes 73760 | tf_op jit(solution)/shard_map/ppermute | solution.py:510
  13.4 0.4 %shard_map.164 = (f32[1152,128]{1,0:T(8,128)S(1)}, f32[1152,128]{1,0:T(8,128)S(1)}, f32[1152,128]{1,0:T(8,128)S(1)}, f32[1152,128]{1,0:T(8,128)S(1)}, bf16[12,48,128]{2,1,0:T(8,128)(2,1)S(1)}) custom-call(f32[48,128]{1,0:T(8,128)S(1)} %broadcast_in_dim.23.valid_column, ...), custom_call_target="tpu_custom_call", output_to_operand_aliasing={{0}: (4, {}), {1}: (5, {}), {2}: (6, {}), {3}: (7, {}), {4}... | custom-call | flops 1048576 | bytes 33554432 | tf_op jit(solution)/shard_map/pallas_call | solution.py:498
  13.8 0.4 %collective-permute-done.1.refs_0_ = bf16[6,48,128]{2,1,0:T(8,128)(2,1)S(1)} collective-permute-done((bf16[6,48,128]{2,1,0:T(8,128)(2,1)S(1)}, bf16[6,48,128]{2,1,0:T(8,128)(2,1)S(1)}, u32[]{:S(2)}, u32[]{:S(2)}) %collective-permute-start.1) | collective-permute-done | bytes 73760 | tf_op jit(solution)/shard_map/ppermute | solution.py:510
  14.2 0.4 %shard_map.165 = (f32[1152,128]{1,0:T(8,128)S(1)}, f32[1152,128]{1,0:T(8,128)S(1)}, f32[1152,128]{1,0:T(8,128)S(1)}, f32[1152,128]{1,0:T(8,128)S(1)}, bf16[12,48,128]{2,1,0:T(8,128)(2,1)S(1)}) custom-call(f32[48,128]{1,0:T(8,128)S(1)} %broadcast_in_dim.23.valid_column, ...), custom_call_target="tpu_custom_call", output_to_operand_aliasing={{0}: (4, {}), {1}: (5, {}), {2}: (6, {}), {3}: (7, {})} | custom-call | flops 1048576 | bytes 33554432 | tf_op jit(solution)/shard_map/pallas_call | solution.py:498
  14.6 0.4 %shard_map.166 = (f32[1152,128]{1,0:T(8,128)S(1)}, f32[1152,128]{1,0:T(8,128)S(1)}, f32[1152,128]{1,0:T(8,128)S(1)}, f32[1152,128]{1,0:T(8,128)S(1)}, bf16[12,48,128]{2,1,0:T(8,128)(2,1)S(1)}) custom-call(f32[48,128]{1,0:T(8,128)S(1)} %broadcast_in_dim.23.valid_column, ...), custom_call_target="tpu_custom_call", output_to_operand_aliasing={{0}: (4, {}), {1}: (5, {}), {2}: (6, {}), {3}: (7, {}), {4}... | custom-call | flops 1048576 | bytes 33554432 | tf_op jit(solution)/shard_map/pallas_call | solution.py:498
  15.1 0.5 %collective-permute-start.4 = (bf16[12,48,128]{2,1,0:T(8,128)(2,1)S(1)}, bf16[12,48,128]{2,1,0:T(8,128)(2,1)S(1)}, u32[]{:S(2)}, u32[]{:S(2)}) collective-permute-start(bf16[12,48,128]{2,1,0:T(8,128)(2,1)S(1)} %get-tuple-element.94), channel_id=1, source_target_pairs={{0,1},{1,0},{2,3},{3,2},{4,5},{5,4},{6,7},{7,6},{8,9},{9,8},{10,11... | collective-permute-start | bytes 442376 | tf_op jit(solution)/shard_map/ppermute | solution.py:510
  15.6 1.2 %shard_map.167.triangle_ref.refs_3_ = f32[1152,128]{1,0:T(8,128)S(1)} custom-call(f32[1152,128]{1,0:T(8,128)S(1)} %get-tuple-element.90.left_ref.refs_0_, f32[1152,128]{1,0:T(8,128)S(1)} %get-tuple-element.93.right_ref), custom_call_target="tpu_custom_call" | custom-call | flops 1048576 | bytes 33554432 | tf_op jit(solution)/shard_map/pallas_call | solution.py:498
  16.8 1.1 %shard_map.168 = (f32[1152,128]{1,0:T(8,128)S(1)}, f32[576,128]{1,0:T(8,128)S(1)}, bf16[576,128]{1,0:T(8,128)(2,1)S(1)}) custom-call(f32[6,128]{1,0:T(8,128)S(1)} %stack.27.norms, bf16[128,128]{1,0:T(8,128)(2,1)S(1)} %copy-done.1, f32[1152,128]{1,0:T(8,128)S(1)} %get-tuple-element.90.left_ref.refs_0_, f32[1152,128]{1,0:T(8,128)S(1)} %get-tuple-element.91.gate_ref.refs_1_, ...), custom_call_target="tpu_custom_call" | custom-call | flops 1048576 | bytes 33554432 | tf_op jit(solution)/shard_map/pallas_call | solution.py:498
  18.0 0.2 %collective-permute-start.7 = (bf16[576,128]{1,0:T(8,128)(2,1)S(1)}, bf16[576,128]{1,0:T(8,128)(2,1)S(1)}, u32[]{:S(2)}, u32[]{:S(2)}) collective-permute-start(bf16[576,128]{1,0:T(8,128)(2,1)S(1)} %get-tuple-element.97.own_att_a), channel_id=1, source_target_pairs={{0,1},{1,0},{2,3},{3,2},{4,5},{5,4},{6,7},{7,6},{8,9},{9,8},{10,11... | collective-permute-start | bytes 442376 | tf_op jit(solution)/shard_map/ppermute | solution.py:510
  18.2 1.1 %shard_map.169.own_att_b = bf16[576,128]{1,0:T(8,128)(2,1)S(1)} custom-call(f32[6,128]{1,0:T(8,128)S(1)} %stack.27.norms, bf16[128,128]{1,0:T(8,128)(2,1)S(1)} %copy-done.1, f32[1152,128]{1,0:T(8,128)S(1)} %get-tuple-element.90.left_ref.refs_0_, f32[1152,128]{1,0:T(8,128)S(1)} %get-tuple-element.91.gate_ref.refs_1_, ...), custom_call_target="tpu_custom_call" | custom-call | flops 1048576 | bytes 33554432 | tf_op jit(solution)/shard_map/pallas_call | solution.py:498
  19.3 0.4 %collective-permute-start.6 = (bf16[576,128]{1,0:T(8,128)(2,1)S(1)}, bf16[576,128]{1,0:T(8,128)(2,1)S(1)}, u32[]{:S(2)}, u32[]{:S(2)}) collective-permute-start(bf16[576,128]{1,0:T(8,128)(2,1)S(1)} %shard_map.169.own_att_b), channel_id=1, source_target_pairs={{0,1},{1,0},{2,3},{3,2},{4,5},{5,4},{6,7},{7,6},{8,9},{9,8},{10,11... | collective-permute-start | bytes 442376 | tf_op jit(solution)/shard_map/ppermute | solution.py:510
  19.8 1.3 %shard_map.170 = (f32[3,3,48,128]{3,2,1,0:T(8,128)S(1)}, f32[144,128]{1,0:T(8,128)S(1)}, f32[144,128]{1,0:T(8,128)S(1)}, f32[144,128]{1,0:T(8,128)S(1)}) custom-call(f32[48,128]{1,0:T(8,128)S(1)} %broadcast_in_dim.23.valid_column, bf16[256,256]{1,0:T(8,128)(2,1)S(1)} %get-tuple-element.58.same_head, bf16[128,128]{1,0:T(8,128)(2,1)S(1)} %copy-done.4, ...), custom_call_target="tpu_custom_call" | custom-call | flops 1048576 | bytes 33554432 | tf_op jit(solution)/shard_map/pallas_call | solution.py:498
  21.1 1.4 %shard_map.171 = bf16[3,48,128]{2,1,0:T(8,128)(2,1)} custom-call(f32[48,128]{1,0:T(8,128)S(1)} %broadcast_in_dim.23.valid_column, bf16[256,256]{1,0:T(8,128)(2,1)S(1)} %get-tuple-element.58.same_head, bf16[128,128]{1,0:T(8,128)(2,1)S(1)} %copy-done.2, bf16[128,128]{1,0:T(8,128)(2,1)S(1)} %copy-done.3, bf16[128,128]{1,0:T(8,128)(2,1)S(1)} %copy-done.6, ...), custom_call_target="tpu_custom_call" | custom-call | flops 1048576 | bytes 33554432 | tf_op jit(solution)/shard_map/pallas_call | solution.py:498
  (41 shorter events, 0.3 us)
Async XLA Ops:
  0.0 10.1 %copy-start = (bf16[128,4]{0,1:T(4,128)(2,1)S(1)}, bf16[128,4]{0,1:T(4,128)(2,1)}, u32[]{:S(2)}) copy-start(bf16[128,4]{0,1:T(4,128)(2,1)} %param.32) | copy-start | bytes 3076
  0.0 6.6 %collective-permute-start = (bf16[3,48,128]{2,1,0:T(8,128)(2,1)}, bf16[3,48,128]{2,1,0:T(8,128)(2,1)S(1)}, u32[]{:S(2)}, u32[]{:S(2)}) collective-permute-start(bf16[3,48,128]{2,1,0:T(8,128)(2,1)} %param.17), channel_id=1, source_target_pairs={{0,8},{1,9},{2,10},{3,11},{4,12},{5,13},{6,14},{7,15},{8,0},{9,1},... | collective-permute-start | bytes 110600 | tf_op jit(solution)/shard_map/ppermute | solution.py:510
  4.1 1.0 %copy-start.7 = (bf16[3,48,128]{2,1,0:T(8,128)(2,1)S(1)}, bf16[3,48,128]{2,1,0:T(8,128)(2,1)}, u32[]{:S(2)}) copy-start(bf16[3,48,128]{2,1,0:T(8,128)(2,1)} %param.17) | copy-start | bytes 110596
  5.1 0.7 %copy-start.11 = (f32[128]{0:T(128)S(1)}, f32[128]{0:T(128)}, u32[]{:S(2)}) copy-start(f32[128]{0:T(128)} %param.24) | copy-start | bytes 1540
  5.1 0.7 %copy-start.12 = (f32[128]{0:T(128)S(1)}, f32[128]{0:T(128)}, u32[]{:S(2)}) copy-start(f32[128]{0:T(128)} %param.26) | copy-start | bytes 1540
  5.1 0.7 %copy-start.13 = (f32[128]{0:T(128)S(1)}, f32[128]{0:T(128)}, u32[]{:S(2)}) copy-start(f32[128]{0:T(128)} %param.27) | copy-start | bytes 1540
  5.1 0.7 %copy-start.8 = (f32[128]{0:T(128)S(1)}, f32[128]{0:T(128)}, u32[]{:S(2)}) copy-start(f32[128]{0:T(128)} %param.19) | copy-start | bytes 1540
  5.1 0.7 %copy-start.9 = (f32[128]{0:T(128)S(1)}, f32[128]{0:T(128)}, u32[]{:S(2)}) copy-start(f32[128]{0:T(128)} %param.20) | copy-start | bytes 1540
  5.1 0.7 %copy-start.10 = (f32[128]{0:T(128)S(1)}, f32[128]{0:T(128)}, u32[]{:S(2)}) copy-start(f32[128]{0:T(128)} %param.23) | copy-start | bytes 1540
  6.6 8.0 %collective-permute-start.3 = (bf16[6,48,128]{2,1,0:T(8,128)(2,1)S(1)}, bf16[6,48,128]{2,1,0:T(8,128)(2,1)S(1)}, u32[]{:S(2)}, u32[]{:S(2)}) collective-permute-start(bf16[6,48,128]{2,1,0:T(8,128)(2,1)S(1)} %constant_dynamic-update-slice_fusion.refs_0_), channel_id=1, source_target_pairs={{0,4},{1,5},{2,6},{3,7},{4,0},{5,1},{6,2},{7,3},{8,12},{9,13},{10,... | collective-permute-start | bytes 221192 | tf_op jit(solution)/shard_map/ppermute | solution.py:510
  8.2 5.3 %collective-permute-start.2 = (bf16[6,48,128]{2,1,0:T(8,128)(2,1)S(1)}, bf16[6,48,128]{2,1,0:T(8,128)(2,1)S(1)}, u32[]{:S(2)}, u32[]{:S(2)}) collective-permute-start(bf16[6,48,128]{2,1,0:T(8,128)(2,1)S(1)} %constant_dynamic-update-slice_fusion.refs_0_), channel_id=1, source_target_pairs={{0,6},{1,7},{2,4},{3,5},{4,2},{5,3},{6,0},{7,1},{8,14},{9,15},{10,... | collective-permute-start | bytes 221192 | tf_op jit(solution)/shard_map/ppermute | solution.py:510
  9.8 4.4 %collective-permute-start.1 = (bf16[6,48,128]{2,1,0:T(8,128)(2,1)S(1)}, bf16[6,48,128]{2,1,0:T(8,128)(2,1)S(1)}, u32[]{:S(2)}, u32[]{:S(2)}) collective-permute-start(bf16[6,48,128]{2,1,0:T(8,128)(2,1)S(1)} %constant_dynamic-update-slice_fusion.refs_0_), channel_id=1, source_target_pairs={{0,2},{1,3},{2,0},{3,1},{4,6},{5,7},{6,4},{7,5},{8,10},{9,11},{10,... | collective-permute-start | bytes 221192 | tf_op jit(solution)/shard_map/ppermute | solution.py:510
  10.1 0.7 %copy-start.14 = (s32[48]{0:T(128)S(1)}, s32[48]{0:T(128)}, u32[]{:S(2)}) copy-start(s32[48]{0:T(128)} %param.18) | copy-start | bytes 580
  15.1 1.8 %collective-permute-start.5 = (bf16[12,48,128]{2,1,0:T(8,128)(2,1)S(1)}, bf16[12,48,128]{2,1,0:T(8,128)(2,1)S(1)}, u32[]{:S(2)}, u32[]{:S(2)}) collective-permute-start(bf16[12,48,128]{2,1,0:T(8,128)(2,1)S(1)} %get-tuple-element.95), channel_id=1, source_target_pairs={{0,1},{1,0},{2,3},{3,2},{4,5},{5,4},{6,7},{7,6},{8,9},{9,8},{10,11... | collective-permute-start | bytes 442376 | tf_op jit(solution)/shard_map/ppermute | solution.py:510
  15.1 1.7 %collective-permute-start.4 = (bf16[12,48,128]{2,1,0:T(8,128)(2,1)S(1)}, bf16[12,48,128]{2,1,0:T(8,128)(2,1)S(1)}, u32[]{:S(2)}, u32[]{:S(2)}) collective-permute-start(bf16[12,48,128]{2,1,0:T(8,128)(2,1)S(1)} %get-tuple-element.94), channel_id=1, source_target_pairs={{0,1},{1,0},{2,3},{3,2},{4,5},{5,4},{6,7},{7,6},{8,9},{9,8},{10,11... | collective-permute-start | bytes 442376 | tf_op jit(solution)/shard_map/ppermute | solution.py:510
  15.6 1.2 %copy-start.1 = (bf16[128,128]{1,0:T(8,128)(2,1)S(1)}, bf16[128,128]{1,0:T(8,128)(2,1)}, u32[]{:S(2)}) copy-start(bf16[128,128]{1,0:T(8,128)(2,1)} %w_out.4) | copy-start | bytes 98308
  18.0 1.8 %collective-permute-start.7 = (bf16[576,128]{1,0:T(8,128)(2,1)S(1)}, bf16[576,128]{1,0:T(8,128)(2,1)S(1)}, u32[]{:S(2)}, u32[]{:S(2)}) collective-permute-start(bf16[576,128]{1,0:T(8,128)(2,1)S(1)} %get-tuple-element.97.own_att_a), channel_id=1, source_target_pairs={{0,1},{1,0},{2,3},{3,2},{4,5},{5,4},{6,7},{7,6},{8,9},{9,8},{10,11... | collective-permute-start | bytes 442376 | tf_op jit(solution)/shard_map/ppermute | solution.py:510
  18.2 1.5 %copy-start.2 = (bf16[128,128]{1,0:T(8,128)(2,1)S(1)}, bf16[128,128]{1,0:T(8,128)(2,1)}, u32[]{:S(2)}) copy-start(bf16[128,128]{1,0:T(8,128)(2,1)} %w_key.3) | copy-start | bytes 98308
  18.2 1.5 %copy-start.3 = (bf16[128,128]{1,0:T(8,128)(2,1)S(1)}, bf16[128,128]{1,0:T(8,128)(2,1)}, u32[]{:S(2)}) copy-start(bf16[128,128]{1,0:T(8,128)(2,1)} %w_value.3) | copy-start | bytes 98308
  18.2 1.5 %copy-start.4 = (bf16[128,128]{1,0:T(8,128)(2,1)S(1)}, bf16[128,128]{1,0:T(8,128)(2,1)}, u32[]{:S(2)}) copy-start(bf16[128,128]{1,0:T(8,128)(2,1)} %w_query.1) | copy-start | bytes 98308
  18.2 1.5 %copy-start.5 = (bf16[128,128]{1,0:T(8,128)(2,1)S(1)}, bf16[128,128]{1,0:T(8,128)(2,1)}, u32[]{:S(2)}) copy-start(bf16[128,128]{1,0:T(8,128)(2,1)} %w_gate.1) | copy-start | bytes 98308
  19.3 1.8 %collective-permute-start.6 = (bf16[576,128]{1,0:T(8,128)(2,1)S(1)}, bf16[576,128]{1,0:T(8,128)(2,1)S(1)}, u32[]{:S(2)}, u32[]{:S(2)}) collective-permute-start(bf16[576,128]{1,0:T(8,128)(2,1)S(1)} %shard_map.169.own_att_b), channel_id=1, source_target_pairs={{0,1},{1,0},{2,3},{3,2},{4,5},{5,4},{6,7},{7,6},{8,9},{9,8},{10,11... | collective-permute-start | bytes 442376 | tf_op jit(solution)/shard_map/ppermute | solution.py:510
  19.8 1.3 %copy-start.6 = (bf16[128,128]{1,0:T(8,128)(2,1)S(1)}, bf16[128,128]{1,0:T(8,128)(2,1)}, u32[]{:S(2)}) copy-start(bf16[128,128]{1,0:T(8,128)(2,1)} %w_out.5) | copy-start | bytes 98308

commit v22 on v16

--- a/solution.py
+++ b/solution.py
@@ -128,6 +128,20 @@
     return centre * lax.rsqrt(squares + 1e-05 * count) * (norm_gain * count**0.5) + norm_bias
 
 
+def row_sums(values, same_half):
+    half, channels = values.shape[0] // 2, values.shape[1]
+    values = values.astype(jnp.bfloat16)
+    sums = dot(jnp.concatenate([values[:half], values[half:]], axis=1), same_half[...])
+    return jnp.concatenate([sums[:, :channels], sums[:, channels:]], axis=0)
+
+
+def row_norm_by_products(values, total, norm_gain, norm_bias, same_half):
+    count = values.shape[1]
+    centre = values - total * (1.0 / count)
+    squares = row_sums(centre * centre, same_half)
+    return centre * lax.rsqrt(squares + 1e-05 * count) * (norm_gain * count**0.5) + norm_bias
+
+
 def dot(left, right):
     return jnp.dot(left, right, preferred_element_type=jnp.float32)
 
@@ -152,11 +166,11 @@
     pair_refs = refs[: len(pieces)]
     left_ref, right_ref, gate_ref, pairs_ref, send_ref = refs[-5:]
     if makes_heads:
-        left_ref, right_ref, gate_ref, pairs_ref, send_ref, same_head_ref = refs[-6:]
-        wide = same_head_ref.shape
-        row = lax.broadcasted_iota(jnp.int32, wide, 0) // HEAD_DIM
-        column = lax.broadcasted_iota(jnp.int32, wide, 1) // HEAD_DIM
-        same_head_ref[...] = jnp.where(row == column, 1.0, 0.0).astype(jnp.bfloat16)
+        left_ref, right_ref, gate_ref, pairs_ref, send_ref, *same_refs = refs[-7:]
+        for same_ref, width in zip(same_refs, (HEAD_DIM, HEADS * HEAD_DIM)):
+            row = lax.broadcasted_iota(jnp.int32, same_ref.shape, 0) // width
+            column = lax.broadcasted_iota(jnp.int32, same_ref.shape, 1) // width
+            same_ref[...] = jnp.where(row == column, 1.0, 0.0).astype(jnp.bfloat16)
     f32, bf16 = jnp.float32, jnp.bfloat16
     res, channels = valid_column.shape
     _, core = chip_and_core()
@@ -243,7 +257,17 @@
 
 
 def attention_inputs(
-    row_count, chips, first, norms, w_out, left_ref, gate_ref, pairs_ref, held_triangle, across_ref,
+    row_count,
+    chips,
+    first,
+    norms,
+    same_half,
+    w_out,
+    left_ref,
+    gate_ref,
+    pairs_ref,
+    held_triangle,
+    across_ref,
     triangle_ref,
 ):
     bf16 = jnp.bfloat16
@@ -255,9 +279,16 @@
     triangle_rows(
         row_count, chips, left_ref, across_ref, triangle_ref, first, half // 2, 1 - core, 0
     )
-    tri_normed = row_norm(triangle_ref[...], norms[2:3, :], norms[3:4, :]).astype(bf16)
+    triangle = triangle_ref[...]
+    total = row_sums(triangle, same_half)
+    tri_normed = row_norm_by_products(
+        triangle, total, norms[2:3, :], norms[3:4, :], same_half
+    ).astype(bf16)
     after_tri = pairs_ref[rows, :] + gate_ref[rows, :] * dot(tri_normed, w_out[...])
-    att_in = row_norm(after_tri, norms[4:5, :], norms[5:6, :]).astype(bf16)
+    total = jnp.sum(after_tri, axis=1, keepdims=True)
+    att_in = row_norm_by_products(
+        after_tri, total, norms[4:5, :], norms[5:6, :], same_half
+    ).astype(bf16)
     return after_tri, att_in
 
 
@@ -271,6 +302,7 @@
     chips,
     blocks,
     norms,
+    same_half,
     w_out,
     left_ref,
     gate_ref,
@@ -288,14 +320,16 @@
     first = first_chip(chips, 0) * row_count
     refs = (left_ref, gate_ref, pairs_ref, triangle_ref, across_ref, scratch_ref)
     after_ref[...], att_ref[...] = attention_inputs(
-        row_count, chips, first, norms, w_out, *refs
-    )
-
-
-def other_inputs_kernel(row_count, chips, norms, w_out, *refs):
+        row_count, chips, first, norms, same_half, w_out, *refs
+    )
+
+
+def other_inputs_kernel(row_count, chips, norms, same_half, w_out, *refs):
     *refs, att_ref, scratch_ref = refs
     first = first_chip(chips, 1) * row_count
-    _, att_ref[...] = attention_inputs(row_count, chips, first, norms, w_out, *refs, scratch_ref)
+    _, att_ref[...] = attention_inputs(
+        row_count, chips, first, norms, same_half, w_out, *refs, scratch_ref
+    )
 
 
 def keys_and_values(att, w_key, w_value, key_ref, value_ref):
@@ -552,7 +586,7 @@
         return call(
             functools.partial(edges_kernel, row_count, chips, blocks, send_row, not held),
             (tall, tall, tall, tall, shaped(bf16, 4 * row_count, res, channels))
-            + (() if held else (shaped(bf16, 2 * channels, 2 * channels),)),
+            + (() if held else (shaped(bf16, 2 * channels, 2 * channels),) * 2),
             operands,
             {first + e: e for e in range(len(held))},
         )
@@ -560,7 +594,7 @@
     diagonal = exchange(own, 6)
     beside = exchange(own, 2)
     near = exchange(own, 4)
-    *edges, early_right, same_head = edges_of([(own, own_blocks)], 0)
+    *edges, early_right, same_head, same_half = edges_of([(own, own_blocks)], 0)
     diagonal, edges = lax.optimization_barrier((diagonal, edges))
     *edges, early_right = edges_of(
         [(diagonal, blocks_from(3))], 2 * row_count, *edges, early_right
@@ -583,13 +617,13 @@
     part = half // 2 * res
     in_part, own_shape = shaped(f32, part, channels), shaped(f32, row_count * res, channels)
     att_part = shaped(bf16, part, channels)
-    shared = (norms, w_tri_out, left, gate, pairs)
+    shared = (norms, same_half, w_tri_out, left, gate, pairs)
     scratch = (pltpu.VMEM((part, channels), f32),)
     across, after_a, att_a = call(
         functools.partial(own_inputs_kernel, row_count, chips, late[1]),
         (tall, in_part, att_part),
         shared + (late[0], triangle, across),
-        {7: 0},
+        {8: 0},
         scratch=scratch,
     )
     far_att_a = exchange(att_a, 1)

time: 21.8 us -> 22.2 us (1.018)
  Pallas kernels: 7.5 us -> 7.88 us
    pallas_call x8, Pallas kernels: 7.5 us -> 7.88 us  [call(): pl.pallas_call(kernel, out_shape=outs, in_specs=[in_vmem] * len(operands)...]
  transfers between devices with their start and end apart: 8 -> 8, of which waited for: 5 -> 5; matrix products, arithmetic and copies ran while one was open for 6% -> 6% of each run, Pallas kernels for 23% -> 24%
where the time goes in v22:
time: 22.2 us; the launch traced here: 22 us
  starting transfers between devices  8.3 us (37%)
  Pallas kernels  7.88 us (35%)
  waiting for transfers between devices  3.18 us (14%)
  local copies, waits for them, and re-layouts  1.28 us (6%)
  other arithmetic  0.99 us (4%)
    ppermute x8, starting transfers between devices, exchange(): return lax.ppermute(values, 'row', [(d, d ^ bit) for d in range(devices)])  8.3 us
    pallas_call x8, Pallas kernels, call(): pl.pallas_call(kernel, out_shape=outs, in_specs=[in_vmem] * len(operands)...  7.88 us
    ppermute x8, waiting for transfers between devices, exchange(): return lax.ppermute(values, 'row', [(d, d ^ bit) for d in range(devices)])  3.18 us
    unnamed x30, local copies, waits for them, and re-layouts  1.16 us
    mul x1, other arithmetic, on_whole_complex(): edge_weights = jnp.concatenate([w_edges, w_tri_gate], axis=1) * halves  0.97 us
  transfers between devices with their start and end apart: 8, of which 5 were waited for; matrix products, arithmetic and copies ran while one was open for 6% of the time, Pallas kernels for 24%

profile of v22, /device:TPU:0, one launch (start us, length us, event | category | flops | bytes accessed | tf_op | source)
XLA Modules:
  0.0 22.0 jit_solution(12762442636490353459)
XLA Ops:
  0.0 4.0 %collective-permute-start = (bf16[3,48,128]{2,1,0:T(8,128)(2,1)}, bf16[3,48,128]{2,1,0:T(8,128)(2,1)S(1)}, u32[]{:S(2)}, u32[]{:S(2)}) collective-permute-start(bf16[3,48,128]{2,1,0:T(8,128)(2,1)} %param.17), channel_id=1, source_target_pairs={{0,8},{1,9},{2,10},{3,11},{4,12},{5,13},{6,14},{7,15},{8,0},{9,1},... | collective-permute-start | bytes 110600 | tf_op jit(solution)/shard_map/ppermute | solution.py:547
  4.1 1.0 %maximum_multiply_fusion.weights = bf16[128,640]{1,0:T(8,128)(2,1)S(1)} fusion(bf16[128,128]{1,0:T(8,128)(2,1)} %param.22, bf16[128,512]{1,0:T(8,128)(2,1)} %param.21, bf16[640]{0:T(1024)(128)(2,1)S(1)} %select_convert_fusion), kind=kLoop, calls=%fused_computation.2 | loop fusion | flops 491520 | bytes 328960 | tf_op jit(solution)/shard_map/mul | solution.py:560
  5.1 0.6 %copy-done.11 = f32[128]{0:T(128)S(1)} copy-done((f32[128]{0:T(128)S(1)}, f32[128]{0:T(128)}, u32[]{:S(2)}) %copy-start.11) | copy-done | bytes 536
  5.8 0.8 %collective-permute-done = bf16[3,48,128]{2,1,0:T(8,128)(2,1)S(1)} collective-permute-done((bf16[3,48,128]{2,1,0:T(8,128)(2,1)}, bf16[3,48,128]{2,1,0:T(8,128)(2,1)S(1)}, u32[]{:S(2)}, u32[]{:S(2)}) %collective-permute-start) | collective-permute-done | bytes 36896 | tf_op jit(solution)/shard_map/ppermute | solution.py:547
  6.6 2.5 %collective-permute-start.2 = (bf16[6,48,128]{2,1,0:T(8,128)(2,1)S(1)}, bf16[6,48,128]{2,1,0:T(8,128)(2,1)S(1)}, u32[]{:S(2)}, u32[]{:S(2)}) collective-permute-start(bf16[6,48,128]{2,1,0:T(8,128)(2,1)S(1)} %constant_dynamic-update-slice_fusion.refs_0_), channel_id=1, source_target_pairs={{0,6},{1,7},{2,4},{3,5},{4,2},{5,3},{6,0},{7,1},{8,14},{9,15},{10,... | collective-permute-start | bytes 221192 | tf_op jit(solution)/shard_map/ppermute | solution.py:547
  9.1 0.5 %collective-permute-start.1 = (bf16[6,48,128]{2,1,0:T(8,128)(2,1)S(1)}, bf16[6,48,128]{2,1,0:T(8,128)(2,1)S(1)}, u32[]{:S(2)}, u32[]{:S(2)}) collective-permute-start(bf16[6,48,128]{2,1,0:T(8,128)(2,1)S(1)} %constant_dynamic-update-slice_fusion.refs_0_), channel_id=1, source_target_pairs={{0,2},{1,3},{2,0},{3,1},{4,6},{5,7},{6,4},{7,5},{8,10},{9,11},{10,... | collective-permute-start | bytes 221192 | tf_op jit(solution)/shard_map/ppermute | solution.py:547
  9.6 0.5 %collective-permute-start.3 = (bf16[6,48,128]{2,1,0:T(8,128)(2,1)S(1)}, bf16[6,48,128]{2,1,0:T(8,128)(2,1)S(1)}, u32[]{:S(2)}, u32[]{:S(2)}) collective-permute-start(bf16[6,48,128]{2,1,0:T(8,128)(2,1)S(1)} %constant_dynamic-update-slice_fusion.refs_0_), channel_id=1, source_target_pairs={{0,4},{1,5},{2,6},{3,7},{4,0},{5,1},{6,2},{7,3},{8,12},{9,13},{10,... | collective-permute-start | bytes 221192 | tf_op jit(solution)/shard_map/ppermute | solution.py:547
  10.1 0.2 fusion.wide_bias
  10.4 0.4 %copy-done.14 = s32[48]{0:T(128)S(1)} copy-done((s32[48]{0:T(128)S(1)}, s32[48]{0:T(128)}, u32[]{:S(2)}) %copy-start.14) | copy-done | bytes 216
  10.8 0.1 broadcast_in_dim.23.valid_column
  10.9 0.4 %shard_map.163 = (f32[1152,128]{1,0:T(8,128)S(1)}, f32[1152,128]{1,0:T(8,128)S(1)}, f32[1152,128]{1,0:T(8,128)S(1)}, f32[1152,128]{1,0:T(8,128)S(1)}, bf16[12,48...) custom-call(f32[48,128]{1,0:T(8,128)S(1)} %broadcast_in_dim.23.valid_column, ...), custom_call_target="tpu_custom_call" | custom-call | flops 1048576 | bytes 33554432 | tf_op jit(solution)/shard_map/pallas_call | solution.py:535
  11.3 1.1 %collective-permute-done.2.refs_0_ = bf16[6,48,128]{2,1,0:T(8,128)(2,1)S(1)} collective-permute-done((bf16[6,48,128]{2,1,0:T(8,128)(2,1)S(1)}, bf16[6,48,128]{2,1,0:T(8,128)(2,1)S(1)}, u32[]{:S(2)}, u32[]{:S(2)}) %collective-permute-start.2) | collective-permute-done | bytes 73760 | tf_op jit(solution)/shard_map/ppermute | solution.py:547
  12.4 0.4 %shard_map.164 = (f32[1152,128]{1,0:T(8,128)S(1)}, f32[1152,128]{1,0:T(8,128)S(1)}, f32[1152,128]{1,0:T(8,128)S(1)}, f32[1152,128]{1,0:T(8,128)S(1)}, bf16[12,48,128]{2,1,0:T(8,128)(2,1)S(1)}) custom-call(f32[48,128]{1,0:T(8,128)S(1)} %broadcast_in_dim.23.valid_column, ...), custom_call_target="tpu_custom_call", output_to_operand_aliasing={{0}: (4, {}), {1}: (5, {}), {2}: (6, {}), {3}: (7, {}), {4}... | custom-call | flops 1048576 | bytes 33554432 | tf_op jit(solution)/shard_map/pallas_call | solution.py:535
  12.8 0.6 %collective-permute-done.1.refs_0_ = bf16[6,48,128]{2,1,0:T(8,128)(2,1)S(1)} collective-permute-done((bf16[6,48,128]{2,1,0:T(8,128)(2,1)S(1)}, bf16[6,48,128]{2,1,0:T(8,128)(2,1)S(1)}, u32[]{:S(2)}, u32[]{:S(2)}) %collective-permute-start.1) | collective-permute-done | bytes 73760 | tf_op jit(solution)/shard_map/ppermute | solution.py:547
  13.4 0.5 %collective-permute-done.3.refs_1_ = bf16[6,48,128]{2,1,0:T(8,128)(2,1)S(1)} collective-permute-done((bf16[6,48,128]{2,1,0:T(8,128)(2,1)S(1)}, bf16[6,48,128]{2,1,0:T(8,128)(2,1)S(1)}, u32[]{:S(2)}, u32[]{:S(2)}) %collective-permute-start.3) | collective-permute-done | bytes 73760 | tf_op jit(solution)/shard_map/ppermute | solution.py:547
  14.0 0.6 %shard_map.165 = (f32[1152,128]{1,0:T(8,128)S(1)}, f32[1152,128]{1,0:T(8,128)S(1)}, f32[1152,128]{1,0:T(8,128)S(1)}, f32[1152,128]{1,0:T(8,128)S(1)}, bf16[12,48,128]{2,1,0:T(8,128)(2,1)S(1)}) custom-call(f32[48,128]{1,0:T(8,128)S(1)} %broadcast_in_dim.23.valid_column, ...), custom_call_target="tpu_custom_call", output_to_operand_aliasing={{0}: (5, {}), {1}: (6, {}), {2}: (7, {}), {3}: (8, {})} | custom-call | flops 1048576 | bytes 33554432 | tf_op jit(solution)/shard_map/pallas_call | solution.py:535
  14.7 0.1 collective-permute-done.4.refs_0_
  14.8 1.2 %shard_map.166 = (f32[1152,128]{1,0:T(8,128)S(1)}, f32[1152,128]{1,0:T(8,128)S(1)}) custom-call(f32[1152,128]{1,0:T(8,128)S(1)} %get-tuple-element.74.left_ref.refs_0_, f32[1152,128]{1,0:T(8,128)S(1)} %get-tuple-element.77.right_ref, bf16[12,48,128]{2,1,0:T(8,128)(2,1)S(1)} %collective-permute-done.4.refs_0_), custom_call_target="tpu_custom_call" | custom-call | flops 1048576 | bytes 33554432 | tf_op jit(solution)/shard_map/pallas_call | solution.py:535
  16.0 1.3 %shard_map.167 = (f32[1152,128]{1,0:T(8,128)S(1)}, f32[576,128]{1,0:T(8,128)S(1)}, bf16[576,128]{1,0:T(8,128)(2,1)S(1)}) custom-call(f32[6,128]{1,0:T(8,128)S(1)} %stack.27.norms, bf16[256,256]{1,0:T(8,128)(2,1)S(1)} %get-tuple-element.68.same_half, bf16[128,128]{1,0:T(8,128)(2,1)S(1)} %copy-done.1, ...), custom_call_target="tpu_custom_call", output_to_operand_aliasing={{0}: (8, {})} | custom-call | flops 1048576 | bytes 33554432 | tf_op jit(solution)/shard_map/pallas_call | solution.py:535
  17.3 0.4 %collective-permute-start.7 = (bf16[576,128]{1,0:T(8,128)(2,1)S(1)}, bf16[576,128]{1,0:T(8,128)(2,1)S(1)}, u32[]{:S(2)}, u32[]{:S(2)}) collective-permute-start(bf16[576,128]{1,0:T(8,128)(2,1)S(1)} %get-tuple-element.83.own_att_a), channel_id=1, source_target_pairs={{0,1},{1,0},{2,3},{3,2},{4,5},{5,4},{6,7},{7,6},{8,9},{9,8},{10,11... | collective-permute-start | bytes 442376 | tf_op jit(solution)/shard_map/ppermute | solution.py:547
  17.8 1.3 %shard_map.168.own_att_b = bf16[576,128]{1,0:T(8,128)(2,1)S(1)} custom-call(f32[6,128]{1,0:T(8,128)S(1)} %stack.27.norms, bf16[256,256]{1,0:T(8,128)(2,1)S(1)} %get-tuple-element.68.same_half, bf16[128,128]{1,0:T(8,128)(2,1)S(1)} %copy-done.1, f32[1152,128]{1,0:T(8,128)S(1)} %get-tuple-element.74.left_ref.refs_0_, ...), custom_call_target="tpu_custom_call" | custom-call | flops 1048576 | bytes 33554432 | tf_op jit(solution)/shard_map/pallas_call | solution.py:535
  19.1 0.2 %collective-permute-start.6 = (bf16[576,128]{1,0:T(8,128)(2,1)S(1)}, bf16[576,128]{1,0:T(8,128)(2,1)S(1)}, u32[]{:S(2)}, u32[]{:S(2)}) collective-permute-start(bf16[576,128]{1,0:T(8,128)(2,1)S(1)} %shard_map.168.own_att_b), channel_id=1, source_target_pairs={{0,1},{1,0},{2,3},{3,2},{4,5},{5,4},{6,7},{7,6},{8,9},{9,8},{10,11... | collective-permute-start | bytes 442376 | tf_op jit(solution)/shard_map/ppermute | solution.py:547
  19.3 1.3 %shard_map.169 = (f32[3,3,48,128]{3,2,1,0:T(8,128)S(1)}, f32[144,128]{1,0:T(8,128)S(1)}, f32[144,128]{1,0:T(8,128)S(1)}, f32[144,128]{1,0:T(8,128)S(1)}) custom-call(f32[48,128]{1,0:T(8,128)S(1)} %broadcast_in_dim.23.valid_column, bf16[256,256]{1,0:T(8,128)(2,1)S(1)} %get-tuple-element.51.same_head, bf16[128,128]{1,0:T(8,128)(2,1)S(1)} %copy-done.4, ...), custom_call_target="tpu_custom_call" | custom-call | flops 1048576 | bytes 33554432 | tf_op jit(solution)/shard_map/pallas_call | solution.py:535
  20.7 1.4 %shard_map.170 = bf16[3,48,128]{2,1,0:T(8,128)(2,1)} custom-call(f32[48,128]{1,0:T(8,128)S(1)} %broadcast_in_dim.23.valid_column, bf16[256,256]{1,0:T(8,128)(2,1)S(1)} %get-tuple-element.51.same_head, bf16[128,128]{1,0:T(8,128)(2,1)S(1)} %copy-done.2, bf16[128,128]{1,0:T(8,128)(2,1)S(1)} %copy-done.3, bf16[128,128]{1,0:T(8,128)(2,1)S(1)} %copy-done.6, ...), custom_call_target="tpu_custom_call" | custom-call | flops 1048576 | bytes 33554432 | tf_op jit(solution)/shard_map/pallas_call | solution.py:535
  (40 shorter events, 0.3 us)
Async XLA Ops:
  0.0 10.1 %copy-start = (bf16[128,4]{0,1:T(4,128)(2,1)S(1)}, bf16[128,4]{0,1:T(4,128)(2,1)}, u32[]{:S(2)}) copy-start(bf16[128,4]{0,1:T(4,128)(2,1)} %param.32) | copy-start | bytes 3076
  0.0 6.6 %collective-permute-start = (bf16[3,48,128]{2,1,0:T(8,128)(2,1)}, bf16[3,48,128]{2,1,0:T(8,128)(2,1)S(1)}, u32[]{:S(2)}, u32[]{:S(2)}) collective-permute-start(bf16[3,48,128]{2,1,0:T(8,128)(2,1)} %param.17), channel_id=1, source_target_pairs={{0,8},{1,9},{2,10},{3,11},{4,12},{5,13},{6,14},{7,15},{8,0},{9,1},... | collective-permute-start | bytes 110600 | tf_op jit(solution)/shard_map/ppermute | solution.py:547
  4.1 1.0 %copy-start.7 = (bf16[3,48,128]{2,1,0:T(8,128)(2,1)S(1)}, bf16[3,48,128]{2,1,0:T(8,128)(2,1)}, u32[]{:S(2)}) copy-start(bf16[3,48,128]{2,1,0:T(8,128)(2,1)} %param.17) | copy-start | bytes 110596
  5.1 0.7 %copy-start.11 = (f32[128]{0:T(128)S(1)}, f32[128]{0:T(128)}, u32[]{:S(2)}) copy-start(f32[128]{0:T(128)} %param.24) | copy-start | bytes 1540
  5.1 0.7 %copy-start.12 = (f32[128]{0:T(128)S(1)}, f32[128]{0:T(128)}, u32[]{:S(2)}) copy-start(f32[128]{0:T(128)} %param.26) | copy-start | bytes 1540
  5.1 0.7 %copy-start.13 = (f32[128]{0:T(128)S(1)}, f32[128]{0:T(128)}, u32[]{:S(2)}) copy-start(f32[128]{0:T(128)} %param.27) | copy-start | bytes 1540
  5.1 0.7 %copy-start.8 = (f32[128]{0:T(128)S(1)}, f32[128]{0:T(128)}, u32[]{:S(2)}) copy-start(f32[128]{0:T(128)} %param.19) | copy-start | bytes 1540
  5.1 0.7 %copy-start.9 = (f32[128]{0:T(128)S(1)}, f32[128]{0:T(128)}, u32[]{:S(2)}) copy-start(f32[128]{0:T(128)} %param.20) | copy-start | bytes 1540
  5.1 0.7 %copy-start.10 = (f32[128]{0:T(128)S(1)}, f32[128]{0:T(128)}, u32[]{:S(2)}) copy-start(f32[128]{0:T(128)} %param.23) | copy-start | bytes 1540
  6.6 5.8 %collective-permute-start.2 = (bf16[6,48,128]{2,1,0:T(8,128)(2,1)S(1)}, bf16[6,48,128]{2,1,0:T(8,128)(2,1)S(1)}, u32[]{:S(2)}, u32[]{:S(2)}) collective-permute-start(bf16[6,48,128]{2,1,0:T(8,128)(2,1)S(1)} %constant_dynamic-update-slice_fusion.refs_0_), channel_id=1, source_target_pairs={{0,6},{1,7},{2,4},{3,5},{4,2},{5,3},{6,0},{7,1},{8,14},{9,15},{10,... | collective-permute-start | bytes 221192 | tf_op jit(solution)/shard_map/ppermute | solution.py:547
  9.1 4.4 %collective-permute-start.1 = (bf16[6,48,128]{2,1,0:T(8,128)(2,1)S(1)}, bf16[6,48,128]{2,1,0:T(8,128)(2,1)S(1)}, u32[]{:S(2)}, u32[]{:S(2)}) collective-permute-start(bf16[6,48,128]{2,1,0:T(8,128)(2,1)S(1)} %constant_dynamic-update-slice_fusion.refs_0_), channel_id=1, source_target_pairs={{0,2},{1,3},{2,0},{3,1},{4,6},{5,7},{6,4},{7,5},{8,10},{9,11},{10,... | collective-permute-start | bytes 221192 | tf_op jit(solution)/shard_map/ppermute | solution.py:547
  9.6 4.4 %collective-permute-start.3 = (bf16[6,48,128]{2,1,0:T(8,128)(2,1)S(1)}, bf16[6,48,128]{2,1,0:T(8,128)(2,1)S(1)}, u32[]{:S(2)}, u32[]{:S(2)}) collective-permute-start(bf16[6,48,128]{2,1,0:T(8,128)(2,1)S(1)} %constant_dynamic-update-slice_fusion.refs_0_), channel_id=1, source_target_pairs={{0,4},{1,5},{2,6},{3,7},{4,0},{5,1},{6,2},{7,3},{8,12},{9,13},{10,... | collective-permute-start | bytes 221192 | tf_op jit(solution)/shard_map/ppermute | solution.py:547
  10.1 0.7 %copy-start.14 = (s32[48]{0:T(128)S(1)}, s32[48]{0:T(128)}, u32[]{:S(2)}) copy-start(s32[48]{0:T(128)} %param.18) | copy-start | bytes 580
  13.4 1.4 %collective-permute-start.4 = (bf16[12,48,128]{2,1,0:T(8,128)(2,1)S(1)}, bf16[12,48,128]{2,1,0:T(8,128)(2,1)S(1)}, u32[]{:S(2)}, u32[]{:S(2)}) collective-permute-start(bf16[12,48,128]{2,1,0:T(8,128)(2,1)S(1)} %get-tuple-element.78), channel_id=1, source_target_pairs={{0,1},{1,0},{2,3},{3,2},{4,5},{5,4},{6,7},{7,6},{8,9},{9,8},{10,11... | collective-permute-start | bytes 442376 | tf_op jit(solution)/shard_map/ppermute | solution.py:547
  14.6 1.4 %collective-permute-start.5 = (bf16[12,48,128]{2,1,0:T(8,128)(2,1)S(1)}, bf16[12,48,128]{2,1,0:T(8,128)(2,1)S(1)}, u32[]{:S(2)}, u32[]{:S(2)}) collective-permute-start(bf16[12,48,128]{2,1,0:T(8,128)(2,1)S(1)} %get-tuple-element.80), channel_id=1, source_target_pairs={{0,1},{1,0},{2,3},{3,2},{4,5},{5,4},{6,7},{7,6},{8,9},{9,8},{10,11... | collective-permute-start | bytes 442376 | tf_op jit(solution)/shard_map/ppermute | solution.py:547
  14.8 1.2 %copy-start.1 = (bf16[128,128]{1,0:T(8,128)(2,1)S(1)}, bf16[128,128]{1,0:T(8,128)(2,1)}, u32[]{:S(2)}) copy-start(bf16[128,128]{1,0:T(8,128)(2,1)} %w_out.4) | copy-start | bytes 98308
  17.3 1.9 %collective-permute-start.7 = (bf16[576,128]{1,0:T(8,128)(2,1)S(1)}, bf16[576,128]{1,0:T(8,128)(2,1)S(1)}, u32[]{:S(2)}, u32[]{:S(2)}) collective-permute-start(bf16[576,128]{1,0:T(8,128)(2,1)S(1)} %get-tuple-element.83.own_att_a), channel_id=1, source_target_pairs={{0,1},{1,0},{2,3},{3,2},{4,5},{5,4},{6,7},{7,6},{8,9},{9,8},{10,11... | collective-permute-start | bytes 442376 | tf_op jit(solution)/shard_map/ppermute | solution.py:547
  17.8 1.5 %copy-start.2 = (bf16[128,128]{1,0:T(8,128)(2,1)S(1)}, bf16[128,128]{1,0:T(8,128)(2,1)}, u32[]{:S(2)}) copy-start(bf16[128,128]{1,0:T(8,128)(2,1)} %w_key.3) | copy-start | bytes 98308
  17.8 1.5 %copy-start.3 = (bf16[128,128]{1,0:T(8,128)(2,1)S(1)}, bf16[128,128]{1,0:T(8,128)(2,1)}, u32[]{:S(2)}) copy-start(bf16[128,128]{1,0:T(8,128)(2,1)} %w_value.3) | copy-start | bytes 98308
  17.8 1.5 %copy-start.4 = (bf16[128,128]{1,0:T(8,128)(2,1)S(1)}, bf16[128,128]{1,0:T(8,128)(2,1)}, u32[]{:S(2)}) copy-start(bf16[128,128]{1,0:T(8,128)(2,1)} %w_query.1) | copy-start | bytes 98308
  17.8 1.5 %copy-start.5 = (bf16[128,128]{1,0:T(8,128)(2,1)S(1)}, bf16[128,128]{1,0:T(8,128)(2,1)}, u32[]{:S(2)}) copy-start(bf16[128,128]{1,0:T(8,128)(2,1)} %w_gate.1) | copy-start | bytes 98308
  19.1 1.6 %collective-permute-start.6 = (bf16[576,128]{1,0:T(8,128)(2,1)S(1)}, bf16[576,128]{1,0:T(8,128)(2,1)S(1)}, u32[]{:S(2)}, u32[]{:S(2)}) collective-permute-start(bf16[576,128]{1,0:T(8,128)(2,1)S(1)} %shard_map.168.own_att_b), channel_id=1, source_target_pairs={{0,1},{1,0},{2,3},{3,2},{4,5},{5,4},{6,7},{7,6},{8,9},{9,8},{10,11... | collective-permute-start | bytes 442376 | tf_op jit(solution)/shard_map/ppermute | solution.py:547
  19.3 1.3 %copy-start.6 = (bf16[128,128]{1,0:T(8,128)(2,1)S(1)}, bf16[128,128]{1,0:T(8,128)(2,1)}, u32[]{:S(2)}) copy-start(bf16[128,128]{1,0:T(8,128)(2,1)} %w_out.5) | copy-start | bytes 98308

commit v23 on v21

--- a/solution.py
+++ b/solution.py
@@ -147,7 +147,7 @@
 
 
 def edges_kernel(
-    row_count, chips, pieces, send_row, makes_heads, valid_column, norms, weights, *refs
+    row_count, chips, pieces, done, send_row, makes_heads, valid_column, norms, weights, *refs
 ):
     pair_refs = refs[: len(pieces)]
     left_ref, right_ref, gate_ref, pairs_ref, send_ref = refs[-5:]
@@ -159,6 +159,16 @@
         same_head_ref[...] = jnp.where(row == column, 1.0, 0.0).astype(jnp.bfloat16)
     f32, bf16 = jnp.float32, jnp.bfloat16
     res, channels = valid_column.shape
+    held_refs = refs[len(pieces) :]
+    for chip, r in rows_of_blocks(row_count, done):
+        held_rows = pl.ds(pl.multiple_of((chip * row_count + r) * res, res), res)
+        held_columns = pl.ds(pl.multiple_of((r * chips + chip) * res, res), res)
+        left_ref[held_rows, :] = held_refs[0][held_rows, :]
+        right_ref[held_columns, :] = held_refs[1][held_columns, :]
+        gate_ref[held_rows, :] = held_refs[2][held_rows, :]
+        pairs_ref[held_rows, :] = held_refs[3][held_rows, :]
+    if send_row:
+        send_ref[:send_row] = held_refs[4][:send_row]
     _, core = chip_and_core()
     pairs = jnp.concatenate(
         [ref[...].astype(f32).reshape(-1, channels) for ref in pair_refs], axis=0
@@ -541,32 +551,32 @@
 
     tall = shaped(f32, half * res, channels)
 
-    def edges_of(pieces, send_row, *held):
+    def edges_of(pieces, done, send_row, *held):
         pairs = tuple(p for p, _ in pieces)
         blocks = tuple(b for _, b in pieces)
         operands = (valid_column, norms, edge_weights) + pairs + held
-        first = len(operands) - len(held)
         return call(
-            functools.partial(edges_kernel, row_count, chips, blocks, send_row, not held),
+            functools.partial(edges_kernel, row_count, chips, blocks, done, send_row, not held),
             (tall, tall, tall, tall, shaped(bf16, 4 * row_count, res, channels))
             + (() if held else (shaped(bf16, 2 * channels, 2 * channels),)),
             operands,
-            {first + e: e for e in range(len(held))},
         )
 
     diagonal = exchange(own, 6)
     beside = exchange(own, 2)
     near = exchange(own, 4)
-    *edges, early_right, same_head = edges_of([(own, own_blocks)], 0)
+    *edges, early_right, same_head = edges_of([(own, own_blocks)], (), 0)
     diagonal, edges = lax.optimization_barrier((diagonal, edges))
     *edges, early_right = edges_of(
-        [(diagonal, blocks_from(3))], 2 * row_count, *edges, early_right
+        [(diagonal, blocks_from(3))], own_blocks, 2 * row_count, *edges, early_right
+    )
+    beside, edges, early_right, wide_bias = lax.optimization_barrier(
+        (beside, edges, early_right, wide_bias)
     )
     early = (exchange(early_right, 1), own_blocks + blocks_from(3))
-    beside, edges, wide_bias = lax.optimization_barrier((beside, edges, wide_bias))
-    *edges, late_right = edges_of([(beside, blocks_from(1))], 0, *edges)
-    near, edges, late_right = lax.optimization_barrier((near, edges, late_right))
-    *edges, late_right = edges_of([(near, blocks_from(2))], 2 * row_count, *edges, late_right)
+    *edges, late_right = edges_of(
+        [(beside, blocks_from(1)), (near, blocks_from(2))], early[1], 0, *edges
+    )
     late = (exchange(late_right, 1), blocks_from(1) + blocks_from(2))
 
     left, right, gate, pairs = edges

time: 22.6 us -> 22.2 us (0.982)
  waiting for transfers between devices: 3.26 us -> 3.02 us
    ppermute x8, waiting for transfers between devices: 3.26 us -> 3.02 us  [exchange(): return lax.ppermute(values, 'row', [(d, d ^ bit) for d in range(devices)])]
    pallas_call x9 -> x8, Pallas kernels: 7.73 us -> 7.54 us  [call(): pl.pallas_call(kernel, out_shape=outs, in_specs=[in_vmem] * len(operands)...]
  transfers between devices with their start and end apart: 8 -> 8, of which waited for: 3 -> 4; matrix products, arithmetic and copies ran while one was open for 6% -> 6% of each run, Pallas kernels for 21% -> 20%
where the time goes in v23:
time: 22.2 us; the launch traced here: 22.1 us
  starting transfers between devices  8.79 us (40%)
  Pallas kernels  7.54 us (34%)
  waiting for transfers between devices  3.02 us (14%)
  local copies, waits for them, and re-layouts  1.28 us (6%)
  other arithmetic  0.99 us (4%)
    ppermute x8, starting transfers between devices, exchange(): return lax.ppermute(values, 'row', [(d, d ^ bit) for d in range(devices)])  8.79 us
    pallas_call x8, Pallas kernels, call(): pl.pallas_call(kernel, out_shape=outs, in_specs=[in_vmem] * len(operands)...  7.54 us
    ppermute x8, waiting for transfers between devices, exchange(): return lax.ppermute(values, 'row', [(d, d ^ bit) for d in range(devices)])  3.02 us
    unnamed x30, local copies, waits for them, and re-layouts  1.16 us
    mul x1, other arithmetic, on_whole_complex(): edge_weights = jnp.concatenate([w_edges, w_tri_gate], axis=1) * halves  0.97 us
  transfers between devices with their start and end apart: 8, of which 4 were waited for; matrix products, arithmetic and copies ran while one was open for 6% of the time, Pallas kernels for 20%

profile of v23, /device:TPU:0, one launch (start us, length us, event | category | flops | bytes accessed | tf_op | source)
XLA Modules:
  0.0 22.1 jit_solution(9703515425337668635)
XLA Ops:
  0.0 4.0 %collective-permute-start = (bf16[3,48,128]{2,1,0:T(8,128)(2,1)}, bf16[3,48,128]{2,1,0:T(8,128)(2,1)S(1)}, u32[]{:S(2)}, u32[]{:S(2)}) collective-permute-start(bf16[3,48,128]{2,1,0:T(8,128)(2,1)} %param.17), channel_id=1, source_target_pairs={{0,8},{1,9},{2,10},{3,11},{4,12},{5,13},{6,14},{7,15},{8,0},{9,1},... | collective-permute-start | bytes 110600 | tf_op jit(solution)/shard_map/ppermute | solution.py:520
  4.1 1.0 %maximum_multiply_fusion.weights = bf16[128,640]{1,0:T(8,128)(2,1)S(1)} fusion(bf16[128,128]{1,0:T(8,128)(2,1)} %param.22, bf16[128,512]{1,0:T(8,128)(2,1)} %param.21, bf16[640]{0:T(1024)(128)(2,1)S(1)} %select_convert_fusion), kind=kLoop, calls=%fused_computation.2 | loop fusion | flops 491520 | bytes 328960 | tf_op jit(solution)/shard_map/mul | solution.py:533
  5.1 0.6 %copy-done.11 = f32[128]{0:T(128)S(1)} copy-done((f32[128]{0:T(128)S(1)}, f32[128]{0:T(128)}, u32[]{:S(2)}) %copy-start.11) | copy-done | bytes 536
  5.8 0.8 %collective-permute-done = bf16[3,48,128]{2,1,0:T(8,128)(2,1)S(1)} collective-permute-done((bf16[3,48,128]{2,1,0:T(8,128)(2,1)}, bf16[3,48,128]{2,1,0:T(8,128)(2,1)S(1)}, u32[]{:S(2)}, u32[]{:S(2)}) %collective-permute-start) | collective-permute-done | bytes 36896 | tf_op jit(solution)/shard_map/ppermute | solution.py:520
  6.6 2.5 %collective-permute-start.2 = (bf16[6,48,128]{2,1,0:T(8,128)(2,1)S(1)}, bf16[6,48,128]{2,1,0:T(8,128)(2,1)S(1)}, u32[]{:S(2)}, u32[]{:S(2)}) collective-permute-start(bf16[6,48,128]{2,1,0:T(8,128)(2,1)S(1)} %constant_dynamic-update-slice_fusion.refs_0_), channel_id=1, source_target_pairs={{0,6},{1,7},{2,4},{3,5},{4,2},{5,3},{6,0},{7,1},{8,14},{9,15},{10,... | collective-permute-start | bytes 221192 | tf_op jit(solution)/shard_map/ppermute | solution.py:520
  9.1 0.5 %collective-permute-start.1 = (bf16[6,48,128]{2,1,0:T(8,128)(2,1)S(1)}, bf16[6,48,128]{2,1,0:T(8,128)(2,1)S(1)}, u32[]{:S(2)}, u32[]{:S(2)}) collective-permute-start(bf16[6,48,128]{2,1,0:T(8,128)(2,1)S(1)} %constant_dynamic-update-slice_fusion.refs_0_), channel_id=1, source_target_pairs={{0,2},{1,3},{2,0},{3,1},{4,6},{5,7},{6,4},{7,5},{8,10},{9,11},{10,... | collective-permute-start | bytes 221192 | tf_op jit(solution)/shard_map/ppermute | solution.py:520
  9.6 0.5 %collective-permute-start.3 = (bf16[6,48,128]{2,1,0:T(8,128)(2,1)S(1)}, bf16[6,48,128]{2,1,0:T(8,128)(2,1)S(1)}, u32[]{:S(2)}, u32[]{:S(2)}) collective-permute-start(bf16[6,48,128]{2,1,0:T(8,128)(2,1)S(1)} %constant_dynamic-update-slice_fusion.refs_0_), channel_id=1, source_target_pairs={{0,4},{1,5},{2,6},{3,7},{4,0},{5,1},{6,2},{7,3},{8,12},{9,13},{10,... | collective-permute-start | bytes 221192 | tf_op jit(solution)/shard_map/ppermute | solution.py:520
  10.1 0.2 fusion.wide_bias
  10.4 0.4 %copy-done.14 = s32[48]{0:T(128)S(1)} copy-done((s32[48]{0:T(128)S(1)}, s32[48]{0:T(128)}, u32[]{:S(2)}) %copy-start.14) | copy-done | bytes 216
  10.8 0.1 broadcast_in_dim.23.valid_column
  10.9 0.4 %shard_map.163 = (f32[1152,128]{1,0:T(8,128)S(1)}, f32[1152,128]{1,0:T(8,128)S(1)}, f32[1152,128]{1,0:T(8,128)S(1)}, f32[1152,128]{1,0:T(8,128)S(1)}, bf16[12,48...) custom-call(f32[48,128]{1,0:T(8,128)S(1)} %broadcast_in_dim.23.valid_column, f32[6,128]{1,0:T(8,128)S(1)} %stack.27.norms, ...), custom_call_target="tpu_custom_call" | custom-call | flops 1048576 | bytes 33554432 | tf_op jit(solution)/shard_map/pallas_call | solution.py:508
  11.3 1.1 %collective-permute-done.2.refs_0_ = bf16[6,48,128]{2,1,0:T(8,128)(2,1)S(1)} collective-permute-done((bf16[6,48,128]{2,1,0:T(8,128)(2,1)S(1)}, bf16[6,48,128]{2,1,0:T(8,128)(2,1)S(1)}, u32[]{:S(2)}, u32[]{:S(2)}) %collective-permute-start.2) | collective-permute-done | bytes 73760 | tf_op jit(solution)/shard_map/ppermute | solution.py:520
  12.4 0.4 %shard_map.164 = (f32[1152,128]{1,0:T(8,128)S(1)}, f32[1152,128]{1,0:T(8,128)S(1)}, f32[1152,128]{1,0:T(8,128)S(1)}, f32[1152,128]{1,0:T(8,128)S(1)}, bf16[12,48,128]{2,1,0:T(8,128)(2,1)S(1)}) custom-call(f32[48,128]{1,0:T(8,128)S(1)} %broadcast_in_dim.23.valid_column, f32[6,128]{1,0:T(8,128)S(1)} %stack.27.norms, ...), custom_call_target="tpu_custom_call" | custom-call | flops 1048576 | bytes 33554432 | tf_op jit(solution)/shard_map/pallas_call | solution.py:508
  12.8 0.6 %collective-permute-done.1.refs_0_ = bf16[6,48,128]{2,1,0:T(8,128)(2,1)S(1)} collective-permute-done((bf16[6,48,128]{2,1,0:T(8,128)(2,1)S(1)}, bf16[6,48,128]{2,1,0:T(8,128)(2,1)S(1)}, u32[]{:S(2)}, u32[]{:S(2)}) %collective-permute-start.1) | collective-permute-done | bytes 73760 | tf_op jit(solution)/shard_map/ppermute | solution.py:520
  13.4 0.5 %collective-permute-done.3.refs_1_ = bf16[6,48,128]{2,1,0:T(8,128)(2,1)S(1)} collective-permute-done((bf16[6,48,128]{2,1,0:T(8,128)(2,1)S(1)}, bf16[6,48,128]{2,1,0:T(8,128)(2,1)S(1)}, u32[]{:S(2)}, u32[]{:S(2)}) %collective-permute-start.3) | collective-permute-done | bytes 73760 | tf_op jit(solution)/shard_map/ppermute | solution.py:520
  14.0 0.6 %shard_map.165 = (f32[1152,128]{1,0:T(8,128)S(1)}, f32[1152,128]{1,0:T(8,128)S(1)}, f32[1152,128]{1,0:T(8,128)S(1)}, f32[1152,128]{1,0:T(8,128)S(1)}, bf16[12,48,128]{2,1,0:T(8,128)(2,1)S(1)}) custom-call(f32[48,128]{1,0:T(8,128)S(1)} %broadcast_in_dim.23.valid_column, f32[6,128]{1,0:T(8,128)S(1)} %stack.27.norms, ...), custom_call_target="tpu_custom_call" | custom-call | flops 1048576 | bytes 33554432 | tf_op jit(solution)/shard_map/pallas_call | solution.py:508
  14.7 0.5 %collective-permute-start.4 = (bf16[12,48,128]{2,1,0:T(8,128)(2,1)S(1)}, bf16[12,48,128]{2,1,0:T(8,128)(2,1)S(1)}, u32[]{:S(2)}, u32[]{:S(2)}) collective-permute-start(bf16[12,48,128]{2,1,0:T(8,128)(2,1)S(1)} %get-tuple-element.74), channel_id=1, source_target_pairs={{0,1},{1,0},{2,3},{3,2},{4,5},{5,4},{6,7},{7,6},{8,9},{9,8},{10,11... | collective-permute-start | bytes 442376 | tf_op jit(solution)/shard_map/ppermute | solution.py:520
  15.2 1.2 %shard_map.166.triangle_ref.refs_3_ = f32[1152,128]{1,0:T(8,128)S(1)} custom-call(f32[1152,128]{1,0:T(8,128)S(1)} %get-tuple-element.70.left_ref.refs_0_, f32[1152,128]{1,0:T(8,128)S(1)} %get-tuple-element.73.right_ref), custom_call_target="tpu_custom_call" | custom-call | flops 1048576 | bytes 33554432 | tf_op jit(solution)/shard_map/pallas_call | solution.py:508
  16.4 1.1 %shard_map.167 = (f32[1152,128]{1,0:T(8,128)S(1)}, f32[576,128]{1,0:T(8,128)S(1)}, bf16[576,128]{1,0:T(8,128)(2,1)S(1)}) custom-call(f32[6,128]{1,0:T(8,128)S(1)} %stack.27.norms, bf16[128,128]{1,0:T(8,128)(2,1)S(1)} %copy-done.1, f32[1152,128]{1,0:T(8,128)S(1)} %get-tuple-element.70.left_ref.refs_0_, f32[1152,128]{1,0:T(8,128)S(1)} %get-tuple-element.71.gate_ref.refs_1_, ...), custom_call_target="tpu_custom_call" | custom-call | flops 1048576 | bytes 33554432 | tf_op jit(solution)/shard_map/pallas_call | solution.py:508
  17.5 0.2 %collective-permute-start.7 = (bf16[576,128]{1,0:T(8,128)(2,1)S(1)}, bf16[576,128]{1,0:T(8,128)(2,1)S(1)}, u32[]{:S(2)}, u32[]{:S(2)}) collective-permute-start(bf16[576,128]{1,0:T(8,128)(2,1)S(1)} %get-tuple-element.77.own_att_a), channel_id=1, source_target_pairs={{0,1},{1,0},{2,3},{3,2},{4,5},{5,4},{6,7},{7,6},{8,9},{9,8},{10,11... | collective-permute-start | bytes 442376 | tf_op jit(solution)/shard_map/ppermute | solution.py:520
  17.8 1.1 %shard_map.168.own_att_b = bf16[576,128]{1,0:T(8,128)(2,1)S(1)} custom-call(f32[6,128]{1,0:T(8,128)S(1)} %stack.27.norms, bf16[128,128]{1,0:T(8,128)(2,1)S(1)} %copy-done.1, f32[1152,128]{1,0:T(8,128)S(1)} %get-tuple-element.70.left_ref.refs_0_, f32[1152,128]{1,0:T(8,128)S(1)} %get-tuple-element.71.gate_ref.refs_1_, ...), custom_call_target="tpu_custom_call" | custom-call | flops 1048576 | bytes 33554432 | tf_op jit(solution)/shard_map/pallas_call | solution.py:508
  18.9 0.4 %collective-permute-start.6 = (bf16[576,128]{1,0:T(8,128)(2,1)S(1)}, bf16[576,128]{1,0:T(8,128)(2,1)S(1)}, u32[]{:S(2)}, u32[]{:S(2)}) collective-permute-start(bf16[576,128]{1,0:T(8,128)(2,1)S(1)} %shard_map.168.own_att_b), channel_id=1, source_target_pairs={{0,1},{1,0},{2,3},{3,2},{4,5},{5,4},{6,7},{7,6},{8,9},{9,8},{10,11... | collective-permute-start | bytes 442376 | tf_op jit(solution)/shard_map/ppermute | solution.py:520
  19.3 1.3 %shard_map.169 = (f32[3,3,48,128]{3,2,1,0:T(8,128)S(1)}, f32[144,128]{1,0:T(8,128)S(1)}, f32[144,128]{1,0:T(8,128)S(1)}, f32[144,128]{1,0:T(8,128)S(1)}) custom-call(f32[48,128]{1,0:T(8,128)S(1)} %broadcast_in_dim.23.valid_column, bf16[256,256]{1,0:T(8,128)(2,1)S(1)} %get-tuple-element.48.same_head, bf16[128,128]{1,0:T(8,128)(2,1)S(1)} %copy-done.4, ...), custom_call_target="tpu_custom_call" | custom-call | flops 1048576 | bytes 33554432 | tf_op jit(solution)/shard_map/pallas_call | solution.py:508
  20.7 1.4 %shard_map.170 = bf16[3,48,128]{2,1,0:T(8,128)(2,1)} custom-call(f32[48,128]{1,0:T(8,128)S(1)} %broadcast_in_dim.23.valid_column, bf16[256,256]{1,0:T(8,128)(2,1)S(1)} %get-tuple-element.48.same_head, bf16[128,128]{1,0:T(8,128)(2,1)S(1)} %copy-done.2, bf16[128,128]{1,0:T(8,128)(2,1)S(1)} %copy-done.3, bf16[128,128]{1,0:T(8,128)(2,1)S(1)} %copy-done.6, ...), custom_call_target="tpu_custom_call" | custom-call | flops 1048576 | bytes 33554432 | tf_op jit(solution)/shard_map/pallas_call | solution.py:508
  (40 shorter events, 0.3 us)
Async XLA Ops:
  0.0 10.1 %copy-start = (bf16[128,4]{0,1:T(4,128)(2,1)S(1)}, bf16[128,4]{0,1:T(4,128)(2,1)}, u32[]{:S(2)}) copy-start(bf16[128,4]{0,1:T(4,128)(2,1)} %param.32) | copy-start | bytes 3076
  0.0 6.6 %collective-permute-start = (bf16[3,48,128]{2,1,0:T(8,128)(2,1)}, bf16[3,48,128]{2,1,0:T(8,128)(2,1)S(1)}, u32[]{:S(2)}, u32[]{:S(2)}) collective-permute-start(bf16[3,48,128]{2,1,0:T(8,128)(2,1)} %param.17), channel_id=1, source_target_pairs={{0,8},{1,9},{2,10},{3,11},{4,12},{5,13},{6,14},{7,15},{8,0},{9,1},... | collective-permute-start | bytes 110600 | tf_op jit(solution)/shard_map/ppermute | solution.py:520
  4.1 1.0 %copy-start.7 = (bf16[3,48,128]{2,1,0:T(8,128)(2,1)S(1)}, bf16[3,48,128]{2,1,0:T(8,128)(2,1)}, u32[]{:S(2)}) copy-start(bf16[3,48,128]{2,1,0:T(8,128)(2,1)} %param.17) | copy-start | bytes 110596
  5.1 0.7 %copy-start.11 = (f32[128]{0:T(128)S(1)}, f32[128]{0:T(128)}, u32[]{:S(2)}) copy-start(f32[128]{0:T(128)} %param.24) | copy-start | bytes 1540
  5.1 0.7 %copy-start.12 = (f32[128]{0:T(128)S(1)}, f32[128]{0:T(128)}, u32[]{:S(2)}) copy-start(f32[128]{0:T(128)} %param.26) | copy-start | bytes 1540
  5.1 0.7 %copy-start.13 = (f32[128]{0:T(128)S(1)}, f32[128]{0:T(128)}, u32[]{:S(2)}) copy-start(f32[128]{0:T(128)} %param.27) | copy-start | bytes 1540
  5.1 0.7 %copy-start.8 = (f32[128]{0:T(128)S(1)}, f32[128]{0:T(128)}, u32[]{:S(2)}) copy-start(f32[128]{0:T(128)} %param.19) | copy-start | bytes 1540
  5.1 0.7 %copy-start.9 = (f32[128]{0:T(128)S(1)}, f32[128]{0:T(128)}, u32[]{:S(2)}) copy-start(f32[128]{0:T(128)} %param.20) | copy-start | bytes 1540
  5.1 0.7 %copy-start.10 = (f32[128]{0:T(128)S(1)}, f32[128]{0:T(128)}, u32[]{:S(2)}) copy-start(f32[128]{0:T(128)} %param.23) | copy-start | bytes 1540
  6.6 5.8 %collective-permute-start.2 = (bf16[6,48,128]{2,1,0:T(8,128)(2,1)S(1)}, bf16[6,48,128]{2,1,0:T(8,128)(2,1)S(1)}, u32[]{:S(2)}, u32[]{:S(2)}) collective-permute-start(bf16[6,48,128]{2,1,0:T(8,128)(2,1)S(1)} %constant_dynamic-update-slice_fusion.refs_0_), channel_id=1, source_target_pairs={{0,6},{1,7},{2,4},{3,5},{4,2},{5,3},{6,0},{7,1},{8,14},{9,15},{10,... | collective-permute-start | bytes 221192 | tf_op jit(solution)/shard_map/ppermute | solution.py:520
  9.1 4.4 %collective-permute-start.1 = (bf16[6,48,128]{2,1,0:T(8,128)(2,1)S(1)}, bf16[6,48,128]{2,1,0:T(8,128)(2,1)S(1)}, u32[]{:S(2)}, u32[]{:S(2)}) collective-permute-start(bf16[6,48,128]{2,1,0:T(8,128)(2,1)S(1)} %constant_dynamic-update-slice_fusion.refs_0_), channel_id=1, source_target_pairs={{0,2},{1,3},{2,0},{3,1},{4,6},{5,7},{6,4},{7,5},{8,10},{9,11},{10,... | collective-permute-start | bytes 221192 | tf_op jit(solution)/shard_map/ppermute | solution.py:520
  9.6 4.4 %collective-permute-start.3 = (bf16[6,48,128]{2,1,0:T(8,128)(2,1)S(1)}, bf16[6,48,128]{2,1,0:T(8,128)(2,1)S(1)}, u32[]{:S(2)}, u32[]{:S(2)}) collective-permute-start(bf16[6,48,128]{2,1,0:T(8,128)(2,1)S(1)} %constant_dynamic-update-slice_fusion.refs_0_), channel_id=1, source_target_pairs={{0,4},{1,5},{2,6},{3,7},{4,0},{5,1},{6,2},{7,3},{8,12},{9,13},{10,... | collective-permute-start | bytes 221192 | tf_op jit(solution)/shard_map/ppermute | solution.py:520
  10.1 0.7 %copy-start.14 = (s32[48]{0:T(128)S(1)}, s32[48]{0:T(128)}, u32[]{:S(2)}) copy-start(s32[48]{0:T(128)} %param.18) | copy-start | bytes 580
  14.6 1.7 %collective-permute-start.5 = (bf16[12,48,128]{2,1,0:T(8,128)(2,1)S(1)}, bf16[12,48,128]{2,1,0:T(8,128)(2,1)S(1)}, u32[]{:S(2)}, u32[]{:S(2)}) collective-permute-start(bf16[12,48,128]{2,1,0:T(8,128)(2,1)S(1)} %get-tuple-element.75), channel_id=1, source_target_pairs={{0,1},{1,0},{2,3},{3,2},{4,5},{5,4},{6,7},{7,6},{8,9},{9,8},{10,11... | collective-permute-start | bytes 442376 | tf_op jit(solution)/shard_map/ppermute | solution.py:520
  14.7 1.7 %collective-permute-start.4 = (bf16[12,48,128]{2,1,0:T(8,128)(2,1)S(1)}, bf16[12,48,128]{2,1,0:T(8,128)(2,1)S(1)}, u32[]{:S(2)}, u32[]{:S(2)}) collective-permute-start(bf16[12,48,128]{2,1,0:T(8,128)(2,1)S(1)} %get-tuple-element.74), channel_id=1, source_target_pairs={{0,1},{1,0},{2,3},{3,2},{4,5},{5,4},{6,7},{7,6},{8,9},{9,8},{10,11... | collective-permute-start | bytes 442376 | tf_op jit(solution)/shard_map/ppermute | solution.py:520
  15.2 1.2 %copy-start.1 = (bf16[128,128]{1,0:T(8,128)(2,1)S(1)}, bf16[128,128]{1,0:T(8,128)(2,1)}, u32[]{:S(2)}) copy-start(bf16[128,128]{1,0:T(8,128)(2,1)} %w_out.4) | copy-start | bytes 98308
  17.5 1.8 %collective-permute-start.7 = (bf16[576,128]{1,0:T(8,128)(2,1)S(1)}, bf16[576,128]{1,0:T(8,128)(2,1)S(1)}, u32[]{:S(2)}, u32[]{:S(2)}) collective-permute-start(bf16[576,128]{1,0:T(8,128)(2,1)S(1)} %get-tuple-element.77.own_att_a), channel_id=1, source_target_pairs={{0,1},{1,0},{2,3},{3,2},{4,5},{5,4},{6,7},{7,6},{8,9},{9,8},{10,11... | collective-permute-start | bytes 442376 | tf_op jit(solution)/shard_map/ppermute | solution.py:520
  17.8 1.5 %copy-start.2 = (bf16[128,128]{1,0:T(8,128)(2,1)S(1)}, bf16[128,128]{1,0:T(8,128)(2,1)}, u32[]{:S(2)}) copy-start(bf16[128,128]{1,0:T(8,128)(2,1)} %w_key.3) | copy-start | bytes 98308
  17.8 1.5 %copy-start.3 = (bf16[128,128]{1,0:T(8,128)(2,1)S(1)}, bf16[128,128]{1,0:T(8,128)(2,1)}, u32[]{:S(2)}) copy-start(bf16[128,128]{1,0:T(8,128)(2,1)} %w_value.3) | copy-start | bytes 98308
  17.8 1.5 %copy-start.4 = (bf16[128,128]{1,0:T(8,128)(2,1)S(1)}, bf16[128,128]{1,0:T(8,128)(2,1)}, u32[]{:S(2)}) copy-start(bf16[128,128]{1,0:T(8,128)(2,1)} %w_query.1) | copy-start | bytes 98308
  17.8 1.5 %copy-start.5 = (bf16[128,128]{1,0:T(8,128)(2,1)S(1)}, bf16[128,128]{1,0:T(8,128)(2,1)}, u32[]{:S(2)}) copy-start(bf16[128,128]{1,0:T(8,128)(2,1)} %w_gate.1) | copy-start | bytes 98308
  18.9 1.8 %collective-permute-start.6 = (bf16[576,128]{1,0:T(8,128)(2,1)S(1)}, bf16[576,128]{1,0:T(8,128)(2,1)S(1)}, u32[]{:S(2)}, u32[]{:S(2)}) collective-permute-start(bf16[576,128]{1,0:T(8,128)(2,1)S(1)} %shard_map.168.own_att_b), channel_id=1, source_target_pairs={{0,1},{1,0},{2,3},{3,2},{4,5},{5,4},{6,7},{7,6},{8,9},{9,8},{10,11... | collective-permute-start | bytes 442376 | tf_op jit(solution)/shard_map/ppermute | solution.py:520
  19.3 1.3 %copy-start.6 = (bf16[128,128]{1,0:T(8,128)(2,1)S(1)}, bf16[128,128]{1,0:T(8,128)(2,1)}, u32[]{:S(2)}) copy-start(bf16[128,128]{1,0:T(8,128)(2,1)} %w_out.5) | copy-start | bytes 98308

commit v24 on v23

--- a/solution.py
+++ b/solution.py
@@ -235,7 +235,8 @@
                 triangle_ref[pl.ds(place, chips, stride=2 * row_count), :] = rounded(sums[m][0])
 
 
-def near_triangle_kernel(row_count, chips, chunk, left_ref, right_ref, triangle_ref):
+def near_triangle_kernel(row_count, chips, chunk, pieces, left_ref, right_ref, *refs):
+    received, (triangle_ref, across_ref) = refs[:-2], refs[-2:]
     _, core = chip_and_core()
 
     def some_rows(step, carry):
@@ -245,6 +246,9 @@
         )
         return carry
 
+    for ref, blocks in zip(received, pieces):
+        for n, (chip, r) in enumerate(rows_of_blocks(row_count, blocks)):
+            place_right(across_ref, chips, chip, r, ref[n])
     lax.fori_loop(0, row_count * chips // chunk, some_rows, 0)
 
 
@@ -281,17 +285,21 @@
     left_ref,
     gate_ref,
     pairs_ref,
-    early,
-    late,
+    received,
     triangle_ref,
+    held_across,
     across_ref,
     after_ref,
     att_ref,
     scratch_ref,
 ):
-    for received, senders in zip((early, late), blocks):
-        for n, (chip, r) in enumerate(rows_of_blocks(row_count, senders)):
-            place_right(across_ref, chips, chip, r, received[n])
+    early, late = blocks
+    res = held_across.shape[0] // (row_count * chips)
+    for chip, r in rows_of_blocks(row_count, early):
+        held = pl.ds(pl.multiple_of((r * chips + chip) * res, res), res)
+        across_ref[held, :] = held_across[held, :]
+    for n, (chip, r) in enumerate(rows_of_blocks(row_count, late)):
+        place_right(across_ref, chips, chip, r, received[n])
     first = first_chip(chips, 0) * row_count
     refs = (left_ref, gate_ref, pairs_ref, triangle_ref, across_ref, scratch_ref)
     after_ref[...], att_ref[...] = attention_inputs(
@@ -504,13 +512,12 @@
     def shaped(dtype, *shape):
         return jax.ShapeDtypeStruct(shape, dtype)
 
-    def call(kernel, outs, operands, aliases=None, scratch=(), cost=2**25):
+    def call(kernel, outs, operands, scratch=(), cost=2**25):
         return pl.pallas_call(
             kernel,
             out_shape=outs,
             in_specs=[in_vmem] * len(operands),
             out_specs=jax.tree.map(lambda _: in_vmem, outs),
-            input_output_aliases=aliases or {},
             scratch_shapes=list(scratch),
             compiler_params=pltpu.CompilerParams(vmem_limit_bytes=24 * 1024 * 1024),
             cost_estimate=pl.CostEstimate(flops=2**20, bytes_accessed=cost, transcendentals=0),
@@ -580,8 +587,10 @@
     late = (exchange(late_right, 1), blocks_from(1) + blocks_from(2))
 
     left, right, gate, pairs = edges
-    triangle = call(
-        functools.partial(near_triangle_kernel, row_count, chips, half // 2), tall, (left, right)
+    triangle, across = call(
+        functools.partial(near_triangle_kernel, row_count, chips, half // 2, [early[1]]),
+        (tall, tall),
+        (left, right, early[0]),
     )
     part = half // 2 * res
     in_part, own_shape = shaped(f32, part, channels), shaped(f32, row_count * res, channels)
@@ -591,7 +600,7 @@
     across, after_a, att_a = call(
         functools.partial(own_inputs_kernel, row_count, chips, (early[1], late[1])),
         (tall, in_part, att_part),
-        shared + (early[0], late[0], triangle),
+        shared + (late[0], triangle, across),
         scratch=scratch,
     )
     far_att_a = exchange(att_a, 1)

time: 22.2 us -> 21.9 us (0.986)
  starting transfers between devices: 8.79 us -> 8.3 us
    ppermute x8, starting transfers between devices: 8.79 us -> 8.3 us  [exchange(): return lax.ppermute(values, 'row', [(d, d ^ bit) for d in range(devices)])]
  transfers between devices with their start and end apart: 8 -> 8, of which waited for: 4 -> 5; matrix products, arithmetic and copies ran while one was open for 6% -> 6% of each run, Pallas kernels for 20% -> 23%
where the time goes in v24:
time: 21.9 us; the launch traced here: 21.7 us
  starting transfers between devices  8.3 us (38%)
  Pallas kernels  7.6 us (35%)
  waiting for transfers between devices  3.16 us (14%)
  local copies, waits for them, and re-layouts  1.28 us (6%)
  other arithmetic  0.99 us (5%)
    ppermute x8, starting transfers between devices, exchange(): return lax.ppermute(values, 'row', [(d, d ^ bit) for d in range(devices)])  8.3 us
    pallas_call x8, Pallas kernels, call(): pl.pallas_call(kernel, out_shape=outs, in_specs=[in_vmem] * len(operands)...  7.6 us
    ppermute x8, waiting for transfers between devices, exchange(): return lax.ppermute(values, 'row', [(d, d ^ bit) for d in range(devices)])  3.16 us
    unnamed x30, local copies, waits for them, and re-layouts  1.16 us
    mul x1, other arithmetic, on_whole_complex(): edge_weights = jnp.concatenate([w_edges, w_tri_gate], axis=1) * halves  0.97 us
  transfers between devices with their start and end apart: 8, of which 5 were waited for; matrix products, arithmetic and copies ran while one was open for 6% of the time, Pallas kernels for 23%

profile of v24, /device:TPU:0, one launch (start us, length us, event | category | flops | bytes accessed | tf_op | source)
XLA Modules:
  0.0 21.7 jit_solution(16066109668655126838)
XLA Ops:
  0.0 4.0 %collective-permute-start = (bf16[3,48,128]{2,1,0:T(8,128)(2,1)}, bf16[3,48,128]{2,1,0:T(8,128)(2,1)S(1)}, u32[]{:S(2)}, u32[]{:S(2)}) collective-permute-start(bf16[3,48,128]{2,1,0:T(8,128)(2,1)} %param.17), channel_id=1, source_target_pairs={{0,8},{1,9},{2,10},{3,11},{4,12},{5,13},{6,14},{7,15},{8,0},{9,1},... | collective-permute-start | bytes 110600 | tf_op jit(solution)/shard_map/ppermute | solution.py:527
  4.1 1.0 %maximum_multiply_fusion.weights = bf16[128,640]{1,0:T(8,128)(2,1)S(1)} fusion(bf16[128,128]{1,0:T(8,128)(2,1)} %param.22, bf16[128,512]{1,0:T(8,128)(2,1)} %param.21, bf16[640]{0:T(1024)(128)(2,1)S(1)} %select_convert_fusion), kind=kLoop, calls=%fused_computation.2 | loop fusion | flops 491520 | bytes 328960 | tf_op jit(solution)/shard_map/mul | solution.py:540
  5.1 0.6 %copy-done.11 = f32[128]{0:T(128)S(1)} copy-done((f32[128]{0:T(128)S(1)}, f32[128]{0:T(128)}, u32[]{:S(2)}) %copy-start.11) | copy-done | bytes 536
  5.8 0.8 %collective-permute-done = bf16[3,48,128]{2,1,0:T(8,128)(2,1)S(1)} collective-permute-done((bf16[3,48,128]{2,1,0:T(8,128)(2,1)}, bf16[3,48,128]{2,1,0:T(8,128)(2,1)S(1)}, u32[]{:S(2)}, u32[]{:S(2)}) %collective-permute-start) | collective-permute-done | bytes 36896 | tf_op jit(solution)/shard_map/ppermute | solution.py:527
  6.6 2.5 %collective-permute-start.2 = (bf16[6,48,128]{2,1,0:T(8,128)(2,1)S(1)}, bf16[6,48,128]{2,1,0:T(8,128)(2,1)S(1)}, u32[]{:S(2)}, u32[]{:S(2)}) collective-permute-start(bf16[6,48,128]{2,1,0:T(8,128)(2,1)S(1)} %constant_dynamic-update-slice_fusion.refs_0_), channel_id=1, source_target_pairs={{0,6},{1,7},{2,4},{3,5},{4,2},{5,3},{6,0},{7,1},{8,14},{9,15},{10,... | collective-permute-start | bytes 221192 | tf_op jit(solution)/shard_map/ppermute | solution.py:527
  9.1 0.5 %collective-permute-start.1 = (bf16[6,48,128]{2,1,0:T(8,128)(2,1)S(1)}, bf16[6,48,128]{2,1,0:T(8,128)(2,1)S(1)}, u32[]{:S(2)}, u32[]{:S(2)}) collective-permute-start(bf16[6,48,128]{2,1,0:T(8,128)(2,1)S(1)} %constant_dynamic-update-slice_fusion.refs_0_), channel_id=1, source_target_pairs={{0,2},{1,3},{2,0},{3,1},{4,6},{5,7},{6,4},{7,5},{8,10},{9,11},{10,... | collective-permute-start | bytes 221192 | tf_op jit(solution)/shard_map/ppermute | solution.py:527
  9.6 0.5 %collective-permute-start.3 = (bf16[6,48,128]{2,1,0:T(8,128)(2,1)S(1)}, bf16[6,48,128]{2,1,0:T(8,128)(2,1)S(1)}, u32[]{:S(2)}, u32[]{:S(2)}) collective-permute-start(bf16[6,48,128]{2,1,0:T(8,128)(2,1)S(1)} %constant_dynamic-update-slice_fusion.refs_0_), channel_id=1, source_target_pairs={{0,4},{1,5},{2,6},{3,7},{4,0},{5,1},{6,2},{7,3},{8,12},{9,13},{10,... | collective-permute-start | bytes 221192 | tf_op jit(solution)/shard_map/ppermute | solution.py:527
  10.1 0.2 fusion.wide_bias
  10.4 0.4 %copy-done.14 = s32[48]{0:T(128)S(1)} copy-done((s32[48]{0:T(128)S(1)}, s32[48]{0:T(128)}, u32[]{:S(2)}) %copy-start.14) | copy-done | bytes 216
  10.8 0.1 broadcast_in_dim.23.valid_column
  10.9 0.4 %shard_map.163 = (f32[1152,128]{1,0:T(8,128)S(1)}, f32[1152,128]{1,0:T(8,128)S(1)}, f32[1152,128]{1,0:T(8,128)S(1)}, f32[1152,128]{1,0:T(8,128)S(1)}, bf16[12,48...) custom-call(f32[48,128]{1,0:T(8,128)S(1)} %broadcast_in_dim.23.valid_column, f32[6,128]{1,0:T(8,128)S(1)} %stack.27.norms, ...), custom_call_target="tpu_custom_call" | custom-call | flops 1048576 | bytes 33554432 | tf_op jit(solution)/shard_map/pallas_call | solution.py:516
  11.3 1.1 %collective-permute-done.2.refs_0_ = bf16[6,48,128]{2,1,0:T(8,128)(2,1)S(1)} collective-permute-done((bf16[6,48,128]{2,1,0:T(8,128)(2,1)S(1)}, bf16[6,48,128]{2,1,0:T(8,128)(2,1)S(1)}, u32[]{:S(2)}, u32[]{:S(2)}) %collective-permute-start.2) | collective-permute-done | bytes 73760 | tf_op jit(solution)/shard_map/ppermute | solution.py:527
  12.4 0.4 %shard_map.164 = (f32[1152,128]{1,0:T(8,128)S(1)}, f32[1152,128]{1,0:T(8,128)S(1)}, f32[1152,128]{1,0:T(8,128)S(1)}, f32[1152,128]{1,0:T(8,128)S(1)}, bf16[12,48,128]{2,1,0:T(8,128)(2,1)S(1)}) custom-call(f32[48,128]{1,0:T(8,128)S(1)} %broadcast_in_dim.23.valid_column, f32[6,128]{1,0:T(8,128)S(1)} %stack.27.norms, ...), custom_call_target="tpu_custom_call" | custom-call | flops 1048576 | bytes 33554432 | tf_op jit(solution)/shard_map/pallas_call | solution.py:516
  12.8 0.6 %collective-permute-done.1.refs_0_ = bf16[6,48,128]{2,1,0:T(8,128)(2,1)S(1)} collective-permute-done((bf16[6,48,128]{2,1,0:T(8,128)(2,1)S(1)}, bf16[6,48,128]{2,1,0:T(8,128)(2,1)S(1)}, u32[]{:S(2)}, u32[]{:S(2)}) %collective-permute-start.1) | collective-permute-done | bytes 73760 | tf_op jit(solution)/shard_map/ppermute | solution.py:527
  13.4 0.5 %collective-permute-done.3.refs_1_ = bf16[6,48,128]{2,1,0:T(8,128)(2,1)S(1)} collective-permute-done((bf16[6,48,128]{2,1,0:T(8,128)(2,1)S(1)}, bf16[6,48,128]{2,1,0:T(8,128)(2,1)S(1)}, u32[]{:S(2)}, u32[]{:S(2)}) %collective-permute-start.3) | collective-permute-done | bytes 73760 | tf_op jit(solution)/shard_map/ppermute | solution.py:527
  14.0 0.6 %shard_map.165 = (f32[1152,128]{1,0:T(8,128)S(1)}, f32[1152,128]{1,0:T(8,128)S(1)}, f32[1152,128]{1,0:T(8,128)S(1)}, f32[1152,128]{1,0:T(8,128)S(1)}, bf16[12,48,128]{2,1,0:T(8,128)(2,1)S(1)}) custom-call(f32[48,128]{1,0:T(8,128)S(1)} %broadcast_in_dim.23.valid_column, f32[6,128]{1,0:T(8,128)S(1)} %stack.27.norms, ...), custom_call_target="tpu_custom_call" | custom-call | flops 1048576 | bytes 33554432 | tf_op jit(solution)/shard_map/pallas_call | solution.py:516
  14.7 0.1 collective-permute-done.4.refs_0_
  14.8 1.2 %shard_map.166 = (f32[1152,128]{1,0:T(8,128)S(1)}, f32[1152,128]{1,0:T(8,128)S(1)}) custom-call(f32[1152,128]{1,0:T(8,128)S(1)} %get-tuple-element.72.left_ref.refs_0_, f32[1152,128]{1,0:T(8,128)S(1)} %get-tuple-element.75.right_ref, bf16[12,48,128]{2,1,0:T(8,128)(2,1)S(1)} %collective-permute-done.4.refs_0_), custom_call_target="tpu_custom_call" | custom-call | flops 1048576 | bytes 33554432 | tf_op jit(solution)/shard_map/pallas_call | solution.py:516
  16.1 1.1 %shard_map.167 = (f32[1152,128]{1,0:T(8,128)S(1)}, f32[576,128]{1,0:T(8,128)S(1)}, bf16[576,128]{1,0:T(8,128)(2,1)S(1)}) custom-call(f32[6,128]{1,0:T(8,128)S(1)} %stack.27.norms, bf16[128,128]{1,0:T(8,128)(2,1)S(1)} %copy-done.1, f32[1152,128]{1,0:T(8,128)S(1)} %get-tuple-element.72.left_ref.refs_0_, f32[1152,128]{1,0:T(8,128)S(1)} %get-tuple-element.73.gate_ref.refs_1_, ...), custom_call_target="tpu_custom_call" | custom-call | flops 1048576 | bytes 33554432 | tf_op jit(solution)/shard_map/pallas_call | solution.py:516
  17.2 0.4 %collective-permute-start.7 = (bf16[576,128]{1,0:T(8,128)(2,1)S(1)}, bf16[576,128]{1,0:T(8,128)(2,1)S(1)}, u32[]{:S(2)}, u32[]{:S(2)}) collective-permute-start(bf16[576,128]{1,0:T(8,128)(2,1)S(1)} %get-tuple-element.81.own_att_a), channel_id=1, source_target_pairs={{0,1},{1,0},{2,3},{3,2},{4,5},{5,4},{6,7},{7,6},{8,9},{9,8},{10,11... | collective-permute-start | bytes 442376 | tf_op jit(solution)/shard_map/ppermute | solution.py:527
  17.7 1.1 %shard_map.168.own_att_b = bf16[576,128]{1,0:T(8,128)(2,1)S(1)} custom-call(f32[6,128]{1,0:T(8,128)S(1)} %stack.27.norms, bf16[128,128]{1,0:T(8,128)(2,1)S(1)} %copy-done.1, f32[1152,128]{1,0:T(8,128)S(1)} %get-tuple-element.72.left_ref.refs_0_, f32[1152,128]{1,0:T(8,128)S(1)} %get-tuple-element.73.gate_ref.refs_1_, ...), custom_call_target="tpu_custom_call" | custom-call | flops 1048576 | bytes 33554432 | tf_op jit(solution)/shard_map/pallas_call | solution.py:516
  18.8 0.2 collective-permute-start.6
  19.0 1.3 %shard_map.169 = (f32[3,3,48,128]{3,2,1,0:T(8,128)S(1)}, f32[144,128]{1,0:T(8,128)S(1)}, f32[144,128]{1,0:T(8,128)S(1)}, f32[144,128]{1,0:T(8,128)S(1)}) custom-call(f32[48,128]{1,0:T(8,128)S(1)} %broadcast_in_dim.23.valid_column, bf16[256,256]{1,0:T(8,128)(2,1)S(1)} %get-tuple-element.50.same_head, bf16[128,128]{1,0:T(8,128)(2,1)S(1)} %copy-done.4, ...), custom_call_target="tpu_custom_call" | custom-call | flops 1048576 | bytes 33554432 | tf_op jit(solution)/shard_map/pallas_call | solution.py:516
  20.3 1.4 %shard_map.170 = bf16[3,48,128]{2,1,0:T(8,128)(2,1)} custom-call(f32[48,128]{1,0:T(8,128)S(1)} %broadcast_in_dim.23.valid_column, bf16[256,256]{1,0:T(8,128)(2,1)S(1)} %get-tuple-element.50.same_head, bf16[128,128]{1,0:T(8,128)(2,1)S(1)} %copy-done.2, bf16[128,128]{1,0:T(8,128)(2,1)S(1)} %copy-done.3, bf16[128,128]{1,0:T(8,128)(2,1)S(1)} %copy-done.6, ...), custom_call_target="tpu_custom_call" | custom-call | flops 1048576 | bytes 33554432 | tf_op jit(solution)/shard_map/pallas_call | solution.py:516
  (40 shorter events, 0.3 us)
Async XLA Ops:
  0.0 10.1 %copy-start = (bf16[128,4]{0,1:T(4,128)(2,1)S(1)}, bf16[128,4]{0,1:T(4,128)(2,1)}, u32[]{:S(2)}) copy-start(bf16[128,4]{0,1:T(4,128)(2,1)} %param.32) | copy-start | bytes 3076
  0.0 6.6 %collective-permute-start = (bf16[3,48,128]{2,1,0:T(8,128)(2,1)}, bf16[3,48,128]{2,1,0:T(8,128)(2,1)S(1)}, u32[]{:S(2)}, u32[]{:S(2)}) collective-permute-start(bf16[3,48,128]{2,1,0:T(8,128)(2,1)} %param.17), channel_id=1, source_target_pairs={{0,8},{1,9},{2,10},{3,11},{4,12},{5,13},{6,14},{7,15},{8,0},{9,1},... | collective-permute-start | bytes 110600 | tf_op jit(solution)/shard_map/ppermute | solution.py:527
  4.1 1.0 %copy-start.7 = (bf16[3,48,128]{2,1,0:T(8,128)(2,1)S(1)}, bf16[3,48,128]{2,1,0:T(8,128)(2,1)}, u32[]{:S(2)}) copy-start(bf16[3,48,128]{2,1,0:T(8,128)(2,1)} %param.17) | copy-start | bytes 110596
  5.1 0.7 %copy-start.11 = (f32[128]{0:T(128)S(1)}, f32[128]{0:T(128)}, u32[]{:S(2)}) copy-start(f32[128]{0:T(128)} %param.24) | copy-start | bytes 1540
  5.1 0.7 %copy-start.12 = (f32[128]{0:T(128)S(1)}, f32[128]{0:T(128)}, u32[]{:S(2)}) copy-start(f32[128]{0:T(128)} %param.26) | copy-start | bytes 1540
  5.1 0.7 %copy-start.13 = (f32[128]{0:T(128)S(1)}, f32[128]{0:T(128)}, u32[]{:S(2)}) copy-start(f32[128]{0:T(128)} %param.27) | copy-start | bytes 1540
  5.1 0.7 %copy-start.8 = (f32[128]{0:T(128)S(1)}, f32[128]{0:T(128)}, u32[]{:S(2)}) copy-start(f32[128]{0:T(128)} %param.19) | copy-start | bytes 1540
  5.1 0.7 %copy-start.9 = (f32[128]{0:T(128)S(1)}, f32[128]{0:T(128)}, u32[]{:S(2)}) copy-start(f32[128]{0:T(128)} %param.20) | copy-start | bytes 1540
  5.1 0.7 %copy-start.10 = (f32[128]{0:T(128)S(1)}, f32[128]{0:T(128)}, u32[]{:S(2)}) copy-start(f32[128]{0:T(128)} %param.23) | copy-start | bytes 1540
  6.6 5.8 %collective-permute-start.2 = (bf16[6,48,128]{2,1,0:T(8,128)(2,1)S(1)}, bf16[6,48,128]{2,1,0:T(8,128)(2,1)S(1)}, u32[]{:S(2)}, u32[]{:S(2)}) collective-permute-start(bf16[6,48,128]{2,1,0:T(8,128)(2,1)S(1)} %constant_dynamic-update-slice_fusion.refs_0_), channel_id=1, source_target_pairs={{0,6},{1,7},{2,4},{3,5},{4,2},{5,3},{6,0},{7,1},{8,14},{9,15},{10,... | collective-permute-start | bytes 221192 | tf_op jit(solution)/shard_map/ppermute | solution.py:527
  9.1 4.4 %collective-permute-start.1 = (bf16[6,48,128]{2,1,0:T(8,128)(2,1)S(1)}, bf16[6,48,128]{2,1,0:T(8,128)(2,1)S(1)}, u32[]{:S(2)}, u32[]{:S(2)}) collective-permute-start(bf16[6,48,128]{2,1,0:T(8,128)(2,1)S(1)} %constant_dynamic-update-slice_fusion.refs_0_), channel_id=1, source_target_pairs={{0,2},{1,3},{2,0},{3,1},{4,6},{5,7},{6,4},{7,5},{8,10},{9,11},{10,... | collective-permute-start | bytes 221192 | tf_op jit(solution)/shard_map/ppermute | solution.py:527
  9.6 4.4 %collective-permute-start.3 = (bf16[6,48,128]{2,1,0:T(8,128)(2,1)S(1)}, bf16[6,48,128]{2,1,0:T(8,128)(2,1)S(1)}, u32[]{:S(2)}, u32[]{:S(2)}) collective-permute-start(bf16[6,48,128]{2,1,0:T(8,128)(2,1)S(1)} %constant_dynamic-update-slice_fusion.refs_0_), channel_id=1, source_target_pairs={{0,4},{1,5},{2,6},{3,7},{4,0},{5,1},{6,2},{7,3},{8,12},{9,13},{10,... | collective-permute-start | bytes 221192 | tf_op jit(solution)/shard_map/ppermute | solution.py:527
  10.1 0.7 %copy-start.14 = (s32[48]{0:T(128)S(1)}, s32[48]{0:T(128)}, u32[]{:S(2)}) copy-start(s32[48]{0:T(128)} %param.18) | copy-start | bytes 580
  13.4 1.4 %collective-permute-start.4 = (bf16[12,48,128]{2,1,0:T(8,128)(2,1)S(1)}, bf16[12,48,128]{2,1,0:T(8,128)(2,1)S(1)}, u32[]{:S(2)}, u32[]{:S(2)}) collective-permute-start(bf16[12,48,128]{2,1,0:T(8,128)(2,1)S(1)} %get-tuple-element.76), channel_id=1, source_target_pairs={{0,1},{1,0},{2,3},{3,2},{4,5},{5,4},{6,7},{7,6},{8,9},{9,8},{10,11... | collective-permute-start | bytes 442376 | tf_op jit(solution)/shard_map/ppermute | solution.py:527
  14.6 1.4 %collective-permute-start.5 = (bf16[12,48,128]{2,1,0:T(8,128)(2,1)S(1)}, bf16[12,48,128]{2,1,0:T(8,128)(2,1)S(1)}, u32[]{:S(2)}, u32[]{:S(2)}) collective-permute-start(bf16[12,48,128]{2,1,0:T(8,128)(2,1)S(1)} %get-tuple-element.78), channel_id=1, source_target_pairs={{0,1},{1,0},{2,3},{3,2},{4,5},{5,4},{6,7},{7,6},{8,9},{9,8},{10,11... | collective-permute-start | bytes 442376 | tf_op jit(solution)/shard_map/ppermute | solution.py:527
  14.8 1.3 %copy-start.1 = (bf16[128,128]{1,0:T(8,128)(2,1)S(1)}, bf16[128,128]{1,0:T(8,128)(2,1)}, u32[]{:S(2)}) copy-start(bf16[128,128]{1,0:T(8,128)(2,1)} %w_out.4) | copy-start | bytes 98308
  17.2 1.8 %collective-permute-start.7 = (bf16[576,128]{1,0:T(8,128)(2,1)S(1)}, bf16[576,128]{1,0:T(8,128)(2,1)S(1)}, u32[]{:S(2)}, u32[]{:S(2)}) collective-permute-start(bf16[576,128]{1,0:T(8,128)(2,1)S(1)} %get-tuple-element.81.own_att_a), channel_id=1, source_target_pairs={{0,1},{1,0},{2,3},{3,2},{4,5},{5,4},{6,7},{7,6},{8,9},{9,8},{10,11... | collective-permute-start | bytes 442376 | tf_op jit(solution)/shard_map/ppermute | solution.py:527
  17.7 1.3 %copy-start.2 = (bf16[128,128]{1,0:T(8,128)(2,1)S(1)}, bf16[128,128]{1,0:T(8,128)(2,1)}, u32[]{:S(2)}) copy-start(bf16[128,128]{1,0:T(8,128)(2,1)} %w_key.3) | copy-start | bytes 98308
  17.7 1.3 %copy-start.3 = (bf16[128,128]{1,0:T(8,128)(2,1)S(1)}, bf16[128,128]{1,0:T(8,128)(2,1)}, u32[]{:S(2)}) copy-start(bf16[128,128]{1,0:T(8,128)(2,1)} %w_value.3) | copy-start | bytes 98308
  17.7 1.3 %copy-start.4 = (bf16[128,128]{1,0:T(8,128)(2,1)S(1)}, bf16[128,128]{1,0:T(8,128)(2,1)}, u32[]{:S(2)}) copy-start(bf16[128,128]{1,0:T(8,128)(2,1)} %w_query.1) | copy-start | bytes 98308
  17.7 1.3 %copy-start.5 = (bf16[128,128]{1,0:T(8,128)(2,1)S(1)}, bf16[128,128]{1,0:T(8,128)(2,1)}, u32[]{:S(2)}) copy-start(bf16[128,128]{1,0:T(8,128)(2,1)} %w_gate.1) | copy-start | bytes 98308
  18.8 1.5 %collective-permute-start.6 = (bf16[576,128]{1,0:T(8,128)(2,1)S(1)}, bf16[576,128]{1,0:T(8,128)(2,1)S(1)}, u32[]{:S(2)}, u32[]{:S(2)}) collective-permute-start(bf16[576,128]{1,0:T(8,128)(2,1)S(1)} %shard_map.168.own_att_b), channel_id=1, source_target_pairs={{0,1},{1,0},{2,3},{3,2},{4,5},{5,4},{6,7},{7,6},{8,9},{9,8},{10,11... | collective-permute-start | bytes 442376 | tf_op jit(solution)/shard_map/ppermute | solution.py:527
  19.0 1.3 %copy-start.6 = (bf16[128,128]{1,0:T(8,128)(2,1)S(1)}, bf16[128,128]{1,0:T(8,128)(2,1)}, u32[]{:S(2)}) copy-start(bf16[128,128]{1,0:T(8,128)(2,1)} %w_out.5) | copy-start | bytes 98308

commit v25 on v24

--- a/solution.py
+++ b/solution.py
@@ -187,7 +187,19 @@
     left = rounded((jnp.tanh(joined[:, channels:]) + 1.0) * joined[:, :channels] * masks)
     joined = dot(normed, weights[:, 2 * channels : 4 * channels])
     right = ((jnp.tanh(joined[:, channels:]) + 1.0) * joined[:, :channels] * masks).astype(bf16)
-    gate = 0.5 * jnp.tanh(dot(normed, weights[:, 4 * channels :])) + 0.5
+    gate_weights = weights[:, 4 * channels :]
+    nothing = jnp.zeros_like(gate_weights)
+    gate_weights = jnp.concatenate(
+        [
+            jnp.concatenate([gate_weights, nothing], axis=1),
+            jnp.concatenate([nothing, gate_weights], axis=1),
+        ],
+        axis=0,
+    )
+    middle = normed.shape[0] // 2
+    joined = dot(jnp.concatenate([normed[:middle], normed[middle:]], axis=1), gate_weights)
+    joined = jnp.concatenate([joined[:, :channels], joined[:, channels:]], axis=0)
+    gate = 0.5 * jnp.tanh(joined) + 0.5
     for n, (chip, r) in enumerate(rows_of):
         rows = slice(n * res, (n + 1) * res)
         start = pl.multiple_of((chip * row_count + r) * res, res)

time: 21.9 us -> 21.9 us (level)
  no operation moved by 1% of the time
where the time goes in v25:
time: 21.9 us; the launch traced here: 21.7 us
  starting transfers between devices  8.3 us (38%)
  Pallas kernels  7.62 us (35%)
  waiting for transfers between devices  3.15 us (14%)
  local copies, waits for them, and re-layouts  1.28 us (6%)
  other arithmetic  0.99 us (5%)
    ppermute x8, starting transfers between devices, exchange(): return lax.ppermute(values, 'row', [(d, d ^ bit) for d in range(devices)])  8.3 us
    pallas_call x8, Pallas kernels, call(): pl.pallas_call(kernel, out_shape=outs, in_specs=[in_vmem] * len(operands)...  7.62 us
    ppermute x8, waiting for transfers between devices, exchange(): return lax.ppermute(values, 'row', [(d, d ^ bit) for d in range(devices)])  3.15 us
    unnamed x30, local copies, waits for them, and re-layouts  1.16 us
    mul x1, other arithmetic, on_whole_complex(): edge_weights = jnp.concatenate([w_edges, w_tri_gate], axis=1) * halves  0.97 us
  transfers between devices with their start and end apart: 8, of which 5 were waited for; matrix products, arithmetic and copies ran while one was open for 6% of the time, Pallas kernels for 23%

profile of v25, /device:TPU:0, one launch (start us, length us, event | category | flops | bytes accessed | tf_op | source)
XLA Modules:
  0.0 21.7 jit_solution(8250909786676074284)
XLA Ops:
  0.0 4.0 %collective-permute-start = (bf16[3,48,128]{2,1,0:T(8,128)(2,1)}, bf16[3,48,128]{2,1,0:T(8,128)(2,1)S(1)}, u32[]{:S(2)}, u32[]{:S(2)}) collective-permute-start(bf16[3,48,128]{2,1,0:T(8,128)(2,1)} %param.17), channel_id=1, source_target_pairs={{0,8},{1,9},{2,10},{3,11},{4,12},{5,13},{6,14},{7,15},{8,0},{9,1},... | collective-permute-start | bytes 110600 | tf_op jit(solution)/shard_map/ppermute | solution.py:539
  4.1 1.0 %maximum_multiply_fusion.weights = bf16[128,640]{1,0:T(8,128)(2,1)S(1)} fusion(bf16[128,128]{1,0:T(8,128)(2,1)} %param.22, bf16[128,512]{1,0:T(8,128)(2,1)} %param.21, bf16[640]{0:T(1024)(128)(2,1)S(1)} %select_convert_fusion), kind=kLoop, calls=%fused_computation.2 | loop fusion | flops 491520 | bytes 328960 | tf_op jit(solution)/shard_map/mul | solution.py:552
  5.1 0.6 %copy-done.11 = f32[128]{0:T(128)S(1)} copy-done((f32[128]{0:T(128)S(1)}, f32[128]{0:T(128)}, u32[]{:S(2)}) %copy-start.11) | copy-done | bytes 536
  5.8 0.8 %collective-permute-done = bf16[3,48,128]{2,1,0:T(8,128)(2,1)S(1)} collective-permute-done((bf16[3,48,128]{2,1,0:T(8,128)(2,1)}, bf16[3,48,128]{2,1,0:T(8,128)(2,1)S(1)}, u32[]{:S(2)}, u32[]{:S(2)}) %collective-permute-start) | collective-permute-done | bytes 36896 | tf_op jit(solution)/shard_map/ppermute | solution.py:539
  6.6 2.5 %collective-permute-start.2 = (bf16[6,48,128]{2,1,0:T(8,128)(2,1)S(1)}, bf16[6,48,128]{2,1,0:T(8,128)(2,1)S(1)}, u32[]{:S(2)}, u32[]{:S(2)}) collective-permute-start(bf16[6,48,128]{2,1,0:T(8,128)(2,1)S(1)} %constant_dynamic-update-slice_fusion.refs_0_), channel_id=1, source_target_pairs={{0,6},{1,7},{2,4},{3,5},{4,2},{5,3},{6,0},{7,1},{8,14},{9,15},{10,... | collective-permute-start | bytes 221192 | tf_op jit(solution)/shard_map/ppermute | solution.py:539
  9.1 0.5 %collective-permute-start.1 = (bf16[6,48,128]{2,1,0:T(8,128)(2,1)S(1)}, bf16[6,48,128]{2,1,0:T(8,128)(2,1)S(1)}, u32[]{:S(2)}, u32[]{:S(2)}) collective-permute-start(bf16[6,48,128]{2,1,0:T(8,128)(2,1)S(1)} %constant_dynamic-update-slice_fusion.refs_0_), channel_id=1, source_target_pairs={{0,2},{1,3},{2,0},{3,1},{4,6},{5,7},{6,4},{7,5},{8,10},{9,11},{10,... | collective-permute-start | bytes 221192 | tf_op jit(solution)/shard_map/ppermute | solution.py:539
  9.6 0.5 %collective-permute-start.3 = (bf16[6,48,128]{2,1,0:T(8,128)(2,1)S(1)}, bf16[6,48,128]{2,1,0:T(8,128)(2,1)S(1)}, u32[]{:S(2)}, u32[]{:S(2)}) collective-permute-start(bf16[6,48,128]{2,1,0:T(8,128)(2,1)S(1)} %constant_dynamic-update-slice_fusion.refs_0_), channel_id=1, source_target_pairs={{0,4},{1,5},{2,6},{3,7},{4,0},{5,1},{6,2},{7,3},{8,12},{9,13},{10,... | collective-permute-start | bytes 221192 | tf_op jit(solution)/shard_map/ppermute | solution.py:539
  10.1 0.2 fusion.wide_bias
  10.4 0.4 %copy-done.14 = s32[48]{0:T(128)S(1)} copy-done((s32[48]{0:T(128)S(1)}, s32[48]{0:T(128)}, u32[]{:S(2)}) %copy-start.14) | copy-done | bytes 216
  10.8 0.1 broadcast_in_dim.23.valid_column
  10.9 0.4 %shard_map.163 = (f32[1152,128]{1,0:T(8,128)S(1)}, f32[1152,128]{1,0:T(8,128)S(1)}, f32[1152,128]{1,0:T(8,128)S(1)}, f32[1152,128]{1,0:T(8,128)S(1)}, bf16[12,48...) custom-call(f32[48,128]{1,0:T(8,128)S(1)} %broadcast_in_dim.23.valid_column, f32[6,128]{1,0:T(8,128)S(1)} %stack.27.norms, ...), custom_call_target="tpu_custom_call" | custom-call | flops 1048576 | bytes 33554432 | tf_op jit(solution)/shard_map/pallas_call | solution.py:528
  11.3 1.1 %collective-permute-done.2.refs_0_ = bf16[6,48,128]{2,1,0:T(8,128)(2,1)S(1)} collective-permute-done((bf16[6,48,128]{2,1,0:T(8,128)(2,1)S(1)}, bf16[6,48,128]{2,1,0:T(8,128)(2,1)S(1)}, u32[]{:S(2)}, u32[]{:S(2)}) %collective-permute-start.2) | collective-permute-done | bytes 73760 | tf_op jit(solution)/shard_map/ppermute | solution.py:539
  12.4 0.4 %shard_map.164 = (f32[1152,128]{1,0:T(8,128)S(1)}, f32[1152,128]{1,0:T(8,128)S(1)}, f32[1152,128]{1,0:T(8,128)S(1)}, f32[1152,128]{1,0:T(8,128)S(1)}, bf16[12,48,128]{2,1,0:T(8,128)(2,1)S(1)}) custom-call(f32[48,128]{1,0:T(8,128)S(1)} %broadcast_in_dim.23.valid_column, f32[6,128]{1,0:T(8,128)S(1)} %stack.27.norms, ...), custom_call_target="tpu_custom_call" | custom-call | flops 1048576 | bytes 33554432 | tf_op jit(solution)/shard_map/pallas_call | solution.py:528
  12.8 0.6 %collective-permute-done.1.refs_0_ = bf16[6,48,128]{2,1,0:T(8,128)(2,1)S(1)} collective-permute-done((bf16[6,48,128]{2,1,0:T(8,128)(2,1)S(1)}, bf16[6,48,128]{2,1,0:T(8,128)(2,1)S(1)}, u32[]{:S(2)}, u32[]{:S(2)}) %collective-permute-start.1) | collective-permute-done | bytes 73760 | tf_op jit(solution)/shard_map/ppermute | solution.py:539
  13.4 0.5 %collective-permute-done.3.refs_1_ = bf16[6,48,128]{2,1,0:T(8,128)(2,1)S(1)} collective-permute-done((bf16[6,48,128]{2,1,0:T(8,128)(2,1)S(1)}, bf16[6,48,128]{2,1,0:T(8,128)(2,1)S(1)}, u32[]{:S(2)}, u32[]{:S(2)}) %collective-permute-start.3) | collective-permute-done | bytes 73760 | tf_op jit(solution)/shard_map/ppermute | solution.py:539
  14.0 0.6 %shard_map.165 = (f32[1152,128]{1,0:T(8,128)S(1)}, f32[1152,128]{1,0:T(8,128)S(1)}, f32[1152,128]{1,0:T(8,128)S(1)}, f32[1152,128]{1,0:T(8,128)S(1)}, bf16[12,48,128]{2,1,0:T(8,128)(2,1)S(1)}) custom-call(f32[48,128]{1,0:T(8,128)S(1)} %broadcast_in_dim.23.valid_column, f32[6,128]{1,0:T(8,128)S(1)} %stack.27.norms, ...), custom_call_target="tpu_custom_call" | custom-call | flops 1048576 | bytes 33554432 | tf_op jit(solution)/shard_map/pallas_call | solution.py:528
  14.7 0.1 collective-permute-done.4.refs_0_
  14.8 1.2 %shard_map.166 = (f32[1152,128]{1,0:T(8,128)S(1)}, f32[1152,128]{1,0:T(8,128)S(1)}) custom-call(f32[1152,128]{1,0:T(8,128)S(1)} %get-tuple-element.72.left_ref.refs_0_, f32[1152,128]{1,0:T(8,128)S(1)} %get-tuple-element.75.right_ref, bf16[12,48,128]{2,1,0:T(8,128)(2,1)S(1)} %collective-permute-done.4.refs_0_), custom_call_target="tpu_custom_call" | custom-call | flops 1048576 | bytes 33554432 | tf_op jit(solution)/shard_map/pallas_call | solution.py:528
  16.1 1.1 %shard_map.167 = (f32[1152,128]{1,0:T(8,128)S(1)}, f32[576,128]{1,0:T(8,128)S(1)}, bf16[576,128]{1,0:T(8,128)(2,1)S(1)}) custom-call(f32[6,128]{1,0:T(8,128)S(1)} %stack.27.norms, bf16[128,128]{1,0:T(8,128)(2,1)S(1)} %copy-done.1, f32[1152,128]{1,0:T(8,128)S(1)} %get-tuple-element.72.left_ref.refs_0_, f32[1152,128]{1,0:T(8,128)S(1)} %get-tuple-element.73.gate_ref.refs_1_, ...), custom_call_target="tpu_custom_call" | custom-call | flops 1048576 | bytes 33554432 | tf_op jit(solution)/shard_map/pallas_call | solution.py:528
  17.2 0.4 %collective-permute-start.7 = (bf16[576,128]{1,0:T(8,128)(2,1)S(1)}, bf16[576,128]{1,0:T(8,128)(2,1)S(1)}, u32[]{:S(2)}, u32[]{:S(2)}) collective-permute-start(bf16[576,128]{1,0:T(8,128)(2,1)S(1)} %get-tuple-element.81.own_att_a), channel_id=1, source_target_pairs={{0,1},{1,0},{2,3},{3,2},{4,5},{5,4},{6,7},{7,6},{8,9},{9,8},{10,11... | collective-permute-start | bytes 442376 | tf_op jit(solution)/shard_map/ppermute | solution.py:539
  17.7 1.1 %shard_map.168.own_att_b = bf16[576,128]{1,0:T(8,128)(2,1)S(1)} custom-call(f32[6,128]{1,0:T(8,128)S(1)} %stack.27.norms, bf16[128,128]{1,0:T(8,128)(2,1)S(1)} %copy-done.1, f32[1152,128]{1,0:T(8,128)S(1)} %get-tuple-element.72.left_ref.refs_0_, f32[1152,128]{1,0:T(8,128)S(1)} %get-tuple-element.73.gate_ref.refs_1_, ...), custom_call_target="tpu_custom_call" | custom-call | flops 1048576 | bytes 33554432 | tf_op jit(solution)/shard_map/pallas_call | solution.py:528
  18.8 0.2 collective-permute-start.6
  19.0 1.3 %shard_map.169 = (f32[3,3,48,128]{3,2,1,0:T(8,128)S(1)}, f32[144,128]{1,0:T(8,128)S(1)}, f32[144,128]{1,0:T(8,128)S(1)}, f32[144,128]{1,0:T(8,128)S(1)}) custom-call(f32[48,128]{1,0:T(8,128)S(1)} %broadcast_in_dim.23.valid_column, bf16[256,256]{1,0:T(8,128)(2,1)S(1)} %get-tuple-element.50.same_head, bf16[128,128]{1,0:T(8,128)(2,1)S(1)} %copy-done.4, ...), custom_call_target="tpu_custom_call" | custom-call | flops 1048576 | bytes 33554432 | tf_op jit(solution)/shard_map/pallas_call | solution.py:528
  20.4 1.4 %shard_map.170 = bf16[3,48,128]{2,1,0:T(8,128)(2,1)} custom-call(f32[48,128]{1,0:T(8,128)S(1)} %broadcast_in_dim.23.valid_column, bf16[256,256]{1,0:T(8,128)(2,1)S(1)} %get-tuple-element.50.same_head, bf16[128,128]{1,0:T(8,128)(2,1)S(1)} %copy-done.2, bf16[128,128]{1,0:T(8,128)(2,1)S(1)} %copy-done.3, bf16[128,128]{1,0:T(8,128)(2,1)S(1)} %copy-done.6, ...), custom_call_target="tpu_custom_call" | custom-call | flops 1048576 | bytes 33554432 | tf_op jit(solution)/shard_map/pallas_call | solution.py:528
  (40 shorter events, 0.3 us)
Async XLA Ops:
  0.0 10.1 %copy-start = (bf16[128,4]{0,1:T(4,128)(2,1)S(1)}, bf16[128,4]{0,1:T(4,128)(2,1)}, u32[]{:S(2)}) copy-start(bf16[128,4]{0,1:T(4,128)(2,1)} %param.32) | copy-start | bytes 3076
  0.0 6.6 %collective-permute-start = (bf16[3,48,128]{2,1,0:T(8,128)(2,1)}, bf16[3,48,128]{2,1,0:T(8,128)(2,1)S(1)}, u32[]{:S(2)}, u32[]{:S(2)}) collective-permute-start(bf16[3,48,128]{2,1,0:T(8,128)(2,1)} %param.17), channel_id=1, source_target_pairs={{0,8},{1,9},{2,10},{3,11},{4,12},{5,13},{6,14},{7,15},{8,0},{9,1},... | collective-permute-start | bytes 110600 | tf_op jit(solution)/shard_map/ppermute | solution.py:539
  4.1 1.0 %copy-start.7 = (bf16[3,48,128]{2,1,0:T(8,128)(2,1)S(1)}, bf16[3,48,128]{2,1,0:T(8,128)(2,1)}, u32[]{:S(2)}) copy-start(bf16[3,48,128]{2,1,0:T(8,128)(2,1)} %param.17) | copy-start | bytes 110596
  5.1 0.7 %copy-start.11 = (f32[128]{0:T(128)S(1)}, f32[128]{0:T(128)}, u32[]{:S(2)}) copy-start(f32[128]{0:T(128)} %param.24) | copy-start | bytes 1540
  5.1 0.7 %copy-start.12 = (f32[128]{0:T(128)S(1)}, f32[128]{0:T(128)}, u32[]{:S(2)}) copy-start(f32[128]{0:T(128)} %param.26) | copy-start | bytes 1540
  5.1 0.7 %copy-start.13 = (f32[128]{0:T(128)S(1)}, f32[128]{0:T(128)}, u32[]{:S(2)}) copy-start(f32[128]{0:T(128)} %param.27) | copy-start | bytes 1540
  5.1 0.7 %copy-start.8 = (f32[128]{0:T(128)S(1)}, f32[128]{0:T(128)}, u32[]{:S(2)}) copy-start(f32[128]{0:T(128)} %param.19) | copy-start | bytes 1540
  5.1 0.7 %copy-start.9 = (f32[128]{0:T(128)S(1)}, f32[128]{0:T(128)}, u32[]{:S(2)}) copy-start(f32[128]{0:T(128)} %param.20) | copy-start | bytes 1540
  5.1 0.7 %copy-start.10 = (f32[128]{0:T(128)S(1)}, f32[128]{0:T(128)}, u32[]{:S(2)}) copy-start(f32[128]{0:T(128)} %param.23) | copy-start | bytes 1540
  6.6 5.8 %collective-permute-start.2 = (bf16[6,48,128]{2,1,0:T(8,128)(2,1)S(1)}, bf16[6,48,128]{2,1,0:T(8,128)(2,1)S(1)}, u32[]{:S(2)}, u32[]{:S(2)}) collective-permute-start(bf16[6,48,128]{2,1,0:T(8,128)(2,1)S(1)} %constant_dynamic-update-slice_fusion.refs_0_), channel_id=1, source_target_pairs={{0,6},{1,7},{2,4},{3,5},{4,2},{5,3},{6,0},{7,1},{8,14},{9,15},{10,... | collective-permute-start | bytes 221192 | tf_op jit(solution)/shard_map/ppermute | solution.py:539
  9.1 4.4 %collective-permute-start.1 = (bf16[6,48,128]{2,1,0:T(8,128)(2,1)S(1)}, bf16[6,48,128]{2,1,0:T(8,128)(2,1)S(1)}, u32[]{:S(2)}, u32[]{:S(2)}) collective-permute-start(bf16[6,48,128]{2,1,0:T(8,128)(2,1)S(1)} %constant_dynamic-update-slice_fusion.refs_0_), channel_id=1, source_target_pairs={{0,2},{1,3},{2,0},{3,1},{4,6},{5,7},{6,4},{7,5},{8,10},{9,11},{10,... | collective-permute-start | bytes 221192 | tf_op jit(solution)/shard_map/ppermute | solution.py:539
  9.6 4.4 %collective-permute-start.3 = (bf16[6,48,128]{2,1,0:T(8,128)(2,1)S(1)}, bf16[6,48,128]{2,1,0:T(8,128)(2,1)S(1)}, u32[]{:S(2)}, u32[]{:S(2)}) collective-permute-start(bf16[6,48,128]{2,1,0:T(8,128)(2,1)S(1)} %constant_dynamic-update-slice_fusion.refs_0_), channel_id=1, source_target_pairs={{0,4},{1,5},{2,6},{3,7},{4,0},{5,1},{6,2},{7,3},{8,12},{9,13},{10,... | collective-permute-start | bytes 221192 | tf_op jit(solution)/shard_map/ppermute | solution.py:539
  10.1 0.7 %copy-start.14 = (s32[48]{0:T(128)S(1)}, s32[48]{0:T(128)}, u32[]{:S(2)}) copy-start(s32[48]{0:T(128)} %param.18) | copy-start | bytes 580
  13.4 1.4 %collective-permute-start.4 = (bf16[12,48,128]{2,1,0:T(8,128)(2,1)S(1)}, bf16[12,48,128]{2,1,0:T(8,128)(2,1)S(1)}, u32[]{:S(2)}, u32[]{:S(2)}) collective-permute-start(bf16[12,48,128]{2,1,0:T(8,128)(2,1)S(1)} %get-tuple-element.76), channel_id=1, source_target_pairs={{0,1},{1,0},{2,3},{3,2},{4,5},{5,4},{6,7},{7,6},{8,9},{9,8},{10,11... | collective-permute-start | bytes 442376 | tf_op jit(solution)/shard_map/ppermute | solution.py:539
  14.6 1.4 %collective-permute-start.5 = (bf16[12,48,128]{2,1,0:T(8,128)(2,1)S(1)}, bf16[12,48,128]{2,1,0:T(8,128)(2,1)S(1)}, u32[]{:S(2)}, u32[]{:S(2)}) collective-permute-start(bf16[12,48,128]{2,1,0:T(8,128)(2,1)S(1)} %get-tuple-element.78), channel_id=1, source_target_pairs={{0,1},{1,0},{2,3},{3,2},{4,5},{5,4},{6,7},{7,6},{8,9},{9,8},{10,11... | collective-permute-start | bytes 442376 | tf_op jit(solution)/shard_map/ppermute | solution.py:539
  14.8 1.3 %copy-start.1 = (bf16[128,128]{1,0:T(8,128)(2,1)S(1)}, bf16[128,128]{1,0:T(8,128)(2,1)}, u32[]{:S(2)}) copy-start(bf16[128,128]{1,0:T(8,128)(2,1)} %w_out.4) | copy-start | bytes 98308
  17.2 1.8 %collective-permute-start.7 = (bf16[576,128]{1,0:T(8,128)(2,1)S(1)}, bf16[576,128]{1,0:T(8,128)(2,1)S(1)}, u32[]{:S(2)}, u32[]{:S(2)}) collective-permute-start(bf16[576,128]{1,0:T(8,128)(2,1)S(1)} %get-tuple-element.81.own_att_a), channel_id=1, source_target_pairs={{0,1},{1,0},{2,3},{3,2},{4,5},{5,4},{6,7},{7,6},{8,9},{9,8},{10,11... | collective-permute-start | bytes 442376 | tf_op jit(solution)/shard_map/ppermute | solution.py:539
  17.7 1.3 %copy-start.2 = (bf16[128,128]{1,0:T(8,128)(2,1)S(1)}, bf16[128,128]{1,0:T(8,128)(2,1)}, u32[]{:S(2)}) copy-start(bf16[128,128]{1,0:T(8,128)(2,1)} %w_key.3) | copy-start | bytes 98308
  17.7 1.3 %copy-start.3 = (bf16[128,128]{1,0:T(8,128)(2,1)S(1)}, bf16[128,128]{1,0:T(8,128)(2,1)}, u32[]{:S(2)}) copy-start(bf16[128,128]{1,0:T(8,128)(2,1)} %w_value.3) | copy-start | bytes 98308
  17.7 1.3 %copy-start.4 = (bf16[128,128]{1,0:T(8,128)(2,1)S(1)}, bf16[128,128]{1,0:T(8,128)(2,1)}, u32[]{:S(2)}) copy-start(bf16[128,128]{1,0:T(8,128)(2,1)} %w_query.1) | copy-start | bytes 98308
  17.7 1.3 %copy-start.5 = (bf16[128,128]{1,0:T(8,128)(2,1)S(1)}, bf16[128,128]{1,0:T(8,128)(2,1)}, u32[]{:S(2)}) copy-start(bf16[128,128]{1,0:T(8,128)(2,1)} %w_gate.1) | copy-start | bytes 98308
  18.8 1.5 %collective-permute-start.6 = (bf16[576,128]{1,0:T(8,128)(2,1)S(1)}, bf16[576,128]{1,0:T(8,128)(2,1)S(1)}, u32[]{:S(2)}, u32[]{:S(2)}) collective-permute-start(bf16[576,128]{1,0:T(8,128)(2,1)S(1)} %shard_map.168.own_att_b), channel_id=1, source_target_pairs={{0,1},{1,0},{2,3},{3,2},{4,5},{5,4},{6,7},{7,6},{8,9},{9,8},{10,11... | collective-permute-start | bytes 442376 | tf_op jit(solution)/shard_map/ppermute | solution.py:539
  19.0 1.3 %copy-start.6 = (bf16[128,128]{1,0:T(8,128)(2,1)S(1)}, bf16[128,128]{1,0:T(8,128)(2,1)}, u32[]{:S(2)}) copy-start(bf16[128,128]{1,0:T(8,128)(2,1)} %w_out.5) | copy-start | bytes 98308

commit v26 on v24

--- a/solution.py
+++ b/solution.py
@@ -361,13 +361,21 @@
         else:
             scores = [dot(product, same_head[...]) for product in products]
 
-        def score_of(n, r):
-            lanes = slice(n % 2 * channels, (n % 2 + 1) * channels)
+        shifts = []
+        for n in range(count):
             k = (2 * (first + n // row_count) + core) * row_count + n % row_count
             key_mask = 1000000000.0 * (valid_column[pl.ds(k, 1), :] - 1.0)
             at = part * count + n
-            shift = (bias_ref[r, at : at + 1, :] + key_mask) * math.log2(math.e)
-            return scores[r][n // 2 * res : (n // 2 + 1) * res, lanes] + shift
+            shifts.append(
+                [
+                    (bias_ref[r, at : at + 1, :] + key_mask) * math.log2(math.e)
+                    for r in range(row_count)
+                ]
+            )
+
+        def score_of(n, r):
+            lanes = slice(n % 2 * channels, (n % 2 + 1) * channels)
+            return scores[r][n // 2 * res : (n // 2 + 1) * res, lanes] + shifts[n][r]
 
         later = []
         for r, (maximum, total, mixed) in enumerate(sums):

time: 21.9 us -> 21.9 us (level)
  no operation moved by 1% of the time
where the time goes in v26:
time: 21.9 us; the launch traced here: 21.7 us
  starting transfers between devices  8.3 us (38%)
  Pallas kernels  7.6 us (35%)
  waiting for transfers between devices  3.16 us (14%)
  local copies, waits for them, and re-layouts  1.28 us (6%)
  other arithmetic  0.99 us (5%)
    ppermute x8, starting transfers between devices, exchange(): return lax.ppermute(values, 'row', [(d, d ^ bit) for d in range(devices)])  8.3 us
    pallas_call x8, Pallas kernels, call(): pl.pallas_call(kernel, out_shape=outs, in_specs=[in_vmem] * len(operands)...  7.6 us
    ppermute x8, waiting for transfers between devices, exchange(): return lax.ppermute(values, 'row', [(d, d ^ bit) for d in range(devices)])  3.16 us
    unnamed x30, local copies, waits for them, and re-layouts  1.16 us
    mul x1, other arithmetic, on_whole_complex(): edge_weights = jnp.concatenate([w_edges, w_tri_gate], axis=1) * halves  0.97 us
  transfers between devices with their start and end apart: 8, of which 5 were waited for; matrix products, arithmetic and copies ran while one was open for 6% of the time, Pallas kernels for 23%

profile of v26, /device:TPU:0, one launch (start us, length us, event | category | flops | bytes accessed | tf_op | source)
XLA Modules:
  0.0 21.7 jit_solution(16066109668655126838)
XLA Ops:
  0.0 4.0 %collective-permute-start = (bf16[3,48,128]{2,1,0:T(8,128)(2,1)}, bf16[3,48,128]{2,1,0:T(8,128)(2,1)S(1)}, u32[]{:S(2)}, u32[]{:S(2)}) collective-permute-start(bf16[3,48,128]{2,1,0:T(8,128)(2,1)} %param.17), channel_id=1, source_target_pairs={{0,8},{1,9},{2,10},{3,11},{4,12},{5,13},{6,14},{7,15},{8,0},{9,1},... | collective-permute-start | bytes 110600 | tf_op jit(solution)/shard_map/ppermute | solution.py:535
  4.1 1.0 %maximum_multiply_fusion.weights = bf16[128,640]{1,0:T(8,128)(2,1)S(1)} fusion(bf16[128,128]{1,0:T(8,128)(2,1)} %param.22, bf16[128,512]{1,0:T(8,128)(2,1)} %param.21, bf16[640]{0:T(1024)(128)(2,1)S(1)} %select_convert_fusion), kind=kLoop, calls=%fused_computation.2 | loop fusion | flops 491520 | bytes 328960 | tf_op jit(solution)/shard_map/mul | solution.py:548
  5.1 0.6 %copy-done.11 = f32[128]{0:T(128)S(1)} copy-done((f32[128]{0:T(128)S(1)}, f32[128]{0:T(128)}, u32[]{:S(2)}) %copy-start.11) | copy-done | bytes 536
  5.8 0.8 %collective-permute-done = bf16[3,48,128]{2,1,0:T(8,128)(2,1)S(1)} collective-permute-done((bf16[3,48,128]{2,1,0:T(8,128)(2,1)}, bf16[3,48,128]{2,1,0:T(8,128)(2,1)S(1)}, u32[]{:S(2)}, u32[]{:S(2)}) %collective-permute-start) | collective-permute-done | bytes 36896 | tf_op jit(solution)/shard_map/ppermute | solution.py:535
  6.6 2.5 %collective-permute-start.2 = (bf16[6,48,128]{2,1,0:T(8,128)(2,1)S(1)}, bf16[6,48,128]{2,1,0:T(8,128)(2,1)S(1)}, u32[]{:S(2)}, u32[]{:S(2)}) collective-permute-start(bf16[6,48,128]{2,1,0:T(8,128)(2,1)S(1)} %constant_dynamic-update-slice_fusion.refs_0_), channel_id=1, source_target_pairs={{0,6},{1,7},{2,4},{3,5},{4,2},{5,3},{6,0},{7,1},{8,14},{9,15},{10,... | collective-permute-start | bytes 221192 | tf_op jit(solution)/shard_map/ppermute | solution.py:535
  9.1 0.5 %collective-permute-start.1 = (bf16[6,48,128]{2,1,0:T(8,128)(2,1)S(1)}, bf16[6,48,128]{2,1,0:T(8,128)(2,1)S(1)}, u32[]{:S(2)}, u32[]{:S(2)}) collective-permute-start(bf16[6,48,128]{2,1,0:T(8,128)(2,1)S(1)} %constant_dynamic-update-slice_fusion.refs_0_), channel_id=1, source_target_pairs={{0,2},{1,3},{2,0},{3,1},{4,6},{5,7},{6,4},{7,5},{8,10},{9,11},{10,... | collective-permute-start | bytes 221192 | tf_op jit(solution)/shard_map/ppermute | solution.py:535
  9.6 0.5 %collective-permute-start.3 = (bf16[6,48,128]{2,1,0:T(8,128)(2,1)S(1)}, bf16[6,48,128]{2,1,0:T(8,128)(2,1)S(1)}, u32[]{:S(2)}, u32[]{:S(2)}) collective-permute-start(bf16[6,48,128]{2,1,0:T(8,128)(2,1)S(1)} %constant_dynamic-update-slice_fusion.refs_0_), channel_id=1, source_target_pairs={{0,4},{1,5},{2,6},{3,7},{4,0},{5,1},{6,2},{7,3},{8,12},{9,13},{10,... | collective-permute-start | bytes 221192 | tf_op jit(solution)/shard_map/ppermute | solution.py:535
  10.1 0.2 fusion.wide_bias
  10.4 0.4 %copy-done.14 = s32[48]{0:T(128)S(1)} copy-done((s32[48]{0:T(128)S(1)}, s32[48]{0:T(128)}, u32[]{:S(2)}) %copy-start.14) | copy-done | bytes 216
  10.8 0.1 broadcast_in_dim.23.valid_column
  10.9 0.4 %shard_map.163 = (f32[1152,128]{1,0:T(8,128)S(1)}, f32[1152,128]{1,0:T(8,128)S(1)}, f32[1152,128]{1,0:T(8,128)S(1)}, f32[1152,128]{1,0:T(8,128)S(1)}, bf16[12,48...) custom-call(f32[48,128]{1,0:T(8,128)S(1)} %broadcast_in_dim.23.valid_column, f32[6,128]{1,0:T(8,128)S(1)} %stack.27.norms, ...), custom_call_target="tpu_custom_call" | custom-call | flops 1048576 | bytes 33554432 | tf_op jit(solution)/shard_map/pallas_call | solution.py:524
  11.3 1.1 %collective-permute-done.2.refs_0_ = bf16[6,48,128]{2,1,0:T(8,128)(2,1)S(1)} collective-permute-done((bf16[6,48,128]{2,1,0:T(8,128)(2,1)S(1)}, bf16[6,48,128]{2,1,0:T(8,128)(2,1)S(1)}, u32[]{:S(2)}, u32[]{:S(2)}) %collective-permute-start.2) | collective-permute-done | bytes 73760 | tf_op jit(solution)/shard_map/ppermute | solution.py:535
  12.4 0.4 %shard_map.164 = (f32[1152,128]{1,0:T(8,128)S(1)}, f32[1152,128]{1,0:T(8,128)S(1)}, f32[1152,128]{1,0:T(8,128)S(1)}, f32[1152,128]{1,0:T(8,128)S(1)}, bf16[12,48,128]{2,1,0:T(8,128)(2,1)S(1)}) custom-call(f32[48,128]{1,0:T(8,128)S(1)} %broadcast_in_dim.23.valid_column, f32[6,128]{1,0:T(8,128)S(1)} %stack.27.norms, ...), custom_call_target="tpu_custom_call" | custom-call | flops 1048576 | bytes 33554432 | tf_op jit(solution)/shard_map/pallas_call | solution.py:524
  12.8 0.6 %collective-permute-done.1.refs_0_ = bf16[6,48,128]{2,1,0:T(8,128)(2,1)S(1)} collective-permute-done((bf16[6,48,128]{2,1,0:T(8,128)(2,1)S(1)}, bf16[6,48,128]{2,1,0:T(8,128)(2,1)S(1)}, u32[]{:S(2)}, u32[]{:S(2)}) %collective-permute-start.1) | collective-permute-done | bytes 73760 | tf_op jit(solution)/shard_map/ppermute | solution.py:535
  13.4 0.5 %collective-permute-done.3.refs_1_ = bf16[6,48,128]{2,1,0:T(8,128)(2,1)S(1)} collective-permute-done((bf16[6,48,128]{2,1,0:T(8,128)(2,1)S(1)}, bf16[6,48,128]{2,1,0:T(8,128)(2,1)S(1)}, u32[]{:S(2)}, u32[]{:S(2)}) %collective-permute-start.3) | collective-permute-done | bytes 73760 | tf_op jit(solution)/shard_map/ppermute | solution.py:535
  14.0 0.6 %shard_map.165 = (f32[1152,128]{1,0:T(8,128)S(1)}, f32[1152,128]{1,0:T(8,128)S(1)}, f32[1152,128]{1,0:T(8,128)S(1)}, f32[1152,128]{1,0:T(8,128)S(1)}, bf16[12,48,128]{2,1,0:T(8,128)(2,1)S(1)}) custom-call(f32[48,128]{1,0:T(8,128)S(1)} %broadcast_in_dim.23.valid_column, f32[6,128]{1,0:T(8,128)S(1)} %stack.27.norms, ...), custom_call_target="tpu_custom_call" | custom-call | flops 1048576 | bytes 33554432 | tf_op jit(solution)/shard_map/pallas_call | solution.py:524
  14.7 0.1 collective-permute-done.4.refs_0_
  14.8 1.2 %shard_map.166 = (f32[1152,128]{1,0:T(8,128)S(1)}, f32[1152,128]{1,0:T(8,128)S(1)}) custom-call(f32[1152,128]{1,0:T(8,128)S(1)} %get-tuple-element.72.left_ref.refs_0_, f32[1152,128]{1,0:T(8,128)S(1)} %get-tuple-element.75.right_ref, bf16[12,48,128]{2,1,0:T(8,128)(2,1)S(1)} %collective-permute-done.4.refs_0_), custom_call_target="tpu_custom_call" | custom-call | flops 1048576 | bytes 33554432 | tf_op jit(solution)/shard_map/pallas_call | solution.py:524
  16.1 1.1 %shard_map.167 = (f32[1152,128]{1,0:T(8,128)S(1)}, f32[576,128]{1,0:T(8,128)S(1)}, bf16[576,128]{1,0:T(8,128)(2,1)S(1)}) custom-call(f32[6,128]{1,0:T(8,128)S(1)} %stack.27.norms, bf16[128,128]{1,0:T(8,128)(2,1)S(1)} %copy-done.1, f32[1152,128]{1,0:T(8,128)S(1)} %get-tuple-element.72.left_ref.refs_0_, f32[1152,128]{1,0:T(8,128)S(1)} %get-tuple-element.73.gate_ref.refs_1_, ...), custom_call_target="tpu_custom_call" | custom-call | flops 1048576 | bytes 33554432 | tf_op jit(solution)/shard_map/pallas_call | solution.py:524
  17.2 0.4 %collective-permute-start.7 = (bf16[576,128]{1,0:T(8,128)(2,1)S(1)}, bf16[576,128]{1,0:T(8,128)(2,1)S(1)}, u32[]{:S(2)}, u32[]{:S(2)}) collective-permute-start(bf16[576,128]{1,0:T(8,128)(2,1)S(1)} %get-tuple-element.81.own_att_a), channel_id=1, source_target_pairs={{0,1},{1,0},{2,3},{3,2},{4,5},{5,4},{6,7},{7,6},{8,9},{9,8},{10,11... | collective-permute-start | bytes 442376 | tf_op jit(solution)/shard_map/ppermute | solution.py:535
  17.7 1.1 %shard_map.168.own_att_b = bf16[576,128]{1,0:T(8,128)(2,1)S(1)} custom-call(f32[6,128]{1,0:T(8,128)S(1)} %stack.27.norms, bf16[128,128]{1,0:T(8,128)(2,1)S(1)} %copy-done.1, f32[1152,128]{1,0:T(8,128)S(1)} %get-tuple-element.72.left_ref.refs_0_, f32[1152,128]{1,0:T(8,128)S(1)} %get-tuple-element.73.gate_ref.refs_1_, ...), custom_call_target="tpu_custom_call" | custom-call | flops 1048576 | bytes 33554432 | tf_op jit(solution)/shard_map/pallas_call | solution.py:524
  18.8 0.2 collective-permute-start.6
  19.0 1.3 %shard_map.169 = (f32[3,3,48,128]{3,2,1,0:T(8,128)S(1)}, f32[144,128]{1,0:T(8,128)S(1)}, f32[144,128]{1,0:T(8,128)S(1)}, f32[144,128]{1,0:T(8,128)S(1)}) custom-call(f32[48,128]{1,0:T(8,128)S(1)} %broadcast_in_dim.23.valid_column, bf16[256,256]{1,0:T(8,128)(2,1)S(1)} %get-tuple-element.50.same_head, bf16[128,128]{1,0:T(8,128)(2,1)S(1)} %copy-done.4, ...), custom_call_target="tpu_custom_call" | custom-call | flops 1048576 | bytes 33554432 | tf_op jit(solution)/shard_map/pallas_call | solution.py:524
  20.3 1.4 %shard_map.170 = bf16[3,48,128]{2,1,0:T(8,128)(2,1)} custom-call(f32[48,128]{1,0:T(8,128)S(1)} %broadcast_in_dim.23.valid_column, bf16[256,256]{1,0:T(8,128)(2,1)S(1)} %get-tuple-element.50.same_head, bf16[128,128]{1,0:T(8,128)(2,1)S(1)} %copy-done.2, bf16[128,128]{1,0:T(8,128)(2,1)S(1)} %copy-done.3, bf16[128,128]{1,0:T(8,128)(2,1)S(1)} %copy-done.6, ...), custom_call_target="tpu_custom_call" | custom-call | flops 1048576 | bytes 33554432 | tf_op jit(solution)/shard_map/pallas_call | solution.py:524
  (40 shorter events, 0.3 us)
Async XLA Ops:
  0.0 10.1 %copy-start = (bf16[128,4]{0,1:T(4,128)(2,1)S(1)}, bf16[128,4]{0,1:T(4,128)(2,1)}, u32[]{:S(2)}) copy-start(bf16[128,4]{0,1:T(4,128)(2,1)} %param.32) | copy-start | bytes 3076
  0.0 6.6 %collective-permute-start = (bf16[3,48,128]{2,1,0:T(8,128)(2,1)}, bf16[3,48,128]{2,1,0:T(8,128)(2,1)S(1)}, u32[]{:S(2)}, u32[]{:S(2)}) collective-permute-start(bf16[3,48,128]{2,1,0:T(8,128)(2,1)} %param.17), channel_id=1, source_target_pairs={{0,8},{1,9},{2,10},{3,11},{4,12},{5,13},{6,14},{7,15},{8,0},{9,1},... | collective-permute-start | bytes 110600 | tf_op jit(solution)/shard_map/ppermute | solution.py:535
  4.1 1.0 %copy-start.7 = (bf16[3,48,128]{2,1,0:T(8,128)(2,1)S(1)}, bf16[3,48,128]{2,1,0:T(8,128)(2,1)}, u32[]{:S(2)}) copy-start(bf16[3,48,128]{2,1,0:T(8,128)(2,1)} %param.17) | copy-start | bytes 110596
  5.1 0.7 %copy-start.11 = (f32[128]{0:T(128)S(1)}, f32[128]{0:T(128)}, u32[]{:S(2)}) copy-start(f32[128]{0:T(128)} %param.24) | copy-start | bytes 1540
  5.1 0.7 %copy-start.12 = (f32[128]{0:T(128)S(1)}, f32[128]{0:T(128)}, u32[]{:S(2)}) copy-start(f32[128]{0:T(128)} %param.26) | copy-start | bytes 1540
  5.1 0.7 %copy-start.13 = (f32[128]{0:T(128)S(1)}, f32[128]{0:T(128)}, u32[]{:S(2)}) copy-start(f32[128]{0:T(128)} %param.27) | copy-start | bytes 1540
  5.1 0.7 %copy-start.8 = (f32[128]{0:T(128)S(1)}, f32[128]{0:T(128)}, u32[]{:S(2)}) copy-start(f32[128]{0:T(128)} %param.19) | copy-start | bytes 1540
  5.1 0.7 %copy-start.9 = (f32[128]{0:T(128)S(1)}, f32[128]{0:T(128)}, u32[]{:S(2)}) copy-start(f32[128]{0:T(128)} %param.20) | copy-start | bytes 1540
  5.1 0.7 %copy-start.10 = (f32[128]{0:T(128)S(1)}, f32[128]{0:T(128)}, u32[]{:S(2)}) copy-start(f32[128]{0:T(128)} %param.23) | copy-start | bytes 1540
  6.6 5.8 %collective-permute-start.2 = (bf16[6,48,128]{2,1,0:T(8,128)(2,1)S(1)}, bf16[6,48,128]{2,1,0:T(8,128)(2,1)S(1)}, u32[]{:S(2)}, u32[]{:S(2)}) collective-permute-start(bf16[6,48,128]{2,1,0:T(8,128)(2,1)S(1)} %constant_dynamic-update-slice_fusion.refs_0_), channel_id=1, source_target_pairs={{0,6},{1,7},{2,4},{3,5},{4,2},{5,3},{6,0},{7,1},{8,14},{9,15},{10,... | collective-permute-start | bytes 221192 | tf_op jit(solution)/shard_map/ppermute | solution.py:535
  9.1 4.4 %collective-permute-start.1 = (bf16[6,48,128]{2,1,0:T(8,128)(2,1)S(1)}, bf16[6,48,128]{2,1,0:T(8,128)(2,1)S(1)}, u32[]{:S(2)}, u32[]{:S(2)}) collective-permute-start(bf16[6,48,128]{2,1,0:T(8,128)(2,1)S(1)} %constant_dynamic-update-slice_fusion.refs_0_), channel_id=1, source_target_pairs={{0,2},{1,3},{2,0},{3,1},{4,6},{5,7},{6,4},{7,5},{8,10},{9,11},{10,... | collective-permute-start | bytes 221192 | tf_op jit(solution)/shard_map/ppermute | solution.py:535
  9.6 4.4 %collective-permute-start.3 = (bf16[6,48,128]{2,1,0:T(8,128)(2,1)S(1)}, bf16[6,48,128]{2,1,0:T(8,128)(2,1)S(1)}, u32[]{:S(2)}, u32[]{:S(2)}) collective-permute-start(bf16[6,48,128]{2,1,0:T(8,128)(2,1)S(1)} %constant_dynamic-update-slice_fusion.refs_0_), channel_id=1, source_target_pairs={{0,4},{1,5},{2,6},{3,7},{4,0},{5,1},{6,2},{7,3},{8,12},{9,13},{10,... | collective-permute-start | bytes 221192 | tf_op jit(solution)/shard_map/ppermute | solution.py:535
  10.1 0.7 %copy-start.14 = (s32[48]{0:T(128)S(1)}, s32[48]{0:T(128)}, u32[]{:S(2)}) copy-start(s32[48]{0:T(128)} %param.18) | copy-start | bytes 580
  13.4 1.4 %collective-permute-start.4 = (bf16[12,48,128]{2,1,0:T(8,128)(2,1)S(1)}, bf16[12,48,128]{2,1,0:T(8,128)(2,1)S(1)}, u32[]{:S(2)}, u32[]{:S(2)}) collective-permute-start(bf16[12,48,128]{2,1,0:T(8,128)(2,1)S(1)} %get-tuple-element.76), channel_id=1, source_target_pairs={{0,1},{1,0},{2,3},{3,2},{4,5},{5,4},{6,7},{7,6},{8,9},{9,8},{10,11... | collective-permute-start | bytes 442376 | tf_op jit(solution)/shard_map/ppermute | solution.py:535
  14.6 1.4 %collective-permute-start.5 = (bf16[12,48,128]{2,1,0:T(8,128)(2,1)S(1)}, bf16[12,48,128]{2,1,0:T(8,128)(2,1)S(1)}, u32[]{:S(2)}, u32[]{:S(2)}) collective-permute-start(bf16[12,48,128]{2,1,0:T(8,128)(2,1)S(1)} %get-tuple-element.78), channel_id=1, source_target_pairs={{0,1},{1,0},{2,3},{3,2},{4,5},{5,4},{6,7},{7,6},{8,9},{9,8},{10,11... | collective-permute-start | bytes 442376 | tf_op jit(solution)/shard_map/ppermute | solution.py:535
  14.8 1.3 %copy-start.1 = (bf16[128,128]{1,0:T(8,128)(2,1)S(1)}, bf16[128,128]{1,0:T(8,128)(2,1)}, u32[]{:S(2)}) copy-start(bf16[128,128]{1,0:T(8,128)(2,1)} %w_out.4) | copy-start | bytes 98308
  17.2 1.8 %collective-permute-start.7 = (bf16[576,128]{1,0:T(8,128)(2,1)S(1)}, bf16[576,128]{1,0:T(8,128)(2,1)S(1)}, u32[]{:S(2)}, u32[]{:S(2)}) collective-permute-start(bf16[576,128]{1,0:T(8,128)(2,1)S(1)} %get-tuple-element.81.own_att_a), channel_id=1, source_target_pairs={{0,1},{1,0},{2,3},{3,2},{4,5},{5,4},{6,7},{7,6},{8,9},{9,8},{10,11... | collective-permute-start | bytes 442376 | tf_op jit(solution)/shard_map/ppermute | solution.py:535
  17.7 1.3 %copy-start.2 = (bf16[128,128]{1,0:T(8,128)(2,1)S(1)}, bf16[128,128]{1,0:T(8,128)(2,1)}, u32[]{:S(2)}) copy-start(bf16[128,128]{1,0:T(8,128)(2,1)} %w_key.3) | copy-start | bytes 98308
  17.7 1.3 %copy-start.3 = (bf16[128,128]{1,0:T(8,128)(2,1)S(1)}, bf16[128,128]{1,0:T(8,128)(2,1)}, u32[]{:S(2)}) copy-start(bf16[128,128]{1,0:T(8,128)(2,1)} %w_value.3) | copy-start | bytes 98308
  17.7 1.3 %copy-start.4 = (bf16[128,128]{1,0:T(8,128)(2,1)S(1)}, bf16[128,128]{1,0:T(8,128)(2,1)}, u32[]{:S(2)}) copy-start(bf16[128,128]{1,0:T(8,128)(2,1)} %w_query.1) | copy-start | bytes 98308
  17.7 1.3 %copy-start.5 = (bf16[128,128]{1,0:T(8,128)(2,1)S(1)}, bf16[128,128]{1,0:T(8,128)(2,1)}, u32[]{:S(2)}) copy-start(bf16[128,128]{1,0:T(8,128)(2,1)} %w_gate.1) | copy-start | bytes 98308
  18.8 1.5 %collective-permute-start.6 = (bf16[576,128]{1,0:T(8,128)(2,1)S(1)}, bf16[576,128]{1,0:T(8,128)(2,1)S(1)}, u32[]{:S(2)}, u32[]{:S(2)}) collective-permute-start(bf16[576,128]{1,0:T(8,128)(2,1)S(1)} %shard_map.168.own_att_b), channel_id=1, source_target_pairs={{0,1},{1,0},{2,3},{3,2},{4,5},{5,4},{6,7},{7,6},{8,9},{9,8},{10,11... | collective-permute-start | bytes 442376 | tf_op jit(solution)/shard_map/ppermute | solution.py:535
  19.0 1.3 %copy-start.6 = (bf16[128,128]{1,0:T(8,128)(2,1)S(1)}, bf16[128,128]{1,0:T(8,128)(2,1)}, u32[]{:S(2)}) copy-start(bf16[128,128]{1,0:T(8,128)(2,1)} %w_out.5) | copy-start | bytes 98308
